TPU v7x, 32 devices: a whole 2x2x4 slice. The times are simulated.
32 devices in a mesh: grp: 2 (over y), ex: 8 (over z, x), dim: 2 (over core).
Axes of the slice: x: 2, y: 2, z: 4, core: 2. Of those that a mesh axis runs over, the one named last changes fastest.
Arguments:
- queries: bfloat16 [96, 16384], P(None, 'ex'), may hold values from -6 to 6
- inverse_fisher: bfloat16 [16384, 16384], P('ex', 'dim'), as said below
- stored_grads: bfloat16 [2048, 16384], P(('grp', 'ex'), 'dim'), parts along dimension 0, may hold values from -0.046875 to 0.046875
Outputs:
- scores: float32 [96, 2048], P('dim', ('grp', 'ex')), parts along dimension 1
There are 2 independent parts, one for each index of `grp`. A program takes and returns all parts, laid end to end along the dimension named above; an argument that names none is the same for every part. Nothing has to cross between parts.
Inputs may be any that keep to these rules, and one draw needn't show every extreme that they name: inverse_fisher is symmetric up to rounding.
All inputs are finite; a program needn't handle non-finite values.
Results may differ from a plain program's by a relative error of at most 0.0029.
Values may be sent and summed in bfloat16 or wider, within the bound.
No kernel may reach another device: no remote copies, remote signals or barrier semaphores. Data moves between devices by JAX's collectives and lax.ppermute only.
A program may use at most 128 MiB of HBM per device.

v0:
```python
import jax
import jax.numpy as jnp
from jax import lax
from jax.sharding import PartitionSpec as P


def per_device(queries, inverse_fisher, stored_grads):
    term_block = jnp.dot(queries, inverse_fisher, preferred_element_type=jnp.float32)
    own_panel = lax.psum_scatter(term_block, "ex", scatter_dimension=1, tiled=True).astype(
        jnp.bfloat16
    )
    partial_scores = lax.dot_general(
        lax.all_gather(own_panel, "ex", axis=1, tiled=True),
        stored_grads,
        (((1,), (1,)), ((), ())),
        preferred_element_type=jnp.float32,
    )
    return lax.psum_scatter(partial_scores, "dim", scatter_dimension=0, tiled=True)


def solution(mesh):
    return jax.shard_map(
        per_device,
        mesh=mesh,
        in_specs=(P(None, "ex"), P("ex", "dim"), P(("grp", "ex"), "dim")),
        out_specs=P("dim", ("grp", "ex")),
        check_vma=False,
    )
```

profile of v0, /device:TPU:0, one launch (start us, length us, event | category | flops | bytes accessed | tf_op | source)
XLA Modules:
  0.0 163.8 jit_solution(5777765130955329271)
XLA Ops:
  6.5 0.0 copy-start
  6.5 0.0 reduce-scatter.3.cloned.1.call-start
  6.5 17.8 %fusion = f32[96,8192]{1,0:T(8,128)} fusion(bf16[96,2048]{1,0:T(8,128)(2,1)} %param.3, bf16[2048,8192]{1,0:T(8,128)(2,1)} %param.4), kind=kOutput, calls=%fused_computation | convolution fusion | flops 3221225472 | bytes 37093376 | tf_op jit(solution)/shard_map/dot_general | solution.py:8
  24.4 0.0 reduce-scatter.3.cloned.1.call-update
  24.4 0.0 all-gather.2.cloned.1.call-start
  24.5 77.7 %reduce-scatter.3.cloned.1.call-done = f32[96,1024]{1,0:T(8,128)} async-done(((f32[96,8192]{1,0:T(8,128)}), f32[96,1024]{1,0:T(8,128)}) %reduce-scatter.3.cloned.1.call-update) | async-done | bytes 393232 | tf_op jit(solution)/shard_map/reduce_scatter | solution.py:9
  102.2 1.7 %convert_element_type.3 = bf16[96,1024]{1,0:T(8,128)(2,1)} convert(f32[96,1024]{1,0:T(8,128)} %reduce-scatter.3.cloned.1.call-done) | non-fusion elementwise | flops 98304 | bytes 589824 | tf_op jit(solution)/shard_map/convert_element_type | solution.py:9
  103.9 0.0 all-gather.2.cloned.1.call-update
  103.9 0.0 reduce-scatter.5.cloned.1.call-start
  104.0 44.1 %all-gather.2.cloned.1.call-done = bf16[96,8192]{1,0:T(8,128)(2,1)} async-done(((bf16[96,1024]{1,0:T(8,128)(2,1)}), bf16[96,8192]{1,0:T(8,128)(2,1)}) %all-gather.2.cloned.1.call-update) | async-done | bytes 1572880 | tf_op jit(solution)/shard_map/all_gather | solution.py:13
  148.0 0.0 copy-done
  148.0 2.8 %fusion.1 = f32[96,128]{1,0:T(8,128)} fusion(bf16[96,8192]{1,0:T(8,128)(2,1)} %all-gather.2.cloned.1.call-done, bf16[128,8192]{1,0:T(8,128)(2,1)S(1)} %copy-done), kind=kOutput, calls=%fused_computation.1 | convolution fusion | flops 201326592 | bytes 3719168 | tf_op jit(solution)/shard_map/dot_general | solution.py:12
  150.9 0.0 reduce-scatter.5.cloned.1.call-update
  150.9 6.4 %reduce-scatter.5.cloned.1.call-done = f32[48,128]{1,0:T(8,128)} async-done(((f32[96,128]{1,0:T(8,128)}), f32[48,128]{1,0:T(8,128)}) %reduce-scatter.5.cloned.1.call-update) | async-done | bytes 24592 | tf_op jit(solution)/shard_map/reduce_scatter | solution.py:18
Async XLA Ops:
  6.5 141.5 %copy-start = (bf16[128,8192]{1,0:T(8,128)(2,1)S(1)}, bf16[128,8192]{1,0:T(8,128)(2,1)}, u32[]{:S(2)}) copy-start(bf16[128,8192]{1,0:T(8,128)(2,1)} %param.5) | copy-start | bytes 6291460
  6.5 95.7 %reduce-scatter.3.cloned.1.call-start = ((), (), s32[]{:S(2)}) async-start(), calls=%async_computation.2 | async-start | bytes 3538944 | tf_op jit(solution)/shard_map/reduce_scatter | solution.py:9
  24.4 123.6 %all-gather.2.cloned.1.call-start = ((), (), s32[]{:S(2)}) async-start(), calls=%async_computation.3 | async-start | bytes 1769472 | tf_op jit(solution)/shard_map/all_gather | solution.py:13
  103.9 53.4 %reduce-scatter.5.cloned.1.call-start = ((), (), s32[]{:S(2)}) async-start(), calls=%async_computation.4 | async-start | bytes 73728 | tf_op jit(solution)/shard_map/reduce_scatter | solution.py:18
Sparse Core Ops, SparseCore 0:
  24.5 77.6 reduce-scatter.2
  104.4 43.6 all-gather.1
  151.0 6.2 reduce-scatter.4
where the time goes:
time: 164 us
  waiting for transfers between devices  128 us (78%)
  matrix products  20.7 us (13%)
  between operations  13.1 us (8%)
  other arithmetic  1.71 us (1%)
    reduce_scatter x1, waiting for transfers between devices, per_device(): lax.psum_scatter(term_block, 'ex', scatter_dimension=1, tiled=True)  77.7 us
    all_gather x1, waiting for transfers between devices, per_device(): lax.all_gather(own_panel, 'ex', axis=1, tiled=True)  44.1 us
    dot_general x1, matrix products, per_device(): jnp.dot(queries, inverse_fisher, preferred_element_type=jnp.float32)  17.8 us
    reduce_scatter x1, waiting for transfers between devices, per_device(): lax.psum_scatter(partial_scores, 'dim', scatter_dimension=0, tiled=True)  6.4 us
  transfers between devices with their start and end apart: 3, of which 3 were waited for; matrix products, arithmetic and copies ran while one was open for 0% of the time, Pallas kernels for 0%

commit v1 on v0

v1 whole, which is shorter than its diff:
```python
import functools

import jax
import jax.numpy as jnp
from jax import lax
from jax.experimental import pallas as pl
from jax.experimental.pallas import tpu as pltpu
from jax.sharding import PartitionSpec as P

AXES = ("grp", "ex", "dim")
NT = (((1,), (1,)), ((), ()))


def per_device_any(queries, inverse_fisher, stored_grads):
    term_block = jnp.dot(queries, inverse_fisher, preferred_element_type=jnp.float32)
    own_panel = lax.psum_scatter(term_block, "ex", scatter_dimension=1, tiled=True).astype(
        jnp.bfloat16
    )
    partial_scores = lax.dot_general(
        lax.all_gather(own_panel, "ex", axis=1, tiled=True),
        stored_grads,
        NT,
        preferred_element_type=jnp.float32,
    )
    return lax.psum_scatter(partial_scores, "dim", scatter_dimension=0, tiled=True)


def fisher_kernel(n, has_base, cols_ref, *refs):
    del cols_ref
    out_ref = refs[-1]
    acc = refs[2 * n][...] if has_base else None
    for i in range(n):
        term = lax.dot_general(refs[i][...], refs[n + i][...], NT, preferred_element_type=jnp.float32)
        acc = term if acc is None else acc + term
    out_ref[...] = acc


def fisher_dot(chunks, cols, fisher, base=None, rows=512):
    n = len(chunks)
    nq, width = chunks[0].shape
    total = fisher.shape[0]
    in_specs = [pl.BlockSpec((nq, width), lambda i, c: (0, 0)) for _ in range(n)]
    in_specs += [
        pl.BlockSpec((rows, width), functools.partial(lambda k, i, c: (i, c[k]), k)) for k in range(n)
    ]
    operands = list(chunks) + [fisher] * n
    if base is not None:
        in_specs.append(pl.BlockSpec((nq, rows), lambda i, c: (0, i)))
        operands.append(base)
    return pl.pallas_call(
        functools.partial(fisher_kernel, n, base is not None),
        out_shape=jax.ShapeDtypeStruct((nq, total), jnp.float32),
        grid_spec=pltpu.PrefetchScalarGridSpec(
            num_scalar_prefetch=1,
            grid=(total // rows,),
            in_specs=in_specs,
            out_specs=pl.BlockSpec((nq, rows), lambda i, c: (0, i)),
        ),
        compiler_params=pltpu.CompilerParams(vmem_limit_bytes=32 * 1024 * 1024),
        cost_estimate=pl.CostEstimate(
            flops=2 * n * nq * width * total,
            bytes_accessed=n * width * total * 2,
            transcendentals=0,
        ),
    )(jnp.stack(cols).astype(jnp.int32), *operands)


def per_device_quad(nz, nx, ny, queries, inverse_fisher, stored_grads):
    nex = nz * nx
    near = nz // 2
    nq, block = queries.shape
    half = block // ny
    y, e, d = (lax.axis_index(a) for a in AXES)
    z = e // nx
    x = e % nx
    u = jnp.where(d == 0, z, nz - 1 - z)
    owner = u < near

    def move(value, target):
        pairs = []
        for sy in range(ny):
            for sz in range(nz):
                for sx in range(nx):
                    for sd in range(2):
                        to = target(sy, sz, sx, sd)
                        if to is not None:
                            ty, tz, tx, td = to
                            pairs.append(((sy * nex + sz * nx + sx) * 2 + sd, (ty * nex + tz * nx + tx) * 2 + td))
        return lax.ppermute(value, AXES, pairs)

    def along_z(value, hops):
        def target(sy, sz, sx, sd):
            su = sz if sd == 0 else nz - 1 - sz
            if su not in hops:
                return None
            tu = hops[su]
            return sy, tu if sd == 0 else nz - 1 - tu, sx, sd

        return move(value, target)

    def gather_z(own):
        swap = along_z(own, {0: 1, 1: 0})
        same = along_z(own, {0: 2, 1: 3})
        other = along_z(own, {0: 3, 1: 2})
        return jnp.where(owner, own, same), jnp.where(owner, swap, other)

    def real_plane(k):
        return jnp.where(d == 0, k, nz - 1 - k)

    planes = [real_plane(u % 2), real_plane(1 - u % 2)]
    first = d * (nex // 2)

    def column(plane, x_):
        return (plane * nx + x_ - first) * ny

    def slab(x_, y_):
        return jnp.concatenate(
            [
                lax.dynamic_slice_in_dim(stored_grads, (column(p, x_) + y_) * half, half, axis=1)
                for p in planes
            ],
            axis=1,
        )

    grads = [slab(x, y)]
    grads.append(move(slab(x, 1 - y), lambda sy, sz, sx, sd: (1 - sy, sz, sx, sd)))

    own = lax.dynamic_slice_in_dim(queries, y * half, half, axis=1)
    near_q = gather_z(own)
    far_q = [move(q, lambda sy, sz, sx, sd: (sy, sz, 1 - sx, sd)) for q in near_q]
    partial = fisher_dot(near_q, [column(p, x) + y for p in planes], inverse_fisher)
    partial = fisher_dot(far_q, [column(p, 1 - x) + y for p in planes], inverse_fisher, partial)

    grads.append(move(slab(1 - x, y), lambda sy, sz, sx, sd: (sy, sz, 1 - sx, sd)))
    grads.append(move(slab(1 - x, 1 - y), lambda sy, sz, sx, sd: (1 - sy, sz, 1 - sx, sd)))

    def to_owner(sy, sz, sx, sd):
        su = sz if sd == 0 else nz - 1 - sz
        return None if su < near else (sy, sz, sx, 1 - sd)

    def across_y(sy, sz, sx, sd):
        su = sz if sd == 0 else nz - 1 - sz
        return (1 - sy, sz, sx, sd) if su < near else None

    partial = partial + move(partial, to_owner)
    theirs = lax.dynamic_slice_in_dim(partial, (1 - y) * half, half, axis=1)
    ours = lax.dynamic_slice_in_dim(partial, y * half, half, axis=1)
    panel = (ours + move(theirs, across_y)).astype(jnp.bfloat16)

    panels = gather_z(panel)
    panels = jnp.concatenate(panels, axis=1)
    scores = [lax.dot_general(panels, g, NT, preferred_element_type=jnp.float32) for g in grads]

    rows = nq // 2
    stacked = jnp.stack(scores)
    keep = lax.dynamic_slice_in_dim(stacked, d * rows, rows, axis=1)
    give = lax.dynamic_slice_in_dim(stacked, (1 - d) * rows, rows, axis=1)
    mine = keep + move(give, lambda sy, sz, sx, sd: (sy, sz, sx, 1 - sd))
    return (
        mine[0]
        + move(mine[1], lambda sy, sz, sx, sd: (1 - sy, sz, sx, sd))
        + move(mine[2], lambda sy, sz, sx, sd: (sy, sz, 1 - sx, sd))
        + move(mine[3], lambda sy, sz, sx, sd: (1 - sy, sz, 1 - sx, sd))
    )


def solution(mesh):
    coords = [getattr(device, "coords", None) for device in mesh.devices.flat]
    nx = 2 if None in coords else len({c[0] for c in coords})
    nz = mesh.shape["ex"] // nx
    ny = mesh.shape["grp"]
    if (nz, nx, ny) == (4, 2, 2):
        body = functools.partial(per_device_quad, nz, nx, ny)
    else:
        body = per_device_any
    return jax.shard_map(
        body,
        mesh=mesh,
        in_specs=(P(None, "ex"), P("ex", "dim"), P(("grp", "ex"), "dim")),
        out_specs=P("dim", ("grp", "ex")),
        check_vma=False,
    )
```

time: 164 us -> 81.6 us (0.50)
  waiting for transfers between devices: 128 us -> 25.2 us
  starting transfers between devices: 0.09 us -> 33.5 us
  matrix products: 20.7 us -> 4.33 us
  between operations: 13.1 us -> 0.38 us
  Pallas kernels: 0 us -> 12.5 us
  local copies, waits for them, and re-layouts: 0.01 us -> 1.92 us
    reduce_scatter x2 -> x0, waiting for transfers between devices: 84.1 us -> none  [the longest x1 77.7 us: per_device(): lax.psum_scatter(term_block, 'ex', scatter_dimension=1, tiled=True)]
    all_gather x1 -> x0, waiting for transfers between devices: 44.1 us -> none  [per_device(): lax.all_gather(own_panel, 'ex', axis=1, tiled=True)]
    ppermute x0 -> x17, starting transfers between devices: none -> 33.5 us  [move(): return lax.ppermute(value, AXES, pairs)]
    ppermute x0 -> x17, waiting for transfers between devices: none -> 25.2 us  [move(): return lax.ppermute(value, AXES, pairs)]
    dot_general x2 -> x4, matrix products: 20.7 us -> 4.33 us  [per_device_quad(): lax.dot_general(panels, g, NT, preferred_element_type=jnp.float32)]
    pallas_call x0 -> x2, Pallas kernels: none -> 12.5 us  [fisher_dot(): pl.pallas_call(functools.partial(fisher_kernel, n, base is not None), out...]
    dynamic_slice x0 -> x4, local copies, waits for them, and re-layouts: none -> 1.91 us  [the longest x1 0.94 us: per_device_quad(): own = lax.dynamic_slice_in_dim(queries, y * half, half, axis=1)]
    add x0 -> x3, other arithmetic: none -> 1.85 us  [the longest x1 1.22 us: per_device_quad(): partial = partial + move(partial, to_owner)]
  transfers between devices with their start and end apart: 3 -> 17, of which waited for: 3 -> 10; matrix products, arithmetic and copies ran while one was open for 0% -> 6% of each run, Pallas kernels for 0% -> 8%
where the time goes in v1:
time: 81.6 us; the launch traced here: 81 us
  starting transfers between devices  33.5 us (41%)
  waiting for transfers between devices  25.2 us (31%)
  Pallas kernels  12.5 us (15%)
  matrix products  4.33 us (5%)
  other arithmetic  3.13 us (4%)
  local copies, waits for them, and re-layouts  1.92 us (2%)
    ppermute x17, starting transfers between devices, move(): return lax.ppermute(value, AXES, pairs)  33.5 us
    ppermute x17, waiting for transfers between devices, move(): return lax.ppermute(value, AXES, pairs)  25.2 us
    pallas_call x2, Pallas kernels, fisher_dot(): pl.pallas_call(functools.partial(fisher_kernel, n, base is not None), out...  12.5 us
    dot_general x4, matrix products, per_device_quad(): lax.dot_general(panels, g, NT, preferred_element_type=jnp.float32)  4.33 us
  transfers between devices with their start and end apart: 17, of which 10 were waited for; matrix products, arithmetic and copies ran while one was open for 6% of the time, Pallas kernels for 8%

profile of v1, /device:TPU:0, one launch (start us, length us, event | category | flops | bytes accessed | tf_op | source)
XLA Modules:
  0.0 81.0 jit_solution(2653079735310008713)
XLA Ops:
  0.0 0.9 %constant_dynamic-slice_fusion.10 = bf16[96,1024]{1,0:T(8,128)(2,1)S(1)} fusion(bf16[96,2048]{1,0:T(8,128)(2,1)} %param.3, s32[]{:T(128)S(6)} %select_n.90), kind=kLoop, calls=%fused_computation.35 | loop fusion | bytes 393220 | tf_op jit(solution)/shard_map/dynamic_slice | solution.py:128
  0.9 4.9 %collective-permute-start.2 = (bf16[96,1024]{1,0:T(8,128)(2,1)S(1)}, bf16[96,1024]{1,0:T(8,128)(2,1)S(1)}, u32[]{:S(2)}, u32[]{:S(2)}) collective-permute-start(bf16[96,1024]{1,0:T(8,128)(2,1)S(1)} %constant_dynamic-slice_fusion.10), channel_id=1, source_target_pairs={{0,4},{2,6},{4,0},{6,2},{9,13},{11,15},{13,9},{15,11},{16,20},{18,... | collective-permute-start | bytes 589832 | tf_op jit(solution)/shard_map/ppermute | solution.py:89
  5.9 2.7 %collective-permute-start.3 = (bf16[96,1024]{1,0:T(8,128)(2,1)S(1)}, bf16[96,1024]{1,0:T(8,128)(2,1)S(1)}, u32[]{:S(2)}, u32[]{:S(2)}) collective-permute-start(bf16[96,1024]{1,0:T(8,128)(2,1)S(1)} %constant_dynamic-slice_fusion.10), channel_id=1, source_target_pairs={{0,12},{2,14},{4,8},{6,10},{9,5},{11,7},{13,1},{15,3},{16,28},{18,... | collective-permute-start | bytes 589832 | tf_op jit(solution)/shard_map/ppermute | solution.py:89
  8.6 1.3 %collective-permute-start = (bf16[96,1024]{1,0:T(8,128)(2,1)S(1)}, bf16[96,1024]{1,0:T(8,128)(2,1)S(1)}, u32[]{:S(2)}, u32[]{:S(2)}) collective-permute-start(bf16[96,1024]{1,0:T(8,128)(2,1)S(1)} %constant_dynamic-slice_fusion.10), channel_id=1, source_target_pairs={{0,8},{2,10},{4,12},{6,14},{9,1},{11,3},{13,5},{15,7},{16,24},{18,... | collective-permute-start | bytes 589832 | tf_op jit(solution)/shard_map/ppermute | solution.py:89
  9.9 1.9 %collective-permute-done.3 = bf16[96,1024]{1,0:T(8,128)(2,1)S(1)} collective-permute-done((bf16[96,1024]{1,0:T(8,128)(2,1)S(1)}, bf16[96,1024]{1,0:T(8,128)(2,1)S(1)}, u32[]{:S(2)}, u32[]{:S(2)}) %collective-permute-start.3) | collective-permute-done | bytes 196640 | tf_op jit(solution)/shard_map/ppermute | solution.py:89
  11.8 1.6 %collective-permute-start.4 = (bf16[96,1024]{1,0:T(8,128)(2,1)S(1)}, bf16[96,1024]{1,0:T(8,128)(2,1)S(1)}, u32[]{:S(2)}, u32[]{:S(2)}) collective-permute-start(bf16[96,1024]{1,0:T(8,128)(2,1)S(1)} %broadcast_select_fusion.2.refs_1_), channel_id=1, source_target_pairs={{0,2},{1,3},{2,0},{3,1},{4,6},{5,7},{6,4},{7,5},{8,10},{9,11},{10,... | collective-permute-start | bytes 589832 | tf_op jit(solution)/shard_map/ppermute | solution.py:89
  13.9 1.0 %broadcast_select_fusion.3.refs_0_ = bf16[96,1024]{1,0:T(8,128)(2,1)S(1)} fusion(bf16[96,1024]{1,0:T(8,128)(2,1)S(1)} %collective-permute-done, pred[]{:T(512)S(6)} %lt.52, bf16[96,2048]{1,0:T(8,128)(2,1)} %param.3, s32[]{:T(128)S(6)} %select_n.90), kind=kLoop, calls=%fused_computation.16 | loop fusion | flops 98304 | bytes 589829 | tf_op jit(solution)/shard_map/jit(_where)/select_n | solution.py:105
  14.9 1.6 %collective-permute-start.1 = (bf16[96,1024]{1,0:T(8,128)(2,1)S(1)}, bf16[96,1024]{1,0:T(8,128)(2,1)S(1)}, u32[]{:S(2)}, u32[]{:S(2)}) collective-permute-start(bf16[96,1024]{1,0:T(8,128)(2,1)S(1)} %broadcast_select_fusion.3.refs_0_), channel_id=1, source_target_pairs={{0,2},{1,3},{2,0},{3,1},{4,6},{5,7},{6,4},{7,5},{8,10},{9,11},{10,... | collective-permute-start | bytes 589832 | tf_op jit(solution)/shard_map/ppermute | solution.py:89
  16.5 6.2 %shard_map.37.refs_4_ = f32[96,2048]{1,0:T(8,128)S(1)} custom-call(s32[2]{0:T(128)S(1)} %get-tuple-element.17.cols_ref, bf16[96,1024]{1,0:T(8,128)(2,1)S(1)} %broadcast_select_fusion.3.refs_0_, bf16[96,1024]{1,0:T(8,128)(2,1)S(1)} %broadcast_select_fusion.2.refs_1_, bf16[2048,8192]{1,0:T(8,128)(2,1)} %refs_3_.3, bf16[2048,8192]{1,0:T(8,128)(2,1)} %refs_3_.3), custom_call_target="tpu_custom_call" | custom-call | flops 805306368 | bytes 8388608 | tf_op jit(solution)/shard_map/pallas_call | solution.py:50
  22.8 6.3 %shard_map.38 = f32[96,2048]{1,0:T(8,128)S(1)} custom-call(s32[2]{0:T(128)S(1)} %get-tuple-element.16.cols_ref, bf16[96,1024]{1,0:T(8,128)(2,1)S(1)} %collective-permute-done.1.refs_0_, bf16[96,1024]{1,0:T(8,128)(2,1)S(1)} %collective-permute-done.4.refs_1_, bf16[2048,8192]{1,0:T(8,128)(2,1)} %refs_3_.3, bf16[2048,8192]{1,0:T(8,128)(2,1)} %refs_3_.3, ...), custom_call_target="tpu_custom_call" | custom-call | flops 805306368 | bytes 8388608 | tf_op jit(solution)/shard_map/pallas_call | solution.py:50
  29.1 1.3 %collective-permute-start.5 = (f32[96,2048]{1,0:T(8,128)S(1)}, f32[96,2048]{1,0:T(8,128)}, u32[]{:S(2)}, u32[]{:S(2)}) collective-permute-start(f32[96,2048]{1,0:T(8,128)S(1)} %shard_map.38), channel_id=1, source_target_pairs={{1,0},{3,2},{5,4},{7,6},{8,9},{10,11},{12,13},{14,15},{17,16},{19,... | collective-permute-start | bytes 2359304 | tf_op jit(solution)/shard_map/ppermute | solution.py:89
  30.5 0.9 %constant_dynamic-slice_fusion.8 = (bf16[128,1024]{1,0:T(8,128)(2,1)S(1)}, bf16[128,1024]{1,0:T(8,128)(2,1)S(1)}, bf16[128,1024]{1,0:T(8,128)(2,1)S(1)}, bf16[12...) fusion(bf16[128,8192]{1,0:T(8,128)(2,1)S(1)} %copy-done, ...), kind=kLoop, calls=%fused_computation.33 | loop fusion | bytes 4194336 | tf_op jit(solution)/shard_map/dynamic_slice | solution.py:119
  31.4 5.1 %collective-permute-done.5 = f32[96,2048]{1,0:T(8,128)} collective-permute-done((f32[96,2048]{1,0:T(8,128)S(1)}, f32[96,2048]{1,0:T(8,128)}, u32[]{:S(2)}, u32[]{:S(2)}) %collective-permute-start.5) | collective-permute-done | bytes 786464 | tf_op jit(solution)/shard_map/ppermute | solution.py:89
  36.5 1.2 %add.123 = f32[96,2048]{1,0:T(8,128)S(1)} add(f32[96,2048]{1,0:T(8,128)S(1)} %shard_map.38, f32[96,2048]{1,0:T(8,128)} %collective-permute-done.5) | non-fusion elementwise | flops 196608 | bytes 2359296 | tf_op jit(solution)/shard_map/add | solution.py:145
  37.7 3.4 %collective-permute-start.6 = (f32[96,1024]{1,0:T(8,128)S(1)}, f32[96,1024]{1,0:T(8,128)S(1)}, u32[]{:S(2)}, u32[]{:S(2)}) collective-permute-start(f32[96,1024]{1,0:T(8,128)S(1)} %constant_dynamic-slice_fusion.9), channel_id=1, source_target_pairs={{0,16},{2,18},{4,20},{6,22},{9,25},{11,27},{13,29},{15,31},{16,0},... | collective-permute-start | bytes 1179656 | tf_op jit(solution)/shard_map/ppermute | solution.py:89
  41.2 0.6 collective-permute-start.10
  41.8 0.6 collective-permute-start.11
  42.4 9.9 %collective-permute-done.6 = f32[96,1024]{1,0:T(8,128)S(1)} collective-permute-done((f32[96,1024]{1,0:T(8,128)S(1)}, f32[96,1024]{1,0:T(8,128)S(1)}, u32[]{:S(2)}, u32[]{:S(2)}) %collective-permute-start.6) | collective-permute-done | bytes 393248 | tf_op jit(solution)/shard_map/ppermute | solution.py:89
  52.4 1.3 %collective-permute-start.7 = (bf16[96,1024]{1,0:T(8,128)(2,1)S(1)}, bf16[96,1024]{1,0:T(8,128)(2,1)S(1)}, u32[]{:S(2)}, u32[]{:S(2)}) collective-permute-start(bf16[96,1024]{1,0:T(8,128)(2,1)S(1)} %add_convert_fusion), channel_id=1, source_target_pairs={{0,8},{2,10},{4,12},{6,14},{9,1},{11,3},{13,5},{15,7},{16,24},{18,... | collective-permute-start | bytes 589832 | tf_op jit(solution)/shard_map/ppermute | solution.py:89
  53.7 0.5 collective-permute-start.12
  54.3 3.2 %collective-permute-start.8 = (bf16[96,1024]{1,0:T(8,128)(2,1)S(1)}, bf16[96,1024]{1,0:T(8,128)(2,1)S(1)}, u32[]{:S(2)}, u32[]{:S(2)}) collective-permute-start(bf16[96,1024]{1,0:T(8,128)(2,1)S(1)} %add_convert_fusion), channel_id=1, source_target_pairs={{0,4},{2,6},{4,0},{6,2},{9,13},{11,15},{13,9},{15,11},{16,20},{18,... | collective-permute-start | bytes 589832 | tf_op jit(solution)/shard_map/ppermute | solution.py:89
  57.5 7.0 %collective-permute-start.9 = (bf16[96,1024]{1,0:T(8,128)(2,1)S(1)}, bf16[96,1024]{1,0:T(8,128)(2,1)S(1)}, u32[]{:S(2)}, u32[]{:S(2)}) collective-permute-start(bf16[96,1024]{1,0:T(8,128)(2,1)S(1)} %add_convert_fusion), channel_id=1, source_target_pairs={{0,12},{2,14},{4,8},{6,10},{9,5},{11,7},{13,1},{15,3},{16,28},{18,... | collective-permute-start | bytes 589832 | tf_op jit(solution)/shard_map/ppermute | solution.py:89
  64.5 3.1 %collective-permute-done.9 = bf16[96,1024]{1,0:T(8,128)(2,1)S(1)} collective-permute-done((bf16[96,1024]{1,0:T(8,128)(2,1)S(1)}, bf16[96,1024]{1,0:T(8,128)(2,1)S(1)}, u32[]{:S(2)}, u32[]{:S(2)}) %collective-permute-start.9) | collective-permute-done | bytes 196640 | tf_op jit(solution)/shard_map/ppermute | solution.py:89
  68.1 1.3 %convolution_bitcast_fusion.2 = f32[1,96,128]{2,1,0:T(8,128)S(1)} fusion(bf16[128,2048]{1,0:T(8,128)(2,1)} %collective-permute-done.10, bf16[96,1024]{1,0:T(8,128)(2,1)S(1)} %broadcast_select_fusion, bf16[96,1024]{1,0:T(8,128)(2,1)S(1)} %broadcast_select_fusion.1), kind=kOutput, calls=%fused_computation.2 | convolution fusion | flops 51118080 | bytes 966656 | tf_op jit(solution)/shard_map/dot_general | solution.py:152
  69.4 1.3 %convolution_bitcast_fusion.1 = f32[1,96,128]{2,1,0:T(8,128)S(1)} fusion(bf16[128,2048]{1,0:T(8,128)(2,1)} %collective-permute-done.11, bf16[96,1024]{1,0:T(8,128)(2,1)S(1)} %broadcast_select_fusion, bf16[96,1024]{1,0:T(8,128)(2,1)S(1)} %broadcast_select_fusion.1), kind=kOutput, calls=%fused_computation.1 | convolution fusion | flops 51118080 | bytes 966656 | tf_op jit(solution)/shard_map/dot_general | solution.py:152
  70.8 1.3 %convolution_bitcast_fusion = f32[1,96,128]{2,1,0:T(8,128)S(1)} fusion(bf16[128,2048]{1,0:T(8,128)(2,1)} %collective-permute-done.12, bf16[96,1024]{1,0:T(8,128)(2,1)S(1)} %broadcast_select_fusion, bf16[96,1024]{1,0:T(8,128)(2,1)S(1)} %broadcast_select_fusion.1), kind=kOutput, calls=%fused_computation | convolution fusion | flops 51118080 | bytes 966656 | tf_op jit(solution)/shard_map/dot_general | solution.py:152
  72.2 1.3 %collective-permute-done.13 = f32[4,48,128]{2,1,0:T(8,128)S(1)} collective-permute-done((f32[4,48,128]{2,1,0:T(8,128)S(1)}, f32[4,48,128]{2,1,0:T(8,128)S(1)}, u32[]{:S(2)}, u32[]{:S(2)}) %collective-permute-start.13) | collective-permute-done | bytes 98336 | tf_op jit(solution)/shard_map/ppermute | solution.py:89
  73.6 1.6 %collective-permute-start.14 = (f32[48,128]{1,0:T(8,128)S(1)}, f32[48,128]{1,0:T(8,128)S(1)}, u32[]{:S(2)}, u32[]{:S(2)}) collective-permute-start(f32[48,128]{1,0:T(8,128)S(1)} %get-tuple-element.13), channel_id=1, source_target_pairs={{0,16},{1,17},{2,18},{3,19},{4,20},{5,21},{6,22},{7,23},{8,24},{9,... | collective-permute-start | bytes 73736 | tf_op jit(solution)/shard_map/ppermute | solution.py:89
  75.7 1.4 %collective-permute-start.16 = (f32[48,128]{1,0:T(8,128)S(1)}, f32[48,128]{1,0:T(8,128)S(1)}, u32[]{:S(2)}, u32[]{:S(2)}) collective-permute-start(f32[48,128]{1,0:T(8,128)S(1)} %get-tuple-element.14), channel_id=1, source_target_pairs={{0,18},{1,19},{2,16},{3,17},{4,22},{5,23},{6,20},{7,21},{8,26},{9,... | collective-permute-start | bytes 73736 | tf_op jit(solution)/shard_map/ppermute | solution.py:89
  77.5 1.5 %collective-permute-done.15 = f32[48,128]{1,0:T(8,128)S(1)} collective-permute-done((f32[48,128]{1,0:T(8,128)S(1)}, f32[48,128]{1,0:T(8,128)S(1)}, u32[]{:S(2)}, u32[]{:S(2)}) %collective-permute-start.15) | collective-permute-done | bytes 24608 | tf_op jit(solution)/shard_map/ppermute | solution.py:89
  79.0 1.4 %collective-permute-done.16 = f32[48,128]{1,0:T(8,128)S(1)} collective-permute-done((f32[48,128]{1,0:T(8,128)S(1)}, f32[48,128]{1,0:T(8,128)S(1)}, u32[]{:S(2)}, u32[]{:S(2)}) %collective-permute-start.16) | collective-permute-done | bytes 24608 | tf_op jit(solution)/shard_map/ppermute | solution.py:89
  80.4 0.6 fusion.5
  (30 shorter events, 2.3 us)
Async XLA Ops:
  0.9 9.0 %collective-permute-start.2 = (bf16[96,1024]{1,0:T(8,128)(2,1)S(1)}, bf16[96,1024]{1,0:T(8,128)(2,1)S(1)}, u32[]{:S(2)}, u32[]{:S(2)}) collective-permute-start(bf16[96,1024]{1,0:T(8,128)(2,1)S(1)} %constant_dynamic-slice_fusion.10), channel_id=1, source_target_pairs={{0,4},{2,6},{4,0},{6,2},{9,13},{11,15},{13,9},{15,11},{16,20},{18,... | collective-permute-start | bytes 589832 | tf_op jit(solution)/shard_map/ppermute | solution.py:89
  5.9 5.9 %collective-permute-start.3 = (bf16[96,1024]{1,0:T(8,128)(2,1)S(1)}, bf16[96,1024]{1,0:T(8,128)(2,1)S(1)}, u32[]{:S(2)}, u32[]{:S(2)}) collective-permute-start(bf16[96,1024]{1,0:T(8,128)(2,1)S(1)} %constant_dynamic-slice_fusion.10), channel_id=1, source_target_pairs={{0,12},{2,14},{4,8},{6,10},{9,5},{11,7},{13,1},{15,3},{16,28},{18,... | collective-permute-start | bytes 589832 | tf_op jit(solution)/shard_map/ppermute | solution.py:89
  8.6 5.3 %collective-permute-start = (bf16[96,1024]{1,0:T(8,128)(2,1)S(1)}, bf16[96,1024]{1,0:T(8,128)(2,1)S(1)}, u32[]{:S(2)}, u32[]{:S(2)}) collective-permute-start(bf16[96,1024]{1,0:T(8,128)(2,1)S(1)} %constant_dynamic-slice_fusion.10), channel_id=1, source_target_pairs={{0,8},{2,10},{4,12},{6,14},{9,1},{11,3},{13,5},{15,7},{16,24},{18,... | collective-permute-start | bytes 589832 | tf_op jit(solution)/shard_map/ppermute | solution.py:89
  11.8 10.9 %collective-permute-start.4 = (bf16[96,1024]{1,0:T(8,128)(2,1)S(1)}, bf16[96,1024]{1,0:T(8,128)(2,1)S(1)}, u32[]{:S(2)}, u32[]{:S(2)}) collective-permute-start(bf16[96,1024]{1,0:T(8,128)(2,1)S(1)} %broadcast_select_fusion.2.refs_1_), channel_id=1, source_target_pairs={{0,2},{1,3},{2,0},{3,1},{4,6},{5,7},{6,4},{7,5},{8,10},{9,11},{10,... | collective-permute-start | bytes 589832 | tf_op jit(solution)/shard_map/ppermute | solution.py:89
  14.9 7.9 %collective-permute-start.1 = (bf16[96,1024]{1,0:T(8,128)(2,1)S(1)}, bf16[96,1024]{1,0:T(8,128)(2,1)S(1)}, u32[]{:S(2)}, u32[]{:S(2)}) collective-permute-start(bf16[96,1024]{1,0:T(8,128)(2,1)S(1)} %broadcast_select_fusion.3.refs_0_), channel_id=1, source_target_pairs={{0,2},{1,3},{2,0},{3,1},{4,6},{5,7},{6,4},{7,5},{8,10},{9,11},{10,... | collective-permute-start | bytes 589832 | tf_op jit(solution)/shard_map/ppermute | solution.py:89
  22.7 7.7 %copy-start = (bf16[128,8192]{1,0:T(8,128)(2,1)S(1)}, bf16[128,8192]{1,0:T(8,128)(2,1)}, u32[]{:S(2)}) copy-start(bf16[128,8192]{1,0:T(8,128)(2,1)} %param.5) | copy-start | bytes 6291460
  29.1 7.4 %collective-permute-start.5 = (f32[96,2048]{1,0:T(8,128)S(1)}, f32[96,2048]{1,0:T(8,128)}, u32[]{:S(2)}, u32[]{:S(2)}) collective-permute-start(f32[96,2048]{1,0:T(8,128)S(1)} %shard_map.38), channel_id=1, source_target_pairs={{1,0},{3,2},{5,4},{7,6},{8,9},{10,11},{12,13},{14,15},{17,16},{19,... | collective-permute-start | bytes 2359304 | tf_op jit(solution)/shard_map/ppermute | solution.py:89
  37.7 14.6 %collective-permute-start.6 = (f32[96,1024]{1,0:T(8,128)S(1)}, f32[96,1024]{1,0:T(8,128)S(1)}, u32[]{:S(2)}, u32[]{:S(2)}) collective-permute-start(f32[96,1024]{1,0:T(8,128)S(1)} %constant_dynamic-slice_fusion.9), channel_id=1, source_target_pairs={{0,16},{2,18},{4,20},{6,22},{9,25},{11,27},{13,29},{15,31},{16,0},... | collective-permute-start | bytes 1179656 | tf_op jit(solution)/shard_map/ppermute | solution.py:89
  41.2 26.8 %collective-permute-start.10 = (bf16[128,2048]{1,0:T(8,128)(2,1)S(1)}, bf16[128,2048]{1,0:T(8,128)(2,1)}, u32[]{:S(2)}, u32[]{:S(2)}) collective-permute-start(bf16[128,2048]{1,0:T(8,128)(2,1)S(1)} %pad_maximum_fusion), channel_id=1, source_target_pairs={{0,16},{1,17},{2,18},{3,19},{4,20},{5,21},{6,22},{7,23},{8,24},{9,... | collective-permute-start | bytes 1572872 | tf_op jit(solution)/shard_map/ppermute | solution.py:89
  41.8 25.8 %copy-start.1 = (bf16[128,1024]{1,0:T(8,128)(2,1)S(1)}, bf16[128,1024]{1,0:T(8,128)(2,1)}, u32[]{:S(2)}) copy-start(bf16[128,1024]{1,0:T(8,128)(2,1)} %get-tuple-element.10) | copy-start | bytes 786436
  41.8 27.6 %collective-permute-start.11 = (bf16[128,2048]{1,0:T(8,128)(2,1)S(1)}, bf16[128,2048]{1,0:T(8,128)(2,1)}, u32[]{:S(2)}, u32[]{:S(2)}) collective-permute-start(bf16[128,2048]{1,0:T(8,128)(2,1)S(1)} %pad_maximum_fusion.1), channel_id=1, source_target_pairs={{0,2},{1,3},{2,0},{3,1},{4,6},{5,7},{6,4},{7,5},{8,10},{9,11},{10,... | collective-permute-start | bytes 1572872 | tf_op jit(solution)/shard_map/ppermute | solution.py:89
  52.4 5.1 %collective-permute-start.7 = (bf16[96,1024]{1,0:T(8,128)(2,1)S(1)}, bf16[96,1024]{1,0:T(8,128)(2,1)S(1)}, u32[]{:S(2)}, u32[]{:S(2)}) collective-permute-start(bf16[96,1024]{1,0:T(8,128)(2,1)S(1)} %add_convert_fusion), channel_id=1, source_target_pairs={{0,8},{2,10},{4,12},{6,14},{9,1},{11,3},{13,5},{15,7},{16,24},{18,... | collective-permute-start | bytes 589832 | tf_op jit(solution)/shard_map/ppermute | solution.py:89
  53.7 17.0 %collective-permute-start.12 = (bf16[128,2048]{1,0:T(8,128)(2,1)S(1)}, bf16[128,2048]{1,0:T(8,128)(2,1)}, u32[]{:S(2)}, u32[]{:S(2)}) collective-permute-start(bf16[128,2048]{1,0:T(8,128)(2,1)S(1)} %pad_maximum_fusion.2), channel_id=1, source_target_pairs={{0,18},{1,19},{2,16},{3,17},{4,22},{5,23},{6,20},{7,21},{8,26},{9,... | collective-permute-start | bytes 1572872 | tf_op jit(solution)/shard_map/ppermute | solution.py:89
  54.3 10.2 %collective-permute-start.8 = (bf16[96,1024]{1,0:T(8,128)(2,1)S(1)}, bf16[96,1024]{1,0:T(8,128)(2,1)S(1)}, u32[]{:S(2)}, u32[]{:S(2)}) collective-permute-start(bf16[96,1024]{1,0:T(8,128)(2,1)S(1)} %add_convert_fusion), channel_id=1, source_target_pairs={{0,4},{2,6},{4,0},{6,2},{9,13},{11,15},{13,9},{15,11},{16,20},{18,... | collective-permute-start | bytes 589832 | tf_op jit(solution)/shard_map/ppermute | solution.py:89
  57.5 10.1 %collective-permute-start.9 = (bf16[96,1024]{1,0:T(8,128)(2,1)S(1)}, bf16[96,1024]{1,0:T(8,128)(2,1)S(1)}, u32[]{:S(2)}, u32[]{:S(2)}) collective-permute-start(bf16[96,1024]{1,0:T(8,128)(2,1)S(1)} %add_convert_fusion), channel_id=1, source_target_pairs={{0,12},{2,14},{4,8},{6,10},{9,5},{11,7},{13,1},{15,3},{16,28},{18,... | collective-permute-start | bytes 589832 | tf_op jit(solution)/shard_map/ppermute | solution.py:89
  72.2 1.4 %collective-permute-start.13 = (f32[4,48,128]{2,1,0:T(8,128)S(1)}, f32[4,48,128]{2,1,0:T(8,128)S(1)}, u32[]{:S(2)}, u32[]{:S(2)}) collective-permute-start(f32[4,48,128]{2,1,0:T(8,128)S(1)} %constant_dynamic-slice_fusion), channel_id=1, source_target_pairs={{0,1},{1,0},{2,3},{3,2},{4,5},{5,4},{6,7},{7,6},{8,9},{9,8},{10,11... | collective-permute-start | bytes 294920 | tf_op jit(solution)/shard_map/ppermute | solution.py:89
  73.6 3.9 %collective-permute-start.14 = (f32[48,128]{1,0:T(8,128)S(1)}, f32[48,128]{1,0:T(8,128)S(1)}, u32[]{:S(2)}, u32[]{:S(2)}) collective-permute-start(f32[48,128]{1,0:T(8,128)S(1)} %get-tuple-element.13), channel_id=1, source_target_pairs={{0,16},{1,17},{2,18},{3,19},{4,20},{5,21},{6,22},{7,23},{8,24},{9,... | collective-permute-start | bytes 73736 | tf_op jit(solution)/shard_map/ppermute | solution.py:89
  75.2 3.8 %collective-permute-start.15 = (f32[48,128]{1,0:T(8,128)S(1)}, f32[48,128]{1,0:T(8,128)S(1)}, u32[]{:S(2)}, u32[]{:S(2)}) collective-permute-start(f32[48,128]{1,0:T(8,128)S(1)} %get-tuple-element.15), channel_id=1, source_target_pairs={{0,2},{1,3},{2,0},{3,1},{4,6},{5,7},{6,4},{7,5},{8,10},{9,11},{10,... | collective-permute-start | bytes 73736 | tf_op jit(solution)/shard_map/ppermute | solution.py:89
  75.7 4.7 %collective-permute-start.16 = (f32[48,128]{1,0:T(8,128)S(1)}, f32[48,128]{1,0:T(8,128)S(1)}, u32[]{:S(2)}, u32[]{:S(2)}) collective-permute-start(f32[48,128]{1,0:T(8,128)S(1)} %get-tuple-element.14), channel_id=1, source_target_pairs={{0,18},{1,19},{2,16},{3,17},{4,22},{5,23},{6,20},{7,21},{8,26},{9,... | collective-permute-start | bytes 73736 | tf_op jit(solution)/shard_map/ppermute | solution.py:89

commit v2 on v1

v2 whole, which is shorter than its diff:
```python
import functools

import jax
import jax.numpy as jnp
from jax import lax
from jax.experimental import pallas as pl
from jax.experimental.pallas import tpu as pltpu
from jax.sharding import PartitionSpec as P

AXES = ("grp", "ex", "dim")
NT = (((1,), (1,)), ((), ()))
VMEM = pl.BlockSpec(memory_space=pltpu.VMEM)


def per_device_any(queries, inverse_fisher, stored_grads):
    term_block = jnp.dot(queries, inverse_fisher, preferred_element_type=jnp.float32)
    own_panel = lax.psum_scatter(term_block, "ex", scatter_dimension=1, tiled=True).astype(
        jnp.bfloat16
    )
    partial_scores = lax.dot_general(
        lax.all_gather(own_panel, "ex", axis=1, tiled=True),
        stored_grads,
        NT,
        preferred_element_type=jnp.float32,
    )
    return lax.psum_scatter(partial_scores, "dim", scatter_dimension=0, tiled=True)


def fisher_kernel(n, has_base, index_ref, *refs):
    del index_ref
    out_ref = refs[-1]
    acc = None
    for i in range(n):
        term = lax.dot_general(refs[n + i][...], refs[i][...], NT, preferred_element_type=jnp.float32)
        acc = term if acc is None else acc + term
    acc = acc.T
    if has_base:
        acc = acc + refs[2 * n][0]
    out_ref[...] = acc.reshape(out_ref.shape)


def cut_kernel(at, at_ref, src_ref, *refs):
    outs, sem = refs[:-1], refs[-1]
    copies = []
    for out_ref, pieces in zip(outs, at):
        width = out_ref.shape[1] // len(pieces)
        for p, i in enumerate(pieces):
            start = pl.multiple_of(at_ref[i] * width, width)
            copies.append(
                pltpu.make_async_copy(
                    src_ref.at[:, pl.ds(start, width)],
                    out_ref.at[:, p * width : (p + 1) * width],
                    sem.at[len(copies)],
                )
            )
            copies[-1].start()
    for copy in copies:
        copy.wait()


def cut(src, width, starts):
    flat = [s for pieces in starts for s in pieces]
    at, i = [], 0
    for pieces in starts:
        at.append(list(range(i, i + len(pieces))))
        i += len(pieces)
    return pl.pallas_call(
        functools.partial(cut_kernel, at),
        out_shape=[jax.ShapeDtypeStruct((src.shape[0], width * len(p)), src.dtype) for p in starts],
        in_specs=[pl.BlockSpec(memory_space=pltpu.SMEM), pl.BlockSpec(memory_space=pltpu.HBM)],
        out_specs=[VMEM] * len(starts),
        scratch_shapes=[pltpu.SemaphoreType.DMA((len(flat),))],
        cost_estimate=pl.CostEstimate(
            flops=0, bytes_accessed=4 * src.shape[0] * width * len(flat), transcendentals=0
        ),
    )(jnp.stack(flat).astype(jnp.int32), src)


def panel_kernel(ours_ref, core_ref, y_ref, after_ref, out_ref):
    del after_ref
    out_ref[...] = ((ours_ref[...] + core_ref[...]) + y_ref[...]).astype(out_ref.dtype)


def panel_sum(ours, from_core, from_y, after):
    return pl.pallas_call(
        panel_kernel,
        out_shape=jax.ShapeDtypeStruct(ours.shape, jnp.bfloat16),
        in_specs=[VMEM] * 3 + [pl.BlockSpec(memory_space=pl.ANY)],
        out_specs=VMEM,
    )(ours, from_core, from_y, after)


def fisher_dot(chunks, cols, row_halves, fisher, base=None, base_at=0, after=(), rows=256):
    n, parts = len(chunks), len(row_halves)
    nq, width = chunks[0].shape
    half = fisher.shape[0] // 2
    steps = half // rows
    in_specs = [pl.BlockSpec((nq, width), lambda h, i, s: (0, 0)) for _ in range(n)]
    in_specs += [
        pl.BlockSpec(
            (rows, width), functools.partial(lambda k, h, i, s: (s[n + h] * steps + i, s[k]), k)
        )
        for k in range(n)
    ]
    operands = list(chunks) + [fisher] * n
    if base is not None:
        in_specs.append(pl.BlockSpec((1, nq, rows), lambda h, i, s: (base_at + h, 0, i)))
        operands.append(base)
    in_specs += [pl.BlockSpec(memory_space=pl.ANY)] * len(after)
    operands += after
    if parts == 1:
        out_shape = jax.ShapeDtypeStruct((nq, half), jnp.float32)
        out_spec = pl.BlockSpec((nq, rows), lambda h, i, s: (0, i))
    else:
        out_shape = jax.ShapeDtypeStruct((parts, nq, half), jnp.float32)
        out_spec = pl.BlockSpec((1, nq, rows), lambda h, i, s: (h, 0, i))
    return pl.pallas_call(
        functools.partial(fisher_kernel, n, base is not None),
        out_shape=out_shape,
        grid_spec=pltpu.PrefetchScalarGridSpec(
            num_scalar_prefetch=1,
            grid=(parts, steps),
            in_specs=in_specs,
            out_specs=out_spec,
        ),
        compiler_params=pltpu.CompilerParams(vmem_limit_bytes=24 * 1024 * 1024),
        cost_estimate=pl.CostEstimate(
            flops=2 * n * nq * width * half * parts,
            bytes_accessed=n * width * half * parts * 2,
            transcendentals=0,
        ),
    )(jnp.stack(list(cols) + list(row_halves)).astype(jnp.int32), *operands)


def score_kernel(n, at, panel_ref, *refs):
    out_ref = refs[n]
    width = panel_ref.shape[1]
    panel = panel_ref[...]
    for k in range(n):
        piece = refs[k][:, at * width : (at + 1) * width]
        term = lax.dot_general(piece, panel, NT, preferred_element_type=jnp.float32)
        out_ref[k] = term.T


def score_end_kernel(n, at, d_ref, panel_ref, *refs):
    base_ref, keep_ref, give_ref, total_ref = refs[n : n + 4]
    width = panel_ref.shape[1]
    rows = keep_ref.shape[1]
    panel = panel_ref[...]
    for k in range(n):
        piece = refs[k][:, at * width : (at + 1) * width]
        term = lax.dot_general(piece, panel, NT, preferred_element_type=jnp.float32)
        total_ref[k] = base_ref[k] + term.T
    d = d_ref[0]
    keep_ref[...] = total_ref[:, pl.ds(pl.multiple_of(d * rows, 8), rows), :]
    give_ref[...] = total_ref[:, pl.ds(pl.multiple_of((1 - d) * rows, 8), rows), :]


def score_dot(panel, slabs):
    n = len(slabs)
    return pl.pallas_call(
        functools.partial(score_kernel, n, 0),
        out_shape=jax.ShapeDtypeStruct((n, panel.shape[0], slabs[0].shape[0]), jnp.float32),
        in_specs=[VMEM] * (n + 1),
        out_specs=VMEM,
        compiler_params=pltpu.CompilerParams(vmem_limit_bytes=24 * 1024 * 1024),
    )(panel, *slabs)


def score_dot_end(panel, slabs, base, d):
    n = len(slabs)
    nq, ne = panel.shape[0], slabs[0].shape[0]
    half = jax.ShapeDtypeStruct((n, nq // 2, ne), jnp.float32)
    return pl.pallas_call(
        functools.partial(score_end_kernel, n, 1),
        out_shape=(half, half),
        in_specs=[pl.BlockSpec(memory_space=pltpu.SMEM)] + [VMEM] * (n + 2),
        out_specs=(VMEM, VMEM),
        scratch_shapes=[pltpu.VMEM((n, nq, ne), jnp.float32)],
        compiler_params=pltpu.CompilerParams(vmem_limit_bytes=24 * 1024 * 1024),
    )(d.reshape(1).astype(jnp.int32), panel, *slabs, base)


def per_device_quad(nz, nx, ny, queries, inverse_fisher, stored_grads):
    nex = nz * nx
    near = nz // 2
    nq, block = queries.shape
    half = block // ny
    y, e, d = (lax.axis_index(a) for a in AXES)
    z = e // nx
    x = e % nx
    u = jnp.where(d == 0, z, nz - 1 - z)
    owner = u < near

    def move(value, target):
        pairs = []
        for sy in range(ny):
            for sz in range(nz):
                for sx in range(nx):
                    for sd in range(2):
                        to = target(sy, sz, sx, sd)
                        if to is not None:
                            ty, tz, tx, td = to
                            pairs.append(((sy * nex + sz * nx + sx) * 2 + sd, (ty * nex + tz * nx + tx) * 2 + td))
        return lax.ppermute(value, AXES, pairs)

    def along_z(value, hops):
        def target(sy, sz, sx, sd):
            su = sz if sd == 0 else nz - 1 - sz
            if su not in hops:
                return None
            tu = hops[su]
            return sy, tu if sd == 0 else nz - 1 - tu, sx, sd

        return move(value, target)

    def swap_x(value):
        return move(value, lambda sy, sz, sx, sd: (sy, sz, 1 - sx, sd))

    def swap_y(value):
        return move(value, lambda sy, sz, sx, sd: (1 - sy, sz, sx, sd))

    def swap_core(value):
        return move(value, lambda sy, sz, sx, sd: (sy, sz, sx, 1 - sd))

    def gather_z(own):
        first = jnp.where(owner, own, along_z(own, {0: 2, 1: 3}))
        return first, along_z(first, {0: 1, 1: 0, 2: 3, 3: 2})

    def real_plane(k):
        return jnp.where(d == 0, k, nz - 1 - k)

    planes = [real_plane(u % 2), real_plane(1 - u % 2)]

    def column(plane, x_, y_):
        return (plane * nx + x_ - d * (nex // 2)) * ny + y_

    def slab(x_, y_):
        return [column(p, x_, y_) for p in planes]

    (own,) = cut(queries, half, [[y]])
    own_slab, to_x, to_y, to_xy = cut(
        stored_grads, half, [slab(x, y), slab(1 - x, y), slab(x, 1 - y), slab(1 - x, 1 - y)]
    )
    pass_on = swap_y(to_xy)
    from_y = swap_y(to_y)
    from_x = swap_x(to_x)
    from_xy = swap_x(pass_on)
    slabs = [own_slab, from_x, from_y, from_xy]

    q0, q1 = gather_z(own)
    q2, q3 = swap_x(q0), swap_x(q1)
    halves = [1 - y, y]
    base = fisher_dot(
        [q0, q1, q2],
        [column(planes[0], x, y), column(planes[1], x, y), column(planes[0], 1 - x, y)],
        halves,
        inverse_fisher,
        after=[pass_on],
    )
    last = [column(planes[1], 1 - x, y)]
    theirs = fisher_dot([q3], last, halves[:1], inverse_fisher, base, 0)
    ours = fisher_dot([q3], last, halves[1:], inverse_fisher, base, 1, [from_y])

    def to_owner(sy, sz, sx, sd):
        su = sz if sd == 0 else nz - 1 - sz
        return None if su < near else (sy, sz, sx, 1 - sd)

    def across_y(sy, sz, sx, sd):
        su = sz if sd == 0 else nz - 1 - sz
        return (1 - sy, sz, sx, sd) if su < near else None

    theirs = move(theirs + move(theirs, to_owner), across_y)
    panel = panel_sum(ours, move(ours, to_owner), theirs, from_x)

    p0, p1 = gather_z(panel)
    keep, give = score_dot_end(p1, slabs, score_dot(p0, slabs), d)

    mine = keep + swap_core(give)
    mine = mine[:2] + swap_y(mine[2:])
    return mine[0] + swap_x(mine[1])


def solution(mesh):
    coords = [getattr(device, "coords", None) for device in mesh.devices.flat]
    nx = 2 if None in coords else len({c[0] for c in coords})
    nz = mesh.shape["ex"] // nx
    ny = mesh.shape["grp"]
    if (nz, nx, ny) == (4, 2, 2):
        body = functools.partial(per_device_quad, nz, nx, ny)
    else:
        body = per_device_any
    return jax.shard_map(
        body,
        mesh=mesh,
        in_specs=(P(None, "ex"), P("ex", "dim"), P(("grp", "ex"), "dim")),
        out_specs=P("dim", ("grp", "ex")),
        check_vma=False,
    )
```

time: 81.6 us -> 88.5 us (1.085)
  Pallas kernels: 12.5 us -> 25.5 us
  matrix products: 4.33 us -> 0 us
  starting transfers between devices: 33.5 us -> 29.6 us
  waiting for transfers between devices: 25.2 us -> 27.2 us
    pallas_call x0 -> x5, Pallas kernels: none -> 8.12 us  [the longest x2 5.18 us: cut(): pl.pallas_call(functools.partial(cut_kernel, at), out_shape=[jax.ShapeDty...]
    pallas_call x2 -> x3, Pallas kernels: 12.5 us -> 17.4 us  [fisher_dot(): pl.pallas_call(functools.partial(fisher_kernel, n, base is not None), out...]
    dot_general x4 -> x0, matrix products: 4.33 us -> none  [per_device_quad(): lax.dot_general(panels, g, NT, preferred_element_type=jnp.float32)]
    ppermute x17 -> x16, starting transfers between devices: 33.5 us -> 29.6 us  [move(): return lax.ppermute(value, AXES, pairs)]
    ppermute x17 -> x16, waiting for transfers between devices: 25.2 us -> 27.2 us  [move(): return lax.ppermute(value, AXES, pairs)]
    dynamic_slice x4 -> x0, local copies, waits for them, and re-layouts: 1.91 us -> none  [the longest x1 0.94 us: per_device_quad(): own = lax.dynamic_slice_in_dim(queries, y * half, half, axis=1)]
    unnamed x4 -> x14, local copies, waits for them, and re-layouts: 0.01 us -> 1.81 us
    add x3 -> x4, other arithmetic: 1.85 us -> 0.69 us  [the longest x1 0.61 us: per_device_quad(): return mine[0] + swap_x(mine[1])]
  transfers between devices with their start and end apart: 17 -> 16, of which waited for: 10 -> 10; matrix products, arithmetic and copies ran while one was open for 6% -> 3% of each run, Pallas kernels for 8% -> 24%
where the time goes in v2:
time: 88.5 us; the launch traced here: 87.8 us
  starting transfers between devices  29.6 us (33%)
  waiting for transfers between devices  27.2 us (31%)
  Pallas kernels  25.5 us (29%)
  other arithmetic  2.74 us (3%)
  local copies, waits for them, and re-layouts  2.52 us (3%)
    ppermute x16, starting transfers between devices, move(): return lax.ppermute(value, AXES, pairs)  29.6 us
    ppermute x16, waiting for transfers between devices, move(): return lax.ppermute(value, AXES, pairs)  27.2 us
    pallas_call x3, Pallas kernels, fisher_dot(): pl.pallas_call(functools.partial(fisher_kernel, n, base is not None), out...  17.4 us
    pallas_call x2, Pallas kernels, cut(): pl.pallas_call(functools.partial(cut_kernel, at), out_shape=[jax.ShapeDty...  5.18 us
    pallas_call x1, Pallas kernels, panel_sum(): pl.pallas_call(panel_kernel, out_shape=jax.ShapeDtypeStruct(ours.shape, j...  1.96 us
    select_n x2, other arithmetic, gather_z(): first = jnp.where(owner, own, along_z(own, {0: 2, 1: 3}))  1.9 us
    unnamed x14, local copies, waits for them, and re-layouts  1.81 us
  transfers between devices with their start and end apart: 16, of which 10 were waited for; matrix products, arithmetic and copies ran while one was open for 3% of the time, Pallas kernels for 24%

profile of v2, /device:TPU:0, one launch (start us, length us, event | category | flops | bytes accessed | tf_op | source)
XLA Modules:
  0.0 87.8 jit_solution(14199608956902583751)
XLA Ops:
  0.0 1.6 %shard_map.37 = bf16[96,1024]{1,0:T(8,128)(2,1)} custom-call(s32[1]{0:T(128)} %bitcast.2.at_ref, bf16[96,2048]{1,0:T(8,128)(2,1)} %src_ref.2), custom_call_target="tpu_custom_call" | custom-call | bytes 393216 | tf_op jit(solution)/shard_map/pallas_call | solution.py:67
  1.6 6.0 %collective-permute-start = (bf16[96,1024]{1,0:T(8,128)(2,1)}, bf16[96,1024]{1,0:T(8,128)(2,1)S(1)}, u32[]{:S(2)}, u32[]{:S(2)}) collective-permute-start(bf16[96,1024]{1,0:T(8,128)(2,1)} %shard_map.37), channel_id=1, source_target_pairs={{0,8},{2,10},{4,12},{6,14},{9,1},{11,3},{13,5},{15,7},{16,24},{18,... | collective-permute-start | bytes 589832 | tf_op jit(solution)/shard_map/ppermute | solution.py:205
  8.3 3.6 %shard_map.38 = (bf16[128,2048]{1,0:T(8,128)(2,1)}, bf16[128,2048]{1,0:T(8,128)(2,1)}, bf16[128,2048]{1,0:T(8,128)(2,1)}, bf16[128,2048]{1,0:T(8,128)(2,1)}) custom-call(s32[8]{0:T(128)} %stack.62.at_ref, bf16[128,8192]{1,0:T(8,128)(2,1)} %src_ref.3), custom_call_target="tpu_custom_call" | custom-call | bytes 4194304 | tf_op jit(solution)/shard_map/pallas_call | solution.py:67
  11.8 1.6 %collective-permute-start.4 = (bf16[128,2048]{1,0:T(8,128)(2,1)}, bf16[128,2048]{1,0:T(8,128)(2,1)S(1)}, u32[]{:S(2)}, u32[]{:S(2)}) collective-permute-start(bf16[128,2048]{1,0:T(8,128)(2,1)} %get-tuple-element.11), channel_id=1, source_target_pairs={{0,16},{1,17},{2,18},{3,19},{4,20},{5,21},{6,22},{7,23},{8,24},{9,... | collective-permute-start | bytes 1572872 | tf_op jit(solution)/shard_map/ppermute | solution.py:205
  13.4 1.0 %broadcast_select_fusion.1.refs_0_ = bf16[96,1024]{1,0:T(8,128)(2,1)S(1)} fusion(bf16[96,1024]{1,0:T(8,128)(2,1)} %shard_map.37, bf16[96,1024]{1,0:T(8,128)(2,1)S(1)} %collective-permute-done, pred[]{:T(512)S(6)} %lt.15), kind=kLoop, calls=%fused_computation.1 | loop fusion | flops 98304 | bytes 589825 | tf_op jit(solution)/shard_map/jit(_where)/select_n | solution.py:227
  14.4 1.6 %collective-permute-start.1 = (bf16[96,1024]{1,0:T(8,128)(2,1)S(1)}, bf16[96,1024]{1,0:T(8,128)(2,1)S(1)}, u32[]{:S(2)}, u32[]{:S(2)}) collective-permute-start(bf16[96,1024]{1,0:T(8,128)(2,1)S(1)} %broadcast_select_fusion.1.refs_0_), channel_id=1, source_target_pairs={{0,4},{1,5},{2,6},{3,7},{4,0},{5,1},{6,2},{7,3},{8,12},{9,13},{10,... | collective-permute-start | bytes 589832 | tf_op jit(solution)/shard_map/ppermute | solution.py:205
  16.0 1.5 %collective-permute-start.3 = (bf16[96,1024]{1,0:T(8,128)(2,1)S(1)}, bf16[96,1024]{1,0:T(8,128)(2,1)S(1)}, u32[]{:S(2)}, u32[]{:S(2)}) collective-permute-start(bf16[96,1024]{1,0:T(8,128)(2,1)S(1)} %broadcast_select_fusion.1.refs_0_), channel_id=1, source_target_pairs={{0,2},{1,3},{2,0},{3,1},{4,6},{5,7},{6,4},{7,5},{8,10},{9,11},{10,... | collective-permute-start | bytes 589832 | tf_op jit(solution)/shard_map/ppermute | solution.py:205
  17.5 1.1 %collective-permute-start.5 = (bf16[128,2048]{1,0:T(8,128)(2,1)}, bf16[128,2048]{1,0:T(8,128)(2,1)S(1)}, u32[]{:S(2)}, u32[]{:S(2)}) collective-permute-start(bf16[128,2048]{1,0:T(8,128)(2,1)} %get-tuple-element.12), channel_id=1, source_target_pairs={{0,16},{1,17},{2,18},{3,19},{4,20},{5,21},{6,22},{7,23},{8,24},{9,... | collective-permute-start | bytes 1572872 | tf_op jit(solution)/shard_map/ppermute | solution.py:205
  18.6 1.5 %collective-permute-done.1.refs_1_ = bf16[96,1024]{1,0:T(8,128)(2,1)S(1)} collective-permute-done((bf16[96,1024]{1,0:T(8,128)(2,1)S(1)}, bf16[96,1024]{1,0:T(8,128)(2,1)S(1)}, u32[]{:S(2)}, u32[]{:S(2)}) %collective-permute-start.1) | collective-permute-done | bytes 196640 | tf_op jit(solution)/shard_map/ppermute | solution.py:205
  20.1 1.5 %collective-permute-start.2 = (bf16[96,1024]{1,0:T(8,128)(2,1)S(1)}, bf16[96,1024]{1,0:T(8,128)(2,1)S(1)}, u32[]{:S(2)}, u32[]{:S(2)}) collective-permute-start(bf16[96,1024]{1,0:T(8,128)(2,1)S(1)} %collective-permute-done.1.refs_1_), channel_id=1, source_target_pairs={{0,2},{1,3},{2,0},{3,1},{4,6},{5,7},{6,4},{7,5},{8,10},{9,11},{10,... | collective-permute-start | bytes 589832 | tf_op jit(solution)/shard_map/ppermute | solution.py:205
  21.8 1.8 %collective-permute-done.3.refs_2_ = bf16[96,1024]{1,0:T(8,128)(2,1)S(1)} collective-permute-done((bf16[96,1024]{1,0:T(8,128)(2,1)S(1)}, bf16[96,1024]{1,0:T(8,128)(2,1)S(1)}, u32[]{:S(2)}, u32[]{:S(2)}) %collective-permute-start.3) | collective-permute-done | bytes 196640 | tf_op jit(solution)/shard_map/ppermute | solution.py:205
  23.6 3.4 %collective-permute-done.4.refs_6_ = bf16[128,2048]{1,0:T(8,128)(2,1)S(1)} collective-permute-done((bf16[128,2048]{1,0:T(8,128)(2,1)}, bf16[128,2048]{1,0:T(8,128)(2,1)S(1)}, u32[]{:S(2)}, u32[]{:S(2)}) %collective-permute-start.4) | collective-permute-done | bytes 524320 | tf_op jit(solution)/shard_map/ppermute | solution.py:205
  27.0 9.7 %shard_map.39.refs_2_ = f32[2,96,1024]{2,1,0:T(8,128)S(1)} custom-call(s32[5]{0:T(128)S(1)} %stack.57.index_ref, bf16[96,1024]{1,0:T(8,128)(2,1)S(1)} %broadcast_select_fusion.1.refs_0_, bf16[96,1024]{1,0:T(8,128)(2,1)S(1)} %collective-permute-done.1.refs_1_, bf16[96,1024]{1,0:T(8,128)(2,1)S(1)} %collective-permute-done.3.refs_2_, ...), custom_call_target="tpu_custom_call" | custom-call | flops 1207959552 | bytes 12582912 | tf_op jit(solution)/shard_map/pallas_call | solution.py:117
  36.7 3.8 %shard_map.41 = f32[96,1024]{1,0:T(8,128)S(1)} custom-call(s32[2]{0:T(128)S(1)} %pad_add_fusion.1.index_ref, bf16[96,1024]{1,0:T(8,128)(2,1)S(1)} %collective-permute-done.2.refs_0_, bf16[2048,8192]{1,0:T(8,128)(2,1)} %refs_1_.3, f32[2,96,1024]{2,1,0:T(8,128)S(1)} %shard_map.39.refs_2_), custom_call_target="tpu_custom_call" | custom-call | flops 201326592 | bytes 2097152 | tf_op jit(solution)/shard_map/pallas_call | solution.py:117
  40.6 1.3 %collective-permute-start.7 = (f32[96,1024]{1,0:T(8,128)S(1)}, f32[96,1024]{1,0:T(8,128)S(1)}, u32[]{:S(2)}, u32[]{:S(2)}) collective-permute-start(f32[96,1024]{1,0:T(8,128)S(1)} %shard_map.41), channel_id=1, source_target_pairs={{1,0},{3,2},{5,4},{7,6},{8,9},{10,11},{12,13},{14,15},{17,16},{19,... | collective-permute-start | bytes 1179656 | tf_op jit(solution)/shard_map/ppermute | solution.py:205
  41.9 1.6 %collective-permute-start.9 = (bf16[128,2048]{1,0:T(8,128)(2,1)S(1)}, bf16[128,2048]{1,0:T(8,128)(2,1)S(1)}, u32[]{:S(2)}, u32[]{:S(2)}) collective-permute-start(bf16[128,2048]{1,0:T(8,128)(2,1)S(1)} %copy-done.6), channel_id=1, source_target_pairs={{0,2},{1,3},{2,0},{3,1},{4,6},{5,7},{6,4},{7,5},{8,10},{9,11},{10,... | collective-permute-start | bytes 1572872 | tf_op jit(solution)/shard_map/ppermute | solution.py:205
  43.5 3.8 %shard_map.40.ours_ref = f32[96,1024]{1,0:T(8,128)S(1)} custom-call(s32[2]{0:T(128)S(1)} %pad_add_fusion.index_ref, bf16[96,1024]{1,0:T(8,128)(2,1)S(1)} %collective-permute-done.2.refs_0_, bf16[2048,8192]{1,0:T(8,128)(2,1)} %refs_1_.3, f32[2,96,1024]{2,1,0:T(8,128)S(1)} %shard_map.39.refs_2_, bf16[128,2048]{1,0:T(8,128)(2,1)S(1)} %collective-permute-done.5.refs_3_.refs_2_), custom_call_target="tpu_custom_call" | custom-call | flops 201326592 | bytes 2097152 | tf_op jit(solution)/shard_map/pallas_call | solution.py:117
  47.4 1.3 %collective-permute-start.6 = (f32[96,1024]{1,0:T(8,128)S(1)}, f32[96,1024]{1,0:T(8,128)S(1)}, u32[]{:S(2)}, u32[]{:S(2)}) collective-permute-start(f32[96,1024]{1,0:T(8,128)S(1)} %shard_map.40.ours_ref), channel_id=1, source_target_pairs={{1,0},{3,2},{5,4},{7,6},{8,9},{10,11},{12,13},{14,15},{17,16},{19,... | collective-permute-start | bytes 1179656 | tf_op jit(solution)/shard_map/ppermute | solution.py:205
  48.8 3.4 %collective-permute-start.8 = (f32[96,1024]{1,0:T(8,128)S(1)}, f32[96,1024]{1,0:T(8,128)S(1)}, u32[]{:S(2)}, u32[]{:S(2)}) collective-permute-start(f32[96,1024]{1,0:T(8,128)S(1)} %add.83), channel_id=1, source_target_pairs={{0,16},{2,18},{4,20},{6,22},{9,25},{11,27},{13,29},{15,31},{16,0},... | collective-permute-start | bytes 1179656 | tf_op jit(solution)/shard_map/ppermute | solution.py:205
  52.2 4.4 %collective-permute-done.9.after_ref.refs_1_ = bf16[128,2048]{1,0:T(8,128)(2,1)S(1)} collective-permute-done((bf16[128,2048]{1,0:T(8,128)(2,1)S(1)}, bf16[128,2048]{1,0:T(8,128)(2,1)S(1)}, u32[]{:S(2)}, u32[]{:S(2)}) %collective-permute-start.9) | collective-permute-done | bytes 524320 | tf_op jit(solution)/shard_map/ppermute | solution.py:205
  56.6 1.8 %collective-permute-done.8.y_ref = f32[96,1024]{1,0:T(8,128)S(1)} collective-permute-done((f32[96,1024]{1,0:T(8,128)S(1)}, f32[96,1024]{1,0:T(8,128)S(1)}, u32[]{:S(2)}, u32[]{:S(2)}) %collective-permute-start.8) | collective-permute-done | bytes 393248 | tf_op jit(solution)/shard_map/ppermute | solution.py:205
  59.2 2.0 %shard_map.42 = bf16[96,1024]{1,0:T(8,128)(2,1)} custom-call(f32[96,1024]{1,0:T(8,128)} %copy-done.3, f32[96,1024]{1,0:T(8,128)} %copy-done.4, f32[96,1024]{1,0:T(8,128)} %copy-done.5, bf16[128,2048]{1,0:T(8,128)(2,1)} %copy-done), custom_call_target="tpu_custom_call" | custom-call | tf_op jit(solution)/shard_map/pallas_call | solution.py:85
  61.2 1.3 %collective-permute-start.10 = (bf16[96,1024]{1,0:T(8,128)(2,1)}, bf16[96,1024]{1,0:T(8,128)(2,1)S(1)}, u32[]{:S(2)}, u32[]{:S(2)}) collective-permute-start(bf16[96,1024]{1,0:T(8,128)(2,1)} %shard_map.42), channel_id=1, source_target_pairs={{0,8},{2,10},{4,12},{6,14},{9,1},{11,3},{13,5},{15,7},{16,24},{18,... | collective-permute-start | bytes 589832 | tf_op jit(solution)/shard_map/ppermute | solution.py:205
  63.1 2.9 %collective-permute-done.10 = bf16[96,1024]{1,0:T(8,128)(2,1)S(1)} collective-permute-done((bf16[96,1024]{1,0:T(8,128)(2,1)}, bf16[96,1024]{1,0:T(8,128)(2,1)S(1)}, u32[]{:S(2)}, u32[]{:S(2)}) %collective-permute-start.10) | collective-permute-done | bytes 196640 | tf_op jit(solution)/shard_map/ppermute | solution.py:205
  66.9 3.6 %collective-permute-start.11 = (bf16[96,1024]{1,0:T(8,128)(2,1)S(1)}, bf16[96,1024]{1,0:T(8,128)(2,1)S(1)}, u32[]{:S(2)}, u32[]{:S(2)}) collective-permute-start(bf16[96,1024]{1,0:T(8,128)(2,1)S(1)} %broadcast_select_fusion.panel_ref), channel_id=1, source_target_pairs={{0,4},{1,5},{2,6},{3,7},{4,0},{5,1},{6,2},{7,3},{8,12},{9,13},{10,... | collective-permute-start | bytes 589832 | tf_op jit(solution)/shard_map/ppermute | solution.py:205
  70.5 5.2 %collective-permute-done.12.refs_3_ = bf16[128,2048]{1,0:T(8,128)(2,1)S(1)} collective-permute-done((bf16[128,2048]{1,0:T(8,128)(2,1)S(1)}, bf16[128,2048]{1,0:T(8,128)(2,1)S(1)}, u32[]{:S(2)}, u32[]{:S(2)}) %collective-permute-start.12) | collective-permute-done | bytes 524320 | tf_op jit(solution)/shard_map/ppermute | solution.py:205
  75.7 1.0 %copy-done.1 = bf16[128,2048]{1,0:T(8,128)(2,1)S(1)} copy-done((bf16[128,2048]{1,0:T(8,128)(2,1)S(1)}, bf16[128,2048]{1,0:T(8,128)(2,1)}, u32[]{:S(2)}) %copy-start.1) | copy-done | bytes 524312
  77.8 1.3 %collective-permute-done.13 = f32[4,48,128]{2,1,0:T(8,128)S(1)} collective-permute-done((f32[4,48,128]{2,1,0:T(8,128)S(1)}, f32[4,48,128]{2,1,0:T(8,128)S(1)}, u32[]{:S(2)}, u32[]{:S(2)}) %collective-permute-start.13) | collective-permute-done | bytes 98336 | tf_op jit(solution)/shard_map/ppermute | solution.py:205
  79.2 1.6 %collective-permute-start.14 = (f32[2,48,128]{2,1,0:T(8,128)S(1)}, f32[2,48,128]{2,1,0:T(8,128)S(1)}, u32[]{:S(2)}, u32[]{:S(2)}) collective-permute-start(f32[2,48,128]{2,1,0:T(8,128)S(1)} %slice.17), channel_id=1, source_target_pairs={{0,16},{1,17},{2,18},{3,19},{4,20},{5,21},{6,22},{7,23},{8,24},{9,... | collective-permute-start | bytes 147464 | tf_op jit(solution)/shard_map/ppermute | solution.py:205
  80.7 2.6 %collective-permute-done.14 = f32[2,48,128]{2,1,0:T(8,128)S(1)} collective-permute-done((f32[2,48,128]{2,1,0:T(8,128)S(1)}, f32[2,48,128]{2,1,0:T(8,128)S(1)}, u32[]{:S(2)}, u32[]{:S(2)}) %collective-permute-start.14) | collective-permute-done | bytes 49184 | tf_op jit(solution)/shard_map/ppermute | solution.py:205
  83.3 1.6 %collective-permute-start.15 = (f32[48,128]{1,0:T(8,128)S(1)}, f32[48,128]{1,0:T(8,128)S(1)}, u32[]{:S(2)}, u32[]{:S(2)}) collective-permute-start(f32[48,128]{1,0:T(8,128)S(1)} %slice_bitcast_fusion), channel_id=1, source_target_pairs={{0,2},{1,3},{2,0},{3,1},{4,6},{5,7},{6,4},{7,5},{8,10},{9,11},{10,... | collective-permute-start | bytes 73736 | tf_op jit(solution)/shard_map/ppermute | solution.py:205
  84.9 2.3 %collective-permute-done.15 = f32[48,128]{1,0:T(8,128)S(1)} collective-permute-done((f32[48,128]{1,0:T(8,128)S(1)}, f32[48,128]{1,0:T(8,128)S(1)}, u32[]{:S(2)}, u32[]{:S(2)}) %collective-permute-start.15) | collective-permute-done | bytes 24608 | tf_op jit(solution)/shard_map/ppermute | solution.py:205
  (34 shorter events, 5.0 us)
Async XLA Ops:
  1.6 11.8 %collective-permute-start = (bf16[96,1024]{1,0:T(8,128)(2,1)}, bf16[96,1024]{1,0:T(8,128)(2,1)S(1)}, u32[]{:S(2)}, u32[]{:S(2)}) collective-permute-start(bf16[96,1024]{1,0:T(8,128)(2,1)} %shard_map.37), channel_id=1, source_target_pairs={{0,8},{2,10},{4,12},{6,14},{9,1},{11,3},{13,5},{15,7},{16,24},{18,... | collective-permute-start | bytes 589832 | tf_op jit(solution)/shard_map/ppermute | solution.py:205
  11.8 15.1 %collective-permute-start.4 = (bf16[128,2048]{1,0:T(8,128)(2,1)}, bf16[128,2048]{1,0:T(8,128)(2,1)S(1)}, u32[]{:S(2)}, u32[]{:S(2)}) collective-permute-start(bf16[128,2048]{1,0:T(8,128)(2,1)} %get-tuple-element.11), channel_id=1, source_target_pairs={{0,16},{1,17},{2,18},{3,19},{4,20},{5,21},{6,22},{7,23},{8,24},{9,... | collective-permute-start | bytes 1572872 | tf_op jit(solution)/shard_map/ppermute | solution.py:205
  14.4 5.7 %collective-permute-start.1 = (bf16[96,1024]{1,0:T(8,128)(2,1)S(1)}, bf16[96,1024]{1,0:T(8,128)(2,1)S(1)}, u32[]{:S(2)}, u32[]{:S(2)}) collective-permute-start(bf16[96,1024]{1,0:T(8,128)(2,1)S(1)} %broadcast_select_fusion.1.refs_0_), channel_id=1, source_target_pairs={{0,4},{1,5},{2,6},{3,7},{4,0},{5,1},{6,2},{7,3},{8,12},{9,13},{10,... | collective-permute-start | bytes 589832 | tf_op jit(solution)/shard_map/ppermute | solution.py:205
  16.0 7.6 %collective-permute-start.3 = (bf16[96,1024]{1,0:T(8,128)(2,1)S(1)}, bf16[96,1024]{1,0:T(8,128)(2,1)S(1)}, u32[]{:S(2)}, u32[]{:S(2)}) collective-permute-start(bf16[96,1024]{1,0:T(8,128)(2,1)S(1)} %broadcast_select_fusion.1.refs_0_), channel_id=1, source_target_pairs={{0,2},{1,3},{2,0},{3,1},{4,6},{5,7},{6,4},{7,5},{8,10},{9,11},{10,... | collective-permute-start | bytes 589832 | tf_op jit(solution)/shard_map/ppermute | solution.py:205
  17.5 26.0 %collective-permute-start.5 = (bf16[128,2048]{1,0:T(8,128)(2,1)}, bf16[128,2048]{1,0:T(8,128)(2,1)S(1)}, u32[]{:S(2)}, u32[]{:S(2)}) collective-permute-start(bf16[128,2048]{1,0:T(8,128)(2,1)} %get-tuple-element.12), channel_id=1, source_target_pairs={{0,16},{1,17},{2,18},{3,19},{4,20},{5,21},{6,22},{7,23},{8,24},{9,... | collective-permute-start | bytes 1572872 | tf_op jit(solution)/shard_map/ppermute | solution.py:205
  20.1 16.6 %collective-permute-start.2 = (bf16[96,1024]{1,0:T(8,128)(2,1)S(1)}, bf16[96,1024]{1,0:T(8,128)(2,1)S(1)}, u32[]{:S(2)}, u32[]{:S(2)}) collective-permute-start(bf16[96,1024]{1,0:T(8,128)(2,1)S(1)} %collective-permute-done.1.refs_1_), channel_id=1, source_target_pairs={{0,2},{1,3},{2,0},{3,1},{4,6},{5,7},{6,4},{7,5},{8,10},{9,11},{10,... | collective-permute-start | bytes 589832 | tf_op jit(solution)/shard_map/ppermute | solution.py:205
  36.7 5.2 %copy-start.6 = (bf16[128,2048]{1,0:T(8,128)(2,1)S(1)}, bf16[128,2048]{1,0:T(8,128)(2,1)}, u32[]{:S(2)}) copy-start(bf16[128,2048]{1,0:T(8,128)(2,1)} %get-tuple-element.13) | copy-start | bytes 1572868
  36.7 39.0 %copy-start.2 = (bf16[128,2048]{1,0:T(8,128)(2,1)S(1)}, bf16[128,2048]{1,0:T(8,128)(2,1)}, u32[]{:S(2)}) copy-start(bf16[128,2048]{1,0:T(8,128)(2,1)} %get-tuple-element.14.refs_0_) | copy-start | bytes 1572868
  40.6 8.1 %collective-permute-start.7 = (f32[96,1024]{1,0:T(8,128)S(1)}, f32[96,1024]{1,0:T(8,128)S(1)}, u32[]{:S(2)}, u32[]{:S(2)}) collective-permute-start(f32[96,1024]{1,0:T(8,128)S(1)} %shard_map.41), channel_id=1, source_target_pairs={{1,0},{3,2},{5,4},{7,6},{8,9},{10,11},{12,13},{14,15},{17,16},{19,... | collective-permute-start | bytes 1179656 | tf_op jit(solution)/shard_map/ppermute | solution.py:205
  41.9 14.7 %collective-permute-start.9 = (bf16[128,2048]{1,0:T(8,128)(2,1)S(1)}, bf16[128,2048]{1,0:T(8,128)(2,1)S(1)}, u32[]{:S(2)}, u32[]{:S(2)}) collective-permute-start(bf16[128,2048]{1,0:T(8,128)(2,1)S(1)} %copy-done.6), channel_id=1, source_target_pairs={{0,2},{1,3},{2,0},{3,1},{4,6},{5,7},{6,4},{7,5},{8,10},{9,11},{10,... | collective-permute-start | bytes 1572872 | tf_op jit(solution)/shard_map/ppermute | solution.py:205
  47.4 11.1 %copy-start.3 = (f32[96,1024]{1,0:T(8,128)}, f32[96,1024]{1,0:T(8,128)S(1)}, u32[]{:S(2)}) copy-start(f32[96,1024]{1,0:T(8,128)S(1)} %shard_map.40.ours_ref) | copy-start | bytes 1179652
  47.4 9.2 %collective-permute-start.6 = (f32[96,1024]{1,0:T(8,128)S(1)}, f32[96,1024]{1,0:T(8,128)S(1)}, u32[]{:S(2)}, u32[]{:S(2)}) collective-permute-start(f32[96,1024]{1,0:T(8,128)S(1)} %shard_map.40.ours_ref), channel_id=1, source_target_pairs={{1,0},{3,2},{5,4},{7,6},{8,9},{10,11},{12,13},{14,15},{17,16},{19,... | collective-permute-start | bytes 1179656 | tf_op jit(solution)/shard_map/ppermute | solution.py:205
  48.8 9.7 %collective-permute-start.8 = (f32[96,1024]{1,0:T(8,128)S(1)}, f32[96,1024]{1,0:T(8,128)S(1)}, u32[]{:S(2)}, u32[]{:S(2)}) collective-permute-start(f32[96,1024]{1,0:T(8,128)S(1)} %add.83), channel_id=1, source_target_pairs={{0,16},{2,18},{4,20},{6,22},{9,25},{11,27},{13,29},{15,31},{16,0},... | collective-permute-start | bytes 1179656 | tf_op jit(solution)/shard_map/ppermute | solution.py:205
  56.6 1.9 %copy-start = (bf16[128,2048]{1,0:T(8,128)(2,1)}, bf16[128,2048]{1,0:T(8,128)(2,1)S(1)}, u32[]{:S(2)}) copy-start(bf16[128,2048]{1,0:T(8,128)(2,1)S(1)} %collective-permute-done.9.after_ref.refs_1_) | copy-start | bytes 1572868
  56.6 1.9 %copy-start.4 = (f32[96,1024]{1,0:T(8,128)}, f32[96,1024]{1,0:T(8,128)S(1)}, u32[]{:S(2)}) copy-start(f32[96,1024]{1,0:T(8,128)S(1)} %collective-permute-done.6.core_ref) | copy-start | bytes 1179652
  58.4 0.8 copy-start.5
  61.2 4.8 %collective-permute-start.10 = (bf16[96,1024]{1,0:T(8,128)(2,1)}, bf16[96,1024]{1,0:T(8,128)(2,1)S(1)}, u32[]{:S(2)}, u32[]{:S(2)}) collective-permute-start(bf16[96,1024]{1,0:T(8,128)(2,1)} %shard_map.42), channel_id=1, source_target_pairs={{0,8},{2,10},{4,12},{6,14},{9,1},{11,3},{13,5},{15,7},{16,24},{18,... | collective-permute-start | bytes 589832 | tf_op jit(solution)/shard_map/ppermute | solution.py:205
  62.5 13.3 %collective-permute-start.12 = (bf16[128,2048]{1,0:T(8,128)(2,1)S(1)}, bf16[128,2048]{1,0:T(8,128)(2,1)S(1)}, u32[]{:S(2)}, u32[]{:S(2)}) collective-permute-start(bf16[128,2048]{1,0:T(8,128)(2,1)S(1)} %collective-permute-done.4.refs_6_), channel_id=1, source_target_pairs={{0,2},{1,3},{2,0},{3,1},{4,6},{5,7},{6,4},{7,5},{8,10},{9,11},{10,... | collective-permute-start | bytes 1572872 | tf_op jit(solution)/shard_map/ppermute | solution.py:205
  66.9 10.3 %collective-permute-start.11 = (bf16[96,1024]{1,0:T(8,128)(2,1)S(1)}, bf16[96,1024]{1,0:T(8,128)(2,1)S(1)}, u32[]{:S(2)}, u32[]{:S(2)}) collective-permute-start(bf16[96,1024]{1,0:T(8,128)(2,1)S(1)} %broadcast_select_fusion.panel_ref), channel_id=1, source_target_pairs={{0,4},{1,5},{2,6},{3,7},{4,0},{5,1},{6,2},{7,3},{8,12},{9,13},{10,... | collective-permute-start | bytes 589832 | tf_op jit(solution)/shard_map/ppermute | solution.py:205
  75.7 1.0 %copy-start.1 = (bf16[128,2048]{1,0:T(8,128)(2,1)S(1)}, bf16[128,2048]{1,0:T(8,128)(2,1)}, u32[]{:S(2)}) copy-start(bf16[128,2048]{1,0:T(8,128)(2,1)} %copy-done) | copy-start | bytes 1572868
  77.8 1.4 %collective-permute-start.13 = (f32[4,48,128]{2,1,0:T(8,128)S(1)}, f32[4,48,128]{2,1,0:T(8,128)S(1)}, u32[]{:S(2)}, u32[]{:S(2)}) collective-permute-start(f32[4,48,128]{2,1,0:T(8,128)S(1)} %get-tuple-element.16), channel_id=1, source_target_pairs={{0,1},{1,0},{2,3},{3,2},{4,5},{5,4},{6,7},{7,6},{8,9},{9,8},{10,11... | collective-permute-start | bytes 294920 | tf_op jit(solution)/shard_map/ppermute | solution.py:205
  79.2 4.2 %collective-permute-start.14 = (f32[2,48,128]{2,1,0:T(8,128)S(1)}, f32[2,48,128]{2,1,0:T(8,128)S(1)}, u32[]{:S(2)}, u32[]{:S(2)}) collective-permute-start(f32[2,48,128]{2,1,0:T(8,128)S(1)} %slice.17), channel_id=1, source_target_pairs={{0,16},{1,17},{2,18},{3,19},{4,20},{5,21},{6,22},{7,23},{8,24},{9,... | collective-permute-start | bytes 147464 | tf_op jit(solution)/shard_map/ppermute | solution.py:205
  83.3 3.9 %collective-permute-start.15 = (f32[48,128]{1,0:T(8,128)S(1)}, f32[48,128]{1,0:T(8,128)S(1)}, u32[]{:S(2)}, u32[]{:S(2)}) collective-permute-start(f32[48,128]{1,0:T(8,128)S(1)} %slice_bitcast_fusion), channel_id=1, source_target_pairs={{0,2},{1,3},{2,0},{3,1},{4,6},{5,7},{6,4},{7,5},{8,10},{9,11},{10,... | collective-permute-start | bytes 73736 | tf_op jit(solution)/shard_map/ppermute | solution.py:205

commit v3 on v0

v3 whole, which is shorter than its diff:
```python
import functools

import jax
import jax.numpy as jnp
from jax import lax
from jax.experimental import pallas as pl
from jax.experimental.pallas import tpu as pltpu
from jax.sharding import PartitionSpec as P

AXES = ("grp", "ex", "dim")
NT = (((1,), (1,)), ((), ()))
VMEM = pl.BlockSpec(memory_space=pltpu.VMEM)
SMEM = pl.BlockSpec(memory_space=pltpu.SMEM)
HBM = pl.BlockSpec(memory_space=pltpu.HBM)
ANY = pl.BlockSpec(memory_space=pl.ANY)


def limit(mib):
    return pltpu.CompilerParams(vmem_limit_bytes=mib * 1024 * 1024)


def per_device_any(queries, inverse_fisher, stored_grads):
    term_block = jnp.dot(queries, inverse_fisher, preferred_element_type=jnp.float32)
    own_panel = lax.psum_scatter(term_block, "ex", scatter_dimension=1, tiled=True).astype(
        jnp.bfloat16
    )
    partial_scores = lax.dot_general(
        lax.all_gather(own_panel, "ex", axis=1, tiled=True),
        stored_grads,
        NT,
        preferred_element_type=jnp.float32,
    )
    return lax.psum_scatter(partial_scores, "dim", scatter_dimension=0, tiled=True)


def scalars(*values):
    return jnp.stack([jnp.asarray(v, jnp.int32) for v in values])


def cut_rows_kernel(at_ref, src_ref, out_ref, sem):
    rows = out_ref.shape[0]
    start = pl.multiple_of(at_ref[0] * rows, rows)
    copy = pltpu.make_async_copy(src_ref.at[pl.ds(start, rows), :], out_ref, sem)
    copy.start()
    copy.wait()


def cut_rows(src, rows, at):
    return pl.pallas_call(
        cut_rows_kernel,
        out_shape=jax.ShapeDtypeStruct((rows, src.shape[1]), src.dtype),
        in_specs=[SMEM, HBM],
        out_specs=VMEM,
        scratch_shapes=[pltpu.SemaphoreType.DMA],
        compiler_params=limit(2),
    )(scalars(at), src)


def cut_kernel(at, at_ref, src_ref, *refs):
    outs, sem = refs[:-1], refs[-1]
    copies = []
    for out_ref, pieces in zip(outs, at):
        width = out_ref.shape[1] // len(pieces)
        for p, i in enumerate(pieces):
            start = pl.multiple_of(at_ref[i] * width, width)
            copies.append(
                pltpu.make_async_copy(
                    src_ref.at[:, pl.ds(start, width)],
                    out_ref.at[:, p * width : (p + 1) * width],
                    sem.at[len(copies)],
                )
            )
            copies[-1].start()
    for copy in copies:
        copy.wait()


def cut(src, width, starts):
    flat = [s for pieces in starts for s in pieces]
    at, i = [], 0
    for pieces in starts:
        at.append(list(range(i, i + len(pieces))))
        i += len(pieces)
    return pl.pallas_call(
        functools.partial(cut_kernel, at),
        out_shape=[jax.ShapeDtypeStruct((src.shape[0], width * len(p)), src.dtype) for p in starts],
        in_specs=[SMEM, HBM],
        out_specs=[VMEM] * len(starts),
        scratch_shapes=[pltpu.SemaphoreType.DMA((len(flat),))],
        compiler_params=limit(4),
        cost_estimate=pl.CostEstimate(
            flops=0, bytes_accessed=2 * src.shape[0] * width * len(flat) * src.dtype.itemsize, transcendentals=0
        ),
    )(scalars(*flat), src)


def fisher_kernel(part, steps, rows, has_base, n_after, at_ref, chunk_ref, fisher_ref, *refs):
    refs = list(refs)
    base_ref = refs.pop(0) if has_base else None
    out_ref, held, sem = refs[n_after:]
    width = chunk_ref.shape[1]
    first = pl.multiple_of(at_ref[1] * (steps * rows), steps * rows) if part else 0
    columns = pl.ds(pl.multiple_of(at_ref[0] * width, width), width)
    copies = []
    for i in range(steps):
        copies.append(
            pltpu.make_async_copy(
                fisher_ref.at[pl.ds(first + i * rows, rows), columns], held.at[i], sem.at[i]
            )
        )
        copies[-1].start()
    chunk = chunk_ref[...].T
    for i in range(steps):
        copies[i].wait()
        term = jnp.dot(held[i], chunk, preferred_element_type=jnp.float32)
        if has_base:
            term = term + base_ref[pl.ds(first + i * rows, rows), :]
        if part:
            out_ref[:, i * rows : (i + 1) * rows] = term.T
        else:
            out_ref[i * rows : (i + 1) * rows, :] = term


def fisher_dot(chunk, column, fisher, base=None, half=None, after=(), rows=256):
    nq, width = chunk.shape
    part = half is not None
    total = fisher.shape[0] // 2 if part else fisher.shape[0]
    steps = total // rows
    operands = [scalars(column, half if part else 0), chunk, fisher]
    operands += [] if base is None else [base]
    return pl.pallas_call(
        functools.partial(fisher_kernel, part, steps, rows, base is not None, len(after)),
        out_shape=jax.ShapeDtypeStruct((nq, total) if part else (total, nq), jnp.float32),
        in_specs=[SMEM, VMEM, HBM] + [VMEM] * (base is not None) + [ANY] * len(after),
        out_specs=VMEM,
        scratch_shapes=[
            pltpu.VMEM((steps, rows, width), fisher.dtype),
            pltpu.SemaphoreType.DMA((steps,)),
        ],
        compiler_params=limit(40),
        cost_estimate=pl.CostEstimate(
            flops=2 * nq * width * total, bytes_accessed=2 * width * total, transcendentals=0
        ),
    )(*operands, *after)


def panel_kernel(mine_ref, core_ref, *refs):
    refs[-1][...] = (mine_ref[...] + core_ref[...]).astype(refs[-1].dtype)


def panel_sum(mine, from_core, after=()):
    return pl.pallas_call(
        panel_kernel,
        out_shape=jax.ShapeDtypeStruct(mine.shape, jnp.bfloat16),
        in_specs=[VMEM] * 2 + [ANY] * len(after),
        out_specs=VMEM,
        compiler_params=limit(2),
    )(mine, from_core, *after)


def score_kernel(n, at_ref, *refs):
    pieces, slabs = refs[:8], refs[8 : 8 + n]
    keep_ref, give_ref, panel, total = refs[8 + n :]
    rows, width = pieces[0].shape
    owner = at_ref[0] == 1
    for q in range(2):
        for p in range(2):
            mine, other = pieces[q * 4 + p * 2], pieces[q * 4 + p * 2 + 1]
            panel[q * rows : (q + 1) * rows, p * width : (p + 1) * width] = jnp.where(
                owner, mine[...], other[...]
            )
    columns = panel[...].T
    for k in range(n):
        total[k] = jnp.dot(slabs[k][...], columns, preferred_element_type=jnp.float32).T
    here = at_ref[1]
    keep_ref[...] = total[:, pl.ds(pl.multiple_of(here * rows, 8), rows), :]
    give_ref[...] = total[:, pl.ds(pl.multiple_of((1 - here) * rows, 8), rows), :]


def score_dot(pieces, slabs, owner, here):
    n = len(slabs)
    rows, width = pieces[0].shape
    ne = slabs[0].shape[0]
    half = jax.ShapeDtypeStruct((n, rows, ne), jnp.float32)
    return pl.pallas_call(
        functools.partial(score_kernel, n),
        out_shape=(half, half),
        in_specs=[SMEM] + [VMEM] * (8 + n),
        out_specs=(VMEM, VMEM),
        scratch_shapes=[
            pltpu.VMEM((2 * rows, 2 * width), jnp.bfloat16),
            pltpu.VMEM((n, 2 * rows, ne), jnp.float32),
        ],
        compiler_params=limit(8),
    )(scalars(owner, here), *pieces, *slabs)


def spread_kernel(a_ref, b_ref, *outs):
    for k, out_ref in enumerate(outs):
        out_ref[...] = a_ref[k] + b_ref[k]


def spread_sum(a, b):
    return pl.pallas_call(
        spread_kernel,
        out_shape=[jax.ShapeDtypeStruct(a.shape[1:], a.dtype)] * a.shape[0],
        in_specs=[VMEM] * 2,
        out_specs=[VMEM] * a.shape[0],
        compiler_params=limit(2),
    )(a, b)


def per_device_quad(nz, nx, ny, queries, inverse_fisher, stored_grads):
    nex = nz * nx
    near = nz // 2
    nq, block = queries.shape
    half = block // ny
    rows = nq // ny
    y, e, d = (lax.axis_index(a) for a in AXES)
    z = e // nx
    x = e % nx
    u = jnp.where(d == 0, z, nz - 1 - z)
    owner = u < near

    def move(value, target):
        pairs = []
        for sy in range(ny):
            for sz in range(nz):
                for sx in range(nx):
                    for sd in range(2):
                        to = target(sy, sz, sx, sd)
                        if to is not None:
                            ty, tz, tx, td = to
                            pairs.append(((sy * nex + sz * nx + sx) * 2 + sd, (ty * nex + tz * nx + tx) * 2 + td))
        return lax.ppermute(value, AXES, pairs)

    def along_z(value, hops, flip=False):
        def target(sy, sz, sx, sd):
            su = sz if sd == 0 else nz - 1 - sz
            if su not in hops:
                return None
            tu = hops[su]
            return 1 - sy if flip else sy, tu if sd == 0 else nz - 1 - tu, sx, sd

        return move(value, target)

    def swap_x(value):
        return move(value, lambda sy, sz, sx, sd: (sy, sz, 1 - sx, sd))

    def swap_y(value):
        return move(value, lambda sy, sz, sx, sd: (1 - sy, sz, sx, sd))

    def swap_xy(value):
        return move(value, lambda sy, sz, sx, sd: (1 - sy, sz, 1 - sx, sd))

    def swap_core(value):
        return move(value, lambda sy, sz, sx, sd: (sy, sz, sx, 1 - sd))

    def to_owner(value):
        def target(sy, sz, sx, sd):
            su = sz if sd == 0 else nz - 1 - sz
            return None if su < near else (sy, sz, sx, 1 - sd)

        return move(value, target)

    same, far, cross, swap = {0: 0, 1: 1}, {0: 2, 1: 3}, {0: 3, 1: 2}, {0: 1, 1: 0}

    def real_plane(k):
        return jnp.where(d == 0, k, nz - 1 - k)

    planes = [real_plane(u % 2), real_plane(1 - u % 2)]

    def column(plane, x_):
        return plane * nx + x_ - d * (nex // 2)

    def slab(x_, y_):
        return [column(p, x_) * ny + y_ for p in planes]

    own = cut_rows(queries, rows, y)
    q0 = jnp.where(owner, own, along_z(own, far))
    q1 = jnp.where(owner, along_z(own, swap), along_z(own, cross))
    q2, q3 = swap_x(q0), swap_x(q1)

    own_slab, to_x, to_y, to_xy = cut(
        stored_grads, half, [slab(x, y), slab(1 - x, y), slab(x, 1 - y), slab(1 - x, 1 - y)]
    )
    pass_on = swap_y(to_xy)
    from_y = swap_y(to_y)
    from_x = swap_x(to_x)
    from_xy = swap_x(pass_on)

    total = fisher_dot(q0, column(planes[0], x), inverse_fisher)
    total = fisher_dot(q1, column(planes[1], x), inverse_fisher, total)
    total = fisher_dot(q2, column(planes[0], 1 - x), inverse_fisher, total, after=[pass_on])
    last = column(planes[1], 1 - x)
    flip = fisher_dot(q3, last, inverse_fisher, total, 1 - y)
    keep = fisher_dot(q3, last, inverse_fisher, total, y, after=[from_y])

    flip = panel_sum(flip, to_owner(flip))
    keep = panel_sum(keep, to_owner(keep), [from_x])

    pieces = [
        keep,
        along_z(keep, far),
        along_z(keep, swap),
        along_z(keep, cross),
        along_z(flip, same, True),
        along_z(flip, far, True),
        along_z(flip, swap, True),
        along_z(flip, cross, True),
    ]
    slabs = [own_slab, from_x, from_y, from_xy]
    keep, give = score_dot(pieces, slabs, owner, y ^ d)

    mine = spread_sum(keep, swap_core(give))
    return ((mine[0] + swap_x(mine[1])) + swap_y(mine[2])) + swap_xy(mine[3])


def solution(mesh):
    coords = [getattr(device, "coords", None) for device in mesh.devices.flat]
    nx = 2 if None in coords else len({c[0] for c in coords})
    nz = mesh.shape["ex"] // nx
    ny = mesh.shape["grp"]
    if (nz, nx, ny) == (4, 2, 2):
        body = functools.partial(per_device_quad, nz, nx, ny)
    else:
        body = per_device_any
    return jax.shard_map(
        body,
        mesh=mesh,
        in_specs=(P(None, "ex"), P("ex", "dim"), P(("grp", "ex"), "dim")),
        out_specs=P("dim", ("grp", "ex")),
        check_vma=False,
    )
```

time: 164 us -> 89.6 us (0.55)
  waiting for transfers between devices: 128 us -> 6.37 us
  starting transfers between devices: 0.09 us -> 43 us
  Pallas kernels: 0 us -> 34 us
  matrix products: 20.7 us -> 0 us
  between operations: 13.1 us -> 0.35 us
  local copies, waits for them, and re-layouts: 0.01 us -> 3.35 us
    reduce_scatter x2 -> x0, waiting for transfers between devices: 84.1 us -> none  [the longest x1 77.7 us: per_device(): lax.psum_scatter(term_block, 'ex', scatter_dimension=1, tiled=True)]
    all_gather x1 -> x0, waiting for transfers between devices: 44.1 us -> none  [per_device(): lax.all_gather(own_panel, 'ex', axis=1, tiled=True)]
    ppermute x0 -> x22, starting transfers between devices: none -> 43 us  [move(): return lax.ppermute(value, AXES, pairs)]
    pallas_call x0 -> x11, Pallas kernels: none -> 34 us  [the longest x5 30.8 us: fisher_dot(): pl.pallas_call(functools.partial(fisher_kernel, part, steps, rows, base i...]
    dot_general x2 -> x0, matrix products: 20.7 us -> none  [the longest x1 17.8 us: per_device(): jnp.dot(queries, inverse_fisher, preferred_element_type=jnp.float32)]
    ppermute x0 -> x22, waiting for transfers between devices: none -> 6.37 us  [move(): return lax.ppermute(value, AXES, pairs)]
    unnamed x2 -> x6, local copies, waits for them, and re-layouts: 0.01 us -> 3.26 us
    convert_element_type x1 -> x0, other arithmetic: 1.71 us -> none  [per_device(): lax.psum_scatter(term_block, 'ex', scatter_dimension=1, tiled=True)]
  transfers between devices with their start and end apart: 3 -> 22, of which waited for: 3 -> 6; matrix products, arithmetic and copies ran while one was open for 0% -> 2% of each run, Pallas kernels for 0% -> 36%
where the time goes in v3:
time: 89.6 us; the launch traced here: 89.1 us
  starting transfers between devices  43 us (48%)
  Pallas kernels  34 us (38%)
  waiting for transfers between devices  6.37 us (7%)
  local copies, waits for them, and re-layouts  3.35 us (4%)
  other arithmetic  2.05 us (2%)
    ppermute x22, starting transfers between devices, move(): return lax.ppermute(value, AXES, pairs)  43 us
    pallas_call x5, Pallas kernels, fisher_dot(): pl.pallas_call(functools.partial(fisher_kernel, part, steps, rows, base i...  30.8 us
    ppermute x22, waiting for transfers between devices, move(): return lax.ppermute(value, AXES, pairs)  6.37 us
    unnamed x6, local copies, waits for them, and re-layouts  3.26 us
  transfers between devices with their start and end apart: 22, of which 6 were waited for; matrix products, arithmetic and copies ran while one was open for 2% of the time, Pallas kernels for 36%

profile of v3, /device:TPU:0, one launch (start us, length us, event | category | flops | bytes accessed | tf_op | source)
XLA Modules:
  0.0 89.1 jit_solution(3780838035737736204)
XLA Ops:
  0.0 1.0 %copy-done.1 = bf16[96,2048]{1,0:T(8,128)(2,1)S(1)} copy-done((bf16[96,2048]{1,0:T(8,128)(2,1)S(1)}, bf16[96,2048]{1,0:T(8,128)(2,1)}, u32[]{:S(2)}) %copy-start.1) | copy-done | bytes 393240
  1.2 6.0 %collective-permute-start.3 = (bf16[48,2048]{1,0:T(8,128)(2,1)S(1)}, bf16[48,2048]{1,0:T(8,128)(2,1)S(1)}, u32[]{:S(2)}, u32[]{:S(2)}) collective-permute-start(bf16[48,2048]{1,0:T(8,128)(2,1)S(1)} %shard_map.37), channel_id=1, source_target_pairs={{0,8},{2,10},{4,12},{6,14},{9,1},{11,3},{13,5},{15,7},{16,24},{18,... | collective-permute-start | bytes 589832 | tf_op jit(solution)/shard_map/ppermute | solution.py:235
  7.2 2.3 %collective-permute-start.1 = (bf16[48,2048]{1,0:T(8,128)(2,1)S(1)}, bf16[48,2048]{1,0:T(8,128)(2,1)S(1)}, u32[]{:S(2)}, u32[]{:S(2)}) collective-permute-start(bf16[48,2048]{1,0:T(8,128)(2,1)S(1)} %shard_map.37), channel_id=1, source_target_pairs={{0,12},{2,14},{4,8},{6,10},{9,5},{11,7},{13,1},{15,3},{16,28},{18,... | collective-permute-start | bytes 589832 | tf_op jit(solution)/shard_map/ppermute | solution.py:235
  9.5 2.5 %collective-permute-start = (bf16[48,2048]{1,0:T(8,128)(2,1)S(1)}, bf16[48,2048]{1,0:T(8,128)(2,1)}, u32[]{:S(2)}, u32[]{:S(2)}) collective-permute-start(bf16[48,2048]{1,0:T(8,128)(2,1)S(1)} %shard_map.37), channel_id=1, source_target_pairs={{0,4},{2,6},{4,0},{6,2},{9,13},{11,15},{13,9},{15,11},{16,20},{18,... | collective-permute-start | bytes 589832 | tf_op jit(solution)/shard_map/ppermute | solution.py:235
  12.2 1.6 %copy-done = bf16[128,8192]{1,0:T(8,128)(2,1)S(1)} copy-done((bf16[128,8192]{1,0:T(8,128)(2,1)S(1)}, bf16[128,8192]{1,0:T(8,128)(2,1)}, u32[]{:S(2)}) %copy-start) | copy-done | bytes 2097176
  13.7 1.6 %shard_map.40 = (bf16[128,2048]{1,0:T(8,128)(2,1)S(1)}, bf16[128,2048]{1,0:T(8,128)(2,1)}, bf16[128,2048]{1,0:T(8,128)(2,1)S(1)}, bf16[128,2048]{1,0:T(8,128)(2,1)S(1)}) custom-call(s32[8]{0:T(128)S(1)} %stack.95.at_ref, bf16[128,8192]{1,0:T(8,128)(2,1)S(1)} %copy-done), custom_call_target="tpu_custom_call" | custom-call | bytes 4194304 | tf_op jit(solution)/shard_map/pallas_call | solution.py:84
  15.4 1.6 %collective-permute-start.5 = (bf16[128,2048]{1,0:T(8,128)(2,1)S(1)}, bf16[128,2048]{1,0:T(8,128)(2,1)S(1)}, u32[]{:S(2)}, u32[]{:S(2)}) collective-permute-start(bf16[128,2048]{1,0:T(8,128)(2,1)S(1)} %get-tuple-element.15), channel_id=1, source_target_pairs={{0,16},{1,17},{2,18},{3,19},{4,20},{5,21},{6,22},{7,23},{8,24},{9,... | collective-permute-start | bytes 1572872 | tf_op jit(solution)/shard_map/ppermute | solution.py:235
  18.4 1.5 %collective-permute-start.8 = (bf16[128,2048]{1,0:T(8,128)(2,1)}, bf16[128,2048]{1,0:T(8,128)(2,1)S(1)}, u32[]{:S(2)}, u32[]{:S(2)}) collective-permute-start(bf16[128,2048]{1,0:T(8,128)(2,1)} %get-tuple-element.17), channel_id=1, source_target_pairs={{0,2},{1,3},{2,0},{3,1},{4,6},{5,7},{6,4},{7,5},{8,10},{9,11},{10,... | collective-permute-start | bytes 1572872 | tf_op jit(solution)/shard_map/ppermute | solution.py:235
  20.5 1.0 %broadcast_select_fusion.1.chunk_ref = bf16[48,2048]{1,0:T(8,128)(2,1)S(1)} fusion(bf16[48,2048]{1,0:T(8,128)(2,1)} %collective-permute-done, bf16[48,2048]{1,0:T(8,128)(2,1)S(1)} %collective-permute-done.1, pred[]{:T(512)S(6)} %lt.15), kind=kLoop, calls=%fused_computation.1 | loop fusion | flops 98304 | bytes 589825 | tf_op jit(solution)/shard_map/jit(_where)/select_n | solution.py:281
  21.5 1.6 %collective-permute-start.2 = (bf16[48,2048]{1,0:T(8,128)(2,1)S(1)}, bf16[48,2048]{1,0:T(8,128)(2,1)S(1)}, u32[]{:S(2)}, u32[]{:S(2)}) collective-permute-start(bf16[48,2048]{1,0:T(8,128)(2,1)S(1)} %broadcast_select_fusion.1.chunk_ref), channel_id=1, source_target_pairs={{0,2},{1,3},{2,0},{3,1},{4,6},{5,7},{6,4},{7,5},{8,10},{9,11},{10,... | collective-permute-start | bytes 589832 | tf_op jit(solution)/shard_map/ppermute | solution.py:235
  23.1 7.2 %shard_map.38.refs_0_ = f32[2048,48]{1,0:T(8,128)S(1)} custom-call(s32[2]{0:T(128)S(1)} %pad_add_fusion.at_ref, bf16[48,2048]{1,0:T(8,128)(2,1)S(1)} %broadcast_select_fusion.chunk_ref, bf16[2048,8192]{1,0:T(8,128)(2,1)} %fisher_ref.9), custom_call_target="tpu_custom_call" | custom-call | flops 402653184 | bytes 8388608 | tf_op jit(solution)/shard_map/pallas_call | solution.py:131
  30.9 7.2 %shard_map.39.refs_0_ = f32[2048,48]{1,0:T(8,128)S(1)} custom-call(s32[2]{0:T(128)S(1)} %pad_add_fusion.1.at_ref, bf16[48,2048]{1,0:T(8,128)(2,1)S(1)} %broadcast_select_fusion.1.chunk_ref, bf16[2048,8192]{1,0:T(8,128)(2,1)} %fisher_ref.9, f32[2048,48]{1,0:T(8,128)S(1)} %shard_map.38.refs_0_), custom_call_target="tpu_custom_call" | custom-call | flops 402653184 | bytes 8388608 | tf_op jit(solution)/shard_map/pallas_call | solution.py:131
  38.1 7.2 %shard_map.41.refs_0_ = f32[2048,48]{1,0:T(8,128)S(1)} custom-call(s32[2]{0:T(128)S(1)} %pad_add_fusion.2.at_ref, bf16[48,2048]{1,0:T(8,128)(2,1)S(1)} %collective-permute-done.4.chunk_ref, bf16[2048,8192]{1,0:T(8,128)(2,1)} %fisher_ref.9, f32[2048,48]{1,0:T(8,128)S(1)} %shard_map.39.refs_0_, bf16[128,2048]{1,0:T(8,128)(2,1)S(1)} %collective-permute-done.5.refs_1_), custom_call_target="tpu_custom_call" | custom-call | flops 402653184 | bytes 8388608 | tf_op jit(solution)/shard_map/pallas_call | solution.py:131
  45.2 4.7 %shard_map.44.mine_ref = f32[48,1024]{1,0:T(8,128)S(1)} custom-call(s32[2]{0:T(128)S(1)} %pad_add_fusion.5.at_ref, bf16[48,2048]{1,0:T(8,128)(2,1)S(1)} %collective-permute-done.2.chunk_ref, bf16[2048,8192]{1,0:T(8,128)(2,1)} %fisher_ref.9, f32[2048,48]{1,0:T(8,128)S(1)} %shard_map.41.refs_0_), custom_call_target="tpu_custom_call" | custom-call | flops 201326592 | bytes 4194304 | tf_op jit(solution)/shard_map/pallas_call | solution.py:131
  49.9 1.3 %collective-permute-start.12 = (f32[48,1024]{1,0:T(8,128)S(1)}, f32[48,1024]{1,0:T(8,128)S(1)}, u32[]{:S(2)}, u32[]{:S(2)}) collective-permute-start(f32[48,1024]{1,0:T(8,128)S(1)} %shard_map.44.mine_ref), channel_id=1, source_target_pairs={{1,0},{3,2},{5,4},{7,6},{8,9},{10,11},{12,13},{14,15},{17,16},{19,... | collective-permute-start | bytes 589832 | tf_op jit(solution)/shard_map/ppermute | solution.py:235
  51.3 4.7 %shard_map.42.mine_ref = f32[48,1024]{1,0:T(8,128)S(1)} custom-call(s32[2]{0:T(128)S(1)} %pad_add_fusion.4.at_ref, bf16[48,2048]{1,0:T(8,128)(2,1)S(1)} %collective-permute-done.2.chunk_ref, bf16[2048,8192]{1,0:T(8,128)(2,1)} %fisher_ref.9, f32[2048,48]{1,0:T(8,128)S(1)} %shard_map.41.refs_0_, bf16[128,2048]{1,0:T(8,128)(2,1)S(1)} %collective-permute-done.6.refs_1_.refs_10_), custom_call_target="tpu_custom_call" | custom-call | flops 201326592 | bytes 4194304 | tf_op jit(solution)/shard_map/pallas_call | solution.py:131
  55.9 1.3 %collective-permute-start.7 = (f32[48,1024]{1,0:T(8,128)S(1)}, f32[48,1024]{1,0:T(8,128)S(1)}, u32[]{:S(2)}, u32[]{:S(2)}) collective-permute-start(f32[48,1024]{1,0:T(8,128)S(1)} %shard_map.42.mine_ref), channel_id=1, source_target_pairs={{1,0},{3,2},{5,4},{7,6},{8,9},{10,11},{12,13},{14,15},{17,16},{19,... | collective-permute-start | bytes 589832 | tf_op jit(solution)/shard_map/ppermute | solution.py:235
  57.3 4.1 %collective-permute-start.16 = (bf16[48,1024]{1,0:T(8,128)(2,1)S(1)}, bf16[48,1024]{1,0:T(8,128)(2,1)S(1)}, u32[]{:S(2)}, u32[]{:S(2)}) collective-permute-start(bf16[48,1024]{1,0:T(8,128)(2,1)S(1)} %shard_map.45), channel_id=1, source_target_pairs={{0,28},{2,30},{4,24},{6,26},{9,21},{11,23},{13,17},{15,19},{16,12}... | collective-permute-start | bytes 294920 | tf_op jit(solution)/shard_map/ppermute | solution.py:235
  61.4 1.9 %collective-permute-start.15 = (bf16[48,1024]{1,0:T(8,128)(2,1)S(1)}, bf16[48,1024]{1,0:T(8,128)(2,1)S(1)}, u32[]{:S(2)}, u32[]{:S(2)}) collective-permute-start(bf16[48,1024]{1,0:T(8,128)(2,1)S(1)} %shard_map.45), channel_id=1, source_target_pairs={{0,20},{2,22},{4,16},{6,18},{9,29},{11,31},{13,25},{15,27},{16,4},... | collective-permute-start | bytes 294920 | tf_op jit(solution)/shard_map/ppermute | solution.py:235
  63.4 1.3 %collective-permute-start.14 = (bf16[48,1024]{1,0:T(8,128)(2,1)S(1)}, bf16[48,1024]{1,0:T(8,128)(2,1)S(1)}, u32[]{:S(2)}, u32[]{:S(2)}) collective-permute-start(bf16[48,1024]{1,0:T(8,128)(2,1)S(1)} %shard_map.45), channel_id=1, source_target_pairs={{0,24},{2,26},{4,28},{6,30},{9,17},{11,19},{13,21},{15,23},{16,8},... | collective-permute-start | bytes 294920 | tf_op jit(solution)/shard_map/ppermute | solution.py:235
  64.7 2.8 %collective-permute-start.13 = (bf16[48,1024]{1,0:T(8,128)(2,1)S(1)}, bf16[48,1024]{1,0:T(8,128)(2,1)S(1)}, u32[]{:S(2)}, u32[]{:S(2)}) collective-permute-start(bf16[48,1024]{1,0:T(8,128)(2,1)S(1)} %shard_map.45), channel_id=1, source_target_pairs={{0,16},{2,18},{4,20},{6,22},{9,25},{11,27},{13,29},{15,31},{16,0},... | collective-permute-start | bytes 294920 | tf_op jit(solution)/shard_map/ppermute | solution.py:235
  67.6 2.1 %collective-permute-start.11 = (bf16[48,1024]{1,0:T(8,128)(2,1)S(1)}, bf16[48,1024]{1,0:T(8,128)(2,1)S(1)}, u32[]{:S(2)}, u32[]{:S(2)}) collective-permute-start(bf16[48,1024]{1,0:T(8,128)(2,1)S(1)} %shard_map.43.refs_0_), channel_id=1, source_target_pairs={{0,12},{2,14},{4,8},{6,10},{9,5},{11,7},{13,1},{15,3},{16,28},{18,... | collective-permute-start | bytes 294920 | tf_op jit(solution)/shard_map/ppermute | solution.py:235
  69.7 3.7 %collective-permute-start.10 = (bf16[48,1024]{1,0:T(8,128)(2,1)S(1)}, bf16[48,1024]{1,0:T(8,128)(2,1)S(1)}, u32[]{:S(2)}, u32[]{:S(2)}) collective-permute-start(bf16[48,1024]{1,0:T(8,128)(2,1)S(1)} %shard_map.43.refs_0_), channel_id=1, source_target_pairs={{0,4},{2,6},{4,0},{6,2},{9,13},{11,15},{13,9},{15,11},{16,20},{18,... | collective-permute-start | bytes 294920 | tf_op jit(solution)/shard_map/ppermute | solution.py:235
  73.4 1.3 %collective-permute-start.9 = (bf16[48,1024]{1,0:T(8,128)(2,1)S(1)}, bf16[48,1024]{1,0:T(8,128)(2,1)S(1)}, u32[]{:S(2)}, u32[]{:S(2)}) collective-permute-start(bf16[48,1024]{1,0:T(8,128)(2,1)S(1)} %shard_map.43.refs_0_), channel_id=1, source_target_pairs={{0,8},{2,10},{4,12},{6,14},{9,1},{11,3},{13,5},{15,7},{16,24},{18,... | collective-permute-start | bytes 294920 | tf_op jit(solution)/shard_map/ppermute | solution.py:235
  74.7 1.4 %collective-permute-done.10.refs_2_ = bf16[48,1024]{1,0:T(8,128)(2,1)S(1)} collective-permute-done((bf16[48,1024]{1,0:T(8,128)(2,1)S(1)}, bf16[48,1024]{1,0:T(8,128)(2,1)S(1)}, u32[]{:S(2)}, u32[]{:S(2)}) %collective-permute-start.10) | collective-permute-done | bytes 98336 | tf_op jit(solution)/shard_map/ppermute | solution.py:235
  76.9 1.3 %shard_map.46 = (f32[4,48,128]{2,1,0:T(8,128)S(1)}, f32[4,48,128]{2,1,0:T(8,128)S(1)}) custom-call(s32[2]{0:T(128)S(1)} %pad_add_fusion.3.at_ref, bf16[48,1024]{1,0:T(8,128)(2,1)S(1)} %shard_map.43.refs_0_, bf16[48,1024]{1,0:T(8,128)(2,1)S(1)} %collective-permute-done.9.refs_1_, bf16[48,1024]{1,0:T(8,128)(2,1)S(1)} %collective-permute-done.10.refs_2_, ...), custom_call_target="tpu_custom_call" | custom-call | tf_op jit(solution)/shard_map/pallas_call | solution.py:185
  78.2 2.5 %collective-permute-start.18 = (f32[4,48,128]{2,1,0:T(8,128)S(1)}, f32[4,48,128]{2,1,0:T(8,128)S(1)}, u32[]{:S(2)}, u32[]{:S(2)}) collective-permute-start(f32[4,48,128]{2,1,0:T(8,128)S(1)} %get-tuple-element.20), channel_id=1, source_target_pairs={{0,1},{1,0},{2,3},{3,2},{4,5},{5,4},{6,7},{7,6},{8,9},{9,8},{10,11... | collective-permute-start | bytes 294920 | tf_op jit(solution)/shard_map/ppermute | solution.py:235
  80.7 0.9 %collective-permute-done.18.b_ref = f32[4,48,128]{2,1,0:T(8,128)S(1)} collective-permute-done((f32[4,48,128]{2,1,0:T(8,128)S(1)}, f32[4,48,128]{2,1,0:T(8,128)S(1)}, u32[]{:S(2)}, u32[]{:S(2)}) %collective-permute-start.18) | collective-permute-done | bytes 98336 | tf_op jit(solution)/shard_map/ppermute | solution.py:235
  81.7 1.6 %collective-permute-start.19 = (f32[48,128]{1,0:T(8,128)S(1)}, f32[48,128]{1,0:T(8,128)S(1)}, u32[]{:S(2)}, u32[]{:S(2)}) collective-permute-start(f32[48,128]{1,0:T(8,128)S(1)} %get-tuple-element.22), channel_id=1, source_target_pairs={{0,2},{1,3},{2,0},{3,1},{4,6},{5,7},{6,4},{7,5},{8,10},{9,11},{10,... | collective-permute-start | bytes 73736 | tf_op jit(solution)/shard_map/ppermute | solution.py:235
  83.8 1.4 %collective-permute-start.21 = (f32[48,128]{1,0:T(8,128)S(1)}, f32[48,128]{1,0:T(8,128)S(1)}, u32[]{:S(2)}, u32[]{:S(2)}) collective-permute-start(f32[48,128]{1,0:T(8,128)S(1)} %get-tuple-element.24), channel_id=1, source_target_pairs={{0,18},{1,19},{2,16},{3,17},{4,22},{5,23},{6,20},{7,21},{8,26},{9,... | collective-permute-start | bytes 73736 | tf_op jit(solution)/shard_map/ppermute | solution.py:235
  85.6 1.5 %collective-permute-done.20 = f32[48,128]{1,0:T(8,128)S(1)} collective-permute-done((f32[48,128]{1,0:T(8,128)S(1)}, f32[48,128]{1,0:T(8,128)S(1)}, u32[]{:S(2)}, u32[]{:S(2)}) %collective-permute-start.20) | collective-permute-done | bytes 24608 | tf_op jit(solution)/shard_map/ppermute | solution.py:235
  87.1 1.4 %collective-permute-done.21 = f32[48,128]{1,0:T(8,128)S(1)} collective-permute-done((f32[48,128]{1,0:T(8,128)S(1)}, f32[48,128]{1,0:T(8,128)S(1)}, u32[]{:S(2)}, u32[]{:S(2)}) %collective-permute-start.21) | collective-permute-done | bytes 24608 | tf_op jit(solution)/shard_map/ppermute | solution.py:235
  (39 shorter events, 5.4 us)
Async XLA Ops:
  0.0 1.0 %copy-start.1 = (bf16[96,2048]{1,0:T(8,128)(2,1)S(1)}, bf16[96,2048]{1,0:T(8,128)(2,1)}, u32[]{:S(2)}) copy-start(bf16[96,2048]{1,0:T(8,128)(2,1)} %src_ref.2) | copy-start | bytes 1179652
  1.2 16.5 %collective-permute-start.3 = (bf16[48,2048]{1,0:T(8,128)(2,1)S(1)}, bf16[48,2048]{1,0:T(8,128)(2,1)S(1)}, u32[]{:S(2)}, u32[]{:S(2)}) collective-permute-start(bf16[48,2048]{1,0:T(8,128)(2,1)S(1)} %shard_map.37), channel_id=1, source_target_pairs={{0,8},{2,10},{4,12},{6,14},{9,1},{11,3},{13,5},{15,7},{16,24},{18,... | collective-permute-start | bytes 589832 | tf_op jit(solution)/shard_map/ppermute | solution.py:235
  7.2 12.7 %collective-permute-start.1 = (bf16[48,2048]{1,0:T(8,128)(2,1)S(1)}, bf16[48,2048]{1,0:T(8,128)(2,1)S(1)}, u32[]{:S(2)}, u32[]{:S(2)}) collective-permute-start(bf16[48,2048]{1,0:T(8,128)(2,1)S(1)} %shard_map.37), channel_id=1, source_target_pairs={{0,12},{2,14},{4,8},{6,10},{9,5},{11,7},{13,1},{15,3},{16,28},{18,... | collective-permute-start | bytes 589832 | tf_op jit(solution)/shard_map/ppermute | solution.py:235
  9.5 11.0 %collective-permute-start = (bf16[48,2048]{1,0:T(8,128)(2,1)S(1)}, bf16[48,2048]{1,0:T(8,128)(2,1)}, u32[]{:S(2)}, u32[]{:S(2)}) collective-permute-start(bf16[48,2048]{1,0:T(8,128)(2,1)S(1)} %shard_map.37), channel_id=1, source_target_pairs={{0,4},{2,6},{4,0},{6,2},{9,13},{11,15},{13,9},{15,11},{16,20},{18,... | collective-permute-start | bytes 589832 | tf_op jit(solution)/shard_map/ppermute | solution.py:235
  12.2 1.6 %copy-start = (bf16[128,8192]{1,0:T(8,128)(2,1)S(1)}, bf16[128,8192]{1,0:T(8,128)(2,1)}, u32[]{:S(2)}) copy-start(bf16[128,8192]{1,0:T(8,128)(2,1)} %src_ref.3) | copy-start | bytes 6291460
  15.4 14.9 %collective-permute-start.5 = (bf16[128,2048]{1,0:T(8,128)(2,1)S(1)}, bf16[128,2048]{1,0:T(8,128)(2,1)S(1)}, u32[]{:S(2)}, u32[]{:S(2)}) collective-permute-start(bf16[128,2048]{1,0:T(8,128)(2,1)S(1)} %get-tuple-element.15), channel_id=1, source_target_pairs={{0,16},{1,17},{2,18},{3,19},{4,20},{5,21},{6,22},{7,23},{8,24},{9,... | collective-permute-start | bytes 1572872 | tf_op jit(solution)/shard_map/ppermute | solution.py:235
  17.0 34.3 %collective-permute-start.6 = (bf16[128,2048]{1,0:T(8,128)(2,1)S(1)}, bf16[128,2048]{1,0:T(8,128)(2,1)S(1)}, u32[]{:S(2)}, u32[]{:S(2)}) collective-permute-start(bf16[128,2048]{1,0:T(8,128)(2,1)S(1)} %get-tuple-element.16), channel_id=1, source_target_pairs={{0,16},{1,17},{2,18},{3,19},{4,20},{5,21},{6,22},{7,23},{8,24},{9,... | collective-permute-start | bytes 1572872 | tf_op jit(solution)/shard_map/ppermute | solution.py:235
  17.7 0.7 copy-start.2
  18.4 45.0 %collective-permute-start.8 = (bf16[128,2048]{1,0:T(8,128)(2,1)}, bf16[128,2048]{1,0:T(8,128)(2,1)S(1)}, u32[]{:S(2)}, u32[]{:S(2)}) collective-permute-start(bf16[128,2048]{1,0:T(8,128)(2,1)} %get-tuple-element.17), channel_id=1, source_target_pairs={{0,2},{1,3},{2,0},{3,1},{4,6},{5,7},{6,4},{7,5},{8,10},{9,11},{10,... | collective-permute-start | bytes 1572872 | tf_op jit(solution)/shard_map/ppermute | solution.py:235
  19.9 18.1 %collective-permute-start.4 = (bf16[48,2048]{1,0:T(8,128)(2,1)S(1)}, bf16[48,2048]{1,0:T(8,128)(2,1)S(1)}, u32[]{:S(2)}, u32[]{:S(2)}) collective-permute-start(bf16[48,2048]{1,0:T(8,128)(2,1)S(1)} %broadcast_select_fusion.chunk_ref), channel_id=1, source_target_pairs={{0,2},{1,3},{2,0},{3,1},{4,6},{5,7},{6,4},{7,5},{8,10},{9,11},{10,... | collective-permute-start | bytes 589832 | tf_op jit(solution)/shard_map/ppermute | solution.py:235
  21.5 23.8 %collective-permute-start.2 = (bf16[48,2048]{1,0:T(8,128)(2,1)S(1)}, bf16[48,2048]{1,0:T(8,128)(2,1)S(1)}, u32[]{:S(2)}, u32[]{:S(2)}) collective-permute-start(bf16[48,2048]{1,0:T(8,128)(2,1)S(1)} %broadcast_select_fusion.1.chunk_ref), channel_id=1, source_target_pairs={{0,2},{1,3},{2,0},{3,1},{4,6},{5,7},{6,4},{7,5},{8,10},{9,11},{10,... | collective-permute-start | bytes 589832 | tf_op jit(solution)/shard_map/ppermute | solution.py:235
  30.3 46.6 %collective-permute-start.17 = (bf16[128,2048]{1,0:T(8,128)(2,1)S(1)}, bf16[128,2048]{1,0:T(8,128)(2,1)S(1)}, u32[]{:S(2)}, u32[]{:S(2)}) collective-permute-start(bf16[128,2048]{1,0:T(8,128)(2,1)S(1)} %collective-permute-done.5.refs_1_), channel_id=1, source_target_pairs={{0,2},{1,3},{2,0},{3,1},{4,6},{5,7},{6,4},{7,5},{8,10},{9,11},{10,... | collective-permute-start | bytes 1572872 | tf_op jit(solution)/shard_map/ppermute | solution.py:235
  49.9 7.3 %collective-permute-start.12 = (f32[48,1024]{1,0:T(8,128)S(1)}, f32[48,1024]{1,0:T(8,128)S(1)}, u32[]{:S(2)}, u32[]{:S(2)}) collective-permute-start(f32[48,1024]{1,0:T(8,128)S(1)} %shard_map.44.mine_ref), channel_id=1, source_target_pairs={{1,0},{3,2},{5,4},{7,6},{8,9},{10,11},{12,13},{14,15},{17,16},{19,... | collective-permute-start | bytes 589832 | tf_op jit(solution)/shard_map/ppermute | solution.py:235
  55.9 8.7 %collective-permute-start.7 = (f32[48,1024]{1,0:T(8,128)S(1)}, f32[48,1024]{1,0:T(8,128)S(1)}, u32[]{:S(2)}, u32[]{:S(2)}) collective-permute-start(f32[48,1024]{1,0:T(8,128)S(1)} %shard_map.42.mine_ref), channel_id=1, source_target_pairs={{1,0},{3,2},{5,4},{7,6},{8,9},{10,11},{12,13},{14,15},{17,16},{19,... | collective-permute-start | bytes 589832 | tf_op jit(solution)/shard_map/ppermute | solution.py:235
  57.3 10.3 %collective-permute-start.16 = (bf16[48,1024]{1,0:T(8,128)(2,1)S(1)}, bf16[48,1024]{1,0:T(8,128)(2,1)S(1)}, u32[]{:S(2)}, u32[]{:S(2)}) collective-permute-start(bf16[48,1024]{1,0:T(8,128)(2,1)S(1)} %shard_map.45), channel_id=1, source_target_pairs={{0,28},{2,30},{4,24},{6,26},{9,21},{11,23},{13,17},{15,19},{16,12}... | collective-permute-start | bytes 294920 | tf_op jit(solution)/shard_map/ppermute | solution.py:235
  61.4 8.2 %collective-permute-start.15 = (bf16[48,1024]{1,0:T(8,128)(2,1)S(1)}, bf16[48,1024]{1,0:T(8,128)(2,1)S(1)}, u32[]{:S(2)}, u32[]{:S(2)}) collective-permute-start(bf16[48,1024]{1,0:T(8,128)(2,1)S(1)} %shard_map.45), channel_id=1, source_target_pairs={{0,20},{2,22},{4,16},{6,18},{9,29},{11,31},{13,25},{15,27},{16,4},... | collective-permute-start | bytes 294920 | tf_op jit(solution)/shard_map/ppermute | solution.py:235
  63.4 10.0 %collective-permute-start.14 = (bf16[48,1024]{1,0:T(8,128)(2,1)S(1)}, bf16[48,1024]{1,0:T(8,128)(2,1)S(1)}, u32[]{:S(2)}, u32[]{:S(2)}) collective-permute-start(bf16[48,1024]{1,0:T(8,128)(2,1)S(1)} %shard_map.45), channel_id=1, source_target_pairs={{0,24},{2,26},{4,28},{6,30},{9,17},{11,19},{13,21},{15,23},{16,8},... | collective-permute-start | bytes 294920 | tf_op jit(solution)/shard_map/ppermute | solution.py:235
  64.7 10.1 %collective-permute-start.13 = (bf16[48,1024]{1,0:T(8,128)(2,1)S(1)}, bf16[48,1024]{1,0:T(8,128)(2,1)S(1)}, u32[]{:S(2)}, u32[]{:S(2)}) collective-permute-start(bf16[48,1024]{1,0:T(8,128)(2,1)S(1)} %shard_map.45), channel_id=1, source_target_pairs={{0,16},{2,18},{4,20},{6,22},{9,25},{11,27},{13,29},{15,31},{16,0},... | collective-permute-start | bytes 294920 | tf_op jit(solution)/shard_map/ppermute | solution.py:235
  67.6 7.2 %collective-permute-start.11 = (bf16[48,1024]{1,0:T(8,128)(2,1)S(1)}, bf16[48,1024]{1,0:T(8,128)(2,1)S(1)}, u32[]{:S(2)}, u32[]{:S(2)}) collective-permute-start(bf16[48,1024]{1,0:T(8,128)(2,1)S(1)} %shard_map.43.refs_0_), channel_id=1, source_target_pairs={{0,12},{2,14},{4,8},{6,10},{9,5},{11,7},{13,1},{15,3},{16,28},{18,... | collective-permute-start | bytes 294920 | tf_op jit(solution)/shard_map/ppermute | solution.py:235
  69.7 6.5 %collective-permute-start.10 = (bf16[48,1024]{1,0:T(8,128)(2,1)S(1)}, bf16[48,1024]{1,0:T(8,128)(2,1)S(1)}, u32[]{:S(2)}, u32[]{:S(2)}) collective-permute-start(bf16[48,1024]{1,0:T(8,128)(2,1)S(1)} %shard_map.43.refs_0_), channel_id=1, source_target_pairs={{0,4},{2,6},{4,0},{6,2},{9,13},{11,15},{13,9},{15,11},{16,20},{18,... | collective-permute-start | bytes 294920 | tf_op jit(solution)/shard_map/ppermute | solution.py:235
  73.4 3.5 %collective-permute-start.9 = (bf16[48,1024]{1,0:T(8,128)(2,1)S(1)}, bf16[48,1024]{1,0:T(8,128)(2,1)S(1)}, u32[]{:S(2)}, u32[]{:S(2)}) collective-permute-start(bf16[48,1024]{1,0:T(8,128)(2,1)S(1)} %shard_map.43.refs_0_), channel_id=1, source_target_pairs={{0,8},{2,10},{4,12},{6,14},{9,1},{11,3},{13,5},{15,7},{16,24},{18,... | collective-permute-start | bytes 294920 | tf_op jit(solution)/shard_map/ppermute | solution.py:235
  78.2 3.5 %collective-permute-start.18 = (f32[4,48,128]{2,1,0:T(8,128)S(1)}, f32[4,48,128]{2,1,0:T(8,128)S(1)}, u32[]{:S(2)}, u32[]{:S(2)}) collective-permute-start(f32[4,48,128]{2,1,0:T(8,128)S(1)} %get-tuple-element.20), channel_id=1, source_target_pairs={{0,1},{1,0},{2,3},{3,2},{4,5},{5,4},{6,7},{7,6},{8,9},{9,8},{10,11... | collective-permute-start | bytes 294920 | tf_op jit(solution)/shard_map/ppermute | solution.py:235
  81.7 3.9 %collective-permute-start.19 = (f32[48,128]{1,0:T(8,128)S(1)}, f32[48,128]{1,0:T(8,128)S(1)}, u32[]{:S(2)}, u32[]{:S(2)}) collective-permute-start(f32[48,128]{1,0:T(8,128)S(1)} %get-tuple-element.22), channel_id=1, source_target_pairs={{0,2},{1,3},{2,0},{3,1},{4,6},{5,7},{6,4},{7,5},{8,10},{9,11},{10,... | collective-permute-start | bytes 73736 | tf_op jit(solution)/shard_map/ppermute | solution.py:235
  83.3 3.8 %collective-permute-start.20 = (f32[48,128]{1,0:T(8,128)S(1)}, f32[48,128]{1,0:T(8,128)S(1)}, u32[]{:S(2)}, u32[]{:S(2)}) collective-permute-start(f32[48,128]{1,0:T(8,128)S(1)} %get-tuple-element.23), channel_id=1, source_target_pairs={{0,16},{1,17},{2,18},{3,19},{4,20},{5,21},{6,22},{7,23},{8,24},{9,... | collective-permute-start | bytes 73736 | tf_op jit(solution)/shard_map/ppermute | solution.py:235
  83.8 4.7 %collective-permute-start.21 = (f32[48,128]{1,0:T(8,128)S(1)}, f32[48,128]{1,0:T(8,128)S(1)}, u32[]{:S(2)}, u32[]{:S(2)}) collective-permute-start(f32[48,128]{1,0:T(8,128)S(1)} %get-tuple-element.24), channel_id=1, source_target_pairs={{0,18},{1,19},{2,16},{3,17},{4,22},{5,23},{6,20},{7,21},{8,26},{9,... | collective-permute-start | bytes 73736 | tf_op jit(solution)/shard_map/ppermute | solution.py:235

commit v4 on v3

--- a/solution.py
+++ b/solution.py
@@ -94,52 +94,59 @@
     )(scalars(*flat), src)
 
 
-def fisher_kernel(part, steps, rows, has_base, n_after, at_ref, chunk_ref, fisher_ref, *refs):
+def fisher_kernel(part, steps, n_after, has_base, at_ref, chunk_ref, fisher_ref, *refs):
     refs = list(refs)
     base_ref = refs.pop(0) if has_base else None
-    out_ref, held, sem = refs[n_after:]
+    out_ref, held, acc, sem = refs[n_after:]
     width = chunk_ref.shape[1]
-    first = pl.multiple_of(at_ref[1] * (steps * rows), steps * rows) if part else 0
-    columns = pl.ds(pl.multiple_of(at_ref[0] * width, width), width)
+    rows, step = held.shape[1:]
+    first = pl.multiple_of(at_ref[1] * rows, rows) if part else 0
+    start = pl.multiple_of(at_ref[0] * width, width)
     copies = []
     for i in range(steps):
         copies.append(
             pltpu.make_async_copy(
-                fisher_ref.at[pl.ds(first + i * rows, rows), columns], held.at[i], sem.at[i]
+                fisher_ref.at[pl.ds(first, rows), pl.ds(start + i * step, step)], held.at[i], sem.at[i]
             )
         )
         copies[-1].start()
     chunk = chunk_ref[...].T
+    total = acc if part else out_ref
     for i in range(steps):
         copies[i].wait()
-        term = jnp.dot(held[i], chunk, preferred_element_type=jnp.float32)
-        if has_base:
-            term = term + base_ref[pl.ds(first + i * rows, rows), :]
-        if part:
-            out_ref[:, i * rows : (i + 1) * rows] = term.T
+        term = jnp.dot(
+            held[i], chunk[i * step : (i + 1) * step], preferred_element_type=jnp.float32
+        )
+        if i:
+            term = term + total[...]
+        elif has_base:
+            term = term + base_ref[pl.ds(first, rows), :]
+        if part and i == steps - 1:
+            out_ref[...] = term.T
         else:
-            out_ref[i * rows : (i + 1) * rows, :] = term
-
-
-def fisher_dot(chunk, column, fisher, base=None, half=None, after=(), rows=256):
+            total[...] = term
+
+
+def fisher_dot(chunk, column, fisher, base=None, half=None, after=(), step=512):
     nq, width = chunk.shape
     part = half is not None
-    total = fisher.shape[0] // 2 if part else fisher.shape[0]
-    steps = total // rows
+    rows = fisher.shape[0] // 2 if part else fisher.shape[0]
+    steps = width // step
     operands = [scalars(column, half if part else 0), chunk, fisher]
     operands += [] if base is None else [base]
     return pl.pallas_call(
-        functools.partial(fisher_kernel, part, steps, rows, base is not None, len(after)),
-        out_shape=jax.ShapeDtypeStruct((nq, total) if part else (total, nq), jnp.float32),
+        functools.partial(fisher_kernel, part, steps, len(after), base is not None),
+        out_shape=jax.ShapeDtypeStruct((nq, rows) if part else (rows, nq), jnp.float32),
         in_specs=[SMEM, VMEM, HBM] + [VMEM] * (base is not None) + [ANY] * len(after),
         out_specs=VMEM,
         scratch_shapes=[
-            pltpu.VMEM((steps, rows, width), fisher.dtype),
+            pltpu.VMEM((steps, rows, step), fisher.dtype),
+            pltpu.VMEM((rows if part else 8, nq), jnp.float32),
             pltpu.SemaphoreType.DMA((steps,)),
         ],
         compiler_params=limit(40),
         cost_estimate=pl.CostEstimate(
-            flops=2 * nq * width * total, bytes_accessed=2 * width * total, transcendentals=0
+            flops=2 * nq * width * rows, bytes_accessed=2 * width * rows, transcendentals=0
         ),
     )(*operands, *after)
 
@@ -160,9 +167,10 @@
 
 def score_kernel(n, at_ref, *refs):
     pieces, slabs = refs[:8], refs[8 : 8 + n]
-    keep_ref, give_ref, panel, total = refs[8 + n :]
+    out_ref, panel = refs[8 + n :]
     rows, width = pieces[0].shape
     owner = at_ref[0] == 1
+    y, x = at_ref[1], at_ref[2]
     for q in range(2):
         for p in range(2):
             mine, other = pieces[q * 4 + p * 2], pieces[q * 4 + p * 2 + 1]
@@ -171,43 +179,23 @@
             )
     columns = panel[...].T
     for k in range(n):
-        total[k] = jnp.dot(slabs[k][...], columns, preferred_element_type=jnp.float32).T
-    here = at_ref[1]
-    keep_ref[...] = total[:, pl.ds(pl.multiple_of(here * rows, 8), rows), :]
-    give_ref[...] = total[:, pl.ds(pl.multiple_of((1 - here) * rows, 8), rows), :]
-
-
-def score_dot(pieces, slabs, owner, here):
+        term = jnp.dot(slabs[k][...], columns, preferred_element_type=jnp.float32).T
+        chip = (y ^ (k // 2)) * 2 + (x ^ (k % 2))
+        for q in range(2):
+            out_ref[chip * 2 + (y ^ q)] = term[q * rows : (q + 1) * rows]
+
+
+def score_dot(pieces, slabs, owner, y, x):
     n = len(slabs)
     rows, width = pieces[0].shape
-    ne = slabs[0].shape[0]
-    half = jax.ShapeDtypeStruct((n, rows, ne), jnp.float32)
     return pl.pallas_call(
         functools.partial(score_kernel, n),
-        out_shape=(half, half),
+        out_shape=jax.ShapeDtypeStruct((2 * n, rows, slabs[0].shape[0]), jnp.float32),
         in_specs=[SMEM] + [VMEM] * (8 + n),
-        out_specs=(VMEM, VMEM),
-        scratch_shapes=[
-            pltpu.VMEM((2 * rows, 2 * width), jnp.bfloat16),
-            pltpu.VMEM((n, 2 * rows, ne), jnp.float32),
-        ],
+        out_specs=VMEM,
+        scratch_shapes=[pltpu.VMEM((2 * rows, 2 * width), jnp.bfloat16)],
         compiler_params=limit(8),
-    )(scalars(owner, here), *pieces, *slabs)
-
-
-def spread_kernel(a_ref, b_ref, *outs):
-    for k, out_ref in enumerate(outs):
-        out_ref[...] = a_ref[k] + b_ref[k]
-
-
-def spread_sum(a, b):
-    return pl.pallas_call(
-        spread_kernel,
-        out_shape=[jax.ShapeDtypeStruct(a.shape[1:], a.dtype)] * a.shape[0],
-        in_specs=[VMEM] * 2,
-        out_specs=[VMEM] * a.shape[0],
-        compiler_params=limit(2),
-    )(a, b)
+    )(scalars(owner, y, x), *pieces, *slabs)
 
 
 def per_device_quad(nz, nx, ny, queries, inverse_fisher, stored_grads):
@@ -250,12 +238,6 @@
     def swap_y(value):
         return move(value, lambda sy, sz, sx, sd: (1 - sy, sz, sx, sd))
 
-    def swap_xy(value):
-        return move(value, lambda sy, sz, sx, sd: (1 - sy, sz, 1 - sx, sd))
-
-    def swap_core(value):
-        return move(value, lambda sy, sz, sx, sd: (sy, sz, sx, 1 - sd))
-
     def to_owner(value):
         def target(sy, sz, sx, sd):
             su = sz if sd == 0 else nz - 1 - sz
@@ -310,10 +292,13 @@
         along_z(flip, cross, True),
     ]
     slabs = [own_slab, from_x, from_y, from_xy]
-    keep, give = score_dot(pieces, slabs, owner, y ^ d)
-
-    mine = spread_sum(keep, swap_core(give))
-    return ((mine[0] + swap_x(mine[1])) + swap_y(mine[2])) + swap_xy(mine[3])
+    scores = score_dot(pieces, slabs, owner, y, x)
+
+    planes_devices = [
+        [(sy * nex + sz * nx + sx) * 2 + sd for sy in range(ny) for sx in range(nx) for sd in range(2)]
+        for sz in range(nz)
+    ]
+    return jnp.sum(lax.all_to_all(scores, AXES, 0, 0, axis_index_groups=planes_devices), axis=0)
 
 
 def solution(mesh):

time: 89.6 us -> 89.8 us (level)
  blocking collectives: 0 us -> 10.9 us
  starting transfers between devices: 43 us -> 37.1 us
  waiting for transfers between devices: 6.37 us -> 2.15 us
    all_to_all x0 -> x1, blocking collectives: none -> 10.9 us  [per_device_quad(): lax.all_to_all(scores, AXES, 0, 0, axis_index_groups=planes_devices)]
    ppermute x22 -> x18, starting transfers between devices: 43 us -> 37.1 us  [move(): return lax.ppermute(value, AXES, pairs)]
    ppermute x22 -> x18, waiting for transfers between devices: 6.37 us -> 2.15 us  [move(): return lax.ppermute(value, AXES, pairs)]
    pallas_call x7 -> x6, Pallas kernels: 32.1 us -> 31.5 us  [the longest x5 30.2 us: fisher_dot(): pl.pallas_call(functools.partial(fisher_kernel, part, steps, len(after),...]
  transfers between devices with their start and end apart: 22 -> 18, of which waited for: 6 -> 2; matrix products, arithmetic and copies ran while one was open for 2% -> 2% of each run, Pallas kernels for 36% -> 36%
where the time goes in v4:
time: 89.8 us; the launch traced here: 89.3 us
  starting transfers between devices  37.1 us (41%)
  Pallas kernels  33.4 us (37%)
  blocking collectives  10.9 us (12%)
  local copies, waits for them, and re-layouts  3.36 us (4%)
  waiting for transfers between devices  2.15 us (2%)
  other arithmetic  2.05 us (2%)
    ppermute x18, starting transfers between devices, move(): return lax.ppermute(value, AXES, pairs)  37.1 us
    pallas_call x5, Pallas kernels, fisher_dot(): pl.pallas_call(functools.partial(fisher_kernel, part, steps, len(after),...  30.2 us
    all_to_all x1, blocking collectives, per_device_quad(): lax.all_to_all(scores, AXES, 0, 0, axis_index_groups=planes_devices)  10.9 us
    unnamed x6, local copies, waits for them, and re-layouts  3.27 us
    ppermute x18, waiting for transfers between devices, move(): return lax.ppermute(value, AXES, pairs)  2.15 us
  transfers between devices with their start and end apart: 18, of which 2 were waited for; matrix products, arithmetic and copies ran while one was open for 2% of the time, Pallas kernels for 36%

profile of v4, /device:TPU:0, one launch (start us, length us, event | category | flops | bytes accessed | tf_op | source)
XLA Modules:
  0.0 89.3 jit_solution(13552538507899419796)
XLA Ops:
  0.0 1.0 %copy-done.1 = bf16[96,2048]{1,0:T(8,128)(2,1)S(1)} copy-done((bf16[96,2048]{1,0:T(8,128)(2,1)S(1)}, bf16[96,2048]{1,0:T(8,128)(2,1)}, u32[]{:S(2)}) %copy-start.1) | copy-done | bytes 393240
  1.2 6.0 %collective-permute-start.3 = (bf16[48,2048]{1,0:T(8,128)(2,1)S(1)}, bf16[48,2048]{1,0:T(8,128)(2,1)S(1)}, u32[]{:S(2)}, u32[]{:S(2)}) collective-permute-start(bf16[48,2048]{1,0:T(8,128)(2,1)S(1)} %shard_map.37), channel_id=1, source_target_pairs={{0,8},{2,10},{4,12},{6,14},{9,1},{11,3},{13,5},{15,7},{16,24},{18,... | collective-permute-start | bytes 589832 | tf_op jit(solution)/shard_map/ppermute | solution.py:223
  7.2 2.3 %collective-permute-start.1 = (bf16[48,2048]{1,0:T(8,128)(2,1)S(1)}, bf16[48,2048]{1,0:T(8,128)(2,1)S(1)}, u32[]{:S(2)}, u32[]{:S(2)}) collective-permute-start(bf16[48,2048]{1,0:T(8,128)(2,1)S(1)} %shard_map.37), channel_id=1, source_target_pairs={{0,12},{2,14},{4,8},{6,10},{9,5},{11,7},{13,1},{15,3},{16,28},{18,... | collective-permute-start | bytes 589832 | tf_op jit(solution)/shard_map/ppermute | solution.py:223
  9.5 2.5 %collective-permute-start = (bf16[48,2048]{1,0:T(8,128)(2,1)S(1)}, bf16[48,2048]{1,0:T(8,128)(2,1)}, u32[]{:S(2)}, u32[]{:S(2)}) collective-permute-start(bf16[48,2048]{1,0:T(8,128)(2,1)S(1)} %shard_map.37), channel_id=1, source_target_pairs={{0,4},{2,6},{4,0},{6,2},{9,13},{11,15},{13,9},{15,11},{16,20},{18,... | collective-permute-start | bytes 589832 | tf_op jit(solution)/shard_map/ppermute | solution.py:223
  12.2 1.6 %copy-done = bf16[128,8192]{1,0:T(8,128)(2,1)S(1)} copy-done((bf16[128,8192]{1,0:T(8,128)(2,1)S(1)}, bf16[128,8192]{1,0:T(8,128)(2,1)}, u32[]{:S(2)}) %copy-start) | copy-done | bytes 2097176
  13.7 1.6 %shard_map.40 = (bf16[128,2048]{1,0:T(8,128)(2,1)S(1)}, bf16[128,2048]{1,0:T(8,128)(2,1)}, bf16[128,2048]{1,0:T(8,128)(2,1)S(1)}, bf16[128,2048]{1,0:T(8,128)(2,1)S(1)}) custom-call(s32[8]{0:T(128)S(1)} %stack.96.at_ref, bf16[128,8192]{1,0:T(8,128)(2,1)S(1)} %copy-done), custom_call_target="tpu_custom_call" | custom-call | bytes 4194304 | tf_op jit(solution)/shard_map/pallas_call | solution.py:84
  15.4 1.6 %collective-permute-start.5 = (bf16[128,2048]{1,0:T(8,128)(2,1)S(1)}, bf16[128,2048]{1,0:T(8,128)(2,1)S(1)}, u32[]{:S(2)}, u32[]{:S(2)}) collective-permute-start(bf16[128,2048]{1,0:T(8,128)(2,1)S(1)} %get-tuple-element.9), channel_id=1, source_target_pairs={{0,16},{1,17},{2,18},{3,19},{4,20},{5,21},{6,22},{7,23},{8,24},{9,... | collective-permute-start | bytes 1572872 | tf_op jit(solution)/shard_map/ppermute | solution.py:223
  17.7 0.7 copy-done.2
  18.4 1.5 %collective-permute-start.8 = (bf16[128,2048]{1,0:T(8,128)(2,1)}, bf16[128,2048]{1,0:T(8,128)(2,1)S(1)}, u32[]{:S(2)}, u32[]{:S(2)}) collective-permute-start(bf16[128,2048]{1,0:T(8,128)(2,1)} %get-tuple-element.11), channel_id=1, source_target_pairs={{0,2},{1,3},{2,0},{3,1},{4,6},{5,7},{6,4},{7,5},{8,10},{9,11},{10,... | collective-permute-start | bytes 1572872 | tf_op jit(solution)/shard_map/ppermute | solution.py:223
  19.9 0.6 collective-permute-start.4
  20.5 1.0 %broadcast_select_fusion.1.chunk_ref = bf16[48,2048]{1,0:T(8,128)(2,1)S(1)} fusion(bf16[48,2048]{1,0:T(8,128)(2,1)} %collective-permute-done, bf16[48,2048]{1,0:T(8,128)(2,1)S(1)} %collective-permute-done.1, pred[]{:T(512)S(6)} %lt.15), kind=kLoop, calls=%fused_computation.1 | loop fusion | flops 98304 | bytes 589825 | tf_op jit(solution)/shard_map/jit(_where)/select_n | solution.py:263
  21.5 1.6 %collective-permute-start.2 = (bf16[48,2048]{1,0:T(8,128)(2,1)S(1)}, bf16[48,2048]{1,0:T(8,128)(2,1)S(1)}, u32[]{:S(2)}, u32[]{:S(2)}) collective-permute-start(bf16[48,2048]{1,0:T(8,128)(2,1)S(1)} %broadcast_select_fusion.1.chunk_ref), channel_id=1, source_target_pairs={{0,2},{1,3},{2,0},{3,1},{4,6},{5,7},{6,4},{7,5},{8,10},{9,11},{10,... | collective-permute-start | bytes 589832 | tf_op jit(solution)/shard_map/ppermute | solution.py:223
  23.1 7.0 %shard_map.38.refs_0_ = f32[2048,48]{1,0:T(8,128)S(1)} custom-call(s32[2]{0:T(128)S(1)} %pad_add_fusion.at_ref, bf16[48,2048]{1,0:T(8,128)(2,1)S(1)} %broadcast_select_fusion.chunk_ref, bf16[2048,8192]{1,0:T(8,128)(2,1)} %fisher_ref.9), custom_call_target="tpu_custom_call" | custom-call | flops 402653184 | bytes 8388608 | tf_op jit(solution)/shard_map/pallas_call | solution.py:137
  30.1 0.6 collective-permute-start.17
  30.8 7.0 %shard_map.39.refs_0_ = f32[2048,48]{1,0:T(8,128)S(1)} custom-call(s32[2]{0:T(128)S(1)} %pad_add_fusion.1.at_ref, bf16[48,2048]{1,0:T(8,128)(2,1)S(1)} %broadcast_select_fusion.1.chunk_ref, bf16[2048,8192]{1,0:T(8,128)(2,1)} %fisher_ref.9, f32[2048,48]{1,0:T(8,128)S(1)} %shard_map.38.refs_0_), custom_call_target="tpu_custom_call" | custom-call | flops 402653184 | bytes 8388608 | tf_op jit(solution)/shard_map/pallas_call | solution.py:137
  37.8 7.0 %shard_map.41.refs_0_ = f32[2048,48]{1,0:T(8,128)S(1)} custom-call(s32[2]{0:T(128)S(1)} %pad_add_fusion.2.at_ref, bf16[48,2048]{1,0:T(8,128)(2,1)S(1)} %collective-permute-done.4.chunk_ref, bf16[2048,8192]{1,0:T(8,128)(2,1)} %fisher_ref.9, f32[2048,48]{1,0:T(8,128)S(1)} %shard_map.39.refs_0_, bf16[128,2048]{1,0:T(8,128)(2,1)S(1)} %collective-permute-done.5.refs_1_), custom_call_target="tpu_custom_call" | custom-call | flops 402653184 | bytes 8388608 | tf_op jit(solution)/shard_map/pallas_call | solution.py:137
  44.9 4.5 %shard_map.44.mine_ref = f32[48,1024]{1,0:T(8,128)S(1)} custom-call(s32[2]{0:T(128)S(1)} %pad_add_fusion.5.at_ref, bf16[48,2048]{1,0:T(8,128)(2,1)S(1)} %collective-permute-done.2.chunk_ref, bf16[2048,8192]{1,0:T(8,128)(2,1)} %fisher_ref.9, f32[2048,48]{1,0:T(8,128)S(1)} %shard_map.41.refs_0_), custom_call_target="tpu_custom_call" | custom-call | flops 201326592 | bytes 4194304 | tf_op jit(solution)/shard_map/pallas_call | solution.py:137
  49.4 1.5 %collective-permute-start.12 = (f32[48,1024]{1,0:T(8,128)S(1)}, f32[48,1024]{1,0:T(8,128)S(1)}, u32[]{:S(2)}, u32[]{:S(2)}) collective-permute-start(f32[48,1024]{1,0:T(8,128)S(1)} %shard_map.44.mine_ref), channel_id=1, source_target_pairs={{1,0},{3,2},{5,4},{7,6},{8,9},{10,11},{12,13},{14,15},{17,16},{19,... | collective-permute-start | bytes 589832 | tf_op jit(solution)/shard_map/ppermute | solution.py:223
  51.0 4.5 %shard_map.42.mine_ref = f32[48,1024]{1,0:T(8,128)S(1)} custom-call(s32[2]{0:T(128)S(1)} %pad_add_fusion.4.at_ref, bf16[48,2048]{1,0:T(8,128)(2,1)S(1)} %collective-permute-done.2.chunk_ref, bf16[2048,8192]{1,0:T(8,128)(2,1)} %fisher_ref.9, f32[2048,48]{1,0:T(8,128)S(1)} %shard_map.41.refs_0_, bf16[128,2048]{1,0:T(8,128)(2,1)S(1)} %collective-permute-done.6.refs_1_.refs_10_), custom_call_target="tpu_custom_call" | custom-call | flops 201326592 | bytes 4194304 | tf_op jit(solution)/shard_map/pallas_call | solution.py:137
  55.5 1.3 %collective-permute-start.7 = (f32[48,1024]{1,0:T(8,128)S(1)}, f32[48,1024]{1,0:T(8,128)S(1)}, u32[]{:S(2)}, u32[]{:S(2)}) collective-permute-start(f32[48,1024]{1,0:T(8,128)S(1)} %shard_map.42.mine_ref), channel_id=1, source_target_pairs={{1,0},{3,2},{5,4},{7,6},{8,9},{10,11},{12,13},{14,15},{17,16},{19,... | collective-permute-start | bytes 589832 | tf_op jit(solution)/shard_map/ppermute | solution.py:223
  56.9 4.1 %collective-permute-start.16 = (bf16[48,1024]{1,0:T(8,128)(2,1)S(1)}, bf16[48,1024]{1,0:T(8,128)(2,1)S(1)}, u32[]{:S(2)}, u32[]{:S(2)}) collective-permute-start(bf16[48,1024]{1,0:T(8,128)(2,1)S(1)} %shard_map.45), channel_id=1, source_target_pairs={{0,28},{2,30},{4,24},{6,26},{9,21},{11,23},{13,17},{15,19},{16,12}... | collective-permute-start | bytes 294920 | tf_op jit(solution)/shard_map/ppermute | solution.py:223
  61.0 1.9 %collective-permute-start.15 = (bf16[48,1024]{1,0:T(8,128)(2,1)S(1)}, bf16[48,1024]{1,0:T(8,128)(2,1)S(1)}, u32[]{:S(2)}, u32[]{:S(2)}) collective-permute-start(bf16[48,1024]{1,0:T(8,128)(2,1)S(1)} %shard_map.45), channel_id=1, source_target_pairs={{0,20},{2,22},{4,16},{6,18},{9,29},{11,31},{13,25},{15,27},{16,4},... | collective-permute-start | bytes 294920 | tf_op jit(solution)/shard_map/ppermute | solution.py:223
  62.9 1.3 %collective-permute-start.14 = (bf16[48,1024]{1,0:T(8,128)(2,1)S(1)}, bf16[48,1024]{1,0:T(8,128)(2,1)S(1)}, u32[]{:S(2)}, u32[]{:S(2)}) collective-permute-start(bf16[48,1024]{1,0:T(8,128)(2,1)S(1)} %shard_map.45), channel_id=1, source_target_pairs={{0,24},{2,26},{4,28},{6,30},{9,17},{11,19},{13,21},{15,23},{16,8},... | collective-permute-start | bytes 294920 | tf_op jit(solution)/shard_map/ppermute | solution.py:223
  64.3 2.8 %collective-permute-start.13 = (bf16[48,1024]{1,0:T(8,128)(2,1)S(1)}, bf16[48,1024]{1,0:T(8,128)(2,1)S(1)}, u32[]{:S(2)}, u32[]{:S(2)}) collective-permute-start(bf16[48,1024]{1,0:T(8,128)(2,1)S(1)} %shard_map.45), channel_id=1, source_target_pairs={{0,16},{2,18},{4,20},{6,22},{9,25},{11,27},{13,29},{15,31},{16,0},... | collective-permute-start | bytes 294920 | tf_op jit(solution)/shard_map/ppermute | solution.py:223
  67.1 2.1 %collective-permute-start.11 = (bf16[48,1024]{1,0:T(8,128)(2,1)S(1)}, bf16[48,1024]{1,0:T(8,128)(2,1)S(1)}, u32[]{:S(2)}, u32[]{:S(2)}) collective-permute-start(bf16[48,1024]{1,0:T(8,128)(2,1)S(1)} %shard_map.43.refs_0_), channel_id=1, source_target_pairs={{0,12},{2,14},{4,8},{6,10},{9,5},{11,7},{13,1},{15,3},{16,28},{18,... | collective-permute-start | bytes 294920 | tf_op jit(solution)/shard_map/ppermute | solution.py:223
  69.3 3.7 %collective-permute-start.10 = (bf16[48,1024]{1,0:T(8,128)(2,1)S(1)}, bf16[48,1024]{1,0:T(8,128)(2,1)S(1)}, u32[]{:S(2)}, u32[]{:S(2)}) collective-permute-start(bf16[48,1024]{1,0:T(8,128)(2,1)S(1)} %shard_map.43.refs_0_), channel_id=1, source_target_pairs={{0,4},{2,6},{4,0},{6,2},{9,13},{11,15},{13,9},{15,11},{16,20},{18,... | collective-permute-start | bytes 294920 | tf_op jit(solution)/shard_map/ppermute | solution.py:223
  72.9 1.3 %collective-permute-start.9 = (bf16[48,1024]{1,0:T(8,128)(2,1)S(1)}, bf16[48,1024]{1,0:T(8,128)(2,1)S(1)}, u32[]{:S(2)}, u32[]{:S(2)}) collective-permute-start(bf16[48,1024]{1,0:T(8,128)(2,1)S(1)} %shard_map.43.refs_0_), channel_id=1, source_target_pairs={{0,8},{2,10},{4,12},{6,14},{9,1},{11,3},{13,5},{15,7},{16,24},{18,... | collective-permute-start | bytes 294920 | tf_op jit(solution)/shard_map/ppermute | solution.py:223
  74.3 1.4 %collective-permute-done.10.refs_2_ = bf16[48,1024]{1,0:T(8,128)(2,1)S(1)} collective-permute-done((bf16[48,1024]{1,0:T(8,128)(2,1)S(1)}, bf16[48,1024]{1,0:T(8,128)(2,1)S(1)}, u32[]{:S(2)}, u32[]{:S(2)}) %collective-permute-start.10) | collective-permute-done | bytes 98336 | tf_op jit(solution)/shard_map/ppermute | solution.py:223
  75.8 0.7 collective-permute-done.9.refs_1_
  76.4 1.3 %shard_map.46 = f32[8,48,128]{2,1,0:T(8,128)S(1)} custom-call(s32[3]{0:T(128)S(1)} %pad_add_fusion.3.at_ref, bf16[48,1024]{1,0:T(8,128)(2,1)S(1)} %shard_map.43.refs_0_, bf16[48,1024]{1,0:T(8,128)(2,1)S(1)} %collective-permute-done.9.refs_1_, bf16[48,1024]{1,0:T(8,128)(2,1)S(1)} %collective-permute-done.10.refs_2_, ...), custom_call_target="tpu_custom_call" | custom-call | tf_op jit(solution)/shard_map/pallas_call | solution.py:191
  77.7 10.9 %all_to_all.5 = f32[8,48,128]{2,1,0:T(8,128)S(1)} all-to-all(f32[8,48,128]{2,1,0:T(8,128)S(1)} %shard_map.46), channel_id=1, replica_groups={{0,1,2,3,16,17,18,19},{4,5,6,7,20,21,22,23},{8,9,10,11,24,25,26,27},{12..., dimensions={0} | all-to-all | bytes 393216 | tf_op jit(solution)/shard_map/all_to_all | solution.py:301
  88.7 0.6 reduce_sum.9
  (31 shorter events, 1.4 us)
Async XLA Ops:
  0.0 1.0 %copy-start.1 = (bf16[96,2048]{1,0:T(8,128)(2,1)S(1)}, bf16[96,2048]{1,0:T(8,128)(2,1)}, u32[]{:S(2)}) copy-start(bf16[96,2048]{1,0:T(8,128)(2,1)} %src_ref.2) | copy-start | bytes 1179652
  1.2 16.5 %collective-permute-start.3 = (bf16[48,2048]{1,0:T(8,128)(2,1)S(1)}, bf16[48,2048]{1,0:T(8,128)(2,1)S(1)}, u32[]{:S(2)}, u32[]{:S(2)}) collective-permute-start(bf16[48,2048]{1,0:T(8,128)(2,1)S(1)} %shard_map.37), channel_id=1, source_target_pairs={{0,8},{2,10},{4,12},{6,14},{9,1},{11,3},{13,5},{15,7},{16,24},{18,... | collective-permute-start | bytes 589832 | tf_op jit(solution)/shard_map/ppermute | solution.py:223
  7.2 12.7 %collective-permute-start.1 = (bf16[48,2048]{1,0:T(8,128)(2,1)S(1)}, bf16[48,2048]{1,0:T(8,128)(2,1)S(1)}, u32[]{:S(2)}, u32[]{:S(2)}) collective-permute-start(bf16[48,2048]{1,0:T(8,128)(2,1)S(1)} %shard_map.37), channel_id=1, source_target_pairs={{0,12},{2,14},{4,8},{6,10},{9,5},{11,7},{13,1},{15,3},{16,28},{18,... | collective-permute-start | bytes 589832 | tf_op jit(solution)/shard_map/ppermute | solution.py:223
  9.5 11.0 %collective-permute-start = (bf16[48,2048]{1,0:T(8,128)(2,1)S(1)}, bf16[48,2048]{1,0:T(8,128)(2,1)}, u32[]{:S(2)}, u32[]{:S(2)}) collective-permute-start(bf16[48,2048]{1,0:T(8,128)(2,1)S(1)} %shard_map.37), channel_id=1, source_target_pairs={{0,4},{2,6},{4,0},{6,2},{9,13},{11,15},{13,9},{15,11},{16,20},{18,... | collective-permute-start | bytes 589832 | tf_op jit(solution)/shard_map/ppermute | solution.py:223
  12.2 1.6 %copy-start = (bf16[128,8192]{1,0:T(8,128)(2,1)S(1)}, bf16[128,8192]{1,0:T(8,128)(2,1)}, u32[]{:S(2)}) copy-start(bf16[128,8192]{1,0:T(8,128)(2,1)} %src_ref.3) | copy-start | bytes 6291460
  15.4 14.8 %collective-permute-start.5 = (bf16[128,2048]{1,0:T(8,128)(2,1)S(1)}, bf16[128,2048]{1,0:T(8,128)(2,1)S(1)}, u32[]{:S(2)}, u32[]{:S(2)}) collective-permute-start(bf16[128,2048]{1,0:T(8,128)(2,1)S(1)} %get-tuple-element.9), channel_id=1, source_target_pairs={{0,16},{1,17},{2,18},{3,19},{4,20},{5,21},{6,22},{7,23},{8,24},{9,... | collective-permute-start | bytes 1572872 | tf_op jit(solution)/shard_map/ppermute | solution.py:223
  16.9 34.0 %collective-permute-start.6 = (bf16[128,2048]{1,0:T(8,128)(2,1)S(1)}, bf16[128,2048]{1,0:T(8,128)(2,1)S(1)}, u32[]{:S(2)}, u32[]{:S(2)}) collective-permute-start(bf16[128,2048]{1,0:T(8,128)(2,1)S(1)} %get-tuple-element.10), channel_id=1, source_target_pairs={{0,16},{1,17},{2,18},{3,19},{4,20},{5,21},{6,22},{7,23},{8,24},{9,... | collective-permute-start | bytes 1572872 | tf_op jit(solution)/shard_map/ppermute | solution.py:223
  17.7 0.7 copy-start.2
  18.4 44.6 %collective-permute-start.8 = (bf16[128,2048]{1,0:T(8,128)(2,1)}, bf16[128,2048]{1,0:T(8,128)(2,1)S(1)}, u32[]{:S(2)}, u32[]{:S(2)}) collective-permute-start(bf16[128,2048]{1,0:T(8,128)(2,1)} %get-tuple-element.11), channel_id=1, source_target_pairs={{0,2},{1,3},{2,0},{3,1},{4,6},{5,7},{6,4},{7,5},{8,10},{9,11},{10,... | collective-permute-start | bytes 1572872 | tf_op jit(solution)/shard_map/ppermute | solution.py:223
  19.9 17.9 %collective-permute-start.4 = (bf16[48,2048]{1,0:T(8,128)(2,1)S(1)}, bf16[48,2048]{1,0:T(8,128)(2,1)S(1)}, u32[]{:S(2)}, u32[]{:S(2)}) collective-permute-start(bf16[48,2048]{1,0:T(8,128)(2,1)S(1)} %broadcast_select_fusion.chunk_ref), channel_id=1, source_target_pairs={{0,2},{1,3},{2,0},{3,1},{4,6},{5,7},{6,4},{7,5},{8,10},{9,11},{10,... | collective-permute-start | bytes 589832 | tf_op jit(solution)/shard_map/ppermute | solution.py:223
  21.5 23.4 %collective-permute-start.2 = (bf16[48,2048]{1,0:T(8,128)(2,1)S(1)}, bf16[48,2048]{1,0:T(8,128)(2,1)S(1)}, u32[]{:S(2)}, u32[]{:S(2)}) collective-permute-start(bf16[48,2048]{1,0:T(8,128)(2,1)S(1)} %broadcast_select_fusion.1.chunk_ref), channel_id=1, source_target_pairs={{0,2},{1,3},{2,0},{3,1},{4,6},{5,7},{6,4},{7,5},{8,10},{9,11},{10,... | collective-permute-start | bytes 589832 | tf_op jit(solution)/shard_map/ppermute | solution.py:223
  30.1 46.3 %collective-permute-start.17 = (bf16[128,2048]{1,0:T(8,128)(2,1)S(1)}, bf16[128,2048]{1,0:T(8,128)(2,1)S(1)}, u32[]{:S(2)}, u32[]{:S(2)}) collective-permute-start(bf16[128,2048]{1,0:T(8,128)(2,1)S(1)} %collective-permute-done.5.refs_1_), channel_id=1, source_target_pairs={{0,2},{1,3},{2,0},{3,1},{4,6},{5,7},{6,4},{7,5},{8,10},{9,11},{10,... | collective-permute-start | bytes 1572872 | tf_op jit(solution)/shard_map/ppermute | solution.py:223
  49.4 7.4 %collective-permute-start.12 = (f32[48,1024]{1,0:T(8,128)S(1)}, f32[48,1024]{1,0:T(8,128)S(1)}, u32[]{:S(2)}, u32[]{:S(2)}) collective-permute-start(f32[48,1024]{1,0:T(8,128)S(1)} %shard_map.44.mine_ref), channel_id=1, source_target_pairs={{1,0},{3,2},{5,4},{7,6},{8,9},{10,11},{12,13},{14,15},{17,16},{19,... | collective-permute-start | bytes 589832 | tf_op jit(solution)/shard_map/ppermute | solution.py:223
  55.5 8.7 %collective-permute-start.7 = (f32[48,1024]{1,0:T(8,128)S(1)}, f32[48,1024]{1,0:T(8,128)S(1)}, u32[]{:S(2)}, u32[]{:S(2)}) collective-permute-start(f32[48,1024]{1,0:T(8,128)S(1)} %shard_map.42.mine_ref), channel_id=1, source_target_pairs={{1,0},{3,2},{5,4},{7,6},{8,9},{10,11},{12,13},{14,15},{17,16},{19,... | collective-permute-start | bytes 589832 | tf_op jit(solution)/shard_map/ppermute | solution.py:223
  56.9 10.3 %collective-permute-start.16 = (bf16[48,1024]{1,0:T(8,128)(2,1)S(1)}, bf16[48,1024]{1,0:T(8,128)(2,1)S(1)}, u32[]{:S(2)}, u32[]{:S(2)}) collective-permute-start(bf16[48,1024]{1,0:T(8,128)(2,1)S(1)} %shard_map.45), channel_id=1, source_target_pairs={{0,28},{2,30},{4,24},{6,26},{9,21},{11,23},{13,17},{15,19},{16,12}... | collective-permute-start | bytes 294920 | tf_op jit(solution)/shard_map/ppermute | solution.py:223
  61.0 8.2 %collective-permute-start.15 = (bf16[48,1024]{1,0:T(8,128)(2,1)S(1)}, bf16[48,1024]{1,0:T(8,128)(2,1)S(1)}, u32[]{:S(2)}, u32[]{:S(2)}) collective-permute-start(bf16[48,1024]{1,0:T(8,128)(2,1)S(1)} %shard_map.45), channel_id=1, source_target_pairs={{0,20},{2,22},{4,16},{6,18},{9,29},{11,31},{13,25},{15,27},{16,4},... | collective-permute-start | bytes 294920 | tf_op jit(solution)/shard_map/ppermute | solution.py:223
  62.9 10.0 %collective-permute-start.14 = (bf16[48,1024]{1,0:T(8,128)(2,1)S(1)}, bf16[48,1024]{1,0:T(8,128)(2,1)S(1)}, u32[]{:S(2)}, u32[]{:S(2)}) collective-permute-start(bf16[48,1024]{1,0:T(8,128)(2,1)S(1)} %shard_map.45), channel_id=1, source_target_pairs={{0,24},{2,26},{4,28},{6,30},{9,17},{11,19},{13,21},{15,23},{16,8},... | collective-permute-start | bytes 294920 | tf_op jit(solution)/shard_map/ppermute | solution.py:223
  64.3 10.1 %collective-permute-start.13 = (bf16[48,1024]{1,0:T(8,128)(2,1)S(1)}, bf16[48,1024]{1,0:T(8,128)(2,1)S(1)}, u32[]{:S(2)}, u32[]{:S(2)}) collective-permute-start(bf16[48,1024]{1,0:T(8,128)(2,1)S(1)} %shard_map.45), channel_id=1, source_target_pairs={{0,16},{2,18},{4,20},{6,22},{9,25},{11,27},{13,29},{15,31},{16,0},... | collective-permute-start | bytes 294920 | tf_op jit(solution)/shard_map/ppermute | solution.py:223
  67.1 7.2 %collective-permute-start.11 = (bf16[48,1024]{1,0:T(8,128)(2,1)S(1)}, bf16[48,1024]{1,0:T(8,128)(2,1)S(1)}, u32[]{:S(2)}, u32[]{:S(2)}) collective-permute-start(bf16[48,1024]{1,0:T(8,128)(2,1)S(1)} %shard_map.43.refs_0_), channel_id=1, source_target_pairs={{0,12},{2,14},{4,8},{6,10},{9,5},{11,7},{13,1},{15,3},{16,28},{18,... | collective-permute-start | bytes 294920 | tf_op jit(solution)/shard_map/ppermute | solution.py:223
  69.3 6.5 %collective-permute-start.10 = (bf16[48,1024]{1,0:T(8,128)(2,1)S(1)}, bf16[48,1024]{1,0:T(8,128)(2,1)S(1)}, u32[]{:S(2)}, u32[]{:S(2)}) collective-permute-start(bf16[48,1024]{1,0:T(8,128)(2,1)S(1)} %shard_map.43.refs_0_), channel_id=1, source_target_pairs={{0,4},{2,6},{4,0},{6,2},{9,13},{11,15},{13,9},{15,11},{16,20},{18,... | collective-permute-start | bytes 294920 | tf_op jit(solution)/shard_map/ppermute | solution.py:223
  72.9 3.5 %collective-permute-start.9 = (bf16[48,1024]{1,0:T(8,128)(2,1)S(1)}, bf16[48,1024]{1,0:T(8,128)(2,1)S(1)}, u32[]{:S(2)}, u32[]{:S(2)}) collective-permute-start(bf16[48,1024]{1,0:T(8,128)(2,1)S(1)} %shard_map.43.refs_0_), channel_id=1, source_target_pairs={{0,8},{2,10},{4,12},{6,14},{9,1},{11,3},{13,5},{15,7},{16,24},{18,... | collective-permute-start | bytes 294920 | tf_op jit(solution)/shard_map/ppermute | solution.py:223

commit v5 on v0

v5 whole, which is shorter than its diff:
```python
import functools

import jax
import jax.numpy as jnp
from jax import lax
from jax.experimental import pallas as pl
from jax.experimental.pallas import tpu as pltpu
from jax.sharding import PartitionSpec as P

AXES = ("grp", "ex", "dim")
NT = (((1,), (1,)), ((), ()))
VMEM = pl.BlockSpec(memory_space=pltpu.VMEM)
SMEM = pl.BlockSpec(memory_space=pltpu.SMEM)
HBM = pl.BlockSpec(memory_space=pltpu.HBM)
ANY = pl.BlockSpec(memory_space=pl.ANY)


def limit(mib):
    return pltpu.CompilerParams(vmem_limit_bytes=mib * 1024 * 1024)


def per_device_any(queries, inverse_fisher, stored_grads):
    term_block = jnp.dot(queries, inverse_fisher, preferred_element_type=jnp.float32)
    own_panel = lax.psum_scatter(term_block, "ex", scatter_dimension=1, tiled=True).astype(
        jnp.bfloat16
    )
    partial_scores = lax.dot_general(
        lax.all_gather(own_panel, "ex", axis=1, tiled=True),
        stored_grads,
        NT,
        preferred_element_type=jnp.float32,
    )
    return lax.psum_scatter(partial_scores, "dim", scatter_dimension=0, tiled=True)


def scalars(*values):
    return jnp.stack([jnp.asarray(v, jnp.int32) for v in values])


def cut_rows_kernel(at_ref, src_ref, out_ref, sem):
    rows = out_ref.shape[0]
    start = pl.multiple_of(at_ref[0] * rows, rows)
    copy = pltpu.make_async_copy(src_ref.at[pl.ds(start, rows), :], out_ref, sem)
    copy.start()
    copy.wait()


def cut_rows(src, rows, at):
    return pl.pallas_call(
        cut_rows_kernel,
        out_shape=jax.ShapeDtypeStruct((rows, src.shape[1]), src.dtype),
        in_specs=[SMEM, HBM],
        out_specs=VMEM,
        scratch_shapes=[pltpu.SemaphoreType.DMA],
        compiler_params=limit(2),
    )(scalars(at), src)


def fisher_kernel(part, steps, has_base, at_ref, chunk_ref, fisher_ref, *refs):
    refs = list(refs)
    base_ref = refs.pop(0) if has_base else None
    out_ref, held, sem = refs
    width = chunk_ref.shape[1]
    rows, step = held.shape[1:]
    first = pl.multiple_of(at_ref[1] * rows, rows) if part else 0
    start = pl.multiple_of(at_ref[0] * width, width)
    copies = []
    for i in range(steps):
        copies.append(
            pltpu.make_async_copy(
                fisher_ref.at[pl.ds(first, rows), pl.ds(start + i * step, step)], held.at[i], sem.at[i]
            )
        )
        copies[-1].start()
    for i in range(steps):
        copies[i].wait()
        term = lax.dot_general(
            chunk_ref[:, i * step : (i + 1) * step], held[i], NT, preferred_element_type=jnp.float32
        )
        if i:
            term = term + out_ref[...]
        elif has_base:
            term = term + base_ref[:, pl.ds(first, rows)]
        out_ref[...] = term


def fisher_dot(chunk, column, fisher, base=None, half=None, step=512):
    nq, width = chunk.shape
    part = half is not None
    rows = fisher.shape[0] // 2 if part else fisher.shape[0]
    steps = width // step
    operands = [scalars(column, half if part else 0), chunk, fisher]
    operands += [] if base is None else [base]
    return pl.pallas_call(
        functools.partial(fisher_kernel, part, steps, base is not None),
        out_shape=jax.ShapeDtypeStruct((nq, rows), jnp.float32),
        in_specs=[SMEM, VMEM, HBM] + [VMEM] * (base is not None),
        out_specs=VMEM,
        scratch_shapes=[
            pltpu.VMEM((steps, rows, step), fisher.dtype),
            pltpu.SemaphoreType.DMA((steps,)),
        ],
        compiler_params=limit(34),
        cost_estimate=pl.CostEstimate(
            flops=2 * nq * width * rows, bytes_accessed=2 * width * rows, transcendentals=0
        ),
    )(*operands)


def panel_kernel(*refs):
    out_ref = refs[-1]
    width = refs[0].shape[1]
    for k in range(len(refs) // 2):
        out_ref[:, k * width : (k + 1) * width] = (refs[2 * k][...] + refs[2 * k + 1][...]).astype(out_ref.dtype)


def panel_sum(*terms):
    rows, width = terms[0].shape
    return pl.pallas_call(
        panel_kernel,
        out_shape=jax.ShapeDtypeStruct((rows, width * len(terms) // 2), jnp.bfloat16),
        in_specs=[VMEM] * len(terms),
        out_specs=VMEM,
        compiler_params=limit(2),
    )(*terms)


def score_kernel(n, at_ref, *refs):
    grads_ref, out_ref = refs[n:]
    width = refs[0].shape[1]
    total = None
    for k in range(n):
        grads = grads_ref[:, pl.ds(pl.multiple_of(at_ref[k] * width, width), width)]
        term = lax.dot_general(refs[k][...], grads, NT, preferred_element_type=jnp.float32)
        total = term if total is None else total + term
    out_ref[...] = total


def score_dot(pieces, columns, grads):
    n = len(pieces)
    rows, width = pieces[0].shape
    return pl.pallas_call(
        functools.partial(score_kernel, n),
        out_shape=jax.ShapeDtypeStruct((rows, grads.shape[0]), jnp.float32),
        in_specs=[SMEM] + [VMEM] * (n + 1),
        out_specs=VMEM,
        compiler_params=limit(8),
        cost_estimate=pl.CostEstimate(
            flops=2 * n * rows * width * grads.shape[0],
            bytes_accessed=2 * n * width * grads.shape[0],
            transcendentals=0,
        ),
    )(scalars(*columns), *pieces, grads)


def per_device_quad(nz, nx, ny, queries, inverse_fisher, stored_grads):
    nex = nz * nx
    near = nz // 2
    nq = queries.shape[0]
    y, e, d = (lax.axis_index(a) for a in AXES)
    z = e // nx
    x = e % nx
    u = jnp.where(d == 0, z, nz - 1 - z)
    owner = u < near

    def move(value, target):
        pairs = []
        for sy in range(ny):
            for sz in range(nz):
                for sx in range(nx):
                    for sd in range(2):
                        to = target(sy, sz, sx, sd)
                        if to is not None:
                            ty, tz, tx, td = to
                            pairs.append(((sy * nex + sz * nx + sx) * 2 + sd, (ty * nex + tz * nx + tx) * 2 + td))
        return lax.ppermute(value, AXES, pairs)

    def along_z(value, hops):
        def target(sy, sz, sx, sd):
            su = sz if sd == 0 else nz - 1 - sz
            if su not in hops:
                return None
            tu = hops[su]
            return sy, tu if sd == 0 else nz - 1 - tu, sx, sd

        return move(value, target)

    def swap_x(value):
        return move(value, lambda sy, sz, sx, sd: (sy, sz, 1 - sx, sd))

    def swap_y(value):
        return move(value, lambda sy, sz, sx, sd: (1 - sy, sz, sx, sd))

    def to_owner(value):
        def target(sy, sz, sx, sd):
            su = sz if sd == 0 else nz - 1 - sz
            return None if su < near else (sy, sz, sx, 1 - sd)

        return move(value, target)

    def real_plane(k):
        return jnp.where(d == 0, k, nz - 1 - k)

    def gather(own):
        first = jnp.where(owner, own, along_z(own, {0: 2, 1: 3}))
        second = jnp.where(owner, along_z(own, {0: 1, 1: 0}), along_z(own, {0: 3, 1: 2}))
        return [first, second, swap_x(first), swap_x(second)]

    planes = [real_plane(u % 2), real_plane(1 - u % 2)]
    columns = [p * nx + x_ - d * (nex // 2) for x_ in (x, 1 - x) for p in planes]

    other_grads = swap_y(stored_grads)

    pieces = gather(cut_rows(queries, nq // ny, y))
    total = None
    for piece, column in zip(pieces[:-1], columns):
        total = fisher_dot(piece, column, inverse_fisher, total)
    halves = [fisher_dot(pieces[-1], columns[-1], inverse_fisher, total, h) for h in range(2)]
    panel = panel_sum(halves[0], to_owner(halves[0]), halves[1], to_owner(halves[1]))

    pieces = gather(panel)
    other = score_dot(pieces, columns, other_grads)
    mine = score_dot(pieces, columns, stored_grads)

    def to_core_y(value):
        return move(value, lambda sy, sz, sx, sd: (sy, sz, sx, sy) if sd != sy else None)

    other = other + to_core_y(other)
    mine = mine + to_core_y(mine)
    other = move(other, lambda sy, sz, sx, sd: (1 - sy, sz, sx, sd) if sd == sy else None)
    return jnp.where(d == y, mine, other)


def solution(mesh):
    coords = [getattr(device, "coords", None) for device in mesh.devices.flat]
    nx = 2 if None in coords else len({c[0] for c in coords})
    nz = mesh.shape["ex"] // nx
    ny = mesh.shape["grp"]
    if (nz, nx, ny) == (4, 2, 2):
        body = functools.partial(per_device_quad, nz, nx, ny)
    else:
        body = per_device_any
    return jax.shard_map(
        body,
        mesh=mesh,
        in_specs=(P(None, "ex"), P("ex", "dim"), P(("grp", "ex"), "dim")),
        out_specs=P("dim", ("grp", "ex")),
        check_vma=False,
    )
```

time: 164 us -> 77.2 us (0.47)
  waiting for transfers between devices: 128 us -> 17.3 us
  starting transfers between devices: 0.09 us -> 33 us
  Pallas kernels: 0 us -> 23.9 us
  matrix products: 20.7 us -> 0 us
  between operations: 13.1 us -> 0.26 us
    reduce_scatter x2 -> x0, waiting for transfers between devices: 84.1 us -> none  [the longest x1 77.7 us: per_device(): lax.psum_scatter(term_block, 'ex', scatter_dimension=1, tiled=True)]
    all_gather x1 -> x0, waiting for transfers between devices: 44.1 us -> none  [per_device(): lax.all_gather(own_panel, 'ex', axis=1, tiled=True)]
    ppermute x0 -> x16, starting transfers between devices: none -> 33 us  [move(): return lax.ppermute(value, AXES, pairs)]
    pallas_call x0 -> x9, Pallas kernels: none -> 23.9 us  [the longest x5 20.9 us: fisher_dot(): pl.pallas_call(functools.partial(fisher_kernel, part, steps, base is not...]
    dot_general x2 -> x0, matrix products: 20.7 us -> none  [the longest x1 17.8 us: per_device(): jnp.dot(queries, inverse_fisher, preferred_element_type=jnp.float32)]
    ppermute x0 -> x16, waiting for transfers between devices: none -> 17.3 us  [move(): return lax.ppermute(value, AXES, pairs)]
    convert_element_type x1 -> x0, other arithmetic: 1.71 us -> none  [per_device(): lax.psum_scatter(term_block, 'ex', scatter_dimension=1, tiled=True)]
  transfers between devices with their start and end apart: 3 -> 16, of which waited for: 3 -> 7; matrix products, arithmetic and copies ran while one was open for 0% -> 1% of each run, Pallas kernels for 0% -> 29%
where the time goes in v5:
time: 77.2 us; the launch traced here: 76.6 us
  starting transfers between devices  33 us (43%)
  Pallas kernels  23.9 us (31%)
  waiting for transfers between devices  17.3 us (22%)
  other arithmetic  1.16 us (2%)
  local copies, waits for them, and re-layouts  1 us (1%)
    ppermute x16, starting transfers between devices, move(): return lax.ppermute(value, AXES, pairs)  33 us
    pallas_call x5, Pallas kernels, fisher_dot(): pl.pallas_call(functools.partial(fisher_kernel, part, steps, base is not...  20.9 us
    ppermute x16, waiting for transfers between devices, move(): return lax.ppermute(value, AXES, pairs)  17.3 us
    pallas_call x2, Pallas kernels, score_dot(): pl.pallas_call(functools.partial(score_kernel, n), out_shape=jax.ShapeDty...  2.75 us
  transfers between devices with their start and end apart: 16, of which 7 were waited for; matrix products, arithmetic and copies ran while one was open for 1% of the time, Pallas kernels for 29%

profile of v5, /device:TPU:0, one launch (start us, length us, event | category | flops | bytes accessed | tf_op | source)
XLA Modules:
  0.0 76.6 jit_solution(8360586379265903842)
XLA Ops:
  0.0 1.0 %copy-done.1 = bf16[96,2048]{1,0:T(8,128)(2,1)S(1)} copy-done((bf16[96,2048]{1,0:T(8,128)(2,1)S(1)}, bf16[96,2048]{1,0:T(8,128)(2,1)}, u32[]{:S(2)}) %copy-start.1) | copy-done | bytes 393240
  1.2 4.9 %collective-permute-start = (bf16[48,2048]{1,0:T(8,128)(2,1)S(1)}, bf16[48,2048]{1,0:T(8,128)(2,1)S(1)}, u32[]{:S(2)}, u32[]{:S(2)}) collective-permute-start(bf16[48,2048]{1,0:T(8,128)(2,1)S(1)} %shard_map.37), channel_id=1, source_target_pairs={{0,4},{2,6},{4,0},{6,2},{9,13},{11,15},{13,9},{15,11},{16,20},{18,... | collective-permute-start | bytes 589832 | tf_op jit(solution)/shard_map/ppermute | solution.py:176
  6.2 2.7 %collective-permute-start.1 = (bf16[48,2048]{1,0:T(8,128)(2,1)S(1)}, bf16[48,2048]{1,0:T(8,128)(2,1)S(1)}, u32[]{:S(2)}, u32[]{:S(2)}) collective-permute-start(bf16[48,2048]{1,0:T(8,128)(2,1)S(1)} %shard_map.37), channel_id=1, source_target_pairs={{0,12},{2,14},{4,8},{6,10},{9,5},{11,7},{13,1},{15,3},{16,28},{18,... | collective-permute-start | bytes 589832 | tf_op jit(solution)/shard_map/ppermute | solution.py:176
  8.9 1.3 %collective-permute-start.3 = (bf16[48,2048]{1,0:T(8,128)(2,1)S(1)}, bf16[48,2048]{1,0:T(8,128)(2,1)S(1)}, u32[]{:S(2)}, u32[]{:S(2)}) collective-permute-start(bf16[48,2048]{1,0:T(8,128)(2,1)S(1)} %shard_map.37), channel_id=1, source_target_pairs={{0,8},{2,10},{4,12},{6,14},{9,1},{11,3},{13,5},{15,7},{16,24},{18,... | collective-permute-start | bytes 589832 | tf_op jit(solution)/shard_map/ppermute | solution.py:176
  10.2 1.6 %collective-permute-start.13 = (bf16[128,8192]{1,0:T(8,128)(2,1)}, bf16[128,8192]{1,0:T(8,128)(2,1)S(1)}, u32[]{:S(2)}, u32[]{:S(2)}) collective-permute-start(bf16[128,8192]{1,0:T(8,128)(2,1)} %refs_4_.1), channel_id=1, source_target_pairs={{0,16},{1,17},{2,18},{3,19},{4,20},{5,21},{6,22},{7,23},{8,24},{9,... | collective-permute-start | bytes 6291464 | tf_op jit(solution)/shard_map/ppermute | solution.py:176
  12.1 2.1 %collective-permute-done.3 = bf16[48,2048]{1,0:T(8,128)(2,1)S(1)} collective-permute-done((bf16[48,2048]{1,0:T(8,128)(2,1)S(1)}, bf16[48,2048]{1,0:T(8,128)(2,1)S(1)}, u32[]{:S(2)}, u32[]{:S(2)}) %collective-permute-start.3) | collective-permute-done | bytes 196640 | tf_op jit(solution)/shard_map/ppermute | solution.py:176
  14.2 1.6 %collective-permute-start.4 = (bf16[48,2048]{1,0:T(8,128)(2,1)S(1)}, bf16[48,2048]{1,0:T(8,128)(2,1)S(1)}, u32[]{:S(2)}, u32[]{:S(2)}) collective-permute-start(bf16[48,2048]{1,0:T(8,128)(2,1)S(1)} %broadcast_select_fusion.2.chunk_ref), channel_id=1, source_target_pairs={{0,2},{1,3},{2,0},{3,1},{4,6},{5,7},{6,4},{7,5},{8,10},{9,11},{10,... | collective-permute-start | bytes 589832 | tf_op jit(solution)/shard_map/ppermute | solution.py:176
  15.8 0.6 collective-permute-start.2
  16.5 4.8 %shard_map.38.refs_0_ = f32[48,2048]{1,0:T(8,128)S(1)} custom-call(s32[2]{0:T(128)S(1)} %pad_add_fusion.at_ref, bf16[48,2048]{1,0:T(8,128)(2,1)S(1)} %broadcast_select_fusion.2.chunk_ref, bf16[2048,8192]{1,0:T(8,128)(2,1)} %fisher_ref.9), custom_call_target="tpu_custom_call" | custom-call | flops 402653184 | bytes 8388608 | tf_op jit(solution)/shard_map/pallas_call | solution.py:94
  21.3 4.8 %shard_map.39.refs_0_ = f32[48,2048]{1,0:T(8,128)S(1)} custom-call(s32[2]{0:T(128)S(1)} %pad_add_fusion.1.at_ref, bf16[48,2048]{1,0:T(8,128)(2,1)S(1)} %broadcast_select_fusion.3.chunk_ref, bf16[2048,8192]{1,0:T(8,128)(2,1)} %fisher_ref.9, f32[48,2048]{1,0:T(8,128)S(1)} %shard_map.38.refs_0_), custom_call_target="tpu_custom_call" | custom-call | flops 402653184 | bytes 8388608 | tf_op jit(solution)/shard_map/pallas_call | solution.py:94
  26.2 4.8 %shard_map.40.refs_0_ = f32[48,2048]{1,0:T(8,128)S(1)} custom-call(s32[2]{0:T(128)S(1)} %pad_add_fusion.2.at_ref, bf16[48,2048]{1,0:T(8,128)(2,1)S(1)} %collective-permute-done.4.chunk_ref, bf16[2048,8192]{1,0:T(8,128)(2,1)} %fisher_ref.9, f32[48,2048]{1,0:T(8,128)S(1)} %shard_map.39.refs_0_), custom_call_target="tpu_custom_call" | custom-call | flops 402653184 | bytes 8388608 | tf_op jit(solution)/shard_map/pallas_call | solution.py:94
  31.0 3.2 %shard_map.41.refs_0_ = f32[48,1024]{1,0:T(8,128)S(1)} custom-call(s32[2]{0:T(128)S(1)} %pad_add_fusion.3.at_ref, bf16[48,2048]{1,0:T(8,128)(2,1)S(1)} %collective-permute-done.2.chunk_ref, bf16[2048,8192]{1,0:T(8,128)(2,1)} %fisher_ref.9, f32[48,2048]{1,0:T(8,128)S(1)} %shard_map.40.refs_0_), custom_call_target="tpu_custom_call" | custom-call | flops 201326592 | bytes 4194304 | tf_op jit(solution)/shard_map/pallas_call | solution.py:94
  34.2 1.3 %collective-permute-start.5 = (f32[48,1024]{1,0:T(8,128)S(1)}, f32[48,1024]{1,0:T(8,128)S(1)}, u32[]{:S(2)}, u32[]{:S(2)}) collective-permute-start(f32[48,1024]{1,0:T(8,128)S(1)} %shard_map.41.refs_0_), channel_id=1, source_target_pairs={{1,0},{3,2},{5,4},{7,6},{8,9},{10,11},{12,13},{14,15},{17,16},{19,... | collective-permute-start | bytes 589832 | tf_op jit(solution)/shard_map/ppermute | solution.py:176
  35.5 3.2 %shard_map.42.refs_2_ = f32[48,1024]{1,0:T(8,128)S(1)} custom-call(s32[2]{0:T(128)S(1)} %pad_add_fusion.5.at_ref, bf16[48,2048]{1,0:T(8,128)(2,1)S(1)} %collective-permute-done.2.chunk_ref, bf16[2048,8192]{1,0:T(8,128)(2,1)} %fisher_ref.9, f32[48,2048]{1,0:T(8,128)S(1)} %shard_map.40.refs_0_), custom_call_target="tpu_custom_call" | custom-call | flops 201326592 | bytes 4194304 | tf_op jit(solution)/shard_map/pallas_call | solution.py:94
  38.7 1.3 %collective-permute-start.6 = (f32[48,1024]{1,0:T(8,128)S(1)}, f32[48,1024]{1,0:T(8,128)S(1)}, u32[]{:S(2)}, u32[]{:S(2)}) collective-permute-start(f32[48,1024]{1,0:T(8,128)S(1)} %shard_map.42.refs_2_), channel_id=1, source_target_pairs={{1,0},{3,2},{5,4},{7,6},{8,9},{10,11},{12,13},{14,15},{17,16},{19,... | collective-permute-start | bytes 589832 | tf_op jit(solution)/shard_map/ppermute | solution.py:176
  40.0 0.3 collective-permute-done.5.refs_1_
  40.3 4.5 %collective-permute-done.6.refs_3_ = f32[48,1024]{1,0:T(8,128)S(1)} collective-permute-done((f32[48,1024]{1,0:T(8,128)S(1)}, f32[48,1024]{1,0:T(8,128)S(1)}, u32[]{:S(2)}, u32[]{:S(2)}) %collective-permute-start.6) | collective-permute-done | bytes 196640 | tf_op jit(solution)/shard_map/ppermute | solution.py:176
  44.9 2.6 %collective-permute-start.7 = (bf16[48,2048]{1,0:T(8,128)(2,1)S(1)}, bf16[48,2048]{1,0:T(8,128)(2,1)S(1)}, u32[]{:S(2)}, u32[]{:S(2)}) collective-permute-start(bf16[48,2048]{1,0:T(8,128)(2,1)S(1)} %shard_map.43), channel_id=1, source_target_pairs={{0,8},{2,10},{4,12},{6,14},{9,1},{11,3},{13,5},{15,7},{16,24},{18,... | collective-permute-start | bytes 589832 | tf_op jit(solution)/shard_map/ppermute | solution.py:176
  47.6 4.6 %collective-permute-start.8 = (bf16[48,2048]{1,0:T(8,128)(2,1)S(1)}, bf16[48,2048]{1,0:T(8,128)(2,1)S(1)}, u32[]{:S(2)}, u32[]{:S(2)}) collective-permute-start(bf16[48,2048]{1,0:T(8,128)(2,1)S(1)} %shard_map.43), channel_id=1, source_target_pairs={{0,4},{2,6},{4,0},{6,2},{9,13},{11,15},{13,9},{15,11},{16,20},{18,... | collective-permute-start | bytes 589832 | tf_op jit(solution)/shard_map/ppermute | solution.py:176
  52.2 1.3 %collective-permute-start.9 = (bf16[48,2048]{1,0:T(8,128)(2,1)S(1)}, bf16[48,2048]{1,0:T(8,128)(2,1)S(1)}, u32[]{:S(2)}, u32[]{:S(2)}) collective-permute-start(bf16[48,2048]{1,0:T(8,128)(2,1)S(1)} %shard_map.43), channel_id=1, source_target_pairs={{0,12},{2,14},{4,8},{6,10},{9,5},{11,7},{13,1},{15,3},{16,28},{18,... | collective-permute-start | bytes 589832 | tf_op jit(solution)/shard_map/ppermute | solution.py:176
  53.6 1.6 %collective-permute-start.10 = (bf16[48,2048]{1,0:T(8,128)(2,1)S(1)}, bf16[48,2048]{1,0:T(8,128)(2,1)S(1)}, u32[]{:S(2)}, u32[]{:S(2)}) collective-permute-start(bf16[48,2048]{1,0:T(8,128)(2,1)S(1)} %broadcast_select_fusion.1.refs_0_), channel_id=1, source_target_pairs={{0,2},{1,3},{2,0},{3,1},{4,6},{5,7},{6,4},{7,5},{8,10},{9,11},{10,... | collective-permute-start | bytes 589832 | tf_op jit(solution)/shard_map/ppermute | solution.py:176
  55.1 3.9 %collective-permute-done.8 = bf16[48,2048]{1,0:T(8,128)(2,1)S(1)} collective-permute-done((bf16[48,2048]{1,0:T(8,128)(2,1)S(1)}, bf16[48,2048]{1,0:T(8,128)(2,1)S(1)}, u32[]{:S(2)}, u32[]{:S(2)}) %collective-permute-start.8) | collective-permute-done | bytes 196640 | tf_op jit(solution)/shard_map/ppermute | solution.py:176
  59.0 1.6 %collective-permute-start.11 = (bf16[48,2048]{1,0:T(8,128)(2,1)S(1)}, bf16[48,2048]{1,0:T(8,128)(2,1)S(1)}, u32[]{:S(2)}, u32[]{:S(2)}) collective-permute-start(bf16[48,2048]{1,0:T(8,128)(2,1)S(1)} %broadcast_select_fusion.refs_1_), channel_id=1, source_target_pairs={{0,2},{1,3},{2,0},{3,1},{4,6},{5,7},{6,4},{7,5},{8,10},{9,11},{10,... | collective-permute-start | bytes 589832 | tf_op jit(solution)/shard_map/ppermute | solution.py:176
  60.7 0.5 collective-permute-done.10.refs_2_
  61.2 4.4 %collective-permute-done.11.refs_3_ = bf16[48,2048]{1,0:T(8,128)(2,1)S(1)} collective-permute-done((bf16[48,2048]{1,0:T(8,128)(2,1)S(1)}, bf16[48,2048]{1,0:T(8,128)(2,1)S(1)}, u32[]{:S(2)}, u32[]{:S(2)}) %collective-permute-start.11) | collective-permute-done | bytes 196640 | tf_op jit(solution)/shard_map/ppermute | solution.py:176
  65.6 1.4 %shard_map.45 = f32[48,128]{1,0:T(8,128)S(1)} custom-call(s32[4]{0:T(128)S(1)} %pad_add_fusion.4.at_ref, bf16[48,2048]{1,0:T(8,128)(2,1)S(1)} %broadcast_select_fusion.1.refs_0_, bf16[48,2048]{1,0:T(8,128)(2,1)S(1)} %broadcast_select_fusion.refs_1_, bf16[48,2048]{1,0:T(8,128)(2,1)S(1)} %collective-permute-done.10.refs_2_, ...), custom_call_target="tpu_custom_call" | custom-call | flops 100663296 | bytes 2097152 | tf_op jit(solution)/shard_map/pallas_call | solution.py:142
  67.0 1.3 %collective-permute-start.14 = (f32[48,128]{1,0:T(8,128)S(1)}, f32[48,128]{1,0:T(8,128)S(1)}, u32[]{:S(2)}, u32[]{:S(2)}) collective-permute-start(f32[48,128]{1,0:T(8,128)S(1)} %shard_map.45), channel_id=1, source_target_pairs={{1,0},{3,2},{5,4},{7,6},{9,8},{11,10},{13,12},{15,14},{16,17},{18,... | collective-permute-start | bytes 73736 | tf_op jit(solution)/shard_map/ppermute | solution.py:176
  68.3 1.4 %shard_map.44 = f32[48,128]{1,0:T(8,128)S(1)} custom-call(s32[4]{0:T(128)S(1)} %pad_add_fusion.4.at_ref, bf16[48,2048]{1,0:T(8,128)(2,1)S(1)} %broadcast_select_fusion.1.refs_0_, bf16[48,2048]{1,0:T(8,128)(2,1)S(1)} %broadcast_select_fusion.refs_1_, bf16[48,2048]{1,0:T(8,128)(2,1)S(1)} %collective-permute-done.10.refs_2_, ...), custom_call_target="tpu_custom_call" | custom-call | flops 100663296 | bytes 2097152 | tf_op jit(solution)/shard_map/pallas_call | solution.py:142
  69.7 1.3 %collective-permute-start.12 = (f32[48,128]{1,0:T(8,128)S(1)}, f32[48,128]{1,0:T(8,128)S(1)}, u32[]{:S(2)}, u32[]{:S(2)}) collective-permute-start(f32[48,128]{1,0:T(8,128)S(1)} %shard_map.44), channel_id=1, source_target_pairs={{1,0},{3,2},{5,4},{7,6},{9,8},{11,10},{13,12},{15,14},{16,17},{18,... | collective-permute-start | bytes 73736 | tf_op jit(solution)/shard_map/ppermute | solution.py:176
  71.0 3.4 %collective-permute-start.15 = (f32[48,128]{1,0:T(8,128)S(1)}, f32[48,128]{1,0:T(8,128)S(1)}, u32[]{:S(2)}, u32[]{:S(2)}) collective-permute-start(f32[48,128]{1,0:T(8,128)S(1)} %add.34), channel_id=1, source_target_pairs={{0,16},{2,18},{4,20},{6,22},{8,24},{10,26},{12,28},{14,30},{17,1},... | collective-permute-start | bytes 73736 | tf_op jit(solution)/shard_map/ppermute | solution.py:176
  74.5 1.5 %collective-permute-done.15 = f32[48,128]{1,0:T(8,128)S(1)} collective-permute-done((f32[48,128]{1,0:T(8,128)S(1)}, f32[48,128]{1,0:T(8,128)S(1)}, u32[]{:S(2)}, u32[]{:S(2)}) %collective-permute-start.15) | collective-permute-done | bytes 24608 | tf_op jit(solution)/shard_map/ppermute | solution.py:176
  75.9 0.6 add_select_fusion
  (25 shorter events, 0.8 us)
Async XLA Ops:
  0.0 1.0 %copy-start.1 = (bf16[96,2048]{1,0:T(8,128)(2,1)S(1)}, bf16[96,2048]{1,0:T(8,128)(2,1)}, u32[]{:S(2)}) copy-start(bf16[96,2048]{1,0:T(8,128)(2,1)} %src_ref.1) | copy-start | bytes 1179652
  1.2 14.6 %collective-permute-start = (bf16[48,2048]{1,0:T(8,128)(2,1)S(1)}, bf16[48,2048]{1,0:T(8,128)(2,1)S(1)}, u32[]{:S(2)}, u32[]{:S(2)}) collective-permute-start(bf16[48,2048]{1,0:T(8,128)(2,1)S(1)} %shard_map.37), channel_id=1, source_target_pairs={{0,4},{2,6},{4,0},{6,2},{9,13},{11,15},{13,9},{15,11},{16,20},{18,... | collective-permute-start | bytes 589832 | tf_op jit(solution)/shard_map/ppermute | solution.py:176
  6.2 9.6 %collective-permute-start.1 = (bf16[48,2048]{1,0:T(8,128)(2,1)S(1)}, bf16[48,2048]{1,0:T(8,128)(2,1)S(1)}, u32[]{:S(2)}, u32[]{:S(2)}) collective-permute-start(bf16[48,2048]{1,0:T(8,128)(2,1)S(1)} %shard_map.37), channel_id=1, source_target_pairs={{0,12},{2,14},{4,8},{6,10},{9,5},{11,7},{13,1},{15,3},{16,28},{18,... | collective-permute-start | bytes 589832 | tf_op jit(solution)/shard_map/ppermute | solution.py:176
  8.9 5.3 %collective-permute-start.3 = (bf16[48,2048]{1,0:T(8,128)(2,1)S(1)}, bf16[48,2048]{1,0:T(8,128)(2,1)S(1)}, u32[]{:S(2)}, u32[]{:S(2)}) collective-permute-start(bf16[48,2048]{1,0:T(8,128)(2,1)S(1)} %shard_map.37), channel_id=1, source_target_pairs={{0,8},{2,10},{4,12},{6,14},{9,1},{11,3},{13,5},{15,7},{16,24},{18,... | collective-permute-start | bytes 589832 | tf_op jit(solution)/shard_map/ppermute | solution.py:176
  10.2 55.4 %collective-permute-start.13 = (bf16[128,8192]{1,0:T(8,128)(2,1)}, bf16[128,8192]{1,0:T(8,128)(2,1)S(1)}, u32[]{:S(2)}, u32[]{:S(2)}) collective-permute-start(bf16[128,8192]{1,0:T(8,128)(2,1)} %refs_4_.1), channel_id=1, source_target_pairs={{0,16},{1,17},{2,18},{3,19},{4,20},{5,21},{6,22},{7,23},{8,24},{9,... | collective-permute-start | bytes 6291464 | tf_op jit(solution)/shard_map/ppermute | solution.py:176
  14.2 11.9 %collective-permute-start.4 = (bf16[48,2048]{1,0:T(8,128)(2,1)S(1)}, bf16[48,2048]{1,0:T(8,128)(2,1)S(1)}, u32[]{:S(2)}, u32[]{:S(2)}) collective-permute-start(bf16[48,2048]{1,0:T(8,128)(2,1)S(1)} %broadcast_select_fusion.2.chunk_ref), channel_id=1, source_target_pairs={{0,2},{1,3},{2,0},{3,1},{4,6},{5,7},{6,4},{7,5},{8,10},{9,11},{10,... | collective-permute-start | bytes 589832 | tf_op jit(solution)/shard_map/ppermute | solution.py:176
  15.8 15.2 %collective-permute-start.2 = (bf16[48,2048]{1,0:T(8,128)(2,1)S(1)}, bf16[48,2048]{1,0:T(8,128)(2,1)S(1)}, u32[]{:S(2)}, u32[]{:S(2)}) collective-permute-start(bf16[48,2048]{1,0:T(8,128)(2,1)S(1)} %broadcast_select_fusion.3.chunk_ref), channel_id=1, source_target_pairs={{0,2},{1,3},{2,0},{3,1},{4,6},{5,7},{6,4},{7,5},{8,10},{9,11},{10,... | collective-permute-start | bytes 589832 | tf_op jit(solution)/shard_map/ppermute | solution.py:176
  34.2 6.1 %collective-permute-start.5 = (f32[48,1024]{1,0:T(8,128)S(1)}, f32[48,1024]{1,0:T(8,128)S(1)}, u32[]{:S(2)}, u32[]{:S(2)}) collective-permute-start(f32[48,1024]{1,0:T(8,128)S(1)} %shard_map.41.refs_0_), channel_id=1, source_target_pairs={{1,0},{3,2},{5,4},{7,6},{8,9},{10,11},{12,13},{14,15},{17,16},{19,... | collective-permute-start | bytes 589832 | tf_op jit(solution)/shard_map/ppermute | solution.py:176
  38.7 6.2 %collective-permute-start.6 = (f32[48,1024]{1,0:T(8,128)S(1)}, f32[48,1024]{1,0:T(8,128)S(1)}, u32[]{:S(2)}, u32[]{:S(2)}) collective-permute-start(f32[48,1024]{1,0:T(8,128)S(1)} %shard_map.42.refs_2_), channel_id=1, source_target_pairs={{1,0},{3,2},{5,4},{7,6},{8,9},{10,11},{12,13},{14,15},{17,16},{19,... | collective-permute-start | bytes 589832 | tf_op jit(solution)/shard_map/ppermute | solution.py:176
  44.9 23.4 %copy-start = (bf16[128,8192]{1,0:T(8,128)(2,1)S(1)}, bf16[128,8192]{1,0:T(8,128)(2,1)}, u32[]{:S(2)}) copy-start(bf16[128,8192]{1,0:T(8,128)(2,1)} %refs_4_.1) | copy-start | bytes 6291460
  44.9 8.6 %collective-permute-start.7 = (bf16[48,2048]{1,0:T(8,128)(2,1)S(1)}, bf16[48,2048]{1,0:T(8,128)(2,1)S(1)}, u32[]{:S(2)}, u32[]{:S(2)}) collective-permute-start(bf16[48,2048]{1,0:T(8,128)(2,1)S(1)} %shard_map.43), channel_id=1, source_target_pairs={{0,8},{2,10},{4,12},{6,14},{9,1},{11,3},{13,5},{15,7},{16,24},{18,... | collective-permute-start | bytes 589832 | tf_op jit(solution)/shard_map/ppermute | solution.py:176
  47.6 11.4 %collective-permute-start.8 = (bf16[48,2048]{1,0:T(8,128)(2,1)S(1)}, bf16[48,2048]{1,0:T(8,128)(2,1)S(1)}, u32[]{:S(2)}, u32[]{:S(2)}) collective-permute-start(bf16[48,2048]{1,0:T(8,128)(2,1)S(1)} %shard_map.43), channel_id=1, source_target_pairs={{0,4},{2,6},{4,0},{6,2},{9,13},{11,15},{13,9},{15,11},{16,20},{18,... | collective-permute-start | bytes 589832 | tf_op jit(solution)/shard_map/ppermute | solution.py:176
  52.2 6.8 %collective-permute-start.9 = (bf16[48,2048]{1,0:T(8,128)(2,1)S(1)}, bf16[48,2048]{1,0:T(8,128)(2,1)S(1)}, u32[]{:S(2)}, u32[]{:S(2)}) collective-permute-start(bf16[48,2048]{1,0:T(8,128)(2,1)S(1)} %shard_map.43), channel_id=1, source_target_pairs={{0,12},{2,14},{4,8},{6,10},{9,5},{11,7},{13,1},{15,3},{16,28},{18,... | collective-permute-start | bytes 589832 | tf_op jit(solution)/shard_map/ppermute | solution.py:176
  53.6 7.6 %collective-permute-start.10 = (bf16[48,2048]{1,0:T(8,128)(2,1)S(1)}, bf16[48,2048]{1,0:T(8,128)(2,1)S(1)}, u32[]{:S(2)}, u32[]{:S(2)}) collective-permute-start(bf16[48,2048]{1,0:T(8,128)(2,1)S(1)} %broadcast_select_fusion.1.refs_0_), channel_id=1, source_target_pairs={{0,2},{1,3},{2,0},{3,1},{4,6},{5,7},{6,4},{7,5},{8,10},{9,11},{10,... | collective-permute-start | bytes 589832 | tf_op jit(solution)/shard_map/ppermute | solution.py:176
  59.0 6.6 %collective-permute-start.11 = (bf16[48,2048]{1,0:T(8,128)(2,1)S(1)}, bf16[48,2048]{1,0:T(8,128)(2,1)S(1)}, u32[]{:S(2)}, u32[]{:S(2)}) collective-permute-start(bf16[48,2048]{1,0:T(8,128)(2,1)S(1)} %broadcast_select_fusion.refs_1_), channel_id=1, source_target_pairs={{0,2},{1,3},{2,0},{3,1},{4,6},{5,7},{6,4},{7,5},{8,10},{9,11},{10,... | collective-permute-start | bytes 589832 | tf_op jit(solution)/shard_map/ppermute | solution.py:176
  67.0 4.0 %collective-permute-start.14 = (f32[48,128]{1,0:T(8,128)S(1)}, f32[48,128]{1,0:T(8,128)S(1)}, u32[]{:S(2)}, u32[]{:S(2)}) collective-permute-start(f32[48,128]{1,0:T(8,128)S(1)} %shard_map.45), channel_id=1, source_target_pairs={{1,0},{3,2},{5,4},{7,6},{9,8},{11,10},{13,12},{15,14},{16,17},{18,... | collective-permute-start | bytes 73736 | tf_op jit(solution)/shard_map/ppermute | solution.py:176
  69.7 4.8 %collective-permute-start.12 = (f32[48,128]{1,0:T(8,128)S(1)}, f32[48,128]{1,0:T(8,128)S(1)}, u32[]{:S(2)}, u32[]{:S(2)}) collective-permute-start(f32[48,128]{1,0:T(8,128)S(1)} %shard_map.44), channel_id=1, source_target_pairs={{1,0},{3,2},{5,4},{7,6},{9,8},{11,10},{13,12},{15,14},{16,17},{18,... | collective-permute-start | bytes 73736 | tf_op jit(solution)/shard_map/ppermute | solution.py:176
  71.0 4.9 %collective-permute-start.15 = (f32[48,128]{1,0:T(8,128)S(1)}, f32[48,128]{1,0:T(8,128)S(1)}, u32[]{:S(2)}, u32[]{:S(2)}) collective-permute-start(f32[48,128]{1,0:T(8,128)S(1)} %add.34), channel_id=1, source_target_pairs={{0,16},{2,18},{4,20},{6,22},{8,24},{10,26},{12,28},{14,30},{17,1},... | collective-permute-start | bytes 73736 | tf_op jit(solution)/shard_map/ppermute | solution.py:176

commit v6 on v5

v6 whole, which is shorter than its diff:
```python
import functools

import jax
import jax.numpy as jnp
from jax import lax
from jax.experimental import pallas as pl
from jax.experimental.pallas import tpu as pltpu
from jax.sharding import PartitionSpec as P

AXES = ("grp", "ex", "dim")
NT = (((1,), (1,)), ((), ()))
VMEM = pl.BlockSpec(memory_space=pltpu.VMEM)
SMEM = pl.BlockSpec(memory_space=pltpu.SMEM)
HBM = pl.BlockSpec(memory_space=pltpu.HBM)
ANY = pl.BlockSpec(memory_space=pl.ANY)


def limit(mib):
    return pltpu.CompilerParams(vmem_limit_bytes=mib * 1024 * 1024)


def per_device_any(queries, inverse_fisher, stored_grads):
    term_block = jnp.dot(queries, inverse_fisher, preferred_element_type=jnp.float32)
    own_panel = lax.psum_scatter(term_block, "ex", scatter_dimension=1, tiled=True).astype(
        jnp.bfloat16
    )
    partial_scores = lax.dot_general(
        lax.all_gather(own_panel, "ex", axis=1, tiled=True),
        stored_grads,
        NT,
        preferred_element_type=jnp.float32,
    )
    return lax.psum_scatter(partial_scores, "dim", scatter_dimension=0, tiled=True)


def scalars(*values):
    return jnp.stack([jnp.asarray(v, jnp.int32) for v in values])


def cut_rows_kernel(at_ref, src_ref, out_ref, sem):
    rows = out_ref.shape[0]
    start = pl.multiple_of(at_ref[0] * rows, rows)
    copy = pltpu.make_async_copy(src_ref.at[pl.ds(start, rows), :], out_ref, sem)
    copy.start()
    copy.wait()


def cut_rows(src, rows, at):
    return pl.pallas_call(
        cut_rows_kernel,
        out_shape=jax.ShapeDtypeStruct((rows, src.shape[1]), src.dtype),
        in_specs=[SMEM, HBM],
        out_specs=VMEM,
        scratch_shapes=[pltpu.SemaphoreType.DMA],
        compiler_params=limit(2),
    )(scalars(at), src)


def start_blocks(fisher_ref, at, held_ref, sem):
    steps = sem.shape[0]
    rows, width = held_ref.shape
    step = rows // steps
    columns = pl.ds(pl.multiple_of(at * width, width), width)
    copies = []
    for i in range(steps):
        block = pl.ds(i * step, step)
        copies.append(pltpu.make_async_copy(fisher_ref.at[block, columns], held_ref.at[block, :], sem.at[i]))
        copies[-1].start()
    return copies


def times(chunk_ref, fisher):
    return lax.dot_general(chunk_ref[...], fisher, NT, preferred_element_type=jnp.float32)


def load_kernel(n, at_ref, fisher_ref, *refs):
    copies = []
    for k in range(n):
        copies += start_blocks(fisher_ref, at_ref[k], refs[k], refs[n].at[k])
    for copy in copies:
        copy.wait()


def load(fisher, columns, width, steps=4):
    n = len(columns)
    return pl.pallas_call(
        functools.partial(load_kernel, n),
        out_shape=[jax.ShapeDtypeStruct((fisher.shape[0], width), fisher.dtype)] * n,
        in_specs=[SMEM, HBM],
        out_specs=[VMEM] * n,
        scratch_shapes=[pltpu.SemaphoreType.DMA((n, steps))],
        compiler_params=limit(34),
        cost_estimate=pl.CostEstimate(
            flops=0, bytes_accessed=2 * n * width * fisher.shape[0], transcendentals=0
        ),
    )(scalars(*columns), fisher)


def fisher_first_kernel(at_ref, chunk0, chunk1, block0, block1, fisher_ref, out_ref, next_ref, sem):
    copies = start_blocks(fisher_ref, at_ref[0], next_ref, sem)
    step = block0.shape[0] // sem.shape[0]
    for i in range(sem.shape[0]):
        rows = slice(i * step, (i + 1) * step)
        out_ref[:, rows] = times(chunk0, block0[rows, :]) + times(chunk1, block1[rows, :])
    for copy in copies:
        copy.wait()


def fisher_first(chunks, blocks, column, fisher, steps=4):
    nq, width = chunks[0].shape
    rows = fisher.shape[0]
    return pl.pallas_call(
        fisher_first_kernel,
        out_shape=[
            jax.ShapeDtypeStruct((nq, rows), jnp.float32),
            jax.ShapeDtypeStruct((rows, width), fisher.dtype),
        ],
        in_specs=[SMEM] + [VMEM] * 4 + [HBM],
        out_specs=[VMEM] * 2,
        scratch_shapes=[pltpu.SemaphoreType.DMA((steps,))],
        compiler_params=limit(8),
        cost_estimate=pl.CostEstimate(
            flops=4 * nq * width * rows, bytes_accessed=2 * width * rows, transcendentals=0
        ),
    )(scalars(column), *chunks, *blocks, fisher)


def fisher_last_kernel(at_ref, chunk0, chunk1, block0, base_ref, fisher_ref, out_ref, held, sem):
    copies = start_blocks(fisher_ref, at_ref[0], held, sem)
    step = held.shape[0] // sem.shape[0]
    for i in range(sem.shape[0]):
        rows = slice(i * step, (i + 1) * step)
        out_ref[:, rows] = base_ref[:, rows] + times(chunk0, block0[rows, :])
    for i in range(sem.shape[0]):
        rows = slice(i * step, (i + 1) * step)
        copies[i].wait()
        out_ref[:, rows] += times(chunk1, held[rows, :])


def fisher_last(chunks, block, base, column, fisher, steps=4):
    nq, width = chunks[0].shape
    rows = fisher.shape[0]
    return pl.pallas_call(
        fisher_last_kernel,
        out_shape=jax.ShapeDtypeStruct((nq, rows), jnp.float32),
        in_specs=[SMEM] + [VMEM] * 4 + [HBM],
        out_specs=VMEM,
        scratch_shapes=[pltpu.VMEM((rows, width), fisher.dtype), pltpu.SemaphoreType.DMA((steps,))],
        compiler_params=limit(16),
        cost_estimate=pl.CostEstimate(
            flops=4 * nq * width * rows, bytes_accessed=2 * width * rows, transcendentals=0
        ),
    )(scalars(column), *chunks, block, base, fisher)


def score_kernel(n, at_ref, *refs):
    grads_ref, out_ref = refs[n], refs[-1]
    width = refs[0].shape[1]
    total = refs[n + 1][...] if len(refs) > n + 2 else None
    for k in range(n):
        grads = grads_ref[:, pl.ds(pl.multiple_of(at_ref[k] * width, width), width)]
        term = times(refs[k], grads)
        total = term if total is None else total + term
    out_ref[...] = total


def score_dot(pieces, columns, grads, *base):
    n = len(pieces)
    rows, width = pieces[0].shape
    return pl.pallas_call(
        functools.partial(score_kernel, n),
        out_shape=jax.ShapeDtypeStruct((rows, grads.shape[0]), jnp.float32),
        in_specs=[SMEM] + [VMEM] * (n + 1 + len(base)),
        out_specs=VMEM,
        compiler_params=limit(8),
        cost_estimate=pl.CostEstimate(
            flops=2 * n * rows * width * grads.shape[0],
            bytes_accessed=2 * n * width * grads.shape[0],
            transcendentals=0,
        ),
    )(scalars(*columns), *pieces, grads, *base)


def pick_kernel(at_ref, a_ref, b_ref, *refs):
    out_ref = refs[-1]

    @pl.when(at_ref[0] == 1)
    def _():
        out_ref[...] = a_ref[...]

    @pl.when(at_ref[0] != 1)
    def _():
        out_ref[...] = b_ref[...]


def pick(condition, a, b, after=()):
    return pl.pallas_call(
        pick_kernel,
        out_shape=jax.ShapeDtypeStruct(a.shape, a.dtype),
        in_specs=[SMEM] + [VMEM] * 2 + [ANY] * len(after),
        out_specs=VMEM,
        compiler_params=limit(2),
        cost_estimate=pl.CostEstimate(flops=0, bytes_accessed=2 * a.size * 2, transcendentals=0),
    )(scalars(condition), a, b, *after)


def per_device_quad(nz, nx, ny, queries, inverse_fisher, stored_grads):
    nex = nz * nx
    near = nz // 2
    nq = queries.shape[0]
    y, e, d = (lax.axis_index(a) for a in AXES)
    z = e // nx
    x = e % nx
    u = jnp.where(d == 0, z, nz - 1 - z)
    owner = u < near

    def move(value, target):
        pairs = []
        for sy in range(ny):
            for sz in range(nz):
                for sx in range(nx):
                    for sd in range(2):
                        to = target(sy, sz, sx, sd)
                        if to is not None:
                            ty, tz, tx, td = to
                            pairs.append(((sy * nex + sz * nx + sx) * 2 + sd, (ty * nex + tz * nx + tx) * 2 + td))
        return lax.ppermute(value, AXES, pairs)

    def along_z(value, hops):
        def target(sy, sz, sx, sd):
            su = sz if sd == 0 else nz - 1 - sz
            if su not in hops:
                return None
            tu = hops[su]
            return sy, tu if sd == 0 else nz - 1 - tu, sx, sd

        return move(value, target)

    def swap_x(value):
        return move(value, lambda sy, sz, sx, sd: (sy, sz, 1 - sx, sd))

    def swap_y(value):
        return move(value, lambda sy, sz, sx, sd: (1 - sy, sz, sx, sd))

    def to_owner(value):
        def target(sy, sz, sx, sd):
            su = sz if sd == 0 else nz - 1 - sz
            return None if su < near else (sy, sz, sx, 1 - sd)

        return move(value, target)

    def real_plane(k):
        return jnp.where(d == 0, k, nz - 1 - k)

    def gather(own, after=()):
        first = pick(owner, own, along_z(own, {0: 2, 1: 3}), after)
        second = pick(owner, along_z(own, {0: 1, 1: 0}), along_z(own, {0: 3, 1: 2}))
        return [first, second, swap_x(first), swap_x(second)]

    planes = [real_plane(u % 2), real_plane(1 - u % 2)]
    columns = [p * nx + x_ - d * (nex // 2) for x_ in (x, 1 - x) for p in planes]

    other_grads = swap_y(stored_grads)

    own = cut_rows(queries, nq // ny, y)
    blocks = load(inverse_fisher, columns[:2], own.shape[1])
    pieces = gather(own, blocks[:1])
    total, block = fisher_first(pieces[:2], blocks, columns[2], inverse_fisher)
    total = fisher_last(pieces[2:], block, total, columns[3], inverse_fisher)
    panel = (total + to_owner(total)).astype(jnp.bfloat16)

    pieces = gather(panel)
    other, mine = (
        score_dot(pieces[3:], columns[3:], grads, score_dot(pieces[:3], columns[:3], grads))
        for grads in (other_grads, stored_grads)
    )
    other = move(other, lambda sy, sz, sx, sd: (1 - sy, sz, sx, sy) if sd != sy else None) + move(
        other, lambda sy, sz, sx, sd: (1 - sy, sz, sx, sy) if sd == sy else None
    )
    mine = mine + move(mine, lambda sy, sz, sx, sd: (sy, sz, sx, sy) if sd != sy else None)
    return jnp.where(d == y, mine, other)


def solution(mesh):
    coords = [getattr(device, "coords", None) for device in mesh.devices.flat]
    nx = 2 if None in coords else len({c[0] for c in coords})
    nz = mesh.shape["ex"] // nx
    ny = mesh.shape["grp"]
    if (nz, nx, ny) == (4, 2, 2):
        body = functools.partial(per_device_quad, nz, nx, ny)
    else:
        body = per_device_any
    return jax.shard_map(
        body,
        mesh=mesh,
        in_specs=(P(None, "ex"), P("ex", "dim"), P(("grp", "ex"), "dim")),
        out_specs=P("dim", ("grp", "ex")),
        check_vma=False,
    )
```

time: 77.2 us -> 83.5 us (1.082)
  local copies, waits for them, and re-layouts: 1 us -> 14.2 us
  waiting for transfers between devices: 17.3 us -> 13 us
  starting transfers between devices: 33 us -> 31.6 us
    unnamed x4 -> x12, local copies, waits for them, and re-layouts: 1 us -> 14.2 us
    ppermute x16 -> x15, waiting for transfers between devices: 17.3 us -> 13 us  [move(): return lax.ppermute(value, AXES, pairs)]
    ppermute x16 -> x15, starting transfers between devices: 33 us -> 31.6 us  [move(): return lax.ppermute(value, AXES, pairs)]
    pallas_call x6 -> x7, Pallas kernels: 20.9 us -> 20 us  [the longest x1 7.86 us: fisher_first(): pl.pallas_call(fisher_first_kernel, out_shape=[jax.ShapeDtypeStruct((nq,...]
    pallas_call x2 -> x4, Pallas kernels: 2.75 us -> 2.96 us  [score_dot(): pl.pallas_call(functools.partial(score_kernel, n), out_shape=jax.ShapeDty...]
  transfers between devices with their start and end apart: 16 -> 15, of which waited for: 7 -> 4; matrix products, arithmetic and copies ran while one was open for 1% -> 0% of each run, Pallas kernels for 29% -> 28%
where the time goes in v6:
time: 83.5 us; the launch traced here: 83.1 us
  starting transfers between devices  31.6 us (38%)
  Pallas kernels  23.2 us (28%)
  local copies, waits for them, and re-layouts  14.2 us (17%)
  waiting for transfers between devices  13 us (16%)
    ppermute x15, starting transfers between devices, move(): return lax.ppermute(value, AXES, pairs)  31.6 us
    unnamed x12, local copies, waits for them, and re-layouts  14.2 us
    ppermute x15, waiting for transfers between devices, move(): return lax.ppermute(value, AXES, pairs)  13 us
    pallas_call x1, Pallas kernels, fisher_first(): pl.pallas_call(fisher_first_kernel, out_shape=[jax.ShapeDtypeStruct((nq,...  7.86 us
    pallas_call x1, Pallas kernels, load(): pl.pallas_call(functools.partial(load_kernel, n), out_shape=[jax.ShapeDty...  6.5 us
    pallas_call x1, Pallas kernels, fisher_last(): pl.pallas_call(fisher_last_kernel, out_shape=jax.ShapeDtypeStruct((nq, ro...  5.54 us
    pallas_call x4, Pallas kernels, score_dot(): pl.pallas_call(functools.partial(score_kernel, n), out_shape=jax.ShapeDty...  2.96 us
  transfers between devices with their start and end apart: 15, of which 4 were waited for; matrix products, arithmetic and copies ran while one was open for 0% of the time, Pallas kernels for 28%

profile of v6, /device:TPU:0, one launch (start us, length us, event | category | flops | bytes accessed | tf_op | source)
XLA Modules:
  0.0 83.1 jit_solution(5989930165498084162)
XLA Ops:
  0.0 3.0 %collective-permute-start.12 = (bf16[128,8192]{1,0:T(8,128)(2,1)}, bf16[128,8192]{1,0:T(8,128)(2,1)S(1)}, u32[]{:S(2)}, u32[]{:S(2)}) collective-permute-start(bf16[128,8192]{1,0:T(8,128)(2,1)} %refs_1_.1), channel_id=1, source_target_pairs={{0,16},{1,17},{2,18},{3,19},{4,20},{5,21},{6,22},{7,23},{8,24},{9,... | collective-permute-start | bytes 6291464 | tf_op jit(solution)/shard_map/ppermute | solution.py:227
  3.0 1.0 %copy-done.5 = bf16[96,2048]{1,0:T(8,128)(2,1)S(1)} copy-done((bf16[96,2048]{1,0:T(8,128)(2,1)S(1)}, bf16[96,2048]{1,0:T(8,128)(2,1)}, u32[]{:S(2)}) %copy-start.5) | copy-done | bytes 393240
  4.2 4.5 %collective-permute-start = (bf16[48,2048]{1,0:T(8,128)(2,1)S(1)}, bf16[48,2048]{1,0:T(8,128)(2,1)S(1)}, u32[]{:S(2)}, u32[]{:S(2)}) collective-permute-start(bf16[48,2048]{1,0:T(8,128)(2,1)S(1)} %shard_map.37.a_ref), channel_id=1, source_target_pairs={{0,8},{2,10},{4,12},{6,14},{9,1},{11,3},{13,5},{15,7},{16,24},{18,... | collective-permute-start | bytes 589832 | tf_op jit(solution)/shard_map/ppermute | solution.py:227
  8.7 3.5 %collective-permute-start.2 = (bf16[48,2048]{1,0:T(8,128)(2,1)S(1)}, bf16[48,2048]{1,0:T(8,128)(2,1)S(1)}, u32[]{:S(2)}, u32[]{:S(2)}) collective-permute-start(bf16[48,2048]{1,0:T(8,128)(2,1)S(1)} %shard_map.37.a_ref), channel_id=1, source_target_pairs={{0,4},{2,6},{4,0},{6,2},{9,13},{11,15},{13,9},{15,11},{16,20},{18,... | collective-permute-start | bytes 589832 | tf_op jit(solution)/shard_map/ppermute | solution.py:227
  12.2 1.3 %collective-permute-start.3 = (bf16[48,2048]{1,0:T(8,128)(2,1)S(1)}, bf16[48,2048]{1,0:T(8,128)(2,1)S(1)}, u32[]{:S(2)}, u32[]{:S(2)}) collective-permute-start(bf16[48,2048]{1,0:T(8,128)(2,1)S(1)} %shard_map.37.a_ref), channel_id=1, source_target_pairs={{0,12},{2,14},{4,8},{6,10},{9,5},{11,7},{13,1},{15,3},{16,28},{18,... | collective-permute-start | bytes 589832 | tf_op jit(solution)/shard_map/ppermute | solution.py:227
  13.6 6.5 %shard_map.38 = (bf16[2048,2048]{1,0:T(8,128)(2,1)S(1)}, bf16[2048,2048]{1,0:T(8,128)(2,1)S(1)}) custom-call(s32[2]{0:T(128)S(1)} %pad_add_fusion.at_ref, bf16[2048,8192]{1,0:T(8,128)(2,1)} %fisher_ref.5), custom_call_target="tpu_custom_call" | custom-call | bytes 16777216 | tf_op jit(solution)/shard_map/pallas_call | solution.py:86
  20.2 3.2 %copy-done.2 = bf16[2048,2048]{1,0:T(8,128)(2,1)} copy-done((bf16[2048,2048]{1,0:T(8,128)(2,1)}, bf16[2048,2048]{1,0:T(8,128)(2,1)S(1)}, u32[]{:S(2)}) %copy-start.2) | copy-done | bytes 8388632
  23.4 3.2 %copy-done = bf16[2048,2048]{1,0:T(8,128)(2,1)} copy-done((bf16[2048,2048]{1,0:T(8,128)(2,1)}, bf16[2048,2048]{1,0:T(8,128)(2,1)S(1)}, u32[]{:S(2)}) %copy-start) | copy-done | bytes 8388632
  26.6 1.5 %collective-permute-start.1 = (bf16[48,2048]{1,0:T(8,128)(2,1)S(1)}, bf16[48,2048]{1,0:T(8,128)(2,1)S(1)}, u32[]{:S(2)}, u32[]{:S(2)}) collective-permute-start(bf16[48,2048]{1,0:T(8,128)(2,1)S(1)} %shard_map.39.chunk0), channel_id=1, source_target_pairs={{0,2},{1,3},{2,0},{3,1},{4,6},{5,7},{6,4},{7,5},{8,10},{9,11},{10,... | collective-permute-start | bytes 589832 | tf_op jit(solution)/shard_map/ppermute | solution.py:227
  28.2 0.6 collective-permute-start.4
  28.8 3.4 %copy-done.1 = bf16[2048,2048]{1,0:T(8,128)(2,1)S(1)} copy-done((bf16[2048,2048]{1,0:T(8,128)(2,1)S(1)}, bf16[2048,2048]{1,0:T(8,128)(2,1)}, u32[]{:S(2)}) %copy-start.1) | copy-done | bytes 8388632
  32.1 3.4 %copy-done.3 = bf16[2048,2048]{1,0:T(8,128)(2,1)S(1)} copy-done((bf16[2048,2048]{1,0:T(8,128)(2,1)S(1)}, bf16[2048,2048]{1,0:T(8,128)(2,1)}, u32[]{:S(2)}) %copy-start.3) | copy-done | bytes 8388632
  35.5 7.9 %shard_map.41 = (f32[48,2048]{1,0:T(8,128)S(1)}, bf16[2048,2048]{1,0:T(8,128)(2,1)S(1)}) custom-call(s32[1]{0:T(128)} %bitcast.5.at_ref, bf16[48,2048]{1,0:T(8,128)(2,1)S(1)} %shard_map.39.chunk0, bf16[48,2048]{1,0:T(8,128)(2,1)S(1)} %shard_map.40.chunk1, bf16[2048,2048]{1,0:T(8,128)(2,1)S(1)} %copy-done.1, bf16[2048,2048]{1,0:T(8,128)(2,1)S(1)} %copy-done.3, ...), custom_call_target="tpu_custom_call" | custom-call | flops 805306368 | bytes 8388608 | tf_op jit(solution)/shard_map/pallas_call | solution.py:112
  43.4 5.5 %shard_map.42 = f32[48,2048]{1,0:T(8,128)S(1)} custom-call(s32[1]{0:T(128)} %bitcast.at_ref, bf16[48,2048]{1,0:T(8,128)(2,1)S(1)} %collective-permute-done.1.chunk0, bf16[48,2048]{1,0:T(8,128)(2,1)S(1)} %collective-permute-done.4.chunk1, bf16[2048,2048]{1,0:T(8,128)(2,1)S(1)} %get-tuple-element.11.block0, f32[48,2048]{1,0:T(8,128)S(1)} %get-tuple-element.12.base_ref, ...), custom_call_target="tpu_custom_call" | custom-call | flops 805306368 | bytes 8388608 | tf_op jit(solution)/shard_map/pallas_call | solution.py:143
  49.0 1.3 %collective-permute-start.5 = (f32[48,2048]{1,0:T(8,128)S(1)}, f32[48,2048]{1,0:T(8,128)S(1)}, u32[]{:S(2)}, u32[]{:S(2)}) collective-permute-start(f32[48,2048]{1,0:T(8,128)S(1)} %shard_map.42), channel_id=1, source_target_pairs={{1,0},{3,2},{5,4},{7,6},{8,9},{10,11},{12,13},{14,15},{17,16},{19,... | collective-permute-start | bytes 1179656 | tf_op jit(solution)/shard_map/ppermute | solution.py:227
  50.3 2.3 %collective-permute-done.5 = f32[48,2048]{1,0:T(8,128)S(1)} collective-permute-done((f32[48,2048]{1,0:T(8,128)S(1)}, f32[48,2048]{1,0:T(8,128)S(1)}, u32[]{:S(2)}, u32[]{:S(2)}) %collective-permute-start.5) | collective-permute-done | bytes 393248 | tf_op jit(solution)/shard_map/ppermute | solution.py:227
  52.6 1.3 %collective-permute-start.9 = (bf16[48,2048]{1,0:T(8,128)(2,1)S(1)}, bf16[48,2048]{1,0:T(8,128)(2,1)S(1)}, u32[]{:S(2)}, u32[]{:S(2)}) collective-permute-start(bf16[48,2048]{1,0:T(8,128)(2,1)S(1)} %add_convert_fusion.a_ref), channel_id=1, source_target_pairs={{0,8},{2,10},{4,12},{6,14},{9,1},{11,3},{13,5},{15,7},{16,24},{18,... | collective-permute-start | bytes 589832 | tf_op jit(solution)/shard_map/ppermute | solution.py:227
  53.9 2.4 %collective-permute-start.6 = (bf16[48,2048]{1,0:T(8,128)(2,1)S(1)}, bf16[48,2048]{1,0:T(8,128)(2,1)S(1)}, u32[]{:S(2)}, u32[]{:S(2)}) collective-permute-start(bf16[48,2048]{1,0:T(8,128)(2,1)S(1)} %add_convert_fusion.a_ref), channel_id=1, source_target_pairs={{0,4},{2,6},{4,0},{6,2},{9,13},{11,15},{13,9},{15,11},{16,20},{18,... | collective-permute-start | bytes 589832 | tf_op jit(solution)/shard_map/ppermute | solution.py:227
  56.3 1.3 %collective-permute-start.7 = (bf16[48,2048]{1,0:T(8,128)(2,1)S(1)}, bf16[48,2048]{1,0:T(8,128)(2,1)S(1)}, u32[]{:S(2)}, u32[]{:S(2)}) collective-permute-start(bf16[48,2048]{1,0:T(8,128)(2,1)S(1)} %add_convert_fusion.a_ref), channel_id=1, source_target_pairs={{0,12},{2,14},{4,8},{6,10},{9,5},{11,7},{13,1},{15,3},{16,28},{18,... | collective-permute-start | bytes 589832 | tf_op jit(solution)/shard_map/ppermute | solution.py:227
  57.7 1.6 %collective-permute-start.10 = (bf16[48,2048]{1,0:T(8,128)(2,1)S(1)}, bf16[48,2048]{1,0:T(8,128)(2,1)S(1)}, u32[]{:S(2)}, u32[]{:S(2)}) collective-permute-start(bf16[48,2048]{1,0:T(8,128)(2,1)S(1)} %shard_map.44.refs_0_), channel_id=1, source_target_pairs={{0,2},{1,3},{2,0},{3,1},{4,6},{5,7},{6,4},{7,5},{8,10},{9,11},{10,... | collective-permute-start | bytes 589832 | tf_op jit(solution)/shard_map/ppermute | solution.py:227
  59.2 4.7 %collective-permute-done.6.a_ref = bf16[48,2048]{1,0:T(8,128)(2,1)S(1)} collective-permute-done((bf16[48,2048]{1,0:T(8,128)(2,1)S(1)}, bf16[48,2048]{1,0:T(8,128)(2,1)S(1)}, u32[]{:S(2)}, u32[]{:S(2)}) %collective-permute-start.6) | collective-permute-done | bytes 196640 | tf_op jit(solution)/shard_map/ppermute | solution.py:227
  63.9 1.6 %collective-permute-start.8 = (bf16[48,2048]{1,0:T(8,128)(2,1)S(1)}, bf16[48,2048]{1,0:T(8,128)(2,1)S(1)}, u32[]{:S(2)}, u32[]{:S(2)}) collective-permute-start(bf16[48,2048]{1,0:T(8,128)(2,1)S(1)} %shard_map.43.refs_1_), channel_id=1, source_target_pairs={{0,2},{1,3},{2,0},{3,1},{4,6},{5,7},{6,4},{7,5},{8,10},{9,11},{10,... | collective-permute-start | bytes 589832 | tf_op jit(solution)/shard_map/ppermute | solution.py:227
  65.6 1.2 %shard_map.45.refs_2_ = f32[48,128]{1,0:T(8,128)S(1)} custom-call(s32[3]{0:T(128)S(1)} %pad_add_fusion.1.at_ref, bf16[48,2048]{1,0:T(8,128)(2,1)S(1)} %shard_map.44.refs_0_, bf16[48,2048]{1,0:T(8,128)(2,1)S(1)} %shard_map.43.refs_1_, bf16[48,2048]{1,0:T(8,128)(2,1)S(1)} %collective-permute-done.10.refs_2_, bf16[128,8192]{1,0:T(8,128)(2,1)S(1)} %copy-done.4), custom_call_target="tpu_custom_call" | custom-call | flops 75497472 | bytes 1572864 | tf_op jit(solution)/shard_map/pallas_call | solution.py:170
  66.8 4.5 %collective-permute-done.8.refs_0_ = bf16[48,2048]{1,0:T(8,128)(2,1)S(1)} collective-permute-done((bf16[48,2048]{1,0:T(8,128)(2,1)S(1)}, bf16[48,2048]{1,0:T(8,128)(2,1)S(1)}, u32[]{:S(2)}, u32[]{:S(2)}) %collective-permute-start.8) | collective-permute-done | bytes 196640 | tf_op jit(solution)/shard_map/ppermute | solution.py:227
  71.3 0.3 shard_map.46
  71.6 1.3 %collective-permute-start.11 = (f32[48,128]{1,0:T(8,128)S(1)}, f32[48,128]{1,0:T(8,128)S(1)}, u32[]{:S(2)}, u32[]{:S(2)}) collective-permute-start(f32[48,128]{1,0:T(8,128)S(1)} %shard_map.46), channel_id=1, source_target_pairs={{1,0},{3,2},{5,4},{7,6},{9,8},{11,10},{13,12},{15,14},{16,17},{18,... | collective-permute-start | bytes 73736 | tf_op jit(solution)/shard_map/ppermute | solution.py:227
  72.9 1.2 %shard_map.47.refs_2_ = f32[48,128]{1,0:T(8,128)S(1)} custom-call(s32[3]{0:T(128)S(1)} %pad_add_fusion.1.at_ref, bf16[48,2048]{1,0:T(8,128)(2,1)S(1)} %shard_map.44.refs_0_, bf16[48,2048]{1,0:T(8,128)(2,1)S(1)} %shard_map.43.refs_1_, bf16[48,2048]{1,0:T(8,128)(2,1)S(1)} %collective-permute-done.10.refs_2_, ...), custom_call_target="tpu_custom_call" | custom-call | flops 75497472 | bytes 1572864 | tf_op jit(solution)/shard_map/pallas_call | solution.py:170
  74.1 0.3 shard_map.48
  74.4 0.7 collective-permute-start.13
  75.1 5.9 %collective-permute-start.14 = (f32[48,128]{1,0:T(8,128)S(1)}, f32[48,128]{1,0:T(8,128)S(1)}, u32[]{:S(2)}, u32[]{:S(2)}) collective-permute-start(f32[48,128]{1,0:T(8,128)S(1)} %shard_map.48), channel_id=1, source_target_pairs={{0,16},{2,18},{4,20},{6,22},{8,24},{10,26},{12,28},{14,30},{17,1},... | collective-permute-start | bytes 73736 | tf_op jit(solution)/shard_map/ppermute | solution.py:227
  81.0 1.5 %collective-permute-done.14 = f32[48,128]{1,0:T(8,128)S(1)} collective-permute-done((f32[48,128]{1,0:T(8,128)S(1)}, f32[48,128]{1,0:T(8,128)S(1)}, u32[]{:S(2)}, u32[]{:S(2)}) %collective-permute-start.14) | collective-permute-done | bytes 24608 | tf_op jit(solution)/shard_map/ppermute | solution.py:227
  82.5 0.6 add_select_fusion
  (26 shorter events, 0.6 us)
Async XLA Ops:
  0.0 72.9 %collective-permute-start.12 = (bf16[128,8192]{1,0:T(8,128)(2,1)}, bf16[128,8192]{1,0:T(8,128)(2,1)S(1)}, u32[]{:S(2)}, u32[]{:S(2)}) collective-permute-start(bf16[128,8192]{1,0:T(8,128)(2,1)} %refs_1_.1), channel_id=1, source_target_pairs={{0,16},{1,17},{2,18},{3,19},{4,20},{5,21},{6,22},{7,23},{8,24},{9,... | collective-permute-start | bytes 6291464 | tf_op jit(solution)/shard_map/ppermute | solution.py:227
  3.0 1.0 %copy-start.5 = (bf16[96,2048]{1,0:T(8,128)(2,1)S(1)}, bf16[96,2048]{1,0:T(8,128)(2,1)}, u32[]{:S(2)}) copy-start(bf16[96,2048]{1,0:T(8,128)(2,1)} %src_ref.1) | copy-start | bytes 1179652
  4.2 16.0 %collective-permute-start = (bf16[48,2048]{1,0:T(8,128)(2,1)S(1)}, bf16[48,2048]{1,0:T(8,128)(2,1)S(1)}, u32[]{:S(2)}, u32[]{:S(2)}) collective-permute-start(bf16[48,2048]{1,0:T(8,128)(2,1)S(1)} %shard_map.37.a_ref), channel_id=1, source_target_pairs={{0,8},{2,10},{4,12},{6,14},{9,1},{11,3},{13,5},{15,7},{16,24},{18,... | collective-permute-start | bytes 589832 | tf_op jit(solution)/shard_map/ppermute | solution.py:227
  8.7 19.4 %collective-permute-start.2 = (bf16[48,2048]{1,0:T(8,128)(2,1)S(1)}, bf16[48,2048]{1,0:T(8,128)(2,1)S(1)}, u32[]{:S(2)}, u32[]{:S(2)}) collective-permute-start(bf16[48,2048]{1,0:T(8,128)(2,1)S(1)} %shard_map.37.a_ref), channel_id=1, source_target_pairs={{0,4},{2,6},{4,0},{6,2},{9,13},{11,15},{13,9},{15,11},{16,20},{18,... | collective-permute-start | bytes 589832 | tf_op jit(solution)/shard_map/ppermute | solution.py:227
  12.2 15.9 %collective-permute-start.3 = (bf16[48,2048]{1,0:T(8,128)(2,1)S(1)}, bf16[48,2048]{1,0:T(8,128)(2,1)S(1)}, u32[]{:S(2)}, u32[]{:S(2)}) collective-permute-start(bf16[48,2048]{1,0:T(8,128)(2,1)S(1)} %shard_map.37.a_ref), channel_id=1, source_target_pairs={{0,12},{2,14},{4,8},{6,10},{9,5},{11,7},{13,1},{15,3},{16,28},{18,... | collective-permute-start | bytes 589832 | tf_op jit(solution)/shard_map/ppermute | solution.py:227
  20.2 3.3 %copy-start.2 = (bf16[2048,2048]{1,0:T(8,128)(2,1)}, bf16[2048,2048]{1,0:T(8,128)(2,1)S(1)}, u32[]{:S(2)}) copy-start(bf16[2048,2048]{1,0:T(8,128)(2,1)S(1)} %get-tuple-element.10.block1) | copy-start | bytes 25165828
  23.4 3.2 %copy-start = (bf16[2048,2048]{1,0:T(8,128)(2,1)}, bf16[2048,2048]{1,0:T(8,128)(2,1)S(1)}, u32[]{:S(2)}) copy-start(bf16[2048,2048]{1,0:T(8,128)(2,1)S(1)} %get-tuple-element.9.refs_0_.block0) | copy-start | bytes 25165828
  26.6 16.8 %collective-permute-start.1 = (bf16[48,2048]{1,0:T(8,128)(2,1)S(1)}, bf16[48,2048]{1,0:T(8,128)(2,1)S(1)}, u32[]{:S(2)}, u32[]{:S(2)}) collective-permute-start(bf16[48,2048]{1,0:T(8,128)(2,1)S(1)} %shard_map.39.chunk0), channel_id=1, source_target_pairs={{0,2},{1,3},{2,0},{3,1},{4,6},{5,7},{6,4},{7,5},{8,10},{9,11},{10,... | collective-permute-start | bytes 589832 | tf_op jit(solution)/shard_map/ppermute | solution.py:227
  28.2 15.2 %collective-permute-start.4 = (bf16[48,2048]{1,0:T(8,128)(2,1)S(1)}, bf16[48,2048]{1,0:T(8,128)(2,1)S(1)}, u32[]{:S(2)}, u32[]{:S(2)}) collective-permute-start(bf16[48,2048]{1,0:T(8,128)(2,1)S(1)} %shard_map.40.chunk1), channel_id=1, source_target_pairs={{0,2},{1,3},{2,0},{3,1},{4,6},{5,7},{6,4},{7,5},{8,10},{9,11},{10,... | collective-permute-start | bytes 589832 | tf_op jit(solution)/shard_map/ppermute | solution.py:227
  28.8 3.4 %copy-start.1 = (bf16[2048,2048]{1,0:T(8,128)(2,1)S(1)}, bf16[2048,2048]{1,0:T(8,128)(2,1)}, u32[]{:S(2)}) copy-start(bf16[2048,2048]{1,0:T(8,128)(2,1)} %copy-done) | copy-start | bytes 25165828
  32.1 3.4 %copy-start.3 = (bf16[2048,2048]{1,0:T(8,128)(2,1)S(1)}, bf16[2048,2048]{1,0:T(8,128)(2,1)}, u32[]{:S(2)}) copy-start(bf16[2048,2048]{1,0:T(8,128)(2,1)} %copy-done.2) | copy-start | bytes 25165828
  43.4 22.2 %copy-start.4 = (bf16[128,8192]{1,0:T(8,128)(2,1)S(1)}, bf16[128,8192]{1,0:T(8,128)(2,1)}, u32[]{:S(2)}) copy-start(bf16[128,8192]{1,0:T(8,128)(2,1)} %refs_1_.1) | copy-start | bytes 6291460
  49.0 3.6 %collective-permute-start.5 = (f32[48,2048]{1,0:T(8,128)S(1)}, f32[48,2048]{1,0:T(8,128)S(1)}, u32[]{:S(2)}, u32[]{:S(2)}) collective-permute-start(f32[48,2048]{1,0:T(8,128)S(1)} %shard_map.42), channel_id=1, source_target_pairs={{1,0},{3,2},{5,4},{7,6},{8,9},{10,11},{12,13},{14,15},{17,16},{19,... | collective-permute-start | bytes 1179656 | tf_op jit(solution)/shard_map/ppermute | solution.py:227
  52.6 5.0 %collective-permute-start.9 = (bf16[48,2048]{1,0:T(8,128)(2,1)S(1)}, bf16[48,2048]{1,0:T(8,128)(2,1)S(1)}, u32[]{:S(2)}, u32[]{:S(2)}) collective-permute-start(bf16[48,2048]{1,0:T(8,128)(2,1)S(1)} %add_convert_fusion.a_ref), channel_id=1, source_target_pairs={{0,8},{2,10},{4,12},{6,14},{9,1},{11,3},{13,5},{15,7},{16,24},{18,... | collective-permute-start | bytes 589832 | tf_op jit(solution)/shard_map/ppermute | solution.py:227
  53.9 10.0 %collective-permute-start.6 = (bf16[48,2048]{1,0:T(8,128)(2,1)S(1)}, bf16[48,2048]{1,0:T(8,128)(2,1)S(1)}, u32[]{:S(2)}, u32[]{:S(2)}) collective-permute-start(bf16[48,2048]{1,0:T(8,128)(2,1)S(1)} %add_convert_fusion.a_ref), channel_id=1, source_target_pairs={{0,4},{2,6},{4,0},{6,2},{9,13},{11,15},{13,9},{15,11},{16,20},{18,... | collective-permute-start | bytes 589832 | tf_op jit(solution)/shard_map/ppermute | solution.py:227
  56.3 7.6 %collective-permute-start.7 = (bf16[48,2048]{1,0:T(8,128)(2,1)S(1)}, bf16[48,2048]{1,0:T(8,128)(2,1)S(1)}, u32[]{:S(2)}, u32[]{:S(2)}) collective-permute-start(bf16[48,2048]{1,0:T(8,128)(2,1)S(1)} %add_convert_fusion.a_ref), channel_id=1, source_target_pairs={{0,12},{2,14},{4,8},{6,10},{9,5},{11,7},{13,1},{15,3},{16,28},{18,... | collective-permute-start | bytes 589832 | tf_op jit(solution)/shard_map/ppermute | solution.py:227
  57.7 7.9 %collective-permute-start.10 = (bf16[48,2048]{1,0:T(8,128)(2,1)S(1)}, bf16[48,2048]{1,0:T(8,128)(2,1)S(1)}, u32[]{:S(2)}, u32[]{:S(2)}) collective-permute-start(bf16[48,2048]{1,0:T(8,128)(2,1)S(1)} %shard_map.44.refs_0_), channel_id=1, source_target_pairs={{0,2},{1,3},{2,0},{3,1},{4,6},{5,7},{6,4},{7,5},{8,10},{9,11},{10,... | collective-permute-start | bytes 589832 | tf_op jit(solution)/shard_map/ppermute | solution.py:227
  63.9 7.4 %collective-permute-start.8 = (bf16[48,2048]{1,0:T(8,128)(2,1)S(1)}, bf16[48,2048]{1,0:T(8,128)(2,1)S(1)}, u32[]{:S(2)}, u32[]{:S(2)}) collective-permute-start(bf16[48,2048]{1,0:T(8,128)(2,1)S(1)} %shard_map.43.refs_1_), channel_id=1, source_target_pairs={{0,2},{1,3},{2,0},{3,1},{4,6},{5,7},{6,4},{7,5},{8,10},{9,11},{10,... | collective-permute-start | bytes 589832 | tf_op jit(solution)/shard_map/ppermute | solution.py:227
  71.6 9.4 %collective-permute-start.11 = (f32[48,128]{1,0:T(8,128)S(1)}, f32[48,128]{1,0:T(8,128)S(1)}, u32[]{:S(2)}, u32[]{:S(2)}) collective-permute-start(f32[48,128]{1,0:T(8,128)S(1)} %shard_map.46), channel_id=1, source_target_pairs={{1,0},{3,2},{5,4},{7,6},{9,8},{11,10},{13,12},{15,14},{16,17},{18,... | collective-permute-start | bytes 73736 | tf_op jit(solution)/shard_map/ppermute | solution.py:227
  74.4 6.6 %collective-permute-start.13 = (f32[48,128]{1,0:T(8,128)S(1)}, f32[48,128]{1,0:T(8,128)S(1)}, u32[]{:S(2)}, u32[]{:S(2)}) collective-permute-start(f32[48,128]{1,0:T(8,128)S(1)} %shard_map.48), channel_id=1, source_target_pairs={{1,16},{3,18},{5,20},{7,22},{9,24},{11,26},{13,28},{15,30},{16,1},... | collective-permute-start | bytes 73736 | tf_op jit(solution)/shard_map/ppermute | solution.py:227
  75.1 7.4 %collective-permute-start.14 = (f32[48,128]{1,0:T(8,128)S(1)}, f32[48,128]{1,0:T(8,128)S(1)}, u32[]{:S(2)}, u32[]{:S(2)}) collective-permute-start(f32[48,128]{1,0:T(8,128)S(1)} %shard_map.48), channel_id=1, source_target_pairs={{0,16},{2,18},{4,20},{6,22},{8,24},{10,26},{12,28},{14,30},{17,1},... | collective-permute-start | bytes 73736 | tf_op jit(solution)/shard_map/ppermute | solution.py:227

commit v7 on v6

--- a/solution.py
+++ b/solution.py
@@ -33,8 +33,11 @@
     return lax.psum_scatter(partial_scores, "dim", scatter_dimension=0, tiled=True)
 
 
-def scalars(*values):
-    return jnp.stack([jnp.asarray(v, jnp.int32) for v in values])
+def scalar(value):
+    return jnp.asarray(value, jnp.int32).reshape(1)
+
+
+ORDER = (0, 2, 1, 3)
 
 
 def cut_rows_kernel(at_ref, src_ref, out_ref, sem):
@@ -53,7 +56,7 @@
         out_specs=VMEM,
         scratch_shapes=[pltpu.SemaphoreType.DMA],
         compiler_params=limit(2),
-    )(scalars(at), src)
+    )(scalar(at), src)
 
 
 def start_blocks(fisher_ref, at, held_ref, sem):
@@ -73,18 +76,17 @@
     return lax.dot_general(chunk_ref[...], fisher, NT, preferred_element_type=jnp.float32)
 
 
-def load_kernel(n, at_ref, fisher_ref, *refs):
+def load_kernel(at_ref, fisher_ref, *refs):
     copies = []
-    for k in range(n):
-        copies += start_blocks(fisher_ref, at_ref[k], refs[k], refs[n].at[k])
+    for k, held_ref in enumerate(refs[:-1]):
+        copies += start_blocks(fisher_ref, at_ref[0] ^ ORDER[k], held_ref, refs[-1].at[k])
     for copy in copies:
         copy.wait()
 
 
-def load(fisher, columns, width, steps=4):
-    n = len(columns)
-    return pl.pallas_call(
-        functools.partial(load_kernel, n),
+def load(fisher, first, n, width, steps=4):
+    return pl.pallas_call(
+        load_kernel,
         out_shape=[jax.ShapeDtypeStruct((fisher.shape[0], width), fisher.dtype)] * n,
         in_specs=[SMEM, HBM],
         out_specs=[VMEM] * n,
@@ -93,20 +95,23 @@
         cost_estimate=pl.CostEstimate(
             flops=0, bytes_accessed=2 * n * width * fisher.shape[0], transcendentals=0
         ),
-    )(scalars(*columns), fisher)
+    )(scalar(first), fisher)
 
 
 def fisher_first_kernel(at_ref, chunk0, chunk1, block0, block1, fisher_ref, out_ref, next_ref, sem):
-    copies = start_blocks(fisher_ref, at_ref[0], next_ref, sem)
+    copies = start_blocks(fisher_ref, at_ref[0] ^ ORDER[2], next_ref, sem)
     step = block0.shape[0] // sem.shape[0]
     for i in range(sem.shape[0]):
         rows = slice(i * step, (i + 1) * step)
-        out_ref[:, rows] = times(chunk0, block0[rows, :]) + times(chunk1, block1[rows, :])
+        out_ref[:, rows] = times(chunk0, block0[rows, :])
+    for i in range(sem.shape[0]):
+        rows = slice(i * step, (i + 1) * step)
+        out_ref[:, rows] += times(chunk1, block1[rows, :])
     for copy in copies:
         copy.wait()
 
 
-def fisher_first(chunks, blocks, column, fisher, steps=4):
+def fisher_first(chunks, blocks, first, fisher, steps=4):
     nq, width = chunks[0].shape
     rows = fisher.shape[0]
     return pl.pallas_call(
@@ -122,11 +127,11 @@
         cost_estimate=pl.CostEstimate(
             flops=4 * nq * width * rows, bytes_accessed=2 * width * rows, transcendentals=0
         ),
-    )(scalars(column), *chunks, *blocks, fisher)
+    )(scalar(first), *chunks, *blocks, fisher)
 
 
 def fisher_last_kernel(at_ref, chunk0, chunk1, block0, base_ref, fisher_ref, out_ref, held, sem):
-    copies = start_blocks(fisher_ref, at_ref[0], held, sem)
+    copies = start_blocks(fisher_ref, at_ref[0] ^ ORDER[3], held, sem)
     step = held.shape[0] // sem.shape[0]
     for i in range(sem.shape[0]):
         rows = slice(i * step, (i + 1) * step)
@@ -137,7 +142,7 @@
         out_ref[:, rows] += times(chunk1, held[rows, :])
 
 
-def fisher_last(chunks, block, base, column, fisher, steps=4):
+def fisher_last(chunks, block, base, first, fisher, steps=4):
     nq, width = chunks[0].shape
     rows = fisher.shape[0]
     return pl.pallas_call(
@@ -150,27 +155,29 @@
         cost_estimate=pl.CostEstimate(
             flops=4 * nq * width * rows, bytes_accessed=2 * width * rows, transcendentals=0
         ),
-    )(scalars(column), *chunks, block, base, fisher)
-
-
-def score_kernel(n, at_ref, *refs):
+    )(scalar(first), *chunks, block, base, fisher)
+
+
+def score_kernel(order, has_base, at_ref, *refs):
+    n = len(order)
     grads_ref, out_ref = refs[n], refs[-1]
     width = refs[0].shape[1]
-    total = refs[n + 1][...] if len(refs) > n + 2 else None
+    total = refs[n + 1][...] if has_base else None
     for k in range(n):
-        grads = grads_ref[:, pl.ds(pl.multiple_of(at_ref[k] * width, width), width)]
-        term = times(refs[k], grads)
+        start = pl.multiple_of((at_ref[0] ^ order[k]) * width, width)
+        term = times(refs[k], grads_ref[:, pl.ds(start, width)])
         total = term if total is None else total + term
     out_ref[...] = total
 
 
-def score_dot(pieces, columns, grads, *base):
+def score_dot(pieces, order, first, grads, base=None, after=()):
     n = len(pieces)
     rows, width = pieces[0].shape
-    return pl.pallas_call(
-        functools.partial(score_kernel, n),
+    operands = [*pieces, grads] + ([] if base is None else [base])
+    return pl.pallas_call(
+        functools.partial(score_kernel, order, base is not None),
         out_shape=jax.ShapeDtypeStruct((rows, grads.shape[0]), jnp.float32),
-        in_specs=[SMEM] + [VMEM] * (n + 1 + len(base)),
+        in_specs=[SMEM] + [VMEM] * len(operands) + [ANY] * len(after),
         out_specs=VMEM,
         compiler_params=limit(8),
         cost_estimate=pl.CostEstimate(
@@ -178,7 +185,7 @@
             bytes_accessed=2 * n * width * grads.shape[0],
             transcendentals=0,
         ),
-    )(scalars(*columns), *pieces, grads, *base)
+    )(scalar(first), *operands, *after)
 
 
 def pick_kernel(at_ref, a_ref, b_ref, *refs):
@@ -201,7 +208,7 @@
         out_specs=VMEM,
         compiler_params=limit(2),
         cost_estimate=pl.CostEstimate(flops=0, bytes_accessed=2 * a.size * 2, transcendentals=0),
-    )(scalars(condition), a, b, *after)
+    )(scalar(condition), a, b, *after)
 
 
 def per_device_quad(nz, nx, ny, queries, inverse_fisher, stored_grads):
@@ -249,31 +256,27 @@
 
         return move(value, target)
 
-    def real_plane(k):
-        return jnp.where(d == 0, k, nz - 1 - k)
-
-    def gather(own, after=()):
-        first = pick(owner, own, along_z(own, {0: 2, 1: 3}), after)
-        second = pick(owner, along_z(own, {0: 1, 1: 0}), along_z(own, {0: 3, 1: 2}))
+    def gather(own, after=((), ())):
+        first = pick(owner, own, along_z(own, {0: 2, 1: 3}), after[0])
+        second = pick(owner, along_z(own, {0: 1, 1: 0}), along_z(own, {0: 3, 1: 2}), after[1])
         return [first, second, swap_x(first), swap_x(second)]
 
-    planes = [real_plane(u % 2), real_plane(1 - u % 2)]
-    columns = [p * nx + x_ - d * (nex // 2) for x_ in (x, 1 - x) for p in planes]
+    plane = jnp.where(d == 0, u % 2, nz - 1 - u % 2)
+    column = plane * nx + x - d * (nex // 2)
 
     other_grads = swap_y(stored_grads)
 
     own = cut_rows(queries, nq // ny, y)
-    blocks = load(inverse_fisher, columns[:2], own.shape[1])
-    pieces = gather(own, blocks[:1])
-    total, block = fisher_first(pieces[:2], blocks, columns[2], inverse_fisher)
-    total = fisher_last(pieces[2:], block, total, columns[3], inverse_fisher)
+    blocks = load(inverse_fisher, column, 2, own.shape[1])
+    pieces = gather(own, (blocks[:1], ()))
+    total, block = fisher_first(pieces[:2], blocks, column, inverse_fisher)
+    total = fisher_last(pieces[2:], block, total, column, inverse_fisher)
     panel = (total + to_owner(total)).astype(jnp.bfloat16)
 
-    pieces = gather(panel)
-    other, mine = (
-        score_dot(pieces[3:], columns[3:], grads, score_dot(pieces[:3], columns[:3], grads))
-        for grads in (other_grads, stored_grads)
-    )
+    pieces = gather(panel, ((), (other_grads,)))
+    other, mine = (score_dot(pieces[:3], ORDER[:3], column, g) for g in (other_grads, stored_grads))
+    other = score_dot(pieces[3:], ORDER[3:], column, other_grads, other)
+    mine = score_dot(pieces[3:], ORDER[3:], column, stored_grads, mine, (other,))
     other = move(other, lambda sy, sz, sx, sd: (1 - sy, sz, sx, sy) if sd != sy else None) + move(
         other, lambda sy, sz, sx, sd: (1 - sy, sz, sx, sy) if sd == sy else None
     )

time: 83.5 us -> 70.1 us (0.84)
  local copies, waits for them, and re-layouts: 14.2 us -> 1 us
  waiting for transfers between devices: 13 us -> 14.4 us
  Pallas kernels: 23.2 us -> 22.2 us
    unnamed x12 -> x4, local copies, waits for them, and re-layouts: 14.2 us -> 1 us
    pallas_call x5, Pallas kernels: 9.46 us -> 7.84 us  [the longest x1 5.96 us: load(): pl.pallas_call(load_kernel, out_shape=[jax.ShapeDtypeStruct((fisher.shape...]
    ppermute x15, waiting for transfers between devices: 13 us -> 14.4 us  [move(): return lax.ppermute(value, AXES, pairs)]
  transfers between devices with their start and end apart: 15 -> 15, of which waited for: 4 -> 4; matrix products, arithmetic and copies ran while one was open for 0% -> 0% of each run, Pallas kernels for 28% -> 31%
where the time goes in v7:
time: 70.1 us; the launch traced here: 69.8 us
  starting transfers between devices  31.3 us (45%)
  Pallas kernels  22.2 us (32%)
  waiting for transfers between devices  14.4 us (21%)
  local copies, waits for them, and re-layouts  1 us (1%)
    ppermute x15, starting transfers between devices, move(): return lax.ppermute(value, AXES, pairs)  31.3 us
    ppermute x15, waiting for transfers between devices, move(): return lax.ppermute(value, AXES, pairs)  14.4 us
    pallas_call x1, Pallas kernels, fisher_first(): pl.pallas_call(fisher_first_kernel, out_shape=[jax.ShapeDtypeStruct((nq,...  8.47 us
    pallas_call x1, Pallas kernels, load(): pl.pallas_call(load_kernel, out_shape=[jax.ShapeDtypeStruct((fisher.shape...  5.96 us
    pallas_call x1, Pallas kernels, fisher_last(): pl.pallas_call(fisher_last_kernel, out_shape=jax.ShapeDtypeStruct((nq, ro...  5.53 us
    pallas_call x4, Pallas kernels, score_dot(): pl.pallas_call(functools.partial(score_kernel, order, base is not None),...  1.88 us
  transfers between devices with their start and end apart: 15, of which 4 were waited for; matrix products, arithmetic and copies ran while one was open for 0% of the time, Pallas kernels for 31%

profile of v7, /device:TPU:0, one launch (start us, length us, event | category | flops | bytes accessed | tf_op | source)
XLA Modules:
  0.0 69.8 jit_solution(14447036407672806582)
XLA Ops:
  0.0 3.0 %collective-permute-start.8 = (bf16[128,8192]{1,0:T(8,128)(2,1)}, bf16[128,8192]{1,0:T(8,128)(2,1)S(1)}, u32[]{:S(2)}, u32[]{:S(2)}) collective-permute-start(bf16[128,8192]{1,0:T(8,128)(2,1)} %refs_1_.1), channel_id=1, source_target_pairs={{0,16},{1,17},{2,18},{3,19},{4,20},{5,21},{6,22},{7,23},{8,24},{9,... | collective-permute-start | bytes 6291464 | tf_op jit(solution)/shard_map/ppermute | solution.py:234
  3.0 1.0 %copy-done.1 = bf16[96,2048]{1,0:T(8,128)(2,1)S(1)} copy-done((bf16[96,2048]{1,0:T(8,128)(2,1)S(1)}, bf16[96,2048]{1,0:T(8,128)(2,1)}, u32[]{:S(2)}) %copy-start.1) | copy-done | bytes 393240
  4.0 0.2 shard_map.37.a_ref
  4.2 4.5 %collective-permute-start = (bf16[48,2048]{1,0:T(8,128)(2,1)S(1)}, bf16[48,2048]{1,0:T(8,128)(2,1)S(1)}, u32[]{:S(2)}, u32[]{:S(2)}) collective-permute-start(bf16[48,2048]{1,0:T(8,128)(2,1)S(1)} %shard_map.37.a_ref), channel_id=1, source_target_pairs={{0,8},{2,10},{4,12},{6,14},{9,1},{11,3},{13,5},{15,7},{16,24},{18,... | collective-permute-start | bytes 589832 | tf_op jit(solution)/shard_map/ppermute | solution.py:234
  8.7 3.5 %collective-permute-start.2 = (bf16[48,2048]{1,0:T(8,128)(2,1)S(1)}, bf16[48,2048]{1,0:T(8,128)(2,1)S(1)}, u32[]{:S(2)}, u32[]{:S(2)}) collective-permute-start(bf16[48,2048]{1,0:T(8,128)(2,1)S(1)} %shard_map.37.a_ref), channel_id=1, source_target_pairs={{0,4},{2,6},{4,0},{6,2},{9,13},{11,15},{13,9},{15,11},{16,20},{18,... | collective-permute-start | bytes 589832 | tf_op jit(solution)/shard_map/ppermute | solution.py:234
  12.2 1.3 %collective-permute-start.3 = (bf16[48,2048]{1,0:T(8,128)(2,1)S(1)}, bf16[48,2048]{1,0:T(8,128)(2,1)S(1)}, u32[]{:S(2)}, u32[]{:S(2)}) collective-permute-start(bf16[48,2048]{1,0:T(8,128)(2,1)S(1)} %shard_map.37.a_ref), channel_id=1, source_target_pairs={{0,12},{2,14},{4,8},{6,10},{9,5},{11,7},{13,1},{15,3},{16,28},{18,... | collective-permute-start | bytes 589832 | tf_op jit(solution)/shard_map/ppermute | solution.py:234
  13.6 6.0 %shard_map.38 = (bf16[2048,2048]{1,0:T(8,128)(2,1)S(1)}, bf16[2048,2048]{1,0:T(8,128)(2,1)S(1)}) custom-call(s32[1]{0:T(128)} %bitcast.at_ref, bf16[2048,8192]{1,0:T(8,128)(2,1)} %fisher_ref.5), custom_call_target="tpu_custom_call" | custom-call | bytes 16777216 | tf_op jit(solution)/shard_map/pallas_call | solution.py:88
  19.5 0.0 collective-permute-done.b_ref
  19.6 1.6 %collective-permute-start.1 = (bf16[48,2048]{1,0:T(8,128)(2,1)S(1)}, bf16[48,2048]{1,0:T(8,128)(2,1)S(1)}, u32[]{:S(2)}, u32[]{:S(2)}) collective-permute-start(bf16[48,2048]{1,0:T(8,128)(2,1)S(1)} %shard_map.39.chunk0), channel_id=1, source_target_pairs={{0,2},{1,3},{2,0},{3,1},{4,6},{5,7},{6,4},{7,5},{8,10},{9,11},{10,... | collective-permute-start | bytes 589832 | tf_op jit(solution)/shard_map/ppermute | solution.py:234
  21.1 0.0 collective-permute-done.2.a_ref
  21.2 0.6 collective-permute-start.4
  21.8 8.5 %shard_map.41 = (f32[48,2048]{1,0:T(8,128)S(1)}, bf16[2048,2048]{1,0:T(8,128)(2,1)S(1)}) custom-call(s32[1]{0:T(128)} %bitcast.at_ref, bf16[48,2048]{1,0:T(8,128)(2,1)S(1)} %shard_map.39.chunk0, bf16[48,2048]{1,0:T(8,128)(2,1)S(1)} %shard_map.40.chunk1, bf16[2048,2048]{1,0:T(8,128)(2,1)S(1)} %get-tuple-element.9.refs_0_.block0, ...), custom_call_target="tpu_custom_call" | custom-call | flops 805306368 | bytes 8388608 | tf_op jit(solution)/shard_map/pallas_call | solution.py:117
  30.3 0.0 copy-start
  30.3 5.5 %shard_map.42 = f32[48,2048]{1,0:T(8,128)S(1)} custom-call(s32[1]{0:T(128)} %bitcast.at_ref, bf16[48,2048]{1,0:T(8,128)(2,1)S(1)} %collective-permute-done.1.chunk0, bf16[48,2048]{1,0:T(8,128)(2,1)S(1)} %collective-permute-done.4.chunk1, bf16[2048,2048]{1,0:T(8,128)(2,1)S(1)} %get-tuple-element.11.block0, f32[48,2048]{1,0:T(8,128)S(1)} %get-tuple-element.12.base_ref, ...), custom_call_target="tpu_custom_call" | custom-call | flops 805306368 | bytes 8388608 | tf_op jit(solution)/shard_map/pallas_call | solution.py:148
  35.8 1.3 %collective-permute-start.5 = (f32[48,2048]{1,0:T(8,128)S(1)}, f32[48,2048]{1,0:T(8,128)S(1)}, u32[]{:S(2)}, u32[]{:S(2)}) collective-permute-start(f32[48,2048]{1,0:T(8,128)S(1)} %shard_map.42), channel_id=1, source_target_pairs={{1,0},{3,2},{5,4},{7,6},{8,9},{10,11},{12,13},{14,15},{17,16},{19,... | collective-permute-start | bytes 1179656 | tf_op jit(solution)/shard_map/ppermute | solution.py:234
  37.1 2.3 %collective-permute-done.5 = f32[48,2048]{1,0:T(8,128)S(1)} collective-permute-done((f32[48,2048]{1,0:T(8,128)S(1)}, f32[48,2048]{1,0:T(8,128)S(1)}, u32[]{:S(2)}, u32[]{:S(2)}) %collective-permute-start.5) | collective-permute-done | bytes 393248 | tf_op jit(solution)/shard_map/ppermute | solution.py:234
  39.5 2.3 %collective-permute-start.10 = (bf16[48,2048]{1,0:T(8,128)(2,1)S(1)}, bf16[48,2048]{1,0:T(8,128)(2,1)S(1)}, u32[]{:S(2)}, u32[]{:S(2)}) collective-permute-start(bf16[48,2048]{1,0:T(8,128)(2,1)S(1)} %add_convert_fusion.a_ref), channel_id=1, source_target_pairs={{0,8},{2,10},{4,12},{6,14},{9,1},{11,3},{13,5},{15,7},{16,24},{18,... | collective-permute-start | bytes 589832 | tf_op jit(solution)/shard_map/ppermute | solution.py:234
  41.8 2.8 %collective-permute-start.6 = (bf16[48,2048]{1,0:T(8,128)(2,1)S(1)}, bf16[48,2048]{1,0:T(8,128)(2,1)S(1)}, u32[]{:S(2)}, u32[]{:S(2)}) collective-permute-start(bf16[48,2048]{1,0:T(8,128)(2,1)S(1)} %add_convert_fusion.a_ref), channel_id=1, source_target_pairs={{0,4},{2,6},{4,0},{6,2},{9,13},{11,15},{13,9},{15,11},{16,20},{18,... | collective-permute-start | bytes 589832 | tf_op jit(solution)/shard_map/ppermute | solution.py:234
  44.6 1.3 %collective-permute-start.7 = (bf16[48,2048]{1,0:T(8,128)(2,1)S(1)}, bf16[48,2048]{1,0:T(8,128)(2,1)S(1)}, u32[]{:S(2)}, u32[]{:S(2)}) collective-permute-start(bf16[48,2048]{1,0:T(8,128)(2,1)S(1)} %add_convert_fusion.a_ref), channel_id=1, source_target_pairs={{0,12},{2,14},{4,8},{6,10},{9,5},{11,7},{13,1},{15,3},{16,28},{18,... | collective-permute-start | bytes 589832 | tf_op jit(solution)/shard_map/ppermute | solution.py:234
  45.9 0.6 collective-permute-start.11
  46.5 6.8 %collective-permute-done.6.a_ref = bf16[48,2048]{1,0:T(8,128)(2,1)S(1)} collective-permute-done((bf16[48,2048]{1,0:T(8,128)(2,1)S(1)}, bf16[48,2048]{1,0:T(8,128)(2,1)S(1)}, u32[]{:S(2)}, u32[]{:S(2)}) %collective-permute-start.6) | collective-permute-done | bytes 196640 | tf_op jit(solution)/shard_map/ppermute | solution.py:234
  53.3 0.8 %collective-permute-start.9 = (bf16[48,2048]{1,0:T(8,128)(2,1)S(1)}, bf16[48,2048]{1,0:T(8,128)(2,1)S(1)}, u32[]{:S(2)}, u32[]{:S(2)}) collective-permute-start(bf16[48,2048]{1,0:T(8,128)(2,1)S(1)} %shard_map.43.refs_1_), channel_id=1, source_target_pairs={{0,2},{1,3},{2,0},{3,1},{4,6},{5,7},{6,4},{7,5},{8,10},{9,11},{10,... | collective-permute-start | bytes 589832 | tf_op jit(solution)/shard_map/ppermute | solution.py:234
  54.1 0.6 shard_map.45.refs_2_
  54.8 0.7 shard_map.46.refs_2_
  55.4 3.7 %collective-permute-done.9.refs_0_ = bf16[48,2048]{1,0:T(8,128)(2,1)S(1)} collective-permute-done((bf16[48,2048]{1,0:T(8,128)(2,1)S(1)}, bf16[48,2048]{1,0:T(8,128)(2,1)S(1)}, u32[]{:S(2)}, u32[]{:S(2)}) %collective-permute-start.9) | collective-permute-done | bytes 196640 | tf_op jit(solution)/shard_map/ppermute | solution.py:234
  59.2 0.3 shard_map.47.refs_3_
  59.5 0.3 shard_map.48
  59.8 1.3 %collective-permute-start.12 = (f32[48,128]{1,0:T(8,128)S(1)}, f32[48,128]{1,0:T(8,128)S(1)}, u32[]{:S(2)}, u32[]{:S(2)}) collective-permute-start(f32[48,128]{1,0:T(8,128)S(1)} %shard_map.48), channel_id=1, source_target_pairs={{1,0},{3,2},{5,4},{7,6},{9,8},{11,10},{13,12},{15,14},{16,17},{18,... | collective-permute-start | bytes 73736 | tf_op jit(solution)/shard_map/ppermute | solution.py:234
  61.1 0.7 collective-permute-start.13
  61.7 5.9 %collective-permute-start.14 = (f32[48,128]{1,0:T(8,128)S(1)}, f32[48,128]{1,0:T(8,128)S(1)}, u32[]{:S(2)}, u32[]{:S(2)}) collective-permute-start(f32[48,128]{1,0:T(8,128)S(1)} %shard_map.47.refs_3_), channel_id=1, source_target_pairs={{0,16},{2,18},{4,20},{6,22},{8,24},{10,26},{12,28},{14,30},{17,1},... | collective-permute-start | bytes 73736 | tf_op jit(solution)/shard_map/ppermute | solution.py:234
  67.7 1.5 %collective-permute-done.14 = f32[48,128]{1,0:T(8,128)S(1)} collective-permute-done((f32[48,128]{1,0:T(8,128)S(1)}, f32[48,128]{1,0:T(8,128)S(1)}, u32[]{:S(2)}, u32[]{:S(2)}) %collective-permute-start.14) | collective-permute-done | bytes 24608 | tf_op jit(solution)/shard_map/ppermute | solution.py:234
  69.2 0.6 add_select_fusion
  (16 shorter events, 0.2 us)
Async XLA Ops:
  0.0 53.3 %collective-permute-start.8 = (bf16[128,8192]{1,0:T(8,128)(2,1)}, bf16[128,8192]{1,0:T(8,128)(2,1)S(1)}, u32[]{:S(2)}, u32[]{:S(2)}) collective-permute-start(bf16[128,8192]{1,0:T(8,128)(2,1)} %refs_1_.1), channel_id=1, source_target_pairs={{0,16},{1,17},{2,18},{3,19},{4,20},{5,21},{6,22},{7,23},{8,24},{9,... | collective-permute-start | bytes 6291464 | tf_op jit(solution)/shard_map/ppermute | solution.py:234
  3.0 1.0 %copy-start.1 = (bf16[96,2048]{1,0:T(8,128)(2,1)S(1)}, bf16[96,2048]{1,0:T(8,128)(2,1)}, u32[]{:S(2)}) copy-start(bf16[96,2048]{1,0:T(8,128)(2,1)} %src_ref.1) | copy-start | bytes 1179652
  4.2 15.3 %collective-permute-start = (bf16[48,2048]{1,0:T(8,128)(2,1)S(1)}, bf16[48,2048]{1,0:T(8,128)(2,1)S(1)}, u32[]{:S(2)}, u32[]{:S(2)}) collective-permute-start(bf16[48,2048]{1,0:T(8,128)(2,1)S(1)} %shard_map.37.a_ref), channel_id=1, source_target_pairs={{0,8},{2,10},{4,12},{6,14},{9,1},{11,3},{13,5},{15,7},{16,24},{18,... | collective-permute-start | bytes 589832 | tf_op jit(solution)/shard_map/ppermute | solution.py:234
  8.7 12.4 %collective-permute-start.2 = (bf16[48,2048]{1,0:T(8,128)(2,1)S(1)}, bf16[48,2048]{1,0:T(8,128)(2,1)S(1)}, u32[]{:S(2)}, u32[]{:S(2)}) collective-permute-start(bf16[48,2048]{1,0:T(8,128)(2,1)S(1)} %shard_map.37.a_ref), channel_id=1, source_target_pairs={{0,4},{2,6},{4,0},{6,2},{9,13},{11,15},{13,9},{15,11},{16,20},{18,... | collective-permute-start | bytes 589832 | tf_op jit(solution)/shard_map/ppermute | solution.py:234
  12.2 8.9 %collective-permute-start.3 = (bf16[48,2048]{1,0:T(8,128)(2,1)S(1)}, bf16[48,2048]{1,0:T(8,128)(2,1)S(1)}, u32[]{:S(2)}, u32[]{:S(2)}) collective-permute-start(bf16[48,2048]{1,0:T(8,128)(2,1)S(1)} %shard_map.37.a_ref), channel_id=1, source_target_pairs={{0,12},{2,14},{4,8},{6,10},{9,5},{11,7},{13,1},{15,3},{16,28},{18,... | collective-permute-start | bytes 589832 | tf_op jit(solution)/shard_map/ppermute | solution.py:234
  19.6 10.7 %collective-permute-start.1 = (bf16[48,2048]{1,0:T(8,128)(2,1)S(1)}, bf16[48,2048]{1,0:T(8,128)(2,1)S(1)}, u32[]{:S(2)}, u32[]{:S(2)}) collective-permute-start(bf16[48,2048]{1,0:T(8,128)(2,1)S(1)} %shard_map.39.chunk0), channel_id=1, source_target_pairs={{0,2},{1,3},{2,0},{3,1},{4,6},{5,7},{6,4},{7,5},{8,10},{9,11},{10,... | collective-permute-start | bytes 589832 | tf_op jit(solution)/shard_map/ppermute | solution.py:234
  21.2 9.1 %collective-permute-start.4 = (bf16[48,2048]{1,0:T(8,128)(2,1)S(1)}, bf16[48,2048]{1,0:T(8,128)(2,1)S(1)}, u32[]{:S(2)}, u32[]{:S(2)}) collective-permute-start(bf16[48,2048]{1,0:T(8,128)(2,1)S(1)} %shard_map.40.chunk1), channel_id=1, source_target_pairs={{0,2},{1,3},{2,0},{3,1},{4,6},{5,7},{6,4},{7,5},{8,10},{9,11},{10,... | collective-permute-start | bytes 589832 | tf_op jit(solution)/shard_map/ppermute | solution.py:234
  30.3 23.9 %copy-start = (bf16[128,8192]{1,0:T(8,128)(2,1)S(1)}, bf16[128,8192]{1,0:T(8,128)(2,1)}, u32[]{:S(2)}) copy-start(bf16[128,8192]{1,0:T(8,128)(2,1)} %refs_1_.1) | copy-start | bytes 6291460
  35.8 3.6 %collective-permute-start.5 = (f32[48,2048]{1,0:T(8,128)S(1)}, f32[48,2048]{1,0:T(8,128)S(1)}, u32[]{:S(2)}, u32[]{:S(2)}) collective-permute-start(f32[48,2048]{1,0:T(8,128)S(1)} %shard_map.42), channel_id=1, source_target_pairs={{1,0},{3,2},{5,4},{7,6},{8,9},{10,11},{12,13},{14,15},{17,16},{19,... | collective-permute-start | bytes 1179656 | tf_op jit(solution)/shard_map/ppermute | solution.py:234
  39.5 6.4 %collective-permute-start.10 = (bf16[48,2048]{1,0:T(8,128)(2,1)S(1)}, bf16[48,2048]{1,0:T(8,128)(2,1)S(1)}, u32[]{:S(2)}, u32[]{:S(2)}) collective-permute-start(bf16[48,2048]{1,0:T(8,128)(2,1)S(1)} %add_convert_fusion.a_ref), channel_id=1, source_target_pairs={{0,8},{2,10},{4,12},{6,14},{9,1},{11,3},{13,5},{15,7},{16,24},{18,... | collective-permute-start | bytes 589832 | tf_op jit(solution)/shard_map/ppermute | solution.py:234
  41.8 11.5 %collective-permute-start.6 = (bf16[48,2048]{1,0:T(8,128)(2,1)S(1)}, bf16[48,2048]{1,0:T(8,128)(2,1)S(1)}, u32[]{:S(2)}, u32[]{:S(2)}) collective-permute-start(bf16[48,2048]{1,0:T(8,128)(2,1)S(1)} %add_convert_fusion.a_ref), channel_id=1, source_target_pairs={{0,4},{2,6},{4,0},{6,2},{9,13},{11,15},{13,9},{15,11},{16,20},{18,... | collective-permute-start | bytes 589832 | tf_op jit(solution)/shard_map/ppermute | solution.py:234
  44.6 8.7 %collective-permute-start.7 = (bf16[48,2048]{1,0:T(8,128)(2,1)S(1)}, bf16[48,2048]{1,0:T(8,128)(2,1)S(1)}, u32[]{:S(2)}, u32[]{:S(2)}) collective-permute-start(bf16[48,2048]{1,0:T(8,128)(2,1)S(1)} %add_convert_fusion.a_ref), channel_id=1, source_target_pairs={{0,12},{2,14},{4,8},{6,10},{9,5},{11,7},{13,1},{15,3},{16,28},{18,... | collective-permute-start | bytes 589832 | tf_op jit(solution)/shard_map/ppermute | solution.py:234
  45.9 8.2 %collective-permute-start.11 = (bf16[48,2048]{1,0:T(8,128)(2,1)S(1)}, bf16[48,2048]{1,0:T(8,128)(2,1)S(1)}, u32[]{:S(2)}, u32[]{:S(2)}) collective-permute-start(bf16[48,2048]{1,0:T(8,128)(2,1)S(1)} %shard_map.44.refs_0_), channel_id=1, source_target_pairs={{0,2},{1,3},{2,0},{3,1},{4,6},{5,7},{6,4},{7,5},{8,10},{9,11},{10,... | collective-permute-start | bytes 589832 | tf_op jit(solution)/shard_map/ppermute | solution.py:234
  53.3 5.8 %collective-permute-start.9 = (bf16[48,2048]{1,0:T(8,128)(2,1)S(1)}, bf16[48,2048]{1,0:T(8,128)(2,1)S(1)}, u32[]{:S(2)}, u32[]{:S(2)}) collective-permute-start(bf16[48,2048]{1,0:T(8,128)(2,1)S(1)} %shard_map.43.refs_1_), channel_id=1, source_target_pairs={{0,2},{1,3},{2,0},{3,1},{4,6},{5,7},{6,4},{7,5},{8,10},{9,11},{10,... | collective-permute-start | bytes 589832 | tf_op jit(solution)/shard_map/ppermute | solution.py:234
  59.8 7.9 %collective-permute-start.12 = (f32[48,128]{1,0:T(8,128)S(1)}, f32[48,128]{1,0:T(8,128)S(1)}, u32[]{:S(2)}, u32[]{:S(2)}) collective-permute-start(f32[48,128]{1,0:T(8,128)S(1)} %shard_map.48), channel_id=1, source_target_pairs={{1,0},{3,2},{5,4},{7,6},{9,8},{11,10},{13,12},{15,14},{16,17},{18,... | collective-permute-start | bytes 73736 | tf_op jit(solution)/shard_map/ppermute | solution.py:234
  61.1 6.6 %collective-permute-start.13 = (f32[48,128]{1,0:T(8,128)S(1)}, f32[48,128]{1,0:T(8,128)S(1)}, u32[]{:S(2)}, u32[]{:S(2)}) collective-permute-start(f32[48,128]{1,0:T(8,128)S(1)} %shard_map.47.refs_3_), channel_id=1, source_target_pairs={{1,16},{3,18},{5,20},{7,22},{9,24},{11,26},{13,28},{15,30},{16,1},... | collective-permute-start | bytes 73736 | tf_op jit(solution)/shard_map/ppermute | solution.py:234
  61.7 7.4 %collective-permute-start.14 = (f32[48,128]{1,0:T(8,128)S(1)}, f32[48,128]{1,0:T(8,128)S(1)}, u32[]{:S(2)}, u32[]{:S(2)}) collective-permute-start(f32[48,128]{1,0:T(8,128)S(1)} %shard_map.47.refs_3_), channel_id=1, source_target_pairs={{0,16},{2,18},{4,20},{6,22},{8,24},{10,26},{12,28},{14,30},{17,1},... | collective-permute-start | bytes 73736 | tf_op jit(solution)/shard_map/ppermute | solution.py:234

commit v8 on v7

--- a/solution.py
+++ b/solution.py
@@ -40,25 +40,6 @@
 ORDER = (0, 2, 1, 3)
 
 
-def cut_rows_kernel(at_ref, src_ref, out_ref, sem):
-    rows = out_ref.shape[0]
-    start = pl.multiple_of(at_ref[0] * rows, rows)
-    copy = pltpu.make_async_copy(src_ref.at[pl.ds(start, rows), :], out_ref, sem)
-    copy.start()
-    copy.wait()
-
-
-def cut_rows(src, rows, at):
-    return pl.pallas_call(
-        cut_rows_kernel,
-        out_shape=jax.ShapeDtypeStruct((rows, src.shape[1]), src.dtype),
-        in_specs=[SMEM, HBM],
-        out_specs=VMEM,
-        scratch_shapes=[pltpu.SemaphoreType.DMA],
-        compiler_params=limit(2),
-    )(scalar(at), src)
-
-
 def start_blocks(fisher_ref, at, held_ref, sem):
     steps = sem.shape[0]
     rows, width = held_ref.shape
@@ -98,21 +79,22 @@
     )(scalar(first), fisher)
 
 
-def fisher_first_kernel(at_ref, chunk0, chunk1, block0, block1, fisher_ref, out_ref, next_ref, sem):
+def fisher_first_kernel(at_ref, chunk, block, fisher_ref, out_ref, next_ref, sem):
+    steps = sem.shape[0]
+    step = block.shape[0] // steps
     copies = start_blocks(fisher_ref, at_ref[0] ^ ORDER[2], next_ref, sem)
-    step = block0.shape[0] // sem.shape[0]
-    for i in range(sem.shape[0]):
-        rows = slice(i * step, (i + 1) * step)
-        out_ref[:, rows] = times(chunk0, block0[rows, :])
-    for i in range(sem.shape[0]):
-        rows = slice(i * step, (i + 1) * step)
-        out_ref[:, rows] += times(chunk1, block1[rows, :])
+
+    @pl.loop(0, steps)
+    def _(i):
+        rows = pl.ds(pl.multiple_of(i * step, step), step)
+        out_ref[:, rows] = times(chunk, block[rows, :])
+
     for copy in copies:
         copy.wait()
 
 
-def fisher_first(chunks, blocks, first, fisher, steps=4):
-    nq, width = chunks[0].shape
+def fisher_first(chunk, block, first, fisher, steps=4):
+    nq, width = chunk.shape
     rows = fisher.shape[0]
     return pl.pallas_call(
         fisher_first_kernel,
@@ -120,42 +102,51 @@
             jax.ShapeDtypeStruct((nq, rows), jnp.float32),
             jax.ShapeDtypeStruct((rows, width), fisher.dtype),
         ],
-        in_specs=[SMEM] + [VMEM] * 4 + [HBM],
+        in_specs=[SMEM] + [VMEM] * 2 + [HBM],
         out_specs=[VMEM] * 2,
         scratch_shapes=[pltpu.SemaphoreType.DMA((steps,))],
         compiler_params=limit(8),
         cost_estimate=pl.CostEstimate(
-            flops=4 * nq * width * rows, bytes_accessed=2 * width * rows, transcendentals=0
-        ),
-    )(scalar(first), *chunks, *blocks, fisher)
-
-
-def fisher_last_kernel(at_ref, chunk0, chunk1, block0, base_ref, fisher_ref, out_ref, held, sem):
+            flops=2 * nq * width * rows, bytes_accessed=2 * width * rows, transcendentals=0
+        ),
+    )(scalar(first), chunk, block, fisher)
+
+
+def fisher_last_kernel(at_ref, chunk0, chunk1, chunk2, block0, block1, base_ref, fisher_ref, out_ref, held, sem):
+    steps = sem.shape[0]
+    step = held.shape[0] // steps
     copies = start_blocks(fisher_ref, at_ref[0] ^ ORDER[3], held, sem)
-    step = held.shape[0] // sem.shape[0]
-    for i in range(sem.shape[0]):
-        rows = slice(i * step, (i + 1) * step)
+
+    @pl.loop(0, steps)
+    def _(i):
+        rows = pl.ds(pl.multiple_of(i * step, step), step)
         out_ref[:, rows] = base_ref[:, rows] + times(chunk0, block0[rows, :])
-    for i in range(sem.shape[0]):
+
+    @pl.loop(0, steps)
+    def _(i):
+        rows = pl.ds(pl.multiple_of(i * step, step), step)
+        out_ref[:, rows] += times(chunk1, block1[rows, :])
+
+    for i in range(steps):
         rows = slice(i * step, (i + 1) * step)
         copies[i].wait()
-        out_ref[:, rows] += times(chunk1, held[rows, :])
-
-
-def fisher_last(chunks, block, base, first, fisher, steps=4):
+        out_ref[:, rows] += times(chunk2, held[rows, :])
+
+
+def fisher_last(chunks, blocks, base, first, fisher, steps=4):
     nq, width = chunks[0].shape
     rows = fisher.shape[0]
     return pl.pallas_call(
         fisher_last_kernel,
         out_shape=jax.ShapeDtypeStruct((nq, rows), jnp.float32),
-        in_specs=[SMEM] + [VMEM] * 4 + [HBM],
+        in_specs=[SMEM] + [VMEM] * 6 + [HBM],
         out_specs=VMEM,
         scratch_shapes=[pltpu.VMEM((rows, width), fisher.dtype), pltpu.SemaphoreType.DMA((steps,))],
         compiler_params=limit(16),
         cost_estimate=pl.CostEstimate(
-            flops=4 * nq * width * rows, bytes_accessed=2 * width * rows, transcendentals=0
-        ),
-    )(scalar(first), *chunks, block, base, fisher)
+            flops=6 * nq * width * rows, bytes_accessed=2 * width * rows, transcendentals=0
+        ),
+    )(scalar(first), *chunks, *blocks, base, fisher)
 
 
 def score_kernel(order, has_base, at_ref, *refs):
@@ -233,13 +224,13 @@
                             pairs.append(((sy * nex + sz * nx + sx) * 2 + sd, (ty * nex + tz * nx + tx) * 2 + td))
         return lax.ppermute(value, AXES, pairs)
 
-    def along_z(value, hops):
+    def along_z(value, hops, flip=False):
         def target(sy, sz, sx, sd):
             su = sz if sd == 0 else nz - 1 - sz
             if su not in hops:
                 return None
             tu = hops[su]
-            return sy, tu if sd == 0 else nz - 1 - tu, sx, sd
+            return sy, tu if sd == 0 else nz - 1 - tu, 1 - sx if flip else sx, sd
 
         return move(value, target)
 
@@ -256,32 +247,33 @@
 
         return move(value, target)
 
-    def gather(own, after=((), ())):
-        first = pick(owner, own, along_z(own, {0: 2, 1: 3}), after[0])
-        second = pick(owner, along_z(own, {0: 1, 1: 0}), along_z(own, {0: 3, 1: 2}), after[1])
-        return [first, second, swap_x(first), swap_x(second)]
+    def gather(own, after=()):
+        first = pick(owner, own, along_z(own, {0: 2, 1: 3}), after)
+        pairs = {0: 1, 1: 0, 2: 3, 3: 2}
+        return [first, along_z(first, pairs), swap_x(first), along_z(first, pairs, True)]
 
     plane = jnp.where(d == 0, u % 2, nz - 1 - u % 2)
     column = plane * nx + x - d * (nex // 2)
 
     other_grads = swap_y(stored_grads)
 
-    own = cut_rows(queries, nq // ny, y)
+    rows = nq // ny
+    own = lax.optimization_barrier(lax.dynamic_slice_in_dim(queries, y * rows, rows, axis=0))
     blocks = load(inverse_fisher, column, 2, own.shape[1])
-    pieces = gather(own, (blocks[:1], ()))
-    total, block = fisher_first(pieces[:2], blocks, column, inverse_fisher)
-    total = fisher_last(pieces[2:], block, total, column, inverse_fisher)
+    pieces = gather(own, blocks[:1])
+    total, block = fisher_first(pieces[0], blocks[0], column, inverse_fisher)
+    total = fisher_last(pieces[1:], (blocks[1], block), total, column, inverse_fisher)
     panel = (total + to_owner(total)).astype(jnp.bfloat16)
 
-    pieces = gather(panel, ((), (other_grads,)))
+    pieces = gather(panel)
     other, mine = (score_dot(pieces[:3], ORDER[:3], column, g) for g in (other_grads, stored_grads))
     other = score_dot(pieces[3:], ORDER[3:], column, other_grads, other)
     mine = score_dot(pieces[3:], ORDER[3:], column, stored_grads, mine, (other,))
-    other = move(other, lambda sy, sz, sx, sd: (1 - sy, sz, sx, sy) if sd != sy else None) + move(
-        other, lambda sy, sz, sx, sd: (1 - sy, sz, sx, sy) if sd == sy else None
-    )
-    mine = mine + move(mine, lambda sy, sz, sx, sd: (sy, sz, sx, sy) if sd != sy else None)
-    return jnp.where(d == y, mine, other)
+
+    other = swap_y(other)
+    keep = jnp.where(d == y, mine, other)
+    give = jnp.where(d == y, other, mine)
+    return keep + move(give, lambda sy, sz, sx, sd: (sy, sz, sx, 1 - sd))
 
 
 def solution(mesh):

time: 70.1 us -> 66.2 us (0.944)
  starting transfers between devices: 31.3 us -> 21 us
  waiting for transfers between devices: 14.4 us -> 20.6 us
  local copies, waits for them, and re-layouts: 1 us -> 3.19 us
  Pallas kernels: 22.2 us -> 20.3 us
    ppermute x15 -> x12, starting transfers between devices: 31.3 us -> 21 us  [move(): return lax.ppermute(value, AXES, pairs)]
    ppermute x15 -> x12, waiting for transfers between devices: 14.4 us -> 20.6 us  [move(): return lax.ppermute(value, AXES, pairs)]
    pallas_call x1, Pallas kernels: 8.47 us -> 3.51 us  [fisher_first(): pl.pallas_call(fisher_first_kernel, out_shape=[jax.ShapeDtypeStruct((nq,...]
    pallas_call x1, Pallas kernels: 5.53 us -> 8.97 us  [fisher_last(): pl.pallas_call(fisher_last_kernel, out_shape=jax.ShapeDtypeStruct((nq, ro...]
    unnamed x4 -> x6, local copies, waits for them, and re-layouts: 1 us -> 3.18 us
  transfers between devices with their start and end apart: 15 -> 12, of which waited for: 4 -> 7; matrix products, arithmetic and copies ran while one was open for 0% -> 0% of each run, Pallas kernels for 31% -> 30%
where the time goes in v8:
time: 66.2 us; the launch traced here: 66 us
  starting transfers between devices  21 us (32%)
  waiting for transfers between devices  20.6 us (31%)
  Pallas kernels  20.3 us (31%)
  local copies, waits for them, and re-layouts  3.19 us (5%)
    ppermute x12, starting transfers between devices, move(): return lax.ppermute(value, AXES, pairs)  21 us
    ppermute x12, waiting for transfers between devices, move(): return lax.ppermute(value, AXES, pairs)  20.6 us
    pallas_call x1, Pallas kernels, fisher_last(): pl.pallas_call(fisher_last_kernel, out_shape=jax.ShapeDtypeStruct((nq, ro...  8.97 us
    pallas_call x1, Pallas kernels, load(): pl.pallas_call(load_kernel, out_shape=[jax.ShapeDtypeStruct((fisher.shape...  5.96 us
    pallas_call x1, Pallas kernels, fisher_first(): pl.pallas_call(fisher_first_kernel, out_shape=[jax.ShapeDtypeStruct((nq,...  3.51 us
    unnamed x6, local copies, waits for them, and re-layouts  3.18 us
    pallas_call x4, Pallas kernels, score_dot(): pl.pallas_call(functools.partial(score_kernel, order, base is not None),...  1.86 us
  transfers between devices with their start and end apart: 12, of which 7 were waited for; matrix products, arithmetic and copies ran while one was open for 0% of the time, Pallas kernels for 30%

profile of v8, /device:TPU:0, one launch (start us, length us, event | category | flops | bytes accessed | tf_op | source)
XLA Modules:
  0.0 66.0 jit_solution(16223573473878755953)
XLA Ops:
  0.0 3.0 %collective-permute-start.9 = (bf16[128,8192]{1,0:T(8,128)(2,1)}, bf16[128,8192]{1,0:T(8,128)(2,1)S(1)}, u32[]{:S(2)}, u32[]{:S(2)}) collective-permute-start(bf16[128,8192]{1,0:T(8,128)(2,1)} %refs_1_.1), channel_id=1, source_target_pairs={{0,16},{1,17},{2,18},{3,19},{4,20},{5,21},{6,22},{7,23},{8,24},{9,... | collective-permute-start | bytes 6291464 | tf_op jit(solution)/shard_map/ppermute | solution.py:225
  3.0 4.5 %collective-permute-start = (bf16[48,2048]{1,0:T(8,128)(2,1)S(1)}, bf16[48,2048]{1,0:T(8,128)(2,1)S(1)}, u32[]{:S(2)}, u32[]{:S(2)}) collective-permute-start(bf16[48,2048]{1,0:T(8,128)(2,1)S(1)} %constant_dynamic-slice_fusion.a_ref), channel_id=1, source_target_pairs={{0,8},{2,10},{4,12},{6,14},{9,1},{11,3},{13,5},{15,7},{16,24},{18,... | collective-permute-start | bytes 589832 | tf_op jit(solution)/shard_map/ppermute | solution.py:225
  7.5 6.0 %shard_map.37 = (bf16[2048,2048]{1,0:T(8,128)(2,1)S(1)}, bf16[2048,2048]{1,0:T(8,128)(2,1)S(1)}) custom-call(s32[1]{0:T(128)} %bitcast.at_ref, bf16[2048,8192]{1,0:T(8,128)(2,1)} %fisher_ref.5), custom_call_target="tpu_custom_call" | custom-call | bytes 16777216 | tf_op jit(solution)/shard_map/pallas_call | solution.py:69
  13.5 0.0 collective-permute-done.b_ref
  13.6 1.6 %collective-permute-start.1 = (bf16[48,2048]{1,0:T(8,128)(2,1)S(1)}, bf16[48,2048]{1,0:T(8,128)(2,1)S(1)}, u32[]{:S(2)}, u32[]{:S(2)}) collective-permute-start(bf16[48,2048]{1,0:T(8,128)(2,1)S(1)} %shard_map.38.chunk), channel_id=1, source_target_pairs={{0,4},{1,5},{2,6},{3,7},{4,0},{5,1},{6,2},{7,3},{8,12},{9,13},{10,... | collective-permute-start | bytes 589832 | tf_op jit(solution)/shard_map/ppermute | solution.py:225
  15.2 1.5 %collective-permute-start.2 = (bf16[48,2048]{1,0:T(8,128)(2,1)S(1)}, bf16[48,2048]{1,0:T(8,128)(2,1)S(1)}, u32[]{:S(2)}, u32[]{:S(2)}) collective-permute-start(bf16[48,2048]{1,0:T(8,128)(2,1)S(1)} %shard_map.38.chunk), channel_id=1, source_target_pairs={{0,2},{1,3},{2,0},{3,1},{4,6},{5,7},{6,4},{7,5},{8,10},{9,11},{10,... | collective-permute-start | bytes 589832 | tf_op jit(solution)/shard_map/ppermute | solution.py:225
  16.7 0.4 collective-permute-start.3
  17.1 3.5 %shard_map.39 = (f32[48,2048]{1,0:T(8,128)S(1)}, bf16[2048,2048]{1,0:T(8,128)(2,1)S(1)}) custom-call(s32[1]{0:T(128)} %bitcast.at_ref, bf16[48,2048]{1,0:T(8,128)(2,1)S(1)} %shard_map.38.chunk, bf16[2048,2048]{1,0:T(8,128)(2,1)S(1)} %get-tuple-element.9.refs_0_.block, bf16[2048,8192]{1,0:T(8,128)(2,1)} %fisher_ref.5), custom_call_target="tpu_custom_call" | custom-call | flops 402653184 | bytes 8388608 | tf_op jit(solution)/shard_map/pallas_call | solution.py:99
  20.6 0.3 collective-permute-done.1.chunk0
  21.0 3.3 %collective-permute-done.2.chunk1 = bf16[48,2048]{1,0:T(8,128)(2,1)S(1)} collective-permute-done((bf16[48,2048]{1,0:T(8,128)(2,1)S(1)}, bf16[48,2048]{1,0:T(8,128)(2,1)S(1)}, u32[]{:S(2)}, u32[]{:S(2)}) %collective-permute-start.2) | collective-permute-done | bytes 196640 | tf_op jit(solution)/shard_map/ppermute | solution.py:225
  24.3 9.0 %shard_map.40 = f32[48,2048]{1,0:T(8,128)S(1)} custom-call(s32[1]{0:T(128)} %bitcast.at_ref, bf16[48,2048]{1,0:T(8,128)(2,1)S(1)} %collective-permute-done.1.chunk0, bf16[48,2048]{1,0:T(8,128)(2,1)S(1)} %collective-permute-done.2.chunk1, bf16[48,2048]{1,0:T(8,128)(2,1)S(1)} %collective-permute-done.3.chunk2, ...), custom_call_target="tpu_custom_call" | custom-call | flops 1207959552 | bytes 8388608 | tf_op jit(solution)/shard_map/pallas_call | solution.py:139
  33.3 1.3 %collective-permute-start.4 = (f32[48,2048]{1,0:T(8,128)S(1)}, f32[48,2048]{1,0:T(8,128)S(1)}, u32[]{:S(2)}, u32[]{:S(2)}) collective-permute-start(f32[48,2048]{1,0:T(8,128)S(1)} %shard_map.40), channel_id=1, source_target_pairs={{1,0},{3,2},{5,4},{7,6},{8,9},{10,11},{12,13},{14,15},{17,16},{19,... | collective-permute-start | bytes 1179656 | tf_op jit(solution)/shard_map/ppermute | solution.py:225
  34.6 2.3 %collective-permute-done.4 = f32[48,2048]{1,0:T(8,128)S(1)} collective-permute-done((f32[48,2048]{1,0:T(8,128)S(1)}, f32[48,2048]{1,0:T(8,128)S(1)}, u32[]{:S(2)}, u32[]{:S(2)}) %collective-permute-start.4) | collective-permute-done | bytes 393248 | tf_op jit(solution)/shard_map/ppermute | solution.py:225
  36.9 2.8 %collective-permute-start.5 = (bf16[48,2048]{1,0:T(8,128)(2,1)S(1)}, bf16[48,2048]{1,0:T(8,128)(2,1)S(1)}, u32[]{:S(2)}, u32[]{:S(2)}) collective-permute-start(bf16[48,2048]{1,0:T(8,128)(2,1)S(1)} %add_convert_fusion.a_ref), channel_id=1, source_target_pairs={{0,8},{2,10},{4,12},{6,14},{9,1},{11,3},{13,5},{15,7},{16,24},{18,... | collective-permute-start | bytes 589832 | tf_op jit(solution)/shard_map/ppermute | solution.py:225
  39.7 3.2 %collective-permute-done.5.b_ref = bf16[48,2048]{1,0:T(8,128)(2,1)S(1)} collective-permute-done((bf16[48,2048]{1,0:T(8,128)(2,1)S(1)}, bf16[48,2048]{1,0:T(8,128)(2,1)S(1)}, u32[]{:S(2)}, u32[]{:S(2)}) %collective-permute-start.5) | collective-permute-done | bytes 196640 | tf_op jit(solution)/shard_map/ppermute | solution.py:225
  42.9 3.0 %collective-permute-start.7 = (bf16[48,2048]{1,0:T(8,128)(2,1)S(1)}, bf16[48,2048]{1,0:T(8,128)(2,1)S(1)}, u32[]{:S(2)}, u32[]{:S(2)}) collective-permute-start(bf16[48,2048]{1,0:T(8,128)(2,1)S(1)} %shard_map.41.refs_0_), channel_id=1, source_target_pairs={{0,4},{1,5},{2,6},{3,7},{4,0},{5,1},{6,2},{7,3},{8,12},{9,13},{10,... | collective-permute-start | bytes 589832 | tf_op jit(solution)/shard_map/ppermute | solution.py:225
  45.9 0.6 collective-permute-start.8
  46.5 1.0 %collective-permute-start.6 = (bf16[48,2048]{1,0:T(8,128)(2,1)S(1)}, bf16[48,2048]{1,0:T(8,128)(2,1)S(1)}, u32[]{:S(2)}, u32[]{:S(2)}) collective-permute-start(bf16[48,2048]{1,0:T(8,128)(2,1)S(1)} %shard_map.41.refs_0_), channel_id=1, source_target_pairs={{0,6},{1,7},{2,4},{3,5},{4,2},{5,3},{6,0},{7,1},{8,14},{9,15},{10,... | collective-permute-start | bytes 589832 | tf_op jit(solution)/shard_map/ppermute | solution.py:225
  47.4 3.8 %collective-permute-done.7.refs_1_ = bf16[48,2048]{1,0:T(8,128)(2,1)S(1)} collective-permute-done((bf16[48,2048]{1,0:T(8,128)(2,1)S(1)}, bf16[48,2048]{1,0:T(8,128)(2,1)S(1)}, u32[]{:S(2)}, u32[]{:S(2)}) %collective-permute-start.7) | collective-permute-done | bytes 196640 | tf_op jit(solution)/shard_map/ppermute | solution.py:225
  51.2 6.4 %collective-permute-done.8.refs_2_ = bf16[48,2048]{1,0:T(8,128)(2,1)S(1)} collective-permute-done((bf16[48,2048]{1,0:T(8,128)(2,1)S(1)}, bf16[48,2048]{1,0:T(8,128)(2,1)S(1)}, u32[]{:S(2)}, u32[]{:S(2)}) %collective-permute-start.8) | collective-permute-done | bytes 196640 | tf_op jit(solution)/shard_map/ppermute | solution.py:225
  57.6 0.0 collective-permute-done.9.refs_3_.refs_1_
  57.6 0.6 shard_map.43.refs_2_
  58.3 0.3 shard_map.44.refs_3_
  58.6 1.3 %collective-permute-start.10 = (f32[48,128]{1,0:T(8,128)S(1)}, f32[48,128]{1,0:T(8,128)S(1)}, u32[]{:S(2)}, u32[]{:S(2)}) collective-permute-start(f32[48,128]{1,0:T(8,128)S(1)} %shard_map.44.refs_3_), channel_id=1, source_target_pairs={{0,16},{1,17},{2,18},{3,19},{4,20},{5,21},{6,22},{7,23},{8,24},{9,... | collective-permute-start | bytes 73736 | tf_op jit(solution)/shard_map/ppermute | solution.py:225
  59.9 1.6 %copy-done.1 = bf16[128,8192]{1,0:T(8,128)(2,1)S(1)} copy-done((bf16[128,8192]{1,0:T(8,128)(2,1)S(1)}, bf16[128,8192]{1,0:T(8,128)(2,1)}, u32[]{:S(2)}) %copy-start.1) | copy-done | bytes 2097176
  61.5 0.6 shard_map.42.refs_2_
  62.2 0.0 copy-start.2
  62.2 1.6 %copy-done.2 = bf16[128,8192]{1,0:T(8,128)(2,1)S(1)} copy-done((bf16[128,8192]{1,0:T(8,128)(2,1)S(1)}, bf16[128,8192]{1,0:T(8,128)(2,1)}, u32[]{:S(2)}) %copy-start.2) | copy-done | bytes 2097176
  63.8 0.3 shard_map.45
  64.1 0.1 collective-permute-start.11
  64.2 1.2 %collective-permute-done.11 = f32[48,128]{1,0:T(8,128)S(1)} collective-permute-done((f32[48,128]{1,0:T(8,128)S(1)}, f32[48,128]{1,0:T(8,128)S(1)}, u32[]{:S(2)}, u32[]{:S(2)}) %collective-permute-start.11) | collective-permute-done | bytes 24608 | tf_op jit(solution)/shard_map/ppermute | solution.py:225
  65.3 0.6 select_add_fusion
  (11 shorter events, 0.1 us)
Async XLA Ops:
  0.0 3.0 %copy-start = (bf16[96,2048]{1,0:T(8,128)(2,1)S(1)}, bf16[96,2048]{1,0:T(8,128)(2,1)}, u32[]{:S(2)}) copy-start(bf16[96,2048]{1,0:T(8,128)(2,1)} %param.3) | copy-start | bytes 1179652
  0.0 57.6 %collective-permute-start.9 = (bf16[128,8192]{1,0:T(8,128)(2,1)}, bf16[128,8192]{1,0:T(8,128)(2,1)S(1)}, u32[]{:S(2)}, u32[]{:S(2)}) collective-permute-start(bf16[128,8192]{1,0:T(8,128)(2,1)} %refs_1_.1), channel_id=1, source_target_pairs={{0,16},{1,17},{2,18},{3,19},{4,20},{5,21},{6,22},{7,23},{8,24},{9,... | collective-permute-start | bytes 6291464 | tf_op jit(solution)/shard_map/ppermute | solution.py:225
  3.0 10.5 %collective-permute-start = (bf16[48,2048]{1,0:T(8,128)(2,1)S(1)}, bf16[48,2048]{1,0:T(8,128)(2,1)S(1)}, u32[]{:S(2)}, u32[]{:S(2)}) collective-permute-start(bf16[48,2048]{1,0:T(8,128)(2,1)S(1)} %constant_dynamic-slice_fusion.a_ref), channel_id=1, source_target_pairs={{0,8},{2,10},{4,12},{6,14},{9,1},{11,3},{13,5},{15,7},{16,24},{18,... | collective-permute-start | bytes 589832 | tf_op jit(solution)/shard_map/ppermute | solution.py:225
  13.6 7.4 %collective-permute-start.1 = (bf16[48,2048]{1,0:T(8,128)(2,1)S(1)}, bf16[48,2048]{1,0:T(8,128)(2,1)S(1)}, u32[]{:S(2)}, u32[]{:S(2)}) collective-permute-start(bf16[48,2048]{1,0:T(8,128)(2,1)S(1)} %shard_map.38.chunk), channel_id=1, source_target_pairs={{0,4},{1,5},{2,6},{3,7},{4,0},{5,1},{6,2},{7,3},{8,12},{9,13},{10,... | collective-permute-start | bytes 589832 | tf_op jit(solution)/shard_map/ppermute | solution.py:225
  15.2 9.1 %collective-permute-start.2 = (bf16[48,2048]{1,0:T(8,128)(2,1)S(1)}, bf16[48,2048]{1,0:T(8,128)(2,1)S(1)}, u32[]{:S(2)}, u32[]{:S(2)}) collective-permute-start(bf16[48,2048]{1,0:T(8,128)(2,1)S(1)} %shard_map.38.chunk), channel_id=1, source_target_pairs={{0,2},{1,3},{2,0},{3,1},{4,6},{5,7},{6,4},{7,5},{8,10},{9,11},{10,... | collective-permute-start | bytes 589832 | tf_op jit(solution)/shard_map/ppermute | solution.py:225
  16.7 7.6 %collective-permute-start.3 = (bf16[48,2048]{1,0:T(8,128)(2,1)S(1)}, bf16[48,2048]{1,0:T(8,128)(2,1)S(1)}, u32[]{:S(2)}, u32[]{:S(2)}) collective-permute-start(bf16[48,2048]{1,0:T(8,128)(2,1)S(1)} %shard_map.38.chunk), channel_id=1, source_target_pairs={{0,6},{1,7},{2,4},{3,5},{4,2},{5,3},{6,0},{7,1},{8,14},{9,15},{10,... | collective-permute-start | bytes 589832 | tf_op jit(solution)/shard_map/ppermute | solution.py:225
  33.3 3.6 %collective-permute-start.4 = (f32[48,2048]{1,0:T(8,128)S(1)}, f32[48,2048]{1,0:T(8,128)S(1)}, u32[]{:S(2)}, u32[]{:S(2)}) collective-permute-start(f32[48,2048]{1,0:T(8,128)S(1)} %shard_map.40), channel_id=1, source_target_pairs={{1,0},{3,2},{5,4},{7,6},{8,9},{10,11},{12,13},{14,15},{17,16},{19,... | collective-permute-start | bytes 1179656 | tf_op jit(solution)/shard_map/ppermute | solution.py:225
  36.9 6.0 %collective-permute-start.5 = (bf16[48,2048]{1,0:T(8,128)(2,1)S(1)}, bf16[48,2048]{1,0:T(8,128)(2,1)S(1)}, u32[]{:S(2)}, u32[]{:S(2)}) collective-permute-start(bf16[48,2048]{1,0:T(8,128)(2,1)S(1)} %add_convert_fusion.a_ref), channel_id=1, source_target_pairs={{0,8},{2,10},{4,12},{6,14},{9,1},{11,3},{13,5},{15,7},{16,24},{18,... | collective-permute-start | bytes 589832 | tf_op jit(solution)/shard_map/ppermute | solution.py:225
  42.9 8.3 %collective-permute-start.7 = (bf16[48,2048]{1,0:T(8,128)(2,1)S(1)}, bf16[48,2048]{1,0:T(8,128)(2,1)S(1)}, u32[]{:S(2)}, u32[]{:S(2)}) collective-permute-start(bf16[48,2048]{1,0:T(8,128)(2,1)S(1)} %shard_map.41.refs_0_), channel_id=1, source_target_pairs={{0,4},{1,5},{2,6},{3,7},{4,0},{5,1},{6,2},{7,3},{8,12},{9,13},{10,... | collective-permute-start | bytes 589832 | tf_op jit(solution)/shard_map/ppermute | solution.py:225
  45.9 11.7 %collective-permute-start.8 = (bf16[48,2048]{1,0:T(8,128)(2,1)S(1)}, bf16[48,2048]{1,0:T(8,128)(2,1)S(1)}, u32[]{:S(2)}, u32[]{:S(2)}) collective-permute-start(bf16[48,2048]{1,0:T(8,128)(2,1)S(1)} %shard_map.41.refs_0_), channel_id=1, source_target_pairs={{0,2},{1,3},{2,0},{3,1},{4,6},{5,7},{6,4},{7,5},{8,10},{9,11},{10,... | collective-permute-start | bytes 589832 | tf_op jit(solution)/shard_map/ppermute | solution.py:225
  46.5 11.8 %collective-permute-start.6 = (bf16[48,2048]{1,0:T(8,128)(2,1)S(1)}, bf16[48,2048]{1,0:T(8,128)(2,1)S(1)}, u32[]{:S(2)}, u32[]{:S(2)}) collective-permute-start(bf16[48,2048]{1,0:T(8,128)(2,1)S(1)} %shard_map.41.refs_0_), channel_id=1, source_target_pairs={{0,6},{1,7},{2,4},{3,5},{4,2},{5,3},{6,0},{7,1},{8,14},{9,15},{10,... | collective-permute-start | bytes 589832 | tf_op jit(solution)/shard_map/ppermute | solution.py:225
  58.6 5.5 %collective-permute-start.10 = (f32[48,128]{1,0:T(8,128)S(1)}, f32[48,128]{1,0:T(8,128)S(1)}, u32[]{:S(2)}, u32[]{:S(2)}) collective-permute-start(f32[48,128]{1,0:T(8,128)S(1)} %shard_map.44.refs_3_), channel_id=1, source_target_pairs={{0,16},{1,17},{2,18},{3,19},{4,20},{5,21},{6,22},{7,23},{8,24},{9,... | collective-permute-start | bytes 73736 | tf_op jit(solution)/shard_map/ppermute | solution.py:225
  59.9 1.6 %copy-start.1 = (bf16[128,8192]{1,0:T(8,128)(2,1)S(1)}, bf16[128,8192]{1,0:T(8,128)(2,1)}, u32[]{:S(2)}) copy-start(bf16[128,8192]{1,0:T(8,128)(2,1)} %refs_1_.1) | copy-start | bytes 6291460
  62.2 1.6 %copy-start.2 = (bf16[128,8192]{1,0:T(8,128)(2,1)S(1)}, bf16[128,8192]{1,0:T(8,128)(2,1)}, u32[]{:S(2)}) copy-start(bf16[128,8192]{1,0:T(8,128)(2,1)} %refs_1_.1) | copy-start | bytes 6291460
  64.1 1.3 %collective-permute-start.11 = (f32[48,128]{1,0:T(8,128)S(1)}, f32[48,128]{1,0:T(8,128)S(1)}, u32[]{:S(2)}, u32[]{:S(2)}) collective-permute-start(f32[48,128]{1,0:T(8,128)S(1)} %broadcast_select_fusion), channel_id=1, source_target_pairs={{0,1},{1,0},{2,3},{3,2},{4,5},{5,4},{6,7},{7,6},{8,9},{9,8},{10,11... | collective-permute-start | bytes 73736 | tf_op jit(solution)/shard_map/ppermute | solution.py:225

commit v9 on v8

v9 whole, which is shorter than its diff:
```python
import functools

import jax
import jax.numpy as jnp
from jax import lax
from jax.experimental import pallas as pl
from jax.experimental.pallas import tpu as pltpu
from jax.sharding import PartitionSpec as P

AXES = ("grp", "ex", "dim")
NT = (((1,), (1,)), ((), ()))
VMEM = pl.BlockSpec(memory_space=pltpu.VMEM)
SMEM = pl.BlockSpec(memory_space=pltpu.SMEM)
HBM = pl.BlockSpec(memory_space=pltpu.HBM)
ANY = pl.BlockSpec(memory_space=pl.ANY)


def limit(mib):
    return pltpu.CompilerParams(vmem_limit_bytes=mib * 1024 * 1024)


def per_device_any(queries, inverse_fisher, stored_grads):
    term_block = jnp.dot(queries, inverse_fisher, preferred_element_type=jnp.float32)
    own_panel = lax.psum_scatter(term_block, "ex", scatter_dimension=1, tiled=True).astype(
        jnp.bfloat16
    )
    partial_scores = lax.dot_general(
        lax.all_gather(own_panel, "ex", axis=1, tiled=True),
        stored_grads,
        NT,
        preferred_element_type=jnp.float32,
    )
    return lax.psum_scatter(partial_scores, "dim", scatter_dimension=0, tiled=True)


def scalar(value):
    return jnp.asarray(value, jnp.int32).reshape(1)


ORDER = (0, 2, 1, 3)


def start_half(fisher_ref, block, half, held_ref, sem):
    steps = sem.shape[0]
    rows, width = held_ref.shape
    step = rows // steps
    columns = pl.ds(pl.multiple_of(block * width, width), width)
    copies = []
    for i in range(steps):
        copies.append(
            pltpu.make_async_copy(
                fisher_ref.at[pl.ds(half * rows + i * step, step), columns],
                held_ref.at[pl.ds(i * step, step), :],
                sem.at[i],
            )
        )
        copies[-1].start()
    return copies


def times(chunk_ref, fisher):
    return lax.dot_general(chunk_ref[...], fisher, NT, preferred_element_type=jnp.float32)


def fisher_kernel(n_in, has_base, fetch, step, *refs):
    if fetch:
        at_ref, fisher_ref, *refs = refs
    chunk_ref, halves = (refs[0], refs[1:3]) if n_in else (None, ())
    base_ref = refs[3] if has_base else None
    outs, sem = refs[n_in + has_base : -1], refs[-1]
    held = outs[1:] if n_in else outs
    copies = []
    for k, (piece, half) in enumerate(fetch):
        copies += start_half(fisher_ref, at_ref[0] ^ ORDER[piece], half, held[k], sem.at[k])
    for h, half_ref in enumerate(halves):
        rows = half_ref.shape[0]

        @pl.loop(0, rows // step)
        def _(i):
            columns = pl.ds(pl.multiple_of(h * rows + i * step, step), step)
            term = times(chunk_ref, half_ref[pl.ds(pl.multiple_of(i * step, step), step), :])
            outs[0][:, columns] = term + base_ref[:, columns] if has_base else term

    for copy in copies:
        copy.wait()


def fisher_step(fisher, first, width, fetch, chunk=None, halves=(), base=None, step=512):
    rows = fisher.shape[0]
    ins = [] if chunk is None else [chunk, *halves]
    has_base = base is not None
    held = jax.ShapeDtypeStruct((rows // 2, width), fisher.dtype)
    out_shape = [] if chunk is None else [jax.ShapeDtypeStruct((chunk.shape[0], rows), jnp.float32)]
    out_shape += [held] * len(fetch)
    return pl.pallas_call(
        functools.partial(fisher_kernel, len(ins), has_base, fetch, step),
        out_shape=out_shape,
        in_specs=[SMEM, HBM][: 2 * bool(fetch)] + [VMEM] * (len(ins) + has_base),
        out_specs=[VMEM] * len(out_shape),
        scratch_shapes=[pltpu.SemaphoreType.DMA((max(len(fetch), 1), 2))],
        compiler_params=limit(34 if chunk is None else 20),
        cost_estimate=pl.CostEstimate(
            flops=0 if chunk is None else 2 * chunk.shape[0] * width * rows,
            bytes_accessed=width * rows * len(fetch),
            transcendentals=0,
        ),
    )(*((scalar(first), fisher) if fetch else ()), *ins, *([base] if has_base else []))


def score_kernel(order, n_grads, has_base, at_ref, *refs):
    n = len(order)
    width = refs[0].shape[1]
    for g in range(n_grads):
        grads_ref, out_ref = refs[n + g], refs[-n_grads + g]
        total = refs[n + n_grads + g][...] if has_base else None
        for k in range(n):
            start = pl.multiple_of((at_ref[0] ^ order[k]) * width, width)
            term = times(refs[k], grads_ref[:, pl.ds(start, width)])
            total = term if total is None else total + term
        out_ref[...] = total


def score_dot(pieces, order, first, grads, base=(), after=()):
    n = len(pieces)
    rows, width = pieces[0].shape
    operands = [*pieces, *grads, *base]
    return pl.pallas_call(
        functools.partial(score_kernel, order, len(grads), len(base) > 0),
        out_shape=[jax.ShapeDtypeStruct((rows, g.shape[0]), jnp.float32) for g in grads],
        in_specs=[SMEM] + [VMEM] * len(operands) + [ANY] * len(after),
        out_specs=[VMEM] * len(grads),
        compiler_params=limit(8),
        cost_estimate=pl.CostEstimate(
            flops=2 * n * rows * width * grads[0].shape[0] * len(grads),
            bytes_accessed=2 * n * width * grads[0].shape[0] * len(grads),
            transcendentals=0,
        ),
    )(scalar(first), *operands, *after)


def pick_kernel(at_ref, a_ref, b_ref, *refs):
    out_ref = refs[-1]

    @pl.when(at_ref[0] == 1)
    def _():
        out_ref[...] = a_ref[...]

    @pl.when(at_ref[0] != 1)
    def _():
        out_ref[...] = b_ref[...]


def pick(condition, a, b, after=()):
    return pl.pallas_call(
        pick_kernel,
        out_shape=jax.ShapeDtypeStruct(a.shape, a.dtype),
        in_specs=[SMEM] + [VMEM] * 2 + [ANY] * len(after),
        out_specs=VMEM,
        compiler_params=limit(2),
        cost_estimate=pl.CostEstimate(flops=0, bytes_accessed=2 * a.size * 2, transcendentals=0),
    )(scalar(condition), a, b, *after)


def per_device_quad(nz, nx, ny, queries, inverse_fisher, stored_grads):
    nex = nz * nx
    near = nz // 2
    nq = queries.shape[0]
    y, e, d = (lax.axis_index(a) for a in AXES)
    z = e // nx
    x = e % nx
    u = jnp.where(d == 0, z, nz - 1 - z)
    owner = u < near

    def move(value, target):
        pairs = []
        for sy in range(ny):
            for sz in range(nz):
                for sx in range(nx):
                    for sd in range(2):
                        to = target(sy, sz, sx, sd)
                        if to is not None:
                            ty, tz, tx, td = to
                            pairs.append(((sy * nex + sz * nx + sx) * 2 + sd, (ty * nex + tz * nx + tx) * 2 + td))
        return lax.ppermute(value, AXES, pairs)

    def along_z(value, hops, flip=False):
        def target(sy, sz, sx, sd):
            su = sz if sd == 0 else nz - 1 - sz
            if su not in hops:
                return None
            tu = hops[su]
            return sy, tu if sd == 0 else nz - 1 - tu, 1 - sx if flip else sx, sd

        return move(value, target)

    def swap_y(value):
        return move(value, lambda sy, sz, sx, sd: (1 - sy, sz, sx, sd))

    def to_owner(value):
        def target(sy, sz, sx, sd):
            su = sz if sd == 0 else nz - 1 - sz
            return None if su < near else (sy, sz, sx, 1 - sd)

        return move(value, target)

    def gather(own, after=()):
        far = along_z(own, {0: 2, 1: 3})
        steps = (((0, 1), (1, 0)), False), (((0, 0), (1, 1)), True), (((0, 1), (1, 0)), True)
        near = [along_z(own, dict(hops), flip) for hops, flip in steps]
        first = pick(owner, own, far, after)
        gate = pick(owner, first, first, near)

        def piece(k, after=()):
            if k == 0:
                return first
            hops, flip = steps[k - 1]
            hops = {2 + s: 2 + t for s, t in hops}
            return pick(owner, near[k - 1], along_z(gate, hops, flip), after)

        return piece

    plane = jnp.where(d == 0, u % 2, nz - 1 - u % 2)
    column = plane * nx + x - d * (nex // 2)

    other_grads = swap_y(stored_grads)

    rows = nq // ny
    own = lax.optimization_barrier(lax.dynamic_slice_in_dim(queries, y * rows, rows, axis=0))
    step = functools.partial(fisher_step, inverse_fisher, column, own.shape[1])
    a0, a1, b0 = step(((0, 0), (0, 1), (1, 0)))
    piece = gather(own, (a0,))
    total, b1, c0 = step(((1, 1), (2, 0)), piece(0), (a0, a1))
    total, c1, d0 = step(((2, 1), (3, 0)), piece(1), (b0, b1), total)
    total, d1 = step(((3, 1),), piece(2, (total,)), (c0, c1), total)
    (total,) = step((), piece(3, (total,)), (d0, d1), total)
    panel = (total + to_owner(total)).astype(jnp.bfloat16)

    piece = gather(panel)
    pieces = [piece(k) for k in range(3)]
    other, mine = score_dot(pieces, ORDER[:3], column, (other_grads, stored_grads))
    pieces = [piece(3, (other,))]
    (other,) = score_dot(pieces, ORDER[3:], column, (other_grads,), (other,))
    (mine,) = score_dot(pieces, ORDER[3:], column, (stored_grads,), (mine,), (other,))

    other = swap_y(other)
    keep = jnp.where(d == y, mine, other)
    give = jnp.where(d == y, other, mine)
    return keep + move(give, lambda sy, sz, sx, sd: (sy, sz, sx, 1 - sd))


def solution(mesh):
    coords = [getattr(device, "coords", None) for device in mesh.devices.flat]
    nx = 2 if None in coords else len({c[0] for c in coords})
    nz = mesh.shape["ex"] // nx
    ny = mesh.shape["grp"]
    if (nz, nx, ny) == (4, 2, 2):
        body = functools.partial(per_device_quad, nz, nx, ny)
    else:
        body = per_device_any
    return jax.shard_map(
        body,
        mesh=mesh,
        in_specs=(P(None, "ex"), P("ex", "dim"), P(("grp", "ex"), "dim")),
        out_specs=P("dim", ("grp", "ex")),
        check_vma=False,
    )
```

time: 66.2 us -> 72 us (1.088); the launches traced: 66 us -> 70.8 us
  starting transfers between devices: 21 us -> 34.7 us
  waiting for transfers between devices: 20.6 us -> 13.6 us
  local copies, waits for them, and re-layouts: 3.19 us -> 1.62 us
    ppermute x12 -> x18, starting transfers between devices: 21 us -> 34.7 us  [move(): return lax.ppermute(value, AXES, pairs)]
    ppermute x12 -> x18, waiting for transfers between devices: 20.6 us -> 13.6 us  [move(): return lax.ppermute(value, AXES, pairs)]
    unnamed x6 -> x8, local copies, waits for them, and re-layouts: 3.18 us -> 1.61 us
    pallas_call x7 -> x8, Pallas kernels: 20.3 us -> 19.5 us  [the longest x5 17.8 us: fisher_step(): pl.pallas_call(functools.partial(fisher_kernel, len(ins), has_base, fetch...]
  transfers between devices with their start and end apart: 12 -> 18, of which waited for: 7 -> 6; matrix products, arithmetic and copies ran while one was open for 0% -> 0% of each run, Pallas kernels for 30% -> 28%
where the time goes in v9:
time: 72 us; the launch traced here: 70.8 us
  starting transfers between devices  34.7 us (48%)
  Pallas kernels  19.8 us (28%)
  waiting for transfers between devices  13.6 us (19%)
  local copies, waits for them, and re-layouts  1.62 us (2%)
    ppermute x18, starting transfers between devices, move(): return lax.ppermute(value, AXES, pairs)  34.7 us
    pallas_call x5, Pallas kernels, fisher_step(): pl.pallas_call(functools.partial(fisher_kernel, len(ins), has_base, fetch...  17.8 us
    ppermute x18, waiting for transfers between devices, move(): return lax.ppermute(value, AXES, pairs)  13.6 us
    pallas_call x3, Pallas kernels, score_dot(): pl.pallas_call(functools.partial(score_kernel, order, len(grads), len(bas...  1.75 us
    unnamed x8, local copies, waits for them, and re-layouts  1.61 us
  transfers between devices with their start and end apart: 18, of which 6 were waited for; matrix products, arithmetic and copies ran while one was open for 0% of the time, Pallas kernels for 28%

profile of v9, /device:TPU:0, one launch (start us, length us, event | category | flops | bytes accessed | tf_op | source)
XLA Modules:
  0.0 70.8 jit_solution(1828764097436255006)
XLA Ops:
  0.0 3.0 %collective-permute-start.15 = (bf16[128,8192]{1,0:T(8,128)(2,1)}, bf16[128,8192]{1,0:T(8,128)(2,1)S(1)}, u32[]{:S(2)}, u32[]{:S(2)}) collective-permute-start(bf16[128,8192]{1,0:T(8,128)(2,1)} %refs_1_.9), channel_id=1, source_target_pairs={{0,16},{1,17},{2,18},{3,19},{4,20},{5,21},{6,22},{7,23},{8,24},{9,... | collective-permute-start | bytes 6291464 | tf_op jit(solution)/shard_map/ppermute | solution.py:184
  3.0 4.5 %collective-permute-start.1 = (bf16[48,2048]{1,0:T(8,128)(2,1)S(1)}, bf16[48,2048]{1,0:T(8,128)(2,1)S(1)}, u32[]{:S(2)}, u32[]{:S(2)}) collective-permute-start(bf16[48,2048]{1,0:T(8,128)(2,1)S(1)} %constant_dynamic-slice_fusion.a_ref), channel_id=1, source_target_pairs={{0,8},{2,10},{4,12},{6,14},{9,1},{11,3},{13,5},{15,7},{16,24},{18,... | collective-permute-start | bytes 589832 | tf_op jit(solution)/shard_map/ppermute | solution.py:184
  7.5 4.4 %collective-permute-start = (bf16[48,2048]{1,0:T(8,128)(2,1)S(1)}, bf16[48,2048]{1,0:T(8,128)(2,1)S(1)}, u32[]{:S(2)}, u32[]{:S(2)}) collective-permute-start(bf16[48,2048]{1,0:T(8,128)(2,1)S(1)} %constant_dynamic-slice_fusion.a_ref), channel_id=1, source_target_pairs={{0,6},{2,4},{4,2},{6,0},{9,15},{11,13},{13,11},{15,9},{16,22},{18,... | collective-permute-start | bytes 589832 | tf_op jit(solution)/shard_map/ppermute | solution.py:184
  11.9 2.4 %collective-permute-start.2 = (bf16[48,2048]{1,0:T(8,128)(2,1)S(1)}, bf16[48,2048]{1,0:T(8,128)(2,1)S(1)}, u32[]{:S(2)}, u32[]{:S(2)}) collective-permute-start(bf16[48,2048]{1,0:T(8,128)(2,1)S(1)} %constant_dynamic-slice_fusion.a_ref), channel_id=1, source_target_pairs={{0,4},{2,6},{4,0},{6,2},{9,13},{11,15},{13,9},{15,11},{16,20},{18,... | collective-permute-start | bytes 589832 | tf_op jit(solution)/shard_map/ppermute | solution.py:184
  14.3 2.4 %collective-permute-start.3 = (bf16[48,2048]{1,0:T(8,128)(2,1)S(1)}, bf16[48,2048]{1,0:T(8,128)(2,1)S(1)}, u32[]{:S(2)}, u32[]{:S(2)}) collective-permute-start(bf16[48,2048]{1,0:T(8,128)(2,1)S(1)} %constant_dynamic-slice_fusion.a_ref), channel_id=1, source_target_pairs={{0,2},{2,0},{4,6},{6,4},{9,11},{11,9},{13,15},{15,13},{16,18},{18,... | collective-permute-start | bytes 589832 | tf_op jit(solution)/shard_map/ppermute | solution.py:184
  16.8 4.7 %shard_map.37 = (bf16[1024,2048]{1,0:T(8,128)(2,1)S(1)}, bf16[1024,2048]{1,0:T(8,128)(2,1)S(1)}, bf16[1024,2048]{1,0:T(8,128)(2,1)S(1)}) custom-call(s32[1]{0:T(128)} %bitcast.refs_0_.at_ref, bf16[2048,8192]{1,0:T(8,128)(2,1)} %refs_1_.8), custom_call_target="tpu_custom_call" | custom-call | bytes 12582912 | tf_op jit(solution)/shard_map/pallas_call | solution.py:95
  21.6 3.2 %collective-permute-done.3.refs_1_.a_ref = bf16[48,2048]{1,0:T(8,128)(2,1)S(1)} collective-permute-done((bf16[48,2048]{1,0:T(8,128)(2,1)S(1)}, bf16[48,2048]{1,0:T(8,128)(2,1)S(1)}, u32[]{:S(2)}, u32[]{:S(2)}) %collective-permute-start.3) | collective-permute-done | bytes 196640 | tf_op jit(solution)/shard_map/ppermute | solution.py:184
  24.8 0.7 collective-permute-start.6
  25.5 0.7 collective-permute-start.5
  26.2 0.7 collective-permute-start.4
  26.9 3.5 %shard_map.41 = (f32[48,2048]{1,0:T(8,128)S(1)}, bf16[1024,2048]{1,0:T(8,128)(2,1)S(1)}, bf16[1024,2048]{1,0:T(8,128)(2,1)S(1)}) custom-call(s32[1]{0:T(128)} %bitcast.refs_0_.at_ref, bf16[2048,8192]{1,0:T(8,128)(2,1)} %refs_1_.8, bf16[48,2048]{1,0:T(8,128)(2,1)S(1)} %shard_map.38.a_ref.b_ref.refs_2_, ...), custom_call_target="tpu_custom_call" | custom-call | flops 402653184 | bytes 8388608 | tf_op jit(solution)/shard_map/pallas_call | solution.py:95
  30.5 3.5 %shard_map.42 = (f32[48,2048]{1,0:T(8,128)S(1)}, bf16[1024,2048]{1,0:T(8,128)(2,1)S(1)}, bf16[1024,2048]{1,0:T(8,128)(2,1)S(1)}) custom-call(s32[1]{0:T(128)} %bitcast.refs_0_.at_ref, bf16[2048,8192]{1,0:T(8,128)(2,1)} %refs_1_.8, bf16[48,2048]{1,0:T(8,128)(2,1)S(1)} %shard_map.40.refs_2_, bf16[1024,2048]{1,0:T(8,128)(2,1)S(1)} %get-tuple-element.19.refs_3_, ...), custom_call_target="tpu_custom_call" | custom-call | flops 402653184 | bytes 8388608 | tf_op jit(solution)/shard_map/pallas_call | solution.py:95
  34.0 3.0 %shard_map.44 = (f32[48,2048]{1,0:T(8,128)S(1)}, bf16[1024,2048]{1,0:T(8,128)(2,1)S(1)}) custom-call(s32[1]{0:T(128)} %bitcast.refs_0_.at_ref, bf16[2048,8192]{1,0:T(8,128)(2,1)} %refs_1_.8, bf16[48,2048]{1,0:T(8,128)(2,1)S(1)} %shard_map.43.refs_2_, bf16[1024,2048]{1,0:T(8,128)(2,1)S(1)} %get-tuple-element.24.refs_3_, ...), custom_call_target="tpu_custom_call" | custom-call | flops 402653184 | bytes 4194304 | tf_op jit(solution)/shard_map/pallas_call | solution.py:95
  37.1 3.0 %shard_map.46 = f32[48,2048]{1,0:T(8,128)S(1)} custom-call(bf16[48,2048]{1,0:T(8,128)(2,1)S(1)} %shard_map.45.refs_0_, bf16[1024,2048]{1,0:T(8,128)(2,1)S(1)} %get-tuple-element.27.refs_1_, bf16[1024,2048]{1,0:T(8,128)(2,1)S(1)} %get-tuple-element.28.refs_2_, f32[48,2048]{1,0:T(8,128)S(1)} %get-tuple-element.26.refs_0_.refs_3_), custom_call_target="tpu_custom_call" | custom-call | flops 402653184 | tf_op jit(solution)/shard_map/pallas_call | solution.py:95
  40.1 1.4 %collective-permute-start.7 = (f32[48,2048]{1,0:T(8,128)S(1)}, f32[48,2048]{1,0:T(8,128)S(1)}, u32[]{:S(2)}, u32[]{:S(2)}) collective-permute-start(f32[48,2048]{1,0:T(8,128)S(1)} %shard_map.46), channel_id=1, source_target_pairs={{1,0},{3,2},{5,4},{7,6},{8,9},{10,11},{12,13},{14,15},{17,16},{19,... | collective-permute-start | bytes 1179656 | tf_op jit(solution)/shard_map/ppermute | solution.py:184
  41.5 2.3 %collective-permute-done.7 = f32[48,2048]{1,0:T(8,128)S(1)} collective-permute-done((f32[48,2048]{1,0:T(8,128)S(1)}, f32[48,2048]{1,0:T(8,128)S(1)}, u32[]{:S(2)}, u32[]{:S(2)}) %collective-permute-start.7) | collective-permute-done | bytes 393248 | tf_op jit(solution)/shard_map/ppermute | solution.py:184
  43.9 1.3 %collective-permute-start.9 = (bf16[48,2048]{1,0:T(8,128)(2,1)S(1)}, bf16[48,2048]{1,0:T(8,128)(2,1)S(1)}, u32[]{:S(2)}, u32[]{:S(2)}) collective-permute-start(bf16[48,2048]{1,0:T(8,128)(2,1)S(1)} %add_convert_fusion.a_ref), channel_id=1, source_target_pairs={{0,8},{2,10},{4,12},{6,14},{9,1},{11,3},{13,5},{15,7},{16,24},{18,... | collective-permute-start | bytes 589832 | tf_op jit(solution)/shard_map/ppermute | solution.py:184
  45.2 3.6 %collective-permute-start.10 = (bf16[48,2048]{1,0:T(8,128)(2,1)S(1)}, bf16[48,2048]{1,0:T(8,128)(2,1)S(1)}, u32[]{:S(2)}, u32[]{:S(2)}) collective-permute-start(bf16[48,2048]{1,0:T(8,128)(2,1)S(1)} %add_convert_fusion.a_ref), channel_id=1, source_target_pairs={{0,4},{2,6},{4,0},{6,2},{9,13},{11,15},{13,9},{15,11},{16,20},{18,... | collective-permute-start | bytes 589832 | tf_op jit(solution)/shard_map/ppermute | solution.py:184
  48.8 3.4 %collective-permute-start.11 = (bf16[48,2048]{1,0:T(8,128)(2,1)S(1)}, bf16[48,2048]{1,0:T(8,128)(2,1)S(1)}, u32[]{:S(2)}, u32[]{:S(2)}) collective-permute-start(bf16[48,2048]{1,0:T(8,128)(2,1)S(1)} %add_convert_fusion.a_ref), channel_id=1, source_target_pairs={{0,2},{2,0},{4,6},{6,4},{9,11},{11,9},{13,15},{15,13},{16,18},{18,... | collective-permute-start | bytes 589832 | tf_op jit(solution)/shard_map/ppermute | solution.py:184
  52.3 2.2 %collective-permute-start.8 = (bf16[48,2048]{1,0:T(8,128)(2,1)S(1)}, bf16[48,2048]{1,0:T(8,128)(2,1)S(1)}, u32[]{:S(2)}, u32[]{:S(2)}) collective-permute-start(bf16[48,2048]{1,0:T(8,128)(2,1)S(1)} %add_convert_fusion.a_ref), channel_id=1, source_target_pairs={{0,6},{2,4},{4,2},{6,0},{9,15},{11,13},{13,11},{15,9},{16,22},{18,... | collective-permute-start | bytes 589832 | tf_op jit(solution)/shard_map/ppermute | solution.py:184
  54.5 1.9 %collective-permute-done.11.refs_1_.a_ref = bf16[48,2048]{1,0:T(8,128)(2,1)S(1)} collective-permute-done((bf16[48,2048]{1,0:T(8,128)(2,1)S(1)}, bf16[48,2048]{1,0:T(8,128)(2,1)S(1)}, u32[]{:S(2)}, u32[]{:S(2)}) %collective-permute-start.11) | collective-permute-done | bytes 196640 | tf_op jit(solution)/shard_map/ppermute | solution.py:184
  56.4 4.4 %collective-permute-done.8.refs_2_.a_ref = bf16[48,2048]{1,0:T(8,128)(2,1)S(1)} collective-permute-done((bf16[48,2048]{1,0:T(8,128)(2,1)S(1)}, bf16[48,2048]{1,0:T(8,128)(2,1)S(1)}, u32[]{:S(2)}, u32[]{:S(2)}) %collective-permute-start.8) | collective-permute-done | bytes 196640 | tf_op jit(solution)/shard_map/ppermute | solution.py:184
  60.8 0.7 collective-permute-start.14
  61.5 0.7 collective-permute-start.13
  62.2 0.7 collective-permute-start.12
  63.0 1.2 %shard_map.51 = (f32[48,128]{1,0:T(8,128)S(1)}, f32[48,128]{1,0:T(8,128)S(1)}) custom-call(s32[1]{0:T(128)} %bitcast.refs_0_.at_ref, bf16[48,2048]{1,0:T(8,128)(2,1)S(1)} %shard_map.47.a_ref.b_ref.refs_0_, bf16[48,2048]{1,0:T(8,128)(2,1)S(1)} %shard_map.49.refs_1_, bf16[48,2048]{1,0:T(8,128)(2,1)S(1)} %shard_map.50.refs_2_, ...), custom_call_target="tpu_custom_call" | custom-call | flops 150994944 | bytes 3145728 | tf_op jit(solution)/shard_map/pallas_call | solution.py:127
  64.5 1.1 %collective-permute-start.16 = (f32[48,128]{1,0:T(8,128)S(1)}, f32[48,128]{1,0:T(8,128)S(1)}, u32[]{:S(2)}, u32[]{:S(2)}) collective-permute-start(f32[48,128]{1,0:T(8,128)S(1)} %shard_map.53.refs_3_), channel_id=1, source_target_pairs={{0,16},{1,17},{2,18},{3,19},{4,20},{5,21},{6,22},{7,23},{8,24},{9,... | collective-permute-start | bytes 73736 | tf_op jit(solution)/shard_map/ppermute | solution.py:184
  65.7 1.6 %copy-done.3 = bf16[128,8192]{1,0:T(8,128)(2,1)S(1)} copy-done((bf16[128,8192]{1,0:T(8,128)(2,1)S(1)}, bf16[128,8192]{1,0:T(8,128)(2,1)}, u32[]{:S(2)}) %copy-start.3) | copy-done | bytes 2097176
  67.5 0.9 %collective-permute-done.16 = f32[48,128]{1,0:T(8,128)S(1)} collective-permute-done((f32[48,128]{1,0:T(8,128)S(1)}, f32[48,128]{1,0:T(8,128)S(1)}, u32[]{:S(2)}, u32[]{:S(2)}) %collective-permute-start.16) | collective-permute-done | bytes 24608 | tf_op jit(solution)/shard_map/ppermute | solution.py:184
  68.4 0.9 %collective-permute-start.17 = (f32[48,128]{1,0:T(8,128)S(1)}, f32[48,128]{1,0:T(8,128)S(1)}, u32[]{:S(2)}, u32[]{:S(2)}) collective-permute-start(f32[48,128]{1,0:T(8,128)S(1)} %broadcast_select_fusion), channel_id=1, source_target_pairs={{0,1},{1,0},{2,3},{3,2},{4,5},{5,4},{6,7},{7,6},{8,9},{9,8},{10,11... | collective-permute-start | bytes 73736 | tf_op jit(solution)/shard_map/ppermute | solution.py:184
  69.4 0.8 %collective-permute-done.17 = f32[48,128]{1,0:T(8,128)S(1)} collective-permute-done((f32[48,128]{1,0:T(8,128)S(1)}, f32[48,128]{1,0:T(8,128)S(1)}, u32[]{:S(2)}, u32[]{:S(2)}) %collective-permute-start.17) | collective-permute-done | bytes 24608 | tf_op jit(solution)/shard_map/ppermute | solution.py:184
  70.2 0.6 select_add_fusion
  (34 shorter events, 0.9 us)
Async XLA Ops:
  0.0 3.0 %copy-start = (bf16[96,2048]{1,0:T(8,128)(2,1)S(1)}, bf16[96,2048]{1,0:T(8,128)(2,1)}, u32[]{:S(2)}) copy-start(bf16[96,2048]{1,0:T(8,128)(2,1)} %param.3) | copy-start | bytes 1179652
  0.0 63.0 %collective-permute-start.15 = (bf16[128,8192]{1,0:T(8,128)(2,1)}, bf16[128,8192]{1,0:T(8,128)(2,1)S(1)}, u32[]{:S(2)}, u32[]{:S(2)}) collective-permute-start(bf16[128,8192]{1,0:T(8,128)(2,1)} %refs_1_.9), channel_id=1, source_target_pairs={{0,16},{1,17},{2,18},{3,19},{4,20},{5,21},{6,22},{7,23},{8,24},{9,... | collective-permute-start | bytes 6291464 | tf_op jit(solution)/shard_map/ppermute | solution.py:184
  3.0 18.5 %collective-permute-start.1 = (bf16[48,2048]{1,0:T(8,128)(2,1)S(1)}, bf16[48,2048]{1,0:T(8,128)(2,1)S(1)}, u32[]{:S(2)}, u32[]{:S(2)}) collective-permute-start(bf16[48,2048]{1,0:T(8,128)(2,1)S(1)} %constant_dynamic-slice_fusion.a_ref), channel_id=1, source_target_pairs={{0,8},{2,10},{4,12},{6,14},{9,1},{11,3},{13,5},{15,7},{16,24},{18,... | collective-permute-start | bytes 589832 | tf_op jit(solution)/shard_map/ppermute | solution.py:184
  7.5 14.1 %collective-permute-start = (bf16[48,2048]{1,0:T(8,128)(2,1)S(1)}, bf16[48,2048]{1,0:T(8,128)(2,1)S(1)}, u32[]{:S(2)}, u32[]{:S(2)}) collective-permute-start(bf16[48,2048]{1,0:T(8,128)(2,1)S(1)} %constant_dynamic-slice_fusion.a_ref), channel_id=1, source_target_pairs={{0,6},{2,4},{4,2},{6,0},{9,15},{11,13},{13,11},{15,9},{16,22},{18,... | collective-permute-start | bytes 589832 | tf_op jit(solution)/shard_map/ppermute | solution.py:184
  11.9 9.7 %collective-permute-start.2 = (bf16[48,2048]{1,0:T(8,128)(2,1)S(1)}, bf16[48,2048]{1,0:T(8,128)(2,1)S(1)}, u32[]{:S(2)}, u32[]{:S(2)}) collective-permute-start(bf16[48,2048]{1,0:T(8,128)(2,1)S(1)} %constant_dynamic-slice_fusion.a_ref), channel_id=1, source_target_pairs={{0,4},{2,6},{4,0},{6,2},{9,13},{11,15},{13,9},{15,11},{16,20},{18,... | collective-permute-start | bytes 589832 | tf_op jit(solution)/shard_map/ppermute | solution.py:184
  14.3 10.5 %collective-permute-start.3 = (bf16[48,2048]{1,0:T(8,128)(2,1)S(1)}, bf16[48,2048]{1,0:T(8,128)(2,1)S(1)}, u32[]{:S(2)}, u32[]{:S(2)}) collective-permute-start(bf16[48,2048]{1,0:T(8,128)(2,1)S(1)} %constant_dynamic-slice_fusion.a_ref), channel_id=1, source_target_pairs={{0,2},{2,0},{4,6},{6,4},{9,11},{11,9},{13,15},{15,13},{16,18},{18,... | collective-permute-start | bytes 589832 | tf_op jit(solution)/shard_map/ppermute | solution.py:184
  24.8 5.6 %collective-permute-start.6 = (bf16[48,2048]{1,0:T(8,128)(2,1)S(1)}, bf16[48,2048]{1,0:T(8,128)(2,1)S(1)}, u32[]{:S(2)}, u32[]{:S(2)}) collective-permute-start(bf16[48,2048]{1,0:T(8,128)(2,1)S(1)} %shard_map.39), channel_id=1, source_target_pairs={{1,5},{3,7},{5,1},{7,3},{8,12},{10,14},{12,8},{14,10},{17,21},{19,... | collective-permute-start | bytes 589832 | tf_op jit(solution)/shard_map/ppermute | solution.py:184
  25.5 8.5 %collective-permute-start.5 = (bf16[48,2048]{1,0:T(8,128)(2,1)S(1)}, bf16[48,2048]{1,0:T(8,128)(2,1)S(1)}, u32[]{:S(2)}, u32[]{:S(2)}) collective-permute-start(bf16[48,2048]{1,0:T(8,128)(2,1)S(1)} %shard_map.39), channel_id=1, source_target_pairs={{1,3},{3,1},{5,7},{7,5},{8,10},{10,8},{12,14},{14,12},{17,19},{19,... | collective-permute-start | bytes 589832 | tf_op jit(solution)/shard_map/ppermute | solution.py:184
  26.2 10.8 %collective-permute-start.4 = (bf16[48,2048]{1,0:T(8,128)(2,1)S(1)}, bf16[48,2048]{1,0:T(8,128)(2,1)S(1)}, u32[]{:S(2)}, u32[]{:S(2)}) collective-permute-start(bf16[48,2048]{1,0:T(8,128)(2,1)S(1)} %shard_map.39), channel_id=1, source_target_pairs={{1,7},{3,5},{5,3},{7,1},{8,14},{10,12},{12,10},{14,8},{17,23},{19,... | collective-permute-start | bytes 589832 | tf_op jit(solution)/shard_map/ppermute | solution.py:184
  40.1 22.9 %copy-start.2 = (bf16[128,8192]{1,0:T(8,128)(2,1)S(1)}, bf16[128,8192]{1,0:T(8,128)(2,1)}, u32[]{:S(2)}) copy-start(bf16[128,8192]{1,0:T(8,128)(2,1)} %refs_1_.9) | copy-start | bytes 6291460
  40.1 3.7 %collective-permute-start.7 = (f32[48,2048]{1,0:T(8,128)S(1)}, f32[48,2048]{1,0:T(8,128)S(1)}, u32[]{:S(2)}, u32[]{:S(2)}) collective-permute-start(f32[48,2048]{1,0:T(8,128)S(1)} %shard_map.46), channel_id=1, source_target_pairs={{1,0},{3,2},{5,4},{7,6},{8,9},{10,11},{12,13},{14,15},{17,16},{19,... | collective-permute-start | bytes 1179656 | tf_op jit(solution)/shard_map/ppermute | solution.py:184
  43.9 10.5 %collective-permute-start.9 = (bf16[48,2048]{1,0:T(8,128)(2,1)S(1)}, bf16[48,2048]{1,0:T(8,128)(2,1)S(1)}, u32[]{:S(2)}, u32[]{:S(2)}) collective-permute-start(bf16[48,2048]{1,0:T(8,128)(2,1)S(1)} %add_convert_fusion.a_ref), channel_id=1, source_target_pairs={{0,8},{2,10},{4,12},{6,14},{9,1},{11,3},{13,5},{15,7},{16,24},{18,... | collective-permute-start | bytes 589832 | tf_op jit(solution)/shard_map/ppermute | solution.py:184
  45.2 9.3 %collective-permute-start.10 = (bf16[48,2048]{1,0:T(8,128)(2,1)S(1)}, bf16[48,2048]{1,0:T(8,128)(2,1)S(1)}, u32[]{:S(2)}, u32[]{:S(2)}) collective-permute-start(bf16[48,2048]{1,0:T(8,128)(2,1)S(1)} %add_convert_fusion.a_ref), channel_id=1, source_target_pairs={{0,4},{2,6},{4,0},{6,2},{9,13},{11,15},{13,9},{15,11},{16,20},{18,... | collective-permute-start | bytes 589832 | tf_op jit(solution)/shard_map/ppermute | solution.py:184
  48.8 7.6 %collective-permute-start.11 = (bf16[48,2048]{1,0:T(8,128)(2,1)S(1)}, bf16[48,2048]{1,0:T(8,128)(2,1)S(1)}, u32[]{:S(2)}, u32[]{:S(2)}) collective-permute-start(bf16[48,2048]{1,0:T(8,128)(2,1)S(1)} %add_convert_fusion.a_ref), channel_id=1, source_target_pairs={{0,2},{2,0},{4,6},{6,4},{9,11},{11,9},{13,15},{15,13},{16,18},{18,... | collective-permute-start | bytes 589832 | tf_op jit(solution)/shard_map/ppermute | solution.py:184
  52.3 8.6 %collective-permute-start.8 = (bf16[48,2048]{1,0:T(8,128)(2,1)S(1)}, bf16[48,2048]{1,0:T(8,128)(2,1)S(1)}, u32[]{:S(2)}, u32[]{:S(2)}) collective-permute-start(bf16[48,2048]{1,0:T(8,128)(2,1)S(1)} %add_convert_fusion.a_ref), channel_id=1, source_target_pairs={{0,6},{2,4},{4,2},{6,0},{9,15},{11,13},{13,11},{15,9},{16,22},{18,... | collective-permute-start | bytes 589832 | tf_op jit(solution)/shard_map/ppermute | solution.py:184
  60.8 2.0 %collective-permute-start.14 = (bf16[48,2048]{1,0:T(8,128)(2,1)S(1)}, bf16[48,2048]{1,0:T(8,128)(2,1)S(1)}, u32[]{:S(2)}, u32[]{:S(2)}) collective-permute-start(bf16[48,2048]{1,0:T(8,128)(2,1)S(1)} %shard_map.48), channel_id=1, source_target_pairs={{1,3},{3,1},{5,7},{7,5},{8,10},{10,8},{12,14},{14,12},{17,19},{19,... | collective-permute-start | bytes 589832 | tf_op jit(solution)/shard_map/ppermute | solution.py:184
  61.5 1.4 %collective-permute-start.13 = (bf16[48,2048]{1,0:T(8,128)(2,1)S(1)}, bf16[48,2048]{1,0:T(8,128)(2,1)S(1)}, u32[]{:S(2)}, u32[]{:S(2)}) collective-permute-start(bf16[48,2048]{1,0:T(8,128)(2,1)S(1)} %shard_map.48), channel_id=1, source_target_pairs={{1,5},{3,7},{5,1},{7,3},{8,12},{10,14},{12,8},{14,10},{17,21},{19,... | collective-permute-start | bytes 589832 | tf_op jit(solution)/shard_map/ppermute | solution.py:184
  62.2 2.0 %collective-permute-start.12 = (bf16[48,2048]{1,0:T(8,128)(2,1)S(1)}, bf16[48,2048]{1,0:T(8,128)(2,1)S(1)}, u32[]{:S(2)}, u32[]{:S(2)}) collective-permute-start(bf16[48,2048]{1,0:T(8,128)(2,1)S(1)} %shard_map.48), channel_id=1, source_target_pairs={{1,7},{3,5},{5,3},{7,1},{8,14},{10,12},{12,10},{14,8},{17,23},{19,... | collective-permute-start | bytes 589832 | tf_op jit(solution)/shard_map/ppermute | solution.py:184
  62.9 7.9 %copy-start.1 = (bf16[96,2048]{1,0:T(8,128)(2,1)S(1)}, bf16[96,2048]{1,0:T(8,128)(2,1)}, u32[]{:S(2)}) copy-start(bf16[96,2048]{1,0:T(8,128)(2,1)} %param.3) | copy-start | bytes 1179652
  64.5 3.9 %collective-permute-start.16 = (f32[48,128]{1,0:T(8,128)S(1)}, f32[48,128]{1,0:T(8,128)S(1)}, u32[]{:S(2)}, u32[]{:S(2)}) collective-permute-start(f32[48,128]{1,0:T(8,128)S(1)} %shard_map.53.refs_3_), channel_id=1, source_target_pairs={{0,16},{1,17},{2,18},{3,19},{4,20},{5,21},{6,22},{7,23},{8,24},{9,... | collective-permute-start | bytes 73736 | tf_op jit(solution)/shard_map/ppermute | solution.py:184
  65.7 1.6 %copy-start.3 = (bf16[128,8192]{1,0:T(8,128)(2,1)S(1)}, bf16[128,8192]{1,0:T(8,128)(2,1)}, u32[]{:S(2)}) copy-start(bf16[128,8192]{1,0:T(8,128)(2,1)} %refs_1_.9) | copy-start | bytes 6291460
  68.4 1.8 %collective-permute-start.17 = (f32[48,128]{1,0:T(8,128)S(1)}, f32[48,128]{1,0:T(8,128)S(1)}, u32[]{:S(2)}, u32[]{:S(2)}) collective-permute-start(f32[48,128]{1,0:T(8,128)S(1)} %broadcast_select_fusion), channel_id=1, source_target_pairs={{0,1},{1,0},{2,3},{3,2},{4,5},{5,4},{6,7},{7,6},{8,9},{9,8},{10,11... | collective-permute-start | bytes 73736 | tf_op jit(solution)/shard_map/ppermute | solution.py:184

commit v10 on v9

--- a/solution.py
+++ b/solution.py
@@ -101,7 +101,7 @@
         compiler_params=limit(34 if chunk is None else 20),
         cost_estimate=pl.CostEstimate(
             flops=0 if chunk is None else 2 * chunk.shape[0] * width * rows,
-            bytes_accessed=width * rows * len(fetch),
+            bytes_accessed=width * rows * (len(fetch) + 2 * bool(ins)),
             transcendentals=0,
         ),
     )(*((scalar(first), fisher) if fetch else ()), *ins, *([base] if has_base else []))
@@ -196,28 +196,23 @@
     def swap_y(value):
         return move(value, lambda sy, sz, sx, sd: (1 - sy, sz, sx, sd))
 
-    def to_owner(value):
-        def target(sy, sz, sx, sd):
+    def swap_core(value):
+        return move(value, lambda sy, sz, sx, sd: (sy, sz, sx, 1 - sd))
+
+    def gather(own, after=()):
+        def start(sy, sz, sx, sd):
             su = sz if sd == 0 else nz - 1 - sz
-            return None if su < near else (sy, sz, sx, 1 - sd)
-
-        return move(value, target)
-
-    def gather(own, after=()):
-        far = along_z(own, {0: 2, 1: 3})
-        steps = (((0, 1), (1, 0)), False), (((0, 0), (1, 1)), True), (((0, 1), (1, 0)), True)
-        near = [along_z(own, dict(hops), flip) for hops, flip in steps]
-        first = pick(owner, own, far, after)
-        gate = pick(owner, first, first, near)
-
-        def piece(k, after=()):
-            if k == 0:
-                return first
-            hops, flip = steps[k - 1]
-            hops = {2 + s: 2 + t for s, t in hops}
-            return pick(owner, near[k - 1], along_z(gate, hops, flip), after)
-
-        return piece
+            if su < near:
+                return sy, sz + 2 if sd == 0 else sz - 2, sx, sd
+            return sy, sz ^ 1, 1 - sx, 1 - sd
+
+        came = move(own, start)
+        first = pick(owner, own, came, after)
+        pairs = {0: 1, 1: 0, 2: 3, 3: 2}
+        beside = along_z(first, pairs)
+        across = along_z(first, {0: 0, 1: 1, 2: 2, 3: 3}, True)
+        diagonal = along_z(first, {2: 3, 3: 2}, True)
+        return lambda *after: [first, beside, across, pick(owner, came, diagonal, after)]
 
     plane = jnp.where(d == 0, u % 2, nz - 1 - u % 2)
     column = plane * nx + x - d * (nex // 2)
@@ -227,25 +222,24 @@
     rows = nq // ny
     own = lax.optimization_barrier(lax.dynamic_slice_in_dim(queries, y * rows, rows, axis=0))
     step = functools.partial(fisher_step, inverse_fisher, column, own.shape[1])
-    a0, a1, b0 = step(((0, 0), (0, 1), (1, 0)))
-    piece = gather(own, (a0,))
-    total, b1, c0 = step(((1, 1), (2, 0)), piece(0), (a0, a1))
-    total, c1, d0 = step(((2, 1), (3, 0)), piece(1), (b0, b1), total)
-    total, d1 = step(((3, 1),), piece(2, (total,)), (c0, c1), total)
-    (total,) = step((), piece(3, (total,)), (d0, d1), total)
-    panel = (total + to_owner(total)).astype(jnp.bfloat16)
-
-    piece = gather(panel)
-    pieces = [piece(k) for k in range(3)]
-    other, mine = score_dot(pieces, ORDER[:3], column, (other_grads, stored_grads))
-    pieces = [piece(3, (other,))]
-    (other,) = score_dot(pieces, ORDER[3:], column, (other_grads,), (other,))
-    (mine,) = score_dot(pieces, ORDER[3:], column, (stored_grads,), (mine,), (other,))
+    a0, a1, b0, b1 = step(((0, 0), (0, 1), (1, 0), (1, 1)))
+    gathered = gather(own, (a0,))
+    q0, q1, q2, _ = gathered()
+    total, c0, c1 = step(((2, 0), (2, 1)), q0, (a0, a1))
+    total, d0 = step(((3, 0),), q1, (b0, b1), total)
+    total, d1 = step(((3, 1),), q2, (c0, c1), total)
+    (total,) = step((), gathered(total)[3], (d0, d1), total)
+    panel = (total + swap_core(total)).astype(jnp.bfloat16)
+
+    grads = (other_grads, stored_grads)
+    gathered = gather(panel)
+    base = score_dot(gathered()[:3], ORDER[:3], column, grads)
+    other, mine = score_dot(gathered(base[0])[3:], ORDER[3:], column, grads, base)
 
     other = swap_y(other)
     keep = jnp.where(d == y, mine, other)
     give = jnp.where(d == y, other, mine)
-    return keep + move(give, lambda sy, sz, sx, sd: (sy, sz, sx, 1 - sd))
+    return keep + swap_core(give)
 
 
 def solution(mesh):

time: 72 us -> 56.8 us (0.79)
  starting transfers between devices: 34.7 us -> 20.2 us
  local copies, waits for them, and re-layouts: 1.62 us -> 0.03 us
  waiting for transfers between devices: 13.6 us -> 15 us
    ppermute x18 -> x12, starting transfers between devices: 34.7 us -> 20.2 us  [move(): return lax.ppermute(value, AXES, pairs)]
    unnamed x8 -> x6, local copies, waits for them, and re-layouts: 1.61 us -> 0.01 us
    ppermute x18 -> x12, waiting for transfers between devices: 13.6 us -> 15 us  [move(): return lax.ppermute(value, AXES, pairs)]
    pallas_call x3 -> x2, Pallas kernels: 1.75 us -> 1.64 us  [score_dot(): pl.pallas_call(functools.partial(score_kernel, order, len(grads), len(bas...]
  transfers between devices with their start and end apart: 18 -> 12, of which waited for: 6 -> 8; matrix products, arithmetic and copies ran while one was open for 0% -> 0% of each run, Pallas kernels for 28% -> 35%
where the time goes in v10:
time: 56.8 us; the launch traced here: 56.2 us
  starting transfers between devices  20.2 us (36%)
  Pallas kernels  20.2 us (36%)
  waiting for transfers between devices  15 us (26%)
  other arithmetic  0.67 us (1%)
    ppermute x12, starting transfers between devices, move(): return lax.ppermute(value, AXES, pairs)  20.2 us
    pallas_call x5, Pallas kernels, fisher_step(): pl.pallas_call(functools.partial(fisher_kernel, len(ins), has_base, fetch...  18.5 us
    ppermute x12, waiting for transfers between devices, move(): return lax.ppermute(value, AXES, pairs)  15 us
    pallas_call x2, Pallas kernels, score_dot(): pl.pallas_call(functools.partial(score_kernel, order, len(grads), len(bas...  1.64 us
  transfers between devices with their start and end apart: 12, of which 8 were waited for; matrix products, arithmetic and copies ran while one was open for 0% of the time, Pallas kernels for 35%

profile of v10, /device:TPU:0, one launch (start us, length us, event | category | flops | bytes accessed | tf_op | source)
XLA Modules:
  0.0 56.2 jit_solution(546779149785918254)
XLA Ops:
  0.0 3.0 %collective-permute-start.9 = (bf16[128,8192]{1,0:T(8,128)(2,1)}, bf16[128,8192]{1,0:T(8,128)(2,1)S(1)}, u32[]{:S(2)}, u32[]{:S(2)}) collective-permute-start(bf16[128,8192]{1,0:T(8,128)(2,1)} %refs_2_.1), channel_id=1, source_target_pairs={{0,16},{1,17},{2,18},{3,19},{4,20},{5,21},{6,22},{7,23},{8,24},{9,... | collective-permute-start | bytes 6291464 | tf_op jit(solution)/shard_map/ppermute | solution.py:184
  3.0 2.7 %collective-permute-start = (bf16[48,2048]{1,0:T(8,128)(2,1)S(1)}, bf16[48,2048]{1,0:T(8,128)(2,1)S(1)}, u32[]{:S(2)}, u32[]{:S(2)}) collective-permute-start(bf16[48,2048]{1,0:T(8,128)(2,1)S(1)} %constant_dynamic-slice_fusion.a_ref), channel_id=1, source_target_pairs={{0,8},{1,6},{2,10},{3,4},{4,12},{5,2},{6,14},{7,0},{8,15},{9,1},{1... | collective-permute-start | bytes 589832 | tf_op jit(solution)/shard_map/ppermute | solution.py:184
  5.6 6.0 %shard_map.37 = (bf16[1024,2048]{1,0:T(8,128)(2,1)S(1)}, bf16[1024,2048]{1,0:T(8,128)(2,1)S(1)}, bf16[1024,2048]{1,0:T(8,128)(2,1)S(1)}, bf16[1024,2048]{1,0:T(8,128)(2,1)S(1)}) custom-call(s32[1]{0:T(128)} %bitcast.refs_0_.at_ref, bf16[2048,8192]{1,0:T(8,128)(2,1)} %refs_1_.7), custom_call_target="tpu_custom_call" | custom-call | bytes 16777216 | tf_op jit(solution)/shard_map/pallas_call | solution.py:95
  11.6 0.0 collective-permute-done.b_ref.a_ref
  11.6 1.6 %collective-permute-start.3 = (bf16[48,2048]{1,0:T(8,128)(2,1)S(1)}, bf16[48,2048]{1,0:T(8,128)(2,1)S(1)}, u32[]{:S(2)}, u32[]{:S(2)}) collective-permute-start(bf16[48,2048]{1,0:T(8,128)(2,1)S(1)} %shard_map.38.refs_2_), channel_id=1, source_target_pairs={{0,4},{1,5},{2,6},{3,7},{4,0},{5,1},{6,2},{7,3},{8,12},{9,13},{10,... | collective-permute-start | bytes 589832 | tf_op jit(solution)/shard_map/ppermute | solution.py:184
  13.3 1.5 %collective-permute-start.2 = (bf16[48,2048]{1,0:T(8,128)(2,1)S(1)}, bf16[48,2048]{1,0:T(8,128)(2,1)S(1)}, u32[]{:S(2)}, u32[]{:S(2)}) collective-permute-start(bf16[48,2048]{1,0:T(8,128)(2,1)S(1)} %shard_map.38.refs_2_), channel_id=1, source_target_pairs={{0,2},{1,3},{2,0},{3,1},{4,6},{5,7},{6,4},{7,5},{8,10},{9,11},{10,... | collective-permute-start | bytes 589832 | tf_op jit(solution)/shard_map/ppermute | solution.py:184
  14.8 0.7 %collective-permute-start.1 = (bf16[48,2048]{1,0:T(8,128)(2,1)S(1)}, bf16[48,2048]{1,0:T(8,128)(2,1)S(1)}, u32[]{:S(2)}, u32[]{:S(2)}) collective-permute-start(bf16[48,2048]{1,0:T(8,128)(2,1)S(1)} %shard_map.38.refs_2_), channel_id=1, source_target_pairs={{1,7},{3,5},{5,3},{7,1},{8,14},{10,12},{12,10},{14,8},{17,23},{19,... | collective-permute-start | bytes 589832 | tf_op jit(solution)/shard_map/ppermute | solution.py:184
  15.4 3.5 %shard_map.39 = (f32[48,2048]{1,0:T(8,128)S(1)}, bf16[1024,2048]{1,0:T(8,128)(2,1)S(1)}, bf16[1024,2048]{1,0:T(8,128)(2,1)S(1)}) custom-call(s32[1]{0:T(128)} %bitcast.refs_0_.at_ref, bf16[2048,8192]{1,0:T(8,128)(2,1)} %refs_1_.7, bf16[48,2048]{1,0:T(8,128)(2,1)S(1)} %shard_map.38.refs_2_, bf16[1024,2048]{1,0:T(8,128)(2,1)S(1)} %get-tuple-element.20.refs_0_.refs_3_, ...), custom_call_target="tpu_custom_call" | custom-call | flops 402653184 | bytes 16777216 | tf_op jit(solution)/shard_map/pallas_call | solution.py:95
  19.0 0.5 collective-permute-done.3.refs_2_
  19.5 3.0 %shard_map.40 = (f32[48,2048]{1,0:T(8,128)S(1)}, bf16[1024,2048]{1,0:T(8,128)(2,1)S(1)}) custom-call(s32[1]{0:T(128)} %bitcast.refs_0_.at_ref, bf16[2048,8192]{1,0:T(8,128)(2,1)} %refs_1_.7, bf16[48,2048]{1,0:T(8,128)(2,1)S(1)} %collective-permute-done.3.refs_2_, bf16[1024,2048]{1,0:T(8,128)(2,1)S(1)} %get-tuple-element.24.refs_3_, ...), custom_call_target="tpu_custom_call" | custom-call | flops 402653184 | bytes 12582912 | tf_op jit(solution)/shard_map/pallas_call | solution.py:95
  22.5 0.0 collective-permute-done.2.refs_2_
  22.5 3.0 %shard_map.41 = (f32[48,2048]{1,0:T(8,128)S(1)}, bf16[1024,2048]{1,0:T(8,128)(2,1)S(1)}) custom-call(s32[1]{0:T(128)} %bitcast.refs_0_.at_ref, bf16[2048,8192]{1,0:T(8,128)(2,1)} %refs_1_.7, bf16[48,2048]{1,0:T(8,128)(2,1)S(1)} %collective-permute-done.2.refs_2_, bf16[1024,2048]{1,0:T(8,128)(2,1)S(1)} %get-tuple-element.22.refs_3_, ...), custom_call_target="tpu_custom_call" | custom-call | flops 402653184 | bytes 12582912 | tf_op jit(solution)/shard_map/pallas_call | solution.py:95
  25.6 0.0 copy-start.2
  25.6 3.0 %shard_map.43 = f32[48,2048]{1,0:T(8,128)S(1)} custom-call(bf16[48,2048]{1,0:T(8,128)(2,1)S(1)} %shard_map.42.refs_0_, bf16[1024,2048]{1,0:T(8,128)(2,1)S(1)} %get-tuple-element.29.refs_1_, bf16[1024,2048]{1,0:T(8,128)(2,1)S(1)} %get-tuple-element.30.refs_2_, f32[48,2048]{1,0:T(8,128)S(1)} %get-tuple-element.28.refs_0_.refs_3_), custom_call_target="tpu_custom_call" | custom-call | flops 402653184 | bytes 8388608 | tf_op jit(solution)/shard_map/pallas_call | solution.py:95
  28.6 0.4 collective-permute-start.4
  29.0 1.4 %collective-permute-done.4 = f32[48,2048]{1,0:T(8,128)S(1)} collective-permute-done((f32[48,2048]{1,0:T(8,128)S(1)}, f32[48,2048]{1,0:T(8,128)S(1)}, u32[]{:S(2)}, u32[]{:S(2)}) %collective-permute-start.4) | collective-permute-done | bytes 393248 | tf_op jit(solution)/shard_map/ppermute | solution.py:184
  30.4 3.5 %collective-permute-start.5 = (bf16[48,2048]{1,0:T(8,128)(2,1)S(1)}, bf16[48,2048]{1,0:T(8,128)(2,1)S(1)}, u32[]{:S(2)}, u32[]{:S(2)}) collective-permute-start(bf16[48,2048]{1,0:T(8,128)(2,1)S(1)} %add_convert_fusion.a_ref), channel_id=1, source_target_pairs={{0,8},{1,6},{2,10},{3,4},{4,12},{5,2},{6,14},{7,0},{8,15},{9,1},{1... | collective-permute-start | bytes 589832 | tf_op jit(solution)/shard_map/ppermute | solution.py:184
  33.9 4.0 %collective-permute-done.5.b_ref.a_ref = bf16[48,2048]{1,0:T(8,128)(2,1)S(1)} collective-permute-done((bf16[48,2048]{1,0:T(8,128)(2,1)S(1)}, bf16[48,2048]{1,0:T(8,128)(2,1)S(1)}, u32[]{:S(2)}, u32[]{:S(2)}) %collective-permute-start.5) | collective-permute-done | bytes 196640 | tf_op jit(solution)/shard_map/ppermute | solution.py:184
  37.9 2.9 %collective-permute-start.7 = (bf16[48,2048]{1,0:T(8,128)(2,1)S(1)}, bf16[48,2048]{1,0:T(8,128)(2,1)S(1)}, u32[]{:S(2)}, u32[]{:S(2)}) collective-permute-start(bf16[48,2048]{1,0:T(8,128)(2,1)S(1)} %shard_map.44.refs_0_), channel_id=1, source_target_pairs={{0,4},{1,5},{2,6},{3,7},{4,0},{5,1},{6,2},{7,3},{8,12},{9,13},{10,... | collective-permute-start | bytes 589832 | tf_op jit(solution)/shard_map/ppermute | solution.py:184
  40.8 1.5 %collective-permute-start.8 = (bf16[48,2048]{1,0:T(8,128)(2,1)S(1)}, bf16[48,2048]{1,0:T(8,128)(2,1)S(1)}, u32[]{:S(2)}, u32[]{:S(2)}) collective-permute-start(bf16[48,2048]{1,0:T(8,128)(2,1)S(1)} %shard_map.44.refs_0_), channel_id=1, source_target_pairs={{0,2},{1,3},{2,0},{3,1},{4,6},{5,7},{6,4},{7,5},{8,10},{9,11},{10,... | collective-permute-start | bytes 589832 | tf_op jit(solution)/shard_map/ppermute | solution.py:184
  42.3 0.7 %collective-permute-start.6 = (bf16[48,2048]{1,0:T(8,128)(2,1)S(1)}, bf16[48,2048]{1,0:T(8,128)(2,1)S(1)}, u32[]{:S(2)}, u32[]{:S(2)}) collective-permute-start(bf16[48,2048]{1,0:T(8,128)(2,1)S(1)} %shard_map.44.refs_0_), channel_id=1, source_target_pairs={{1,7},{3,5},{5,3},{7,1},{8,14},{10,12},{12,10},{14,8},{17,23},{19,... | collective-permute-start | bytes 589832 | tf_op jit(solution)/shard_map/ppermute | solution.py:184
  43.0 3.0 %collective-permute-done.7.refs_1_ = bf16[48,2048]{1,0:T(8,128)(2,1)S(1)} collective-permute-done((bf16[48,2048]{1,0:T(8,128)(2,1)S(1)}, bf16[48,2048]{1,0:T(8,128)(2,1)S(1)}, u32[]{:S(2)}, u32[]{:S(2)}) %collective-permute-start.7) | collective-permute-done | bytes 196640 | tf_op jit(solution)/shard_map/ppermute | solution.py:184
  46.0 2.2 %collective-permute-done.8.refs_2_ = bf16[48,2048]{1,0:T(8,128)(2,1)S(1)} collective-permute-done((bf16[48,2048]{1,0:T(8,128)(2,1)S(1)}, bf16[48,2048]{1,0:T(8,128)(2,1)S(1)}, u32[]{:S(2)}, u32[]{:S(2)}) %collective-permute-start.8) | collective-permute-done | bytes 196640 | tf_op jit(solution)/shard_map/ppermute | solution.py:184
  48.2 0.6 %collective-permute-done.9.refs_3_.refs_1_ = bf16[128,8192]{1,0:T(8,128)(2,1)S(1)} collective-permute-done((bf16[128,8192]{1,0:T(8,128)(2,1)}, bf16[128,8192]{1,0:T(8,128)(2,1)S(1)}, u32[]{:S(2)}, u32[]{:S(2)}) %collective-permute-start.9) | collective-permute-done | bytes 2097184 | tf_op jit(solution)/shard_map/ppermute | solution.py:184
  48.8 1.2 %shard_map.45 = (f32[48,128]{1,0:T(8,128)S(1)}, f32[48,128]{1,0:T(8,128)S(1)}) custom-call(s32[1]{0:T(128)} %bitcast.refs_0_.at_ref, bf16[48,2048]{1,0:T(8,128)(2,1)S(1)} %shard_map.44.refs_0_, bf16[48,2048]{1,0:T(8,128)(2,1)S(1)} %collective-permute-done.7.refs_1_, bf16[48,2048]{1,0:T(8,128)(2,1)S(1)} %collective-permute-done.8.refs_2_, ...), custom_call_target="tpu_custom_call" | custom-call | flops 150994944 | bytes 3145728 | tf_op jit(solution)/shard_map/pallas_call | solution.py:127
  50.0 0.0 collective-permute-done.6.b_ref
  50.0 0.5 shard_map.47
  50.5 1.8 %collective-permute-start.10 = (f32[48,128]{1,0:T(8,128)S(1)}, f32[48,128]{1,0:T(8,128)S(1)}, u32[]{:S(2)}, u32[]{:S(2)}) collective-permute-start(f32[48,128]{1,0:T(8,128)S(1)} %get-tuple-element.34), channel_id=1, source_target_pairs={{0,16},{1,17},{2,18},{3,19},{4,20},{5,21},{6,22},{7,23},{8,24},{9,... | collective-permute-start | bytes 73736 | tf_op jit(solution)/shard_map/ppermute | solution.py:184
  52.3 2.1 %collective-permute-done.10 = f32[48,128]{1,0:T(8,128)S(1)} collective-permute-done((f32[48,128]{1,0:T(8,128)S(1)}, f32[48,128]{1,0:T(8,128)S(1)}, u32[]{:S(2)}, u32[]{:S(2)}) %collective-permute-start.10) | collective-permute-done | bytes 24608 | tf_op jit(solution)/shard_map/ppermute | solution.py:184
  54.4 0.0 collective-permute-start.11
  54.4 1.2 %collective-permute-done.11 = f32[48,128]{1,0:T(8,128)S(1)} collective-permute-done((f32[48,128]{1,0:T(8,128)S(1)}, f32[48,128]{1,0:T(8,128)S(1)}, u32[]{:S(2)}, u32[]{:S(2)}) %collective-permute-start.11) | collective-permute-done | bytes 24608 | tf_op jit(solution)/shard_map/ppermute | solution.py:184
  55.6 0.6 %select_add_fusion = f32[48,128]{1,0:T(8,128)} fusion(f32[48,128]{1,0:T(8,128)S(1)} %collective-permute-done.11, f32[48,128]{1,0:T(8,128)S(1)} %get-tuple-element.33, f32[48,128]{1,0:T(8,128)S(1)} %collective-permute-done.10, pred[]{:T(512)S(6)} %eq.12), kind=kLoop, calls=%fused_computation.1 | loop fusion | flops 12288 | bytes 98305 | tf_op jit(solution)/shard_map/add | solution.py:242
  (13 shorter events, 0.2 us)
Async XLA Ops:
  0.0 3.0 %copy-start = (bf16[96,2048]{1,0:T(8,128)(2,1)S(1)}, bf16[96,2048]{1,0:T(8,128)(2,1)}, u32[]{:S(2)}) copy-start(bf16[96,2048]{1,0:T(8,128)(2,1)} %param.3) | copy-start | bytes 1179652
  0.0 48.8 %collective-permute-start.9 = (bf16[128,8192]{1,0:T(8,128)(2,1)}, bf16[128,8192]{1,0:T(8,128)(2,1)S(1)}, u32[]{:S(2)}, u32[]{:S(2)}) collective-permute-start(bf16[128,8192]{1,0:T(8,128)(2,1)} %refs_2_.1), channel_id=1, source_target_pairs={{0,16},{1,17},{2,18},{3,19},{4,20},{5,21},{6,22},{7,23},{8,24},{9,... | collective-permute-start | bytes 6291464 | tf_op jit(solution)/shard_map/ppermute | solution.py:184
  3.0 8.6 %collective-permute-start = (bf16[48,2048]{1,0:T(8,128)(2,1)S(1)}, bf16[48,2048]{1,0:T(8,128)(2,1)S(1)}, u32[]{:S(2)}, u32[]{:S(2)}) collective-permute-start(bf16[48,2048]{1,0:T(8,128)(2,1)S(1)} %constant_dynamic-slice_fusion.a_ref), channel_id=1, source_target_pairs={{0,8},{1,6},{2,10},{3,4},{4,12},{5,2},{6,14},{7,0},{8,15},{9,1},{1... | collective-permute-start | bytes 589832 | tf_op jit(solution)/shard_map/ppermute | solution.py:184
  11.6 7.8 %collective-permute-start.3 = (bf16[48,2048]{1,0:T(8,128)(2,1)S(1)}, bf16[48,2048]{1,0:T(8,128)(2,1)S(1)}, u32[]{:S(2)}, u32[]{:S(2)}) collective-permute-start(bf16[48,2048]{1,0:T(8,128)(2,1)S(1)} %shard_map.38.refs_2_), channel_id=1, source_target_pairs={{0,4},{1,5},{2,6},{3,7},{4,0},{5,1},{6,2},{7,3},{8,12},{9,13},{10,... | collective-permute-start | bytes 589832 | tf_op jit(solution)/shard_map/ppermute | solution.py:184
  13.3 9.2 %collective-permute-start.2 = (bf16[48,2048]{1,0:T(8,128)(2,1)S(1)}, bf16[48,2048]{1,0:T(8,128)(2,1)S(1)}, u32[]{:S(2)}, u32[]{:S(2)}) collective-permute-start(bf16[48,2048]{1,0:T(8,128)(2,1)S(1)} %shard_map.38.refs_2_), channel_id=1, source_target_pairs={{0,2},{1,3},{2,0},{3,1},{4,6},{5,7},{6,4},{7,5},{8,10},{9,11},{10,... | collective-permute-start | bytes 589832 | tf_op jit(solution)/shard_map/ppermute | solution.py:184
  14.8 10.7 %collective-permute-start.1 = (bf16[48,2048]{1,0:T(8,128)(2,1)S(1)}, bf16[48,2048]{1,0:T(8,128)(2,1)S(1)}, u32[]{:S(2)}, u32[]{:S(2)}) collective-permute-start(bf16[48,2048]{1,0:T(8,128)(2,1)S(1)} %shard_map.38.refs_2_), channel_id=1, source_target_pairs={{1,7},{3,5},{5,3},{7,1},{8,14},{10,12},{12,10},{14,8},{17,23},{19,... | collective-permute-start | bytes 589832 | tf_op jit(solution)/shard_map/ppermute | solution.py:184
  25.6 23.2 %copy-start.2 = (bf16[128,8192]{1,0:T(8,128)(2,1)S(1)}, bf16[128,8192]{1,0:T(8,128)(2,1)}, u32[]{:S(2)}) copy-start(bf16[128,8192]{1,0:T(8,128)(2,1)} %refs_2_.1) | copy-start | bytes 6291460
  28.6 1.8 %collective-permute-start.4 = (f32[48,2048]{1,0:T(8,128)S(1)}, f32[48,2048]{1,0:T(8,128)S(1)}, u32[]{:S(2)}, u32[]{:S(2)}) collective-permute-start(f32[48,2048]{1,0:T(8,128)S(1)} %shard_map.43), channel_id=1, source_target_pairs={{0,1},{1,0},{2,3},{3,2},{4,5},{5,4},{6,7},{7,6},{8,9},{9,8},{10,11... | collective-permute-start | bytes 1179656 | tf_op jit(solution)/shard_map/ppermute | solution.py:184
  30.4 7.5 %collective-permute-start.5 = (bf16[48,2048]{1,0:T(8,128)(2,1)S(1)}, bf16[48,2048]{1,0:T(8,128)(2,1)S(1)}, u32[]{:S(2)}, u32[]{:S(2)}) collective-permute-start(bf16[48,2048]{1,0:T(8,128)(2,1)S(1)} %add_convert_fusion.a_ref), channel_id=1, source_target_pairs={{0,8},{1,6},{2,10},{3,4},{4,12},{5,2},{6,14},{7,0},{8,15},{9,1},{1... | collective-permute-start | bytes 589832 | tf_op jit(solution)/shard_map/ppermute | solution.py:184
  37.9 18.3 %copy-start.1 = (bf16[96,2048]{1,0:T(8,128)(2,1)S(1)}, bf16[96,2048]{1,0:T(8,128)(2,1)}, u32[]{:S(2)}) copy-start(bf16[96,2048]{1,0:T(8,128)(2,1)} %param.3) | copy-start | bytes 1179652
  37.9 8.1 %collective-permute-start.7 = (bf16[48,2048]{1,0:T(8,128)(2,1)S(1)}, bf16[48,2048]{1,0:T(8,128)(2,1)S(1)}, u32[]{:S(2)}, u32[]{:S(2)}) collective-permute-start(bf16[48,2048]{1,0:T(8,128)(2,1)S(1)} %shard_map.44.refs_0_), channel_id=1, source_target_pairs={{0,4},{1,5},{2,6},{3,7},{4,0},{5,1},{6,2},{7,3},{8,12},{9,13},{10,... | collective-permute-start | bytes 589832 | tf_op jit(solution)/shard_map/ppermute | solution.py:184
  40.8 7.4 %collective-permute-start.8 = (bf16[48,2048]{1,0:T(8,128)(2,1)S(1)}, bf16[48,2048]{1,0:T(8,128)(2,1)S(1)}, u32[]{:S(2)}, u32[]{:S(2)}) collective-permute-start(bf16[48,2048]{1,0:T(8,128)(2,1)S(1)} %shard_map.44.refs_0_), channel_id=1, source_target_pairs={{0,2},{1,3},{2,0},{3,1},{4,6},{5,7},{6,4},{7,5},{8,10},{9,11},{10,... | collective-permute-start | bytes 589832 | tf_op jit(solution)/shard_map/ppermute | solution.py:184
  42.3 7.7 %collective-permute-start.6 = (bf16[48,2048]{1,0:T(8,128)(2,1)S(1)}, bf16[48,2048]{1,0:T(8,128)(2,1)S(1)}, u32[]{:S(2)}, u32[]{:S(2)}) collective-permute-start(bf16[48,2048]{1,0:T(8,128)(2,1)S(1)} %shard_map.44.refs_0_), channel_id=1, source_target_pairs={{1,7},{3,5},{5,3},{7,1},{8,14},{10,12},{12,10},{14,8},{17,23},{19,... | collective-permute-start | bytes 589832 | tf_op jit(solution)/shard_map/ppermute | solution.py:184
  50.5 3.9 %collective-permute-start.10 = (f32[48,128]{1,0:T(8,128)S(1)}, f32[48,128]{1,0:T(8,128)S(1)}, u32[]{:S(2)}, u32[]{:S(2)}) collective-permute-start(f32[48,128]{1,0:T(8,128)S(1)} %get-tuple-element.34), channel_id=1, source_target_pairs={{0,16},{1,17},{2,18},{3,19},{4,20},{5,21},{6,22},{7,23},{8,24},{9,... | collective-permute-start | bytes 73736 | tf_op jit(solution)/shard_map/ppermute | solution.py:184
  54.4 1.2 %collective-permute-start.11 = (f32[48,128]{1,0:T(8,128)S(1)}, f32[48,128]{1,0:T(8,128)S(1)}, u32[]{:S(2)}, u32[]{:S(2)}) collective-permute-start(f32[48,128]{1,0:T(8,128)S(1)} %broadcast_select_fusion), channel_id=1, source_target_pairs={{0,1},{1,0},{2,3},{3,2},{4,5},{5,4},{6,7},{7,6},{8,9},{9,8},{10,11... | collective-permute-start | bytes 73736 | tf_op jit(solution)/shard_map/ppermute | solution.py:184

commit v11 on v10

--- a/solution.py
+++ b/solution.py
@@ -85,7 +85,7 @@
         copy.wait()
 
 
-def fisher_step(fisher, first, width, fetch, chunk=None, halves=(), base=None, step=512):
+def fisher_step(fisher, first, width, fetch, chunk=None, halves=(), base=None, step=1024):
     rows = fisher.shape[0]
     ins = [] if chunk is None else [chunk, *halves]
     has_base = base is not None
@@ -107,35 +107,69 @@
     )(*((scalar(first), fisher) if fetch else ()), *ins, *([base] if has_base else []))
 
 
-def score_kernel(order, n_grads, has_base, at_ref, *refs):
-    n = len(order)
-    width = refs[0].shape[1]
-    for g in range(n_grads):
-        grads_ref, out_ref = refs[n + g], refs[-n_grads + g]
-        total = refs[n + n_grads + g][...] if has_base else None
-        for k in range(n):
-            start = pl.multiple_of((at_ref[0] ^ order[k]) * width, width)
-            term = times(refs[k], grads_ref[:, pl.ds(start, width)])
-            total = term if total is None else total + term
-        out_ref[...] = total
-
-
-def score_dot(pieces, order, first, grads, base=(), after=()):
-    n = len(pieces)
-    rows, width = pieces[0].shape
-    operands = [*pieces, *grads, *base]
+def base_kernel(at_ref, piece0, piece1, piece2, swapped, mine_grads, other_grads, mine, other, theirs):
+    width = piece0.shape[1]
+    starts = [pl.multiple_of((at_ref[0] ^ mask) * width, width) for mask in ORDER[:3]]
+    total = None
+    for piece, start in zip((piece0, piece1, piece2), starts):
+        term = times(piece, mine_grads[:, pl.ds(start, width)])
+        total = term if total is None else total + term
+    mine[...] = total
+    theirs[...] = times(swapped, mine_grads[:, pl.ds(starts[0], width)])
+    other[...] = times(piece1, other_grads[:, :width]) + times(piece2, other_grads[:, width : 2 * width])
+
+
+def last_kernel(at_ref, piece3, mine_grads, other_grads, mine_base, other_base, mine, other):
+    width = piece3.shape[1]
+    start = pl.multiple_of((at_ref[0] ^ ORDER[3]) * width, width)
+    other[...] = other_base[...] + times(piece3, other_grads[:, 2 * width :])
+    mine[...] = mine_base[...] + times(piece3, mine_grads[:, pl.ds(start, width)])
+
+
+def score_call(kernel, n_out, examples, first, *operands):
+    rows, width = operands[0].shape
     return pl.pallas_call(
-        functools.partial(score_kernel, order, len(grads), len(base) > 0),
-        out_shape=[jax.ShapeDtypeStruct((rows, g.shape[0]), jnp.float32) for g in grads],
-        in_specs=[SMEM] + [VMEM] * len(operands) + [ANY] * len(after),
-        out_specs=[VMEM] * len(grads),
+        kernel,
+        out_shape=[jax.ShapeDtypeStruct((rows, examples), jnp.float32)] * n_out,
+        in_specs=[SMEM] + [VMEM] * len(operands),
+        out_specs=[VMEM] * n_out,
         compiler_params=limit(8),
         cost_estimate=pl.CostEstimate(
-            flops=2 * n * rows * width * grads[0].shape[0] * len(grads),
-            bytes_accessed=2 * n * width * grads[0].shape[0] * len(grads),
+            flops=2 * rows * width * examples * 2 * n_out,
+            bytes_accessed=2 * width * examples * 2 * n_out,
             transcendentals=0,
         ),
-    )(scalar(first), *operands, *after)
+    )(scalar(first), *operands)
+
+
+def cut_kernel(order, at_ref, src_ref, out_ref, sem):
+    width = out_ref.shape[1] // len(order)
+    copies = []
+    for k, mask in enumerate(order):
+        start = pl.multiple_of((at_ref[0] ^ mask) * width, width)
+        copies.append(
+            pltpu.make_async_copy(
+                src_ref.at[:, pl.ds(start, width)], out_ref.at[:, k * width : (k + 1) * width], sem.at[k]
+            )
+        )
+        copies[-1].start()
+    for copy in copies:
+        copy.wait()
+
+
+def cut(src, order, first, width):
+    n = len(order)
+    return pl.pallas_call(
+        functools.partial(cut_kernel, order),
+        out_shape=jax.ShapeDtypeStruct((src.shape[0], n * width), src.dtype),
+        in_specs=[SMEM, HBM],
+        out_specs=VMEM,
+        scratch_shapes=[pltpu.SemaphoreType.DMA((n,))],
+        compiler_params=limit(57),
+        cost_estimate=pl.CostEstimate(
+            flops=0, bytes_accessed=2 * n * width * src.shape[0], transcendentals=0
+        ),
+    )(scalar(first), src)
 
 
 def pick_kernel(at_ref, a_ref, b_ref, *refs):
@@ -208,35 +242,45 @@
 
         came = move(own, start)
         first = pick(owner, own, came, after)
-        pairs = {0: 1, 1: 0, 2: 3, 3: 2}
-        beside = along_z(first, pairs)
+        beside = along_z(first, {0: 1, 1: 0, 2: 3, 3: 2})
         across = along_z(first, {0: 0, 1: 1, 2: 2, 3: 3}, True)
-        diagonal = along_z(first, {2: 3, 3: 2}, True)
-        return lambda *after: [first, beside, across, pick(owner, came, diagonal, after)]
+
+        def corner(after):
+            ready, _ = lax.optimization_barrier((beside, after))
+            return pick(owner, came, along_z(ready, {2: 2, 3: 3}, True))
+
+        return first, beside, across, corner
 
     plane = jnp.where(d == 0, u % 2, nz - 1 - u % 2)
     column = plane * nx + x - d * (nex // 2)
 
-    other_grads = swap_y(stored_grads)
-
-    rows = nq // ny
+    rows, width = nq // ny, queries.shape[1]
     own = lax.optimization_barrier(lax.dynamic_slice_in_dim(queries, y * rows, rows, axis=0))
-    step = functools.partial(fisher_step, inverse_fisher, column, own.shape[1])
-    a0, a1, b0, b1 = step(((0, 0), (0, 1), (1, 0), (1, 1)))
-    gathered = gather(own, (a0,))
-    q0, q1, q2, _ = gathered()
-    total, c0, c1 = step(((2, 0), (2, 1)), q0, (a0, a1))
-    total, d0 = step(((3, 0),), q1, (b0, b1), total)
+    to_y = cut(stored_grads, ORDER[1:], column, width)
+    other_grads = swap_y(to_y)
+    at, _ = lax.optimization_barrier((column, to_y))
+    step = functools.partial(fisher_step, inverse_fisher, at, width)
+    a0, a1, b0 = step(((0, 0), (0, 1), (1, 0)))
+    q0, q1, q2, corner = gather(own, (a0,))
+    total, b1, c0 = step(((1, 1), (2, 0)), q0, (a0, a1))
+    q3 = corner(total)
+    total, c1, d0 = step(((2, 1), (3, 0)), q1, (b0, b1), total)
     total, d1 = step(((3, 1),), q2, (c0, c1), total)
-    (total,) = step((), gathered(total)[3], (d0, d1), total)
+    (total,) = step((), q3, (d0, d1), total)
     panel = (total + swap_core(total)).astype(jnp.bfloat16)
 
-    grads = (other_grads, stored_grads)
-    gathered = gather(panel)
-    base = score_dot(gathered()[:3], ORDER[:3], column, grads)
-    other, mine = score_dot(gathered(base[0])[3:], ORDER[3:], column, grads, base)
-
-    other = swap_y(other)
+    p0, p1, p2, corner = gather(panel, (other_grads,))
+    p3 = corner(p1)
+    examples = stored_grads.shape[0]
+    mine, other, theirs = score_call(
+        base_kernel, 3, examples, column, p0, p1, p2, swap_y(p0), stored_grads, other_grads
+    )
+    p3, _ = lax.optimization_barrier((p3, mine))
+    mine, other = score_call(
+        last_kernel, 2, examples, column, p3, stored_grads, other_grads, mine, other
+    )
+
+    other = swap_y(other) + theirs
     keep = jnp.where(d == y, mine, other)
     give = jnp.where(d == y, other, mine)
     return keep + swap_core(give)

time: 56.8 us -> 63.4 us (1.12)
  the two profiles are of different devices: /device:TPU:0 before, /device:TPU:25 now
where the time goes in v11:
time: 63.4 us; the launch traced here: 63.2 us
  Pallas kernels  25.4 us (40%)
  starting transfers between devices  21.6 us (34%)
  waiting for transfers between devices  14.3 us (23%)
  local copies, waits for them, and re-layouts  1.02 us (2%)
  other arithmetic  0.66 us (1%)
    ppermute x13, starting transfers between devices, move(): return lax.ppermute(value, AXES, pairs)  21.6 us
    pallas_call x5, Pallas kernels, fisher_step(): pl.pallas_call(functools.partial(fisher_kernel, len(ins), has_base, fetch...  21.1 us
    ppermute x13, waiting for transfers between devices, move(): return lax.ppermute(value, AXES, pairs)  14.3 us
    pallas_call x1, Pallas kernels, cut(): pl.pallas_call(functools.partial(cut_kernel, order), out_shape=jax.ShapeD...  2.56 us
    pallas_call x2, Pallas kernels, score_call(): pl.pallas_call(kernel, out_shape=[jax.ShapeDtypeStruct((rows, examples),...  1.65 us
  transfers between devices with their start and end apart: 13, of which 6 were waited for; matrix products, arithmetic and copies ran while one was open for 0% of the time, Pallas kernels for 39%

profile of v11, /device:TPU:25, one launch (start us, length us, event | category | flops | bytes accessed | tf_op | source)
XLA Modules:
  0.0 63.2 jit_solution(8348394264018272251)
XLA Ops:
  0.0 1.0 %copy-done = bf16[96,2048]{1,0:T(8,128)(2,1)S(1)} copy-done((bf16[96,2048]{1,0:T(8,128)(2,1)S(1)}, bf16[96,2048]{1,0:T(8,128)(2,1)}, u32[]{:S(2)}) %copy-start) | copy-done | bytes 393240
  1.0 0.1 collective-permute-start
  1.1 2.6 %shard_map.37 = bf16[128,6144]{1,0:T(8,128)(2,1)} custom-call(s32[1]{0:T(128)} %bitcast.at_ref, bf16[128,8192]{1,0:T(8,128)(2,1)} %mine_grads.3), custom_call_target="tpu_custom_call" | custom-call | bytes 1572864 | tf_op jit(solution)/shard_map/pallas_call | solution.py:162
  3.7 1.3 %collective-permute-start.6 = (bf16[128,6144]{1,0:T(8,128)(2,1)}, bf16[128,6144]{1,0:T(8,128)(2,1)S(1)}, u32[]{:S(2)}, u32[]{:S(2)}) collective-permute-start(bf16[128,6144]{1,0:T(8,128)(2,1)} %shard_map.37), channel_id=1, source_target_pairs={{0,16},{1,17},{2,18},{3,19},{4,20},{5,21},{6,22},{7,23},{8,24},{9,... | collective-permute-start | bytes 4718600 | tf_op jit(solution)/shard_map/ppermute | solution.py:218
  5.0 4.7 %shard_map.38 = (bf16[1024,2048]{1,0:T(8,128)(2,1)S(1)}, bf16[1024,2048]{1,0:T(8,128)(2,1)S(1)}, bf16[1024,2048]{1,0:T(8,128)(2,1)S(1)}) custom-call(s32[1]{0:T(128)} %bitcast.2.refs_0_, bf16[2048,8192]{1,0:T(8,128)(2,1)} %refs_1_.7), custom_call_target="tpu_custom_call" | custom-call | bytes 12582912 | tf_op jit(solution)/shard_map/pallas_call | solution.py:95
  9.7 0.0 collective-permute-done.b_ref.a_ref
  9.8 0.2 collective-permute-start.1
  10.0 1.2 %collective-permute-start.3 = (bf16[48,2048]{1,0:T(8,128)(2,1)S(1)}, bf16[48,2048]{1,0:T(8,128)(2,1)S(1)}, u32[]{:S(2)}, u32[]{:S(2)}) collective-permute-start(bf16[48,2048]{1,0:T(8,128)(2,1)S(1)} %shard_map.39.refs_2_), channel_id=1, source_target_pairs={{0,2},{1,3},{2,0},{3,1},{4,6},{5,7},{6,4},{7,5},{8,10},{9,11},{10,... | collective-permute-start | bytes 589832 | tf_op jit(solution)/shard_map/ppermute | solution.py:218
  11.2 5.4 %shard_map.40 = (f32[48,2048]{1,0:T(8,128)S(1)}, bf16[1024,2048]{1,0:T(8,128)(2,1)S(1)}, bf16[1024,2048]{1,0:T(8,128)(2,1)S(1)}) custom-call(s32[1]{0:T(128)} %bitcast.2.refs_0_, bf16[2048,8192]{1,0:T(8,128)(2,1)} %refs_1_.7, bf16[48,2048]{1,0:T(8,128)(2,1)S(1)} %shard_map.39.refs_2_, bf16[1024,2048]{1,0:T(8,128)(2,1)S(1)} %get-tuple-element.26.refs_0_.refs_3_, ...), custom_call_target="tpu_custom_call" | custom-call | flops 402653184 | bytes 16777216 | tf_op jit(solution)/shard_map/pallas_call | solution.py:95
  16.6 0.0 collective-permute-done.1.refs_2_
  16.6 0.7 %collective-permute-start.2 = (bf16[48,2048]{1,0:T(8,128)(2,1)S(1)}, bf16[48,2048]{1,0:T(8,128)(2,1)S(1)}, u32[]{:S(2)}, u32[]{:S(2)}) collective-permute-start(bf16[48,2048]{1,0:T(8,128)(2,1)S(1)} %collective-permute-done.1.refs_2_), channel_id=1, source_target_pairs={{1,3},{3,1},{5,7},{7,5},{8,10},{10,8},{12,14},{14,12},{17,19},{19,... | collective-permute-start | bytes 589832 | tf_op jit(solution)/shard_map/ppermute | solution.py:218
  17.3 4.2 %shard_map.42 = (f32[48,2048]{1,0:T(8,128)S(1)}, bf16[1024,2048]{1,0:T(8,128)(2,1)S(1)}, bf16[1024,2048]{1,0:T(8,128)(2,1)S(1)}) custom-call(s32[1]{0:T(128)} %bitcast.2.refs_0_, bf16[2048,8192]{1,0:T(8,128)(2,1)} %refs_1_.7, bf16[48,2048]{1,0:T(8,128)(2,1)S(1)} %collective-permute-done.1.refs_2_, bf16[1024,2048]{1,0:T(8,128)(2,1)S(1)} %get-tuple-element.30.refs_3_, ...), custom_call_target="tpu_custom_call" | custom-call | flops 402653184 | bytes 16777216 | tf_op jit(solution)/shard_map/pallas_call | solution.py:95
  21.6 4.1 %shard_map.43 = (f32[48,2048]{1,0:T(8,128)S(1)}, bf16[1024,2048]{1,0:T(8,128)(2,1)S(1)}) custom-call(s32[1]{0:T(128)} %bitcast.2.refs_0_, bf16[2048,8192]{1,0:T(8,128)(2,1)} %refs_1_.7, bf16[48,2048]{1,0:T(8,128)(2,1)S(1)} %collective-permute-done.3.refs_2_, bf16[1024,2048]{1,0:T(8,128)(2,1)S(1)} %get-tuple-element.33.refs_3_, ...), custom_call_target="tpu_custom_call" | custom-call | flops 402653184 | bytes 12582912 | tf_op jit(solution)/shard_map/pallas_call | solution.py:95
  25.7 0.0 copy-start.2
  25.7 2.6 %shard_map.44 = f32[48,2048]{1,0:T(8,128)S(1)} custom-call(bf16[48,2048]{1,0:T(8,128)(2,1)S(1)} %shard_map.41.refs_0_, bf16[1024,2048]{1,0:T(8,128)(2,1)S(1)} %get-tuple-element.32.refs_1_, bf16[1024,2048]{1,0:T(8,128)(2,1)S(1)} %get-tuple-element.36.refs_2_, f32[48,2048]{1,0:T(8,128)S(1)} %get-tuple-element.37.refs_3_), custom_call_target="tpu_custom_call" | custom-call | flops 402653184 | bytes 8388608 | tf_op jit(solution)/shard_map/pallas_call | solution.py:95
  28.4 5.2 %collective-permute-start.4 = (f32[48,2048]{1,0:T(8,128)S(1)}, f32[48,2048]{1,0:T(8,128)S(1)}, u32[]{:S(2)}, u32[]{:S(2)}) collective-permute-start(f32[48,2048]{1,0:T(8,128)S(1)} %shard_map.44), channel_id=1, source_target_pairs={{0,1},{1,0},{2,3},{3,2},{4,5},{5,4},{6,7},{7,6},{8,9},{9,8},{10,11... | collective-permute-start | bytes 1179656 | tf_op jit(solution)/shard_map/ppermute | solution.py:218
  33.6 1.3 %collective-permute-done.4 = f32[48,2048]{1,0:T(8,128)S(1)} collective-permute-done((f32[48,2048]{1,0:T(8,128)S(1)}, f32[48,2048]{1,0:T(8,128)S(1)}, u32[]{:S(2)}, u32[]{:S(2)}) %collective-permute-start.4) | collective-permute-done | bytes 393248 | tf_op jit(solution)/shard_map/ppermute | solution.py:218
  35.0 0.1 collective-permute-start.5
  35.1 6.9 %collective-permute-done.5.b_ref.a_ref = bf16[48,2048]{1,0:T(8,128)(2,1)S(1)} collective-permute-done((bf16[48,2048]{1,0:T(8,128)(2,1)S(1)}, bf16[48,2048]{1,0:T(8,128)(2,1)S(1)}, u32[]{:S(2)}, u32[]{:S(2)}) %collective-permute-start.5) | collective-permute-done | bytes 196640 | tf_op jit(solution)/shard_map/ppermute | solution.py:218
  42.0 0.1 collective-permute-start.7
  42.1 0.6 collective-permute-start.10
  42.7 0.7 %collective-permute-start.9 = (bf16[48,2048]{1,0:T(8,128)(2,1)S(1)}, bf16[48,2048]{1,0:T(8,128)(2,1)S(1)}, u32[]{:S(2)}, u32[]{:S(2)}) collective-permute-start(bf16[48,2048]{1,0:T(8,128)(2,1)S(1)} %shard_map.45.piece0), channel_id=1, source_target_pairs={{0,2},{1,3},{2,0},{3,1},{4,6},{5,7},{6,4},{7,5},{8,10},{9,11},{10,... | collective-permute-start | bytes 589832 | tf_op jit(solution)/shard_map/ppermute | solution.py:218
  43.3 3.3 %collective-permute-done.7.piece1 = bf16[48,2048]{1,0:T(8,128)(2,1)S(1)} collective-permute-done((bf16[48,2048]{1,0:T(8,128)(2,1)S(1)}, bf16[48,2048]{1,0:T(8,128)(2,1)S(1)}, u32[]{:S(2)}, u32[]{:S(2)}) %collective-permute-start.7) | collective-permute-done | bytes 196640 | tf_op jit(solution)/shard_map/ppermute | solution.py:218
  46.6 0.7 %collective-permute-start.8 = (bf16[48,2048]{1,0:T(8,128)(2,1)S(1)}, bf16[48,2048]{1,0:T(8,128)(2,1)S(1)}, u32[]{:S(2)}, u32[]{:S(2)}) collective-permute-start(bf16[48,2048]{1,0:T(8,128)(2,1)S(1)} %collective-permute-done.7.piece1), channel_id=1, source_target_pairs={{1,3},{3,1},{5,7},{7,5},{8,10},{10,8},{12,14},{14,12},{17,19},{19,... | collective-permute-start | bytes 589832 | tf_op jit(solution)/shard_map/ppermute | solution.py:218
  47.3 0.2 collective-permute-done.9.piece2
  47.5 1.2 %shard_map.47 = (f32[48,128]{1,0:T(8,128)S(1)}, f32[48,128]{1,0:T(8,128)S(1)}, f32[48,128]{1,0:T(8,128)S(1)}) custom-call(s32[1]{0:T(128)} %bitcast.at_ref, bf16[48,2048]{1,0:T(8,128)(2,1)S(1)} %shard_map.45.piece0, bf16[48,2048]{1,0:T(8,128)(2,1)S(1)} %collective-permute-done.7.piece1, bf16[48,2048]{1,0:T(8,128)(2,1)S(1)} %collective-permute-done.9.piece2, ...), custom_call_target="tpu_custom_call" | custom-call | flops 150994944 | bytes 3145728 | tf_op jit(solution)/shard_map/pallas_call | solution.py:131
  48.7 0.5 shard_map.48
  49.2 1.0 %collective-permute-start.11 = (f32[48,128]{1,0:T(8,128)S(1)}, f32[48,128]{1,0:T(8,128)S(1)}, u32[]{:S(2)}, u32[]{:S(2)}) collective-permute-start(f32[48,128]{1,0:T(8,128)S(1)} %get-tuple-element.43), channel_id=1, source_target_pairs={{0,16},{1,17},{2,18},{3,19},{4,20},{5,21},{6,22},{7,23},{8,24},{9,... | collective-permute-start | bytes 73736 | tf_op jit(solution)/shard_map/ppermute | solution.py:218
  50.2 1.7 %collective-permute-done.11 = f32[48,128]{1,0:T(8,128)S(1)} collective-permute-done((f32[48,128]{1,0:T(8,128)S(1)}, f32[48,128]{1,0:T(8,128)S(1)}, u32[]{:S(2)}, u32[]{:S(2)}) %collective-permute-start.11) | collective-permute-done | bytes 24608 | tf_op jit(solution)/shard_map/ppermute | solution.py:218
  51.9 9.8 %collective-permute-start.12 = (f32[48,128]{1,0:T(8,128)S(1)}, f32[48,128]{1,0:T(8,128)S(1)}, u32[]{:S(2)}, u32[]{:S(2)}) collective-permute-start(f32[48,128]{1,0:T(8,128)S(1)} %broadcast_select_fusion), channel_id=1, source_target_pairs={{0,1},{1,0},{2,3},{3,2},{4,5},{5,4},{6,7},{7,6},{8,9},{9,8},{10,11... | collective-permute-start | bytes 73736 | tf_op jit(solution)/shard_map/ppermute | solution.py:218
  61.7 0.8 %collective-permute-done.12 = f32[48,128]{1,0:T(8,128)S(1)} collective-permute-done((f32[48,128]{1,0:T(8,128)S(1)}, f32[48,128]{1,0:T(8,128)S(1)}, u32[]{:S(2)}, u32[]{:S(2)}) %collective-permute-start.12) | collective-permute-done | bytes 24608 | tf_op jit(solution)/shard_map/ppermute | solution.py:218
  62.6 0.6 select_add_fusion
  (16 shorter events, 0.2 us)
Async XLA Ops:
  0.0 1.0 %copy-start = (bf16[96,2048]{1,0:T(8,128)(2,1)S(1)}, bf16[96,2048]{1,0:T(8,128)(2,1)}, u32[]{:S(2)}) copy-start(bf16[96,2048]{1,0:T(8,128)(2,1)} %param.3) | copy-start | bytes 1179652
  1.0 8.7 %collective-permute-start = (bf16[48,2048]{1,0:T(8,128)(2,1)S(1)}, bf16[48,2048]{1,0:T(8,128)(2,1)S(1)}, u32[]{:S(2)}, u32[]{:S(2)}) collective-permute-start(bf16[48,2048]{1,0:T(8,128)(2,1)S(1)} %constant_dynamic-slice_fusion.a_ref), channel_id=1, source_target_pairs={{0,8},{1,6},{2,10},{3,4},{4,12},{5,2},{6,14},{7,0},{8,15},{9,1},{1... | collective-permute-start | bytes 589832 | tf_op jit(solution)/shard_map/ppermute | solution.py:218
  3.7 38.3 %collective-permute-start.6 = (bf16[128,6144]{1,0:T(8,128)(2,1)}, bf16[128,6144]{1,0:T(8,128)(2,1)S(1)}, u32[]{:S(2)}, u32[]{:S(2)}) collective-permute-start(bf16[128,6144]{1,0:T(8,128)(2,1)} %shard_map.37), channel_id=1, source_target_pairs={{0,16},{1,17},{2,18},{3,19},{4,20},{5,21},{6,22},{7,23},{8,24},{9,... | collective-permute-start | bytes 4718600 | tf_op jit(solution)/shard_map/ppermute | solution.py:218
  9.8 6.8 %collective-permute-start.1 = (bf16[48,2048]{1,0:T(8,128)(2,1)S(1)}, bf16[48,2048]{1,0:T(8,128)(2,1)S(1)}, u32[]{:S(2)}, u32[]{:S(2)}) collective-permute-start(bf16[48,2048]{1,0:T(8,128)(2,1)S(1)} %shard_map.39.refs_2_), channel_id=1, source_target_pairs={{0,4},{1,5},{2,6},{3,7},{4,0},{5,1},{6,2},{7,3},{8,12},{9,13},{10,... | collective-permute-start | bytes 589832 | tf_op jit(solution)/shard_map/ppermute | solution.py:218
  10.0 11.5 %collective-permute-start.3 = (bf16[48,2048]{1,0:T(8,128)(2,1)S(1)}, bf16[48,2048]{1,0:T(8,128)(2,1)S(1)}, u32[]{:S(2)}, u32[]{:S(2)}) collective-permute-start(bf16[48,2048]{1,0:T(8,128)(2,1)S(1)} %shard_map.39.refs_2_), channel_id=1, source_target_pairs={{0,2},{1,3},{2,0},{3,1},{4,6},{5,7},{6,4},{7,5},{8,10},{9,11},{10,... | collective-permute-start | bytes 589832 | tf_op jit(solution)/shard_map/ppermute | solution.py:218
  16.6 9.0 %collective-permute-start.2 = (bf16[48,2048]{1,0:T(8,128)(2,1)S(1)}, bf16[48,2048]{1,0:T(8,128)(2,1)S(1)}, u32[]{:S(2)}, u32[]{:S(2)}) collective-permute-start(bf16[48,2048]{1,0:T(8,128)(2,1)S(1)} %collective-permute-done.1.refs_2_), channel_id=1, source_target_pairs={{1,3},{3,1},{5,7},{7,5},{8,10},{10,8},{12,14},{14,12},{17,19},{19,... | collective-permute-start | bytes 589832 | tf_op jit(solution)/shard_map/ppermute | solution.py:218
  25.7 21.7 %copy-start.2 = (bf16[128,8192]{1,0:T(8,128)(2,1)S(1)}, bf16[128,8192]{1,0:T(8,128)(2,1)}, u32[]{:S(2)}) copy-start(bf16[128,8192]{1,0:T(8,128)(2,1)} %mine_grads.3) | copy-start | bytes 6291460
  28.4 6.6 %collective-permute-start.4 = (f32[48,2048]{1,0:T(8,128)S(1)}, f32[48,2048]{1,0:T(8,128)S(1)}, u32[]{:S(2)}, u32[]{:S(2)}) collective-permute-start(f32[48,2048]{1,0:T(8,128)S(1)} %shard_map.44), channel_id=1, source_target_pairs={{0,1},{1,0},{2,3},{3,2},{4,5},{5,4},{6,7},{7,6},{8,9},{9,8},{10,11... | collective-permute-start | bytes 1179656 | tf_op jit(solution)/shard_map/ppermute | solution.py:218
  35.0 7.0 %collective-permute-start.5 = (bf16[48,2048]{1,0:T(8,128)(2,1)S(1)}, bf16[48,2048]{1,0:T(8,128)(2,1)S(1)}, u32[]{:S(2)}, u32[]{:S(2)}) collective-permute-start(bf16[48,2048]{1,0:T(8,128)(2,1)S(1)} %add_convert_fusion.a_ref), channel_id=1, source_target_pairs={{0,8},{1,6},{2,10},{3,4},{4,12},{5,2},{6,14},{7,0},{8,15},{9,1},{1... | collective-permute-start | bytes 589832 | tf_op jit(solution)/shard_map/ppermute | solution.py:218
  42.0 21.2 %copy-start.1 = (bf16[96,2048]{1,0:T(8,128)(2,1)S(1)}, bf16[96,2048]{1,0:T(8,128)(2,1)}, u32[]{:S(2)}) copy-start(bf16[96,2048]{1,0:T(8,128)(2,1)} %param.3) | copy-start | bytes 1179652
  42.0 4.6 %collective-permute-start.7 = (bf16[48,2048]{1,0:T(8,128)(2,1)S(1)}, bf16[48,2048]{1,0:T(8,128)(2,1)S(1)}, u32[]{:S(2)}, u32[]{:S(2)}) collective-permute-start(bf16[48,2048]{1,0:T(8,128)(2,1)S(1)} %shard_map.45.piece0), channel_id=1, source_target_pairs={{0,4},{1,5},{2,6},{3,7},{4,0},{5,1},{6,2},{7,3},{8,12},{9,13},{10,... | collective-permute-start | bytes 589832 | tf_op jit(solution)/shard_map/ppermute | solution.py:218
  42.1 5.2 %collective-permute-start.10 = (bf16[48,2048]{1,0:T(8,128)(2,1)S(1)}, bf16[48,2048]{1,0:T(8,128)(2,1)S(1)}, u32[]{:S(2)}, u32[]{:S(2)}) collective-permute-start(bf16[48,2048]{1,0:T(8,128)(2,1)S(1)} %shard_map.45.piece0), channel_id=1, source_target_pairs={{0,16},{1,17},{2,18},{3,19},{4,20},{5,21},{6,22},{7,23},{8,24},{9,... | collective-permute-start | bytes 589832 | tf_op jit(solution)/shard_map/ppermute | solution.py:218
  42.7 4.8 %collective-permute-start.9 = (bf16[48,2048]{1,0:T(8,128)(2,1)S(1)}, bf16[48,2048]{1,0:T(8,128)(2,1)S(1)}, u32[]{:S(2)}, u32[]{:S(2)}) collective-permute-start(bf16[48,2048]{1,0:T(8,128)(2,1)S(1)} %shard_map.45.piece0), channel_id=1, source_target_pairs={{0,2},{1,3},{2,0},{3,1},{4,6},{5,7},{6,4},{7,5},{8,10},{9,11},{10,... | collective-permute-start | bytes 589832 | tf_op jit(solution)/shard_map/ppermute | solution.py:218
  46.6 2.1 %collective-permute-start.8 = (bf16[48,2048]{1,0:T(8,128)(2,1)S(1)}, bf16[48,2048]{1,0:T(8,128)(2,1)S(1)}, u32[]{:S(2)}, u32[]{:S(2)}) collective-permute-start(bf16[48,2048]{1,0:T(8,128)(2,1)S(1)} %collective-permute-done.7.piece1), channel_id=1, source_target_pairs={{1,3},{3,1},{5,7},{7,5},{8,10},{10,8},{12,14},{14,12},{17,19},{19,... | collective-permute-start | bytes 589832 | tf_op jit(solution)/shard_map/ppermute | solution.py:218
  49.2 2.7 %collective-permute-start.11 = (f32[48,128]{1,0:T(8,128)S(1)}, f32[48,128]{1,0:T(8,128)S(1)}, u32[]{:S(2)}, u32[]{:S(2)}) collective-permute-start(f32[48,128]{1,0:T(8,128)S(1)} %get-tuple-element.43), channel_id=1, source_target_pairs={{0,16},{1,17},{2,18},{3,19},{4,20},{5,21},{6,22},{7,23},{8,24},{9,... | collective-permute-start | bytes 73736 | tf_op jit(solution)/shard_map/ppermute | solution.py:218
  51.9 10.6 %collective-permute-start.12 = (f32[48,128]{1,0:T(8,128)S(1)}, f32[48,128]{1,0:T(8,128)S(1)}, u32[]{:S(2)}, u32[]{:S(2)}) collective-permute-start(f32[48,128]{1,0:T(8,128)S(1)} %broadcast_select_fusion), channel_id=1, source_target_pairs={{0,1},{1,0},{2,3},{3,2},{4,5},{5,4},{6,7},{7,6},{8,9},{9,8},{10,11... | collective-permute-start | bytes 73736 | tf_op jit(solution)/shard_map/ppermute | solution.py:218

commit v12 on v11

--- a/solution.py
+++ b/solution.py
@@ -40,7 +40,7 @@
 ORDER = (0, 2, 1, 3)
 
 
-def start_half(fisher_ref, block, half, held_ref, sem):
+def half_copies(fisher_ref, block, half, held_ref, sem):
     steps = sem.shape[0]
     rows, width = held_ref.shape
     step = rows // steps
@@ -54,7 +54,6 @@
                 sem.at[i],
             )
         )
-        copies[-1].start()
     return copies
 
 
@@ -62,7 +61,7 @@
     return lax.dot_general(chunk_ref[...], fisher, NT, preferred_element_type=jnp.float32)
 
 
-def fisher_kernel(n_in, has_base, fetch, step, *refs):
+def fisher_kernel(n_in, has_base, fetch, *refs):
     if fetch:
         at_ref, fisher_ref, *refs = refs
     chunk_ref, halves = (refs[0], refs[1:3]) if n_in else (None, ())
@@ -71,21 +70,25 @@
     held = outs[1:] if n_in else outs
     copies = []
     for k, (piece, half) in enumerate(fetch):
-        copies += start_half(fisher_ref, at_ref[0] ^ ORDER[piece], half, held[k], sem.at[k])
+        copies += half_copies(fisher_ref, at_ref[0] ^ ORDER[piece], half, held[k], sem.at[k])
+    if fetch:
+
+        @pl.when(at_ref[0] >= 0)
+        def _():
+            for copy in copies:
+                copy.start()
+
     for h, half_ref in enumerate(halves):
         rows = half_ref.shape[0]
-
-        @pl.loop(0, rows // step)
-        def _(i):
-            columns = pl.ds(pl.multiple_of(h * rows + i * step, step), step)
-            term = times(chunk_ref, half_ref[pl.ds(pl.multiple_of(i * step, step), step), :])
-            outs[0][:, columns] = term + base_ref[:, columns] if has_base else term
+        columns = slice(h * rows, (h + 1) * rows)
+        term = times(chunk_ref, half_ref[...])
+        outs[0][:, columns] = term + base_ref[:, columns] if has_base else term
 
     for copy in copies:
         copy.wait()
 
 
-def fisher_step(fisher, first, width, fetch, chunk=None, halves=(), base=None, step=1024):
+def fisher_step(fisher, first, width, fetch, chunk=None, halves=(), base=None):
     rows = fisher.shape[0]
     ins = [] if chunk is None else [chunk, *halves]
     has_base = base is not None
@@ -93,7 +96,7 @@
     out_shape = [] if chunk is None else [jax.ShapeDtypeStruct((chunk.shape[0], rows), jnp.float32)]
     out_shape += [held] * len(fetch)
     return pl.pallas_call(
-        functools.partial(fisher_kernel, len(ins), has_base, fetch, step),
+        functools.partial(fisher_kernel, len(ins), has_base, fetch),
         out_shape=out_shape,
         in_specs=[SMEM, HBM][: 2 * bool(fetch)] + [VMEM] * (len(ins) + has_base),
         out_specs=[VMEM] * len(out_shape),
@@ -107,23 +110,23 @@
     )(*((scalar(first), fisher) if fetch else ()), *ins, *([base] if has_base else []))
 
 
-def base_kernel(at_ref, piece0, piece1, piece2, swapped, mine_grads, other_grads, mine, other, theirs):
+def base_kernel(at_ref, piece0, piece1, piece2, mine_grads, other_grads, mine, other):
     width = piece0.shape[1]
-    starts = [pl.multiple_of((at_ref[0] ^ mask) * width, width) for mask in ORDER[:3]]
     total = None
-    for piece, start in zip((piece0, piece1, piece2), starts):
+    for piece, mask in zip((piece0, piece1, piece2), ORDER):
+        start = pl.multiple_of((at_ref[0] ^ mask) * width, width)
         term = times(piece, mine_grads[:, pl.ds(start, width)])
         total = term if total is None else total + term
     mine[...] = total
-    theirs[...] = times(swapped, mine_grads[:, pl.ds(starts[0], width)])
     other[...] = times(piece1, other_grads[:, :width]) + times(piece2, other_grads[:, width : 2 * width])
 
 
-def last_kernel(at_ref, piece3, mine_grads, other_grads, mine_base, other_base, mine, other):
+def last_kernel(at_ref, piece3, swapped, mine_grads, other_grads, mine_base, other_base, mine, other, theirs):
     width = piece3.shape[1]
-    start = pl.multiple_of((at_ref[0] ^ ORDER[3]) * width, width)
+    start0, start3 = (pl.multiple_of((at_ref[0] ^ ORDER[k]) * width, width) for k in (0, 3))
     other[...] = other_base[...] + times(piece3, other_grads[:, 2 * width :])
-    mine[...] = mine_base[...] + times(piece3, mine_grads[:, pl.ds(start, width)])
+    mine[...] = mine_base[...] + times(piece3, mine_grads[:, pl.ds(start3, width)])
+    theirs[...] = times(swapped, mine_grads[:, pl.ds(start0, width)])
 
 
 def score_call(kernel, n_out, examples, first, *operands):
@@ -165,7 +168,7 @@
         in_specs=[SMEM, HBM],
         out_specs=VMEM,
         scratch_shapes=[pltpu.SemaphoreType.DMA((n,))],
-        compiler_params=limit(57),
+        compiler_params=limit(51),
         cost_estimate=pl.CostEstimate(
             flops=0, bytes_accessed=2 * n * width * src.shape[0], transcendentals=0
         ),
@@ -244,10 +247,11 @@
         first = pick(owner, own, came, after)
         beside = along_z(first, {0: 1, 1: 0, 2: 3, 3: 2})
         across = along_z(first, {0: 0, 1: 1, 2: 2, 3: 3}, True)
+        diagonal = along_z(first, {2: 3, 3: 2}, True)
 
         def corner(after):
-            ready, _ = lax.optimization_barrier((beside, after))
-            return pick(owner, came, along_z(ready, {2: 2, 3: 3}, True))
+            ready, _ = lax.optimization_barrier((came, after))
+            return pick(owner, ready, diagonal)
 
         return first, beside, across, corner
 
@@ -255,29 +259,26 @@
     column = plane * nx + x - d * (nex // 2)
 
     rows, width = nq // ny, queries.shape[1]
-    own = lax.optimization_barrier(lax.dynamic_slice_in_dim(queries, y * rows, rows, axis=0))
-    to_y = cut(stored_grads, ORDER[1:], column, width)
+    own, grads = lax.optimization_barrier(
+        (lax.dynamic_slice_in_dim(queries, y * rows, rows, axis=0), stored_grads)
+    )
+    to_y = cut(grads, ORDER[1:], column, width)
     other_grads = swap_y(to_y)
     at, _ = lax.optimization_barrier((column, to_y))
     step = functools.partial(fisher_step, inverse_fisher, at, width)
-    a0, a1, b0 = step(((0, 0), (0, 1), (1, 0)))
+    a0, a1, b0, b1 = step(((0, 0), (0, 1), (1, 0), (1, 1)))
     q0, q1, q2, corner = gather(own, (a0,))
-    total, b1, c0 = step(((1, 1), (2, 0)), q0, (a0, a1))
-    q3 = corner(total)
-    total, c1, d0 = step(((2, 1), (3, 0)), q1, (b0, b1), total)
+    total, c0, c1 = step(((2, 0), (2, 1)), q0, (a0, a1))
+    total, d0 = step(((3, 0),), q1, (b0, b1), total)
     total, d1 = step(((3, 1),), q2, (c0, c1), total)
-    (total,) = step((), q3, (d0, d1), total)
+    (total,) = step((), corner(total), (d0, d1), total)
     panel = (total + swap_core(total)).astype(jnp.bfloat16)
 
-    p0, p1, p2, corner = gather(panel, (other_grads,))
-    p3 = corner(p1)
+    p0, p1, p2, corner = gather(panel)
     examples = stored_grads.shape[0]
+    mine, other = score_call(base_kernel, 2, examples, column, p0, p1, p2, stored_grads, other_grads)
     mine, other, theirs = score_call(
-        base_kernel, 3, examples, column, p0, p1, p2, swap_y(p0), stored_grads, other_grads
-    )
-    p3, _ = lax.optimization_barrier((p3, mine))
-    mine, other = score_call(
-        last_kernel, 2, examples, column, p3, stored_grads, other_grads, mine, other
+        last_kernel, 3, examples, column, corner(mine), swap_y(p0), stored_grads, other_grads, mine, other
     )
 
     other = swap_y(other) + theirs

time: 63.4 us -> 62 us (0.978)
  the two profiles are of different devices: /device:TPU:25 before, /device:TPU:0 now
where the time goes in v12:
time: 62 us; the launch traced here: 61.7 us
  Pallas kernels  25.3 us (41%)
  starting transfers between devices  19.7 us (32%)
  waiting for transfers between devices  14.2 us (23%)
  local copies, waits for them, and re-layouts  1.68 us (3%)
  other arithmetic  0.67 us (1%)
    pallas_call x5, Pallas kernels, fisher_step(): pl.pallas_call(functools.partial(fisher_kernel, len(ins), has_base, fetch...  21.2 us
    ppermute x13, starting transfers between devices, move(): return lax.ppermute(value, AXES, pairs)  19.7 us
    ppermute x13, waiting for transfers between devices, move(): return lax.ppermute(value, AXES, pairs)  14.2 us
    pallas_call x2, Pallas kernels, score_call(): pl.pallas_call(kernel, out_shape=[jax.ShapeDtypeStruct((rows, examples),...  1.7 us
    pallas_call x1, Pallas kernels, cut(): pl.pallas_call(functools.partial(cut_kernel, order), out_shape=jax.ShapeD...  1.38 us
  transfers between devices with their start and end apart: 13, of which 6 were waited for; matrix products, arithmetic and copies ran while one was open for 0% of the time, Pallas kernels for 40%

profile of v12, /device:TPU:0, one launch (start us, length us, event | category | flops | bytes accessed | tf_op | source)
XLA Modules:
  0.0 61.7 jit_solution(4032004841172114426)
XLA Ops:
  0.0 1.0 %copy-done = bf16[96,2048]{1,0:T(8,128)(2,1)S(1)} copy-done((bf16[96,2048]{1,0:T(8,128)(2,1)S(1)}, bf16[96,2048]{1,0:T(8,128)(2,1)}, u32[]{:S(2)}) %copy-start) | copy-done | bytes 393240
  1.0 0.7 %constant_dynamic-slice_fusion.a_ref = bf16[48,2048]{1,0:T(8,128)(2,1)} fusion(bf16[96,2048]{1,0:T(8,128)(2,1)S(1)} %copy-done, s32[]{:T(128)S(6)} %select_n.44), kind=kLoop, calls=%fused_computation.3 | loop fusion | bytes 393220 | tf_op jit(solution)/shard_map/dynamic_slice | solution.py:263
  1.7 4.0 %collective-permute-start = (bf16[48,2048]{1,0:T(8,128)(2,1)}, bf16[48,2048]{1,0:T(8,128)(2,1)S(1)}, u32[]{:S(2)}, u32[]{:S(2)}) collective-permute-start(bf16[48,2048]{1,0:T(8,128)(2,1)} %constant_dynamic-slice_fusion.a_ref), channel_id=1, source_target_pairs={{0,8},{1,6},{2,10},{3,4},{4,12},{5,2},{6,14},{7,0},{8,15},{9,1},{1... | collective-permute-start | bytes 589832 | tf_op jit(solution)/shard_map/ppermute | solution.py:221
  5.7 1.4 %shard_map.37 = bf16[128,6144]{1,0:T(8,128)(2,1)S(1)} custom-call(s32[1]{0:T(128)} %bitcast.at_ref, bf16[128,8192]{1,0:T(8,128)(2,1)} %mine_grads.3), custom_call_target="tpu_custom_call" | custom-call | bytes 1572864 | tf_op jit(solution)/shard_map/pallas_call | solution.py:165
  7.1 1.6 %collective-permute-start.8 = (bf16[128,6144]{1,0:T(8,128)(2,1)S(1)}, bf16[128,6144]{1,0:T(8,128)(2,1)S(1)}, u32[]{:S(2)}, u32[]{:S(2)}) collective-permute-start(bf16[128,6144]{1,0:T(8,128)(2,1)S(1)} %shard_map.37), channel_id=1, source_target_pairs={{0,16},{1,17},{2,18},{3,19},{4,20},{5,21},{6,22},{7,23},{8,24},{9,... | collective-permute-start | bytes 4718600 | tf_op jit(solution)/shard_map/ppermute | solution.py:221
  8.7 6.0 %shard_map.38 = (bf16[1024,2048]{1,0:T(8,128)(2,1)S(1)}, bf16[1024,2048]{1,0:T(8,128)(2,1)S(1)}, bf16[1024,2048]{1,0:T(8,128)(2,1)S(1)}, bf16[1024,2048]{1,0:T(8,128)(2,1)S(1)}) custom-call(s32[1]{0:T(128)} %bitcast.2.refs_0_, bf16[2048,8192]{1,0:T(8,128)(2,1)} %refs_1_.7), custom_call_target="tpu_custom_call" | custom-call | bytes 16777216 | tf_op jit(solution)/shard_map/pallas_call | solution.py:98
  14.7 0.9 %shard_map.39.refs_2_ = bf16[48,2048]{1,0:T(8,128)(2,1)S(1)} custom-call(s32[1]{0:T(128)} %bitcast.1.at_ref, bf16[48,2048]{1,0:T(8,128)(2,1)} %constant_dynamic-slice_fusion.a_ref, bf16[48,2048]{1,0:T(8,128)(2,1)S(1)} %collective-permute-done.b_ref.a_ref, bf16[1024,2048]{1,0:T(8,128)(2,1)S(1)} %get-tuple-element.29.refs_0_.refs_3_), custom_call_target="tpu_custom_call" | custom-call | bytes 393216 | tf_op jit(solution)/shard_map/pallas_call | solution.py:191
  15.6 1.6 %collective-permute-start.2 = (bf16[48,2048]{1,0:T(8,128)(2,1)S(1)}, bf16[48,2048]{1,0:T(8,128)(2,1)S(1)}, u32[]{:S(2)}, u32[]{:S(2)}) collective-permute-start(bf16[48,2048]{1,0:T(8,128)(2,1)S(1)} %shard_map.39.refs_2_), channel_id=1, source_target_pairs={{0,4},{1,5},{2,6},{3,7},{4,0},{5,1},{6,2},{7,3},{8,12},{9,13},{10,... | collective-permute-start | bytes 589832 | tf_op jit(solution)/shard_map/ppermute | solution.py:221
  17.3 1.5 %collective-permute-start.1 = (bf16[48,2048]{1,0:T(8,128)(2,1)S(1)}, bf16[48,2048]{1,0:T(8,128)(2,1)S(1)}, u32[]{:S(2)}, u32[]{:S(2)}) collective-permute-start(bf16[48,2048]{1,0:T(8,128)(2,1)S(1)} %shard_map.39.refs_2_), channel_id=1, source_target_pairs={{0,2},{1,3},{2,0},{3,1},{4,6},{5,7},{6,4},{7,5},{8,10},{9,11},{10,... | collective-permute-start | bytes 589832 | tf_op jit(solution)/shard_map/ppermute | solution.py:221
  18.7 0.7 %collective-permute-start.3 = (bf16[48,2048]{1,0:T(8,128)(2,1)S(1)}, bf16[48,2048]{1,0:T(8,128)(2,1)S(1)}, u32[]{:S(2)}, u32[]{:S(2)}) collective-permute-start(bf16[48,2048]{1,0:T(8,128)(2,1)S(1)} %shard_map.39.refs_2_), channel_id=1, source_target_pairs={{1,7},{3,5},{5,3},{7,1},{8,14},{10,12},{12,10},{14,8},{17,23},{19,... | collective-permute-start | bytes 589832 | tf_op jit(solution)/shard_map/ppermute | solution.py:221
  19.4 5.5 %shard_map.40 = (f32[48,2048]{1,0:T(8,128)S(1)}, bf16[1024,2048]{1,0:T(8,128)(2,1)S(1)}, bf16[1024,2048]{1,0:T(8,128)(2,1)S(1)}) custom-call(s32[1]{0:T(128)} %bitcast.2.refs_0_, bf16[2048,8192]{1,0:T(8,128)(2,1)} %refs_1_.7, bf16[48,2048]{1,0:T(8,128)(2,1)S(1)} %shard_map.39.refs_2_, bf16[1024,2048]{1,0:T(8,128)(2,1)S(1)} %get-tuple-element.29.refs_0_.refs_3_, ...), custom_call_target="tpu_custom_call" | custom-call | flops 402653184 | bytes 16777216 | tf_op jit(solution)/shard_map/pallas_call | solution.py:98
  25.0 0.0 collective-permute-done.2.refs_2_
  25.0 2.9 %shard_map.41 = (f32[48,2048]{1,0:T(8,128)S(1)}, bf16[1024,2048]{1,0:T(8,128)(2,1)S(1)}) custom-call(s32[1]{0:T(128)} %bitcast.2.refs_0_, bf16[2048,8192]{1,0:T(8,128)(2,1)} %refs_1_.7, bf16[48,2048]{1,0:T(8,128)(2,1)S(1)} %collective-permute-done.2.refs_2_, bf16[1024,2048]{1,0:T(8,128)(2,1)S(1)} %get-tuple-element.33.refs_3_, ...), custom_call_target="tpu_custom_call" | custom-call | flops 402653184 | bytes 12582912 | tf_op jit(solution)/shard_map/pallas_call | solution.py:98
  27.9 4.1 %shard_map.42 = (f32[48,2048]{1,0:T(8,128)S(1)}, bf16[1024,2048]{1,0:T(8,128)(2,1)S(1)}) custom-call(s32[1]{0:T(128)} %bitcast.2.refs_0_, bf16[2048,8192]{1,0:T(8,128)(2,1)} %refs_1_.7, bf16[48,2048]{1,0:T(8,128)(2,1)S(1)} %collective-permute-done.1.refs_2_, bf16[1024,2048]{1,0:T(8,128)(2,1)S(1)} %get-tuple-element.31.refs_3_, ...), custom_call_target="tpu_custom_call" | custom-call | flops 402653184 | bytes 12582912 | tf_op jit(solution)/shard_map/pallas_call | solution.py:98
  32.1 0.0 copy-start.2
  32.1 2.6 %shard_map.44 = f32[48,2048]{1,0:T(8,128)S(1)} custom-call(bf16[48,2048]{1,0:T(8,128)(2,1)S(1)} %shard_map.43.refs_0_, bf16[1024,2048]{1,0:T(8,128)(2,1)S(1)} %get-tuple-element.39.refs_1_, bf16[1024,2048]{1,0:T(8,128)(2,1)S(1)} %get-tuple-element.40.refs_2_, f32[48,2048]{1,0:T(8,128)S(1)} %get-tuple-element.37.refs_3_), custom_call_target="tpu_custom_call" | custom-call | flops 402653184 | bytes 8388608 | tf_op jit(solution)/shard_map/pallas_call | solution.py:98
  34.7 0.6 %collective-permute-start.4 = (f32[48,2048]{1,0:T(8,128)S(1)}, f32[48,2048]{1,0:T(8,128)S(1)}, u32[]{:S(2)}, u32[]{:S(2)}) collective-permute-start(f32[48,2048]{1,0:T(8,128)S(1)} %shard_map.44), channel_id=1, source_target_pairs={{0,1},{1,0},{2,3},{3,2},{4,5},{5,4},{6,7},{7,6},{8,9},{9,8},{10,11... | collective-permute-start | bytes 1179656 | tf_op jit(solution)/shard_map/ppermute | solution.py:221
  35.4 1.3 %collective-permute-done.4 = f32[48,2048]{1,0:T(8,128)S(1)} collective-permute-done((f32[48,2048]{1,0:T(8,128)S(1)}, f32[48,2048]{1,0:T(8,128)S(1)}, u32[]{:S(2)}, u32[]{:S(2)}) %collective-permute-start.4) | collective-permute-done | bytes 393248 | tf_op jit(solution)/shard_map/ppermute | solution.py:221
  36.8 3.5 %collective-permute-start.5 = (bf16[48,2048]{1,0:T(8,128)(2,1)S(1)}, bf16[48,2048]{1,0:T(8,128)(2,1)S(1)}, u32[]{:S(2)}, u32[]{:S(2)}) collective-permute-start(bf16[48,2048]{1,0:T(8,128)(2,1)S(1)} %add_convert_fusion.a_ref), channel_id=1, source_target_pairs={{0,8},{1,6},{2,10},{3,4},{4,12},{5,2},{6,14},{7,0},{8,15},{9,1},{1... | collective-permute-start | bytes 589832 | tf_op jit(solution)/shard_map/ppermute | solution.py:221
  40.2 3.2 %collective-permute-done.5.b_ref.a_ref = bf16[48,2048]{1,0:T(8,128)(2,1)S(1)} collective-permute-done((bf16[48,2048]{1,0:T(8,128)(2,1)S(1)}, bf16[48,2048]{1,0:T(8,128)(2,1)S(1)}, u32[]{:S(2)}, u32[]{:S(2)}) %collective-permute-start.5) | collective-permute-done | bytes 196640 | tf_op jit(solution)/shard_map/ppermute | solution.py:221
  43.5 2.6 %collective-permute-start.6 = (bf16[48,2048]{1,0:T(8,128)(2,1)S(1)}, bf16[48,2048]{1,0:T(8,128)(2,1)S(1)}, u32[]{:S(2)}, u32[]{:S(2)}) collective-permute-start(bf16[48,2048]{1,0:T(8,128)(2,1)S(1)} %shard_map.45.piece0), channel_id=1, source_target_pairs={{0,4},{1,5},{2,6},{3,7},{4,0},{5,1},{6,2},{7,3},{8,12},{9,13},{10,... | collective-permute-start | bytes 589832 | tf_op jit(solution)/shard_map/ppermute | solution.py:221
  46.1 0.6 %collective-permute-start.7 = (bf16[48,2048]{1,0:T(8,128)(2,1)S(1)}, bf16[48,2048]{1,0:T(8,128)(2,1)S(1)}, u32[]{:S(2)}, u32[]{:S(2)}) collective-permute-start(bf16[48,2048]{1,0:T(8,128)(2,1)S(1)} %shard_map.45.piece0), channel_id=1, source_target_pairs={{0,2},{1,3},{2,0},{3,1},{4,6},{5,7},{6,4},{7,5},{8,10},{9,11},{10,... | collective-permute-start | bytes 589832 | tf_op jit(solution)/shard_map/ppermute | solution.py:221
  46.7 0.7 %collective-permute-start.9 = (bf16[48,2048]{1,0:T(8,128)(2,1)S(1)}, bf16[48,2048]{1,0:T(8,128)(2,1)S(1)}, u32[]{:S(2)}, u32[]{:S(2)}) collective-permute-start(bf16[48,2048]{1,0:T(8,128)(2,1)S(1)} %shard_map.45.piece0), channel_id=1, source_target_pairs={{1,7},{3,5},{5,3},{7,1},{8,14},{10,12},{12,10},{14,8},{17,23},{19,... | collective-permute-start | bytes 589832 | tf_op jit(solution)/shard_map/ppermute | solution.py:221
  47.4 1.4 %collective-permute-start.10 = (bf16[48,2048]{1,0:T(8,128)(2,1)S(1)}, bf16[48,2048]{1,0:T(8,128)(2,1)S(1)}, u32[]{:S(2)}, u32[]{:S(2)}) collective-permute-start(bf16[48,2048]{1,0:T(8,128)(2,1)S(1)} %shard_map.45.piece0), channel_id=1, source_target_pairs={{0,16},{1,17},{2,18},{3,19},{4,20},{5,21},{6,22},{7,23},{8,24},{9,... | collective-permute-start | bytes 589832 | tf_op jit(solution)/shard_map/ppermute | solution.py:221
  48.9 2.8 %collective-permute-done.6.piece1 = bf16[48,2048]{1,0:T(8,128)(2,1)S(1)} collective-permute-done((bf16[48,2048]{1,0:T(8,128)(2,1)S(1)}, bf16[48,2048]{1,0:T(8,128)(2,1)S(1)}, u32[]{:S(2)}, u32[]{:S(2)}) %collective-permute-start.6) | collective-permute-done | bytes 196640 | tf_op jit(solution)/shard_map/ppermute | solution.py:221
  51.7 2.5 %collective-permute-done.7.piece2 = bf16[48,2048]{1,0:T(8,128)(2,1)S(1)} collective-permute-done((bf16[48,2048]{1,0:T(8,128)(2,1)S(1)}, bf16[48,2048]{1,0:T(8,128)(2,1)S(1)}, u32[]{:S(2)}, u32[]{:S(2)}) %collective-permute-start.7) | collective-permute-done | bytes 196640 | tf_op jit(solution)/shard_map/ppermute | solution.py:221
  54.2 1.0 %shard_map.46 = (f32[48,128]{1,0:T(8,128)S(1)}, f32[48,128]{1,0:T(8,128)S(1)}) custom-call(s32[1]{0:T(128)} %bitcast.at_ref, bf16[48,2048]{1,0:T(8,128)(2,1)S(1)} %shard_map.45.piece0, bf16[48,2048]{1,0:T(8,128)(2,1)S(1)} %collective-permute-done.6.piece1, bf16[48,2048]{1,0:T(8,128)(2,1)S(1)} %collective-permute-done.7.piece2, ...), custom_call_target="tpu_custom_call" | custom-call | flops 100663296 | bytes 2097152 | tf_op jit(solution)/shard_map/pallas_call | solution.py:134
  55.3 0.7 %shard_map.48 = (f32[48,128]{1,0:T(8,128)S(1)}, f32[48,128]{1,0:T(8,128)S(1)}, f32[48,128]{1,0:T(8,128)S(1)}) custom-call(s32[1]{0:T(128)} %bitcast.at_ref, bf16[48,2048]{1,0:T(8,128)(2,1)S(1)} %shard_map.47.piece3, bf16[48,2048]{1,0:T(8,128)(2,1)S(1)} %collective-permute-done.10.swapped, bf16[128,8192]{1,0:T(8,128)(2,1)S(1)} %copy-done.2, ...), custom_call_target="tpu_custom_call" | custom-call | flops 150994944 | bytes 3145728 | tf_op jit(solution)/shard_map/pallas_call | solution.py:134
  56.0 0.9 %collective-permute-start.11 = (f32[48,128]{1,0:T(8,128)S(1)}, f32[48,128]{1,0:T(8,128)S(1)}, u32[]{:S(2)}, u32[]{:S(2)}) collective-permute-start(f32[48,128]{1,0:T(8,128)S(1)} %get-tuple-element.45), channel_id=1, source_target_pairs={{0,16},{1,17},{2,18},{3,19},{4,20},{5,21},{6,22},{7,23},{8,24},{9,... | collective-permute-start | bytes 73736 | tf_op jit(solution)/shard_map/ppermute | solution.py:221
  56.9 3.0 %collective-permute-done.11 = f32[48,128]{1,0:T(8,128)S(1)} collective-permute-done((f32[48,128]{1,0:T(8,128)S(1)}, f32[48,128]{1,0:T(8,128)S(1)}, u32[]{:S(2)}, u32[]{:S(2)}) %collective-permute-start.11) | collective-permute-done | bytes 24608 | tf_op jit(solution)/shard_map/ppermute | solution.py:221
  59.9 1.2 %collective-permute-done.12 = f32[48,128]{1,0:T(8,128)S(1)} collective-permute-done((f32[48,128]{1,0:T(8,128)S(1)}, f32[48,128]{1,0:T(8,128)S(1)}, u32[]{:S(2)}, u32[]{:S(2)}) %collective-permute-start.12) | collective-permute-done | bytes 24608 | tf_op jit(solution)/shard_map/ppermute | solution.py:221
  61.1 0.6 %select_add_fusion = f32[48,128]{1,0:T(8,128)} fusion(f32[48,128]{1,0:T(8,128)S(1)} %collective-permute-done.12, f32[48,128]{1,0:T(8,128)S(1)} %get-tuple-element.44, pred[]{:T(512)S(6)} %eq.12, f32[48,128]{1,0:T(8,128)S(1)} %collective-permute-done.11, f32[48,128]{1,0:T(8,128)S(1)} %get-tuple-element.46), kind=kLoop, calls=%fused_computation.1 | loop fusion | flops 18432 | bytes 122881 | tf_op jit(solution)/shard_map/add | solution.py:287
  (16 shorter events, 0.1 us)
Async XLA Ops:
  0.0 1.0 %copy-start = (bf16[96,2048]{1,0:T(8,128)(2,1)S(1)}, bf16[96,2048]{1,0:T(8,128)(2,1)}, u32[]{:S(2)}) copy-start(bf16[96,2048]{1,0:T(8,128)(2,1)} %param.3) | copy-start | bytes 1179652
  1.7 13.0 %collective-permute-start = (bf16[48,2048]{1,0:T(8,128)(2,1)}, bf16[48,2048]{1,0:T(8,128)(2,1)S(1)}, u32[]{:S(2)}, u32[]{:S(2)}) collective-permute-start(bf16[48,2048]{1,0:T(8,128)(2,1)} %constant_dynamic-slice_fusion.a_ref), channel_id=1, source_target_pairs={{0,8},{1,6},{2,10},{3,4},{4,12},{5,2},{6,14},{7,0},{8,15},{9,1},{1... | collective-permute-start | bytes 589832 | tf_op jit(solution)/shard_map/ppermute | solution.py:221
  7.1 47.1 %collective-permute-start.8 = (bf16[128,6144]{1,0:T(8,128)(2,1)S(1)}, bf16[128,6144]{1,0:T(8,128)(2,1)S(1)}, u32[]{:S(2)}, u32[]{:S(2)}) collective-permute-start(bf16[128,6144]{1,0:T(8,128)(2,1)S(1)} %shard_map.37), channel_id=1, source_target_pairs={{0,16},{1,17},{2,18},{3,19},{4,20},{5,21},{6,22},{7,23},{8,24},{9,... | collective-permute-start | bytes 4718600 | tf_op jit(solution)/shard_map/ppermute | solution.py:221
  15.6 9.3 %collective-permute-start.2 = (bf16[48,2048]{1,0:T(8,128)(2,1)S(1)}, bf16[48,2048]{1,0:T(8,128)(2,1)S(1)}, u32[]{:S(2)}, u32[]{:S(2)}) collective-permute-start(bf16[48,2048]{1,0:T(8,128)(2,1)S(1)} %shard_map.39.refs_2_), channel_id=1, source_target_pairs={{0,4},{1,5},{2,6},{3,7},{4,0},{5,1},{6,2},{7,3},{8,12},{9,13},{10,... | collective-permute-start | bytes 589832 | tf_op jit(solution)/shard_map/ppermute | solution.py:221
  17.3 10.6 %collective-permute-start.1 = (bf16[48,2048]{1,0:T(8,128)(2,1)S(1)}, bf16[48,2048]{1,0:T(8,128)(2,1)S(1)}, u32[]{:S(2)}, u32[]{:S(2)}) collective-permute-start(bf16[48,2048]{1,0:T(8,128)(2,1)S(1)} %shard_map.39.refs_2_), channel_id=1, source_target_pairs={{0,2},{1,3},{2,0},{3,1},{4,6},{5,7},{6,4},{7,5},{8,10},{9,11},{10,... | collective-permute-start | bytes 589832 | tf_op jit(solution)/shard_map/ppermute | solution.py:221
  18.7 13.3 %collective-permute-start.3 = (bf16[48,2048]{1,0:T(8,128)(2,1)S(1)}, bf16[48,2048]{1,0:T(8,128)(2,1)S(1)}, u32[]{:S(2)}, u32[]{:S(2)}) collective-permute-start(bf16[48,2048]{1,0:T(8,128)(2,1)S(1)} %shard_map.39.refs_2_), channel_id=1, source_target_pairs={{1,7},{3,5},{5,3},{7,1},{8,14},{10,12},{12,10},{14,8},{17,23},{19,... | collective-permute-start | bytes 589832 | tf_op jit(solution)/shard_map/ppermute | solution.py:221
  32.1 22.2 %copy-start.2 = (bf16[128,8192]{1,0:T(8,128)(2,1)S(1)}, bf16[128,8192]{1,0:T(8,128)(2,1)}, u32[]{:S(2)}) copy-start(bf16[128,8192]{1,0:T(8,128)(2,1)} %mine_grads.3) | copy-start | bytes 6291460
  34.7 2.0 %collective-permute-start.4 = (f32[48,2048]{1,0:T(8,128)S(1)}, f32[48,2048]{1,0:T(8,128)S(1)}, u32[]{:S(2)}, u32[]{:S(2)}) collective-permute-start(f32[48,2048]{1,0:T(8,128)S(1)} %shard_map.44), channel_id=1, source_target_pairs={{0,1},{1,0},{2,3},{3,2},{4,5},{5,4},{6,7},{7,6},{8,9},{9,8},{10,11... | collective-permute-start | bytes 1179656 | tf_op jit(solution)/shard_map/ppermute | solution.py:221
  36.8 6.7 %collective-permute-start.5 = (bf16[48,2048]{1,0:T(8,128)(2,1)S(1)}, bf16[48,2048]{1,0:T(8,128)(2,1)S(1)}, u32[]{:S(2)}, u32[]{:S(2)}) collective-permute-start(bf16[48,2048]{1,0:T(8,128)(2,1)S(1)} %add_convert_fusion.a_ref), channel_id=1, source_target_pairs={{0,8},{1,6},{2,10},{3,4},{4,12},{5,2},{6,14},{7,0},{8,15},{9,1},{1... | collective-permute-start | bytes 589832 | tf_op jit(solution)/shard_map/ppermute | solution.py:221
  43.5 18.2 %copy-start.1 = (bf16[96,2048]{1,0:T(8,128)(2,1)S(1)}, bf16[96,2048]{1,0:T(8,128)(2,1)}, u32[]{:S(2)}) copy-start(bf16[96,2048]{1,0:T(8,128)(2,1)} %param.3) | copy-start | bytes 1179652
  43.5 8.2 %collective-permute-start.6 = (bf16[48,2048]{1,0:T(8,128)(2,1)S(1)}, bf16[48,2048]{1,0:T(8,128)(2,1)S(1)}, u32[]{:S(2)}, u32[]{:S(2)}) collective-permute-start(bf16[48,2048]{1,0:T(8,128)(2,1)S(1)} %shard_map.45.piece0), channel_id=1, source_target_pairs={{0,4},{1,5},{2,6},{3,7},{4,0},{5,1},{6,2},{7,3},{8,12},{9,13},{10,... | collective-permute-start | bytes 589832 | tf_op jit(solution)/shard_map/ppermute | solution.py:221
  46.1 8.1 %collective-permute-start.7 = (bf16[48,2048]{1,0:T(8,128)(2,1)S(1)}, bf16[48,2048]{1,0:T(8,128)(2,1)S(1)}, u32[]{:S(2)}, u32[]{:S(2)}) collective-permute-start(bf16[48,2048]{1,0:T(8,128)(2,1)S(1)} %shard_map.45.piece0), channel_id=1, source_target_pairs={{0,2},{1,3},{2,0},{3,1},{4,6},{5,7},{6,4},{7,5},{8,10},{9,11},{10,... | collective-permute-start | bytes 589832 | tf_op jit(solution)/shard_map/ppermute | solution.py:221
  46.7 8.5 %collective-permute-start.9 = (bf16[48,2048]{1,0:T(8,128)(2,1)S(1)}, bf16[48,2048]{1,0:T(8,128)(2,1)S(1)}, u32[]{:S(2)}, u32[]{:S(2)}) collective-permute-start(bf16[48,2048]{1,0:T(8,128)(2,1)S(1)} %shard_map.45.piece0), channel_id=1, source_target_pairs={{1,7},{3,5},{5,3},{7,1},{8,14},{10,12},{12,10},{14,8},{17,23},{19,... | collective-permute-start | bytes 589832 | tf_op jit(solution)/shard_map/ppermute | solution.py:221
  47.4 7.9 %collective-permute-start.10 = (bf16[48,2048]{1,0:T(8,128)(2,1)S(1)}, bf16[48,2048]{1,0:T(8,128)(2,1)S(1)}, u32[]{:S(2)}, u32[]{:S(2)}) collective-permute-start(bf16[48,2048]{1,0:T(8,128)(2,1)S(1)} %shard_map.45.piece0), channel_id=1, source_target_pairs={{0,16},{1,17},{2,18},{3,19},{4,20},{5,21},{6,22},{7,23},{8,24},{9,... | collective-permute-start | bytes 589832 | tf_op jit(solution)/shard_map/ppermute | solution.py:221
  56.0 3.9 %collective-permute-start.11 = (f32[48,128]{1,0:T(8,128)S(1)}, f32[48,128]{1,0:T(8,128)S(1)}, u32[]{:S(2)}, u32[]{:S(2)}) collective-permute-start(f32[48,128]{1,0:T(8,128)S(1)} %get-tuple-element.45), channel_id=1, source_target_pairs={{0,16},{1,17},{2,18},{3,19},{4,20},{5,21},{6,22},{7,23},{8,24},{9,... | collective-permute-start | bytes 73736 | tf_op jit(solution)/shard_map/ppermute | solution.py:221
  59.9 1.2 %collective-permute-start.12 = (f32[48,128]{1,0:T(8,128)S(1)}, f32[48,128]{1,0:T(8,128)S(1)}, u32[]{:S(2)}, u32[]{:S(2)}) collective-permute-start(f32[48,128]{1,0:T(8,128)S(1)} %broadcast_select_fusion), channel_id=1, source_target_pairs={{0,1},{1,0},{2,3},{3,2},{4,5},{5,4},{6,7},{7,6},{8,9},{9,8},{10,11... | collective-permute-start | bytes 73736 | tf_op jit(solution)/shard_map/ppermute | solution.py:221

commit v13 on v12

--- a/solution.py
+++ b/solution.py
@@ -70,19 +70,24 @@
     held = outs[1:] if n_in else outs
     copies = []
     for k, (piece, half) in enumerate(fetch):
-        copies += half_copies(fisher_ref, at_ref[0] ^ ORDER[piece], half, held[k], sem.at[k])
-    if fetch:
-
-        @pl.when(at_ref[0] >= 0)
-        def _():
-            for copy in copies:
-                copy.start()
+        for copy in half_copies(fisher_ref, at_ref[0] ^ ORDER[piece], half, held[k], sem.at[k]):
+            copy.start()
+            copies.append(copy)
+
+    def product(h, start, step):
+        columns = pl.ds(h * halves[h].shape[0] + start, step)
+        term = times(chunk_ref, halves[h][pl.ds(start, step), :])
+        outs[0][:, columns] = term + base_ref[:, columns] if has_base else term
 
     for h, half_ref in enumerate(halves):
         rows = half_ref.shape[0]
-        columns = slice(h * rows, (h + 1) * rows)
-        term = times(chunk_ref, half_ref[...])
-        outs[0][:, columns] = term + base_ref[:, columns] if has_base else term
+        if fetch:
+
+            @pl.loop(0, 2)
+            def _(i):
+                product(h, pl.multiple_of(i * (rows // 2), rows // 2), rows // 2)
+        else:
+            product(h, 0, rows)
 
     for copy in copies:
         copy.wait()
@@ -101,7 +106,7 @@
         in_specs=[SMEM, HBM][: 2 * bool(fetch)] + [VMEM] * (len(ins) + has_base),
         out_specs=[VMEM] * len(out_shape),
         scratch_shapes=[pltpu.SemaphoreType.DMA((max(len(fetch), 1), 2))],
-        compiler_params=limit(34 if chunk is None else 20),
+        compiler_params=limit(24 if chunk is None else 20),
         cost_estimate=pl.CostEstimate(
             flops=0 if chunk is None else 2 * chunk.shape[0] * width * rows,
             bytes_accessed=width * rows * (len(fetch) + 2 * bool(ins)),
@@ -121,12 +126,17 @@
     other[...] = times(piece1, other_grads[:, :width]) + times(piece2, other_grads[:, width : 2 * width])
 
 
-def last_kernel(at_ref, piece3, swapped, mine_grads, other_grads, mine_base, other_base, mine, other, theirs):
+def last_kernel(at_ref, piece3, mine_grads, other_grads, mine_base, other_base, mine, other):
     width = piece3.shape[1]
-    start0, start3 = (pl.multiple_of((at_ref[0] ^ ORDER[k]) * width, width) for k in (0, 3))
+    start = pl.multiple_of((at_ref[0] ^ ORDER[3]) * width, width)
     other[...] = other_base[...] + times(piece3, other_grads[:, 2 * width :])
-    mine[...] = mine_base[...] + times(piece3, mine_grads[:, pl.ds(start3, width)])
-    theirs[...] = times(swapped, mine_grads[:, pl.ds(start0, width)])
+    mine[...] = mine_base[...] + times(piece3, mine_grads[:, pl.ds(start, width)])
+
+
+def first_kernel(at_ref, piece0, mine_grads, theirs):
+    width = piece0.shape[1]
+    start = pl.multiple_of((at_ref[0] ^ ORDER[0]) * width, width)
+    theirs[...] = times(piece0, mine_grads[:, pl.ds(start, width)])
 
 
 def score_call(kernel, n_out, examples, first, *operands):
@@ -168,7 +178,7 @@
         in_specs=[SMEM, HBM],
         out_specs=VMEM,
         scratch_shapes=[pltpu.SemaphoreType.DMA((n,))],
-        compiler_params=limit(51),
+        compiler_params=limit(50),
         cost_estimate=pl.CostEstimate(
             flops=0, bytes_accessed=2 * n * width * src.shape[0], transcendentals=0
         ),
@@ -266,10 +276,10 @@
     other_grads = swap_y(to_y)
     at, _ = lax.optimization_barrier((column, to_y))
     step = functools.partial(fisher_step, inverse_fisher, at, width)
-    a0, a1, b0, b1 = step(((0, 0), (0, 1), (1, 0), (1, 1)))
+    a0, a1, b0 = step(((0, 0), (0, 1), (1, 0)))
     q0, q1, q2, corner = gather(own, (a0,))
-    total, c0, c1 = step(((2, 0), (2, 1)), q0, (a0, a1))
-    total, d0 = step(((3, 0),), q1, (b0, b1), total)
+    total, b1, c0 = step(((1, 1), (2, 0)), q0, (a0, a1))
+    total, c1, d0 = step(((2, 1), (3, 0)), q1, (b0, b1), total)
     total, d1 = step(((3, 1),), q2, (c0, c1), total)
     (total,) = step((), corner(total), (d0, d1), total)
     panel = (total + swap_core(total)).astype(jnp.bfloat16)
@@ -277,9 +287,11 @@
     p0, p1, p2, corner = gather(panel)
     examples = stored_grads.shape[0]
     mine, other = score_call(base_kernel, 2, examples, column, p0, p1, p2, stored_grads, other_grads)
-    mine, other, theirs = score_call(
-        last_kernel, 3, examples, column, corner(mine), swap_y(p0), stored_grads, other_grads, mine, other
-    )
+    mine, other = score_call(
+        last_kernel, 2, examples, column, corner(mine), stored_grads, other_grads, mine, other
+    )
+    swapped, _ = lax.optimization_barrier((swap_y(p0), other))
+    (theirs,) = score_call(first_kernel, 1, examples, column, swapped, stored_grads)
 
     other = swap_y(other) + theirs
     keep = jnp.where(d == y, mine, other)

time: 62 us -> 60.9 us (0.982)
  Pallas kernels: 25.3 us -> 23.5 us
  starting transfers between devices: 19.7 us -> 18.4 us
  waiting for transfers between devices: 14.2 us -> 15.3 us
  local copies, waits for them, and re-layouts: 1.68 us -> 2.61 us
    pallas_call x5, Pallas kernels: 21.2 us -> 17.4 us  [fisher_step(): pl.pallas_call(functools.partial(fisher_kernel, len(ins), has_base, fetch...]
    pallas_call x2 -> x3, Pallas kernels: 1.7 us -> 4.65 us  [score_call(): pl.pallas_call(kernel, out_shape=[jax.ShapeDtypeStruct((rows, examples),...]
    unnamed x6 -> x8, local copies, waits for them, and re-layouts: 1.01 us -> 2.6 us
    ppermute x13, starting transfers between devices: 19.7 us -> 18.4 us  [move(): return lax.ppermute(value, AXES, pairs)]
    ppermute x13, waiting for transfers between devices: 14.2 us -> 15.3 us  [move(): return lax.ppermute(value, AXES, pairs)]
    pallas_call x4, Pallas kernels: 1.02 us -> 0.1 us  [pick(): pl.pallas_call(pick_kernel, out_shape=jax.ShapeDtypeStruct(a.shape, a.dty...]
    dynamic_slice x1, local copies, waits for them, and re-layouts: 0.67 us -> 0.01 us  [per_device_quad(): lax.dynamic_slice_in_dim(queries, y * rows, rows, axis=0)]
  transfers between devices with their start and end apart: 13 -> 13, of which waited for: 6 -> 7; matrix products, arithmetic and copies ran while one was open for 0% -> 0% of each run, Pallas kernels for 40% -> 39%
where the time goes in v13:
time: 60.9 us; the launch traced here: 60.6 us
  Pallas kernels  23.5 us (39%)
  starting transfers between devices  18.4 us (30%)
  waiting for transfers between devices  15.3 us (25%)
  local copies, waits for them, and re-layouts  2.61 us (4%)
  other arithmetic  0.67 us (1%)
    ppermute x13, starting transfers between devices, move(): return lax.ppermute(value, AXES, pairs)  18.4 us
    pallas_call x5, Pallas kernels, fisher_step(): pl.pallas_call(functools.partial(fisher_kernel, len(ins), has_base, fetch...  17.4 us
    ppermute x13, waiting for transfers between devices, move(): return lax.ppermute(value, AXES, pairs)  15.3 us
    pallas_call x3, Pallas kernels, score_call(): pl.pallas_call(kernel, out_shape=[jax.ShapeDtypeStruct((rows, examples),...  4.65 us
    unnamed x8, local copies, waits for them, and re-layouts  2.6 us
    pallas_call x1, Pallas kernels, cut(): pl.pallas_call(functools.partial(cut_kernel, order), out_shape=jax.ShapeD...  1.28 us
  transfers between devices with their start and end apart: 13, of which 7 were waited for; matrix products, arithmetic and copies ran while one was open for 0% of the time, Pallas kernels for 39%

profile of v13, /device:TPU:0, one launch (start us, length us, event | category | flops | bytes accessed | tf_op | source)
XLA Modules:
  0.0 60.6 jit_solution(13322945110115525605)
XLA Ops:
  0.0 1.0 %copy-done = bf16[96,2048]{1,0:T(8,128)(2,1)S(1)} copy-done((bf16[96,2048]{1,0:T(8,128)(2,1)S(1)}, bf16[96,2048]{1,0:T(8,128)(2,1)}, u32[]{:S(2)}) %copy-start) | copy-done | bytes 393240
  1.0 4.1 %collective-permute-start = (bf16[48,2048]{1,0:T(8,128)(2,1)S(1)}, bf16[48,2048]{1,0:T(8,128)(2,1)S(1)}, u32[]{:S(2)}, u32[]{:S(2)}) collective-permute-start(bf16[48,2048]{1,0:T(8,128)(2,1)S(1)} %constant_dynamic-slice_fusion.a_ref), channel_id=1, source_target_pairs={{0,8},{1,6},{2,10},{3,4},{4,12},{5,2},{6,14},{7,0},{8,15},{9,1},{1... | collective-permute-start | bytes 589832 | tf_op jit(solution)/shard_map/ppermute | solution.py:231
  5.1 1.6 %copy-done.2 = bf16[128,8192]{1,0:T(8,128)(2,1)S(1)} copy-done((bf16[128,8192]{1,0:T(8,128)(2,1)S(1)}, bf16[128,8192]{1,0:T(8,128)(2,1)}, u32[]{:S(2)}) %copy-start.2) | copy-done | bytes 2097176
  6.7 1.3 %shard_map.37 = bf16[128,6144]{1,0:T(8,128)(2,1)} custom-call(s32[1]{0:T(128)} %bitcast.at_ref, bf16[128,8192]{1,0:T(8,128)(2,1)S(1)} %copy-done.2), custom_call_target="tpu_custom_call" | custom-call | bytes 1572864 | tf_op jit(solution)/shard_map/pallas_call | solution.py:175
  8.0 1.6 %collective-permute-start.8 = (bf16[128,6144]{1,0:T(8,128)(2,1)}, bf16[128,6144]{1,0:T(8,128)(2,1)}, u32[]{:S(2)}, u32[]{:S(2)}) collective-permute-start(bf16[128,6144]{1,0:T(8,128)(2,1)} %shard_map.37), channel_id=1, source_target_pairs={{0,16},{1,17},{2,18},{3,19},{4,20},{5,21},{6,22},{7,23},{8,24},{9,... | collective-permute-start | bytes 4718600 | tf_op jit(solution)/shard_map/ppermute | solution.py:231
  9.6 4.7 %shard_map.38 = (bf16[1024,2048]{1,0:T(8,128)(2,1)S(1)}, bf16[1024,2048]{1,0:T(8,128)(2,1)S(1)}, bf16[1024,2048]{1,0:T(8,128)(2,1)S(1)}) custom-call(s32[1]{0:T(128)} %bitcast.2.refs_0_, bf16[2048,8192]{1,0:T(8,128)(2,1)} %refs_1_.7), custom_call_target="tpu_custom_call" | custom-call | bytes 12582912 | tf_op jit(solution)/shard_map/pallas_call | solution.py:103
  14.4 1.6 %collective-permute-start.2 = (bf16[48,2048]{1,0:T(8,128)(2,1)S(1)}, bf16[48,2048]{1,0:T(8,128)(2,1)S(1)}, u32[]{:S(2)}, u32[]{:S(2)}) collective-permute-start(bf16[48,2048]{1,0:T(8,128)(2,1)S(1)} %shard_map.39.refs_2_), channel_id=1, source_target_pairs={{0,4},{1,5},{2,6},{3,7},{4,0},{5,1},{6,2},{7,3},{8,12},{9,13},{10,... | collective-permute-start | bytes 589832 | tf_op jit(solution)/shard_map/ppermute | solution.py:231
  16.0 1.5 %collective-permute-start.1 = (bf16[48,2048]{1,0:T(8,128)(2,1)S(1)}, bf16[48,2048]{1,0:T(8,128)(2,1)S(1)}, u32[]{:S(2)}, u32[]{:S(2)}) collective-permute-start(bf16[48,2048]{1,0:T(8,128)(2,1)S(1)} %shard_map.39.refs_2_), channel_id=1, source_target_pairs={{0,2},{1,3},{2,0},{3,1},{4,6},{5,7},{6,4},{7,5},{8,10},{9,11},{10,... | collective-permute-start | bytes 589832 | tf_op jit(solution)/shard_map/ppermute | solution.py:231
  17.5 0.7 %collective-permute-start.3 = (bf16[48,2048]{1,0:T(8,128)(2,1)S(1)}, bf16[48,2048]{1,0:T(8,128)(2,1)S(1)}, u32[]{:S(2)}, u32[]{:S(2)}) collective-permute-start(bf16[48,2048]{1,0:T(8,128)(2,1)S(1)} %shard_map.39.refs_2_), channel_id=1, source_target_pairs={{1,7},{3,5},{5,3},{7,1},{8,14},{10,12},{12,10},{14,8},{17,23},{19,... | collective-permute-start | bytes 589832 | tf_op jit(solution)/shard_map/ppermute | solution.py:231
  18.2 3.5 %shard_map.40 = (f32[48,2048]{1,0:T(8,128)S(1)}, bf16[1024,2048]{1,0:T(8,128)(2,1)S(1)}, bf16[1024,2048]{1,0:T(8,128)(2,1)S(1)}) custom-call(s32[1]{0:T(128)} %bitcast.2.refs_0_, bf16[2048,8192]{1,0:T(8,128)(2,1)} %refs_1_.7, bf16[48,2048]{1,0:T(8,128)(2,1)S(1)} %shard_map.39.refs_2_, bf16[1024,2048]{1,0:T(8,128)(2,1)S(1)} %get-tuple-element.29.refs_0_.refs_3_, ...), custom_call_target="tpu_custom_call" | custom-call | flops 402653184 | bytes 16777216 | tf_op jit(solution)/shard_map/pallas_call | solution.py:103
  21.7 0.2 collective-permute-done.2.refs_2_
  21.9 3.5 %shard_map.41 = (f32[48,2048]{1,0:T(8,128)S(1)}, bf16[1024,2048]{1,0:T(8,128)(2,1)S(1)}, bf16[1024,2048]{1,0:T(8,128)(2,1)S(1)}) custom-call(s32[1]{0:T(128)} %bitcast.2.refs_0_, bf16[2048,8192]{1,0:T(8,128)(2,1)} %refs_1_.7, bf16[48,2048]{1,0:T(8,128)(2,1)S(1)} %collective-permute-done.2.refs_2_, bf16[1024,2048]{1,0:T(8,128)(2,1)S(1)} %get-tuple-element.32.refs_3_, ...), custom_call_target="tpu_custom_call" | custom-call | flops 402653184 | bytes 16777216 | tf_op jit(solution)/shard_map/pallas_call | solution.py:103
  25.4 3.0 %shard_map.42 = (f32[48,2048]{1,0:T(8,128)S(1)}, bf16[1024,2048]{1,0:T(8,128)(2,1)S(1)}) custom-call(s32[1]{0:T(128)} %bitcast.2.refs_0_, bf16[2048,8192]{1,0:T(8,128)(2,1)} %refs_1_.7, bf16[48,2048]{1,0:T(8,128)(2,1)S(1)} %collective-permute-done.1.refs_2_, bf16[1024,2048]{1,0:T(8,128)(2,1)S(1)} %get-tuple-element.31.refs_3_, ...), custom_call_target="tpu_custom_call" | custom-call | flops 402653184 | bytes 12582912 | tf_op jit(solution)/shard_map/pallas_call | solution.py:103
  28.5 0.0 copy-start.3
  28.5 2.6 %shard_map.44 = f32[48,2048]{1,0:T(8,128)S(1)} custom-call(bf16[48,2048]{1,0:T(8,128)(2,1)S(1)} %shard_map.43.refs_0_, bf16[1024,2048]{1,0:T(8,128)(2,1)S(1)} %get-tuple-element.39.refs_1_, bf16[1024,2048]{1,0:T(8,128)(2,1)S(1)} %get-tuple-element.40.refs_2_, f32[48,2048]{1,0:T(8,128)S(1)} %get-tuple-element.37.refs_3_), custom_call_target="tpu_custom_call" | custom-call | flops 402653184 | bytes 8388608 | tf_op jit(solution)/shard_map/pallas_call | solution.py:103
  31.2 0.4 collective-permute-start.4
  31.6 1.3 %collective-permute-done.4 = f32[48,2048]{1,0:T(8,128)S(1)} collective-permute-done((f32[48,2048]{1,0:T(8,128)S(1)}, f32[48,2048]{1,0:T(8,128)S(1)}, u32[]{:S(2)}, u32[]{:S(2)}) %collective-permute-start.4) | collective-permute-done | bytes 393248 | tf_op jit(solution)/shard_map/ppermute | solution.py:231
  33.0 3.5 %collective-permute-start.5 = (bf16[48,2048]{1,0:T(8,128)(2,1)S(1)}, bf16[48,2048]{1,0:T(8,128)(2,1)S(1)}, u32[]{:S(2)}, u32[]{:S(2)}) collective-permute-start(bf16[48,2048]{1,0:T(8,128)(2,1)S(1)} %add_convert_fusion.a_ref), channel_id=1, source_target_pairs={{0,8},{1,6},{2,10},{3,4},{4,12},{5,2},{6,14},{7,0},{8,15},{9,1},{1... | collective-permute-start | bytes 589832 | tf_op jit(solution)/shard_map/ppermute | solution.py:231
  36.5 3.2 %collective-permute-done.5.b_ref.a_ref = bf16[48,2048]{1,0:T(8,128)(2,1)S(1)} collective-permute-done((bf16[48,2048]{1,0:T(8,128)(2,1)S(1)}, bf16[48,2048]{1,0:T(8,128)(2,1)S(1)}, u32[]{:S(2)}, u32[]{:S(2)}) %collective-permute-start.5) | collective-permute-done | bytes 196640 | tf_op jit(solution)/shard_map/ppermute | solution.py:231
  39.7 2.6 %collective-permute-start.6 = (bf16[48,2048]{1,0:T(8,128)(2,1)S(1)}, bf16[48,2048]{1,0:T(8,128)(2,1)S(1)}, u32[]{:S(2)}, u32[]{:S(2)}) collective-permute-start(bf16[48,2048]{1,0:T(8,128)(2,1)S(1)} %shard_map.45.piece0), channel_id=1, source_target_pairs={{0,4},{1,5},{2,6},{3,7},{4,0},{5,1},{6,2},{7,3},{8,12},{9,13},{10,... | collective-permute-start | bytes 589832 | tf_op jit(solution)/shard_map/ppermute | solution.py:231
  42.4 0.7 %collective-permute-start.7 = (bf16[48,2048]{1,0:T(8,128)(2,1)S(1)}, bf16[48,2048]{1,0:T(8,128)(2,1)S(1)}, u32[]{:S(2)}, u32[]{:S(2)}) collective-permute-start(bf16[48,2048]{1,0:T(8,128)(2,1)S(1)} %shard_map.45.piece0), channel_id=1, source_target_pairs={{0,2},{1,3},{2,0},{3,1},{4,6},{5,7},{6,4},{7,5},{8,10},{9,11},{10,... | collective-permute-start | bytes 589832 | tf_op jit(solution)/shard_map/ppermute | solution.py:231
  43.1 0.7 %collective-permute-start.9 = (bf16[48,2048]{1,0:T(8,128)(2,1)S(1)}, bf16[48,2048]{1,0:T(8,128)(2,1)S(1)}, u32[]{:S(2)}, u32[]{:S(2)}) collective-permute-start(bf16[48,2048]{1,0:T(8,128)(2,1)S(1)} %shard_map.45.piece0), channel_id=1, source_target_pairs={{1,7},{3,5},{5,3},{7,1},{8,14},{10,12},{12,10},{14,8},{17,23},{19,... | collective-permute-start | bytes 589832 | tf_op jit(solution)/shard_map/ppermute | solution.py:231
  43.7 0.9 %collective-permute-start.11 = (bf16[48,2048]{1,0:T(8,128)(2,1)S(1)}, bf16[48,2048]{1,0:T(8,128)(2,1)S(1)}, u32[]{:S(2)}, u32[]{:S(2)}) collective-permute-start(bf16[48,2048]{1,0:T(8,128)(2,1)S(1)} %shard_map.45.piece0), channel_id=1, source_target_pairs={{0,16},{1,17},{2,18},{3,19},{4,20},{5,21},{6,22},{7,23},{8,24},{9,... | collective-permute-start | bytes 589832 | tf_op jit(solution)/shard_map/ppermute | solution.py:231
  44.7 3.3 %collective-permute-done.6.piece1 = bf16[48,2048]{1,0:T(8,128)(2,1)S(1)} collective-permute-done((bf16[48,2048]{1,0:T(8,128)(2,1)S(1)}, bf16[48,2048]{1,0:T(8,128)(2,1)S(1)}, u32[]{:S(2)}, u32[]{:S(2)}) %collective-permute-start.6) | collective-permute-done | bytes 196640 | tf_op jit(solution)/shard_map/ppermute | solution.py:231
  48.0 2.5 %collective-permute-done.7.piece2 = bf16[48,2048]{1,0:T(8,128)(2,1)S(1)} collective-permute-done((bf16[48,2048]{1,0:T(8,128)(2,1)S(1)}, bf16[48,2048]{1,0:T(8,128)(2,1)S(1)}, u32[]{:S(2)}, u32[]{:S(2)}) %collective-permute-start.7) | collective-permute-done | bytes 196640 | tf_op jit(solution)/shard_map/ppermute | solution.py:231
  50.5 2.5 %shard_map.46 = (f32[48,128]{1,0:T(8,128)S(1)}, f32[48,128]{1,0:T(8,128)S(1)}) custom-call(s32[1]{0:T(128)} %bitcast.at_ref, bf16[48,2048]{1,0:T(8,128)(2,1)S(1)} %shard_map.45.piece0, bf16[48,2048]{1,0:T(8,128)(2,1)S(1)} %collective-permute-done.6.piece1, bf16[48,2048]{1,0:T(8,128)(2,1)S(1)} %collective-permute-done.7.piece2, ...), custom_call_target="tpu_custom_call" | custom-call | flops 100663296 | bytes 2097152 | tf_op jit(solution)/shard_map/pallas_call | solution.py:144
  53.0 1.9 %shard_map.48 = (f32[48,128]{1,0:T(8,128)S(1)}, f32[48,128]{1,0:T(8,128)S(1)}) custom-call(s32[1]{0:T(128)} %bitcast.at_ref, bf16[48,2048]{1,0:T(8,128)(2,1)S(1)} %shard_map.47.piece3, bf16[128,8192]{1,0:T(8,128)(2,1)S(1)} %copy-done.3, bf16[128,6144]{1,0:T(8,128)(2,1)} %collective-permute-done.8.other_grads, f32[48,128]{1,0:T(8,128)S(1)} %get-tuple-element.41.mine_base, ...), custom_call_target="tpu_custom_call" | custom-call | flops 100663296 | bytes 2097152 | tf_op jit(solution)/shard_map/pallas_call | solution.py:144
  54.9 0.1 collective-permute-start.10
  55.0 0.3 shard_map.49
  55.3 3.5 %collective-permute-done.10 = f32[48,128]{1,0:T(8,128)S(1)} collective-permute-done((f32[48,128]{1,0:T(8,128)S(1)}, f32[48,128]{1,0:T(8,128)S(1)}, u32[]{:S(2)}, u32[]{:S(2)}) %collective-permute-start.10) | collective-permute-done | bytes 24608 | tf_op jit(solution)/shard_map/ppermute | solution.py:231
  58.8 1.2 %collective-permute-done.12 = f32[48,128]{1,0:T(8,128)S(1)} collective-permute-done((f32[48,128]{1,0:T(8,128)S(1)}, f32[48,128]{1,0:T(8,128)S(1)}, u32[]{:S(2)}, u32[]{:S(2)}) %collective-permute-start.12) | collective-permute-done | bytes 24608 | tf_op jit(solution)/shard_map/ppermute | solution.py:231
  60.0 0.6 %select_add_fusion = f32[48,128]{1,0:T(8,128)} fusion(f32[48,128]{1,0:T(8,128)S(1)} %collective-permute-done.12, f32[48,128]{1,0:T(8,128)S(1)} %get-tuple-element.44, pred[]{:T(512)S(6)} %eq.12, f32[48,128]{1,0:T(8,128)S(1)} %collective-permute-done.10, f32[48,128]{1,0:T(8,128)S(1)} %shard_map.49), kind=kLoop, calls=%fused_computation.1 | loop fusion | flops 18432 | bytes 122881 | tf_op jit(solution)/shard_map/add | solution.py:299
  (19 shorter events, 0.2 us)
Async XLA Ops:
  0.0 1.0 %copy-start = (bf16[96,2048]{1,0:T(8,128)(2,1)S(1)}, bf16[96,2048]{1,0:T(8,128)(2,1)}, u32[]{:S(2)}) copy-start(bf16[96,2048]{1,0:T(8,128)(2,1)} %param.3) | copy-start | bytes 1179652
  1.0 13.3 %collective-permute-start = (bf16[48,2048]{1,0:T(8,128)(2,1)S(1)}, bf16[48,2048]{1,0:T(8,128)(2,1)S(1)}, u32[]{:S(2)}, u32[]{:S(2)}) collective-permute-start(bf16[48,2048]{1,0:T(8,128)(2,1)S(1)} %constant_dynamic-slice_fusion.a_ref), channel_id=1, source_target_pairs={{0,8},{1,6},{2,10},{3,4},{4,12},{5,2},{6,14},{7,0},{8,15},{9,1},{1... | collective-permute-start | bytes 589832 | tf_op jit(solution)/shard_map/ppermute | solution.py:231
  5.1 1.6 %copy-start.2 = (bf16[128,8192]{1,0:T(8,128)(2,1)S(1)}, bf16[128,8192]{1,0:T(8,128)(2,1)}, u32[]{:S(2)}) copy-start(bf16[128,8192]{1,0:T(8,128)(2,1)} %mine_grads.5) | copy-start | bytes 6291460
  8.0 42.5 %collective-permute-start.8 = (bf16[128,6144]{1,0:T(8,128)(2,1)}, bf16[128,6144]{1,0:T(8,128)(2,1)}, u32[]{:S(2)}, u32[]{:S(2)}) collective-permute-start(bf16[128,6144]{1,0:T(8,128)(2,1)} %shard_map.37), channel_id=1, source_target_pairs={{0,16},{1,17},{2,18},{3,19},{4,20},{5,21},{6,22},{7,23},{8,24},{9,... | collective-permute-start | bytes 4718600 | tf_op jit(solution)/shard_map/ppermute | solution.py:231
  14.4 7.5 %collective-permute-start.2 = (bf16[48,2048]{1,0:T(8,128)(2,1)S(1)}, bf16[48,2048]{1,0:T(8,128)(2,1)S(1)}, u32[]{:S(2)}, u32[]{:S(2)}) collective-permute-start(bf16[48,2048]{1,0:T(8,128)(2,1)S(1)} %shard_map.39.refs_2_), channel_id=1, source_target_pairs={{0,4},{1,5},{2,6},{3,7},{4,0},{5,1},{6,2},{7,3},{8,12},{9,13},{10,... | collective-permute-start | bytes 589832 | tf_op jit(solution)/shard_map/ppermute | solution.py:231
  16.0 9.4 %collective-permute-start.1 = (bf16[48,2048]{1,0:T(8,128)(2,1)S(1)}, bf16[48,2048]{1,0:T(8,128)(2,1)S(1)}, u32[]{:S(2)}, u32[]{:S(2)}) collective-permute-start(bf16[48,2048]{1,0:T(8,128)(2,1)S(1)} %shard_map.39.refs_2_), channel_id=1, source_target_pairs={{0,2},{1,3},{2,0},{3,1},{4,6},{5,7},{6,4},{7,5},{8,10},{9,11},{10,... | collective-permute-start | bytes 589832 | tf_op jit(solution)/shard_map/ppermute | solution.py:231
  17.5 11.0 %collective-permute-start.3 = (bf16[48,2048]{1,0:T(8,128)(2,1)S(1)}, bf16[48,2048]{1,0:T(8,128)(2,1)S(1)}, u32[]{:S(2)}, u32[]{:S(2)}) collective-permute-start(bf16[48,2048]{1,0:T(8,128)(2,1)S(1)} %shard_map.39.refs_2_), channel_id=1, source_target_pairs={{1,7},{3,5},{5,3},{7,1},{8,14},{10,12},{12,10},{14,8},{17,23},{19,... | collective-permute-start | bytes 589832 | tf_op jit(solution)/shard_map/ppermute | solution.py:231
  28.5 22.0 %copy-start.3 = (bf16[128,8192]{1,0:T(8,128)(2,1)S(1)}, bf16[128,8192]{1,0:T(8,128)(2,1)}, u32[]{:S(2)}) copy-start(bf16[128,8192]{1,0:T(8,128)(2,1)} %mine_grads.5) | copy-start | bytes 6291460
  31.2 1.8 %collective-permute-start.4 = (f32[48,2048]{1,0:T(8,128)S(1)}, f32[48,2048]{1,0:T(8,128)S(1)}, u32[]{:S(2)}, u32[]{:S(2)}) collective-permute-start(f32[48,2048]{1,0:T(8,128)S(1)} %shard_map.44), channel_id=1, source_target_pairs={{0,1},{1,0},{2,3},{3,2},{4,5},{5,4},{6,7},{7,6},{8,9},{9,8},{10,11... | collective-permute-start | bytes 1179656 | tf_op jit(solution)/shard_map/ppermute | solution.py:231
  33.0 6.7 %collective-permute-start.5 = (bf16[48,2048]{1,0:T(8,128)(2,1)S(1)}, bf16[48,2048]{1,0:T(8,128)(2,1)S(1)}, u32[]{:S(2)}, u32[]{:S(2)}) collective-permute-start(bf16[48,2048]{1,0:T(8,128)(2,1)S(1)} %add_convert_fusion.a_ref), channel_id=1, source_target_pairs={{0,8},{1,6},{2,10},{3,4},{4,12},{5,2},{6,14},{7,0},{8,15},{9,1},{1... | collective-permute-start | bytes 589832 | tf_op jit(solution)/shard_map/ppermute | solution.py:231
  39.7 8.2 %collective-permute-start.6 = (bf16[48,2048]{1,0:T(8,128)(2,1)S(1)}, bf16[48,2048]{1,0:T(8,128)(2,1)S(1)}, u32[]{:S(2)}, u32[]{:S(2)}) collective-permute-start(bf16[48,2048]{1,0:T(8,128)(2,1)S(1)} %shard_map.45.piece0), channel_id=1, source_target_pairs={{0,4},{1,5},{2,6},{3,7},{4,0},{5,1},{6,2},{7,3},{8,12},{9,13},{10,... | collective-permute-start | bytes 589832 | tf_op jit(solution)/shard_map/ppermute | solution.py:231
  42.4 8.1 %collective-permute-start.7 = (bf16[48,2048]{1,0:T(8,128)(2,1)S(1)}, bf16[48,2048]{1,0:T(8,128)(2,1)S(1)}, u32[]{:S(2)}, u32[]{:S(2)}) collective-permute-start(bf16[48,2048]{1,0:T(8,128)(2,1)S(1)} %shard_map.45.piece0), channel_id=1, source_target_pairs={{0,2},{1,3},{2,0},{3,1},{4,6},{5,7},{6,4},{7,5},{8,10},{9,11},{10,... | collective-permute-start | bytes 589832 | tf_op jit(solution)/shard_map/ppermute | solution.py:231
  43.1 9.9 %collective-permute-start.9 = (bf16[48,2048]{1,0:T(8,128)(2,1)S(1)}, bf16[48,2048]{1,0:T(8,128)(2,1)S(1)}, u32[]{:S(2)}, u32[]{:S(2)}) collective-permute-start(bf16[48,2048]{1,0:T(8,128)(2,1)S(1)} %shard_map.45.piece0), channel_id=1, source_target_pairs={{1,7},{3,5},{5,3},{7,1},{8,14},{10,12},{12,10},{14,8},{17,23},{19,... | collective-permute-start | bytes 589832 | tf_op jit(solution)/shard_map/ppermute | solution.py:231
  43.7 11.3 %collective-permute-start.11 = (bf16[48,2048]{1,0:T(8,128)(2,1)S(1)}, bf16[48,2048]{1,0:T(8,128)(2,1)S(1)}, u32[]{:S(2)}, u32[]{:S(2)}) collective-permute-start(bf16[48,2048]{1,0:T(8,128)(2,1)S(1)} %shard_map.45.piece0), channel_id=1, source_target_pairs={{0,16},{1,17},{2,18},{3,19},{4,20},{5,21},{6,22},{7,23},{8,24},{9,... | collective-permute-start | bytes 589832 | tf_op jit(solution)/shard_map/ppermute | solution.py:231
  50.5 10.1 %copy-start.1 = (bf16[96,2048]{1,0:T(8,128)(2,1)S(1)}, bf16[96,2048]{1,0:T(8,128)(2,1)}, u32[]{:S(2)}) copy-start(bf16[96,2048]{1,0:T(8,128)(2,1)} %param.3) | copy-start | bytes 1179652
  54.9 3.9 %collective-permute-start.10 = (f32[48,128]{1,0:T(8,128)S(1)}, f32[48,128]{1,0:T(8,128)S(1)}, u32[]{:S(2)}, u32[]{:S(2)}) collective-permute-start(f32[48,128]{1,0:T(8,128)S(1)} %get-tuple-element.45), channel_id=1, source_target_pairs={{0,16},{1,17},{2,18},{3,19},{4,20},{5,21},{6,22},{7,23},{8,24},{9,... | collective-permute-start | bytes 73736 | tf_op jit(solution)/shard_map/ppermute | solution.py:231
  58.8 1.2 %collective-permute-start.12 = (f32[48,128]{1,0:T(8,128)S(1)}, f32[48,128]{1,0:T(8,128)S(1)}, u32[]{:S(2)}, u32[]{:S(2)}) collective-permute-start(f32[48,128]{1,0:T(8,128)S(1)} %broadcast_select_fusion), channel_id=1, source_target_pairs={{0,1},{1,0},{2,3},{3,2},{4,5},{5,4},{6,7},{7,6},{8,9},{9,8},{10,11... | collective-permute-start | bytes 73736 | tf_op jit(solution)/shard_map/ppermute | solution.py:231

commit v14 on v10

--- a/solution.py
+++ b/solution.py
@@ -40,7 +40,7 @@
 ORDER = (0, 2, 1, 3)
 
 
-def start_half(fisher_ref, block, half, held_ref, sem):
+def half_copies(fisher_ref, block, half, held_ref, sem):
     steps = sem.shape[0]
     rows, width = held_ref.shape
     step = rows // steps
@@ -54,7 +54,6 @@
                 sem.at[i],
             )
         )
-        copies[-1].start()
     return copies
 
 
@@ -62,7 +61,7 @@
     return lax.dot_general(chunk_ref[...], fisher, NT, preferred_element_type=jnp.float32)
 
 
-def fisher_kernel(n_in, has_base, fetch, step, *refs):
+def fisher_kernel(n_in, has_base, fetch, *refs):
     if fetch:
         at_ref, fisher_ref, *refs = refs
     chunk_ref, halves = (refs[0], refs[1:3]) if n_in else (None, ())
@@ -71,21 +70,30 @@
     held = outs[1:] if n_in else outs
     copies = []
     for k, (piece, half) in enumerate(fetch):
-        copies += start_half(fisher_ref, at_ref[0] ^ ORDER[piece], half, held[k], sem.at[k])
+        for copy in half_copies(fisher_ref, at_ref[0] ^ ORDER[piece], half, held[k], sem.at[k]):
+            copy.start()
+            copies.append(copy)
+
+    def product(h, start, step):
+        columns = pl.ds(h * halves[h].shape[0] + start, step)
+        term = times(chunk_ref, halves[h][pl.ds(start, step), :])
+        outs[0][:, columns] = term + base_ref[:, columns] if has_base else term
+
     for h, half_ref in enumerate(halves):
         rows = half_ref.shape[0]
-
-        @pl.loop(0, rows // step)
-        def _(i):
-            columns = pl.ds(pl.multiple_of(h * rows + i * step, step), step)
-            term = times(chunk_ref, half_ref[pl.ds(pl.multiple_of(i * step, step), step), :])
-            outs[0][:, columns] = term + base_ref[:, columns] if has_base else term
+        if fetch:
+
+            @pl.loop(0, 2)
+            def _(i):
+                product(h, pl.multiple_of(i * (rows // 2), rows // 2), rows // 2)
+        else:
+            product(h, 0, rows)
 
     for copy in copies:
         copy.wait()
 
 
-def fisher_step(fisher, first, width, fetch, chunk=None, halves=(), base=None, step=512):
+def fisher_step(fisher, first, width, fetch, chunk=None, halves=(), base=None):
     rows = fisher.shape[0]
     ins = [] if chunk is None else [chunk, *halves]
     has_base = base is not None
@@ -93,12 +101,12 @@
     out_shape = [] if chunk is None else [jax.ShapeDtypeStruct((chunk.shape[0], rows), jnp.float32)]
     out_shape += [held] * len(fetch)
     return pl.pallas_call(
-        functools.partial(fisher_kernel, len(ins), has_base, fetch, step),
+        functools.partial(fisher_kernel, len(ins), has_base, fetch),
         out_shape=out_shape,
         in_specs=[SMEM, HBM][: 2 * bool(fetch)] + [VMEM] * (len(ins) + has_base),
         out_specs=[VMEM] * len(out_shape),
         scratch_shapes=[pltpu.SemaphoreType.DMA((max(len(fetch), 1), 2))],
-        compiler_params=limit(34 if chunk is None else 20),
+        compiler_params=limit(24 if chunk is None else 20),
         cost_estimate=pl.CostEstimate(
             flops=0 if chunk is None else 2 * chunk.shape[0] * width * rows,
             bytes_accessed=width * rows * (len(fetch) + 2 * bool(ins)),
@@ -107,35 +115,34 @@
     )(*((scalar(first), fisher) if fetch else ()), *ins, *([base] if has_base else []))
 
 
-def score_kernel(order, n_grads, has_base, at_ref, *refs):
+def score_kernel(order, has_base, at_ref, *refs):
     n = len(order)
+    grads_ref, out_ref = refs[n], refs[-1]
     width = refs[0].shape[1]
-    for g in range(n_grads):
-        grads_ref, out_ref = refs[n + g], refs[-n_grads + g]
-        total = refs[n + n_grads + g][...] if has_base else None
-        for k in range(n):
-            start = pl.multiple_of((at_ref[0] ^ order[k]) * width, width)
-            term = times(refs[k], grads_ref[:, pl.ds(start, width)])
-            total = term if total is None else total + term
-        out_ref[...] = total
-
-
-def score_dot(pieces, order, first, grads, base=(), after=()):
+    total = refs[n + 1][...] if has_base else None
+    for k in range(n):
+        start = pl.multiple_of((at_ref[0] ^ order[k]) * width, width)
+        term = times(refs[k], grads_ref[:, pl.ds(start, width)])
+        total = term if total is None else total + term
+    out_ref[...] = total
+
+
+def score_dot(pieces, order, first, grads, base=None):
     n = len(pieces)
     rows, width = pieces[0].shape
-    operands = [*pieces, *grads, *base]
+    operands = [*pieces, grads] + ([] if base is None else [base])
     return pl.pallas_call(
-        functools.partial(score_kernel, order, len(grads), len(base) > 0),
-        out_shape=[jax.ShapeDtypeStruct((rows, g.shape[0]), jnp.float32) for g in grads],
-        in_specs=[SMEM] + [VMEM] * len(operands) + [ANY] * len(after),
-        out_specs=[VMEM] * len(grads),
+        functools.partial(score_kernel, order, base is not None),
+        out_shape=jax.ShapeDtypeStruct((rows, grads.shape[0]), jnp.float32),
+        in_specs=[SMEM] + [VMEM] * len(operands),
+        out_specs=VMEM,
         compiler_params=limit(8),
         cost_estimate=pl.CostEstimate(
-            flops=2 * n * rows * width * grads[0].shape[0] * len(grads),
-            bytes_accessed=2 * n * width * grads[0].shape[0] * len(grads),
+            flops=2 * n * rows * width * grads.shape[0],
+            bytes_accessed=2 * n * width * grads.shape[0],
             transcendentals=0,
         ),
-    )(scalar(first), *operands, *after)
+    )(scalar(first), *operands)
 
 
 def pick_kernel(at_ref, a_ref, b_ref, *refs):
@@ -212,7 +219,12 @@
         beside = along_z(first, pairs)
         across = along_z(first, {0: 0, 1: 1, 2: 2, 3: 3}, True)
         diagonal = along_z(first, {2: 3, 3: 2}, True)
-        return lambda *after: [first, beside, across, pick(owner, came, diagonal, after)]
+
+        def corner(after):
+            ready, _ = lax.optimization_barrier((came, after))
+            return pick(owner, ready, diagonal)
+
+        return first, beside, across, corner
 
     plane = jnp.where(d == 0, u % 2, nz - 1 - u % 2)
     column = plane * nx + x - d * (nex // 2)
@@ -222,19 +234,21 @@
     rows = nq // ny
     own = lax.optimization_barrier(lax.dynamic_slice_in_dim(queries, y * rows, rows, axis=0))
     step = functools.partial(fisher_step, inverse_fisher, column, own.shape[1])
-    a0, a1, b0, b1 = step(((0, 0), (0, 1), (1, 0), (1, 1)))
-    gathered = gather(own, (a0,))
-    q0, q1, q2, _ = gathered()
-    total, c0, c1 = step(((2, 0), (2, 1)), q0, (a0, a1))
+    a0, a1, b0, b1, c0 = step(((0, 0), (0, 1), (1, 0), (1, 1), (2, 0)))
+    q0, q1, q2, corner = gather(own, (a0,))
+    total, c1 = step(((2, 1),), q0, (a0, a1))
     total, d0 = step(((3, 0),), q1, (b0, b1), total)
     total, d1 = step(((3, 1),), q2, (c0, c1), total)
-    (total,) = step((), gathered(total)[3], (d0, d1), total)
+    (total,) = step((), corner(total), (d0, d1), total)
     panel = (total + swap_core(total)).astype(jnp.bfloat16)
 
-    grads = (other_grads, stored_grads)
-    gathered = gather(panel)
-    base = score_dot(gathered()[:3], ORDER[:3], column, grads)
-    other, mine = score_dot(gathered(base[0])[3:], ORDER[3:], column, grads, base)
+    p0, p1, p2, corner = gather(panel)
+    p3 = corner(panel)
+    mine = score_dot([p0, p1], ORDER[:2], column, stored_grads)
+    p2, _ = lax.optimization_barrier((p2, mine))
+    other = score_dot([p0, p1, p2, p3], ORDER, column, other_grads)
+    p2, p3, mine, _ = lax.optimization_barrier((p2, p3, mine, other))
+    mine = score_dot([p2, p3], ORDER[2:], column, stored_grads, mine)
 
     other = swap_y(other)
     keep = jnp.where(d == y, mine, other)

time: 56.8 us -> 57.9 us (1.019)
  starting transfers between devices: 20.2 us -> 16.5 us
  waiting for transfers between devices: 15 us -> 17.4 us
  Pallas kernels: 20.2 us -> 22.3 us
    ppermute x12, starting transfers between devices: 20.2 us -> 16.5 us  [move(): return lax.ppermute(value, AXES, pairs)]
    ppermute x12, waiting for transfers between devices: 15 us -> 17.4 us  [move(): return lax.ppermute(value, AXES, pairs)]
    pallas_call x2 -> x3, Pallas kernels: 1.64 us -> 3.36 us  [score_dot(): pl.pallas_call(functools.partial(score_kernel, order, base is not None),...]
where the time goes in v14:
time: 57.9 us; the launch traced here: 57.1 us
  Pallas kernels  22.3 us (39%)
  waiting for transfers between devices  17.4 us (30%)
  starting transfers between devices  16.5 us (28%)
  other arithmetic  0.67 us (1%)
    pallas_call x5, Pallas kernels, fisher_step(): pl.pallas_call(functools.partial(fisher_kernel, len(ins), has_base, fetch...  18.8 us
    ppermute x12, waiting for transfers between devices, move(): return lax.ppermute(value, AXES, pairs)  17.4 us
    ppermute x12, starting transfers between devices, move(): return lax.ppermute(value, AXES, pairs)  16.5 us
    pallas_call x3, Pallas kernels, score_dot(): pl.pallas_call(functools.partial(score_kernel, order, base is not None),...  3.36 us
  transfers between devices with their start and end apart: 12, of which 8 were waited for; matrix products, arithmetic and copies ran while one was open for 0% of the time, Pallas kernels for 35%

profile of v14, /device:TPU:0, one launch (start us, length us, event | category | flops | bytes accessed | tf_op | source)
XLA Modules:
  0.0 57.1 jit_solution(4411608657416729209)
XLA Ops:
  0.0 3.0 %collective-permute-start.9 = (bf16[128,8192]{1,0:T(8,128)(2,1)}, bf16[128,8192]{1,0:T(8,128)(2,1)}, u32[]{:S(2)}, u32[]{:S(2)}) collective-permute-start(bf16[128,8192]{1,0:T(8,128)(2,1)} %refs_2_.3), channel_id=1, source_target_pairs={{0,16},{1,17},{2,18},{3,19},{4,20},{5,21},{6,22},{7,23},{8,24},{9,... | collective-permute-start | bytes 6291464 | tf_op jit(solution)/shard_map/ppermute | solution.py:191
  3.0 2.7 %collective-permute-start = (bf16[48,2048]{1,0:T(8,128)(2,1)S(1)}, bf16[48,2048]{1,0:T(8,128)(2,1)S(1)}, u32[]{:S(2)}, u32[]{:S(2)}) collective-permute-start(bf16[48,2048]{1,0:T(8,128)(2,1)S(1)} %constant_dynamic-slice_fusion.a_ref), channel_id=1, source_target_pairs={{0,8},{1,6},{2,10},{3,4},{4,12},{5,2},{6,14},{7,0},{8,15},{9,1},{1... | collective-permute-start | bytes 589832 | tf_op jit(solution)/shard_map/ppermute | solution.py:191
  5.6 7.2 %shard_map.37 = (bf16[1024,2048]{1,0:T(8,128)(2,1)S(1)}, bf16[1024,2048]{1,0:T(8,128)(2,1)S(1)}, bf16[1024,2048]{1,0:T(8,128)(2,1)S(1)}, bf16[1024,2048]{1,0:T(8,128)(2,1)S(1)}, bf16[1024,2048]{1,0:T(8,128)(2,1)S(1)}) custom-call(s32[1]{0:T(128)} %bitcast.refs_0_.at_ref, bf16[2048,8192]{1,0:T(8,128)(2,1)} %refs_1_.7), custom_call_target="tpu_custom_call" | custom-call | bytes 20971520 | tf_op jit(solution)/shard_map/pallas_call | solution.py:103
  12.8 0.0 collective-permute-done.b_ref.a_ref
  12.9 1.6 %collective-permute-start.2 = (bf16[48,2048]{1,0:T(8,128)(2,1)S(1)}, bf16[48,2048]{1,0:T(8,128)(2,1)S(1)}, u32[]{:S(2)}, u32[]{:S(2)}) collective-permute-start(bf16[48,2048]{1,0:T(8,128)(2,1)S(1)} %shard_map.38.refs_2_), channel_id=1, source_target_pairs={{0,4},{1,5},{2,6},{3,7},{4,0},{5,1},{6,2},{7,3},{8,12},{9,13},{10,... | collective-permute-start | bytes 589832 | tf_op jit(solution)/shard_map/ppermute | solution.py:191
  14.5 1.5 %collective-permute-start.1 = (bf16[48,2048]{1,0:T(8,128)(2,1)S(1)}, bf16[48,2048]{1,0:T(8,128)(2,1)S(1)}, u32[]{:S(2)}, u32[]{:S(2)}) collective-permute-start(bf16[48,2048]{1,0:T(8,128)(2,1)S(1)} %shard_map.38.refs_2_), channel_id=1, source_target_pairs={{0,2},{1,3},{2,0},{3,1},{4,6},{5,7},{6,4},{7,5},{8,10},{9,11},{10,... | collective-permute-start | bytes 589832 | tf_op jit(solution)/shard_map/ppermute | solution.py:191
  16.0 0.7 %collective-permute-start.3 = (bf16[48,2048]{1,0:T(8,128)(2,1)S(1)}, bf16[48,2048]{1,0:T(8,128)(2,1)S(1)}, u32[]{:S(2)}, u32[]{:S(2)}) collective-permute-start(bf16[48,2048]{1,0:T(8,128)(2,1)S(1)} %shard_map.38.refs_2_), channel_id=1, source_target_pairs={{1,7},{3,5},{5,3},{7,1},{8,14},{10,12},{12,10},{14,8},{17,23},{19,... | collective-permute-start | bytes 589832 | tf_op jit(solution)/shard_map/ppermute | solution.py:191
  16.7 3.0 %shard_map.39 = (f32[48,2048]{1,0:T(8,128)S(1)}, bf16[1024,2048]{1,0:T(8,128)(2,1)S(1)}) custom-call(s32[1]{0:T(128)} %bitcast.refs_0_.at_ref, bf16[2048,8192]{1,0:T(8,128)(2,1)} %refs_1_.7, bf16[48,2048]{1,0:T(8,128)(2,1)S(1)} %shard_map.38.refs_2_, bf16[1024,2048]{1,0:T(8,128)(2,1)S(1)} %get-tuple-element.22.refs_0_.refs_3_, ...), custom_call_target="tpu_custom_call" | custom-call | flops 402653184 | bytes 12582912 | tf_op jit(solution)/shard_map/pallas_call | solution.py:103
  19.7 1.0 %collective-permute-done.2.refs_2_ = bf16[48,2048]{1,0:T(8,128)(2,1)S(1)} collective-permute-done((bf16[48,2048]{1,0:T(8,128)(2,1)S(1)}, bf16[48,2048]{1,0:T(8,128)(2,1)S(1)}, u32[]{:S(2)}, u32[]{:S(2)}) %collective-permute-start.2) | collective-permute-done | bytes 196640 | tf_op jit(solution)/shard_map/ppermute | solution.py:191
  20.7 3.0 %shard_map.40 = (f32[48,2048]{1,0:T(8,128)S(1)}, bf16[1024,2048]{1,0:T(8,128)(2,1)S(1)}) custom-call(s32[1]{0:T(128)} %bitcast.refs_0_.at_ref, bf16[2048,8192]{1,0:T(8,128)(2,1)} %refs_1_.7, bf16[48,2048]{1,0:T(8,128)(2,1)S(1)} %collective-permute-done.2.refs_2_, bf16[1024,2048]{1,0:T(8,128)(2,1)S(1)} %get-tuple-element.26.refs_3_, ...), custom_call_target="tpu_custom_call" | custom-call | flops 402653184 | bytes 12582912 | tf_op jit(solution)/shard_map/pallas_call | solution.py:103
  23.7 0.0 collective-permute-done.1.refs_2_
  23.7 3.0 %shard_map.41 = (f32[48,2048]{1,0:T(8,128)S(1)}, bf16[1024,2048]{1,0:T(8,128)(2,1)S(1)}) custom-call(s32[1]{0:T(128)} %bitcast.refs_0_.at_ref, bf16[2048,8192]{1,0:T(8,128)(2,1)} %refs_1_.7, bf16[48,2048]{1,0:T(8,128)(2,1)S(1)} %collective-permute-done.1.refs_2_, bf16[1024,2048]{1,0:T(8,128)(2,1)S(1)} %get-tuple-element.23.refs_3_, ...), custom_call_target="tpu_custom_call" | custom-call | flops 402653184 | bytes 12582912 | tf_op jit(solution)/shard_map/pallas_call | solution.py:103
  26.8 0.0 copy-start.2
  26.8 2.7 %shard_map.43 = f32[48,2048]{1,0:T(8,128)S(1)} custom-call(bf16[48,2048]{1,0:T(8,128)(2,1)S(1)} %shard_map.42.refs_0_, bf16[1024,2048]{1,0:T(8,128)(2,1)S(1)} %get-tuple-element.32.refs_1_, bf16[1024,2048]{1,0:T(8,128)(2,1)S(1)} %get-tuple-element.33.refs_2_, f32[48,2048]{1,0:T(8,128)S(1)} %get-tuple-element.30.refs_3_), custom_call_target="tpu_custom_call" | custom-call | flops 402653184 | bytes 8388608 | tf_op jit(solution)/shard_map/pallas_call | solution.py:103
  29.4 0.1 collective-permute-start.4
  29.5 1.7 %collective-permute-done.4 = f32[48,2048]{1,0:T(8,128)S(1)} collective-permute-done((f32[48,2048]{1,0:T(8,128)S(1)}, f32[48,2048]{1,0:T(8,128)S(1)}, u32[]{:S(2)}, u32[]{:S(2)}) %collective-permute-start.4) | collective-permute-done | bytes 393248 | tf_op jit(solution)/shard_map/ppermute | solution.py:191
  31.3 2.4 %collective-permute-start.5 = (bf16[48,2048]{1,0:T(8,128)(2,1)S(1)}, bf16[48,2048]{1,0:T(8,128)(2,1)S(1)}, u32[]{:S(2)}, u32[]{:S(2)}) collective-permute-start(bf16[48,2048]{1,0:T(8,128)(2,1)S(1)} %add_convert_fusion.a_ref), channel_id=1, source_target_pairs={{0,8},{1,6},{2,10},{3,4},{4,12},{5,2},{6,14},{7,0},{8,15},{9,1},{1... | collective-permute-start | bytes 589832 | tf_op jit(solution)/shard_map/ppermute | solution.py:191
  33.7 5.5 %collective-permute-done.5.b_ref.a_ref = bf16[48,2048]{1,0:T(8,128)(2,1)S(1)} collective-permute-done((bf16[48,2048]{1,0:T(8,128)(2,1)S(1)}, bf16[48,2048]{1,0:T(8,128)(2,1)S(1)}, u32[]{:S(2)}, u32[]{:S(2)}) %collective-permute-start.5) | collective-permute-done | bytes 196640 | tf_op jit(solution)/shard_map/ppermute | solution.py:191
  39.2 1.1 %collective-permute-start.7 = (bf16[48,2048]{1,0:T(8,128)(2,1)S(1)}, bf16[48,2048]{1,0:T(8,128)(2,1)S(1)}, u32[]{:S(2)}, u32[]{:S(2)}) collective-permute-start(bf16[48,2048]{1,0:T(8,128)(2,1)S(1)} %shard_map.44.refs_0_), channel_id=1, source_target_pairs={{0,4},{1,5},{2,6},{3,7},{4,0},{5,1},{6,2},{7,3},{8,12},{9,13},{10,... | collective-permute-start | bytes 589832 | tf_op jit(solution)/shard_map/ppermute | solution.py:191
  40.4 1.1 %collective-permute-start.6 = (bf16[48,2048]{1,0:T(8,128)(2,1)S(1)}, bf16[48,2048]{1,0:T(8,128)(2,1)S(1)}, u32[]{:S(2)}, u32[]{:S(2)}) collective-permute-start(bf16[48,2048]{1,0:T(8,128)(2,1)S(1)} %shard_map.44.refs_0_), channel_id=1, source_target_pairs={{0,2},{1,3},{2,0},{3,1},{4,6},{5,7},{6,4},{7,5},{8,10},{9,11},{10,... | collective-permute-start | bytes 589832 | tf_op jit(solution)/shard_map/ppermute | solution.py:191
  41.4 0.7 %collective-permute-start.8 = (bf16[48,2048]{1,0:T(8,128)(2,1)S(1)}, bf16[48,2048]{1,0:T(8,128)(2,1)S(1)}, u32[]{:S(2)}, u32[]{:S(2)}) collective-permute-start(bf16[48,2048]{1,0:T(8,128)(2,1)S(1)} %shard_map.44.refs_0_), channel_id=1, source_target_pairs={{1,7},{3,5},{5,3},{7,1},{8,14},{10,12},{12,10},{14,8},{17,23},{19,... | collective-permute-start | bytes 589832 | tf_op jit(solution)/shard_map/ppermute | solution.py:191
  42.1 5.0 %collective-permute-done.7.refs_1_ = bf16[48,2048]{1,0:T(8,128)(2,1)S(1)} collective-permute-done((bf16[48,2048]{1,0:T(8,128)(2,1)S(1)}, bf16[48,2048]{1,0:T(8,128)(2,1)S(1)}, u32[]{:S(2)}, u32[]{:S(2)}) %collective-permute-start.7) | collective-permute-done | bytes 196640 | tf_op jit(solution)/shard_map/ppermute | solution.py:191
  47.1 0.5 shard_map.45.refs_3_
  47.5 0.8 %collective-permute-done.6.refs_2_.refs_0_ = bf16[48,2048]{1,0:T(8,128)(2,1)S(1)} collective-permute-done((bf16[48,2048]{1,0:T(8,128)(2,1)S(1)}, bf16[48,2048]{1,0:T(8,128)(2,1)S(1)}, u32[]{:S(2)}, u32[]{:S(2)}) %collective-permute-start.6) | collective-permute-done | bytes 196640 | tf_op jit(solution)/shard_map/ppermute | solution.py:191
  48.4 0.0 collective-permute-done.8.b_ref
  48.4 0.5 collective-permute-done.9.refs_4_
  48.9 2.4 %shard_map.47 = f32[48,128]{1,0:T(8,128)S(1)} custom-call(s32[1]{0:T(128)} %bitcast.refs_0_.at_ref, bf16[48,2048]{1,0:T(8,128)(2,1)S(1)} %shard_map.44.refs_0_, bf16[48,2048]{1,0:T(8,128)(2,1)S(1)} %collective-permute-done.7.refs_1_, bf16[48,2048]{1,0:T(8,128)(2,1)S(1)} %collective-permute-done.6.refs_2_.refs_0_, ...), custom_call_target="tpu_custom_call" | custom-call | flops 100663296 | bytes 2097152 | tf_op jit(solution)/shard_map/pallas_call | solution.py:134
  51.3 1.8 %collective-permute-start.10 = (f32[48,128]{1,0:T(8,128)S(1)}, f32[48,128]{1,0:T(8,128)S(1)}, u32[]{:S(2)}, u32[]{:S(2)}) collective-permute-start(f32[48,128]{1,0:T(8,128)S(1)} %shard_map.47), channel_id=1, source_target_pairs={{0,16},{1,17},{2,18},{3,19},{4,20},{5,21},{6,22},{7,23},{8,24},{9,... | collective-permute-start | bytes 73736 | tf_op jit(solution)/shard_map/ppermute | solution.py:191
  53.2 0.5 shard_map.48
  53.6 1.6 %collective-permute-done.10 = f32[48,128]{1,0:T(8,128)S(1)} collective-permute-done((f32[48,128]{1,0:T(8,128)S(1)}, f32[48,128]{1,0:T(8,128)S(1)}, u32[]{:S(2)}, u32[]{:S(2)}) %collective-permute-start.10) | collective-permute-done | bytes 24608 | tf_op jit(solution)/shard_map/ppermute | solution.py:191
  55.3 1.2 %collective-permute-done.11 = f32[48,128]{1,0:T(8,128)S(1)} collective-permute-done((f32[48,128]{1,0:T(8,128)S(1)}, f32[48,128]{1,0:T(8,128)S(1)}, u32[]{:S(2)}, u32[]{:S(2)}) %collective-permute-start.11) | collective-permute-done | bytes 24608 | tf_op jit(solution)/shard_map/ppermute | solution.py:191
  56.4 0.6 %select_add_fusion = f32[48,128]{1,0:T(8,128)} fusion(f32[48,128]{1,0:T(8,128)S(1)} %collective-permute-done.11, f32[48,128]{1,0:T(8,128)S(1)} %shard_map.48, f32[48,128]{1,0:T(8,128)S(1)} %collective-permute-done.10, pred[]{:T(512)S(6)} %eq.12), kind=kLoop, calls=%fused_computation.1 | loop fusion | flops 12288 | bytes 98305 | tf_op jit(solution)/shard_map/add | solution.py:256
  (14 shorter events, 0.2 us)
Async XLA Ops:
  0.0 3.0 %copy-start = (bf16[96,2048]{1,0:T(8,128)(2,1)S(1)}, bf16[96,2048]{1,0:T(8,128)(2,1)}, u32[]{:S(2)}) copy-start(bf16[96,2048]{1,0:T(8,128)(2,1)} %param.3) | copy-start | bytes 1179652
  0.0 48.9 %collective-permute-start.9 = (bf16[128,8192]{1,0:T(8,128)(2,1)}, bf16[128,8192]{1,0:T(8,128)(2,1)}, u32[]{:S(2)}, u32[]{:S(2)}) collective-permute-start(bf16[128,8192]{1,0:T(8,128)(2,1)} %refs_2_.3), channel_id=1, source_target_pairs={{0,16},{1,17},{2,18},{3,19},{4,20},{5,21},{6,22},{7,23},{8,24},{9,... | collective-permute-start | bytes 6291464 | tf_op jit(solution)/shard_map/ppermute | solution.py:191
  3.0 9.8 %collective-permute-start = (bf16[48,2048]{1,0:T(8,128)(2,1)S(1)}, bf16[48,2048]{1,0:T(8,128)(2,1)S(1)}, u32[]{:S(2)}, u32[]{:S(2)}) collective-permute-start(bf16[48,2048]{1,0:T(8,128)(2,1)S(1)} %constant_dynamic-slice_fusion.a_ref), channel_id=1, source_target_pairs={{0,8},{1,6},{2,10},{3,4},{4,12},{5,2},{6,14},{7,0},{8,15},{9,1},{1... | collective-permute-start | bytes 589832 | tf_op jit(solution)/shard_map/ppermute | solution.py:191
  12.9 7.8 %collective-permute-start.2 = (bf16[48,2048]{1,0:T(8,128)(2,1)S(1)}, bf16[48,2048]{1,0:T(8,128)(2,1)S(1)}, u32[]{:S(2)}, u32[]{:S(2)}) collective-permute-start(bf16[48,2048]{1,0:T(8,128)(2,1)S(1)} %shard_map.38.refs_2_), channel_id=1, source_target_pairs={{0,4},{1,5},{2,6},{3,7},{4,0},{5,1},{6,2},{7,3},{8,12},{9,13},{10,... | collective-permute-start | bytes 589832 | tf_op jit(solution)/shard_map/ppermute | solution.py:191
  14.5 9.2 %collective-permute-start.1 = (bf16[48,2048]{1,0:T(8,128)(2,1)S(1)}, bf16[48,2048]{1,0:T(8,128)(2,1)S(1)}, u32[]{:S(2)}, u32[]{:S(2)}) collective-permute-start(bf16[48,2048]{1,0:T(8,128)(2,1)S(1)} %shard_map.38.refs_2_), channel_id=1, source_target_pairs={{0,2},{1,3},{2,0},{3,1},{4,6},{5,7},{6,4},{7,5},{8,10},{9,11},{10,... | collective-permute-start | bytes 589832 | tf_op jit(solution)/shard_map/ppermute | solution.py:191
  16.0 10.7 %collective-permute-start.3 = (bf16[48,2048]{1,0:T(8,128)(2,1)S(1)}, bf16[48,2048]{1,0:T(8,128)(2,1)S(1)}, u32[]{:S(2)}, u32[]{:S(2)}) collective-permute-start(bf16[48,2048]{1,0:T(8,128)(2,1)S(1)} %shard_map.38.refs_2_), channel_id=1, source_target_pairs={{1,7},{3,5},{5,3},{7,1},{8,14},{10,12},{12,10},{14,8},{17,23},{19,... | collective-permute-start | bytes 589832 | tf_op jit(solution)/shard_map/ppermute | solution.py:191
  26.8 20.3 %copy-start.2 = (bf16[128,8192]{1,0:T(8,128)(2,1)S(1)}, bf16[128,8192]{1,0:T(8,128)(2,1)}, u32[]{:S(2)}) copy-start(bf16[128,8192]{1,0:T(8,128)(2,1)} %refs_2_.3) | copy-start | bytes 6291460
  29.4 1.8 %collective-permute-start.4 = (f32[48,2048]{1,0:T(8,128)S(1)}, f32[48,2048]{1,0:T(8,128)S(1)}, u32[]{:S(2)}, u32[]{:S(2)}) collective-permute-start(f32[48,2048]{1,0:T(8,128)S(1)} %shard_map.43), channel_id=1, source_target_pairs={{0,1},{1,0},{2,3},{3,2},{4,5},{5,4},{6,7},{7,6},{8,9},{9,8},{10,11... | collective-permute-start | bytes 1179656 | tf_op jit(solution)/shard_map/ppermute | solution.py:191
  31.3 7.9 %collective-permute-start.5 = (bf16[48,2048]{1,0:T(8,128)(2,1)S(1)}, bf16[48,2048]{1,0:T(8,128)(2,1)S(1)}, u32[]{:S(2)}, u32[]{:S(2)}) collective-permute-start(bf16[48,2048]{1,0:T(8,128)(2,1)S(1)} %add_convert_fusion.a_ref), channel_id=1, source_target_pairs={{0,8},{1,6},{2,10},{3,4},{4,12},{5,2},{6,14},{7,0},{8,15},{9,1},{1... | collective-permute-start | bytes 589832 | tf_op jit(solution)/shard_map/ppermute | solution.py:191
  39.2 17.8 %copy-start.1 = (bf16[96,2048]{1,0:T(8,128)(2,1)S(1)}, bf16[96,2048]{1,0:T(8,128)(2,1)}, u32[]{:S(2)}) copy-start(bf16[96,2048]{1,0:T(8,128)(2,1)} %param.3) | copy-start | bytes 1179652
  39.2 7.8 %collective-permute-start.7 = (bf16[48,2048]{1,0:T(8,128)(2,1)S(1)}, bf16[48,2048]{1,0:T(8,128)(2,1)S(1)}, u32[]{:S(2)}, u32[]{:S(2)}) collective-permute-start(bf16[48,2048]{1,0:T(8,128)(2,1)S(1)} %shard_map.44.refs_0_), channel_id=1, source_target_pairs={{0,4},{1,5},{2,6},{3,7},{4,0},{5,1},{6,2},{7,3},{8,12},{9,13},{10,... | collective-permute-start | bytes 589832 | tf_op jit(solution)/shard_map/ppermute | solution.py:191
  40.4 8.0 %collective-permute-start.6 = (bf16[48,2048]{1,0:T(8,128)(2,1)S(1)}, bf16[48,2048]{1,0:T(8,128)(2,1)S(1)}, u32[]{:S(2)}, u32[]{:S(2)}) collective-permute-start(bf16[48,2048]{1,0:T(8,128)(2,1)S(1)} %shard_map.44.refs_0_), channel_id=1, source_target_pairs={{0,2},{1,3},{2,0},{3,1},{4,6},{5,7},{6,4},{7,5},{8,10},{9,11},{10,... | collective-permute-start | bytes 589832 | tf_op jit(solution)/shard_map/ppermute | solution.py:191
  41.4 7.0 %collective-permute-start.8 = (bf16[48,2048]{1,0:T(8,128)(2,1)S(1)}, bf16[48,2048]{1,0:T(8,128)(2,1)S(1)}, u32[]{:S(2)}, u32[]{:S(2)}) collective-permute-start(bf16[48,2048]{1,0:T(8,128)(2,1)S(1)} %shard_map.44.refs_0_), channel_id=1, source_target_pairs={{1,7},{3,5},{5,3},{7,1},{8,14},{10,12},{12,10},{14,8},{17,23},{19,... | collective-permute-start | bytes 589832 | tf_op jit(solution)/shard_map/ppermute | solution.py:191
  51.3 3.9 %collective-permute-start.10 = (f32[48,128]{1,0:T(8,128)S(1)}, f32[48,128]{1,0:T(8,128)S(1)}, u32[]{:S(2)}, u32[]{:S(2)}) collective-permute-start(f32[48,128]{1,0:T(8,128)S(1)} %shard_map.47), channel_id=1, source_target_pairs={{0,16},{1,17},{2,18},{3,19},{4,20},{5,21},{6,22},{7,23},{8,24},{9,... | collective-permute-start | bytes 73736 | tf_op jit(solution)/shard_map/ppermute | solution.py:191
  55.2 1.2 %collective-permute-start.11 = (f32[48,128]{1,0:T(8,128)S(1)}, f32[48,128]{1,0:T(8,128)S(1)}, u32[]{:S(2)}, u32[]{:S(2)}) collective-permute-start(f32[48,128]{1,0:T(8,128)S(1)} %broadcast_select_fusion), channel_id=1, source_target_pairs={{0,1},{1,0},{2,3},{3,2},{4,5},{5,4},{6,7},{7,6},{8,9},{9,8},{10,11... | collective-permute-start | bytes 73736 | tf_op jit(solution)/shard_map/ppermute | solution.py:191

commit v15 on v14

--- a/solution.py
+++ b/solution.py
@@ -106,7 +106,7 @@
         in_specs=[SMEM, HBM][: 2 * bool(fetch)] + [VMEM] * (len(ins) + has_base),
         out_specs=[VMEM] * len(out_shape),
         scratch_shapes=[pltpu.SemaphoreType.DMA((max(len(fetch), 1), 2))],
-        compiler_params=limit(24 if chunk is None else 20),
+        compiler_params=limit(34 if chunk is None else 20),
         cost_estimate=pl.CostEstimate(
             flops=0 if chunk is None else 2 * chunk.shape[0] * width * rows,
             bytes_accessed=width * rows * (len(fetch) + 2 * bool(ins)),
@@ -234,9 +234,9 @@
     rows = nq // ny
     own = lax.optimization_barrier(lax.dynamic_slice_in_dim(queries, y * rows, rows, axis=0))
     step = functools.partial(fisher_step, inverse_fisher, column, own.shape[1])
-    a0, a1, b0, b1, c0 = step(((0, 0), (0, 1), (1, 0), (1, 1), (2, 0)))
+    a0, a1, b0, b1 = step(((0, 0), (0, 1), (1, 0), (1, 1)))
     q0, q1, q2, corner = gather(own, (a0,))
-    total, c1 = step(((2, 1),), q0, (a0, a1))
+    total, c0, c1 = step(((2, 0), (2, 1)), q0, (a0, a1))
     total, d0 = step(((3, 0),), q1, (b0, b1), total)
     total, d1 = step(((3, 1),), q2, (c0, c1), total)
     (total,) = step((), corner(total), (d0, d1), total)

time: 57.9 us -> 58.4 us (level)
  the two profiles are of different devices: /device:TPU:0 before, /device:TPU:17 now
where the time goes in v15:
time: 58.4 us; the launch traced here: 58.2 us
  Pallas kernels  21.6 us (37%)
  starting transfers between devices  18.4 us (32%)
  waiting for transfers between devices  17.3 us (30%)
  other arithmetic  0.67 us (1%)
    ppermute x12, starting transfers between devices, move(): return lax.ppermute(value, AXES, pairs)  18.4 us
    pallas_call x5, Pallas kernels, fisher_step(): pl.pallas_call(functools.partial(fisher_kernel, len(ins), has_base, fetch...  18.1 us
    ppermute x12, waiting for transfers between devices, move(): return lax.ppermute(value, AXES, pairs)  17.3 us
    pallas_call x3, Pallas kernels, score_dot(): pl.pallas_call(functools.partial(score_kernel, order, base is not None),...  3.36 us
  transfers between devices with their start and end apart: 12, of which 8 were waited for; matrix products, arithmetic and copies ran while one was open for 0% of the time, Pallas kernels for 33%

profile of v15, /device:TPU:17, one launch (start us, length us, event | category | flops | bytes accessed | tf_op | source)
XLA Modules:
  0.0 58.2 jit_solution(3925829456660228037)
XLA Ops:
  0.0 1.2 %collective-permute-start.9 = (bf16[128,8192]{1,0:T(8,128)(2,1)}, bf16[128,8192]{1,0:T(8,128)(2,1)}, u32[]{:S(2)}, u32[]{:S(2)}) collective-permute-start(bf16[128,8192]{1,0:T(8,128)(2,1)} %refs_2_.3), channel_id=1, source_target_pairs={{0,16},{1,17},{2,18},{3,19},{4,20},{5,21},{6,22},{7,23},{8,24},{9,... | collective-permute-start | bytes 6291464 | tf_op jit(solution)/shard_map/ppermute | solution.py:191
  1.3 0.1 collective-permute-start
  1.4 6.0 %shard_map.37 = (bf16[1024,2048]{1,0:T(8,128)(2,1)S(1)}, bf16[1024,2048]{1,0:T(8,128)(2,1)S(1)}, bf16[1024,2048]{1,0:T(8,128)(2,1)S(1)}, bf16[1024,2048]{1,0:T(8,128)(2,1)S(1)}) custom-call(s32[1]{0:T(128)} %bitcast.refs_0_.at_ref, bf16[2048,8192]{1,0:T(8,128)(2,1)} %refs_1_.7), custom_call_target="tpu_custom_call" | custom-call | bytes 16777216 | tf_op jit(solution)/shard_map/pallas_call | solution.py:103
  7.3 1.8 %collective-permute-done.b_ref.a_ref = bf16[48,2048]{1,0:T(8,128)(2,1)S(1)} collective-permute-done((bf16[48,2048]{1,0:T(8,128)(2,1)S(1)}, bf16[48,2048]{1,0:T(8,128)(2,1)S(1)}, u32[]{:S(2)}, u32[]{:S(2)}) %collective-permute-start) | collective-permute-done | bytes 196640 | tf_op jit(solution)/shard_map/ppermute | solution.py:191
  9.1 0.2 collective-permute-start.2
  9.3 2.2 %collective-permute-start.1 = (bf16[48,2048]{1,0:T(8,128)(2,1)S(1)}, bf16[48,2048]{1,0:T(8,128)(2,1)S(1)}, u32[]{:S(2)}, u32[]{:S(2)}) collective-permute-start(bf16[48,2048]{1,0:T(8,128)(2,1)S(1)} %shard_map.38.refs_2_), channel_id=1, source_target_pairs={{0,2},{1,3},{2,0},{3,1},{4,6},{5,7},{6,4},{7,5},{8,10},{9,11},{10,... | collective-permute-start | bytes 589832 | tf_op jit(solution)/shard_map/ppermute | solution.py:191
  11.5 0.7 %collective-permute-start.3 = (bf16[48,2048]{1,0:T(8,128)(2,1)S(1)}, bf16[48,2048]{1,0:T(8,128)(2,1)S(1)}, u32[]{:S(2)}, u32[]{:S(2)}) collective-permute-start(bf16[48,2048]{1,0:T(8,128)(2,1)S(1)} %shard_map.38.refs_2_), channel_id=1, source_target_pairs={{1,7},{3,5},{5,3},{7,1},{8,14},{10,12},{12,10},{14,8},{17,23},{19,... | collective-permute-start | bytes 589832 | tf_op jit(solution)/shard_map/ppermute | solution.py:191
  12.2 3.5 %shard_map.39 = (f32[48,2048]{1,0:T(8,128)S(1)}, bf16[1024,2048]{1,0:T(8,128)(2,1)S(1)}, bf16[1024,2048]{1,0:T(8,128)(2,1)S(1)}) custom-call(s32[1]{0:T(128)} %bitcast.refs_0_.at_ref, bf16[2048,8192]{1,0:T(8,128)(2,1)} %refs_1_.7, bf16[48,2048]{1,0:T(8,128)(2,1)S(1)} %shard_map.38.refs_2_, bf16[1024,2048]{1,0:T(8,128)(2,1)S(1)} %get-tuple-element.22.refs_0_.refs_3_, ...), custom_call_target="tpu_custom_call" | custom-call | flops 402653184 | bytes 16777216 | tf_op jit(solution)/shard_map/pallas_call | solution.py:103
  15.7 3.0 %shard_map.40 = (f32[48,2048]{1,0:T(8,128)S(1)}, bf16[1024,2048]{1,0:T(8,128)(2,1)S(1)}) custom-call(s32[1]{0:T(128)} %bitcast.refs_0_.at_ref, bf16[2048,8192]{1,0:T(8,128)(2,1)} %refs_1_.7, bf16[48,2048]{1,0:T(8,128)(2,1)S(1)} %collective-permute-done.2.refs_2_, bf16[1024,2048]{1,0:T(8,128)(2,1)S(1)} %get-tuple-element.26.refs_3_, ...), custom_call_target="tpu_custom_call" | custom-call | flops 402653184 | bytes 12582912 | tf_op jit(solution)/shard_map/pallas_call | solution.py:103
  18.7 0.0 collective-permute-done.1.refs_2_
  18.7 3.0 %shard_map.41 = (f32[48,2048]{1,0:T(8,128)S(1)}, bf16[1024,2048]{1,0:T(8,128)(2,1)S(1)}) custom-call(s32[1]{0:T(128)} %bitcast.refs_0_.at_ref, bf16[2048,8192]{1,0:T(8,128)(2,1)} %refs_1_.7, bf16[48,2048]{1,0:T(8,128)(2,1)S(1)} %collective-permute-done.1.refs_2_, bf16[1024,2048]{1,0:T(8,128)(2,1)S(1)} %get-tuple-element.24.refs_3_, ...), custom_call_target="tpu_custom_call" | custom-call | flops 402653184 | bytes 12582912 | tf_op jit(solution)/shard_map/pallas_call | solution.py:103
  21.8 0.0 collective-permute-done.3.b_ref
  21.8 0.0 copy-start.2
  21.8 2.7 %shard_map.43 = f32[48,2048]{1,0:T(8,128)S(1)} custom-call(bf16[48,2048]{1,0:T(8,128)(2,1)S(1)} %shard_map.42.refs_0_, bf16[1024,2048]{1,0:T(8,128)(2,1)S(1)} %get-tuple-element.32.refs_1_, bf16[1024,2048]{1,0:T(8,128)(2,1)S(1)} %get-tuple-element.33.refs_2_, f32[48,2048]{1,0:T(8,128)S(1)} %get-tuple-element.30.refs_3_), custom_call_target="tpu_custom_call" | custom-call | flops 402653184 | bytes 8388608 | tf_op jit(solution)/shard_map/pallas_call | solution.py:103
  24.5 3.9 %collective-permute-start.4 = (f32[48,2048]{1,0:T(8,128)S(1)}, f32[48,2048]{1,0:T(8,128)S(1)}, u32[]{:S(2)}, u32[]{:S(2)}) collective-permute-start(f32[48,2048]{1,0:T(8,128)S(1)} %shard_map.43), channel_id=1, source_target_pairs={{0,1},{1,0},{2,3},{3,2},{4,5},{5,4},{6,7},{7,6},{8,9},{9,8},{10,11... | collective-permute-start | bytes 1179656 | tf_op jit(solution)/shard_map/ppermute | solution.py:191
  28.4 1.3 %collective-permute-done.4 = f32[48,2048]{1,0:T(8,128)S(1)} collective-permute-done((f32[48,2048]{1,0:T(8,128)S(1)}, f32[48,2048]{1,0:T(8,128)S(1)}, u32[]{:S(2)}, u32[]{:S(2)}) %collective-permute-start.4) | collective-permute-done | bytes 393248 | tf_op jit(solution)/shard_map/ppermute | solution.py:191
  29.8 0.1 collective-permute-start.5
  29.8 7.8 %collective-permute-done.5.b_ref.a_ref = bf16[48,2048]{1,0:T(8,128)(2,1)S(1)} collective-permute-done((bf16[48,2048]{1,0:T(8,128)(2,1)S(1)}, bf16[48,2048]{1,0:T(8,128)(2,1)S(1)}, u32[]{:S(2)}, u32[]{:S(2)}) %collective-permute-start.5) | collective-permute-done | bytes 196640 | tf_op jit(solution)/shard_map/ppermute | solution.py:191
  37.7 0.3 collective-permute-start.7
  37.9 3.1 %collective-permute-start.6 = (bf16[48,2048]{1,0:T(8,128)(2,1)S(1)}, bf16[48,2048]{1,0:T(8,128)(2,1)S(1)}, u32[]{:S(2)}, u32[]{:S(2)}) collective-permute-start(bf16[48,2048]{1,0:T(8,128)(2,1)S(1)} %shard_map.44.refs_0_), channel_id=1, source_target_pairs={{0,2},{1,3},{2,0},{3,1},{4,6},{5,7},{6,4},{7,5},{8,10},{9,11},{10,... | collective-permute-start | bytes 589832 | tf_op jit(solution)/shard_map/ppermute | solution.py:191
  41.0 0.7 %collective-permute-start.8 = (bf16[48,2048]{1,0:T(8,128)(2,1)S(1)}, bf16[48,2048]{1,0:T(8,128)(2,1)S(1)}, u32[]{:S(2)}, u32[]{:S(2)}) collective-permute-start(bf16[48,2048]{1,0:T(8,128)(2,1)S(1)} %shard_map.44.refs_0_), channel_id=1, source_target_pairs={{1,7},{3,5},{5,3},{7,1},{8,14},{10,12},{12,10},{14,8},{17,23},{19,... | collective-permute-start | bytes 589832 | tf_op jit(solution)/shard_map/ppermute | solution.py:191
  41.7 1.8 %collective-permute-done.7.refs_1_ = bf16[48,2048]{1,0:T(8,128)(2,1)S(1)} collective-permute-done((bf16[48,2048]{1,0:T(8,128)(2,1)S(1)}, bf16[48,2048]{1,0:T(8,128)(2,1)S(1)}, u32[]{:S(2)}, u32[]{:S(2)}) %collective-permute-start.7) | collective-permute-done | bytes 196640 | tf_op jit(solution)/shard_map/ppermute | solution.py:191
  43.5 0.5 shard_map.45.refs_3_
  44.0 1.1 %collective-permute-done.6.refs_2_.refs_0_ = bf16[48,2048]{1,0:T(8,128)(2,1)S(1)} collective-permute-done((bf16[48,2048]{1,0:T(8,128)(2,1)S(1)}, bf16[48,2048]{1,0:T(8,128)(2,1)S(1)}, u32[]{:S(2)}, u32[]{:S(2)}) %collective-permute-start.6) | collective-permute-done | bytes 196640 | tf_op jit(solution)/shard_map/ppermute | solution.py:191
  45.1 1.7 %collective-permute-done.9.refs_4_ = bf16[128,8192]{1,0:T(8,128)(2,1)} collective-permute-done((bf16[128,8192]{1,0:T(8,128)(2,1)}, bf16[128,8192]{1,0:T(8,128)(2,1)}, u32[]{:S(2)}, u32[]{:S(2)}) %collective-permute-start.9) | collective-permute-done | bytes 2097184 | tf_op jit(solution)/shard_map/ppermute | solution.py:191
  46.8 2.4 %shard_map.47 = f32[48,128]{1,0:T(8,128)S(1)} custom-call(s32[1]{0:T(128)} %bitcast.refs_0_.at_ref, bf16[48,2048]{1,0:T(8,128)(2,1)S(1)} %shard_map.44.refs_0_, bf16[48,2048]{1,0:T(8,128)(2,1)S(1)} %collective-permute-done.7.refs_1_, bf16[48,2048]{1,0:T(8,128)(2,1)S(1)} %collective-permute-done.6.refs_2_.refs_0_, ...), custom_call_target="tpu_custom_call" | custom-call | flops 100663296 | bytes 2097152 | tf_op jit(solution)/shard_map/pallas_call | solution.py:134
  49.3 1.3 %collective-permute-start.10 = (f32[48,128]{1,0:T(8,128)S(1)}, f32[48,128]{1,0:T(8,128)S(1)}, u32[]{:S(2)}, u32[]{:S(2)}) collective-permute-start(f32[48,128]{1,0:T(8,128)S(1)} %shard_map.47), channel_id=1, source_target_pairs={{0,16},{1,17},{2,18},{3,19},{4,20},{5,21},{6,22},{7,23},{8,24},{9,... | collective-permute-start | bytes 73736 | tf_op jit(solution)/shard_map/ppermute | solution.py:191
  50.6 0.5 shard_map.48
  51.0 1.0 %collective-permute-done.10 = f32[48,128]{1,0:T(8,128)S(1)} collective-permute-done((f32[48,128]{1,0:T(8,128)S(1)}, f32[48,128]{1,0:T(8,128)S(1)}, u32[]{:S(2)}, u32[]{:S(2)}) %collective-permute-start.10) | collective-permute-done | bytes 24608 | tf_op jit(solution)/shard_map/ppermute | solution.py:191
  52.0 4.8 %collective-permute-start.11 = (f32[48,128]{1,0:T(8,128)S(1)}, f32[48,128]{1,0:T(8,128)S(1)}, u32[]{:S(2)}, u32[]{:S(2)}) collective-permute-start(f32[48,128]{1,0:T(8,128)S(1)} %broadcast_select_fusion), channel_id=1, source_target_pairs={{0,1},{1,0},{2,3},{3,2},{4,5},{5,4},{6,7},{7,6},{8,9},{9,8},{10,11... | collective-permute-start | bytes 73736 | tf_op jit(solution)/shard_map/ppermute | solution.py:191
  56.8 0.8 %collective-permute-done.11 = f32[48,128]{1,0:T(8,128)S(1)} collective-permute-done((f32[48,128]{1,0:T(8,128)S(1)}, f32[48,128]{1,0:T(8,128)S(1)}, u32[]{:S(2)}, u32[]{:S(2)}) %collective-permute-start.11) | collective-permute-done | bytes 24608 | tf_op jit(solution)/shard_map/ppermute | solution.py:191
  57.6 0.6 %select_add_fusion = f32[48,128]{1,0:T(8,128)} fusion(f32[48,128]{1,0:T(8,128)S(1)} %collective-permute-done.11, f32[48,128]{1,0:T(8,128)S(1)} %shard_map.48, f32[48,128]{1,0:T(8,128)S(1)} %collective-permute-done.10, pred[]{:T(512)S(6)} %eq.12), kind=kLoop, calls=%fused_computation.1 | loop fusion | flops 12288 | bytes 98305 | tf_op jit(solution)/shard_map/add | solution.py:256
  (14 shorter events, 0.2 us)
Async XLA Ops:
  0.0 1.2 %copy-start = (bf16[96,2048]{1,0:T(8,128)(2,1)S(1)}, bf16[96,2048]{1,0:T(8,128)(2,1)}, u32[]{:S(2)}) copy-start(bf16[96,2048]{1,0:T(8,128)(2,1)} %param.3) | copy-start | bytes 1179652
  0.0 46.8 %collective-permute-start.9 = (bf16[128,8192]{1,0:T(8,128)(2,1)}, bf16[128,8192]{1,0:T(8,128)(2,1)}, u32[]{:S(2)}, u32[]{:S(2)}) collective-permute-start(bf16[128,8192]{1,0:T(8,128)(2,1)} %refs_2_.3), channel_id=1, source_target_pairs={{0,16},{1,17},{2,18},{3,19},{4,20},{5,21},{6,22},{7,23},{8,24},{9,... | collective-permute-start | bytes 6291464 | tf_op jit(solution)/shard_map/ppermute | solution.py:191
  1.3 7.8 %collective-permute-start = (bf16[48,2048]{1,0:T(8,128)(2,1)S(1)}, bf16[48,2048]{1,0:T(8,128)(2,1)S(1)}, u32[]{:S(2)}, u32[]{:S(2)}) collective-permute-start(bf16[48,2048]{1,0:T(8,128)(2,1)S(1)} %constant_dynamic-slice_fusion.a_ref), channel_id=1, source_target_pairs={{0,8},{1,6},{2,10},{3,4},{4,12},{5,2},{6,14},{7,0},{8,15},{9,1},{1... | collective-permute-start | bytes 589832 | tf_op jit(solution)/shard_map/ppermute | solution.py:191
  9.1 6.6 %collective-permute-start.2 = (bf16[48,2048]{1,0:T(8,128)(2,1)S(1)}, bf16[48,2048]{1,0:T(8,128)(2,1)S(1)}, u32[]{:S(2)}, u32[]{:S(2)}) collective-permute-start(bf16[48,2048]{1,0:T(8,128)(2,1)S(1)} %shard_map.38.refs_2_), channel_id=1, source_target_pairs={{0,4},{1,5},{2,6},{3,7},{4,0},{5,1},{6,2},{7,3},{8,12},{9,13},{10,... | collective-permute-start | bytes 589832 | tf_op jit(solution)/shard_map/ppermute | solution.py:191
  9.3 9.4 %collective-permute-start.1 = (bf16[48,2048]{1,0:T(8,128)(2,1)S(1)}, bf16[48,2048]{1,0:T(8,128)(2,1)S(1)}, u32[]{:S(2)}, u32[]{:S(2)}) collective-permute-start(bf16[48,2048]{1,0:T(8,128)(2,1)S(1)} %shard_map.38.refs_2_), channel_id=1, source_target_pairs={{0,2},{1,3},{2,0},{3,1},{4,6},{5,7},{6,4},{7,5},{8,10},{9,11},{10,... | collective-permute-start | bytes 589832 | tf_op jit(solution)/shard_map/ppermute | solution.py:191
  11.5 10.3 %collective-permute-start.3 = (bf16[48,2048]{1,0:T(8,128)(2,1)S(1)}, bf16[48,2048]{1,0:T(8,128)(2,1)S(1)}, u32[]{:S(2)}, u32[]{:S(2)}) collective-permute-start(bf16[48,2048]{1,0:T(8,128)(2,1)S(1)} %shard_map.38.refs_2_), channel_id=1, source_target_pairs={{1,7},{3,5},{5,3},{7,1},{8,14},{10,12},{12,10},{14,8},{17,23},{19,... | collective-permute-start | bytes 589832 | tf_op jit(solution)/shard_map/ppermute | solution.py:191
  21.8 21.7 %copy-start.2 = (bf16[128,8192]{1,0:T(8,128)(2,1)S(1)}, bf16[128,8192]{1,0:T(8,128)(2,1)}, u32[]{:S(2)}) copy-start(bf16[128,8192]{1,0:T(8,128)(2,1)} %refs_2_.3) | copy-start | bytes 6291460
  24.5 5.2 %collective-permute-start.4 = (f32[48,2048]{1,0:T(8,128)S(1)}, f32[48,2048]{1,0:T(8,128)S(1)}, u32[]{:S(2)}, u32[]{:S(2)}) collective-permute-start(f32[48,2048]{1,0:T(8,128)S(1)} %shard_map.43), channel_id=1, source_target_pairs={{0,1},{1,0},{2,3},{3,2},{4,5},{5,4},{6,7},{7,6},{8,9},{9,8},{10,11... | collective-permute-start | bytes 1179656 | tf_op jit(solution)/shard_map/ppermute | solution.py:191
  29.8 7.9 %collective-permute-start.5 = (bf16[48,2048]{1,0:T(8,128)(2,1)S(1)}, bf16[48,2048]{1,0:T(8,128)(2,1)S(1)}, u32[]{:S(2)}, u32[]{:S(2)}) collective-permute-start(bf16[48,2048]{1,0:T(8,128)(2,1)S(1)} %add_convert_fusion.a_ref), channel_id=1, source_target_pairs={{0,8},{1,6},{2,10},{3,4},{4,12},{5,2},{6,14},{7,0},{8,15},{9,1},{1... | collective-permute-start | bytes 589832 | tf_op jit(solution)/shard_map/ppermute | solution.py:191
  37.6 20.6 %copy-start.1 = (bf16[96,2048]{1,0:T(8,128)(2,1)S(1)}, bf16[96,2048]{1,0:T(8,128)(2,1)}, u32[]{:S(2)}) copy-start(bf16[96,2048]{1,0:T(8,128)(2,1)} %param.3) | copy-start | bytes 1179652
  37.7 5.8 %collective-permute-start.7 = (bf16[48,2048]{1,0:T(8,128)(2,1)S(1)}, bf16[48,2048]{1,0:T(8,128)(2,1)S(1)}, u32[]{:S(2)}, u32[]{:S(2)}) collective-permute-start(bf16[48,2048]{1,0:T(8,128)(2,1)S(1)} %shard_map.44.refs_0_), channel_id=1, source_target_pairs={{0,4},{1,5},{2,6},{3,7},{4,0},{5,1},{6,2},{7,3},{8,12},{9,13},{10,... | collective-permute-start | bytes 589832 | tf_op jit(solution)/shard_map/ppermute | solution.py:191
  37.9 7.1 %collective-permute-start.6 = (bf16[48,2048]{1,0:T(8,128)(2,1)S(1)}, bf16[48,2048]{1,0:T(8,128)(2,1)S(1)}, u32[]{:S(2)}, u32[]{:S(2)}) collective-permute-start(bf16[48,2048]{1,0:T(8,128)(2,1)S(1)} %shard_map.44.refs_0_), channel_id=1, source_target_pairs={{0,2},{1,3},{2,0},{3,1},{4,6},{5,7},{6,4},{7,5},{8,10},{9,11},{10,... | collective-permute-start | bytes 589832 | tf_op jit(solution)/shard_map/ppermute | solution.py:191
  41.0 4.1 %collective-permute-start.8 = (bf16[48,2048]{1,0:T(8,128)(2,1)S(1)}, bf16[48,2048]{1,0:T(8,128)(2,1)S(1)}, u32[]{:S(2)}, u32[]{:S(2)}) collective-permute-start(bf16[48,2048]{1,0:T(8,128)(2,1)S(1)} %shard_map.44.refs_0_), channel_id=1, source_target_pairs={{1,7},{3,5},{5,3},{7,1},{8,14},{10,12},{12,10},{14,8},{17,23},{19,... | collective-permute-start | bytes 589832 | tf_op jit(solution)/shard_map/ppermute | solution.py:191
  49.3 2.7 %collective-permute-start.10 = (f32[48,128]{1,0:T(8,128)S(1)}, f32[48,128]{1,0:T(8,128)S(1)}, u32[]{:S(2)}, u32[]{:S(2)}) collective-permute-start(f32[48,128]{1,0:T(8,128)S(1)} %shard_map.47), channel_id=1, source_target_pairs={{0,16},{1,17},{2,18},{3,19},{4,20},{5,21},{6,22},{7,23},{8,24},{9,... | collective-permute-start | bytes 73736 | tf_op jit(solution)/shard_map/ppermute | solution.py:191
  52.0 5.6 %collective-permute-start.11 = (f32[48,128]{1,0:T(8,128)S(1)}, f32[48,128]{1,0:T(8,128)S(1)}, u32[]{:S(2)}, u32[]{:S(2)}) collective-permute-start(f32[48,128]{1,0:T(8,128)S(1)} %broadcast_select_fusion), channel_id=1, source_target_pairs={{0,1},{1,0},{2,3},{3,2},{4,5},{5,4},{6,7},{7,6},{8,9},{9,8},{10,11... | collective-permute-start | bytes 73736 | tf_op jit(solution)/shard_map/ppermute | solution.py:191

commit v16 on v15

--- a/solution.py
+++ b/solution.py
@@ -246,7 +246,9 @@
     p3 = corner(panel)
     mine = score_dot([p0, p1], ORDER[:2], column, stored_grads)
     p2, _ = lax.optimization_barrier((p2, mine))
-    other = score_dot([p0, p1, p2, p3], ORDER, column, other_grads)
+    other = score_dot([p0, p1, p2], ORDER[:3], column, other_grads)
+    p3, _ = lax.optimization_barrier((p3, other))
+    other = score_dot([p3], ORDER[3:], column, other_grads, other)
     p2, p3, mine, _ = lax.optimization_barrier((p2, p3, mine, other))
     mine = score_dot([p2, p3], ORDER[2:], column, stored_grads, mine)
 

time: 58.4 us -> 56.9 us (0.974)
  local copies, waits for them, and re-layouts: 0.03 us -> 1.62 us
  Pallas kernels: 21.6 us -> 20.1 us
  waiting for transfers between devices: 17.3 us -> 16.3 us
    unnamed x6 -> x8, local copies, waits for them, and re-layouts: 0.01 us -> 1.6 us
    pallas_call x3 -> x4, Pallas kernels: 3.36 us -> 1.89 us  [score_dot(): pl.pallas_call(functools.partial(score_kernel, order, base is not None),...]
    ppermute x12, waiting for transfers between devices: 17.3 us -> 16.3 us  [move(): return lax.ppermute(value, AXES, pairs)]
  transfers between devices with their start and end apart: 12 -> 12, of which waited for: 8 -> 7; matrix products, arithmetic and copies ran while one was open for 0% -> 0% of each run, Pallas kernels for 33% -> 34%
where the time goes in v16:
time: 56.9 us; the launch traced here: 56.8 us
  Pallas kernels  20.1 us (35%)
  starting transfers between devices  17.9 us (31%)
  waiting for transfers between devices  16.3 us (29%)
  local copies, waits for them, and re-layouts  1.62 us (3%)
  other arithmetic  0.67 us (1%)
    pallas_call x5, Pallas kernels, fisher_step(): pl.pallas_call(functools.partial(fisher_kernel, len(ins), has_base, fetch...  18.2 us
    ppermute x12, starting transfers between devices, move(): return lax.ppermute(value, AXES, pairs)  17.9 us
    ppermute x12, waiting for transfers between devices, move(): return lax.ppermute(value, AXES, pairs)  16.3 us
    pallas_call x4, Pallas kernels, score_dot(): pl.pallas_call(functools.partial(score_kernel, order, base is not None),...  1.89 us
    unnamed x8, local copies, waits for them, and re-layouts  1.6 us
  transfers between devices with their start and end apart: 12, of which 7 were waited for; matrix products, arithmetic and copies ran while one was open for 0% of the time, Pallas kernels for 34%

profile of v16, /device:TPU:17, one launch (start us, length us, event | category | flops | bytes accessed | tf_op | source)
XLA Modules:
  0.0 56.8 jit_solution(8434882710011638374)
XLA Ops:
  0.0 1.2 %collective-permute-start.9 = (bf16[128,8192]{1,0:T(8,128)(2,1)}, bf16[128,8192]{1,0:T(8,128)(2,1)S(1)}, u32[]{:S(2)}, u32[]{:S(2)}) collective-permute-start(bf16[128,8192]{1,0:T(8,128)(2,1)} %refs_2_.3), channel_id=1, source_target_pairs={{0,16},{1,17},{2,18},{3,19},{4,20},{5,21},{6,22},{7,23},{8,24},{9,... | collective-permute-start | bytes 6291464 | tf_op jit(solution)/shard_map/ppermute | solution.py:191
  1.3 0.1 collective-permute-start
  1.4 6.0 %shard_map.37 = (bf16[1024,2048]{1,0:T(8,128)(2,1)S(1)}, bf16[1024,2048]{1,0:T(8,128)(2,1)S(1)}, bf16[1024,2048]{1,0:T(8,128)(2,1)S(1)}, bf16[1024,2048]{1,0:T(8,128)(2,1)S(1)}) custom-call(s32[1]{0:T(128)} %bitcast.refs_0_.at_ref, bf16[2048,8192]{1,0:T(8,128)(2,1)} %refs_1_.7), custom_call_target="tpu_custom_call" | custom-call | bytes 16777216 | tf_op jit(solution)/shard_map/pallas_call | solution.py:103
  7.3 1.8 %collective-permute-done.b_ref.a_ref = bf16[48,2048]{1,0:T(8,128)(2,1)S(1)} collective-permute-done((bf16[48,2048]{1,0:T(8,128)(2,1)S(1)}, bf16[48,2048]{1,0:T(8,128)(2,1)S(1)}, u32[]{:S(2)}, u32[]{:S(2)}) %collective-permute-start) | collective-permute-done | bytes 196640 | tf_op jit(solution)/shard_map/ppermute | solution.py:191
  9.1 0.2 collective-permute-start.2
  9.3 2.2 %collective-permute-start.1 = (bf16[48,2048]{1,0:T(8,128)(2,1)S(1)}, bf16[48,2048]{1,0:T(8,128)(2,1)S(1)}, u32[]{:S(2)}, u32[]{:S(2)}) collective-permute-start(bf16[48,2048]{1,0:T(8,128)(2,1)S(1)} %shard_map.38.refs_2_), channel_id=1, source_target_pairs={{0,2},{1,3},{2,0},{3,1},{4,6},{5,7},{6,4},{7,5},{8,10},{9,11},{10,... | collective-permute-start | bytes 589832 | tf_op jit(solution)/shard_map/ppermute | solution.py:191
  11.5 0.7 %collective-permute-start.3 = (bf16[48,2048]{1,0:T(8,128)(2,1)S(1)}, bf16[48,2048]{1,0:T(8,128)(2,1)S(1)}, u32[]{:S(2)}, u32[]{:S(2)}) collective-permute-start(bf16[48,2048]{1,0:T(8,128)(2,1)S(1)} %shard_map.38.refs_2_), channel_id=1, source_target_pairs={{1,7},{3,5},{5,3},{7,1},{8,14},{10,12},{12,10},{14,8},{17,23},{19,... | collective-permute-start | bytes 589832 | tf_op jit(solution)/shard_map/ppermute | solution.py:191
  12.2 3.5 %shard_map.39 = (f32[48,2048]{1,0:T(8,128)S(1)}, bf16[1024,2048]{1,0:T(8,128)(2,1)S(1)}, bf16[1024,2048]{1,0:T(8,128)(2,1)S(1)}) custom-call(s32[1]{0:T(128)} %bitcast.refs_0_.at_ref, bf16[2048,8192]{1,0:T(8,128)(2,1)} %refs_1_.7, bf16[48,2048]{1,0:T(8,128)(2,1)S(1)} %shard_map.38.refs_2_, bf16[1024,2048]{1,0:T(8,128)(2,1)S(1)} %get-tuple-element.23.refs_0_.refs_3_, ...), custom_call_target="tpu_custom_call" | custom-call | flops 402653184 | bytes 16777216 | tf_op jit(solution)/shard_map/pallas_call | solution.py:103
  15.7 3.0 %shard_map.40 = (f32[48,2048]{1,0:T(8,128)S(1)}, bf16[1024,2048]{1,0:T(8,128)(2,1)S(1)}) custom-call(s32[1]{0:T(128)} %bitcast.refs_0_.at_ref, bf16[2048,8192]{1,0:T(8,128)(2,1)} %refs_1_.7, bf16[48,2048]{1,0:T(8,128)(2,1)S(1)} %collective-permute-done.2.refs_2_, bf16[1024,2048]{1,0:T(8,128)(2,1)S(1)} %get-tuple-element.27.refs_3_, ...), custom_call_target="tpu_custom_call" | custom-call | flops 402653184 | bytes 12582912 | tf_op jit(solution)/shard_map/pallas_call | solution.py:103
  18.7 0.0 collective-permute-done.1.refs_2_
  18.7 3.0 %shard_map.41 = (f32[48,2048]{1,0:T(8,128)S(1)}, bf16[1024,2048]{1,0:T(8,128)(2,1)S(1)}) custom-call(s32[1]{0:T(128)} %bitcast.refs_0_.at_ref, bf16[2048,8192]{1,0:T(8,128)(2,1)} %refs_1_.7, bf16[48,2048]{1,0:T(8,128)(2,1)S(1)} %collective-permute-done.1.refs_2_, bf16[1024,2048]{1,0:T(8,128)(2,1)S(1)} %get-tuple-element.25.refs_3_, ...), custom_call_target="tpu_custom_call" | custom-call | flops 402653184 | bytes 12582912 | tf_op jit(solution)/shard_map/pallas_call | solution.py:103
  21.8 0.0 copy-start.2
  21.8 2.6 %shard_map.43 = f32[48,2048]{1,0:T(8,128)S(1)} custom-call(bf16[48,2048]{1,0:T(8,128)(2,1)S(1)} %shard_map.42.refs_0_, bf16[1024,2048]{1,0:T(8,128)(2,1)S(1)} %get-tuple-element.33.refs_1_, bf16[1024,2048]{1,0:T(8,128)(2,1)S(1)} %get-tuple-element.34.refs_2_, f32[48,2048]{1,0:T(8,128)S(1)} %get-tuple-element.31.refs_3_), custom_call_target="tpu_custom_call" | custom-call | flops 402653184 | bytes 8388608 | tf_op jit(solution)/shard_map/pallas_call | solution.py:103
  24.5 3.9 %collective-permute-start.4 = (f32[48,2048]{1,0:T(8,128)S(1)}, f32[48,2048]{1,0:T(8,128)S(1)}, u32[]{:S(2)}, u32[]{:S(2)}) collective-permute-start(f32[48,2048]{1,0:T(8,128)S(1)} %shard_map.43), channel_id=1, source_target_pairs={{0,1},{1,0},{2,3},{3,2},{4,5},{5,4},{6,7},{7,6},{8,9},{9,8},{10,11... | collective-permute-start | bytes 1179656 | tf_op jit(solution)/shard_map/ppermute | solution.py:191
  28.4 1.3 %collective-permute-done.4 = f32[48,2048]{1,0:T(8,128)S(1)} collective-permute-done((f32[48,2048]{1,0:T(8,128)S(1)}, f32[48,2048]{1,0:T(8,128)S(1)}, u32[]{:S(2)}, u32[]{:S(2)}) %collective-permute-start.4) | collective-permute-done | bytes 393248 | tf_op jit(solution)/shard_map/ppermute | solution.py:191
  29.8 0.1 collective-permute-start.5
  29.8 7.8 %collective-permute-done.5.b_ref.a_ref = bf16[48,2048]{1,0:T(8,128)(2,1)S(1)} collective-permute-done((bf16[48,2048]{1,0:T(8,128)(2,1)S(1)}, bf16[48,2048]{1,0:T(8,128)(2,1)S(1)}, u32[]{:S(2)}, u32[]{:S(2)}) %collective-permute-start.5) | collective-permute-done | bytes 196640 | tf_op jit(solution)/shard_map/ppermute | solution.py:191
  37.7 0.3 collective-permute-start.7
  38.0 3.1 %collective-permute-start.6 = (bf16[48,2048]{1,0:T(8,128)(2,1)S(1)}, bf16[48,2048]{1,0:T(8,128)(2,1)S(1)}, u32[]{:S(2)}, u32[]{:S(2)}) collective-permute-start(bf16[48,2048]{1,0:T(8,128)(2,1)S(1)} %shard_map.44.refs_0_), channel_id=1, source_target_pairs={{0,2},{1,3},{2,0},{3,1},{4,6},{5,7},{6,4},{7,5},{8,10},{9,11},{10,... | collective-permute-start | bytes 589832 | tf_op jit(solution)/shard_map/ppermute | solution.py:191
  41.0 0.7 %collective-permute-start.8 = (bf16[48,2048]{1,0:T(8,128)(2,1)S(1)}, bf16[48,2048]{1,0:T(8,128)(2,1)S(1)}, u32[]{:S(2)}, u32[]{:S(2)}) collective-permute-start(bf16[48,2048]{1,0:T(8,128)(2,1)S(1)} %shard_map.44.refs_0_), channel_id=1, source_target_pairs={{1,7},{3,5},{5,3},{7,1},{8,14},{10,12},{12,10},{14,8},{17,23},{19,... | collective-permute-start | bytes 589832 | tf_op jit(solution)/shard_map/ppermute | solution.py:191
  41.7 1.7 %collective-permute-done.7.refs_1_ = bf16[48,2048]{1,0:T(8,128)(2,1)S(1)} collective-permute-done((bf16[48,2048]{1,0:T(8,128)(2,1)S(1)}, bf16[48,2048]{1,0:T(8,128)(2,1)S(1)}, u32[]{:S(2)}, u32[]{:S(2)}) %collective-permute-start.7) | collective-permute-done | bytes 196640 | tf_op jit(solution)/shard_map/ppermute | solution.py:191
  43.4 0.5 shard_map.45.refs_3_
  43.9 1.1 %collective-permute-done.6.refs_2_.refs_0_ = bf16[48,2048]{1,0:T(8,128)(2,1)S(1)} collective-permute-done((bf16[48,2048]{1,0:T(8,128)(2,1)S(1)}, bf16[48,2048]{1,0:T(8,128)(2,1)S(1)}, u32[]{:S(2)}, u32[]{:S(2)}) %collective-permute-start.6) | collective-permute-done | bytes 196640 | tf_op jit(solution)/shard_map/ppermute | solution.py:191
  45.0 1.7 %collective-permute-done.9.refs_3_.refs_1_ = bf16[128,8192]{1,0:T(8,128)(2,1)S(1)} collective-permute-done((bf16[128,8192]{1,0:T(8,128)(2,1)}, bf16[128,8192]{1,0:T(8,128)(2,1)S(1)}, u32[]{:S(2)}, u32[]{:S(2)}) %collective-permute-start.9) | collective-permute-done | bytes 2097184 | tf_op jit(solution)/shard_map/ppermute | solution.py:191
  46.7 0.7 %shard_map.47.refs_2_ = f32[48,128]{1,0:T(8,128)S(1)} custom-call(s32[1]{0:T(128)} %bitcast.refs_0_.at_ref, bf16[48,2048]{1,0:T(8,128)(2,1)S(1)} %shard_map.44.refs_0_, bf16[48,2048]{1,0:T(8,128)(2,1)S(1)} %collective-permute-done.7.refs_1_, bf16[48,2048]{1,0:T(8,128)(2,1)S(1)} %collective-permute-done.6.refs_2_.refs_0_, ...), custom_call_target="tpu_custom_call" | custom-call | flops 75497472 | bytes 1572864 | tf_op jit(solution)/shard_map/pallas_call | solution.py:134
  47.4 0.3 shard_map.48
  47.7 1.3 %collective-permute-start.10 = (f32[48,128]{1,0:T(8,128)S(1)}, f32[48,128]{1,0:T(8,128)S(1)}, u32[]{:S(2)}, u32[]{:S(2)}) collective-permute-start(f32[48,128]{1,0:T(8,128)S(1)} %shard_map.48), channel_id=1, source_target_pairs={{0,16},{1,17},{2,18},{3,19},{4,20},{5,21},{6,22},{7,23},{8,24},{9,... | collective-permute-start | bytes 73736 | tf_op jit(solution)/shard_map/ppermute | solution.py:191
  49.0 1.6 %copy-done.3 = bf16[128,8192]{1,0:T(8,128)(2,1)S(1)} copy-done((bf16[128,8192]{1,0:T(8,128)(2,1)S(1)}, bf16[128,8192]{1,0:T(8,128)(2,1)}, u32[]{:S(2)}) %copy-start.3) | copy-done | bytes 2097176
  50.6 0.5 shard_map.49
  51.1 4.2 %collective-permute-start.11 = (f32[48,128]{1,0:T(8,128)S(1)}, f32[48,128]{1,0:T(8,128)S(1)}, u32[]{:S(2)}, u32[]{:S(2)}) collective-permute-start(f32[48,128]{1,0:T(8,128)S(1)} %broadcast_select_fusion), channel_id=1, source_target_pairs={{0,1},{1,0},{2,3},{3,2},{4,5},{5,4},{6,7},{7,6},{8,9},{9,8},{10,11... | collective-permute-start | bytes 73736 | tf_op jit(solution)/shard_map/ppermute | solution.py:191
  55.3 0.8 %collective-permute-done.11 = f32[48,128]{1,0:T(8,128)S(1)} collective-permute-done((f32[48,128]{1,0:T(8,128)S(1)}, f32[48,128]{1,0:T(8,128)S(1)}, u32[]{:S(2)}, u32[]{:S(2)}) %collective-permute-start.11) | collective-permute-done | bytes 24608 | tf_op jit(solution)/shard_map/ppermute | solution.py:191
  56.1 0.6 %select_add_fusion = f32[48,128]{1,0:T(8,128)} fusion(f32[48,128]{1,0:T(8,128)S(1)} %collective-permute-done.11, f32[48,128]{1,0:T(8,128)S(1)} %shard_map.49, f32[48,128]{1,0:T(8,128)S(1)} %collective-permute-done.10, pred[]{:T(512)S(6)} %eq.12), kind=kLoop, calls=%fused_computation.1 | loop fusion | flops 12288 | bytes 98305 | tf_op jit(solution)/shard_map/add | solution.py:258
  (17 shorter events, 0.2 us)
Async XLA Ops:
  0.0 1.2 %copy-start = (bf16[96,2048]{1,0:T(8,128)(2,1)S(1)}, bf16[96,2048]{1,0:T(8,128)(2,1)}, u32[]{:S(2)}) copy-start(bf16[96,2048]{1,0:T(8,128)(2,1)} %param.3) | copy-start | bytes 1179652
  0.0 46.7 %collective-permute-start.9 = (bf16[128,8192]{1,0:T(8,128)(2,1)}, bf16[128,8192]{1,0:T(8,128)(2,1)S(1)}, u32[]{:S(2)}, u32[]{:S(2)}) collective-permute-start(bf16[128,8192]{1,0:T(8,128)(2,1)} %refs_2_.3), channel_id=1, source_target_pairs={{0,16},{1,17},{2,18},{3,19},{4,20},{5,21},{6,22},{7,23},{8,24},{9,... | collective-permute-start | bytes 6291464 | tf_op jit(solution)/shard_map/ppermute | solution.py:191
  1.3 7.8 %collective-permute-start = (bf16[48,2048]{1,0:T(8,128)(2,1)S(1)}, bf16[48,2048]{1,0:T(8,128)(2,1)S(1)}, u32[]{:S(2)}, u32[]{:S(2)}) collective-permute-start(bf16[48,2048]{1,0:T(8,128)(2,1)S(1)} %constant_dynamic-slice_fusion.a_ref), channel_id=1, source_target_pairs={{0,8},{1,6},{2,10},{3,4},{4,12},{5,2},{6,14},{7,0},{8,15},{9,1},{1... | collective-permute-start | bytes 589832 | tf_op jit(solution)/shard_map/ppermute | solution.py:191
  9.1 6.6 %collective-permute-start.2 = (bf16[48,2048]{1,0:T(8,128)(2,1)S(1)}, bf16[48,2048]{1,0:T(8,128)(2,1)S(1)}, u32[]{:S(2)}, u32[]{:S(2)}) collective-permute-start(bf16[48,2048]{1,0:T(8,128)(2,1)S(1)} %shard_map.38.refs_2_), channel_id=1, source_target_pairs={{0,4},{1,5},{2,6},{3,7},{4,0},{5,1},{6,2},{7,3},{8,12},{9,13},{10,... | collective-permute-start | bytes 589832 | tf_op jit(solution)/shard_map/ppermute | solution.py:191
  9.3 9.4 %collective-permute-start.1 = (bf16[48,2048]{1,0:T(8,128)(2,1)S(1)}, bf16[48,2048]{1,0:T(8,128)(2,1)S(1)}, u32[]{:S(2)}, u32[]{:S(2)}) collective-permute-start(bf16[48,2048]{1,0:T(8,128)(2,1)S(1)} %shard_map.38.refs_2_), channel_id=1, source_target_pairs={{0,2},{1,3},{2,0},{3,1},{4,6},{5,7},{6,4},{7,5},{8,10},{9,11},{10,... | collective-permute-start | bytes 589832 | tf_op jit(solution)/shard_map/ppermute | solution.py:191
  11.5 10.3 %collective-permute-start.3 = (bf16[48,2048]{1,0:T(8,128)(2,1)S(1)}, bf16[48,2048]{1,0:T(8,128)(2,1)S(1)}, u32[]{:S(2)}, u32[]{:S(2)}) collective-permute-start(bf16[48,2048]{1,0:T(8,128)(2,1)S(1)} %shard_map.38.refs_2_), channel_id=1, source_target_pairs={{1,7},{3,5},{5,3},{7,1},{8,14},{10,12},{12,10},{14,8},{17,23},{19,... | collective-permute-start | bytes 589832 | tf_op jit(solution)/shard_map/ppermute | solution.py:191
  21.8 21.6 %copy-start.2 = (bf16[128,8192]{1,0:T(8,128)(2,1)S(1)}, bf16[128,8192]{1,0:T(8,128)(2,1)}, u32[]{:S(2)}) copy-start(bf16[128,8192]{1,0:T(8,128)(2,1)} %refs_2_.3) | copy-start | bytes 6291460
  24.5 5.2 %collective-permute-start.4 = (f32[48,2048]{1,0:T(8,128)S(1)}, f32[48,2048]{1,0:T(8,128)S(1)}, u32[]{:S(2)}, u32[]{:S(2)}) collective-permute-start(f32[48,2048]{1,0:T(8,128)S(1)} %shard_map.43), channel_id=1, source_target_pairs={{0,1},{1,0},{2,3},{3,2},{4,5},{5,4},{6,7},{7,6},{8,9},{9,8},{10,11... | collective-permute-start | bytes 1179656 | tf_op jit(solution)/shard_map/ppermute | solution.py:191
  29.8 7.9 %collective-permute-start.5 = (bf16[48,2048]{1,0:T(8,128)(2,1)S(1)}, bf16[48,2048]{1,0:T(8,128)(2,1)S(1)}, u32[]{:S(2)}, u32[]{:S(2)}) collective-permute-start(bf16[48,2048]{1,0:T(8,128)(2,1)S(1)} %add_convert_fusion.a_ref), channel_id=1, source_target_pairs={{0,8},{1,6},{2,10},{3,4},{4,12},{5,2},{6,14},{7,0},{8,15},{9,1},{1... | collective-permute-start | bytes 589832 | tf_op jit(solution)/shard_map/ppermute | solution.py:191
  37.7 5.7 %collective-permute-start.7 = (bf16[48,2048]{1,0:T(8,128)(2,1)S(1)}, bf16[48,2048]{1,0:T(8,128)(2,1)S(1)}, u32[]{:S(2)}, u32[]{:S(2)}) collective-permute-start(bf16[48,2048]{1,0:T(8,128)(2,1)S(1)} %shard_map.44.refs_0_), channel_id=1, source_target_pairs={{0,4},{1,5},{2,6},{3,7},{4,0},{5,1},{6,2},{7,3},{8,12},{9,13},{10,... | collective-permute-start | bytes 589832 | tf_op jit(solution)/shard_map/ppermute | solution.py:191
  38.0 7.0 %collective-permute-start.6 = (bf16[48,2048]{1,0:T(8,128)(2,1)S(1)}, bf16[48,2048]{1,0:T(8,128)(2,1)S(1)}, u32[]{:S(2)}, u32[]{:S(2)}) collective-permute-start(bf16[48,2048]{1,0:T(8,128)(2,1)S(1)} %shard_map.44.refs_0_), channel_id=1, source_target_pairs={{0,2},{1,3},{2,0},{3,1},{4,6},{5,7},{6,4},{7,5},{8,10},{9,11},{10,... | collective-permute-start | bytes 589832 | tf_op jit(solution)/shard_map/ppermute | solution.py:191
  41.0 4.0 %collective-permute-start.8 = (bf16[48,2048]{1,0:T(8,128)(2,1)S(1)}, bf16[48,2048]{1,0:T(8,128)(2,1)S(1)}, u32[]{:S(2)}, u32[]{:S(2)}) collective-permute-start(bf16[48,2048]{1,0:T(8,128)(2,1)S(1)} %shard_map.44.refs_0_), channel_id=1, source_target_pairs={{1,7},{3,5},{5,3},{7,1},{8,14},{10,12},{12,10},{14,8},{17,23},{19,... | collective-permute-start | bytes 589832 | tf_op jit(solution)/shard_map/ppermute | solution.py:191
  43.4 13.4 %copy-start.1 = (bf16[96,2048]{1,0:T(8,128)(2,1)S(1)}, bf16[96,2048]{1,0:T(8,128)(2,1)}, u32[]{:S(2)}) copy-start(bf16[96,2048]{1,0:T(8,128)(2,1)} %param.3) | copy-start | bytes 1179652
  47.7 3.4 %collective-permute-start.10 = (f32[48,128]{1,0:T(8,128)S(1)}, f32[48,128]{1,0:T(8,128)S(1)}, u32[]{:S(2)}, u32[]{:S(2)}) collective-permute-start(f32[48,128]{1,0:T(8,128)S(1)} %shard_map.48), channel_id=1, source_target_pairs={{0,16},{1,17},{2,18},{3,19},{4,20},{5,21},{6,22},{7,23},{8,24},{9,... | collective-permute-start | bytes 73736 | tf_op jit(solution)/shard_map/ppermute | solution.py:191
  49.0 1.6 %copy-start.3 = (bf16[128,8192]{1,0:T(8,128)(2,1)S(1)}, bf16[128,8192]{1,0:T(8,128)(2,1)}, u32[]{:S(2)}) copy-start(bf16[128,8192]{1,0:T(8,128)(2,1)} %refs_2_.3) | copy-start | bytes 6291460
  51.1 5.1 %collective-permute-start.11 = (f32[48,128]{1,0:T(8,128)S(1)}, f32[48,128]{1,0:T(8,128)S(1)}, u32[]{:S(2)}, u32[]{:S(2)}) collective-permute-start(f32[48,128]{1,0:T(8,128)S(1)} %broadcast_select_fusion), channel_id=1, source_target_pairs={{0,1},{1,0},{2,3},{3,2},{4,5},{5,4},{6,7},{7,6},{8,9},{9,8},{10,11... | collective-permute-start | bytes 73736 | tf_op jit(solution)/shard_map/ppermute | solution.py:191

commit v17 on v15

--- a/solution.py
+++ b/solution.py
@@ -115,13 +115,14 @@
     )(*((scalar(first), fisher) if fetch else ()), *ins, *([base] if has_base else []))
 
 
-def score_kernel(order, has_base, at_ref, *refs):
+def score_kernel(order, relative, has_base, at_ref, *refs):
     n = len(order)
     grads_ref, out_ref = refs[n], refs[-1]
     width = refs[0].shape[1]
     total = refs[n + 1][...] if has_base else None
     for k in range(n):
-        start = pl.multiple_of((at_ref[0] ^ order[k]) * width, width)
+        block = at_ref[0] ^ order[k] if relative else order[k]
+        start = pl.multiple_of(block * width, width)
         term = times(refs[k], grads_ref[:, pl.ds(start, width)])
         total = term if total is None else total + term
     out_ref[...] = total
@@ -132,7 +133,7 @@
     rows, width = pieces[0].shape
     operands = [*pieces, grads] + ([] if base is None else [base])
     return pl.pallas_call(
-        functools.partial(score_kernel, order, base is not None),
+        functools.partial(score_kernel, order, first is not None, base is not None),
         out_shape=jax.ShapeDtypeStruct((rows, grads.shape[0]), jnp.float32),
         in_specs=[SMEM] + [VMEM] * len(operands),
         out_specs=VMEM,
@@ -142,7 +143,37 @@
             bytes_accessed=2 * n * width * grads.shape[0],
             transcendentals=0,
         ),
-    )(scalar(first), *operands)
+    )(scalar(0 if first is None else first), *operands)
+
+
+def cut_kernel(order, at_ref, src_ref, out_ref, sem):
+    width = out_ref.shape[1] // len(order)
+    copies = []
+    for k, mask in enumerate(order):
+        start = pl.multiple_of((at_ref[0] ^ mask) * width, width)
+        copies.append(
+            pltpu.make_async_copy(
+                src_ref.at[:, pl.ds(start, width)], out_ref.at[:, k * width : (k + 1) * width], sem.at[k]
+            )
+        )
+        copies[-1].start()
+    for copy in copies:
+        copy.wait()
+
+
+def cut(src, order, first, width):
+    n = len(order)
+    return pl.pallas_call(
+        functools.partial(cut_kernel, order),
+        out_shape=jax.ShapeDtypeStruct((src.shape[0], n * width), src.dtype),
+        in_specs=[SMEM, HBM],
+        out_specs=VMEM,
+        scratch_shapes=[pltpu.SemaphoreType.DMA((n,))],
+        compiler_params=limit(51),
+        cost_estimate=pl.CostEstimate(
+            flops=0, bytes_accessed=2 * n * width * src.shape[0], transcendentals=0
+        ),
+    )(scalar(first), src)
 
 
 def pick_kernel(at_ref, a_ref, b_ref, *refs):
@@ -206,7 +237,7 @@
     def swap_core(value):
         return move(value, lambda sy, sz, sx, sd: (sy, sz, sx, 1 - sd))
 
-    def gather(own, after=()):
+    def gather(own, direct, after=()):
         def start(sy, sz, sx, sd):
             su = sz if sd == 0 else nz - 1 - sz
             if su < near:
@@ -214,43 +245,55 @@
             return sy, sz ^ 1, 1 - sx, 1 - sd
 
         came = move(own, start)
+        if direct:
+            corner = along_z(own, {0: 3, 1: 2}, True)
         first = pick(owner, own, came, after)
-        pairs = {0: 1, 1: 0, 2: 3, 3: 2}
-        beside = along_z(first, pairs)
+        beside = along_z(first, {0: 1, 1: 0, 2: 3, 3: 2})
+        if direct:
+            beside, corner = lax.optimization_barrier((beside, corner))
         across = along_z(first, {0: 0, 1: 1, 2: 2, 3: 3}, True)
-        diagonal = along_z(first, {2: 3, 3: 2}, True)
-
-        def corner(after):
-            ready, _ = lax.optimization_barrier((came, after))
-            return pick(owner, ready, diagonal)
-
-        return first, beside, across, corner
+
+        def last(after):
+            if direct:
+                piece, _ = lax.optimization_barrier((corner, after))
+            else:
+                ready, _ = lax.optimization_barrier((beside, after))
+                piece = along_z(ready, {2: 2, 3: 3}, True)
+            return pick(owner, came, piece)
+
+        return first, beside, across, last
 
     plane = jnp.where(d == 0, u % 2, nz - 1 - u % 2)
     column = plane * nx + x - d * (nex // 2)
 
-    other_grads = swap_y(stored_grads)
-
-    rows = nq // ny
-    own = lax.optimization_barrier(lax.dynamic_slice_in_dim(queries, y * rows, rows, axis=0))
-    step = functools.partial(fisher_step, inverse_fisher, column, own.shape[1])
+    rows, width = nq // ny, queries.shape[1]
+    to_y = cut(stored_grads, ORDER[1:], column, width)
+    queries, to_y = lax.optimization_barrier((queries, to_y))
+    own = lax.dynamic_slice_in_dim(queries, y * rows, rows, axis=0)
+    own, to_y = lax.optimization_barrier((own, to_y))
+    other_grads = swap_y(to_y)
+    step = functools.partial(fisher_step, inverse_fisher, column, width)
     a0, a1, b0, b1 = step(((0, 0), (0, 1), (1, 0), (1, 1)))
-    q0, q1, q2, corner = gather(own, (a0,))
+    q0, q1, q2, last = gather(own, False, (a0,))
     total, c0, c1 = step(((2, 0), (2, 1)), q0, (a0, a1))
     total, d0 = step(((3, 0),), q1, (b0, b1), total)
+    q3 = last(total)
     total, d1 = step(((3, 1),), q2, (c0, c1), total)
-    (total,) = step((), corner(total), (d0, d1), total)
+    (total,) = step((), q3, (d0, d1), total)
     panel = (total + swap_core(total)).astype(jnp.bfloat16)
 
-    p0, p1, p2, corner = gather(panel)
-    p3 = corner(panel)
+    p0, p1, p2, last = gather(panel, True, (other_grads,))
+    swapped = swap_y(p0)
     mine = score_dot([p0, p1], ORDER[:2], column, stored_grads)
     p2, _ = lax.optimization_barrier((p2, mine))
-    other = score_dot([p0, p1, p2, p3], ORDER, column, other_grads)
-    p2, p3, mine, _ = lax.optimization_barrier((p2, p3, mine, other))
+    other = score_dot([p1, p2], (0, 1), None, other_grads)
+    p3 = last(other)
+    other = score_dot([p3], (2,), None, other_grads, other)
+    p2, p3, mine, swapped, _ = lax.optimization_barrier((p2, p3, mine, swapped, other))
     mine = score_dot([p2, p3], ORDER[2:], column, stored_grads, mine)
-
-    other = swap_y(other)
+    theirs = score_dot([swapped], ORDER[:1], column, stored_grads)
+
+    other = swap_y(other) + theirs
     keep = jnp.where(d == y, mine, other)
     give = jnp.where(d == y, other, mine)
     return keep + swap_core(give)

time: 58.4 us -> 74.5 us (1.28)
  the two profiles are of different devices: /device:TPU:17 before, /device:TPU:0 now
where the time goes in v17:
time: 74.5 us; the launch traced here: 74.1 us
  Pallas kernels  25.8 us (35%)
  starting transfers between devices  22.7 us (30%)
  local copies, waits for them, and re-layouts  14.6 us (20%)
  waiting for transfers between devices  10.1 us (14%)
    ppermute x13, starting transfers between devices, move(): return lax.ppermute(value, AXES, pairs)  22.7 us
    pallas_call x5, Pallas kernels, fisher_step(): pl.pallas_call(functools.partial(fisher_kernel, len(ins), has_base, fetch...  18.3 us
    unnamed x24, local copies, waits for them, and re-layouts  14.6 us
    ppermute x13, waiting for transfers between devices, move(): return lax.ppermute(value, AXES, pairs)  10.1 us
    pallas_call x5, Pallas kernels, score_dot(): pl.pallas_call(functools.partial(score_kernel, order, first is not None,...  4.84 us
    pallas_call x1, Pallas kernels, cut(): pl.pallas_call(functools.partial(cut_kernel, order), out_shape=jax.ShapeD...  2.59 us
  transfers between devices with their start and end apart: 13, of which 5 were waited for; matrix products, arithmetic and copies ran while one was open for 0% of the time, Pallas kernels for 31%

profile of v17, /device:TPU:0, one launch (start us, length us, event | category | flops | bytes accessed | tf_op | source)
XLA Modules:
  0.0 74.1 jit_solution(145446352088050689)
XLA Ops:
  0.0 2.6 %shard_map.37 = bf16[128,6144]{1,0:T(8,128)(2,1)} custom-call(s32[1]{0:T(128)} %bitcast.at_ref.refs_0_, bf16[128,8192]{1,0:T(8,128)(2,1)} %refs_1_.9), custom_call_target="tpu_custom_call" | custom-call | bytes 1572864 | tf_op jit(solution)/shard_map/pallas_call | solution.py:166
  2.6 4.1 %collective-permute-start = (bf16[48,2048]{1,0:T(8,128)(2,1)S(1)}, bf16[48,2048]{1,0:T(8,128)(2,1)S(1)}, u32[]{:S(2)}, u32[]{:S(2)}) collective-permute-start(bf16[48,2048]{1,0:T(8,128)(2,1)S(1)} %constant_dynamic-slice_fusion.a_ref), channel_id=1, source_target_pairs={{0,8},{1,6},{2,10},{3,4},{4,12},{5,2},{6,14},{7,0},{8,15},{9,1},{1... | collective-permute-start | bytes 589832 | tf_op jit(solution)/shard_map/ppermute | solution.py:222
  6.7 1.5 %collective-permute-start.6 = (bf16[128,6144]{1,0:T(8,128)(2,1)}, bf16[128,6144]{1,0:T(8,128)(2,1)}, u32[]{:S(2)}, u32[]{:S(2)}) collective-permute-start(bf16[128,6144]{1,0:T(8,128)(2,1)} %shard_map.37), channel_id=1, source_target_pairs={{0,16},{1,17},{2,18},{3,19},{4,20},{5,21},{6,22},{7,23},{8,24},{9,... | collective-permute-start | bytes 4718600 | tf_op jit(solution)/shard_map/ppermute | solution.py:222
  8.3 6.0 %shard_map.38 = (bf16[1024,2048]{1,0:T(8,128)(2,1)S(1)}, bf16[1024,2048]{1,0:T(8,128)(2,1)S(1)}, bf16[1024,2048]{1,0:T(8,128)(2,1)S(1)}, bf16[1024,2048]{1,0:T(8,128)(2,1)S(1)}) custom-call(s32[1]{0:T(128)} %bitcast.at_ref.refs_0_, bf16[2048,8192]{1,0:T(8,128)(2,1)} %refs_1_.8), custom_call_target="tpu_custom_call" | custom-call | bytes 16777216 | tf_op jit(solution)/shard_map/pallas_call | solution.py:103
  14.2 2.0 %copy-done.3 = bf16[1024,2048]{1,0:T(8,128)(2,1)} copy-done((bf16[1024,2048]{1,0:T(8,128)(2,1)}, bf16[1024,2048]{1,0:T(8,128)(2,1)S(1)}, u32[]{:S(2)}) %copy-start.3) | copy-done | bytes 4194328
  16.2 1.9 %copy-done.6 = bf16[1024,2048]{1,0:T(8,128)(2,1)} copy-done((bf16[1024,2048]{1,0:T(8,128)(2,1)}, bf16[1024,2048]{1,0:T(8,128)(2,1)S(1)}, u32[]{:S(2)}) %copy-start.6) | copy-done | bytes 4194328
  18.2 2.0 %copy-done.8 = bf16[1024,2048]{1,0:T(8,128)(2,1)} copy-done((bf16[1024,2048]{1,0:T(8,128)(2,1)}, bf16[1024,2048]{1,0:T(8,128)(2,1)S(1)}, u32[]{:S(2)}) %copy-start.8) | copy-done | bytes 4194328
  20.2 1.9 %copy-done.10 = bf16[1024,2048]{1,0:T(8,128)(2,1)} copy-done((bf16[1024,2048]{1,0:T(8,128)(2,1)}, bf16[1024,2048]{1,0:T(8,128)(2,1)S(1)}, u32[]{:S(2)}) %copy-start.10) | copy-done | bytes 4194328
  22.1 2.2 %copy-done.4 = bf16[1024,2048]{1,0:T(8,128)(2,1)S(1)} copy-done((bf16[1024,2048]{1,0:T(8,128)(2,1)S(1)}, bf16[1024,2048]{1,0:T(8,128)(2,1)}, u32[]{:S(2)}) %copy-start.4) | copy-done | bytes 4194328
  24.4 1.6 %collective-permute-start.1 = (bf16[48,2048]{1,0:T(8,128)(2,1)S(1)}, bf16[48,2048]{1,0:T(8,128)(2,1)S(1)}, u32[]{:S(2)}, u32[]{:S(2)}) collective-permute-start(bf16[48,2048]{1,0:T(8,128)(2,1)S(1)} %shard_map.39.refs_2_), channel_id=1, source_target_pairs={{0,4},{1,5},{2,6},{3,7},{4,0},{5,1},{6,2},{7,3},{8,12},{9,13},{10,... | collective-permute-start | bytes 589832 | tf_op jit(solution)/shard_map/ppermute | solution.py:222
  26.0 1.5 %collective-permute-start.3 = (bf16[48,2048]{1,0:T(8,128)(2,1)S(1)}, bf16[48,2048]{1,0:T(8,128)(2,1)S(1)}, u32[]{:S(2)}, u32[]{:S(2)}) collective-permute-start(bf16[48,2048]{1,0:T(8,128)(2,1)S(1)} %shard_map.39.refs_2_), channel_id=1, source_target_pairs={{0,2},{1,3},{2,0},{3,1},{4,6},{5,7},{6,4},{7,5},{8,10},{9,11},{10,... | collective-permute-start | bytes 589832 | tf_op jit(solution)/shard_map/ppermute | solution.py:222
  27.5 2.2 %copy-done.11 = bf16[1024,2048]{1,0:T(8,128)(2,1)S(1)} copy-done((bf16[1024,2048]{1,0:T(8,128)(2,1)S(1)}, bf16[1024,2048]{1,0:T(8,128)(2,1)}, u32[]{:S(2)}) %copy-start.11) | copy-done | bytes 4194328
  29.7 3.7 %shard_map.40 = (f32[48,2048]{1,0:T(8,128)S(1)}, bf16[1024,2048]{1,0:T(8,128)(2,1)S(1)}, bf16[1024,2048]{1,0:T(8,128)(2,1)S(1)}) custom-call(s32[1]{0:T(128)} %bitcast.at_ref.refs_0_, bf16[2048,8192]{1,0:T(8,128)(2,1)} %refs_1_.8, bf16[48,2048]{1,0:T(8,128)(2,1)S(1)} %shard_map.39.refs_2_, bf16[1024,2048]{1,0:T(8,128)(2,1)S(1)} %copy-done.5, ...), custom_call_target="tpu_custom_call" | custom-call | flops 402653184 | bytes 16777216 | tf_op jit(solution)/shard_map/pallas_call | solution.py:103
  33.4 1.0 %copy-done.7 = bf16[1024,2048]{1,0:T(8,128)(2,1)S(1)} copy-done((bf16[1024,2048]{1,0:T(8,128)(2,1)S(1)}, bf16[1024,2048]{1,0:T(8,128)(2,1)}, u32[]{:S(2)}) %copy-start.7) | copy-done | bytes 4194328
  34.3 1.3 %copy-done.9 = bf16[1024,2048]{1,0:T(8,128)(2,1)S(1)} copy-done((bf16[1024,2048]{1,0:T(8,128)(2,1)S(1)}, bf16[1024,2048]{1,0:T(8,128)(2,1)}, u32[]{:S(2)}) %copy-start.9) | copy-done | bytes 4194328
  35.6 3.0 %shard_map.41 = (f32[48,2048]{1,0:T(8,128)S(1)}, bf16[1024,2048]{1,0:T(8,128)(2,1)S(1)}) custom-call(s32[1]{0:T(128)} %bitcast.at_ref.refs_0_, bf16[2048,8192]{1,0:T(8,128)(2,1)} %refs_1_.8, bf16[48,2048]{1,0:T(8,128)(2,1)S(1)} %collective-permute-done.1.refs_2_, bf16[1024,2048]{1,0:T(8,128)(2,1)S(1)} %copy-done.7, bf16[1024,2048]{1,0:T(8,128)(2,1)S(1)} %copy-done.9, ...), custom_call_target="tpu_custom_call" | custom-call | flops 402653184 | bytes 12582912 | tf_op jit(solution)/shard_map/pallas_call | solution.py:103
  38.6 0.7 collective-permute-start.2
  39.3 3.0 %shard_map.43 = (f32[48,2048]{1,0:T(8,128)S(1)}, bf16[1024,2048]{1,0:T(8,128)(2,1)S(1)}) custom-call(s32[1]{0:T(128)} %bitcast.at_ref.refs_0_, bf16[2048,8192]{1,0:T(8,128)(2,1)} %refs_1_.8, bf16[48,2048]{1,0:T(8,128)(2,1)S(1)} %collective-permute-done.3.refs_2_, bf16[1024,2048]{1,0:T(8,128)(2,1)S(1)} %get-tuple-element.40.refs_3_, ...), custom_call_target="tpu_custom_call" | custom-call | flops 402653184 | bytes 12582912 | tf_op jit(solution)/shard_map/pallas_call | solution.py:103
  42.4 2.6 %shard_map.44 = f32[48,2048]{1,0:T(8,128)S(1)} custom-call(bf16[48,2048]{1,0:T(8,128)(2,1)S(1)} %shard_map.42.refs_0_, bf16[1024,2048]{1,0:T(8,128)(2,1)S(1)} %get-tuple-element.39.refs_1_, bf16[1024,2048]{1,0:T(8,128)(2,1)S(1)} %get-tuple-element.42.refs_2_, f32[48,2048]{1,0:T(8,128)S(1)} %get-tuple-element.43.refs_3_), custom_call_target="tpu_custom_call" | custom-call | flops 402653184 | bytes 8388608 | tf_op jit(solution)/shard_map/pallas_call | solution.py:103
  45.1 1.5 %collective-permute-start.4 = (f32[48,2048]{1,0:T(8,128)S(1)}, f32[48,2048]{1,0:T(8,128)S(1)}, u32[]{:S(2)}, u32[]{:S(2)}) collective-permute-start(f32[48,2048]{1,0:T(8,128)S(1)} %shard_map.44), channel_id=1, source_target_pairs={{0,1},{1,0},{2,3},{3,2},{4,5},{5,4},{6,7},{7,6},{8,9},{9,8},{10,11... | collective-permute-start | bytes 1179656 | tf_op jit(solution)/shard_map/ppermute | solution.py:222
  46.6 1.3 %collective-permute-done.4 = f32[48,2048]{1,0:T(8,128)S(1)} collective-permute-done((f32[48,2048]{1,0:T(8,128)S(1)}, f32[48,2048]{1,0:T(8,128)S(1)}, u32[]{:S(2)}, u32[]{:S(2)}) %collective-permute-start.4) | collective-permute-done | bytes 393248 | tf_op jit(solution)/shard_map/ppermute | solution.py:222
  48.0 3.8 %collective-permute-start.5 = (bf16[48,2048]{1,0:T(8,128)(2,1)S(1)}, bf16[48,2048]{1,0:T(8,128)(2,1)S(1)}, u32[]{:S(2)}, u32[]{:S(2)}) collective-permute-start(bf16[48,2048]{1,0:T(8,128)(2,1)S(1)} %add_convert_fusion.a_ref), channel_id=1, source_target_pairs={{0,8},{1,6},{2,10},{3,4},{4,12},{5,2},{6,14},{7,0},{8,15},{9,1},{1... | collective-permute-start | bytes 589832 | tf_op jit(solution)/shard_map/ppermute | solution.py:222
  51.7 4.0 %collective-permute-start.9 = (bf16[48,2048]{1,0:T(8,128)(2,1)S(1)}, bf16[48,2048]{1,0:T(8,128)(2,1)S(1)}, u32[]{:S(2)}, u32[]{:S(2)}) collective-permute-start(bf16[48,2048]{1,0:T(8,128)(2,1)S(1)} %add_convert_fusion.a_ref), channel_id=1, source_target_pairs={{0,14},{2,12},{4,10},{6,8},{9,7},{11,5},{13,3},{15,1},{16,30},{18,... | collective-permute-start | bytes 589832 | tf_op jit(solution)/shard_map/ppermute | solution.py:222
  55.8 1.8 %collective-permute-start.8 = (bf16[48,2048]{1,0:T(8,128)(2,1)S(1)}, bf16[48,2048]{1,0:T(8,128)(2,1)S(1)}, u32[]{:S(2)}, u32[]{:S(2)}) collective-permute-start(bf16[48,2048]{1,0:T(8,128)(2,1)S(1)} %shard_map.45.refs_0_), channel_id=1, source_target_pairs={{0,4},{1,5},{2,6},{3,7},{4,0},{5,1},{6,2},{7,3},{8,12},{9,13},{10,... | collective-permute-start | bytes 589832 | tf_op jit(solution)/shard_map/ppermute | solution.py:222
  57.6 1.5 %collective-permute-start.7 = (bf16[48,2048]{1,0:T(8,128)(2,1)S(1)}, bf16[48,2048]{1,0:T(8,128)(2,1)S(1)}, u32[]{:S(2)}, u32[]{:S(2)}) collective-permute-start(bf16[48,2048]{1,0:T(8,128)(2,1)S(1)} %shard_map.45.refs_0_), channel_id=1, source_target_pairs={{0,2},{1,3},{2,0},{3,1},{4,6},{5,7},{6,4},{7,5},{8,10},{9,11},{10,... | collective-permute-start | bytes 589832 | tf_op jit(solution)/shard_map/ppermute | solution.py:222
  59.7 3.5 %collective-permute-done.8.refs_1_.refs_0_ = bf16[48,2048]{1,0:T(8,128)(2,1)S(1)} collective-permute-done((bf16[48,2048]{1,0:T(8,128)(2,1)S(1)}, bf16[48,2048]{1,0:T(8,128)(2,1)S(1)}, u32[]{:S(2)}, u32[]{:S(2)}) %collective-permute-start.8) | collective-permute-done | bytes 196640 | tf_op jit(solution)/shard_map/ppermute | solution.py:222
  63.7 1.0 %collective-permute-done.7.refs_1_.refs_0_ = bf16[48,2048]{1,0:T(8,128)(2,1)S(1)} collective-permute-done((bf16[48,2048]{1,0:T(8,128)(2,1)S(1)}, bf16[48,2048]{1,0:T(8,128)(2,1)S(1)}, u32[]{:S(2)}, u32[]{:S(2)}) %collective-permute-start.7) | collective-permute-done | bytes 196640 | tf_op jit(solution)/shard_map/ppermute | solution.py:222
  64.7 1.9 %shard_map.47.refs_2_ = f32[48,128]{1,0:T(8,128)S(1)} custom-call(s32[1]{0:T(128)} %constant.52.clone.1.at_ref, bf16[48,2048]{1,0:T(8,128)(2,1)S(1)} %collective-permute-done.8.refs_1_.refs_0_, bf16[48,2048]{1,0:T(8,128)(2,1)S(1)} %collective-permute-done.7.refs_1_.refs_0_, bf16[128,6144]{1,0:T(8,128)(2,1)} %collective-permute-done.6.refs_0_.refs_2_.refs_1_), custom_call_target="tpu_custom_call" | custom-call | flops 50331648 | bytes 1048576 | tf_op jit(solution)/shard_map/pallas_call | solution.py:135
  66.7 1.7 %shard_map.49 = f32[48,128]{1,0:T(8,128)S(1)} custom-call(s32[1]{0:T(128)} %constant.52.clone.1.at_ref, bf16[48,2048]{1,0:T(8,128)(2,1)S(1)} %shard_map.48.refs_0_.refs_1_, bf16[128,6144]{1,0:T(8,128)(2,1)} %collective-permute-done.6.refs_0_.refs_2_.refs_1_, f32[48,128]{1,0:T(8,128)S(1)} %shard_map.47.refs_2_), custom_call_target="tpu_custom_call" | custom-call | flops 25165824 | bytes 524288 | tf_op jit(solution)/shard_map/pallas_call | solution.py:135
  69.3 3.0 %collective-permute-done.11 = f32[48,128]{1,0:T(8,128)S(1)} collective-permute-done((f32[48,128]{1,0:T(8,128)S(1)}, f32[48,128]{1,0:T(8,128)S(1)}, u32[]{:S(2)}, u32[]{:S(2)}) %collective-permute-start.11) | collective-permute-done | bytes 24608 | tf_op jit(solution)/shard_map/ppermute | solution.py:222
  72.3 1.2 %collective-permute-done.12 = f32[48,128]{1,0:T(8,128)S(1)} collective-permute-done((f32[48,128]{1,0:T(8,128)S(1)}, f32[48,128]{1,0:T(8,128)S(1)}, u32[]{:S(2)}, u32[]{:S(2)}) %collective-permute-start.12) | collective-permute-done | bytes 24608 | tf_op jit(solution)/shard_map/ppermute | solution.py:222
  73.4 0.6 select_add_fusion
  (37 shorter events, 2.1 us)
Async XLA Ops:
  0.0 2.6 %copy-start = (bf16[96,2048]{1,0:T(8,128)(2,1)S(1)}, bf16[96,2048]{1,0:T(8,128)(2,1)}, u32[]{:S(2)}) copy-start(bf16[96,2048]{1,0:T(8,128)(2,1)} %param.3) | copy-start | bytes 1179652
  2.6 19.5 %collective-permute-start = (bf16[48,2048]{1,0:T(8,128)(2,1)S(1)}, bf16[48,2048]{1,0:T(8,128)(2,1)S(1)}, u32[]{:S(2)}, u32[]{:S(2)}) collective-permute-start(bf16[48,2048]{1,0:T(8,128)(2,1)S(1)} %constant_dynamic-slice_fusion.a_ref), channel_id=1, source_target_pairs={{0,8},{1,6},{2,10},{3,4},{4,12},{5,2},{6,14},{7,0},{8,15},{9,1},{1... | collective-permute-start | bytes 589832 | tf_op jit(solution)/shard_map/ppermute | solution.py:222
  6.7 49.0 %collective-permute-start.6 = (bf16[128,6144]{1,0:T(8,128)(2,1)}, bf16[128,6144]{1,0:T(8,128)(2,1)}, u32[]{:S(2)}, u32[]{:S(2)}) collective-permute-start(bf16[128,6144]{1,0:T(8,128)(2,1)} %shard_map.37), channel_id=1, source_target_pairs={{0,16},{1,17},{2,18},{3,19},{4,20},{5,21},{6,22},{7,23},{8,24},{9,... | collective-permute-start | bytes 4718600 | tf_op jit(solution)/shard_map/ppermute | solution.py:222
  14.2 2.0 %copy-start.3 = (bf16[1024,2048]{1,0:T(8,128)(2,1)}, bf16[1024,2048]{1,0:T(8,128)(2,1)S(1)}, u32[]{:S(2)}) copy-start(bf16[1024,2048]{1,0:T(8,128)(2,1)S(1)} %get-tuple-element.32.refs_0_.refs_3_) | copy-start | bytes 12582916
  16.2 1.9 %copy-start.6 = (bf16[1024,2048]{1,0:T(8,128)(2,1)}, bf16[1024,2048]{1,0:T(8,128)(2,1)S(1)}, u32[]{:S(2)}) copy-start(bf16[1024,2048]{1,0:T(8,128)(2,1)S(1)} %get-tuple-element.33.refs_3_) | copy-start | bytes 12582916
  18.2 2.0 %copy-start.8 = (bf16[1024,2048]{1,0:T(8,128)(2,1)}, bf16[1024,2048]{1,0:T(8,128)(2,1)S(1)}, u32[]{:S(2)}) copy-start(bf16[1024,2048]{1,0:T(8,128)(2,1)S(1)} %get-tuple-element.34.refs_4_) | copy-start | bytes 12582916
  20.2 1.9 %copy-start.10 = (bf16[1024,2048]{1,0:T(8,128)(2,1)}, bf16[1024,2048]{1,0:T(8,128)(2,1)S(1)}, u32[]{:S(2)}) copy-start(bf16[1024,2048]{1,0:T(8,128)(2,1)S(1)} %get-tuple-element.35.refs_4_) | copy-start | bytes 12582916
  22.1 2.2 %copy-start.4 = (bf16[1024,2048]{1,0:T(8,128)(2,1)S(1)}, bf16[1024,2048]{1,0:T(8,128)(2,1)}, u32[]{:S(2)}) copy-start(bf16[1024,2048]{1,0:T(8,128)(2,1)} %copy-done.3) | copy-start | bytes 12582916
  24.3 3.2 %copy-start.5 = (bf16[1024,2048]{1,0:T(8,128)(2,1)S(1)}, bf16[1024,2048]{1,0:T(8,128)(2,1)}, u32[]{:S(2)}) copy-start(bf16[1024,2048]{1,0:T(8,128)(2,1)} %copy-done.3) | copy-start | bytes 12582916
  24.4 9.0 %collective-permute-start.1 = (bf16[48,2048]{1,0:T(8,128)(2,1)S(1)}, bf16[48,2048]{1,0:T(8,128)(2,1)S(1)}, u32[]{:S(2)}, u32[]{:S(2)}) collective-permute-start(bf16[48,2048]{1,0:T(8,128)(2,1)S(1)} %shard_map.39.refs_2_), channel_id=1, source_target_pairs={{0,4},{1,5},{2,6},{3,7},{4,0},{5,1},{6,2},{7,3},{8,12},{9,13},{10,... | collective-permute-start | bytes 589832 | tf_op jit(solution)/shard_map/ppermute | solution.py:222
  26.0 13.3 %collective-permute-start.3 = (bf16[48,2048]{1,0:T(8,128)(2,1)S(1)}, bf16[48,2048]{1,0:T(8,128)(2,1)S(1)}, u32[]{:S(2)}, u32[]{:S(2)}) collective-permute-start(bf16[48,2048]{1,0:T(8,128)(2,1)S(1)} %shard_map.39.refs_2_), channel_id=1, source_target_pairs={{0,2},{1,3},{2,0},{3,1},{4,6},{5,7},{6,4},{7,5},{8,10},{9,11},{10,... | collective-permute-start | bytes 589832 | tf_op jit(solution)/shard_map/ppermute | solution.py:222
  27.5 2.2 %copy-start.11 = (bf16[1024,2048]{1,0:T(8,128)(2,1)S(1)}, bf16[1024,2048]{1,0:T(8,128)(2,1)}, u32[]{:S(2)}) copy-start(bf16[1024,2048]{1,0:T(8,128)(2,1)} %copy-done.10) | copy-start | bytes 12582916
  29.7 4.7 %copy-start.7 = (bf16[1024,2048]{1,0:T(8,128)(2,1)S(1)}, bf16[1024,2048]{1,0:T(8,128)(2,1)}, u32[]{:S(2)}) copy-start(bf16[1024,2048]{1,0:T(8,128)(2,1)} %copy-done.6) | copy-start | bytes 12582916
  29.7 5.9 %copy-start.9 = (bf16[1024,2048]{1,0:T(8,128)(2,1)S(1)}, bf16[1024,2048]{1,0:T(8,128)(2,1)}, u32[]{:S(2)}) copy-start(bf16[1024,2048]{1,0:T(8,128)(2,1)} %copy-done.8) | copy-start | bytes 12582916
  38.6 3.7 %collective-permute-start.2 = (bf16[48,2048]{1,0:T(8,128)(2,1)S(1)}, bf16[48,2048]{1,0:T(8,128)(2,1)S(1)}, u32[]{:S(2)}, u32[]{:S(2)}) collective-permute-start(bf16[48,2048]{1,0:T(8,128)(2,1)S(1)} %collective-permute-done.1.refs_2_), channel_id=1, source_target_pairs={{1,3},{3,1},{5,7},{7,5},{8,10},{10,8},{12,14},{14,12},{17,19},{19,... | collective-permute-start | bytes 589832 | tf_op jit(solution)/shard_map/ppermute | solution.py:222
  42.4 20.8 %copy-start.2 = (bf16[128,8192]{1,0:T(8,128)(2,1)S(1)}, bf16[128,8192]{1,0:T(8,128)(2,1)}, u32[]{:S(2)}) copy-start(bf16[128,8192]{1,0:T(8,128)(2,1)} %refs_1_.9) | copy-start | bytes 6291460
  45.1 2.9 %collective-permute-start.4 = (f32[48,2048]{1,0:T(8,128)S(1)}, f32[48,2048]{1,0:T(8,128)S(1)}, u32[]{:S(2)}, u32[]{:S(2)}) collective-permute-start(f32[48,2048]{1,0:T(8,128)S(1)} %shard_map.44), channel_id=1, source_target_pairs={{0,1},{1,0},{2,3},{3,2},{4,5},{5,4},{6,7},{7,6},{8,9},{9,8},{10,11... | collective-permute-start | bytes 1179656 | tf_op jit(solution)/shard_map/ppermute | solution.py:222
  48.0 7.8 %collective-permute-start.5 = (bf16[48,2048]{1,0:T(8,128)(2,1)S(1)}, bf16[48,2048]{1,0:T(8,128)(2,1)S(1)}, u32[]{:S(2)}, u32[]{:S(2)}) collective-permute-start(bf16[48,2048]{1,0:T(8,128)(2,1)S(1)} %add_convert_fusion.a_ref), channel_id=1, source_target_pairs={{0,8},{1,6},{2,10},{3,4},{4,12},{5,2},{6,14},{7,0},{8,15},{9,1},{1... | collective-permute-start | bytes 589832 | tf_op jit(solution)/shard_map/ppermute | solution.py:222
  51.7 7.9 %collective-permute-start.9 = (bf16[48,2048]{1,0:T(8,128)(2,1)S(1)}, bf16[48,2048]{1,0:T(8,128)(2,1)S(1)}, u32[]{:S(2)}, u32[]{:S(2)}) collective-permute-start(bf16[48,2048]{1,0:T(8,128)(2,1)S(1)} %add_convert_fusion.a_ref), channel_id=1, source_target_pairs={{0,14},{2,12},{4,10},{6,8},{9,7},{11,5},{13,3},{15,1},{16,30},{18,... | collective-permute-start | bytes 589832 | tf_op jit(solution)/shard_map/ppermute | solution.py:222
  55.8 7.4 %collective-permute-start.8 = (bf16[48,2048]{1,0:T(8,128)(2,1)S(1)}, bf16[48,2048]{1,0:T(8,128)(2,1)S(1)}, u32[]{:S(2)}, u32[]{:S(2)}) collective-permute-start(bf16[48,2048]{1,0:T(8,128)(2,1)S(1)} %shard_map.45.refs_0_), channel_id=1, source_target_pairs={{0,4},{1,5},{2,6},{3,7},{4,0},{5,1},{6,2},{7,3},{8,12},{9,13},{10,... | collective-permute-start | bytes 589832 | tf_op jit(solution)/shard_map/ppermute | solution.py:222
  57.6 7.0 %collective-permute-start.7 = (bf16[48,2048]{1,0:T(8,128)(2,1)S(1)}, bf16[48,2048]{1,0:T(8,128)(2,1)S(1)}, u32[]{:S(2)}, u32[]{:S(2)}) collective-permute-start(bf16[48,2048]{1,0:T(8,128)(2,1)S(1)} %shard_map.45.refs_0_), channel_id=1, source_target_pairs={{0,2},{1,3},{2,0},{3,1},{4,6},{5,7},{6,4},{7,5},{8,10},{9,11},{10,... | collective-permute-start | bytes 589832 | tf_op jit(solution)/shard_map/ppermute | solution.py:222
  59.1 9.4 %collective-permute-start.10 = (bf16[48,2048]{1,0:T(8,128)(2,1)S(1)}, bf16[48,2048]{1,0:T(8,128)(2,1)S(1)}, u32[]{:S(2)}, u32[]{:S(2)}) collective-permute-start(bf16[48,2048]{1,0:T(8,128)(2,1)S(1)} %shard_map.45.refs_0_), channel_id=1, source_target_pairs={{0,16},{1,17},{2,18},{3,19},{4,20},{5,21},{6,22},{7,23},{8,24},{9,... | collective-permute-start | bytes 589832 | tf_op jit(solution)/shard_map/ppermute | solution.py:222
  64.7 9.4 %copy-start.1 = (bf16[96,2048]{1,0:T(8,128)(2,1)S(1)}, bf16[96,2048]{1,0:T(8,128)(2,1)}, u32[]{:S(2)}) copy-start(bf16[96,2048]{1,0:T(8,128)(2,1)} %param.3) | copy-start | bytes 1179652
  68.3 3.9 %collective-permute-start.11 = (f32[48,128]{1,0:T(8,128)S(1)}, f32[48,128]{1,0:T(8,128)S(1)}, u32[]{:S(2)}, u32[]{:S(2)}) collective-permute-start(f32[48,128]{1,0:T(8,128)S(1)} %shard_map.49), channel_id=1, source_target_pairs={{0,16},{1,17},{2,18},{3,19},{4,20},{5,21},{6,22},{7,23},{8,24},{9,... | collective-permute-start | bytes 73736 | tf_op jit(solution)/shard_map/ppermute | solution.py:222
  72.2 1.2 %collective-permute-start.12 = (f32[48,128]{1,0:T(8,128)S(1)}, f32[48,128]{1,0:T(8,128)S(1)}, u32[]{:S(2)}, u32[]{:S(2)}) collective-permute-start(f32[48,128]{1,0:T(8,128)S(1)} %broadcast_select_fusion), channel_id=1, source_target_pairs={{0,1},{1,0},{2,3},{3,2},{4,5},{5,4},{6,7},{7,6},{8,9},{9,8},{10,11... | collective-permute-start | bytes 73736 | tf_op jit(solution)/shard_map/ppermute | solution.py:222

commit v18 on v16

--- a/solution.py
+++ b/solution.py
@@ -206,7 +206,7 @@
     def swap_core(value):
         return move(value, lambda sy, sz, sx, sd: (sy, sz, sx, 1 - sd))
 
-    def gather(own, after=()):
+    def gather(own, direct, after=()):
         def start(sy, sz, sx, sd):
             su = sz if sd == 0 else nz - 1 - sz
             if su < near:
@@ -214,17 +214,22 @@
             return sy, sz ^ 1, 1 - sx, 1 - sd
 
         came = move(own, start)
+        if direct:
+            corner = along_z(own, {0: 3, 1: 2}, True)
         first = pick(owner, own, came, after)
         pairs = {0: 1, 1: 0, 2: 3, 3: 2}
         beside = along_z(first, pairs)
         across = along_z(first, {0: 0, 1: 1, 2: 2, 3: 3}, True)
-        diagonal = along_z(first, {2: 3, 3: 2}, True)
-
-        def corner(after):
+        if direct:
+            beside, corner = lax.optimization_barrier((beside, corner))
+        else:
+            corner = along_z(first, {2: 3, 3: 2}, True)
+
+        def last(after):
             ready, _ = lax.optimization_barrier((came, after))
-            return pick(owner, ready, diagonal)
-
-        return first, beside, across, corner
+            return pick(owner, ready, corner)
+
+        return first, beside, across, last
 
     plane = jnp.where(d == 0, u % 2, nz - 1 - u % 2)
     column = plane * nx + x - d * (nex // 2)
@@ -235,15 +240,15 @@
     own = lax.optimization_barrier(lax.dynamic_slice_in_dim(queries, y * rows, rows, axis=0))
     step = functools.partial(fisher_step, inverse_fisher, column, own.shape[1])
     a0, a1, b0, b1 = step(((0, 0), (0, 1), (1, 0), (1, 1)))
-    q0, q1, q2, corner = gather(own, (a0,))
+    q0, q1, q2, last = gather(own, False, (a0,))
     total, c0, c1 = step(((2, 0), (2, 1)), q0, (a0, a1))
     total, d0 = step(((3, 0),), q1, (b0, b1), total)
     total, d1 = step(((3, 1),), q2, (c0, c1), total)
-    (total,) = step((), corner(total), (d0, d1), total)
+    (total,) = step((), last(total), (d0, d1), total)
     panel = (total + swap_core(total)).astype(jnp.bfloat16)
 
-    p0, p1, p2, corner = gather(panel)
-    p3 = corner(panel)
+    p0, p1, p2, last = gather(panel, True)
+    p3 = last(panel)
     mine = score_dot([p0, p1], ORDER[:2], column, stored_grads)
     p2, _ = lax.optimization_barrier((p2, mine))
     other = score_dot([p0, p1, p2], ORDER[:3], column, other_grads)

time: 56.9 us -> 55.7 us (0.979)
  the two profiles are of different devices: /device:TPU:17 before, /device:TPU:0 now
where the time goes in v18:
time: 55.7 us; the launch traced here: 55.5 us
  starting transfers between devices  23.6 us (42%)
  Pallas kernels  20.1 us (36%)
  waiting for transfers between devices  9.36 us (17%)
  local copies, waits for them, and re-layouts  1.62 us (3%)
  other arithmetic  0.67 us (1%)
    ppermute x12, starting transfers between devices, move(): return lax.ppermute(value, AXES, pairs)  23.6 us
    pallas_call x5, Pallas kernels, fisher_step(): pl.pallas_call(functools.partial(fisher_kernel, len(ins), has_base, fetch...  18.1 us
    ppermute x12, waiting for transfers between devices, move(): return lax.ppermute(value, AXES, pairs)  9.36 us
    pallas_call x4, Pallas kernels, score_dot(): pl.pallas_call(functools.partial(score_kernel, order, base is not None),...  1.89 us
    unnamed x8, local copies, waits for them, and re-layouts  1.6 us
  transfers between devices with their start and end apart: 12, of which 7 were waited for; matrix products, arithmetic and copies ran while one was open for 0% of the time, Pallas kernels for 35%

profile of v18, /device:TPU:0, one launch (start us, length us, event | category | flops | bytes accessed | tf_op | source)
XLA Modules:
  0.0 55.5 jit_solution(5021304543435727901)
XLA Ops:
  0.0 3.0 %collective-permute-start.9 = (bf16[128,8192]{1,0:T(8,128)(2,1)}, bf16[128,8192]{1,0:T(8,128)(2,1)S(1)}, u32[]{:S(2)}, u32[]{:S(2)}) collective-permute-start(bf16[128,8192]{1,0:T(8,128)(2,1)} %refs_2_.3), channel_id=1, source_target_pairs={{0,16},{1,17},{2,18},{3,19},{4,20},{5,21},{6,22},{7,23},{8,24},{9,... | collective-permute-start | bytes 6291464 | tf_op jit(solution)/shard_map/ppermute | solution.py:191
  3.0 2.7 %collective-permute-start = (bf16[48,2048]{1,0:T(8,128)(2,1)S(1)}, bf16[48,2048]{1,0:T(8,128)(2,1)S(1)}, u32[]{:S(2)}, u32[]{:S(2)}) collective-permute-start(bf16[48,2048]{1,0:T(8,128)(2,1)S(1)} %constant_dynamic-slice_fusion.a_ref), channel_id=1, source_target_pairs={{0,8},{1,6},{2,10},{3,4},{4,12},{5,2},{6,14},{7,0},{8,15},{9,1},{1... | collective-permute-start | bytes 589832 | tf_op jit(solution)/shard_map/ppermute | solution.py:191
  5.6 6.0 %shard_map.37 = (bf16[1024,2048]{1,0:T(8,128)(2,1)S(1)}, bf16[1024,2048]{1,0:T(8,128)(2,1)S(1)}, bf16[1024,2048]{1,0:T(8,128)(2,1)S(1)}, bf16[1024,2048]{1,0:T(8,128)(2,1)S(1)}) custom-call(s32[1]{0:T(128)} %bitcast.refs_0_.at_ref, bf16[2048,8192]{1,0:T(8,128)(2,1)} %refs_1_.7), custom_call_target="tpu_custom_call" | custom-call | bytes 16777216 | tf_op jit(solution)/shard_map/pallas_call | solution.py:103
  11.6 1.6 %collective-permute-start.2 = (bf16[48,2048]{1,0:T(8,128)(2,1)S(1)}, bf16[48,2048]{1,0:T(8,128)(2,1)S(1)}, u32[]{:S(2)}, u32[]{:S(2)}) collective-permute-start(bf16[48,2048]{1,0:T(8,128)(2,1)S(1)} %shard_map.38.refs_2_), channel_id=1, source_target_pairs={{0,4},{1,5},{2,6},{3,7},{4,0},{5,1},{6,2},{7,3},{8,12},{9,13},{10,... | collective-permute-start | bytes 589832 | tf_op jit(solution)/shard_map/ppermute | solution.py:191
  13.3 1.5 %collective-permute-start.1 = (bf16[48,2048]{1,0:T(8,128)(2,1)S(1)}, bf16[48,2048]{1,0:T(8,128)(2,1)S(1)}, u32[]{:S(2)}, u32[]{:S(2)}) collective-permute-start(bf16[48,2048]{1,0:T(8,128)(2,1)S(1)} %shard_map.38.refs_2_), channel_id=1, source_target_pairs={{0,2},{1,3},{2,0},{3,1},{4,6},{5,7},{6,4},{7,5},{8,10},{9,11},{10,... | collective-permute-start | bytes 589832 | tf_op jit(solution)/shard_map/ppermute | solution.py:191
  14.8 0.7 %collective-permute-start.3 = (bf16[48,2048]{1,0:T(8,128)(2,1)S(1)}, bf16[48,2048]{1,0:T(8,128)(2,1)S(1)}, u32[]{:S(2)}, u32[]{:S(2)}) collective-permute-start(bf16[48,2048]{1,0:T(8,128)(2,1)S(1)} %shard_map.38.refs_2_), channel_id=1, source_target_pairs={{1,7},{3,5},{5,3},{7,1},{8,14},{10,12},{12,10},{14,8},{17,23},{19,... | collective-permute-start | bytes 589832 | tf_op jit(solution)/shard_map/ppermute | solution.py:191
  15.4 3.5 %shard_map.39 = (f32[48,2048]{1,0:T(8,128)S(1)}, bf16[1024,2048]{1,0:T(8,128)(2,1)S(1)}, bf16[1024,2048]{1,0:T(8,128)(2,1)S(1)}) custom-call(s32[1]{0:T(128)} %bitcast.refs_0_.at_ref, bf16[2048,8192]{1,0:T(8,128)(2,1)} %refs_1_.7, bf16[48,2048]{1,0:T(8,128)(2,1)S(1)} %shard_map.38.refs_2_, bf16[1024,2048]{1,0:T(8,128)(2,1)S(1)} %get-tuple-element.25.refs_0_.refs_3_, ...), custom_call_target="tpu_custom_call" | custom-call | flops 402653184 | bytes 16777216 | tf_op jit(solution)/shard_map/pallas_call | solution.py:103
  19.0 0.5 collective-permute-done.2.refs_2_
  19.5 3.0 %shard_map.40 = (f32[48,2048]{1,0:T(8,128)S(1)}, bf16[1024,2048]{1,0:T(8,128)(2,1)S(1)}) custom-call(s32[1]{0:T(128)} %bitcast.refs_0_.at_ref, bf16[2048,8192]{1,0:T(8,128)(2,1)} %refs_1_.7, bf16[48,2048]{1,0:T(8,128)(2,1)S(1)} %collective-permute-done.2.refs_2_, bf16[1024,2048]{1,0:T(8,128)(2,1)S(1)} %get-tuple-element.29.refs_3_, ...), custom_call_target="tpu_custom_call" | custom-call | flops 402653184 | bytes 12582912 | tf_op jit(solution)/shard_map/pallas_call | solution.py:103
  22.5 3.0 %shard_map.41 = (f32[48,2048]{1,0:T(8,128)S(1)}, bf16[1024,2048]{1,0:T(8,128)(2,1)S(1)}) custom-call(s32[1]{0:T(128)} %bitcast.refs_0_.at_ref, bf16[2048,8192]{1,0:T(8,128)(2,1)} %refs_1_.7, bf16[48,2048]{1,0:T(8,128)(2,1)S(1)} %collective-permute-done.1.refs_2_, bf16[1024,2048]{1,0:T(8,128)(2,1)S(1)} %get-tuple-element.27.refs_3_, ...), custom_call_target="tpu_custom_call" | custom-call | flops 402653184 | bytes 12582912 | tf_op jit(solution)/shard_map/pallas_call | solution.py:103
  25.6 0.0 copy-start.2
  25.6 2.7 %shard_map.43 = f32[48,2048]{1,0:T(8,128)S(1)} custom-call(bf16[48,2048]{1,0:T(8,128)(2,1)S(1)} %shard_map.42.refs_0_, bf16[1024,2048]{1,0:T(8,128)(2,1)S(1)} %get-tuple-element.35.refs_1_, bf16[1024,2048]{1,0:T(8,128)(2,1)S(1)} %get-tuple-element.36.refs_2_, f32[48,2048]{1,0:T(8,128)S(1)} %get-tuple-element.33.refs_3_), custom_call_target="tpu_custom_call" | custom-call | flops 402653184 | bytes 8388608 | tf_op jit(solution)/shard_map/pallas_call | solution.py:103
  28.2 0.4 collective-permute-start.4
  28.7 1.4 %collective-permute-done.4 = f32[48,2048]{1,0:T(8,128)S(1)} collective-permute-done((f32[48,2048]{1,0:T(8,128)S(1)}, f32[48,2048]{1,0:T(8,128)S(1)}, u32[]{:S(2)}, u32[]{:S(2)}) %collective-permute-start.4) | collective-permute-done | bytes 393248 | tf_op jit(solution)/shard_map/ppermute | solution.py:191
  30.1 3.5 %collective-permute-start.5 = (bf16[48,2048]{1,0:T(8,128)(2,1)S(1)}, bf16[48,2048]{1,0:T(8,128)(2,1)S(1)}, u32[]{:S(2)}, u32[]{:S(2)}) collective-permute-start(bf16[48,2048]{1,0:T(8,128)(2,1)S(1)} %add_convert_fusion.a_ref), channel_id=1, source_target_pairs={{0,8},{1,6},{2,10},{3,4},{4,12},{5,2},{6,14},{7,0},{8,15},{9,1},{1... | collective-permute-start | bytes 589832 | tf_op jit(solution)/shard_map/ppermute | solution.py:191
  33.6 4.3 %collective-permute-start.8 = (bf16[48,2048]{1,0:T(8,128)(2,1)S(1)}, bf16[48,2048]{1,0:T(8,128)(2,1)S(1)}, u32[]{:S(2)}, u32[]{:S(2)}) collective-permute-start(bf16[48,2048]{1,0:T(8,128)(2,1)S(1)} %add_convert_fusion.a_ref), channel_id=1, source_target_pairs={{0,14},{2,12},{4,10},{6,8},{9,7},{11,5},{13,3},{15,1},{16,30},{18,... | collective-permute-start | bytes 589832 | tf_op jit(solution)/shard_map/ppermute | solution.py:191
  37.9 2.6 %collective-permute-start.7 = (bf16[48,2048]{1,0:T(8,128)(2,1)S(1)}, bf16[48,2048]{1,0:T(8,128)(2,1)S(1)}, u32[]{:S(2)}, u32[]{:S(2)}) collective-permute-start(bf16[48,2048]{1,0:T(8,128)(2,1)S(1)} %shard_map.44.refs_0_), channel_id=1, source_target_pairs={{0,4},{1,5},{2,6},{3,7},{4,0},{5,1},{6,2},{7,3},{8,12},{9,13},{10,... | collective-permute-start | bytes 589832 | tf_op jit(solution)/shard_map/ppermute | solution.py:191
  40.5 1.5 %collective-permute-start.6 = (bf16[48,2048]{1,0:T(8,128)(2,1)S(1)}, bf16[48,2048]{1,0:T(8,128)(2,1)S(1)}, u32[]{:S(2)}, u32[]{:S(2)}) collective-permute-start(bf16[48,2048]{1,0:T(8,128)(2,1)S(1)} %shard_map.44.refs_0_), channel_id=1, source_target_pairs={{0,2},{1,3},{2,0},{3,1},{4,6},{5,7},{6,4},{7,5},{8,10},{9,11},{10,... | collective-permute-start | bytes 589832 | tf_op jit(solution)/shard_map/ppermute | solution.py:191
  42.0 0.7 %collective-permute-done.8.b_ref = bf16[48,2048]{1,0:T(8,128)(2,1)S(1)} collective-permute-done((bf16[48,2048]{1,0:T(8,128)(2,1)S(1)}, bf16[48,2048]{1,0:T(8,128)(2,1)S(1)}, u32[]{:S(2)}, u32[]{:S(2)}) %collective-permute-start.8) | collective-permute-done | bytes 196640 | tf_op jit(solution)/shard_map/ppermute | solution.py:191
  42.7 3.7 %collective-permute-done.7.refs_1_ = bf16[48,2048]{1,0:T(8,128)(2,1)S(1)} collective-permute-done((bf16[48,2048]{1,0:T(8,128)(2,1)S(1)}, bf16[48,2048]{1,0:T(8,128)(2,1)S(1)}, u32[]{:S(2)}, u32[]{:S(2)}) %collective-permute-start.7) | collective-permute-done | bytes 196640 | tf_op jit(solution)/shard_map/ppermute | solution.py:191
  46.4 0.5 shard_map.45.refs_3_
  46.9 0.6 %collective-permute-done.6.refs_2_.refs_0_ = bf16[48,2048]{1,0:T(8,128)(2,1)S(1)} collective-permute-done((bf16[48,2048]{1,0:T(8,128)(2,1)S(1)}, bf16[48,2048]{1,0:T(8,128)(2,1)S(1)}, u32[]{:S(2)}, u32[]{:S(2)}) %collective-permute-start.6) | collective-permute-done | bytes 196640 | tf_op jit(solution)/shard_map/ppermute | solution.py:191
  47.5 1.3 %collective-permute-done.9.refs_3_.refs_1_ = bf16[128,8192]{1,0:T(8,128)(2,1)S(1)} collective-permute-done((bf16[128,8192]{1,0:T(8,128)(2,1)}, bf16[128,8192]{1,0:T(8,128)(2,1)S(1)}, u32[]{:S(2)}, u32[]{:S(2)}) %collective-permute-start.9) | collective-permute-done | bytes 2097184 | tf_op jit(solution)/shard_map/ppermute | solution.py:191
  48.8 0.7 %shard_map.47.refs_2_ = f32[48,128]{1,0:T(8,128)S(1)} custom-call(s32[1]{0:T(128)} %bitcast.refs_0_.at_ref, bf16[48,2048]{1,0:T(8,128)(2,1)S(1)} %shard_map.44.refs_0_, bf16[48,2048]{1,0:T(8,128)(2,1)S(1)} %collective-permute-done.7.refs_1_, bf16[48,2048]{1,0:T(8,128)(2,1)S(1)} %collective-permute-done.6.refs_2_.refs_0_, ...), custom_call_target="tpu_custom_call" | custom-call | flops 75497472 | bytes 1572864 | tf_op jit(solution)/shard_map/pallas_call | solution.py:134
  49.5 0.3 shard_map.48
  49.8 1.8 %collective-permute-start.10 = (f32[48,128]{1,0:T(8,128)S(1)}, f32[48,128]{1,0:T(8,128)S(1)}, u32[]{:S(2)}, u32[]{:S(2)}) collective-permute-start(f32[48,128]{1,0:T(8,128)S(1)} %shard_map.48), channel_id=1, source_target_pairs={{0,16},{1,17},{2,18},{3,19},{4,20},{5,21},{6,22},{7,23},{8,24},{9,... | collective-permute-start | bytes 73736 | tf_op jit(solution)/shard_map/ppermute | solution.py:191
  51.6 1.6 %copy-done.3 = bf16[128,8192]{1,0:T(8,128)(2,1)S(1)} copy-done((bf16[128,8192]{1,0:T(8,128)(2,1)S(1)}, bf16[128,8192]{1,0:T(8,128)(2,1)}, u32[]{:S(2)}) %copy-start.3) | copy-done | bytes 2097176
  53.2 0.5 shard_map.49
  53.6 0.0 collective-permute-done.10
  53.7 0.1 collective-permute-start.11
  53.7 1.2 %collective-permute-done.11 = f32[48,128]{1,0:T(8,128)S(1)} collective-permute-done((f32[48,128]{1,0:T(8,128)S(1)}, f32[48,128]{1,0:T(8,128)S(1)}, u32[]{:S(2)}, u32[]{:S(2)}) %collective-permute-start.11) | collective-permute-done | bytes 24608 | tf_op jit(solution)/shard_map/ppermute | solution.py:191
  54.9 0.6 %select_add_fusion = f32[48,128]{1,0:T(8,128)} fusion(f32[48,128]{1,0:T(8,128)S(1)} %collective-permute-done.11, f32[48,128]{1,0:T(8,128)S(1)} %shard_map.49, f32[48,128]{1,0:T(8,128)S(1)} %collective-permute-done.10, pred[]{:T(512)S(6)} %eq.12), kind=kLoop, calls=%fused_computation.1 | loop fusion | flops 12288 | bytes 98305 | tf_op jit(solution)/shard_map/add | solution.py:263
  (17 shorter events, 0.2 us)
Async XLA Ops:
  0.0 3.0 %copy-start = (bf16[96,2048]{1,0:T(8,128)(2,1)S(1)}, bf16[96,2048]{1,0:T(8,128)(2,1)}, u32[]{:S(2)}) copy-start(bf16[96,2048]{1,0:T(8,128)(2,1)} %param.3) | copy-start | bytes 1179652
  0.0 48.8 %collective-permute-start.9 = (bf16[128,8192]{1,0:T(8,128)(2,1)}, bf16[128,8192]{1,0:T(8,128)(2,1)S(1)}, u32[]{:S(2)}, u32[]{:S(2)}) collective-permute-start(bf16[128,8192]{1,0:T(8,128)(2,1)} %refs_2_.3), channel_id=1, source_target_pairs={{0,16},{1,17},{2,18},{3,19},{4,20},{5,21},{6,22},{7,23},{8,24},{9,... | collective-permute-start | bytes 6291464 | tf_op jit(solution)/shard_map/ppermute | solution.py:191
  3.0 8.6 %collective-permute-start = (bf16[48,2048]{1,0:T(8,128)(2,1)S(1)}, bf16[48,2048]{1,0:T(8,128)(2,1)S(1)}, u32[]{:S(2)}, u32[]{:S(2)}) collective-permute-start(bf16[48,2048]{1,0:T(8,128)(2,1)S(1)} %constant_dynamic-slice_fusion.a_ref), channel_id=1, source_target_pairs={{0,8},{1,6},{2,10},{3,4},{4,12},{5,2},{6,14},{7,0},{8,15},{9,1},{1... | collective-permute-start | bytes 589832 | tf_op jit(solution)/shard_map/ppermute | solution.py:191
  11.6 7.8 %collective-permute-start.2 = (bf16[48,2048]{1,0:T(8,128)(2,1)S(1)}, bf16[48,2048]{1,0:T(8,128)(2,1)S(1)}, u32[]{:S(2)}, u32[]{:S(2)}) collective-permute-start(bf16[48,2048]{1,0:T(8,128)(2,1)S(1)} %shard_map.38.refs_2_), channel_id=1, source_target_pairs={{0,4},{1,5},{2,6},{3,7},{4,0},{5,1},{6,2},{7,3},{8,12},{9,13},{10,... | collective-permute-start | bytes 589832 | tf_op jit(solution)/shard_map/ppermute | solution.py:191
  13.3 9.2 %collective-permute-start.1 = (bf16[48,2048]{1,0:T(8,128)(2,1)S(1)}, bf16[48,2048]{1,0:T(8,128)(2,1)S(1)}, u32[]{:S(2)}, u32[]{:S(2)}) collective-permute-start(bf16[48,2048]{1,0:T(8,128)(2,1)S(1)} %shard_map.38.refs_2_), channel_id=1, source_target_pairs={{0,2},{1,3},{2,0},{3,1},{4,6},{5,7},{6,4},{7,5},{8,10},{9,11},{10,... | collective-permute-start | bytes 589832 | tf_op jit(solution)/shard_map/ppermute | solution.py:191
  14.8 10.7 %collective-permute-start.3 = (bf16[48,2048]{1,0:T(8,128)(2,1)S(1)}, bf16[48,2048]{1,0:T(8,128)(2,1)S(1)}, u32[]{:S(2)}, u32[]{:S(2)}) collective-permute-start(bf16[48,2048]{1,0:T(8,128)(2,1)S(1)} %shard_map.38.refs_2_), channel_id=1, source_target_pairs={{1,7},{3,5},{5,3},{7,1},{8,14},{10,12},{12,10},{14,8},{17,23},{19,... | collective-permute-start | bytes 589832 | tf_op jit(solution)/shard_map/ppermute | solution.py:191
  25.6 20.8 %copy-start.2 = (bf16[128,8192]{1,0:T(8,128)(2,1)S(1)}, bf16[128,8192]{1,0:T(8,128)(2,1)}, u32[]{:S(2)}) copy-start(bf16[128,8192]{1,0:T(8,128)(2,1)} %refs_2_.3) | copy-start | bytes 6291460
  28.2 1.8 %collective-permute-start.4 = (f32[48,2048]{1,0:T(8,128)S(1)}, f32[48,2048]{1,0:T(8,128)S(1)}, u32[]{:S(2)}, u32[]{:S(2)}) collective-permute-start(f32[48,2048]{1,0:T(8,128)S(1)} %shard_map.43), channel_id=1, source_target_pairs={{0,1},{1,0},{2,3},{3,2},{4,5},{5,4},{6,7},{7,6},{8,9},{9,8},{10,11... | collective-permute-start | bytes 1179656 | tf_op jit(solution)/shard_map/ppermute | solution.py:191
  30.1 7.8 %collective-permute-start.5 = (bf16[48,2048]{1,0:T(8,128)(2,1)S(1)}, bf16[48,2048]{1,0:T(8,128)(2,1)S(1)}, u32[]{:S(2)}, u32[]{:S(2)}) collective-permute-start(bf16[48,2048]{1,0:T(8,128)(2,1)S(1)} %add_convert_fusion.a_ref), channel_id=1, source_target_pairs={{0,8},{1,6},{2,10},{3,4},{4,12},{5,2},{6,14},{7,0},{8,15},{9,1},{1... | collective-permute-start | bytes 589832 | tf_op jit(solution)/shard_map/ppermute | solution.py:191
  33.6 9.1 %collective-permute-start.8 = (bf16[48,2048]{1,0:T(8,128)(2,1)S(1)}, bf16[48,2048]{1,0:T(8,128)(2,1)S(1)}, u32[]{:S(2)}, u32[]{:S(2)}) collective-permute-start(bf16[48,2048]{1,0:T(8,128)(2,1)S(1)} %add_convert_fusion.a_ref), channel_id=1, source_target_pairs={{0,14},{2,12},{4,10},{6,8},{9,7},{11,5},{13,3},{15,1},{16,30},{18,... | collective-permute-start | bytes 589832 | tf_op jit(solution)/shard_map/ppermute | solution.py:191
  37.9 8.5 %collective-permute-start.7 = (bf16[48,2048]{1,0:T(8,128)(2,1)S(1)}, bf16[48,2048]{1,0:T(8,128)(2,1)S(1)}, u32[]{:S(2)}, u32[]{:S(2)}) collective-permute-start(bf16[48,2048]{1,0:T(8,128)(2,1)S(1)} %shard_map.44.refs_0_), channel_id=1, source_target_pairs={{0,4},{1,5},{2,6},{3,7},{4,0},{5,1},{6,2},{7,3},{8,12},{9,13},{10,... | collective-permute-start | bytes 589832 | tf_op jit(solution)/shard_map/ppermute | solution.py:191
  40.5 7.0 %collective-permute-start.6 = (bf16[48,2048]{1,0:T(8,128)(2,1)S(1)}, bf16[48,2048]{1,0:T(8,128)(2,1)S(1)}, u32[]{:S(2)}, u32[]{:S(2)}) collective-permute-start(bf16[48,2048]{1,0:T(8,128)(2,1)S(1)} %shard_map.44.refs_0_), channel_id=1, source_target_pairs={{0,2},{1,3},{2,0},{3,1},{4,6},{5,7},{6,4},{7,5},{8,10},{9,11},{10,... | collective-permute-start | bytes 589832 | tf_op jit(solution)/shard_map/ppermute | solution.py:191
  46.4 9.2 %copy-start.1 = (bf16[96,2048]{1,0:T(8,128)(2,1)S(1)}, bf16[96,2048]{1,0:T(8,128)(2,1)}, u32[]{:S(2)}) copy-start(bf16[96,2048]{1,0:T(8,128)(2,1)} %param.3) | copy-start | bytes 1179652
  49.8 3.9 %collective-permute-start.10 = (f32[48,128]{1,0:T(8,128)S(1)}, f32[48,128]{1,0:T(8,128)S(1)}, u32[]{:S(2)}, u32[]{:S(2)}) collective-permute-start(f32[48,128]{1,0:T(8,128)S(1)} %shard_map.48), channel_id=1, source_target_pairs={{0,16},{1,17},{2,18},{3,19},{4,20},{5,21},{6,22},{7,23},{8,24},{9,... | collective-permute-start | bytes 73736 | tf_op jit(solution)/shard_map/ppermute | solution.py:191
  51.6 1.6 %copy-start.3 = (bf16[128,8192]{1,0:T(8,128)(2,1)S(1)}, bf16[128,8192]{1,0:T(8,128)(2,1)}, u32[]{:S(2)}) copy-start(bf16[128,8192]{1,0:T(8,128)(2,1)} %refs_2_.3) | copy-start | bytes 6291460
  53.7 1.3 %collective-permute-start.11 = (f32[48,128]{1,0:T(8,128)S(1)}, f32[48,128]{1,0:T(8,128)S(1)}, u32[]{:S(2)}, u32[]{:S(2)}) collective-permute-start(f32[48,128]{1,0:T(8,128)S(1)} %broadcast_select_fusion), channel_id=1, source_target_pairs={{0,1},{1,0},{2,3},{3,2},{4,5},{5,4},{6,7},{7,6},{8,9},{9,8},{10,11... | collective-permute-start | bytes 73736 | tf_op jit(solution)/shard_map/ppermute | solution.py:191

commit v19 on v17

--- a/solution.py
+++ b/solution.py
@@ -10,7 +10,6 @@
 AXES = ("grp", "ex", "dim")
 NT = (((1,), (1,)), ((), ()))
 VMEM = pl.BlockSpec(memory_space=pltpu.VMEM)
-SMEM = pl.BlockSpec(memory_space=pltpu.SMEM)
 HBM = pl.BlockSpec(memory_space=pltpu.HBM)
 ANY = pl.BlockSpec(memory_space=pl.ANY)
 
@@ -33,8 +32,14 @@
     return lax.psum_scatter(partial_scores, "dim", scatter_dimension=0, tiled=True)
 
 
-def scalar(value):
-    return jnp.asarray(value, jnp.int32).reshape(1)
+class Place:
+    def __init__(self, nz, nx):
+        self.y, e, self.d = (lax.axis_index(a) for a in AXES)
+        z, x = lax.div(e, nx), lax.rem(e, nx)
+        u = jnp.where(self.d == 0, z, nz - 1 - z)
+        self.owner = u < nz // 2
+        local = jnp.where(self.d == 0, lax.rem(u, 2), nz // 2 - 1 - lax.rem(u, 2))
+        self.column = local * nx + x
 
 
 ORDER = (0, 2, 1, 3)
@@ -61,16 +66,17 @@
     return lax.dot_general(chunk_ref[...], fisher, NT, preferred_element_type=jnp.float32)
 
 
-def fisher_kernel(n_in, has_base, fetch, *refs):
+def fisher_kernel(dims, n_in, has_base, fetch, *refs):
     if fetch:
-        at_ref, fisher_ref, *refs = refs
+        column = Place(*dims).column
+        fisher_ref, *refs = refs
     chunk_ref, halves = (refs[0], refs[1:3]) if n_in else (None, ())
     base_ref = refs[3] if has_base else None
     outs, sem = refs[n_in + has_base : -1], refs[-1]
     held = outs[1:] if n_in else outs
     copies = []
     for k, (piece, half) in enumerate(fetch):
-        for copy in half_copies(fisher_ref, at_ref[0] ^ ORDER[piece], half, held[k], sem.at[k]):
+        for copy in half_copies(fisher_ref, column ^ ORDER[piece], half, held[k], sem.at[k]):
             copy.start()
             copies.append(copy)
 
@@ -93,7 +99,7 @@
         copy.wait()
 
 
-def fisher_step(fisher, first, width, fetch, chunk=None, halves=(), base=None):
+def fisher_step(fisher, dims, width, fetch, chunk=None, halves=(), base=None):
     rows = fisher.shape[0]
     ins = [] if chunk is None else [chunk, *halves]
     has_base = base is not None
@@ -101,9 +107,9 @@
     out_shape = [] if chunk is None else [jax.ShapeDtypeStruct((chunk.shape[0], rows), jnp.float32)]
     out_shape += [held] * len(fetch)
     return pl.pallas_call(
-        functools.partial(fisher_kernel, len(ins), has_base, fetch),
+        functools.partial(fisher_kernel, dims, len(ins), has_base, fetch),
         out_shape=out_shape,
-        in_specs=[SMEM, HBM][: 2 * bool(fetch)] + [VMEM] * (len(ins) + has_base),
+        in_specs=[HBM] * bool(fetch) + [VMEM] * (len(ins) + has_base),
         out_specs=[VMEM] * len(out_shape),
         scratch_shapes=[pltpu.SemaphoreType.DMA((max(len(fetch), 1), 2))],
         compiler_params=limit(34 if chunk is None else 20),
@@ -112,30 +118,31 @@
             bytes_accessed=width * rows * (len(fetch) + 2 * bool(ins)),
             transcendentals=0,
         ),
-    )(*((scalar(first), fisher) if fetch else ()), *ins, *([base] if has_base else []))
-
-
-def score_kernel(order, relative, has_base, at_ref, *refs):
+    )(*([fisher] if fetch else []), *ins, *([base] if has_base else []))
+
+
+def score_kernel(dims, order, has_base, *refs):
     n = len(order)
+    column = Place(*dims).column if dims else 0
     grads_ref, out_ref = refs[n], refs[-1]
     width = refs[0].shape[1]
     total = refs[n + 1][...] if has_base else None
     for k in range(n):
-        block = at_ref[0] ^ order[k] if relative else order[k]
-        start = pl.multiple_of(block * width, width)
+        block = column ^ order[k]
+        start = pl.multiple_of(block * width, width) if dims else block * width
         term = times(refs[k], grads_ref[:, pl.ds(start, width)])
         total = term if total is None else total + term
     out_ref[...] = total
 
 
-def score_dot(pieces, order, first, grads, base=None):
+def score_dot(pieces, order, dims, grads, base=None):
     n = len(pieces)
     rows, width = pieces[0].shape
     operands = [*pieces, grads] + ([] if base is None else [base])
     return pl.pallas_call(
-        functools.partial(score_kernel, order, first is not None, base is not None),
+        functools.partial(score_kernel, dims, order, base is not None),
         out_shape=jax.ShapeDtypeStruct((rows, grads.shape[0]), jnp.float32),
-        in_specs=[SMEM] + [VMEM] * len(operands),
+        in_specs=[VMEM] * len(operands),
         out_specs=VMEM,
         compiler_params=limit(8),
         cost_estimate=pl.CostEstimate(
@@ -143,14 +150,15 @@
             bytes_accessed=2 * n * width * grads.shape[0],
             transcendentals=0,
         ),
-    )(scalar(0 if first is None else first), *operands)
-
-
-def cut_kernel(order, at_ref, src_ref, out_ref, sem):
+    )(*operands)
+
+
+def cut_kernel(dims, order, src_ref, out_ref, sem):
+    column = Place(*dims).column
     width = out_ref.shape[1] // len(order)
     copies = []
     for k, mask in enumerate(order):
-        start = pl.multiple_of((at_ref[0] ^ mask) * width, width)
+        start = pl.multiple_of((column ^ mask) * width, width)
         copies.append(
             pltpu.make_async_copy(
                 src_ref.at[:, pl.ds(start, width)], out_ref.at[:, k * width : (k + 1) * width], sem.at[k]
@@ -161,53 +169,66 @@
         copy.wait()
 
 
-def cut(src, order, first, width):
+def cut(src, order, dims, width):
     n = len(order)
     return pl.pallas_call(
-        functools.partial(cut_kernel, order),
+        functools.partial(cut_kernel, dims, order),
         out_shape=jax.ShapeDtypeStruct((src.shape[0], n * width), src.dtype),
-        in_specs=[SMEM, HBM],
+        in_specs=[HBM],
         out_specs=VMEM,
         scratch_shapes=[pltpu.SemaphoreType.DMA((n,))],
         compiler_params=limit(51),
         cost_estimate=pl.CostEstimate(
             flops=0, bytes_accessed=2 * n * width * src.shape[0], transcendentals=0
         ),
-    )(scalar(first), src)
-
-
-def pick_kernel(at_ref, a_ref, b_ref, *refs):
+    )(src)
+
+
+def pick_kernel(dims, mine_ref, other_ref, *refs):
     out_ref = refs[-1]
-
-    @pl.when(at_ref[0] == 1)
+    owner = Place(*dims).owner
+
+    @pl.when(owner)
     def _():
-        out_ref[...] = a_ref[...]
-
-    @pl.when(at_ref[0] != 1)
+        out_ref[...] = mine_ref[...]
+
+    @pl.when(jnp.logical_not(owner))
     def _():
-        out_ref[...] = b_ref[...]
-
-
-def pick(condition, a, b, after=()):
-    return pl.pallas_call(
-        pick_kernel,
-        out_shape=jax.ShapeDtypeStruct(a.shape, a.dtype),
-        in_specs=[SMEM] + [VMEM] * 2 + [ANY] * len(after),
+        out_ref[...] = other_ref[...]
+
+
+def pick(dims, mine, other, after=()):
+    return pl.pallas_call(
+        functools.partial(pick_kernel, dims),
+        out_shape=jax.ShapeDtypeStruct(mine.shape, mine.dtype),
+        in_specs=[VMEM] * 2 + [ANY] * len(after),
         out_specs=VMEM,
         compiler_params=limit(2),
-        cost_estimate=pl.CostEstimate(flops=0, bytes_accessed=2 * a.size * 2, transcendentals=0),
-    )(scalar(condition), a, b, *after)
+        cost_estimate=pl.CostEstimate(flops=0, bytes_accessed=4 * mine.size, transcendentals=0),
+    )(mine, other, *after)
+
+
+def sort_kernel(mine_ref, other_ref, theirs_ref, keep_ref, give_ref):
+    here = lax.axis_index("dim") == lax.axis_index("grp")
+    mine, other = mine_ref[...], other_ref[...] + theirs_ref[...]
+    keep_ref[...] = jnp.where(here, mine, other)
+    give_ref[...] = jnp.where(here, other, mine)
+
+
+def sort_out(mine, other, theirs):
+    return pl.pallas_call(
+        sort_kernel,
+        out_shape=[jax.ShapeDtypeStruct(mine.shape, mine.dtype)] * 2,
+        in_specs=[VMEM] * 3,
+        out_specs=[VMEM] * 2,
+        compiler_params=limit(2),
+    )(mine, other, theirs)
 
 
 def per_device_quad(nz, nx, ny, queries, inverse_fisher, stored_grads):
-    nex = nz * nx
+    nex, dims = nz * nx, (nz, nx)
     near = nz // 2
     nq = queries.shape[0]
-    y, e, d = (lax.axis_index(a) for a in AXES)
-    z = e // nx
-    x = e % nx
-    u = jnp.where(d == 0, z, nz - 1 - z)
-    owner = u < near
 
     def move(value, target):
         pairs = []
@@ -247,55 +268,49 @@
         came = move(own, start)
         if direct:
             corner = along_z(own, {0: 3, 1: 2}, True)
-        first = pick(owner, own, came, after)
-        beside = along_z(first, {0: 1, 1: 0, 2: 3, 3: 2})
+        first = pick(dims, own, came, after)
+        pairs = {0: 1, 1: 0, 2: 3, 3: 2}
+        beside = along_z(first, pairs)
+        across = along_z(first, {0: 0, 1: 1, 2: 2, 3: 3}, True)
         if direct:
             beside, corner = lax.optimization_barrier((beside, corner))
-        across = along_z(first, {0: 0, 1: 1, 2: 2, 3: 3}, True)
+        else:
+            corner = along_z(first, {2: 3, 3: 2}, True)
 
         def last(after):
-            if direct:
-                piece, _ = lax.optimization_barrier((corner, after))
-            else:
-                ready, _ = lax.optimization_barrier((beside, after))
-                piece = along_z(ready, {2: 2, 3: 3}, True)
-            return pick(owner, came, piece)
+            ready, _ = lax.optimization_barrier((came, after))
+            return pick(dims, ready, corner)
 
         return first, beside, across, last
 
-    plane = jnp.where(d == 0, u % 2, nz - 1 - u % 2)
-    column = plane * nx + x - d * (nex // 2)
-
     rows, width = nq // ny, queries.shape[1]
-    to_y = cut(stored_grads, ORDER[1:], column, width)
+    to_y = cut(stored_grads, ORDER[1:], dims, width)
     queries, to_y = lax.optimization_barrier((queries, to_y))
-    own = lax.dynamic_slice_in_dim(queries, y * rows, rows, axis=0)
+    own = lax.dynamic_slice_in_dim(queries, lax.axis_index("grp") * rows, rows, axis=0)
     own, to_y = lax.optimization_barrier((own, to_y))
     other_grads = swap_y(to_y)
-    step = functools.partial(fisher_step, inverse_fisher, column, width)
+    step = functools.partial(fisher_step, inverse_fisher, dims, width)
     a0, a1, b0, b1 = step(((0, 0), (0, 1), (1, 0), (1, 1)))
     q0, q1, q2, last = gather(own, False, (a0,))
     total, c0, c1 = step(((2, 0), (2, 1)), q0, (a0, a1))
     total, d0 = step(((3, 0),), q1, (b0, b1), total)
-    q3 = last(total)
     total, d1 = step(((3, 1),), q2, (c0, c1), total)
-    (total,) = step((), q3, (d0, d1), total)
+    (total,) = step((), last(total), (d0, d1), total)
     panel = (total + swap_core(total)).astype(jnp.bfloat16)
 
-    p0, p1, p2, last = gather(panel, True, (other_grads,))
+    p0, p1, p2, last = gather(panel, True)
     swapped = swap_y(p0)
-    mine = score_dot([p0, p1], ORDER[:2], column, stored_grads)
+    p1, other_grads = lax.optimization_barrier((p1, other_grads))
+    mine = score_dot([p0, p1], ORDER[:2], dims, stored_grads)
     p2, _ = lax.optimization_barrier((p2, mine))
     other = score_dot([p1, p2], (0, 1), None, other_grads)
     p3 = last(other)
     other = score_dot([p3], (2,), None, other_grads, other)
     p2, p3, mine, swapped, _ = lax.optimization_barrier((p2, p3, mine, swapped, other))
-    mine = score_dot([p2, p3], ORDER[2:], column, stored_grads, mine)
-    theirs = score_dot([swapped], ORDER[:1], column, stored_grads)
-
-    other = swap_y(other) + theirs
-    keep = jnp.where(d == y, mine, other)
-    give = jnp.where(d == y, other, mine)
+    mine = score_dot([p2, p3], ORDER[2:], dims, stored_grads, mine)
+    theirs = score_dot([swapped], ORDER[:1], dims, stored_grads)
+
+    keep, give = sort_out(mine, swap_y(other), theirs)
     return keep + swap_core(give)
 
 

time: 74.5 us -> 54.4 us (0.73)
  local copies, waits for them, and re-layouts: 14.6 us -> 0.05 us
  Pallas kernels: 25.8 us -> 21.7 us
  waiting for transfers between devices: 10.1 us -> 8.11 us
  starting transfers between devices: 22.7 us -> 23.5 us
    unnamed x24 -> x6, local copies, waits for them, and re-layouts: 14.6 us -> 0.04 us
    pallas_call x15 -> x16, Pallas kernels: 25.8 us -> 21.7 us  [the longest x5 18.2 us: fisher_step(): pl.pallas_call(functools.partial(fisher_kernel, dims, len(ins), has_base,...]
    ppermute x13, waiting for transfers between devices: 10.1 us -> 8.11 us  [move(): return lax.ppermute(value, AXES, pairs)]
    ppermute x13, starting transfers between devices: 22.7 us -> 23.5 us  [move(): return lax.ppermute(value, AXES, pairs)]
  transfers between devices with their start and end apart: 13 -> 13, of which waited for: 5 -> 6; matrix products, arithmetic and copies ran while one was open for 0% -> 0% of each run, Pallas kernels for 31% -> 37%
where the time goes in v19:
time: 54.4 us; the launch traced here: 54.2 us
  starting transfers between devices  23.5 us (43%)
  Pallas kernels  21.7 us (40%)
  waiting for transfers between devices  8.11 us (15%)
  other arithmetic  0.65 us (1%)
    ppermute x13, starting transfers between devices, move(): return lax.ppermute(value, AXES, pairs)  23.5 us
    pallas_call x5, Pallas kernels, fisher_step(): pl.pallas_call(functools.partial(fisher_kernel, dims, len(ins), has_base,...  18.2 us
    ppermute x13, waiting for transfers between devices, move(): return lax.ppermute(value, AXES, pairs)  8.11 us
    pallas_call x5, Pallas kernels, score_dot(): pl.pallas_call(functools.partial(score_kernel, dims, order, base is not N...  2 us
    pallas_call x1, Pallas kernels, cut(): pl.pallas_call(functools.partial(cut_kernel, dims, order), out_shape=jax....  1.43 us
  transfers between devices with their start and end apart: 13, of which 6 were waited for; matrix products, arithmetic and copies ran while one was open for 0% of the time, Pallas kernels for 37%

profile of v19, /device:TPU:0, one launch (start us, length us, event | category | flops | bytes accessed | tf_op | source)
XLA Modules:
  0.0 54.2 jit_solution(7521971744497958292)
XLA Ops:
  0.0 1.4 %shard_map.37 = bf16[128,6144]{1,0:T(8,128)(2,1)S(1)} custom-call(bf16[128,8192]{1,0:T(8,128)(2,1)} %refs_1_.1), custom_call_target="tpu_custom_call" | custom-call | bytes 1572864 | tf_op jit(solution)/shard_map/pallas_call | solution.py:174
  1.4 0.0 copy-done
  1.5 4.1 %collective-permute-start = (bf16[48,2048]{1,0:T(8,128)(2,1)S(1)}, bf16[48,2048]{1,0:T(8,128)(2,1)S(1)}, u32[]{:S(2)}, u32[]{:S(2)}) collective-permute-start(bf16[48,2048]{1,0:T(8,128)(2,1)S(1)} %constant_dynamic-slice_fusion.mine_ref), channel_id=1, source_target_pairs={{0,8},{1,6},{2,10},{3,4},{4,12},{5,2},{6,14},{7,0},{8,15},{9,1},{1... | collective-permute-start | bytes 589832 | tf_op jit(solution)/shard_map/ppermute | solution.py:243
  5.6 1.5 %collective-permute-start.9 = (bf16[128,6144]{1,0:T(8,128)(2,1)S(1)}, bf16[128,6144]{1,0:T(8,128)(2,1)S(1)}, u32[]{:S(2)}, u32[]{:S(2)}) collective-permute-start(bf16[128,6144]{1,0:T(8,128)(2,1)S(1)} %shard_map.37), channel_id=1, source_target_pairs={{0,16},{1,17},{2,18},{3,19},{4,20},{5,21},{6,22},{7,23},{8,24},{9,... | collective-permute-start | bytes 4718600 | tf_op jit(solution)/shard_map/ppermute | solution.py:243
  7.1 6.0 %shard_map.38 = (bf16[1024,2048]{1,0:T(8,128)(2,1)S(1)}, bf16[1024,2048]{1,0:T(8,128)(2,1)S(1)}, bf16[1024,2048]{1,0:T(8,128)(2,1)S(1)}, bf16[1024,2048]{1,0:T(8,128)(2,1)S(1)}) custom-call(bf16[2048,8192]{1,0:T(8,128)(2,1)} %refs_0_.7), custom_call_target="tpu_custom_call" | custom-call | bytes 16777216 | tf_op jit(solution)/shard_map/pallas_call | solution.py:109
  13.1 1.6 %collective-permute-start.2 = (bf16[48,2048]{1,0:T(8,128)(2,1)S(1)}, bf16[48,2048]{1,0:T(8,128)(2,1)S(1)}, u32[]{:S(2)}, u32[]{:S(2)}) collective-permute-start(bf16[48,2048]{1,0:T(8,128)(2,1)S(1)} %shard_map.39.refs_1_), channel_id=1, source_target_pairs={{0,4},{1,5},{2,6},{3,7},{4,0},{5,1},{6,2},{7,3},{8,12},{9,13},{10,... | collective-permute-start | bytes 589832 | tf_op jit(solution)/shard_map/ppermute | solution.py:243
  14.8 1.5 %collective-permute-start.1 = (bf16[48,2048]{1,0:T(8,128)(2,1)S(1)}, bf16[48,2048]{1,0:T(8,128)(2,1)S(1)}, u32[]{:S(2)}, u32[]{:S(2)}) collective-permute-start(bf16[48,2048]{1,0:T(8,128)(2,1)S(1)} %shard_map.39.refs_1_), channel_id=1, source_target_pairs={{0,2},{1,3},{2,0},{3,1},{4,6},{5,7},{6,4},{7,5},{8,10},{9,11},{10,... | collective-permute-start | bytes 589832 | tf_op jit(solution)/shard_map/ppermute | solution.py:243
  16.3 0.7 %collective-permute-start.3 = (bf16[48,2048]{1,0:T(8,128)(2,1)S(1)}, bf16[48,2048]{1,0:T(8,128)(2,1)S(1)}, u32[]{:S(2)}, u32[]{:S(2)}) collective-permute-start(bf16[48,2048]{1,0:T(8,128)(2,1)S(1)} %shard_map.39.refs_1_), channel_id=1, source_target_pairs={{1,7},{3,5},{5,3},{7,1},{8,14},{10,12},{12,10},{14,8},{17,23},{19,... | collective-permute-start | bytes 589832 | tf_op jit(solution)/shard_map/ppermute | solution.py:243
  16.9 3.5 %shard_map.40 = (f32[48,2048]{1,0:T(8,128)S(1)}, bf16[1024,2048]{1,0:T(8,128)(2,1)S(1)}, bf16[1024,2048]{1,0:T(8,128)(2,1)S(1)}) custom-call(bf16[2048,8192]{1,0:T(8,128)(2,1)} %refs_0_.7, bf16[48,2048]{1,0:T(8,128)(2,1)S(1)} %shard_map.39.refs_1_, bf16[1024,2048]{1,0:T(8,128)(2,1)S(1)} %get-tuple-element.36.refs_0_.refs_2_, ...), custom_call_target="tpu_custom_call" | custom-call | flops 402653184 | bytes 16777216 | tf_op jit(solution)/shard_map/pallas_call | solution.py:109
  20.5 0.2 collective-permute-done.2.refs_1_
  20.7 3.0 %shard_map.41 = (f32[48,2048]{1,0:T(8,128)S(1)}, bf16[1024,2048]{1,0:T(8,128)(2,1)S(1)}) custom-call(bf16[2048,8192]{1,0:T(8,128)(2,1)} %refs_0_.7, bf16[48,2048]{1,0:T(8,128)(2,1)S(1)} %collective-permute-done.2.refs_1_, bf16[1024,2048]{1,0:T(8,128)(2,1)S(1)} %get-tuple-element.40.refs_2_, bf16[1024,2048]{1,0:T(8,128)(2,1)S(1)} %get-tuple-element.41.refs_3_, ...), custom_call_target="tpu_custom_call" | custom-call | flops 402653184 | bytes 12582912 | tf_op jit(solution)/shard_map/pallas_call | solution.py:109
  23.7 3.0 %shard_map.42 = (f32[48,2048]{1,0:T(8,128)S(1)}, bf16[1024,2048]{1,0:T(8,128)(2,1)S(1)}) custom-call(bf16[2048,8192]{1,0:T(8,128)(2,1)} %refs_0_.7, bf16[48,2048]{1,0:T(8,128)(2,1)S(1)} %collective-permute-done.1.refs_1_, bf16[1024,2048]{1,0:T(8,128)(2,1)S(1)} %get-tuple-element.38.refs_2_, bf16[1024,2048]{1,0:T(8,128)(2,1)S(1)} %get-tuple-element.39.refs_3_, ...), custom_call_target="tpu_custom_call" | custom-call | flops 402653184 | bytes 12582912 | tf_op jit(solution)/shard_map/pallas_call | solution.py:109
  26.8 2.6 %shard_map.44 = f32[48,2048]{1,0:T(8,128)S(1)} custom-call(bf16[48,2048]{1,0:T(8,128)(2,1)S(1)} %shard_map.43.refs_0_, bf16[1024,2048]{1,0:T(8,128)(2,1)S(1)} %get-tuple-element.46.refs_1_, bf16[1024,2048]{1,0:T(8,128)(2,1)S(1)} %get-tuple-element.47.refs_2_, f32[48,2048]{1,0:T(8,128)S(1)} %get-tuple-element.44.refs_3_), custom_call_target="tpu_custom_call" | custom-call | flops 402653184 | bytes 8388608 | tf_op jit(solution)/shard_map/pallas_call | solution.py:109
  29.4 0.5 collective-permute-start.4
  29.9 1.3 %collective-permute-done.4 = f32[48,2048]{1,0:T(8,128)S(1)} collective-permute-done((f32[48,2048]{1,0:T(8,128)S(1)}, f32[48,2048]{1,0:T(8,128)S(1)}, u32[]{:S(2)}, u32[]{:S(2)}) %collective-permute-start.4) | collective-permute-done | bytes 393248 | tf_op jit(solution)/shard_map/ppermute | solution.py:243
  31.3 3.5 %collective-permute-start.5 = (bf16[48,2048]{1,0:T(8,128)(2,1)S(1)}, bf16[48,2048]{1,0:T(8,128)(2,1)S(1)}, u32[]{:S(2)}, u32[]{:S(2)}) collective-permute-start(bf16[48,2048]{1,0:T(8,128)(2,1)S(1)} %add_convert_fusion.mine_ref), channel_id=1, source_target_pairs={{0,8},{1,6},{2,10},{3,4},{4,12},{5,2},{6,14},{7,0},{8,15},{9,1},{1... | collective-permute-start | bytes 589832 | tf_op jit(solution)/shard_map/ppermute | solution.py:243
  34.8 4.0 %collective-permute-start.8 = (bf16[48,2048]{1,0:T(8,128)(2,1)S(1)}, bf16[48,2048]{1,0:T(8,128)(2,1)S(1)}, u32[]{:S(2)}, u32[]{:S(2)}) collective-permute-start(bf16[48,2048]{1,0:T(8,128)(2,1)S(1)} %add_convert_fusion.mine_ref), channel_id=1, source_target_pairs={{0,14},{2,12},{4,10},{6,8},{9,7},{11,5},{13,3},{15,1},{16,30},{18,... | collective-permute-start | bytes 589832 | tf_op jit(solution)/shard_map/ppermute | solution.py:243
  38.8 2.0 %collective-permute-start.7 = (bf16[48,2048]{1,0:T(8,128)(2,1)S(1)}, bf16[48,2048]{1,0:T(8,128)(2,1)S(1)}, u32[]{:S(2)}, u32[]{:S(2)}) collective-permute-start(bf16[48,2048]{1,0:T(8,128)(2,1)S(1)} %shard_map.45.refs_0_), channel_id=1, source_target_pairs={{0,4},{1,5},{2,6},{3,7},{4,0},{5,1},{6,2},{7,3},{8,12},{9,13},{10,... | collective-permute-start | bytes 589832 | tf_op jit(solution)/shard_map/ppermute | solution.py:243
  40.9 1.3 %collective-permute-start.6 = (bf16[48,2048]{1,0:T(8,128)(2,1)S(1)}, bf16[48,2048]{1,0:T(8,128)(2,1)S(1)}, u32[]{:S(2)}, u32[]{:S(2)}) collective-permute-start(bf16[48,2048]{1,0:T(8,128)(2,1)S(1)} %shard_map.45.refs_0_), channel_id=1, source_target_pairs={{0,2},{1,3},{2,0},{3,1},{4,6},{5,7},{6,4},{7,5},{8,10},{9,11},{10,... | collective-permute-start | bytes 589832 | tf_op jit(solution)/shard_map/ppermute | solution.py:243
  42.2 1.3 %collective-permute-start.10 = (bf16[48,2048]{1,0:T(8,128)(2,1)S(1)}, bf16[48,2048]{1,0:T(8,128)(2,1)S(1)}, u32[]{:S(2)}, u32[]{:S(2)}) collective-permute-start(bf16[48,2048]{1,0:T(8,128)(2,1)S(1)} %shard_map.45.refs_0_), channel_id=1, source_target_pairs={{0,16},{1,17},{2,18},{3,19},{4,20},{5,21},{6,22},{7,23},{8,24},{9,... | collective-permute-start | bytes 589832 | tf_op jit(solution)/shard_map/ppermute | solution.py:243
  43.5 2.7 %collective-permute-done.7.refs_1_.refs_0_ = bf16[48,2048]{1,0:T(8,128)(2,1)S(1)} collective-permute-done((bf16[48,2048]{1,0:T(8,128)(2,1)S(1)}, bf16[48,2048]{1,0:T(8,128)(2,1)S(1)}, u32[]{:S(2)}, u32[]{:S(2)}) %collective-permute-start.7) | collective-permute-done | bytes 196640 | tf_op jit(solution)/shard_map/ppermute | solution.py:243
  46.2 0.5 shard_map.46.refs_3_
  46.7 1.0 %collective-permute-done.6.refs_1_.refs_0_ = bf16[48,2048]{1,0:T(8,128)(2,1)S(1)} collective-permute-done((bf16[48,2048]{1,0:T(8,128)(2,1)S(1)}, bf16[48,2048]{1,0:T(8,128)(2,1)S(1)}, u32[]{:S(2)}, u32[]{:S(2)}) %collective-permute-start.6) | collective-permute-done | bytes 196640 | tf_op jit(solution)/shard_map/ppermute | solution.py:243
  47.7 0.5 shard_map.47.refs_2_
  48.2 0.3 shard_map.49
  48.5 1.4 %collective-permute-start.11 = (f32[48,128]{1,0:T(8,128)S(1)}, f32[48,128]{1,0:T(8,128)S(1)}, u32[]{:S(2)}, u32[]{:S(2)}) collective-permute-start(f32[48,128]{1,0:T(8,128)S(1)} %shard_map.49), channel_id=1, source_target_pairs={{0,16},{1,17},{2,18},{3,19},{4,20},{5,21},{6,22},{7,23},{8,24},{9,... | collective-permute-start | bytes 73736 | tf_op jit(solution)/shard_map/ppermute | solution.py:243
  49.8 0.3 shard_map.51.theirs_ref
  50.1 0.5 shard_map.50.mine_ref
  50.6 1.7 %collective-permute-done.11.other_ref = f32[48,128]{1,0:T(8,128)S(1)} collective-permute-done((f32[48,128]{1,0:T(8,128)S(1)}, f32[48,128]{1,0:T(8,128)S(1)}, u32[]{:S(2)}, u32[]{:S(2)}) %collective-permute-start.11) | collective-permute-done | bytes 24608 | tf_op jit(solution)/shard_map/ppermute | solution.py:243
  52.4 0.1 collective-permute-start.12
  52.4 1.2 %collective-permute-done.12 = f32[48,128]{1,0:T(8,128)S(1)} collective-permute-done((f32[48,128]{1,0:T(8,128)S(1)}, f32[48,128]{1,0:T(8,128)S(1)}, u32[]{:S(2)}, u32[]{:S(2)}) %collective-permute-start.12) | collective-permute-done | bytes 24608 | tf_op jit(solution)/shard_map/ppermute | solution.py:243
  53.6 0.6 %add.11 = f32[48,128]{1,0:T(8,128)} add(f32[48,128]{1,0:T(8,128)S(1)} %get-tuple-element.59, f32[48,128]{1,0:T(8,128)S(1)} %collective-permute-done.12) | non-fusion elementwise | flops 6144 | bytes 73728 | tf_op jit(solution)/shard_map/add | solution.py:314
  (19 shorter events, 0.2 us)
Async XLA Ops:
  0.0 1.5 %copy-start = (bf16[96,2048]{1,0:T(8,128)(2,1)S(1)}, bf16[96,2048]{1,0:T(8,128)(2,1)}, u32[]{:S(2)}) copy-start(bf16[96,2048]{1,0:T(8,128)(2,1)} %param.3) | copy-start | bytes 1179652
  1.5 11.6 %collective-permute-start = (bf16[48,2048]{1,0:T(8,128)(2,1)S(1)}, bf16[48,2048]{1,0:T(8,128)(2,1)S(1)}, u32[]{:S(2)}, u32[]{:S(2)}) collective-permute-start(bf16[48,2048]{1,0:T(8,128)(2,1)S(1)} %constant_dynamic-slice_fusion.mine_ref), channel_id=1, source_target_pairs={{0,8},{1,6},{2,10},{3,4},{4,12},{5,2},{6,14},{7,0},{8,15},{9,1},{1... | collective-permute-start | bytes 589832 | tf_op jit(solution)/shard_map/ppermute | solution.py:243
  5.6 40.6 %collective-permute-start.9 = (bf16[128,6144]{1,0:T(8,128)(2,1)S(1)}, bf16[128,6144]{1,0:T(8,128)(2,1)S(1)}, u32[]{:S(2)}, u32[]{:S(2)}) collective-permute-start(bf16[128,6144]{1,0:T(8,128)(2,1)S(1)} %shard_map.37), channel_id=1, source_target_pairs={{0,16},{1,17},{2,18},{3,19},{4,20},{5,21},{6,22},{7,23},{8,24},{9,... | collective-permute-start | bytes 4718600 | tf_op jit(solution)/shard_map/ppermute | solution.py:243
  13.1 7.5 %collective-permute-start.2 = (bf16[48,2048]{1,0:T(8,128)(2,1)S(1)}, bf16[48,2048]{1,0:T(8,128)(2,1)S(1)}, u32[]{:S(2)}, u32[]{:S(2)}) collective-permute-start(bf16[48,2048]{1,0:T(8,128)(2,1)S(1)} %shard_map.39.refs_1_), channel_id=1, source_target_pairs={{0,4},{1,5},{2,6},{3,7},{4,0},{5,1},{6,2},{7,3},{8,12},{9,13},{10,... | collective-permute-start | bytes 589832 | tf_op jit(solution)/shard_map/ppermute | solution.py:243
  14.8 8.9 %collective-permute-start.1 = (bf16[48,2048]{1,0:T(8,128)(2,1)S(1)}, bf16[48,2048]{1,0:T(8,128)(2,1)S(1)}, u32[]{:S(2)}, u32[]{:S(2)}) collective-permute-start(bf16[48,2048]{1,0:T(8,128)(2,1)S(1)} %shard_map.39.refs_1_), channel_id=1, source_target_pairs={{0,2},{1,3},{2,0},{3,1},{4,6},{5,7},{6,4},{7,5},{8,10},{9,11},{10,... | collective-permute-start | bytes 589832 | tf_op jit(solution)/shard_map/ppermute | solution.py:243
  16.3 10.5 %collective-permute-start.3 = (bf16[48,2048]{1,0:T(8,128)(2,1)S(1)}, bf16[48,2048]{1,0:T(8,128)(2,1)S(1)}, u32[]{:S(2)}, u32[]{:S(2)}) collective-permute-start(bf16[48,2048]{1,0:T(8,128)(2,1)S(1)} %shard_map.39.refs_1_), channel_id=1, source_target_pairs={{1,7},{3,5},{5,3},{7,1},{8,14},{10,12},{12,10},{14,8},{17,23},{19,... | collective-permute-start | bytes 589832 | tf_op jit(solution)/shard_map/ppermute | solution.py:243
  26.8 19.4 %copy-start.2 = (bf16[128,8192]{1,0:T(8,128)(2,1)S(1)}, bf16[128,8192]{1,0:T(8,128)(2,1)}, u32[]{:S(2)}) copy-start(bf16[128,8192]{1,0:T(8,128)(2,1)} %refs_1_.1) | copy-start | bytes 6291460
  29.4 1.8 %collective-permute-start.4 = (f32[48,2048]{1,0:T(8,128)S(1)}, f32[48,2048]{1,0:T(8,128)S(1)}, u32[]{:S(2)}, u32[]{:S(2)}) collective-permute-start(f32[48,2048]{1,0:T(8,128)S(1)} %shard_map.44), channel_id=1, source_target_pairs={{0,1},{1,0},{2,3},{3,2},{4,5},{5,4},{6,7},{7,6},{8,9},{9,8},{10,11... | collective-permute-start | bytes 1179656 | tf_op jit(solution)/shard_map/ppermute | solution.py:243
  31.3 7.5 %collective-permute-start.5 = (bf16[48,2048]{1,0:T(8,128)(2,1)S(1)}, bf16[48,2048]{1,0:T(8,128)(2,1)S(1)}, u32[]{:S(2)}, u32[]{:S(2)}) collective-permute-start(bf16[48,2048]{1,0:T(8,128)(2,1)S(1)} %add_convert_fusion.mine_ref), channel_id=1, source_target_pairs={{0,8},{1,6},{2,10},{3,4},{4,12},{5,2},{6,14},{7,0},{8,15},{9,1},{1... | collective-permute-start | bytes 589832 | tf_op jit(solution)/shard_map/ppermute | solution.py:243
  34.8 8.7 %collective-permute-start.8 = (bf16[48,2048]{1,0:T(8,128)(2,1)S(1)}, bf16[48,2048]{1,0:T(8,128)(2,1)S(1)}, u32[]{:S(2)}, u32[]{:S(2)}) collective-permute-start(bf16[48,2048]{1,0:T(8,128)(2,1)S(1)} %add_convert_fusion.mine_ref), channel_id=1, source_target_pairs={{0,14},{2,12},{4,10},{6,8},{9,7},{11,5},{13,3},{15,1},{16,30},{18,... | collective-permute-start | bytes 589832 | tf_op jit(solution)/shard_map/ppermute | solution.py:243
  38.8 7.4 %collective-permute-start.7 = (bf16[48,2048]{1,0:T(8,128)(2,1)S(1)}, bf16[48,2048]{1,0:T(8,128)(2,1)S(1)}, u32[]{:S(2)}, u32[]{:S(2)}) collective-permute-start(bf16[48,2048]{1,0:T(8,128)(2,1)S(1)} %shard_map.45.refs_0_), channel_id=1, source_target_pairs={{0,4},{1,5},{2,6},{3,7},{4,0},{5,1},{6,2},{7,3},{8,12},{9,13},{10,... | collective-permute-start | bytes 589832 | tf_op jit(solution)/shard_map/ppermute | solution.py:243
  40.9 6.8 %collective-permute-start.6 = (bf16[48,2048]{1,0:T(8,128)(2,1)S(1)}, bf16[48,2048]{1,0:T(8,128)(2,1)S(1)}, u32[]{:S(2)}, u32[]{:S(2)}) collective-permute-start(bf16[48,2048]{1,0:T(8,128)(2,1)S(1)} %shard_map.45.refs_0_), channel_id=1, source_target_pairs={{0,2},{1,3},{2,0},{3,1},{4,6},{5,7},{6,4},{7,5},{8,10},{9,11},{10,... | collective-permute-start | bytes 589832 | tf_op jit(solution)/shard_map/ppermute | solution.py:243
  42.2 7.7 %collective-permute-start.10 = (bf16[48,2048]{1,0:T(8,128)(2,1)S(1)}, bf16[48,2048]{1,0:T(8,128)(2,1)S(1)}, u32[]{:S(2)}, u32[]{:S(2)}) collective-permute-start(bf16[48,2048]{1,0:T(8,128)(2,1)S(1)} %shard_map.45.refs_0_), channel_id=1, source_target_pairs={{0,16},{1,17},{2,18},{3,19},{4,20},{5,21},{6,22},{7,23},{8,24},{9,... | collective-permute-start | bytes 589832 | tf_op jit(solution)/shard_map/ppermute | solution.py:243
  47.7 6.6 %copy-start.1 = (bf16[96,2048]{1,0:T(8,128)(2,1)S(1)}, bf16[96,2048]{1,0:T(8,128)(2,1)}, u32[]{:S(2)}) copy-start(bf16[96,2048]{1,0:T(8,128)(2,1)} %param.3) | copy-start | bytes 1179652
  48.5 3.9 %collective-permute-start.11 = (f32[48,128]{1,0:T(8,128)S(1)}, f32[48,128]{1,0:T(8,128)S(1)}, u32[]{:S(2)}, u32[]{:S(2)}) collective-permute-start(f32[48,128]{1,0:T(8,128)S(1)} %shard_map.49), channel_id=1, source_target_pairs={{0,16},{1,17},{2,18},{3,19},{4,20},{5,21},{6,22},{7,23},{8,24},{9,... | collective-permute-start | bytes 73736 | tf_op jit(solution)/shard_map/ppermute | solution.py:243
  52.4 1.3 %collective-permute-start.12 = (f32[48,128]{1,0:T(8,128)S(1)}, f32[48,128]{1,0:T(8,128)S(1)}, u32[]{:S(2)}, u32[]{:S(2)}) collective-permute-start(f32[48,128]{1,0:T(8,128)S(1)} %get-tuple-element.60), channel_id=1, source_target_pairs={{0,1},{1,0},{2,3},{3,2},{4,5},{5,4},{6,7},{7,6},{8,9},{9,8},{10,11... | collective-permute-start | bytes 73736 | tf_op jit(solution)/shard_map/ppermute | solution.py:243

commit v20 on v19

--- a/solution.py
+++ b/solution.py
@@ -85,15 +85,14 @@
         term = times(chunk_ref, halves[h][pl.ds(start, step), :])
         outs[0][:, columns] = term + base_ref[:, columns] if has_base else term
 
-    for h, half_ref in enumerate(halves):
-        rows = half_ref.shape[0]
-        if fetch:
-
-            @pl.loop(0, 2)
-            def _(i):
-                product(h, pl.multiple_of(i * (rows // 2), rows // 2), rows // 2)
-        else:
-            product(h, 0, rows)
+    if halves:
+        rows = halves[0].shape[0]
+        step = rows // 2 if fetch else rows
+
+        @pl.loop(0, rows // step)
+        def _(i):
+            for h in range(len(halves)):
+                product(h, pl.multiple_of(i * step, step), step)
 
     for copy in copies:
         copy.wait()
@@ -274,12 +273,15 @@
         across = along_z(first, {0: 0, 1: 1, 2: 2, 3: 3}, True)
         if direct:
             beside, corner = lax.optimization_barrier((beside, corner))
-        else:
-            corner = along_z(first, {2: 3, 3: 2}, True)
-
-        def last(after):
+
+        def last(before, after):
+            if direct:
+                piece = corner
+            else:
+                ready, _ = lax.optimization_barrier((first, before))
+                piece = along_z(ready, {2: 3, 3: 2}, True)
             ready, _ = lax.optimization_barrier((came, after))
-            return pick(dims, ready, corner)
+            return pick(dims, ready, piece)
 
         return first, beside, across, last
 
@@ -292,10 +294,10 @@
     step = functools.partial(fisher_step, inverse_fisher, dims, width)
     a0, a1, b0, b1 = step(((0, 0), (0, 1), (1, 0), (1, 1)))
     q0, q1, q2, last = gather(own, False, (a0,))
-    total, c0, c1 = step(((2, 0), (2, 1)), q0, (a0, a1))
-    total, d0 = step(((3, 0),), q1, (b0, b1), total)
+    total0, c0, c1 = step(((2, 0), (2, 1)), q0, (a0, a1))
+    total, d0 = step(((3, 0),), q1, (b0, b1), total0)
     total, d1 = step(((3, 1),), q2, (c0, c1), total)
-    (total,) = step((), last(total), (d0, d1), total)
+    (total,) = step((), last(total0, total), (d0, d1), total)
     panel = (total + swap_core(total)).astype(jnp.bfloat16)
 
     p0, p1, p2, last = gather(panel, True)
@@ -304,7 +306,7 @@
     mine = score_dot([p0, p1], ORDER[:2], dims, stored_grads)
     p2, _ = lax.optimization_barrier((p2, mine))
     other = score_dot([p1, p2], (0, 1), None, other_grads)
-    p3 = last(other)
+    p3 = last(other, other)
     other = score_dot([p3], (2,), None, other_grads, other)
     p2, p3, mine, swapped, _ = lax.optimization_barrier((p2, p3, mine, swapped, other))
     mine = score_dot([p2, p3], ORDER[2:], dims, stored_grads, mine)

time: 54.4 us -> 54 us (level)
  transfers between devices with their start and end apart: 13 -> 13, of which waited for: 6 -> 5; matrix products, arithmetic and copies ran while one was open for 0% -> 0% of each run, Pallas kernels for 37% -> 37%
where the time goes in v20:
time: 54 us; the launch traced here: 53.7 us
  starting transfers between devices  23.9 us (44%)
  Pallas kernels  21.3 us (39%)
  waiting for transfers between devices  7.61 us (14%)
  other arithmetic  0.65 us (1%)
    ppermute x13, starting transfers between devices, move(): return lax.ppermute(value, AXES, pairs)  23.9 us
    pallas_call x5, Pallas kernels, fisher_step(): pl.pallas_call(functools.partial(fisher_kernel, dims, len(ins), has_base,...  17.7 us
    ppermute x13, waiting for transfers between devices, move(): return lax.ppermute(value, AXES, pairs)  7.61 us
    pallas_call x5, Pallas kernels, score_dot(): pl.pallas_call(functools.partial(score_kernel, dims, order, base is not N...  2.01 us
    pallas_call x1, Pallas kernels, cut(): pl.pallas_call(functools.partial(cut_kernel, dims, order), out_shape=jax....  1.43 us
  transfers between devices with their start and end apart: 13, of which 5 were waited for; matrix products, arithmetic and copies ran while one was open for 0% of the time, Pallas kernels for 37%

profile of v20, /device:TPU:0, one launch (start us, length us, event | category | flops | bytes accessed | tf_op | source)
XLA Modules:
  0.0 53.7 jit_solution(6051277782774500006)
XLA Ops:
  0.0 1.4 %shard_map.37 = bf16[128,6144]{1,0:T(8,128)(2,1)S(1)} custom-call(bf16[128,8192]{1,0:T(8,128)(2,1)} %refs_1_.1), custom_call_target="tpu_custom_call" | custom-call | bytes 1572864 | tf_op jit(solution)/shard_map/pallas_call | solution.py:173
  1.4 0.0 copy-done
  1.5 4.1 %collective-permute-start = (bf16[48,2048]{1,0:T(8,128)(2,1)S(1)}, bf16[48,2048]{1,0:T(8,128)(2,1)S(1)}, u32[]{:S(2)}, u32[]{:S(2)}) collective-permute-start(bf16[48,2048]{1,0:T(8,128)(2,1)S(1)} %constant_dynamic-slice_fusion.mine_ref), channel_id=1, source_target_pairs={{0,8},{1,6},{2,10},{3,4},{4,12},{5,2},{6,14},{7,0},{8,15},{9,1},{1... | collective-permute-start | bytes 589832 | tf_op jit(solution)/shard_map/ppermute | solution.py:242
  5.6 1.5 %collective-permute-start.9 = (bf16[128,6144]{1,0:T(8,128)(2,1)S(1)}, bf16[128,6144]{1,0:T(8,128)(2,1)S(1)}, u32[]{:S(2)}, u32[]{:S(2)}) collective-permute-start(bf16[128,6144]{1,0:T(8,128)(2,1)S(1)} %shard_map.37), channel_id=1, source_target_pairs={{0,16},{1,17},{2,18},{3,19},{4,20},{5,21},{6,22},{7,23},{8,24},{9,... | collective-permute-start | bytes 4718600 | tf_op jit(solution)/shard_map/ppermute | solution.py:242
  7.1 6.0 %shard_map.38 = (bf16[1024,2048]{1,0:T(8,128)(2,1)S(1)}, bf16[1024,2048]{1,0:T(8,128)(2,1)S(1)}, bf16[1024,2048]{1,0:T(8,128)(2,1)S(1)}, bf16[1024,2048]{1,0:T(8,128)(2,1)S(1)}) custom-call(bf16[2048,8192]{1,0:T(8,128)(2,1)} %refs_0_.7), custom_call_target="tpu_custom_call" | custom-call | bytes 16777216 | tf_op jit(solution)/shard_map/pallas_call | solution.py:108
  13.1 1.6 %collective-permute-start.2 = (bf16[48,2048]{1,0:T(8,128)(2,1)S(1)}, bf16[48,2048]{1,0:T(8,128)(2,1)S(1)}, u32[]{:S(2)}, u32[]{:S(2)}) collective-permute-start(bf16[48,2048]{1,0:T(8,128)(2,1)S(1)} %shard_map.39.refs_1_), channel_id=1, source_target_pairs={{0,4},{1,5},{2,6},{3,7},{4,0},{5,1},{6,2},{7,3},{8,12},{9,13},{10,... | collective-permute-start | bytes 589832 | tf_op jit(solution)/shard_map/ppermute | solution.py:242
  14.8 1.5 %collective-permute-start.1 = (bf16[48,2048]{1,0:T(8,128)(2,1)S(1)}, bf16[48,2048]{1,0:T(8,128)(2,1)S(1)}, u32[]{:S(2)}, u32[]{:S(2)}) collective-permute-start(bf16[48,2048]{1,0:T(8,128)(2,1)S(1)} %shard_map.39.refs_1_), channel_id=1, source_target_pairs={{0,2},{1,3},{2,0},{3,1},{4,6},{5,7},{6,4},{7,5},{8,10},{9,11},{10,... | collective-permute-start | bytes 589832 | tf_op jit(solution)/shard_map/ppermute | solution.py:242
  16.3 3.5 %shard_map.40 = (f32[48,2048]{1,0:T(8,128)S(1)}, bf16[1024,2048]{1,0:T(8,128)(2,1)S(1)}, bf16[1024,2048]{1,0:T(8,128)(2,1)S(1)}) custom-call(bf16[2048,8192]{1,0:T(8,128)(2,1)} %refs_0_.7, bf16[48,2048]{1,0:T(8,128)(2,1)S(1)} %shard_map.39.refs_1_, bf16[1024,2048]{1,0:T(8,128)(2,1)S(1)} %get-tuple-element.37.refs_0_.refs_2_, ...), custom_call_target="tpu_custom_call" | custom-call | flops 402653184 | bytes 16777216 | tf_op jit(solution)/shard_map/pallas_call | solution.py:108
  19.8 0.7 %collective-permute-start.3 = (bf16[48,2048]{1,0:T(8,128)(2,1)S(1)}, bf16[48,2048]{1,0:T(8,128)(2,1)S(1)}, u32[]{:S(2)}, u32[]{:S(2)}) collective-permute-start(bf16[48,2048]{1,0:T(8,128)(2,1)S(1)} %shard_map.39.refs_1_), channel_id=1, source_target_pairs={{1,7},{3,5},{5,3},{7,1},{8,14},{10,12},{12,10},{14,8},{17,23},{19,... | collective-permute-start | bytes 589832 | tf_op jit(solution)/shard_map/ppermute | solution.py:242
  20.5 2.8 %shard_map.41 = (f32[48,2048]{1,0:T(8,128)S(1)}, bf16[1024,2048]{1,0:T(8,128)(2,1)S(1)}) custom-call(bf16[2048,8192]{1,0:T(8,128)(2,1)} %refs_0_.7, bf16[48,2048]{1,0:T(8,128)(2,1)S(1)} %collective-permute-done.2.refs_1_, bf16[1024,2048]{1,0:T(8,128)(2,1)S(1)} %get-tuple-element.41.refs_2_, bf16[1024,2048]{1,0:T(8,128)(2,1)S(1)} %get-tuple-element.42.refs_3_, ...), custom_call_target="tpu_custom_call" | custom-call | flops 402653184 | bytes 12582912 | tf_op jit(solution)/shard_map/pallas_call | solution.py:108
  23.3 2.8 %shard_map.42 = (f32[48,2048]{1,0:T(8,128)S(1)}, bf16[1024,2048]{1,0:T(8,128)(2,1)S(1)}) custom-call(bf16[2048,8192]{1,0:T(8,128)(2,1)} %refs_0_.7, bf16[48,2048]{1,0:T(8,128)(2,1)S(1)} %collective-permute-done.1.refs_1_, bf16[1024,2048]{1,0:T(8,128)(2,1)S(1)} %get-tuple-element.39.refs_2_, bf16[1024,2048]{1,0:T(8,128)(2,1)S(1)} %get-tuple-element.40.refs_3_, ...), custom_call_target="tpu_custom_call" | custom-call | flops 402653184 | bytes 12582912 | tf_op jit(solution)/shard_map/pallas_call | solution.py:108
  26.1 0.0 copy-start.2
  26.1 2.6 %shard_map.44 = f32[48,2048]{1,0:T(8,128)S(1)} custom-call(bf16[48,2048]{1,0:T(8,128)(2,1)S(1)} %shard_map.43.refs_0_, bf16[1024,2048]{1,0:T(8,128)(2,1)S(1)} %get-tuple-element.48.refs_1_, bf16[1024,2048]{1,0:T(8,128)(2,1)S(1)} %get-tuple-element.49.refs_2_, f32[48,2048]{1,0:T(8,128)S(1)} %get-tuple-element.45.refs_3_), custom_call_target="tpu_custom_call" | custom-call | flops 402653184 | bytes 8388608 | tf_op jit(solution)/shard_map/pallas_call | solution.py:108
  28.8 0.6 %collective-permute-start.4 = (f32[48,2048]{1,0:T(8,128)S(1)}, f32[48,2048]{1,0:T(8,128)S(1)}, u32[]{:S(2)}, u32[]{:S(2)}) collective-permute-start(f32[48,2048]{1,0:T(8,128)S(1)} %shard_map.44), channel_id=1, source_target_pairs={{0,1},{1,0},{2,3},{3,2},{4,5},{5,4},{6,7},{7,6},{8,9},{9,8},{10,11... | collective-permute-start | bytes 1179656 | tf_op jit(solution)/shard_map/ppermute | solution.py:242
  29.4 1.3 %collective-permute-done.4 = f32[48,2048]{1,0:T(8,128)S(1)} collective-permute-done((f32[48,2048]{1,0:T(8,128)S(1)}, f32[48,2048]{1,0:T(8,128)S(1)}, u32[]{:S(2)}, u32[]{:S(2)}) %collective-permute-start.4) | collective-permute-done | bytes 393248 | tf_op jit(solution)/shard_map/ppermute | solution.py:242
  30.8 3.5 %collective-permute-start.5 = (bf16[48,2048]{1,0:T(8,128)(2,1)S(1)}, bf16[48,2048]{1,0:T(8,128)(2,1)S(1)}, u32[]{:S(2)}, u32[]{:S(2)}) collective-permute-start(bf16[48,2048]{1,0:T(8,128)(2,1)S(1)} %add_convert_fusion.mine_ref), channel_id=1, source_target_pairs={{0,8},{1,6},{2,10},{3,4},{4,12},{5,2},{6,14},{7,0},{8,15},{9,1},{1... | collective-permute-start | bytes 589832 | tf_op jit(solution)/shard_map/ppermute | solution.py:242
  34.3 4.0 %collective-permute-start.8 = (bf16[48,2048]{1,0:T(8,128)(2,1)S(1)}, bf16[48,2048]{1,0:T(8,128)(2,1)S(1)}, u32[]{:S(2)}, u32[]{:S(2)}) collective-permute-start(bf16[48,2048]{1,0:T(8,128)(2,1)S(1)} %add_convert_fusion.mine_ref), channel_id=1, source_target_pairs={{0,14},{2,12},{4,10},{6,8},{9,7},{11,5},{13,3},{15,1},{16,30},{18,... | collective-permute-start | bytes 589832 | tf_op jit(solution)/shard_map/ppermute | solution.py:242
  38.3 2.0 %collective-permute-start.7 = (bf16[48,2048]{1,0:T(8,128)(2,1)S(1)}, bf16[48,2048]{1,0:T(8,128)(2,1)S(1)}, u32[]{:S(2)}, u32[]{:S(2)}) collective-permute-start(bf16[48,2048]{1,0:T(8,128)(2,1)S(1)} %shard_map.45.refs_0_), channel_id=1, source_target_pairs={{0,4},{1,5},{2,6},{3,7},{4,0},{5,1},{6,2},{7,3},{8,12},{9,13},{10,... | collective-permute-start | bytes 589832 | tf_op jit(solution)/shard_map/ppermute | solution.py:242
  40.4 1.3 %collective-permute-start.6 = (bf16[48,2048]{1,0:T(8,128)(2,1)S(1)}, bf16[48,2048]{1,0:T(8,128)(2,1)S(1)}, u32[]{:S(2)}, u32[]{:S(2)}) collective-permute-start(bf16[48,2048]{1,0:T(8,128)(2,1)S(1)} %shard_map.45.refs_0_), channel_id=1, source_target_pairs={{0,2},{1,3},{2,0},{3,1},{4,6},{5,7},{6,4},{7,5},{8,10},{9,11},{10,... | collective-permute-start | bytes 589832 | tf_op jit(solution)/shard_map/ppermute | solution.py:242
  41.7 1.3 %collective-permute-start.10 = (bf16[48,2048]{1,0:T(8,128)(2,1)S(1)}, bf16[48,2048]{1,0:T(8,128)(2,1)S(1)}, u32[]{:S(2)}, u32[]{:S(2)}) collective-permute-start(bf16[48,2048]{1,0:T(8,128)(2,1)S(1)} %shard_map.45.refs_0_), channel_id=1, source_target_pairs={{0,16},{1,17},{2,18},{3,19},{4,20},{5,21},{6,22},{7,23},{8,24},{9,... | collective-permute-start | bytes 589832 | tf_op jit(solution)/shard_map/ppermute | solution.py:242
  43.0 2.7 %collective-permute-done.7.refs_1_.refs_0_ = bf16[48,2048]{1,0:T(8,128)(2,1)S(1)} collective-permute-done((bf16[48,2048]{1,0:T(8,128)(2,1)S(1)}, bf16[48,2048]{1,0:T(8,128)(2,1)S(1)}, u32[]{:S(2)}, u32[]{:S(2)}) %collective-permute-start.7) | collective-permute-done | bytes 196640 | tf_op jit(solution)/shard_map/ppermute | solution.py:242
  45.7 0.5 shard_map.46.refs_3_
  46.2 0.9 %collective-permute-done.6.refs_1_.refs_0_ = bf16[48,2048]{1,0:T(8,128)(2,1)S(1)} collective-permute-done((bf16[48,2048]{1,0:T(8,128)(2,1)S(1)}, bf16[48,2048]{1,0:T(8,128)(2,1)S(1)}, u32[]{:S(2)}, u32[]{:S(2)}) %collective-permute-start.6) | collective-permute-done | bytes 196640 | tf_op jit(solution)/shard_map/ppermute | solution.py:242
  47.1 0.5 shard_map.47.refs_2_
  47.6 0.3 shard_map.49
  47.9 1.6 %collective-permute-start.11 = (f32[48,128]{1,0:T(8,128)S(1)}, f32[48,128]{1,0:T(8,128)S(1)}, u32[]{:S(2)}, u32[]{:S(2)}) collective-permute-start(f32[48,128]{1,0:T(8,128)S(1)} %shard_map.49), channel_id=1, source_target_pairs={{0,16},{1,17},{2,18},{3,19},{4,20},{5,21},{6,22},{7,23},{8,24},{9,... | collective-permute-start | bytes 73736 | tf_op jit(solution)/shard_map/ppermute | solution.py:242
  49.5 0.3 shard_map.51.theirs_ref
  49.8 0.5 shard_map.50.mine_ref
  50.3 1.5 %collective-permute-done.11.other_ref = f32[48,128]{1,0:T(8,128)S(1)} collective-permute-done((f32[48,128]{1,0:T(8,128)S(1)}, f32[48,128]{1,0:T(8,128)S(1)}, u32[]{:S(2)}, u32[]{:S(2)}) %collective-permute-start.11) | collective-permute-done | bytes 24608 | tf_op jit(solution)/shard_map/ppermute | solution.py:242
  51.8 0.1 collective-permute-start.12
  51.9 1.2 %collective-permute-done.12 = f32[48,128]{1,0:T(8,128)S(1)} collective-permute-done((f32[48,128]{1,0:T(8,128)S(1)}, f32[48,128]{1,0:T(8,128)S(1)}, u32[]{:S(2)}, u32[]{:S(2)}) %collective-permute-start.12) | collective-permute-done | bytes 24608 | tf_op jit(solution)/shard_map/ppermute | solution.py:242
  53.0 0.6 %add.11 = f32[48,128]{1,0:T(8,128)} add(f32[48,128]{1,0:T(8,128)S(1)} %get-tuple-element.61, f32[48,128]{1,0:T(8,128)S(1)} %collective-permute-done.12) | non-fusion elementwise | flops 6144 | bytes 73728 | tf_op jit(solution)/shard_map/add | solution.py:316
  (19 shorter events, 0.2 us)
Async XLA Ops:
  0.0 1.5 %copy-start = (bf16[96,2048]{1,0:T(8,128)(2,1)S(1)}, bf16[96,2048]{1,0:T(8,128)(2,1)}, u32[]{:S(2)}) copy-start(bf16[96,2048]{1,0:T(8,128)(2,1)} %param.3) | copy-start | bytes 1179652
  1.5 11.6 %collective-permute-start = (bf16[48,2048]{1,0:T(8,128)(2,1)S(1)}, bf16[48,2048]{1,0:T(8,128)(2,1)S(1)}, u32[]{:S(2)}, u32[]{:S(2)}) collective-permute-start(bf16[48,2048]{1,0:T(8,128)(2,1)S(1)} %constant_dynamic-slice_fusion.mine_ref), channel_id=1, source_target_pairs={{0,8},{1,6},{2,10},{3,4},{4,12},{5,2},{6,14},{7,0},{8,15},{9,1},{1... | collective-permute-start | bytes 589832 | tf_op jit(solution)/shard_map/ppermute | solution.py:242
  5.6 40.1 %collective-permute-start.9 = (bf16[128,6144]{1,0:T(8,128)(2,1)S(1)}, bf16[128,6144]{1,0:T(8,128)(2,1)S(1)}, u32[]{:S(2)}, u32[]{:S(2)}) collective-permute-start(bf16[128,6144]{1,0:T(8,128)(2,1)S(1)} %shard_map.37), channel_id=1, source_target_pairs={{0,16},{1,17},{2,18},{3,19},{4,20},{5,21},{6,22},{7,23},{8,24},{9,... | collective-permute-start | bytes 4718600 | tf_op jit(solution)/shard_map/ppermute | solution.py:242
  13.1 7.3 %collective-permute-start.2 = (bf16[48,2048]{1,0:T(8,128)(2,1)S(1)}, bf16[48,2048]{1,0:T(8,128)(2,1)S(1)}, u32[]{:S(2)}, u32[]{:S(2)}) collective-permute-start(bf16[48,2048]{1,0:T(8,128)(2,1)S(1)} %shard_map.39.refs_1_), channel_id=1, source_target_pairs={{0,4},{1,5},{2,6},{3,7},{4,0},{5,1},{6,2},{7,3},{8,12},{9,13},{10,... | collective-permute-start | bytes 589832 | tf_op jit(solution)/shard_map/ppermute | solution.py:242
  14.8 8.5 %collective-permute-start.1 = (bf16[48,2048]{1,0:T(8,128)(2,1)S(1)}, bf16[48,2048]{1,0:T(8,128)(2,1)S(1)}, u32[]{:S(2)}, u32[]{:S(2)}) collective-permute-start(bf16[48,2048]{1,0:T(8,128)(2,1)S(1)} %shard_map.39.refs_1_), channel_id=1, source_target_pairs={{0,2},{1,3},{2,0},{3,1},{4,6},{5,7},{6,4},{7,5},{8,10},{9,11},{10,... | collective-permute-start | bytes 589832 | tf_op jit(solution)/shard_map/ppermute | solution.py:242
  19.8 6.3 %collective-permute-start.3 = (bf16[48,2048]{1,0:T(8,128)(2,1)S(1)}, bf16[48,2048]{1,0:T(8,128)(2,1)S(1)}, u32[]{:S(2)}, u32[]{:S(2)}) collective-permute-start(bf16[48,2048]{1,0:T(8,128)(2,1)S(1)} %shard_map.39.refs_1_), channel_id=1, source_target_pairs={{1,7},{3,5},{5,3},{7,1},{8,14},{10,12},{12,10},{14,8},{17,23},{19,... | collective-permute-start | bytes 589832 | tf_op jit(solution)/shard_map/ppermute | solution.py:242
  26.1 19.6 %copy-start.2 = (bf16[128,8192]{1,0:T(8,128)(2,1)S(1)}, bf16[128,8192]{1,0:T(8,128)(2,1)}, u32[]{:S(2)}) copy-start(bf16[128,8192]{1,0:T(8,128)(2,1)} %refs_1_.1) | copy-start | bytes 6291460
  28.8 2.0 %collective-permute-start.4 = (f32[48,2048]{1,0:T(8,128)S(1)}, f32[48,2048]{1,0:T(8,128)S(1)}, u32[]{:S(2)}, u32[]{:S(2)}) collective-permute-start(f32[48,2048]{1,0:T(8,128)S(1)} %shard_map.44), channel_id=1, source_target_pairs={{0,1},{1,0},{2,3},{3,2},{4,5},{5,4},{6,7},{7,6},{8,9},{9,8},{10,11... | collective-permute-start | bytes 1179656 | tf_op jit(solution)/shard_map/ppermute | solution.py:242
  30.8 7.5 %collective-permute-start.5 = (bf16[48,2048]{1,0:T(8,128)(2,1)S(1)}, bf16[48,2048]{1,0:T(8,128)(2,1)S(1)}, u32[]{:S(2)}, u32[]{:S(2)}) collective-permute-start(bf16[48,2048]{1,0:T(8,128)(2,1)S(1)} %add_convert_fusion.mine_ref), channel_id=1, source_target_pairs={{0,8},{1,6},{2,10},{3,4},{4,12},{5,2},{6,14},{7,0},{8,15},{9,1},{1... | collective-permute-start | bytes 589832 | tf_op jit(solution)/shard_map/ppermute | solution.py:242
  34.3 8.7 %collective-permute-start.8 = (bf16[48,2048]{1,0:T(8,128)(2,1)S(1)}, bf16[48,2048]{1,0:T(8,128)(2,1)S(1)}, u32[]{:S(2)}, u32[]{:S(2)}) collective-permute-start(bf16[48,2048]{1,0:T(8,128)(2,1)S(1)} %add_convert_fusion.mine_ref), channel_id=1, source_target_pairs={{0,14},{2,12},{4,10},{6,8},{9,7},{11,5},{13,3},{15,1},{16,30},{18,... | collective-permute-start | bytes 589832 | tf_op jit(solution)/shard_map/ppermute | solution.py:242
  38.3 7.4 %collective-permute-start.7 = (bf16[48,2048]{1,0:T(8,128)(2,1)S(1)}, bf16[48,2048]{1,0:T(8,128)(2,1)S(1)}, u32[]{:S(2)}, u32[]{:S(2)}) collective-permute-start(bf16[48,2048]{1,0:T(8,128)(2,1)S(1)} %shard_map.45.refs_0_), channel_id=1, source_target_pairs={{0,4},{1,5},{2,6},{3,7},{4,0},{5,1},{6,2},{7,3},{8,12},{9,13},{10,... | collective-permute-start | bytes 589832 | tf_op jit(solution)/shard_map/ppermute | solution.py:242
  40.4 6.7 %collective-permute-start.6 = (bf16[48,2048]{1,0:T(8,128)(2,1)S(1)}, bf16[48,2048]{1,0:T(8,128)(2,1)S(1)}, u32[]{:S(2)}, u32[]{:S(2)}) collective-permute-start(bf16[48,2048]{1,0:T(8,128)(2,1)S(1)} %shard_map.45.refs_0_), channel_id=1, source_target_pairs={{0,2},{1,3},{2,0},{3,1},{4,6},{5,7},{6,4},{7,5},{8,10},{9,11},{10,... | collective-permute-start | bytes 589832 | tf_op jit(solution)/shard_map/ppermute | solution.py:242
  41.7 7.8 %collective-permute-start.10 = (bf16[48,2048]{1,0:T(8,128)(2,1)S(1)}, bf16[48,2048]{1,0:T(8,128)(2,1)S(1)}, u32[]{:S(2)}, u32[]{:S(2)}) collective-permute-start(bf16[48,2048]{1,0:T(8,128)(2,1)S(1)} %shard_map.45.refs_0_), channel_id=1, source_target_pairs={{0,16},{1,17},{2,18},{3,19},{4,20},{5,21},{6,22},{7,23},{8,24},{9,... | collective-permute-start | bytes 589832 | tf_op jit(solution)/shard_map/ppermute | solution.py:242
  47.1 6.6 %copy-start.1 = (bf16[96,2048]{1,0:T(8,128)(2,1)S(1)}, bf16[96,2048]{1,0:T(8,128)(2,1)}, u32[]{:S(2)}) copy-start(bf16[96,2048]{1,0:T(8,128)(2,1)} %param.3) | copy-start | bytes 1179652
  47.9 3.9 %collective-permute-start.11 = (f32[48,128]{1,0:T(8,128)S(1)}, f32[48,128]{1,0:T(8,128)S(1)}, u32[]{:S(2)}, u32[]{:S(2)}) collective-permute-start(f32[48,128]{1,0:T(8,128)S(1)} %shard_map.49), channel_id=1, source_target_pairs={{0,16},{1,17},{2,18},{3,19},{4,20},{5,21},{6,22},{7,23},{8,24},{9,... | collective-permute-start | bytes 73736 | tf_op jit(solution)/shard_map/ppermute | solution.py:242
  51.8 1.3 %collective-permute-start.12 = (f32[48,128]{1,0:T(8,128)S(1)}, f32[48,128]{1,0:T(8,128)S(1)}, u32[]{:S(2)}, u32[]{:S(2)}) collective-permute-start(f32[48,128]{1,0:T(8,128)S(1)} %get-tuple-element.62), channel_id=1, source_target_pairs={{0,1},{1,0},{2,3},{3,2},{4,5},{5,4},{6,7},{7,6},{8,9},{9,8},{10,11... | collective-permute-start | bytes 73736 | tf_op jit(solution)/shard_map/ppermute | solution.py:242

commit v21 on v20

--- a/solution.py
+++ b/solution.py
@@ -276,12 +276,11 @@
 
         def last(before, after):
             if direct:
-                piece = corner
-            else:
-                ready, _ = lax.optimization_barrier((first, before))
-                piece = along_z(ready, {2: 3, 3: 2}, True)
-            ready, _ = lax.optimization_barrier((came, after))
-            return pick(dims, ready, piece)
+                ready, _ = lax.optimization_barrier((came, after))
+                return pick(dims, ready, corner)
+            ready, _ = lax.optimization_barrier((first, before))
+            piece, _ = lax.optimization_barrier((along_z(ready, pairs, True), after))
+            return piece
 
         return first, beside, across, last
 

time: 54 us -> 53.3 us (0.987)
  starting transfers between devices: 23.9 us -> 19.8 us
  waiting for transfers between devices: 7.61 us -> 11.3 us
    ppermute x13, starting transfers between devices: 23.9 us -> 19.8 us  [move(): return lax.ppermute(value, AXES, pairs)]
    ppermute x13, waiting for transfers between devices: 7.61 us -> 11.3 us  [move(): return lax.ppermute(value, AXES, pairs)]
  transfers between devices with their start and end apart: 13 -> 13, of which waited for: 5 -> 7; matrix products, arithmetic and copies ran while one was open for 0% -> 0% of each run, Pallas kernels for 37% -> 37%
where the time goes in v21:
time: 53.3 us; the launch traced here: 53.2 us
  Pallas kernels  21.2 us (40%)
  starting transfers between devices  19.8 us (37%)
  waiting for transfers between devices  11.3 us (21%)
  other arithmetic  0.65 us (1%)
    ppermute x13, starting transfers between devices, move(): return lax.ppermute(value, AXES, pairs)  19.8 us
    pallas_call x5, Pallas kernels, fisher_step(): pl.pallas_call(functools.partial(fisher_kernel, dims, len(ins), has_base,...  17.7 us
    ppermute x13, waiting for transfers between devices, move(): return lax.ppermute(value, AXES, pairs)  11.3 us
    pallas_call x5, Pallas kernels, score_dot(): pl.pallas_call(functools.partial(score_kernel, dims, order, base is not N...  2.01 us
    pallas_call x1, Pallas kernels, cut(): pl.pallas_call(functools.partial(cut_kernel, dims, order), out_shape=jax....  1.43 us
  transfers between devices with their start and end apart: 13, of which 7 were waited for; matrix products, arithmetic and copies ran while one was open for 0% of the time, Pallas kernels for 37%

profile of v21, /device:TPU:0, one launch (start us, length us, event | category | flops | bytes accessed | tf_op | source)
XLA Modules:
  0.0 53.2 jit_solution(2953731806421532844)
XLA Ops:
  0.0 1.4 %shard_map.37 = bf16[128,6144]{1,0:T(8,128)(2,1)S(1)} custom-call(bf16[128,8192]{1,0:T(8,128)(2,1)} %refs_1_.1), custom_call_target="tpu_custom_call" | custom-call | bytes 1572864 | tf_op jit(solution)/shard_map/pallas_call | solution.py:173
  1.5 4.1 %collective-permute-start = (bf16[48,2048]{1,0:T(8,128)(2,1)S(1)}, bf16[48,2048]{1,0:T(8,128)(2,1)S(1)}, u32[]{:S(2)}, u32[]{:S(2)}) collective-permute-start(bf16[48,2048]{1,0:T(8,128)(2,1)S(1)} %constant_dynamic-slice_fusion.mine_ref), channel_id=1, source_target_pairs={{0,8},{1,6},{2,10},{3,4},{4,12},{5,2},{6,14},{7,0},{8,15},{9,1},{1... | collective-permute-start | bytes 589832 | tf_op jit(solution)/shard_map/ppermute | solution.py:242
  5.6 1.5 %collective-permute-start.9 = (bf16[128,6144]{1,0:T(8,128)(2,1)S(1)}, bf16[128,6144]{1,0:T(8,128)(2,1)S(1)}, u32[]{:S(2)}, u32[]{:S(2)}) collective-permute-start(bf16[128,6144]{1,0:T(8,128)(2,1)S(1)} %shard_map.37), channel_id=1, source_target_pairs={{0,16},{1,17},{2,18},{3,19},{4,20},{5,21},{6,22},{7,23},{8,24},{9,... | collective-permute-start | bytes 4718600 | tf_op jit(solution)/shard_map/ppermute | solution.py:242
  7.1 6.0 %shard_map.38 = (bf16[1024,2048]{1,0:T(8,128)(2,1)S(1)}, bf16[1024,2048]{1,0:T(8,128)(2,1)S(1)}, bf16[1024,2048]{1,0:T(8,128)(2,1)S(1)}, bf16[1024,2048]{1,0:T(8,128)(2,1)S(1)}) custom-call(bf16[2048,8192]{1,0:T(8,128)(2,1)} %refs_0_.7), custom_call_target="tpu_custom_call" | custom-call | bytes 16777216 | tf_op jit(solution)/shard_map/pallas_call | solution.py:108
  13.1 1.6 %collective-permute-start.3 = (bf16[48,2048]{1,0:T(8,128)(2,1)S(1)}, bf16[48,2048]{1,0:T(8,128)(2,1)S(1)}, u32[]{:S(2)}, u32[]{:S(2)}) collective-permute-start(bf16[48,2048]{1,0:T(8,128)(2,1)S(1)} %shard_map.39.refs_1_), channel_id=1, source_target_pairs={{0,4},{1,5},{2,6},{3,7},{4,0},{5,1},{6,2},{7,3},{8,12},{9,13},{10,... | collective-permute-start | bytes 589832 | tf_op jit(solution)/shard_map/ppermute | solution.py:242
  14.8 1.5 %collective-permute-start.2 = (bf16[48,2048]{1,0:T(8,128)(2,1)S(1)}, bf16[48,2048]{1,0:T(8,128)(2,1)S(1)}, u32[]{:S(2)}, u32[]{:S(2)}) collective-permute-start(bf16[48,2048]{1,0:T(8,128)(2,1)S(1)} %shard_map.39.refs_1_), channel_id=1, source_target_pairs={{0,2},{1,3},{2,0},{3,1},{4,6},{5,7},{6,4},{7,5},{8,10},{9,11},{10,... | collective-permute-start | bytes 589832 | tf_op jit(solution)/shard_map/ppermute | solution.py:242
  16.3 3.5 %shard_map.40 = (f32[48,2048]{1,0:T(8,128)S(1)}, bf16[1024,2048]{1,0:T(8,128)(2,1)S(1)}, bf16[1024,2048]{1,0:T(8,128)(2,1)S(1)}) custom-call(bf16[2048,8192]{1,0:T(8,128)(2,1)} %refs_0_.7, bf16[48,2048]{1,0:T(8,128)(2,1)S(1)} %shard_map.39.refs_1_, bf16[1024,2048]{1,0:T(8,128)(2,1)S(1)} %get-tuple-element.37.refs_0_.refs_2_, ...), custom_call_target="tpu_custom_call" | custom-call | flops 402653184 | bytes 16777216 | tf_op jit(solution)/shard_map/pallas_call | solution.py:108
  19.8 0.5 collective-permute-start.1
  20.3 2.8 %shard_map.41 = (f32[48,2048]{1,0:T(8,128)S(1)}, bf16[1024,2048]{1,0:T(8,128)(2,1)S(1)}) custom-call(bf16[2048,8192]{1,0:T(8,128)(2,1)} %refs_0_.7, bf16[48,2048]{1,0:T(8,128)(2,1)S(1)} %collective-permute-done.3.refs_1_, bf16[1024,2048]{1,0:T(8,128)(2,1)S(1)} %get-tuple-element.43.refs_2_, bf16[1024,2048]{1,0:T(8,128)(2,1)S(1)} %get-tuple-element.44.refs_3_, ...), custom_call_target="tpu_custom_call" | custom-call | flops 402653184 | bytes 12582912 | tf_op jit(solution)/shard_map/pallas_call | solution.py:108
  23.0 2.8 %shard_map.42 = (f32[48,2048]{1,0:T(8,128)S(1)}, bf16[1024,2048]{1,0:T(8,128)(2,1)S(1)}) custom-call(bf16[2048,8192]{1,0:T(8,128)(2,1)} %refs_0_.7, bf16[48,2048]{1,0:T(8,128)(2,1)S(1)} %collective-permute-done.2.refs_1_, bf16[1024,2048]{1,0:T(8,128)(2,1)S(1)} %get-tuple-element.41.refs_2_, bf16[1024,2048]{1,0:T(8,128)(2,1)S(1)} %get-tuple-element.42.refs_3_, ...), custom_call_target="tpu_custom_call" | custom-call | flops 402653184 | bytes 12582912 | tf_op jit(solution)/shard_map/pallas_call | solution.py:108
  25.8 0.6 %collective-permute-done.1.refs_0_ = bf16[48,2048]{1,0:T(8,128)(2,1)S(1)} collective-permute-done((bf16[48,2048]{1,0:T(8,128)(2,1)S(1)}, bf16[48,2048]{1,0:T(8,128)(2,1)S(1)}, u32[]{:S(2)}, u32[]{:S(2)}) %collective-permute-start.1) | collective-permute-done | bytes 196640 | tf_op jit(solution)/shard_map/ppermute | solution.py:242
  26.4 2.6 %shard_map.43 = f32[48,2048]{1,0:T(8,128)S(1)} custom-call(bf16[48,2048]{1,0:T(8,128)(2,1)S(1)} %collective-permute-done.1.refs_0_, bf16[1024,2048]{1,0:T(8,128)(2,1)S(1)} %get-tuple-element.48.refs_1_, bf16[1024,2048]{1,0:T(8,128)(2,1)S(1)} %get-tuple-element.49.refs_2_, f32[48,2048]{1,0:T(8,128)S(1)} %get-tuple-element.46.refs_3_), custom_call_target="tpu_custom_call" | custom-call | flops 402653184 | bytes 8388608 | tf_op jit(solution)/shard_map/pallas_call | solution.py:108
  29.1 0.1 collective-permute-start.4
  29.1 1.7 %collective-permute-done.4 = f32[48,2048]{1,0:T(8,128)S(1)} collective-permute-done((f32[48,2048]{1,0:T(8,128)S(1)}, f32[48,2048]{1,0:T(8,128)S(1)}, u32[]{:S(2)}, u32[]{:S(2)}) %collective-permute-start.4) | collective-permute-done | bytes 393248 | tf_op jit(solution)/shard_map/ppermute | solution.py:242
  30.9 1.5 %collective-permute-start.5 = (bf16[48,2048]{1,0:T(8,128)(2,1)S(1)}, bf16[48,2048]{1,0:T(8,128)(2,1)S(1)}, u32[]{:S(2)}, u32[]{:S(2)}) collective-permute-start(bf16[48,2048]{1,0:T(8,128)(2,1)S(1)} %add_convert_fusion.mine_ref), channel_id=1, source_target_pairs={{0,8},{1,6},{2,10},{3,4},{4,12},{5,2},{6,14},{7,0},{8,15},{9,1},{1... | collective-permute-start | bytes 589832 | tf_op jit(solution)/shard_map/ppermute | solution.py:242
  32.4 4.0 %collective-permute-start.8 = (bf16[48,2048]{1,0:T(8,128)(2,1)S(1)}, bf16[48,2048]{1,0:T(8,128)(2,1)S(1)}, u32[]{:S(2)}, u32[]{:S(2)}) collective-permute-start(bf16[48,2048]{1,0:T(8,128)(2,1)S(1)} %add_convert_fusion.mine_ref), channel_id=1, source_target_pairs={{0,14},{2,12},{4,10},{6,8},{9,7},{11,5},{13,3},{15,1},{16,30},{18,... | collective-permute-start | bytes 589832 | tf_op jit(solution)/shard_map/ppermute | solution.py:242
  36.4 2.7 %collective-permute-done.5.other_ref.mine_ref = bf16[48,2048]{1,0:T(8,128)(2,1)S(1)} collective-permute-done((bf16[48,2048]{1,0:T(8,128)(2,1)S(1)}, bf16[48,2048]{1,0:T(8,128)(2,1)S(1)}, u32[]{:S(2)}, u32[]{:S(2)}) %collective-permute-start.5) | collective-permute-done | bytes 196640 | tf_op jit(solution)/shard_map/ppermute | solution.py:242
  39.1 1.1 %collective-permute-start.7 = (bf16[48,2048]{1,0:T(8,128)(2,1)S(1)}, bf16[48,2048]{1,0:T(8,128)(2,1)S(1)}, u32[]{:S(2)}, u32[]{:S(2)}) collective-permute-start(bf16[48,2048]{1,0:T(8,128)(2,1)S(1)} %shard_map.44.refs_0_), channel_id=1, source_target_pairs={{0,4},{1,5},{2,6},{3,7},{4,0},{5,1},{6,2},{7,3},{8,12},{9,13},{10,... | collective-permute-start | bytes 589832 | tf_op jit(solution)/shard_map/ppermute | solution.py:242
  40.2 1.5 %collective-permute-start.6 = (bf16[48,2048]{1,0:T(8,128)(2,1)S(1)}, bf16[48,2048]{1,0:T(8,128)(2,1)S(1)}, u32[]{:S(2)}, u32[]{:S(2)}) collective-permute-start(bf16[48,2048]{1,0:T(8,128)(2,1)S(1)} %shard_map.44.refs_0_), channel_id=1, source_target_pairs={{0,2},{1,3},{2,0},{3,1},{4,6},{5,7},{6,4},{7,5},{8,10},{9,11},{10,... | collective-permute-start | bytes 589832 | tf_op jit(solution)/shard_map/ppermute | solution.py:242
  41.7 1.8 %collective-permute-start.10 = (bf16[48,2048]{1,0:T(8,128)(2,1)S(1)}, bf16[48,2048]{1,0:T(8,128)(2,1)S(1)}, u32[]{:S(2)}, u32[]{:S(2)}) collective-permute-start(bf16[48,2048]{1,0:T(8,128)(2,1)S(1)} %shard_map.44.refs_0_), channel_id=1, source_target_pairs={{0,16},{1,17},{2,18},{3,19},{4,20},{5,21},{6,22},{7,23},{8,24},{9,... | collective-permute-start | bytes 589832 | tf_op jit(solution)/shard_map/ppermute | solution.py:242
  43.4 2.2 %collective-permute-done.7.refs_1_.refs_0_ = bf16[48,2048]{1,0:T(8,128)(2,1)S(1)} collective-permute-done((bf16[48,2048]{1,0:T(8,128)(2,1)S(1)}, bf16[48,2048]{1,0:T(8,128)(2,1)S(1)}, u32[]{:S(2)}, u32[]{:S(2)}) %collective-permute-start.7) | collective-permute-done | bytes 196640 | tf_op jit(solution)/shard_map/ppermute | solution.py:242
  45.6 0.5 shard_map.45.refs_3_
  46.1 0.5 collective-permute-done.6.refs_1_.refs_0_
  46.6 0.5 shard_map.46.refs_2_
  47.1 0.3 shard_map.48
  47.4 0.6 %collective-permute-start.11 = (f32[48,128]{1,0:T(8,128)S(1)}, f32[48,128]{1,0:T(8,128)S(1)}, u32[]{:S(2)}, u32[]{:S(2)}) collective-permute-start(f32[48,128]{1,0:T(8,128)S(1)} %shard_map.48), channel_id=1, source_target_pairs={{0,16},{1,17},{2,18},{3,19},{4,20},{5,21},{6,22},{7,23},{8,24},{9,... | collective-permute-start | bytes 73736 | tf_op jit(solution)/shard_map/ppermute | solution.py:242
  48.0 0.3 shard_map.50.theirs_ref
  48.3 0.5 shard_map.49.mine_ref
  48.8 2.5 %collective-permute-done.11.other_ref = f32[48,128]{1,0:T(8,128)S(1)} collective-permute-done((f32[48,128]{1,0:T(8,128)S(1)}, f32[48,128]{1,0:T(8,128)S(1)}, u32[]{:S(2)}, u32[]{:S(2)}) %collective-permute-start.11) | collective-permute-done | bytes 24608 | tf_op jit(solution)/shard_map/ppermute | solution.py:242
  51.3 0.1 collective-permute-start.12
  51.4 1.2 %collective-permute-done.12 = f32[48,128]{1,0:T(8,128)S(1)} collective-permute-done((f32[48,128]{1,0:T(8,128)S(1)}, f32[48,128]{1,0:T(8,128)S(1)}, u32[]{:S(2)}, u32[]{:S(2)}) %collective-permute-start.12) | collective-permute-done | bytes 24608 | tf_op jit(solution)/shard_map/ppermute | solution.py:242
  52.6 0.6 %add.11 = f32[48,128]{1,0:T(8,128)} add(f32[48,128]{1,0:T(8,128)S(1)} %get-tuple-element.61, f32[48,128]{1,0:T(8,128)S(1)} %collective-permute-done.12) | non-fusion elementwise | flops 6144 | bytes 73728 | tf_op jit(solution)/shard_map/add | solution.py:315
  (18 shorter events, 0.2 us)
Async XLA Ops:
  0.0 1.5 %copy-start = (bf16[96,2048]{1,0:T(8,128)(2,1)S(1)}, bf16[96,2048]{1,0:T(8,128)(2,1)}, u32[]{:S(2)}) copy-start(bf16[96,2048]{1,0:T(8,128)(2,1)} %param.3) | copy-start | bytes 1179652
  1.5 11.6 %collective-permute-start = (bf16[48,2048]{1,0:T(8,128)(2,1)S(1)}, bf16[48,2048]{1,0:T(8,128)(2,1)S(1)}, u32[]{:S(2)}, u32[]{:S(2)}) collective-permute-start(bf16[48,2048]{1,0:T(8,128)(2,1)S(1)} %constant_dynamic-slice_fusion.mine_ref), channel_id=1, source_target_pairs={{0,8},{1,6},{2,10},{3,4},{4,12},{5,2},{6,14},{7,0},{8,15},{9,1},{1... | collective-permute-start | bytes 589832 | tf_op jit(solution)/shard_map/ppermute | solution.py:242
  5.6 40.0 %collective-permute-start.9 = (bf16[128,6144]{1,0:T(8,128)(2,1)S(1)}, bf16[128,6144]{1,0:T(8,128)(2,1)S(1)}, u32[]{:S(2)}, u32[]{:S(2)}) collective-permute-start(bf16[128,6144]{1,0:T(8,128)(2,1)S(1)} %shard_map.37), channel_id=1, source_target_pairs={{0,16},{1,17},{2,18},{3,19},{4,20},{5,21},{6,22},{7,23},{8,24},{9,... | collective-permute-start | bytes 4718600 | tf_op jit(solution)/shard_map/ppermute | solution.py:242
  13.1 7.1 %collective-permute-start.3 = (bf16[48,2048]{1,0:T(8,128)(2,1)S(1)}, bf16[48,2048]{1,0:T(8,128)(2,1)S(1)}, u32[]{:S(2)}, u32[]{:S(2)}) collective-permute-start(bf16[48,2048]{1,0:T(8,128)(2,1)S(1)} %shard_map.39.refs_1_), channel_id=1, source_target_pairs={{0,4},{1,5},{2,6},{3,7},{4,0},{5,1},{6,2},{7,3},{8,12},{9,13},{10,... | collective-permute-start | bytes 589832 | tf_op jit(solution)/shard_map/ppermute | solution.py:242
  14.8 8.3 %collective-permute-start.2 = (bf16[48,2048]{1,0:T(8,128)(2,1)S(1)}, bf16[48,2048]{1,0:T(8,128)(2,1)S(1)}, u32[]{:S(2)}, u32[]{:S(2)}) collective-permute-start(bf16[48,2048]{1,0:T(8,128)(2,1)S(1)} %shard_map.39.refs_1_), channel_id=1, source_target_pairs={{0,2},{1,3},{2,0},{3,1},{4,6},{5,7},{6,4},{7,5},{8,10},{9,11},{10,... | collective-permute-start | bytes 589832 | tf_op jit(solution)/shard_map/ppermute | solution.py:242
  19.8 6.6 %collective-permute-start.1 = (bf16[48,2048]{1,0:T(8,128)(2,1)S(1)}, bf16[48,2048]{1,0:T(8,128)(2,1)S(1)}, u32[]{:S(2)}, u32[]{:S(2)}) collective-permute-start(bf16[48,2048]{1,0:T(8,128)(2,1)S(1)} %shard_map.39.refs_1_), channel_id=1, source_target_pairs={{0,6},{1,7},{2,4},{3,5},{4,2},{5,3},{6,0},{7,1},{8,14},{9,15},{10,... | collective-permute-start | bytes 589832 | tf_op jit(solution)/shard_map/ppermute | solution.py:242
  26.4 19.2 %copy-start.2 = (bf16[128,8192]{1,0:T(8,128)(2,1)S(1)}, bf16[128,8192]{1,0:T(8,128)(2,1)}, u32[]{:S(2)}) copy-start(bf16[128,8192]{1,0:T(8,128)(2,1)} %refs_1_.1) | copy-start | bytes 6291460
  29.1 1.8 %collective-permute-start.4 = (f32[48,2048]{1,0:T(8,128)S(1)}, f32[48,2048]{1,0:T(8,128)S(1)}, u32[]{:S(2)}, u32[]{:S(2)}) collective-permute-start(f32[48,2048]{1,0:T(8,128)S(1)} %shard_map.43), channel_id=1, source_target_pairs={{0,1},{1,0},{2,3},{3,2},{4,5},{5,4},{6,7},{7,6},{8,9},{9,8},{10,11... | collective-permute-start | bytes 1179656 | tf_op jit(solution)/shard_map/ppermute | solution.py:242
  30.9 8.2 %collective-permute-start.5 = (bf16[48,2048]{1,0:T(8,128)(2,1)S(1)}, bf16[48,2048]{1,0:T(8,128)(2,1)S(1)}, u32[]{:S(2)}, u32[]{:S(2)}) collective-permute-start(bf16[48,2048]{1,0:T(8,128)(2,1)S(1)} %add_convert_fusion.mine_ref), channel_id=1, source_target_pairs={{0,8},{1,6},{2,10},{3,4},{4,12},{5,2},{6,14},{7,0},{8,15},{9,1},{1... | collective-permute-start | bytes 589832 | tf_op jit(solution)/shard_map/ppermute | solution.py:242
  32.4 11.1 %collective-permute-start.8 = (bf16[48,2048]{1,0:T(8,128)(2,1)S(1)}, bf16[48,2048]{1,0:T(8,128)(2,1)S(1)}, u32[]{:S(2)}, u32[]{:S(2)}) collective-permute-start(bf16[48,2048]{1,0:T(8,128)(2,1)S(1)} %add_convert_fusion.mine_ref), channel_id=1, source_target_pairs={{0,14},{2,12},{4,10},{6,8},{9,7},{11,5},{13,3},{15,1},{16,30},{18,... | collective-permute-start | bytes 589832 | tf_op jit(solution)/shard_map/ppermute | solution.py:242
  39.1 6.5 %collective-permute-start.7 = (bf16[48,2048]{1,0:T(8,128)(2,1)S(1)}, bf16[48,2048]{1,0:T(8,128)(2,1)S(1)}, u32[]{:S(2)}, u32[]{:S(2)}) collective-permute-start(bf16[48,2048]{1,0:T(8,128)(2,1)S(1)} %shard_map.44.refs_0_), channel_id=1, source_target_pairs={{0,4},{1,5},{2,6},{3,7},{4,0},{5,1},{6,2},{7,3},{8,12},{9,13},{10,... | collective-permute-start | bytes 589832 | tf_op jit(solution)/shard_map/ppermute | solution.py:242
  40.2 6.4 %collective-permute-start.6 = (bf16[48,2048]{1,0:T(8,128)(2,1)S(1)}, bf16[48,2048]{1,0:T(8,128)(2,1)S(1)}, u32[]{:S(2)}, u32[]{:S(2)}) collective-permute-start(bf16[48,2048]{1,0:T(8,128)(2,1)S(1)} %shard_map.44.refs_0_), channel_id=1, source_target_pairs={{0,2},{1,3},{2,0},{3,1},{4,6},{5,7},{6,4},{7,5},{8,10},{9,11},{10,... | collective-permute-start | bytes 589832 | tf_op jit(solution)/shard_map/ppermute | solution.py:242
  41.7 6.3 %collective-permute-start.10 = (bf16[48,2048]{1,0:T(8,128)(2,1)S(1)}, bf16[48,2048]{1,0:T(8,128)(2,1)S(1)}, u32[]{:S(2)}, u32[]{:S(2)}) collective-permute-start(bf16[48,2048]{1,0:T(8,128)(2,1)S(1)} %shard_map.44.refs_0_), channel_id=1, source_target_pairs={{0,16},{1,17},{2,18},{3,19},{4,20},{5,21},{6,22},{7,23},{8,24},{9,... | collective-permute-start | bytes 589832 | tf_op jit(solution)/shard_map/ppermute | solution.py:242
  46.6 6.6 %copy-start.1 = (bf16[96,2048]{1,0:T(8,128)(2,1)S(1)}, bf16[96,2048]{1,0:T(8,128)(2,1)}, u32[]{:S(2)}) copy-start(bf16[96,2048]{1,0:T(8,128)(2,1)} %param.3) | copy-start | bytes 1179652
  47.4 3.9 %collective-permute-start.11 = (f32[48,128]{1,0:T(8,128)S(1)}, f32[48,128]{1,0:T(8,128)S(1)}, u32[]{:S(2)}, u32[]{:S(2)}) collective-permute-start(f32[48,128]{1,0:T(8,128)S(1)} %shard_map.48), channel_id=1, source_target_pairs={{0,16},{1,17},{2,18},{3,19},{4,20},{5,21},{6,22},{7,23},{8,24},{9,... | collective-permute-start | bytes 73736 | tf_op jit(solution)/shard_map/ppermute | solution.py:242
  51.3 1.3 %collective-permute-start.12 = (f32[48,128]{1,0:T(8,128)S(1)}, f32[48,128]{1,0:T(8,128)S(1)}, u32[]{:S(2)}, u32[]{:S(2)}) collective-permute-start(f32[48,128]{1,0:T(8,128)S(1)} %get-tuple-element.62), channel_id=1, source_target_pairs={{0,1},{1,0},{2,3},{3,2},{4,5},{5,4},{6,7},{7,6},{8,9},{9,8},{10,11... | collective-permute-start | bytes 73736 | tf_op jit(solution)/shard_map/ppermute | solution.py:242

commit v22 on v21

--- a/solution.py
+++ b/solution.py
@@ -45,76 +45,75 @@
 ORDER = (0, 2, 1, 3)
 
 
-def half_copies(fisher_ref, block, half, held_ref, sem):
-    steps = sem.shape[0]
+def block_copies(fisher_ref, block, start, held_ref, sem):
     rows, width = held_ref.shape
-    step = rows // steps
+    step = 512
     columns = pl.ds(pl.multiple_of(block * width, width), width)
-    copies = []
-    for i in range(steps):
-        copies.append(
-            pltpu.make_async_copy(
-                fisher_ref.at[pl.ds(half * rows + i * step, step), columns],
-                held_ref.at[pl.ds(i * step, step), :],
-                sem.at[i],
-            )
+    return [
+        pltpu.make_async_copy(
+            fisher_ref.at[pl.ds(start + i * step, step), columns],
+            held_ref.at[pl.ds(i * step, step), :],
+            sem.at[i],
         )
-    return copies
+        for i in range(rows // step)
+    ]
 
 
 def times(chunk_ref, fisher):
     return lax.dot_general(chunk_ref[...], fisher, NT, preferred_element_type=jnp.float32)
 
 
-def fisher_kernel(dims, n_in, has_base, fetch, *refs):
+def fisher_kernel(dims, n_parts, has_base, fetch, *refs):
     if fetch:
         column = Place(*dims).column
         fisher_ref, *refs = refs
-    chunk_ref, halves = (refs[0], refs[1:3]) if n_in else (None, ())
-    base_ref = refs[3] if has_base else None
+    n_in = n_parts + bool(n_parts)
+    chunk_ref, parts = (refs[0], refs[1:n_in]) if n_parts else (None, ())
+    base_ref = refs[n_in] if has_base else None
     outs, sem = refs[n_in + has_base : -1], refs[-1]
-    held = outs[1:] if n_in else outs
+    held = outs[1:] if n_parts else outs
     copies = []
-    for k, (piece, half) in enumerate(fetch):
-        for copy in half_copies(fisher_ref, column ^ ORDER[piece], half, held[k], sem.at[k]):
+    for k, (piece, start, _) in enumerate(fetch):
+        for copy in block_copies(fisher_ref, column ^ ORDER[piece], start, held[k], sem.at[k]):
             copy.start()
             copies.append(copy)
 
-    def product(h, start, step):
-        columns = pl.ds(h * halves[h].shape[0] + start, step)
-        term = times(chunk_ref, halves[h][pl.ds(start, step), :])
-        outs[0][:, columns] = term + base_ref[:, columns] if has_base else term
-
-    if halves:
-        rows = halves[0].shape[0]
-        step = rows // 2 if fetch else rows
-
-        @pl.loop(0, rows // step)
+    if parts:
+        loops = 2 if fetch else 1
+
+        @pl.loop(0, loops)
         def _(i):
-            for h in range(len(halves)):
-                product(h, pl.multiple_of(i * step, step), step)
+            before = 0
+            for part_ref in parts:
+                rows = part_ref.shape[0]
+                step = rows // loops
+                start = pl.multiple_of(i * step, step)
+                columns = pl.ds(before + start, step)
+                term = times(chunk_ref, part_ref[pl.ds(start, step), :])
+                outs[0][:, columns] = term + base_ref[:, columns] if has_base else term
+                before += rows
 
     for copy in copies:
         copy.wait()
 
 
-def fisher_step(fisher, dims, width, fetch, chunk=None, halves=(), base=None):
-    rows = fisher.shape[0]
-    ins = [] if chunk is None else [chunk, *halves]
+def fisher_step(fisher, dims, width, fetch, chunk=None, parts=(), base=None):
+    total = fisher.shape[0]
+    ins = [] if chunk is None else [chunk, *parts]
     has_base = base is not None
-    held = jax.ShapeDtypeStruct((rows // 2, width), fisher.dtype)
-    out_shape = [] if chunk is None else [jax.ShapeDtypeStruct((chunk.shape[0], rows), jnp.float32)]
-    out_shape += [held] * len(fetch)
-    return pl.pallas_call(
-        functools.partial(fisher_kernel, dims, len(ins), has_base, fetch),
+    out_shape = [] if chunk is None else [jax.ShapeDtypeStruct((chunk.shape[0], total), jnp.float32)]
+    out_shape += [jax.ShapeDtypeStruct((rows, width), fisher.dtype) for _, _, rows in fetch]
+    fetched = sum(rows for _, _, rows in fetch)
+    return pl.pallas_call(
+        functools.partial(fisher_kernel, dims, len(parts), has_base, fetch),
         out_shape=out_shape,
         in_specs=[HBM] * bool(fetch) + [VMEM] * (len(ins) + has_base),
         out_specs=[VMEM] * len(out_shape),
         scratch_shapes=[pltpu.SemaphoreType.DMA((max(len(fetch), 1), 2))],
         compiler_params=limit(34 if chunk is None else 20),
         cost_estimate=pl.CostEstimate(
-            flops=0 if chunk is None else 2 * chunk.shape[0] * width * rows,
-            bytes_accessed=width * rows * (len(fetch) + 2 * bool(ins)),
+            flops=0 if chunk is None else 2 * chunk.shape[0] * width * total,
+            bytes_accessed=2 * width * (fetched + total * bool(ins)),
             transcendentals=0,
         ),
     )(*([fisher] if fetch else []), *ins, *([base] if has_base else []))
@@ -291,24 +290,24 @@
     own, to_y = lax.optimization_barrier((own, to_y))
     other_grads = swap_y(to_y)
     step = functools.partial(fisher_step, inverse_fisher, dims, width)
-    a0, a1, b0, b1 = step(((0, 0), (0, 1), (1, 0), (1, 1)))
+    half, quarter = inverse_fisher.shape[0] // 2, inverse_fisher.shape[0] // 4
+    a0, a1, b0, b1 = step(((0, 0, half), (0, half, half), (1, 0, half), (1, half, half)))
     q0, q1, q2, last = gather(own, False, (a0,))
-    total0, c0, c1 = step(((2, 0), (2, 1)), q0, (a0, a1))
-    total, d0 = step(((3, 0),), q1, (b0, b1), total0)
-    total, d1 = step(((3, 1),), q2, (c0, c1), total)
+    total0, c0, c1 = step(((2, 0, half), (2, half, quarter)), q0, (a0, a1))
+    total, c2, d0 = step(((2, half + quarter, quarter), (3, 0, half)), q1, (b0, b1), total0)
+    total, d1 = step(((3, half, half),), q2, (c0, c1, c2), total)
     (total,) = step((), last(total0, total), (d0, d1), total)
     panel = (total + swap_core(total)).astype(jnp.bfloat16)
 
     p0, p1, p2, last = gather(panel, True)
     swapped = swap_y(p0)
     p1, other_grads = lax.optimization_barrier((p1, other_grads))
-    mine = score_dot([p0, p1], ORDER[:2], dims, stored_grads)
-    p2, _ = lax.optimization_barrier((p2, mine))
-    other = score_dot([p1, p2], (0, 1), None, other_grads)
-    p3 = last(other, other)
-    other = score_dot([p3], (2,), None, other_grads, other)
-    p2, p3, mine, swapped, _ = lax.optimization_barrier((p2, p3, mine, swapped, other))
-    mine = score_dot([p2, p3], ORDER[2:], dims, stored_grads, mine)
+    p3 = last(p1, p1)
+    other = score_dot([p1, p3], (0, 2), None, other_grads)
+    p2, _ = lax.optimization_barrier((p2, other))
+    other = score_dot([p2], (1,), None, other_grads, other)
+    p2, swapped, _ = lax.optimization_barrier((p2, swapped, other))
+    mine = score_dot([p0, p1, p2, p3], ORDER, dims, stored_grads)
     theirs = score_dot([swapped], ORDER[:1], dims, stored_grads)
 
     keep, give = sort_out(mine, swap_y(other), theirs)

time: 53.3 us -> 52.3 us (0.981)
  waiting for transfers between devices: 11.3 us -> 10.4 us
  Pallas kernels: 21.2 us -> 20.6 us
    ppermute x13, waiting for transfers between devices: 11.3 us -> 10.4 us  [move(): return lax.ppermute(value, AXES, pairs)]
    pallas_call x5 -> x4, Pallas kernels: 2.01 us -> 1.89 us  [score_dot(): pl.pallas_call(functools.partial(score_kernel, dims, order, base is not N...]
  transfers between devices with their start and end apart: 13 -> 13, of which waited for: 7 -> 9; matrix products, arithmetic and copies ran while one was open for 0% -> 0% of each run, Pallas kernels for 37% -> 37%
where the time goes in v22:
time: 52.3 us; the launch traced here: 52.2 us
  Pallas kernels  20.6 us (39%)
  starting transfers between devices  20.3 us (39%)
  waiting for transfers between devices  10.4 us (20%)
  other arithmetic  0.65 us (1%)
    ppermute x13, starting transfers between devices, move(): return lax.ppermute(value, AXES, pairs)  20.3 us
    pallas_call x5, Pallas kernels, fisher_step(): pl.pallas_call(functools.partial(fisher_kernel, dims, len(parts), has_bas...  17.2 us
    ppermute x13, waiting for transfers between devices, move(): return lax.ppermute(value, AXES, pairs)  10.4 us
    pallas_call x4, Pallas kernels, score_dot(): pl.pallas_call(functools.partial(score_kernel, dims, order, base is not N...  1.89 us
    pallas_call x1, Pallas kernels, cut(): pl.pallas_call(functools.partial(cut_kernel, dims, order), out_shape=jax....  1.43 us
  transfers between devices with their start and end apart: 13, of which 9 were waited for; matrix products, arithmetic and copies ran while one was open for 0% of the time, Pallas kernels for 37%

profile of v22, /device:TPU:0, one launch (start us, length us, event | category | flops | bytes accessed | tf_op | source)
XLA Modules:
  0.0 52.2 jit_solution(17075517153840882849)
XLA Ops:
  0.0 1.4 %shard_map.37 = bf16[128,6144]{1,0:T(8,128)(2,1)S(1)} custom-call(bf16[128,8192]{1,0:T(8,128)(2,1)} %refs_1_.1), custom_call_target="tpu_custom_call" | custom-call | bytes 1572864 | tf_op jit(solution)/shard_map/pallas_call | solution.py:172
  1.5 4.1 %collective-permute-start = (bf16[48,2048]{1,0:T(8,128)(2,1)S(1)}, bf16[48,2048]{1,0:T(8,128)(2,1)S(1)}, u32[]{:S(2)}, u32[]{:S(2)}) collective-permute-start(bf16[48,2048]{1,0:T(8,128)(2,1)S(1)} %constant_dynamic-slice_fusion.mine_ref), channel_id=1, source_target_pairs={{0,8},{1,6},{2,10},{3,4},{4,12},{5,2},{6,14},{7,0},{8,15},{9,1},{1... | collective-permute-start | bytes 589832 | tf_op jit(solution)/shard_map/ppermute | solution.py:241
  5.6 1.5 %collective-permute-start.8 = (bf16[128,6144]{1,0:T(8,128)(2,1)S(1)}, bf16[128,6144]{1,0:T(8,128)(2,1)S(1)}, u32[]{:S(2)}, u32[]{:S(2)}) collective-permute-start(bf16[128,6144]{1,0:T(8,128)(2,1)S(1)} %shard_map.37), channel_id=1, source_target_pairs={{0,16},{1,17},{2,18},{3,19},{4,20},{5,21},{6,22},{7,23},{8,24},{9,... | collective-permute-start | bytes 4718600 | tf_op jit(solution)/shard_map/ppermute | solution.py:241
  7.1 6.0 %shard_map.38 = (bf16[1024,2048]{1,0:T(8,128)(2,1)S(1)}, bf16[1024,2048]{1,0:T(8,128)(2,1)S(1)}, bf16[1024,2048]{1,0:T(8,128)(2,1)S(1)}, bf16[1024,2048]{1,0:T(8,128)(2,1)S(1)}) custom-call(bf16[2048,8192]{1,0:T(8,128)(2,1)} %refs_0_.7), custom_call_target="tpu_custom_call" | custom-call | bytes 16777216 | tf_op jit(solution)/shard_map/pallas_call | solution.py:107
  13.1 1.6 %collective-permute-start.3 = (bf16[48,2048]{1,0:T(8,128)(2,1)S(1)}, bf16[48,2048]{1,0:T(8,128)(2,1)S(1)}, u32[]{:S(2)}, u32[]{:S(2)}) collective-permute-start(bf16[48,2048]{1,0:T(8,128)(2,1)S(1)} %shard_map.39.refs_1_), channel_id=1, source_target_pairs={{0,4},{1,5},{2,6},{3,7},{4,0},{5,1},{6,2},{7,3},{8,12},{9,13},{10,... | collective-permute-start | bytes 589832 | tf_op jit(solution)/shard_map/ppermute | solution.py:241
  14.8 1.5 %collective-permute-start.2 = (bf16[48,2048]{1,0:T(8,128)(2,1)S(1)}, bf16[48,2048]{1,0:T(8,128)(2,1)S(1)}, u32[]{:S(2)}, u32[]{:S(2)}) collective-permute-start(bf16[48,2048]{1,0:T(8,128)(2,1)S(1)} %shard_map.39.refs_1_), channel_id=1, source_target_pairs={{0,2},{1,3},{2,0},{3,1},{4,6},{5,7},{6,4},{7,5},{8,10},{9,11},{10,... | collective-permute-start | bytes 589832 | tf_op jit(solution)/shard_map/ppermute | solution.py:241
  16.3 2.9 %shard_map.40 = (f32[48,2048]{1,0:T(8,128)S(1)}, bf16[1024,2048]{1,0:T(8,128)(2,1)S(1)}, bf16[512,2048]{1,0:T(8,128)(2,1)S(1)}) custom-call(bf16[2048,8192]{1,0:T(8,128)(2,1)} %refs_0_.7, bf16[48,2048]{1,0:T(8,128)(2,1)S(1)} %shard_map.39.refs_1_, bf16[1024,2048]{1,0:T(8,128)(2,1)S(1)} %get-tuple-element.36.refs_0_.refs_2_, ...), custom_call_target="tpu_custom_call" | custom-call | flops 402653184 | bytes 14680064 | tf_op jit(solution)/shard_map/pallas_call | solution.py:107
  19.2 0.5 collective-permute-start.1
  19.6 0.1 collective-permute-done.3.refs_1_
  19.7 2.9 %shard_map.41 = (f32[48,2048]{1,0:T(8,128)S(1)}, bf16[512,2048]{1,0:T(8,128)(2,1)S(1)}, bf16[1024,2048]{1,0:T(8,128)(2,1)S(1)}) custom-call(bf16[2048,8192]{1,0:T(8,128)(2,1)} %refs_0_.7, bf16[48,2048]{1,0:T(8,128)(2,1)S(1)} %collective-permute-done.3.refs_1_, bf16[1024,2048]{1,0:T(8,128)(2,1)S(1)} %get-tuple-element.42.refs_2_, ...), custom_call_target="tpu_custom_call" | custom-call | flops 402653184 | bytes 14680064 | tf_op jit(solution)/shard_map/pallas_call | solution.py:107
  22.7 2.8 %shard_map.42 = (f32[48,2048]{1,0:T(8,128)S(1)}, bf16[1024,2048]{1,0:T(8,128)(2,1)S(1)}) custom-call(bf16[2048,8192]{1,0:T(8,128)(2,1)} %refs_0_.7, bf16[48,2048]{1,0:T(8,128)(2,1)S(1)} %collective-permute-done.2.refs_1_, bf16[1024,2048]{1,0:T(8,128)(2,1)S(1)} %get-tuple-element.40.refs_2_, bf16[512,2048]{1,0:T(8,128)(2,1)S(1)} %get-tuple-element.41.refs_3_, ...), custom_call_target="tpu_custom_call" | custom-call | flops 402653184 | bytes 12582912 | tf_op jit(solution)/shard_map/pallas_call | solution.py:107
  25.5 0.3 collective-permute-done.1.refs_0_
  25.8 2.6 %shard_map.43 = f32[48,2048]{1,0:T(8,128)S(1)} custom-call(bf16[48,2048]{1,0:T(8,128)(2,1)S(1)} %collective-permute-done.1.refs_0_, bf16[1024,2048]{1,0:T(8,128)(2,1)S(1)} %get-tuple-element.48.refs_1_, bf16[1024,2048]{1,0:T(8,128)(2,1)S(1)} %get-tuple-element.49.refs_2_, f32[48,2048]{1,0:T(8,128)S(1)} %get-tuple-element.46.refs_3_), custom_call_target="tpu_custom_call" | custom-call | flops 402653184 | bytes 8388608 | tf_op jit(solution)/shard_map/pallas_call | solution.py:107
  28.5 0.1 collective-permute-start.4
  28.5 1.7 %collective-permute-done.4 = f32[48,2048]{1,0:T(8,128)S(1)} collective-permute-done((f32[48,2048]{1,0:T(8,128)S(1)}, f32[48,2048]{1,0:T(8,128)S(1)}, u32[]{:S(2)}, u32[]{:S(2)}) %collective-permute-start.4) | collective-permute-done | bytes 393248 | tf_op jit(solution)/shard_map/ppermute | solution.py:241
  30.3 1.6 %collective-permute-start.5 = (bf16[48,2048]{1,0:T(8,128)(2,1)S(1)}, bf16[48,2048]{1,0:T(8,128)(2,1)S(1)}, u32[]{:S(2)}, u32[]{:S(2)}) collective-permute-start(bf16[48,2048]{1,0:T(8,128)(2,1)S(1)} %add_convert_fusion.mine_ref), channel_id=1, source_target_pairs={{0,8},{1,6},{2,10},{3,4},{4,12},{5,2},{6,14},{7,0},{8,15},{9,1},{1... | collective-permute-start | bytes 589832 | tf_op jit(solution)/shard_map/ppermute | solution.py:241
  31.9 4.0 %collective-permute-start.7 = (bf16[48,2048]{1,0:T(8,128)(2,1)S(1)}, bf16[48,2048]{1,0:T(8,128)(2,1)S(1)}, u32[]{:S(2)}, u32[]{:S(2)}) collective-permute-start(bf16[48,2048]{1,0:T(8,128)(2,1)S(1)} %add_convert_fusion.mine_ref), channel_id=1, source_target_pairs={{0,14},{2,12},{4,10},{6,8},{9,7},{11,5},{13,3},{15,1},{16,30},{18,... | collective-permute-start | bytes 589832 | tf_op jit(solution)/shard_map/ppermute | solution.py:241
  35.9 2.6 %collective-permute-done.5.other_ref.mine_ref = bf16[48,2048]{1,0:T(8,128)(2,1)S(1)} collective-permute-done((bf16[48,2048]{1,0:T(8,128)(2,1)S(1)}, bf16[48,2048]{1,0:T(8,128)(2,1)S(1)}, u32[]{:S(2)}, u32[]{:S(2)}) %collective-permute-start.5) | collective-permute-done | bytes 196640 | tf_op jit(solution)/shard_map/ppermute | solution.py:241
  38.5 1.1 %collective-permute-start.6 = (bf16[48,2048]{1,0:T(8,128)(2,1)S(1)}, bf16[48,2048]{1,0:T(8,128)(2,1)S(1)}, u32[]{:S(2)}, u32[]{:S(2)}) collective-permute-start(bf16[48,2048]{1,0:T(8,128)(2,1)S(1)} %shard_map.44.refs_0_), channel_id=1, source_target_pairs={{0,4},{1,5},{2,6},{3,7},{4,0},{5,1},{6,2},{7,3},{8,12},{9,13},{10,... | collective-permute-start | bytes 589832 | tf_op jit(solution)/shard_map/ppermute | solution.py:241
  39.6 1.6 %collective-permute-start.9 = (bf16[48,2048]{1,0:T(8,128)(2,1)S(1)}, bf16[48,2048]{1,0:T(8,128)(2,1)S(1)}, u32[]{:S(2)}, u32[]{:S(2)}) collective-permute-start(bf16[48,2048]{1,0:T(8,128)(2,1)S(1)} %shard_map.44.refs_0_), channel_id=1, source_target_pairs={{0,2},{1,3},{2,0},{3,1},{4,6},{5,7},{6,4},{7,5},{8,10},{9,11},{10,... | collective-permute-start | bytes 589832 | tf_op jit(solution)/shard_map/ppermute | solution.py:241
  41.2 1.9 %collective-permute-start.10 = (bf16[48,2048]{1,0:T(8,128)(2,1)S(1)}, bf16[48,2048]{1,0:T(8,128)(2,1)S(1)}, u32[]{:S(2)}, u32[]{:S(2)}) collective-permute-start(bf16[48,2048]{1,0:T(8,128)(2,1)S(1)} %shard_map.44.refs_0_), channel_id=1, source_target_pairs={{0,16},{1,17},{2,18},{3,19},{4,20},{5,21},{6,22},{7,23},{8,24},{9,... | collective-permute-start | bytes 589832 | tf_op jit(solution)/shard_map/ppermute | solution.py:241
  43.1 2.0 %collective-permute-done.6.refs_0_.refs_1_ = bf16[48,2048]{1,0:T(8,128)(2,1)S(1)} collective-permute-done((bf16[48,2048]{1,0:T(8,128)(2,1)S(1)}, bf16[48,2048]{1,0:T(8,128)(2,1)S(1)}, u32[]{:S(2)}, u32[]{:S(2)}) %collective-permute-start.6) | collective-permute-done | bytes 196640 | tf_op jit(solution)/shard_map/ppermute | solution.py:241
  45.2 0.5 shard_map.46.refs_2_
  45.6 0.5 collective-permute-done.9.refs_0_.refs_2_
  46.1 0.3 shard_map.47
  46.4 0.7 %collective-permute-start.11 = (f32[48,128]{1,0:T(8,128)S(1)}, f32[48,128]{1,0:T(8,128)S(1)}, u32[]{:S(2)}, u32[]{:S(2)}) collective-permute-start(f32[48,128]{1,0:T(8,128)S(1)} %shard_map.47), channel_id=1, source_target_pairs={{0,16},{1,17},{2,18},{3,19},{4,20},{5,21},{6,22},{7,23},{8,24},{9,... | collective-permute-start | bytes 73736 | tf_op jit(solution)/shard_map/ppermute | solution.py:241
  47.1 0.2 collective-permute-done.10.refs_0_
  47.3 0.3 shard_map.49.theirs_ref
  47.6 0.8 %shard_map.48.mine_ref = f32[48,128]{1,0:T(8,128)S(1)} custom-call(bf16[48,2048]{1,0:T(8,128)(2,1)S(1)} %shard_map.44.refs_0_, bf16[48,2048]{1,0:T(8,128)(2,1)S(1)} %collective-permute-done.6.refs_0_.refs_1_, bf16[48,2048]{1,0:T(8,128)(2,1)S(1)} %collective-permute-done.9.refs_0_.refs_2_, bf16[48,2048]{1,0:T(8,128)(2,1)S(1)} %shard_map.45.refs_1_.refs_3_, ...), custom_call_target="tpu_custom_call" | custom-call | flops 100663296 | bytes 2097152 | tf_op jit(solution)/shard_map/pallas_call | solution.py:140
  48.4 1.8 %collective-permute-done.11.other_ref = f32[48,128]{1,0:T(8,128)S(1)} collective-permute-done((f32[48,128]{1,0:T(8,128)S(1)}, f32[48,128]{1,0:T(8,128)S(1)}, u32[]{:S(2)}, u32[]{:S(2)}) %collective-permute-start.11) | collective-permute-done | bytes 24608 | tf_op jit(solution)/shard_map/ppermute | solution.py:241
  50.4 1.2 %collective-permute-done.12 = f32[48,128]{1,0:T(8,128)S(1)} collective-permute-done((f32[48,128]{1,0:T(8,128)S(1)}, f32[48,128]{1,0:T(8,128)S(1)}, u32[]{:S(2)}, u32[]{:S(2)}) %collective-permute-start.12) | collective-permute-done | bytes 24608 | tf_op jit(solution)/shard_map/ppermute | solution.py:241
  51.6 0.6 %add.11 = f32[48,128]{1,0:T(8,128)} add(f32[48,128]{1,0:T(8,128)S(1)} %get-tuple-element.59, f32[48,128]{1,0:T(8,128)S(1)} %collective-permute-done.12) | non-fusion elementwise | flops 6144 | bytes 73728 | tf_op jit(solution)/shard_map/add | solution.py:314
  (17 shorter events, 0.2 us)
Async XLA Ops:
  0.0 1.5 %copy-start = (bf16[96,2048]{1,0:T(8,128)(2,1)S(1)}, bf16[96,2048]{1,0:T(8,128)(2,1)}, u32[]{:S(2)}) copy-start(bf16[96,2048]{1,0:T(8,128)(2,1)} %param.3) | copy-start | bytes 1179652
  1.5 11.6 %collective-permute-start = (bf16[48,2048]{1,0:T(8,128)(2,1)S(1)}, bf16[48,2048]{1,0:T(8,128)(2,1)S(1)}, u32[]{:S(2)}, u32[]{:S(2)}) collective-permute-start(bf16[48,2048]{1,0:T(8,128)(2,1)S(1)} %constant_dynamic-slice_fusion.mine_ref), channel_id=1, source_target_pairs={{0,8},{1,6},{2,10},{3,4},{4,12},{5,2},{6,14},{7,0},{8,15},{9,1},{1... | collective-permute-start | bytes 589832 | tf_op jit(solution)/shard_map/ppermute | solution.py:241
  5.6 39.5 %collective-permute-start.8 = (bf16[128,6144]{1,0:T(8,128)(2,1)S(1)}, bf16[128,6144]{1,0:T(8,128)(2,1)S(1)}, u32[]{:S(2)}, u32[]{:S(2)}) collective-permute-start(bf16[128,6144]{1,0:T(8,128)(2,1)S(1)} %shard_map.37), channel_id=1, source_target_pairs={{0,16},{1,17},{2,18},{3,19},{4,20},{5,21},{6,22},{7,23},{8,24},{9,... | collective-permute-start | bytes 4718600 | tf_op jit(solution)/shard_map/ppermute | solution.py:241
  13.1 6.6 %collective-permute-start.3 = (bf16[48,2048]{1,0:T(8,128)(2,1)S(1)}, bf16[48,2048]{1,0:T(8,128)(2,1)S(1)}, u32[]{:S(2)}, u32[]{:S(2)}) collective-permute-start(bf16[48,2048]{1,0:T(8,128)(2,1)S(1)} %shard_map.39.refs_1_), channel_id=1, source_target_pairs={{0,4},{1,5},{2,6},{3,7},{4,0},{5,1},{6,2},{7,3},{8,12},{9,13},{10,... | collective-permute-start | bytes 589832 | tf_op jit(solution)/shard_map/ppermute | solution.py:241
  14.8 7.9 %collective-permute-start.2 = (bf16[48,2048]{1,0:T(8,128)(2,1)S(1)}, bf16[48,2048]{1,0:T(8,128)(2,1)S(1)}, u32[]{:S(2)}, u32[]{:S(2)}) collective-permute-start(bf16[48,2048]{1,0:T(8,128)(2,1)S(1)} %shard_map.39.refs_1_), channel_id=1, source_target_pairs={{0,2},{1,3},{2,0},{3,1},{4,6},{5,7},{6,4},{7,5},{8,10},{9,11},{10,... | collective-permute-start | bytes 589832 | tf_op jit(solution)/shard_map/ppermute | solution.py:241
  19.2 6.6 %collective-permute-start.1 = (bf16[48,2048]{1,0:T(8,128)(2,1)S(1)}, bf16[48,2048]{1,0:T(8,128)(2,1)S(1)}, u32[]{:S(2)}, u32[]{:S(2)}) collective-permute-start(bf16[48,2048]{1,0:T(8,128)(2,1)S(1)} %shard_map.39.refs_1_), channel_id=1, source_target_pairs={{0,6},{1,7},{2,4},{3,5},{4,2},{5,3},{6,0},{7,1},{8,14},{9,15},{10,... | collective-permute-start | bytes 589832 | tf_op jit(solution)/shard_map/ppermute | solution.py:241
  28.4 18.8 %copy-start.2 = (bf16[128,8192]{1,0:T(8,128)(2,1)S(1)}, bf16[128,8192]{1,0:T(8,128)(2,1)}, u32[]{:S(2)}) copy-start(bf16[128,8192]{1,0:T(8,128)(2,1)} %refs_1_.1) | copy-start | bytes 6291460
  28.5 1.8 %collective-permute-start.4 = (f32[48,2048]{1,0:T(8,128)S(1)}, f32[48,2048]{1,0:T(8,128)S(1)}, u32[]{:S(2)}, u32[]{:S(2)}) collective-permute-start(f32[48,2048]{1,0:T(8,128)S(1)} %shard_map.43), channel_id=1, source_target_pairs={{0,1},{1,0},{2,3},{3,2},{4,5},{5,4},{6,7},{7,6},{8,9},{9,8},{10,11... | collective-permute-start | bytes 1179656 | tf_op jit(solution)/shard_map/ppermute | solution.py:241
  30.3 8.2 %collective-permute-start.5 = (bf16[48,2048]{1,0:T(8,128)(2,1)S(1)}, bf16[48,2048]{1,0:T(8,128)(2,1)S(1)}, u32[]{:S(2)}, u32[]{:S(2)}) collective-permute-start(bf16[48,2048]{1,0:T(8,128)(2,1)S(1)} %add_convert_fusion.mine_ref), channel_id=1, source_target_pairs={{0,8},{1,6},{2,10},{3,4},{4,12},{5,2},{6,14},{7,0},{8,15},{9,1},{1... | collective-permute-start | bytes 589832 | tf_op jit(solution)/shard_map/ppermute | solution.py:241
  31.9 11.2 %collective-permute-start.7 = (bf16[48,2048]{1,0:T(8,128)(2,1)S(1)}, bf16[48,2048]{1,0:T(8,128)(2,1)S(1)}, u32[]{:S(2)}, u32[]{:S(2)}) collective-permute-start(bf16[48,2048]{1,0:T(8,128)(2,1)S(1)} %add_convert_fusion.mine_ref), channel_id=1, source_target_pairs={{0,14},{2,12},{4,10},{6,8},{9,7},{11,5},{13,3},{15,1},{16,30},{18,... | collective-permute-start | bytes 589832 | tf_op jit(solution)/shard_map/ppermute | solution.py:241
  38.5 6.7 %collective-permute-start.6 = (bf16[48,2048]{1,0:T(8,128)(2,1)S(1)}, bf16[48,2048]{1,0:T(8,128)(2,1)S(1)}, u32[]{:S(2)}, u32[]{:S(2)}) collective-permute-start(bf16[48,2048]{1,0:T(8,128)(2,1)S(1)} %shard_map.44.refs_0_), channel_id=1, source_target_pairs={{0,4},{1,5},{2,6},{3,7},{4,0},{5,1},{6,2},{7,3},{8,12},{9,13},{10,... | collective-permute-start | bytes 589832 | tf_op jit(solution)/shard_map/ppermute | solution.py:241
  39.6 6.5 %collective-permute-start.9 = (bf16[48,2048]{1,0:T(8,128)(2,1)S(1)}, bf16[48,2048]{1,0:T(8,128)(2,1)S(1)}, u32[]{:S(2)}, u32[]{:S(2)}) collective-permute-start(bf16[48,2048]{1,0:T(8,128)(2,1)S(1)} %shard_map.44.refs_0_), channel_id=1, source_target_pairs={{0,2},{1,3},{2,0},{3,1},{4,6},{5,7},{6,4},{7,5},{8,10},{9,11},{10,... | collective-permute-start | bytes 589832 | tf_op jit(solution)/shard_map/ppermute | solution.py:241
  41.2 6.1 %collective-permute-start.10 = (bf16[48,2048]{1,0:T(8,128)(2,1)S(1)}, bf16[48,2048]{1,0:T(8,128)(2,1)S(1)}, u32[]{:S(2)}, u32[]{:S(2)}) collective-permute-start(bf16[48,2048]{1,0:T(8,128)(2,1)S(1)} %shard_map.44.refs_0_), channel_id=1, source_target_pairs={{0,16},{1,17},{2,18},{3,19},{4,20},{5,21},{6,22},{7,23},{8,24},{9,... | collective-permute-start | bytes 589832 | tf_op jit(solution)/shard_map/ppermute | solution.py:241
  45.1 7.0 %copy-start.1 = (bf16[96,2048]{1,0:T(8,128)(2,1)S(1)}, bf16[96,2048]{1,0:T(8,128)(2,1)}, u32[]{:S(2)}) copy-start(bf16[96,2048]{1,0:T(8,128)(2,1)} %param.3) | copy-start | bytes 1179652
  46.4 3.9 %collective-permute-start.11 = (f32[48,128]{1,0:T(8,128)S(1)}, f32[48,128]{1,0:T(8,128)S(1)}, u32[]{:S(2)}, u32[]{:S(2)}) collective-permute-start(f32[48,128]{1,0:T(8,128)S(1)} %shard_map.47), channel_id=1, source_target_pairs={{0,16},{1,17},{2,18},{3,19},{4,20},{5,21},{6,22},{7,23},{8,24},{9,... | collective-permute-start | bytes 73736 | tf_op jit(solution)/shard_map/ppermute | solution.py:241
  50.3 1.3 %collective-permute-start.12 = (f32[48,128]{1,0:T(8,128)S(1)}, f32[48,128]{1,0:T(8,128)S(1)}, u32[]{:S(2)}, u32[]{:S(2)}) collective-permute-start(f32[48,128]{1,0:T(8,128)S(1)} %get-tuple-element.60), channel_id=1, source_target_pairs={{0,1},{1,0},{2,3},{3,2},{4,5},{5,4},{6,7},{7,6},{8,9},{9,8},{10,11... | collective-permute-start | bytes 73736 | tf_op jit(solution)/shard_map/ppermute | solution.py:241

commit v23 on v22

--- a/solution.py
+++ b/solution.py
@@ -263,25 +263,39 @@
                 return sy, sz + 2 if sd == 0 else sz - 2, sx, sd
             return sy, sz ^ 1, 1 - sx, 1 - sd
 
+        def start_direct(sy, sz, sx, sd):
+            su = sz if sd == 0 else nz - 1 - sz
+            if su < near:
+                return sy, nz - 1 - sz, 1 - sx, sd
+            return sy, sz, 1 - sx, 1 - sd
+
         came = move(own, start)
         if direct:
-            corner = along_z(own, {0: 3, 1: 2}, True)
+            came_too = move(own, start_direct)
         first = pick(dims, own, came, after)
         pairs = {0: 1, 1: 0, 2: 3, 3: 2}
         beside = along_z(first, pairs)
-        across = along_z(first, {0: 0, 1: 1, 2: 2, 3: 3}, True)
         if direct:
-            beside, corner = lax.optimization_barrier((beside, corner))
+            across = along_z(first, {2: 2, 3: 3}, True)
+            beside, came_too = lax.optimization_barrier((beside, came_too))
+        else:
+            across = along_z(first, {0: 0, 1: 1, 2: 2, 3: 3}, True)
 
         def last(before, after):
             if direct:
                 ready, _ = lax.optimization_barrier((came, after))
-                return pick(dims, ready, corner)
+                return pick(dims, ready, came_too)
             ready, _ = lax.optimization_barrier((first, before))
             piece, _ = lax.optimization_barrier((along_z(ready, pairs, True), after))
             return piece
 
-        return first, beside, across, last
+        def third(after):
+            if direct:
+                ready, _ = lax.optimization_barrier((came_too, after))
+                return pick(dims, ready, across)
+            return across
+
+        return first, beside, third, last
 
     rows, width = nq // ny, queries.shape[1]
     to_y = cut(stored_grads, ORDER[1:], dims, width)
@@ -291,20 +305,20 @@
     other_grads = swap_y(to_y)
     step = functools.partial(fisher_step, inverse_fisher, dims, width)
     half, quarter = inverse_fisher.shape[0] // 2, inverse_fisher.shape[0] // 4
-    a0, a1, b0, b1 = step(((0, 0, half), (0, half, half), (1, 0, half), (1, half, half)))
-    q0, q1, q2, last = gather(own, False, (a0,))
-    total0, c0, c1 = step(((2, 0, half), (2, half, quarter)), q0, (a0, a1))
-    total, c2, d0 = step(((2, half + quarter, quarter), (3, 0, half)), q1, (b0, b1), total0)
-    total, d1 = step(((3, half, half),), q2, (c0, c1, c2), total)
-    (total,) = step((), last(total0, total), (d0, d1), total)
+    a0, a1, b0, b1 = step(((0, 0, half), (0, half, half), (1, 0, half), (1, half, quarter)))
+    q0, q1, third, last = gather(own, False, (a0,))
+    total0, b2, c0 = step(((1, half + quarter, quarter), (2, 0, half)), q0, (a0, a1))
+    total, c1, d0 = step(((2, half, half), (3, 0, quarter)), q1, (b0, b1, b2), total0)
+    total, d1, d2 = step(((3, quarter, quarter), (3, half, half)), third(total), (c0, c1), total)
+    (total,) = step((), last(total0, total), (d0, d1, d2), total)
     panel = (total + swap_core(total)).astype(jnp.bfloat16)
 
-    p0, p1, p2, last = gather(panel, True)
+    p0, p1, third, last = gather(panel, True)
     swapped = swap_y(p0)
     p1, other_grads = lax.optimization_barrier((p1, other_grads))
     p3 = last(p1, p1)
     other = score_dot([p1, p3], (0, 2), None, other_grads)
-    p2, _ = lax.optimization_barrier((p2, other))
+    p2 = third(other)
     other = score_dot([p2], (1,), None, other_grads, other)
     p2, swapped, _ = lax.optimization_barrier((p2, swapped, other))
     mine = score_dot([p0, p1, p2, p3], ORDER, dims, stored_grads)

time: 52.3 us -> 53.8 us (1.029)
  the two profiles are of different devices: /device:TPU:0 before, /device:TPU:21 now
where the time goes in v23:
time: 53.8 us; the launch traced here: 53.6 us
  Pallas kernels  20.1 us (37%)
  starting transfers between devices  17.9 us (33%)
  waiting for transfers between devices  14.6 us (27%)
  other arithmetic  0.65 us (1%)
    ppermute x13, starting transfers between devices, move(): return lax.ppermute(value, AXES, pairs)  17.9 us
    pallas_call x5, Pallas kernels, fisher_step(): pl.pallas_call(functools.partial(fisher_kernel, dims, len(parts), has_bas...  16.7 us
    ppermute x13, waiting for transfers between devices, move(): return lax.ppermute(value, AXES, pairs)  14.6 us
    pallas_call x4, Pallas kernels, score_dot(): pl.pallas_call(functools.partial(score_kernel, dims, order, base is not N...  1.91 us
    pallas_call x1, Pallas kernels, cut(): pl.pallas_call(functools.partial(cut_kernel, dims, order), out_shape=jax....  1.43 us
  transfers between devices with their start and end apart: 13, of which 5 were waited for; matrix products, arithmetic and copies ran while one was open for 0% of the time, Pallas kernels for 35%

profile of v23, /device:TPU:21, one launch (start us, length us, event | category | flops | bytes accessed | tf_op | source)
XLA Modules:
  0.0 53.6 jit_solution(11819043915611678361)
XLA Ops:
  0.0 1.4 %shard_map.37 = bf16[128,6144]{1,0:T(8,128)(2,1)S(1)} custom-call(bf16[128,8192]{1,0:T(8,128)(2,1)} %refs_1_.1), custom_call_target="tpu_custom_call" | custom-call | bytes 1572864 | tf_op jit(solution)/shard_map/pallas_call | solution.py:172
  1.4 0.0 copy-done
  1.5 0.1 collective-permute-start
  1.6 0.2 collective-permute-start.8
  1.9 5.3 %shard_map.38 = (bf16[1024,2048]{1,0:T(8,128)(2,1)S(1)}, bf16[1024,2048]{1,0:T(8,128)(2,1)S(1)}, bf16[1024,2048]{1,0:T(8,128)(2,1)S(1)}, bf16[512,2048]{1,0:T(8,128)(2,1)S(1)}) custom-call(bf16[2048,8192]{1,0:T(8,128)(2,1)} %refs_0_.7), custom_call_target="tpu_custom_call" | custom-call | bytes 14680064 | tf_op jit(solution)/shard_map/pallas_call | solution.py:107
  7.2 2.1 %collective-permute-done.other_ref = bf16[48,2048]{1,0:T(8,128)(2,1)S(1)} collective-permute-done((bf16[48,2048]{1,0:T(8,128)(2,1)S(1)}, bf16[48,2048]{1,0:T(8,128)(2,1)S(1)}, u32[]{:S(2)}, u32[]{:S(2)}) %collective-permute-start) | collective-permute-done | bytes 196640 | tf_op jit(solution)/shard_map/ppermute | solution.py:241
  9.3 0.4 collective-permute-start.3
  9.7 2.2 %collective-permute-start.2 = (bf16[48,2048]{1,0:T(8,128)(2,1)S(1)}, bf16[48,2048]{1,0:T(8,128)(2,1)S(1)}, u32[]{:S(2)}, u32[]{:S(2)}) collective-permute-start(bf16[48,2048]{1,0:T(8,128)(2,1)S(1)} %shard_map.39.refs_1_), channel_id=1, source_target_pairs={{0,2},{1,3},{2,0},{3,1},{4,6},{5,7},{6,4},{7,5},{8,10},{9,11},{10,... | collective-permute-start | bytes 589832 | tf_op jit(solution)/shard_map/ppermute | solution.py:241
  12.0 2.9 %shard_map.40 = (f32[48,2048]{1,0:T(8,128)S(1)}, bf16[512,2048]{1,0:T(8,128)(2,1)S(1)}, bf16[1024,2048]{1,0:T(8,128)(2,1)S(1)}) custom-call(bf16[2048,8192]{1,0:T(8,128)(2,1)} %refs_0_.7, bf16[48,2048]{1,0:T(8,128)(2,1)S(1)} %shard_map.39.refs_1_, bf16[1024,2048]{1,0:T(8,128)(2,1)S(1)} %get-tuple-element.37.refs_0_.refs_2_, ...), custom_call_target="tpu_custom_call" | custom-call | flops 402653184 | bytes 14680064 | tf_op jit(solution)/shard_map/pallas_call | solution.py:107
  14.9 0.1 collective-permute-start.1
  15.0 2.9 %shard_map.41 = (f32[48,2048]{1,0:T(8,128)S(1)}, bf16[1024,2048]{1,0:T(8,128)(2,1)S(1)}, bf16[512,2048]{1,0:T(8,128)(2,1)S(1)}) custom-call(bf16[2048,8192]{1,0:T(8,128)(2,1)} %refs_0_.7, bf16[48,2048]{1,0:T(8,128)(2,1)S(1)} %collective-permute-done.3.refs_1_, bf16[1024,2048]{1,0:T(8,128)(2,1)S(1)} %get-tuple-element.42.refs_2_, ...), custom_call_target="tpu_custom_call" | custom-call | flops 402653184 | bytes 14680064 | tf_op jit(solution)/shard_map/pallas_call | solution.py:107
  17.9 2.9 %shard_map.42 = (f32[48,2048]{1,0:T(8,128)S(1)}, bf16[512,2048]{1,0:T(8,128)(2,1)S(1)}, bf16[1024,2048]{1,0:T(8,128)(2,1)S(1)}) custom-call(bf16[2048,8192]{1,0:T(8,128)(2,1)} %refs_0_.7, bf16[48,2048]{1,0:T(8,128)(2,1)S(1)} %collective-permute-done.2.refs_1_, bf16[1024,2048]{1,0:T(8,128)(2,1)S(1)} %get-tuple-element.41.refs_2_, ...), custom_call_target="tpu_custom_call" | custom-call | flops 402653184 | bytes 14680064 | tf_op jit(solution)/shard_map/pallas_call | solution.py:107
  20.9 2.6 %shard_map.43 = f32[48,2048]{1,0:T(8,128)S(1)} custom-call(bf16[48,2048]{1,0:T(8,128)(2,1)S(1)} %collective-permute-done.1.refs_0_, bf16[512,2048]{1,0:T(8,128)(2,1)S(1)} %get-tuple-element.49.refs_1_, bf16[512,2048]{1,0:T(8,128)(2,1)S(1)} %get-tuple-element.50.refs_2_, bf16[1024,2048]{1,0:T(8,128)(2,1)S(1)} %get-tuple-element.51.refs_3_, ...), custom_call_target="tpu_custom_call" | custom-call | flops 402653184 | bytes 8388608 | tf_op jit(solution)/shard_map/pallas_call | solution.py:107
  23.5 0.0 copy-start.2
  23.5 2.8 %collective-permute-start.4 = (f32[48,2048]{1,0:T(8,128)S(1)}, f32[48,2048]{1,0:T(8,128)S(1)}, u32[]{:S(2)}, u32[]{:S(2)}) collective-permute-start(f32[48,2048]{1,0:T(8,128)S(1)} %shard_map.43), channel_id=1, source_target_pairs={{0,1},{1,0},{2,3},{3,2},{4,5},{5,4},{6,7},{7,6},{8,9},{9,8},{10,11... | collective-permute-start | bytes 1179656 | tf_op jit(solution)/shard_map/ppermute | solution.py:241
  26.3 1.3 %collective-permute-done.4 = f32[48,2048]{1,0:T(8,128)S(1)} collective-permute-done((f32[48,2048]{1,0:T(8,128)S(1)}, f32[48,2048]{1,0:T(8,128)S(1)}, u32[]{:S(2)}, u32[]{:S(2)}) %collective-permute-start.4) | collective-permute-done | bytes 393248 | tf_op jit(solution)/shard_map/ppermute | solution.py:241
  27.7 0.1 collective-permute-start.5
  27.8 1.3 %collective-permute-start.7 = (bf16[48,2048]{1,0:T(8,128)(2,1)S(1)}, bf16[48,2048]{1,0:T(8,128)(2,1)S(1)}, u32[]{:S(2)}, u32[]{:S(2)}) collective-permute-start(bf16[48,2048]{1,0:T(8,128)(2,1)S(1)} %add_convert_fusion.mine_ref), channel_id=1, source_target_pairs={{0,14},{1,2},{2,12},{3,0},{4,10},{5,6},{6,8},{7,4},{8,11},{9,7},{1... | collective-permute-start | bytes 589832 | tf_op jit(solution)/shard_map/ppermute | solution.py:241
  29.1 6.8 %collective-permute-done.5.other_ref.mine_ref = bf16[48,2048]{1,0:T(8,128)(2,1)S(1)} collective-permute-done((bf16[48,2048]{1,0:T(8,128)(2,1)S(1)}, bf16[48,2048]{1,0:T(8,128)(2,1)S(1)}, u32[]{:S(2)}, u32[]{:S(2)}) %collective-permute-start.5) | collective-permute-done | bytes 196640 | tf_op jit(solution)/shard_map/ppermute | solution.py:241
  35.9 0.1 collective-permute-start.6
  36.0 0.7 %collective-permute-start.9 = (bf16[48,2048]{1,0:T(8,128)(2,1)S(1)}, bf16[48,2048]{1,0:T(8,128)(2,1)S(1)}, u32[]{:S(2)}, u32[]{:S(2)}) collective-permute-start(bf16[48,2048]{1,0:T(8,128)(2,1)S(1)} %shard_map.44.refs_0_), channel_id=1, source_target_pairs={{1,3},{3,1},{5,7},{7,5},{8,10},{10,8},{12,14},{14,12},{17,19},{19,... | collective-permute-start | bytes 589832 | tf_op jit(solution)/shard_map/ppermute | solution.py:241
  36.6 0.6 %collective-permute-start.10 = (bf16[48,2048]{1,0:T(8,128)(2,1)S(1)}, bf16[48,2048]{1,0:T(8,128)(2,1)S(1)}, u32[]{:S(2)}, u32[]{:S(2)}) collective-permute-start(bf16[48,2048]{1,0:T(8,128)(2,1)S(1)} %shard_map.44.refs_0_), channel_id=1, source_target_pairs={{0,16},{1,17},{2,18},{3,19},{4,20},{5,21},{6,22},{7,23},{8,24},{9,... | collective-permute-start | bytes 589832 | tf_op jit(solution)/shard_map/ppermute | solution.py:241
  37.2 3.5 %collective-permute-done.6.refs_0_.refs_1_ = bf16[48,2048]{1,0:T(8,128)(2,1)S(1)} collective-permute-done((bf16[48,2048]{1,0:T(8,128)(2,1)S(1)}, bf16[48,2048]{1,0:T(8,128)(2,1)S(1)}, u32[]{:S(2)}, u32[]{:S(2)}) %collective-permute-start.6) | collective-permute-done | bytes 196640 | tf_op jit(solution)/shard_map/ppermute | solution.py:241
  40.8 0.5 shard_map.46.refs_2_
  41.3 0.3 shard_map.48
  41.6 1.6 %collective-permute-start.11 = (f32[48,128]{1,0:T(8,128)S(1)}, f32[48,128]{1,0:T(8,128)S(1)}, u32[]{:S(2)}, u32[]{:S(2)}) collective-permute-start(f32[48,128]{1,0:T(8,128)S(1)} %shard_map.48), channel_id=1, source_target_pairs={{0,16},{1,17},{2,18},{3,19},{4,20},{5,21},{6,22},{7,23},{8,24},{9,... | collective-permute-start | bytes 73736 | tf_op jit(solution)/shard_map/ppermute | solution.py:241
  43.2 0.3 shard_map.50.theirs_ref
  43.5 0.9 %shard_map.49.mine_ref = f32[48,128]{1,0:T(8,128)S(1)} custom-call(bf16[48,2048]{1,0:T(8,128)(2,1)S(1)} %shard_map.44.refs_0_, bf16[48,2048]{1,0:T(8,128)(2,1)S(1)} %collective-permute-done.6.refs_0_.refs_1_, bf16[48,2048]{1,0:T(8,128)(2,1)S(1)} %shard_map.47.refs_0_.refs_2_, bf16[48,2048]{1,0:T(8,128)(2,1)S(1)} %shard_map.45.refs_1_.refs_3_, ...), custom_call_target="tpu_custom_call" | custom-call | flops 100663296 | bytes 2097152 | tf_op jit(solution)/shard_map/pallas_call | solution.py:140
  44.3 0.0 collective-permute-done.11.other_ref
  44.4 7.8 %collective-permute-start.12 = (f32[48,128]{1,0:T(8,128)S(1)}, f32[48,128]{1,0:T(8,128)S(1)}, u32[]{:S(2)}, u32[]{:S(2)}) collective-permute-start(f32[48,128]{1,0:T(8,128)S(1)} %get-tuple-element.62), channel_id=1, source_target_pairs={{0,1},{1,0},{2,3},{3,2},{4,5},{5,4},{6,7},{7,6},{8,9},{9,8},{10,11... | collective-permute-start | bytes 73736 | tf_op jit(solution)/shard_map/ppermute | solution.py:241
  52.2 0.8 %collective-permute-done.12 = f32[48,128]{1,0:T(8,128)S(1)} collective-permute-done((f32[48,128]{1,0:T(8,128)S(1)}, f32[48,128]{1,0:T(8,128)S(1)}, u32[]{:S(2)}, u32[]{:S(2)}) %collective-permute-start.12) | collective-permute-done | bytes 24608 | tf_op jit(solution)/shard_map/ppermute | solution.py:241
  53.0 0.6 %add.11 = f32[48,128]{1,0:T(8,128)} add(f32[48,128]{1,0:T(8,128)S(1)} %get-tuple-element.61, f32[48,128]{1,0:T(8,128)S(1)} %collective-permute-done.12) | non-fusion elementwise | flops 6144 | bytes 73728 | tf_op jit(solution)/shard_map/add | solution.py:328
  (18 shorter events, 0.2 us)
Async XLA Ops:
  0.0 1.5 %copy-start = (bf16[96,2048]{1,0:T(8,128)(2,1)S(1)}, bf16[96,2048]{1,0:T(8,128)(2,1)}, u32[]{:S(2)}) copy-start(bf16[96,2048]{1,0:T(8,128)(2,1)} %param.3) | copy-start | bytes 1179652
  1.5 7.8 %collective-permute-start = (bf16[48,2048]{1,0:T(8,128)(2,1)S(1)}, bf16[48,2048]{1,0:T(8,128)(2,1)S(1)}, u32[]{:S(2)}, u32[]{:S(2)}) collective-permute-start(bf16[48,2048]{1,0:T(8,128)(2,1)S(1)} %constant_dynamic-slice_fusion.mine_ref), channel_id=1, source_target_pairs={{0,8},{1,6},{2,10},{3,4},{4,12},{5,2},{6,14},{7,0},{8,15},{9,1},{1... | collective-permute-start | bytes 589832 | tf_op jit(solution)/shard_map/ppermute | solution.py:241
  1.6 39.2 %collective-permute-start.8 = (bf16[128,6144]{1,0:T(8,128)(2,1)S(1)}, bf16[128,6144]{1,0:T(8,128)(2,1)S(1)}, u32[]{:S(2)}, u32[]{:S(2)}) collective-permute-start(bf16[128,6144]{1,0:T(8,128)(2,1)S(1)} %shard_map.37), channel_id=1, source_target_pairs={{0,16},{1,17},{2,18},{3,19},{4,20},{5,21},{6,22},{7,23},{8,24},{9,... | collective-permute-start | bytes 4718600 | tf_op jit(solution)/shard_map/ppermute | solution.py:241
  9.3 5.7 %collective-permute-start.3 = (bf16[48,2048]{1,0:T(8,128)(2,1)S(1)}, bf16[48,2048]{1,0:T(8,128)(2,1)S(1)}, u32[]{:S(2)}, u32[]{:S(2)}) collective-permute-start(bf16[48,2048]{1,0:T(8,128)(2,1)S(1)} %shard_map.39.refs_1_), channel_id=1, source_target_pairs={{0,4},{1,5},{2,6},{3,7},{4,0},{5,1},{6,2},{7,3},{8,12},{9,13},{10,... | collective-permute-start | bytes 589832 | tf_op jit(solution)/shard_map/ppermute | solution.py:241
  9.7 8.2 %collective-permute-start.2 = (bf16[48,2048]{1,0:T(8,128)(2,1)S(1)}, bf16[48,2048]{1,0:T(8,128)(2,1)S(1)}, u32[]{:S(2)}, u32[]{:S(2)}) collective-permute-start(bf16[48,2048]{1,0:T(8,128)(2,1)S(1)} %shard_map.39.refs_1_), channel_id=1, source_target_pairs={{0,2},{1,3},{2,0},{3,1},{4,6},{5,7},{6,4},{7,5},{8,10},{9,11},{10,... | collective-permute-start | bytes 589832 | tf_op jit(solution)/shard_map/ppermute | solution.py:241
  14.9 6.0 %collective-permute-start.1 = (bf16[48,2048]{1,0:T(8,128)(2,1)S(1)}, bf16[48,2048]{1,0:T(8,128)(2,1)S(1)}, u32[]{:S(2)}, u32[]{:S(2)}) collective-permute-start(bf16[48,2048]{1,0:T(8,128)(2,1)S(1)} %shard_map.39.refs_1_), channel_id=1, source_target_pairs={{0,6},{1,7},{2,4},{3,5},{4,2},{5,3},{6,0},{7,1},{8,14},{9,15},{10,... | collective-permute-start | bytes 589832 | tf_op jit(solution)/shard_map/ppermute | solution.py:241
  23.5 19.7 %copy-start.2 = (bf16[128,8192]{1,0:T(8,128)(2,1)S(1)}, bf16[128,8192]{1,0:T(8,128)(2,1)}, u32[]{:S(2)}) copy-start(bf16[128,8192]{1,0:T(8,128)(2,1)} %refs_1_.1) | copy-start | bytes 6291460
  23.5 4.1 %collective-permute-start.4 = (f32[48,2048]{1,0:T(8,128)S(1)}, f32[48,2048]{1,0:T(8,128)S(1)}, u32[]{:S(2)}, u32[]{:S(2)}) collective-permute-start(f32[48,2048]{1,0:T(8,128)S(1)} %shard_map.43), channel_id=1, source_target_pairs={{0,1},{1,0},{2,3},{3,2},{4,5},{5,4},{6,7},{7,6},{8,9},{9,8},{10,11... | collective-permute-start | bytes 1179656 | tf_op jit(solution)/shard_map/ppermute | solution.py:241
  27.7 8.2 %collective-permute-start.5 = (bf16[48,2048]{1,0:T(8,128)(2,1)S(1)}, bf16[48,2048]{1,0:T(8,128)(2,1)S(1)}, u32[]{:S(2)}, u32[]{:S(2)}) collective-permute-start(bf16[48,2048]{1,0:T(8,128)(2,1)S(1)} %add_convert_fusion.mine_ref), channel_id=1, source_target_pairs={{0,8},{1,6},{2,10},{3,4},{4,12},{5,2},{6,14},{7,0},{8,15},{9,1},{1... | collective-permute-start | bytes 589832 | tf_op jit(solution)/shard_map/ppermute | solution.py:241
  27.8 9.5 %collective-permute-start.7 = (bf16[48,2048]{1,0:T(8,128)(2,1)S(1)}, bf16[48,2048]{1,0:T(8,128)(2,1)S(1)}, u32[]{:S(2)}, u32[]{:S(2)}) collective-permute-start(bf16[48,2048]{1,0:T(8,128)(2,1)S(1)} %add_convert_fusion.mine_ref), channel_id=1, source_target_pairs={{0,14},{1,2},{2,12},{3,0},{4,10},{5,6},{6,8},{7,4},{8,11},{9,7},{1... | collective-permute-start | bytes 589832 | tf_op jit(solution)/shard_map/ppermute | solution.py:241
  35.9 4.9 %collective-permute-start.6 = (bf16[48,2048]{1,0:T(8,128)(2,1)S(1)}, bf16[48,2048]{1,0:T(8,128)(2,1)S(1)}, u32[]{:S(2)}, u32[]{:S(2)}) collective-permute-start(bf16[48,2048]{1,0:T(8,128)(2,1)S(1)} %shard_map.44.refs_0_), channel_id=1, source_target_pairs={{0,4},{1,5},{2,6},{3,7},{4,0},{5,1},{6,2},{7,3},{8,12},{9,13},{10,... | collective-permute-start | bytes 589832 | tf_op jit(solution)/shard_map/ppermute | solution.py:241
  36.0 5.3 %collective-permute-start.9 = (bf16[48,2048]{1,0:T(8,128)(2,1)S(1)}, bf16[48,2048]{1,0:T(8,128)(2,1)S(1)}, u32[]{:S(2)}, u32[]{:S(2)}) collective-permute-start(bf16[48,2048]{1,0:T(8,128)(2,1)S(1)} %shard_map.44.refs_0_), channel_id=1, source_target_pairs={{1,3},{3,1},{5,7},{7,5},{8,10},{10,8},{12,14},{14,12},{17,19},{19,... | collective-permute-start | bytes 589832 | tf_op jit(solution)/shard_map/ppermute | solution.py:241
  36.6 6.5 %collective-permute-start.10 = (bf16[48,2048]{1,0:T(8,128)(2,1)S(1)}, bf16[48,2048]{1,0:T(8,128)(2,1)S(1)}, u32[]{:S(2)}, u32[]{:S(2)}) collective-permute-start(bf16[48,2048]{1,0:T(8,128)(2,1)S(1)} %shard_map.44.refs_0_), channel_id=1, source_target_pairs={{0,16},{1,17},{2,18},{3,19},{4,20},{5,21},{6,22},{7,23},{8,24},{9,... | collective-permute-start | bytes 589832 | tf_op jit(solution)/shard_map/ppermute | solution.py:241
  40.8 12.8 %copy-start.1 = (bf16[96,2048]{1,0:T(8,128)(2,1)S(1)}, bf16[96,2048]{1,0:T(8,128)(2,1)}, u32[]{:S(2)}) copy-start(bf16[96,2048]{1,0:T(8,128)(2,1)} %param.3) | copy-start | bytes 1179652
  41.6 2.8 %collective-permute-start.11 = (f32[48,128]{1,0:T(8,128)S(1)}, f32[48,128]{1,0:T(8,128)S(1)}, u32[]{:S(2)}, u32[]{:S(2)}) collective-permute-start(f32[48,128]{1,0:T(8,128)S(1)} %shard_map.48), channel_id=1, source_target_pairs={{0,16},{1,17},{2,18},{3,19},{4,20},{5,21},{6,22},{7,23},{8,24},{9,... | collective-permute-start | bytes 73736 | tf_op jit(solution)/shard_map/ppermute | solution.py:241
  44.4 8.6 %collective-permute-start.12 = (f32[48,128]{1,0:T(8,128)S(1)}, f32[48,128]{1,0:T(8,128)S(1)}, u32[]{:S(2)}, u32[]{:S(2)}) collective-permute-start(f32[48,128]{1,0:T(8,128)S(1)} %get-tuple-element.62), channel_id=1, source_target_pairs={{0,1},{1,0},{2,3},{3,2},{4,5},{5,4},{6,7},{7,6},{8,9},{9,8},{10,11... | collective-permute-start | bytes 73736 | tf_op jit(solution)/shard_map/ppermute | solution.py:241

commit v24 on v23

--- a/solution.py
+++ b/solution.py
@@ -269,6 +269,10 @@
                 return sy, nz - 1 - sz, 1 - sx, sd
             return sy, sz, 1 - sx, 1 - sd
 
+        def far_x(sy, sz, sx, sd):
+            su = sz if sd == 0 else nz - 1 - sz
+            return (1 - sy, sz, sx, sd) if su < near else (sy, sz, 1 - sx, sd)
+
         came = move(own, start)
         if direct:
             came_too = move(own, start_direct)
@@ -276,7 +280,7 @@
         pairs = {0: 1, 1: 0, 2: 3, 3: 2}
         beside = along_z(first, pairs)
         if direct:
-            across = along_z(first, {2: 2, 3: 3}, True)
+            across = move(first, far_x)
             beside, came_too = lax.optimization_barrier((beside, came_too))
         else:
             across = along_z(first, {0: 0, 1: 1, 2: 2, 3: 3}, True)

time: 53.8 us -> 53 us (0.985)
  the two profiles are of different devices: /device:TPU:21 before, /device:TPU:0 now
where the time goes in v24:
time: 53 us; the launch traced here: 52.8 us
  Pallas kernels  20.1 us (38%)
  starting transfers between devices  18.1 us (34%)
  waiting for transfers between devices  13.7 us (26%)
  other arithmetic  0.65 us (1%)
    ppermute x13, starting transfers between devices, move(): return lax.ppermute(value, AXES, pairs)  18.1 us
    pallas_call x5, Pallas kernels, fisher_step(): pl.pallas_call(functools.partial(fisher_kernel, dims, len(parts), has_bas...  16.7 us
    ppermute x13, waiting for transfers between devices, move(): return lax.ppermute(value, AXES, pairs)  13.7 us
    pallas_call x4, Pallas kernels, score_dot(): pl.pallas_call(functools.partial(score_kernel, dims, order, base is not N...  1.89 us
    pallas_call x1, Pallas kernels, cut(): pl.pallas_call(functools.partial(cut_kernel, dims, order), out_shape=jax....  1.43 us
  transfers between devices with their start and end apart: 13, of which 9 were waited for; matrix products, arithmetic and copies ran while one was open for 0% of the time, Pallas kernels for 35%

profile of v24, /device:TPU:0, one launch (start us, length us, event | category | flops | bytes accessed | tf_op | source)
XLA Modules:
  0.0 52.8 jit_solution(4247419451544579449)
XLA Ops:
  0.0 1.4 %shard_map.37 = bf16[128,6144]{1,0:T(8,128)(2,1)S(1)} custom-call(bf16[128,8192]{1,0:T(8,128)(2,1)} %refs_1_.1), custom_call_target="tpu_custom_call" | custom-call | bytes 1572864 | tf_op jit(solution)/shard_map/pallas_call | solution.py:172
  1.5 4.1 %collective-permute-start = (bf16[48,2048]{1,0:T(8,128)(2,1)S(1)}, bf16[48,2048]{1,0:T(8,128)(2,1)S(1)}, u32[]{:S(2)}, u32[]{:S(2)}) collective-permute-start(bf16[48,2048]{1,0:T(8,128)(2,1)S(1)} %constant_dynamic-slice_fusion.mine_ref), channel_id=1, source_target_pairs={{0,8},{1,6},{2,10},{3,4},{4,12},{5,2},{6,14},{7,0},{8,15},{9,1},{1... | collective-permute-start | bytes 589832 | tf_op jit(solution)/shard_map/ppermute | solution.py:241
  5.6 1.5 %collective-permute-start.8 = (bf16[128,6144]{1,0:T(8,128)(2,1)S(1)}, bf16[128,6144]{1,0:T(8,128)(2,1)S(1)}, u32[]{:S(2)}, u32[]{:S(2)}) collective-permute-start(bf16[128,6144]{1,0:T(8,128)(2,1)S(1)} %shard_map.37), channel_id=1, source_target_pairs={{0,16},{1,17},{2,18},{3,19},{4,20},{5,21},{6,22},{7,23},{8,24},{9,... | collective-permute-start | bytes 4718600 | tf_op jit(solution)/shard_map/ppermute | solution.py:241
  7.1 5.3 %shard_map.38 = (bf16[1024,2048]{1,0:T(8,128)(2,1)S(1)}, bf16[1024,2048]{1,0:T(8,128)(2,1)S(1)}, bf16[1024,2048]{1,0:T(8,128)(2,1)S(1)}, bf16[512,2048]{1,0:T(8,128)(2,1)S(1)}) custom-call(bf16[2048,8192]{1,0:T(8,128)(2,1)} %refs_0_.7), custom_call_target="tpu_custom_call" | custom-call | bytes 14680064 | tf_op jit(solution)/shard_map/pallas_call | solution.py:107
  12.5 1.6 %collective-permute-start.3 = (bf16[48,2048]{1,0:T(8,128)(2,1)S(1)}, bf16[48,2048]{1,0:T(8,128)(2,1)S(1)}, u32[]{:S(2)}, u32[]{:S(2)}) collective-permute-start(bf16[48,2048]{1,0:T(8,128)(2,1)S(1)} %shard_map.39.refs_1_), channel_id=1, source_target_pairs={{0,4},{1,5},{2,6},{3,7},{4,0},{5,1},{6,2},{7,3},{8,12},{9,13},{10,... | collective-permute-start | bytes 589832 | tf_op jit(solution)/shard_map/ppermute | solution.py:241
  14.2 1.5 %collective-permute-start.2 = (bf16[48,2048]{1,0:T(8,128)(2,1)S(1)}, bf16[48,2048]{1,0:T(8,128)(2,1)S(1)}, u32[]{:S(2)}, u32[]{:S(2)}) collective-permute-start(bf16[48,2048]{1,0:T(8,128)(2,1)S(1)} %shard_map.39.refs_1_), channel_id=1, source_target_pairs={{0,2},{1,3},{2,0},{3,1},{4,6},{5,7},{6,4},{7,5},{8,10},{9,11},{10,... | collective-permute-start | bytes 589832 | tf_op jit(solution)/shard_map/ppermute | solution.py:241
  15.7 2.9 %shard_map.40 = (f32[48,2048]{1,0:T(8,128)S(1)}, bf16[512,2048]{1,0:T(8,128)(2,1)S(1)}, bf16[1024,2048]{1,0:T(8,128)(2,1)S(1)}) custom-call(bf16[2048,8192]{1,0:T(8,128)(2,1)} %refs_0_.7, bf16[48,2048]{1,0:T(8,128)(2,1)S(1)} %shard_map.39.refs_1_, bf16[1024,2048]{1,0:T(8,128)(2,1)S(1)} %get-tuple-element.37.refs_0_.refs_2_, ...), custom_call_target="tpu_custom_call" | custom-call | flops 402653184 | bytes 14680064 | tf_op jit(solution)/shard_map/pallas_call | solution.py:107
  18.6 0.5 collective-permute-start.1
  19.0 0.1 collective-permute-done.3.refs_1_
  19.1 2.9 %shard_map.41 = (f32[48,2048]{1,0:T(8,128)S(1)}, bf16[1024,2048]{1,0:T(8,128)(2,1)S(1)}, bf16[512,2048]{1,0:T(8,128)(2,1)S(1)}) custom-call(bf16[2048,8192]{1,0:T(8,128)(2,1)} %refs_0_.7, bf16[48,2048]{1,0:T(8,128)(2,1)S(1)} %collective-permute-done.3.refs_1_, bf16[1024,2048]{1,0:T(8,128)(2,1)S(1)} %get-tuple-element.42.refs_2_, ...), custom_call_target="tpu_custom_call" | custom-call | flops 402653184 | bytes 14680064 | tf_op jit(solution)/shard_map/pallas_call | solution.py:107
  22.1 2.9 %shard_map.42 = (f32[48,2048]{1,0:T(8,128)S(1)}, bf16[512,2048]{1,0:T(8,128)(2,1)S(1)}, bf16[1024,2048]{1,0:T(8,128)(2,1)S(1)}) custom-call(bf16[2048,8192]{1,0:T(8,128)(2,1)} %refs_0_.7, bf16[48,2048]{1,0:T(8,128)(2,1)S(1)} %collective-permute-done.2.refs_1_, bf16[1024,2048]{1,0:T(8,128)(2,1)S(1)} %get-tuple-element.41.refs_2_, ...), custom_call_target="tpu_custom_call" | custom-call | flops 402653184 | bytes 14680064 | tf_op jit(solution)/shard_map/pallas_call | solution.py:107
  25.0 0.2 collective-permute-done.1.refs_0_
  25.2 2.6 %shard_map.43 = f32[48,2048]{1,0:T(8,128)S(1)} custom-call(bf16[48,2048]{1,0:T(8,128)(2,1)S(1)} %collective-permute-done.1.refs_0_, bf16[512,2048]{1,0:T(8,128)(2,1)S(1)} %get-tuple-element.49.refs_1_, bf16[512,2048]{1,0:T(8,128)(2,1)S(1)} %get-tuple-element.50.refs_2_, bf16[1024,2048]{1,0:T(8,128)(2,1)S(1)} %get-tuple-element.51.refs_3_, ...), custom_call_target="tpu_custom_call" | custom-call | flops 402653184 | bytes 8388608 | tf_op jit(solution)/shard_map/pallas_call | solution.py:107
  27.9 0.1 collective-permute-start.4
  27.9 1.7 %collective-permute-done.4 = f32[48,2048]{1,0:T(8,128)S(1)} collective-permute-done((f32[48,2048]{1,0:T(8,128)S(1)}, f32[48,2048]{1,0:T(8,128)S(1)}, u32[]{:S(2)}, u32[]{:S(2)}) %collective-permute-start.4) | collective-permute-done | bytes 393248 | tf_op jit(solution)/shard_map/ppermute | solution.py:241
  29.7 1.8 %collective-permute-start.5 = (bf16[48,2048]{1,0:T(8,128)(2,1)S(1)}, bf16[48,2048]{1,0:T(8,128)(2,1)S(1)}, u32[]{:S(2)}, u32[]{:S(2)}) collective-permute-start(bf16[48,2048]{1,0:T(8,128)(2,1)S(1)} %add_convert_fusion.mine_ref), channel_id=1, source_target_pairs={{0,8},{1,6},{2,10},{3,4},{4,12},{5,2},{6,14},{7,0},{8,15},{9,1},{1... | collective-permute-start | bytes 589832 | tf_op jit(solution)/shard_map/ppermute | solution.py:241
  31.5 2.1 %collective-permute-start.7 = (bf16[48,2048]{1,0:T(8,128)(2,1)S(1)}, bf16[48,2048]{1,0:T(8,128)(2,1)S(1)}, u32[]{:S(2)}, u32[]{:S(2)}) collective-permute-start(bf16[48,2048]{1,0:T(8,128)(2,1)S(1)} %add_convert_fusion.mine_ref), channel_id=1, source_target_pairs={{0,14},{1,2},{2,12},{3,0},{4,10},{5,6},{6,8},{7,4},{8,11},{9,7},{1... | collective-permute-start | bytes 589832 | tf_op jit(solution)/shard_map/ppermute | solution.py:241
  33.6 4.3 %collective-permute-done.5.other_ref.mine_ref = bf16[48,2048]{1,0:T(8,128)(2,1)S(1)} collective-permute-done((bf16[48,2048]{1,0:T(8,128)(2,1)S(1)}, bf16[48,2048]{1,0:T(8,128)(2,1)S(1)}, u32[]{:S(2)}, u32[]{:S(2)}) %collective-permute-start.5) | collective-permute-done | bytes 196640 | tf_op jit(solution)/shard_map/ppermute | solution.py:241
  37.9 0.7 %collective-permute-start.6 = (bf16[48,2048]{1,0:T(8,128)(2,1)S(1)}, bf16[48,2048]{1,0:T(8,128)(2,1)S(1)}, u32[]{:S(2)}, u32[]{:S(2)}) collective-permute-start(bf16[48,2048]{1,0:T(8,128)(2,1)S(1)} %shard_map.44.refs_0_), channel_id=1, source_target_pairs={{0,4},{1,5},{2,6},{3,7},{4,0},{5,1},{6,2},{7,3},{8,12},{9,13},{10,... | collective-permute-start | bytes 589832 | tf_op jit(solution)/shard_map/ppermute | solution.py:241
  38.7 3.1 %collective-permute-start.9 = (bf16[48,2048]{1,0:T(8,128)(2,1)S(1)}, bf16[48,2048]{1,0:T(8,128)(2,1)S(1)}, u32[]{:S(2)}, u32[]{:S(2)}) collective-permute-start(bf16[48,2048]{1,0:T(8,128)(2,1)S(1)} %shard_map.44.refs_0_), channel_id=1, source_target_pairs={{0,16},{1,3},{2,18},{3,1},{4,20},{5,7},{6,22},{7,5},{8,10},{9,25},... | collective-permute-start | bytes 589832 | tf_op jit(solution)/shard_map/ppermute | solution.py:241
  41.8 2.9 %collective-permute-done.6.refs_0_.refs_1_ = bf16[48,2048]{1,0:T(8,128)(2,1)S(1)} collective-permute-done((bf16[48,2048]{1,0:T(8,128)(2,1)S(1)}, bf16[48,2048]{1,0:T(8,128)(2,1)S(1)}, u32[]{:S(2)}, u32[]{:S(2)}) %collective-permute-start.6) | collective-permute-done | bytes 196640 | tf_op jit(solution)/shard_map/ppermute | solution.py:241
  44.7 0.5 shard_map.46.refs_2_
  45.2 1.6 %collective-permute-done.9.other_ref = bf16[48,2048]{1,0:T(8,128)(2,1)S(1)} collective-permute-done((bf16[48,2048]{1,0:T(8,128)(2,1)S(1)}, bf16[48,2048]{1,0:T(8,128)(2,1)S(1)}, u32[]{:S(2)}, u32[]{:S(2)}) %collective-permute-start.9) | collective-permute-done | bytes 196640 | tf_op jit(solution)/shard_map/ppermute | solution.py:241
  46.8 0.3 shard_map.48
  47.0 1.0 %collective-permute-start.11 = (f32[48,128]{1,0:T(8,128)S(1)}, f32[48,128]{1,0:T(8,128)S(1)}, u32[]{:S(2)}, u32[]{:S(2)}) collective-permute-start(f32[48,128]{1,0:T(8,128)S(1)} %shard_map.48), channel_id=1, source_target_pairs={{0,16},{1,17},{2,18},{3,19},{4,20},{5,21},{6,22},{7,23},{8,24},{9,... | collective-permute-start | bytes 73736 | tf_op jit(solution)/shard_map/ppermute | solution.py:241
  48.0 1.1 %collective-permute-done.10.refs_0_ = bf16[48,2048]{1,0:T(8,128)(2,1)S(1)} collective-permute-done((bf16[48,2048]{1,0:T(8,128)(2,1)S(1)}, bf16[48,2048]{1,0:T(8,128)(2,1)S(1)}, u32[]{:S(2)}, u32[]{:S(2)}) %collective-permute-start.10) | collective-permute-done | bytes 196640 | tf_op jit(solution)/shard_map/ppermute | solution.py:241
  49.1 0.3 shard_map.50.theirs_ref
  49.4 0.9 %shard_map.49.mine_ref = f32[48,128]{1,0:T(8,128)S(1)} custom-call(bf16[48,2048]{1,0:T(8,128)(2,1)S(1)} %shard_map.44.refs_0_, bf16[48,2048]{1,0:T(8,128)(2,1)S(1)} %collective-permute-done.6.refs_0_.refs_1_, bf16[48,2048]{1,0:T(8,128)(2,1)S(1)} %shard_map.47.refs_0_.refs_2_, bf16[48,2048]{1,0:T(8,128)(2,1)S(1)} %shard_map.45.refs_1_.refs_3_, ...), custom_call_target="tpu_custom_call" | custom-call | flops 100663296 | bytes 2097152 | tf_op jit(solution)/shard_map/pallas_call | solution.py:140
  50.3 0.7 %collective-permute-done.11.other_ref = f32[48,128]{1,0:T(8,128)S(1)} collective-permute-done((f32[48,128]{1,0:T(8,128)S(1)}, f32[48,128]{1,0:T(8,128)S(1)}, u32[]{:S(2)}, u32[]{:S(2)}) %collective-permute-start.11) | collective-permute-done | bytes 24608 | tf_op jit(solution)/shard_map/ppermute | solution.py:241
  50.9 0.1 collective-permute-start.12
  51.0 1.2 %collective-permute-done.12 = f32[48,128]{1,0:T(8,128)S(1)} collective-permute-done((f32[48,128]{1,0:T(8,128)S(1)}, f32[48,128]{1,0:T(8,128)S(1)}, u32[]{:S(2)}, u32[]{:S(2)}) %collective-permute-start.12) | collective-permute-done | bytes 24608 | tf_op jit(solution)/shard_map/ppermute | solution.py:241
  52.2 0.6 %add.11 = f32[48,128]{1,0:T(8,128)} add(f32[48,128]{1,0:T(8,128)S(1)} %get-tuple-element.61, f32[48,128]{1,0:T(8,128)S(1)} %collective-permute-done.12) | non-fusion elementwise | flops 6144 | bytes 73728 | tf_op jit(solution)/shard_map/add | solution.py:332
  (18 shorter events, 0.2 us)
Async XLA Ops:
  0.0 1.5 %copy-start = (bf16[96,2048]{1,0:T(8,128)(2,1)S(1)}, bf16[96,2048]{1,0:T(8,128)(2,1)}, u32[]{:S(2)}) copy-start(bf16[96,2048]{1,0:T(8,128)(2,1)} %param.3) | copy-start | bytes 1179652
  1.5 11.0 %collective-permute-start = (bf16[48,2048]{1,0:T(8,128)(2,1)S(1)}, bf16[48,2048]{1,0:T(8,128)(2,1)S(1)}, u32[]{:S(2)}, u32[]{:S(2)}) collective-permute-start(bf16[48,2048]{1,0:T(8,128)(2,1)S(1)} %constant_dynamic-slice_fusion.mine_ref), channel_id=1, source_target_pairs={{0,8},{1,6},{2,10},{3,4},{4,12},{5,2},{6,14},{7,0},{8,15},{9,1},{1... | collective-permute-start | bytes 589832 | tf_op jit(solution)/shard_map/ppermute | solution.py:241
  5.6 39.1 %collective-permute-start.8 = (bf16[128,6144]{1,0:T(8,128)(2,1)S(1)}, bf16[128,6144]{1,0:T(8,128)(2,1)S(1)}, u32[]{:S(2)}, u32[]{:S(2)}) collective-permute-start(bf16[128,6144]{1,0:T(8,128)(2,1)S(1)} %shard_map.37), channel_id=1, source_target_pairs={{0,16},{1,17},{2,18},{3,19},{4,20},{5,21},{6,22},{7,23},{8,24},{9,... | collective-permute-start | bytes 4718600 | tf_op jit(solution)/shard_map/ppermute | solution.py:241
  12.5 6.6 %collective-permute-start.3 = (bf16[48,2048]{1,0:T(8,128)(2,1)S(1)}, bf16[48,2048]{1,0:T(8,128)(2,1)S(1)}, u32[]{:S(2)}, u32[]{:S(2)}) collective-permute-start(bf16[48,2048]{1,0:T(8,128)(2,1)S(1)} %shard_map.39.refs_1_), channel_id=1, source_target_pairs={{0,4},{1,5},{2,6},{3,7},{4,0},{5,1},{6,2},{7,3},{8,12},{9,13},{10,... | collective-permute-start | bytes 589832 | tf_op jit(solution)/shard_map/ppermute | solution.py:241
  14.2 7.9 %collective-permute-start.2 = (bf16[48,2048]{1,0:T(8,128)(2,1)S(1)}, bf16[48,2048]{1,0:T(8,128)(2,1)S(1)}, u32[]{:S(2)}, u32[]{:S(2)}) collective-permute-start(bf16[48,2048]{1,0:T(8,128)(2,1)S(1)} %shard_map.39.refs_1_), channel_id=1, source_target_pairs={{0,2},{1,3},{2,0},{3,1},{4,6},{5,7},{6,4},{7,5},{8,10},{9,11},{10,... | collective-permute-start | bytes 589832 | tf_op jit(solution)/shard_map/ppermute | solution.py:241
  18.6 6.6 %collective-permute-start.1 = (bf16[48,2048]{1,0:T(8,128)(2,1)S(1)}, bf16[48,2048]{1,0:T(8,128)(2,1)S(1)}, u32[]{:S(2)}, u32[]{:S(2)}) collective-permute-start(bf16[48,2048]{1,0:T(8,128)(2,1)S(1)} %shard_map.39.refs_1_), channel_id=1, source_target_pairs={{0,6},{1,7},{2,4},{3,5},{4,2},{5,3},{6,0},{7,1},{8,14},{9,15},{10,... | collective-permute-start | bytes 589832 | tf_op jit(solution)/shard_map/ppermute | solution.py:241
  27.8 21.3 %copy-start.2 = (bf16[128,8192]{1,0:T(8,128)(2,1)S(1)}, bf16[128,8192]{1,0:T(8,128)(2,1)}, u32[]{:S(2)}) copy-start(bf16[128,8192]{1,0:T(8,128)(2,1)} %refs_1_.1) | copy-start | bytes 6291460
  27.9 1.8 %collective-permute-start.4 = (f32[48,2048]{1,0:T(8,128)S(1)}, f32[48,2048]{1,0:T(8,128)S(1)}, u32[]{:S(2)}, u32[]{:S(2)}) collective-permute-start(f32[48,2048]{1,0:T(8,128)S(1)} %shard_map.43), channel_id=1, source_target_pairs={{0,1},{1,0},{2,3},{3,2},{4,5},{5,4},{6,7},{7,6},{8,9},{9,8},{10,11... | collective-permute-start | bytes 1179656 | tf_op jit(solution)/shard_map/ppermute | solution.py:241
  29.7 8.2 %collective-permute-start.5 = (bf16[48,2048]{1,0:T(8,128)(2,1)S(1)}, bf16[48,2048]{1,0:T(8,128)(2,1)S(1)}, u32[]{:S(2)}, u32[]{:S(2)}) collective-permute-start(bf16[48,2048]{1,0:T(8,128)(2,1)S(1)} %add_convert_fusion.mine_ref), channel_id=1, source_target_pairs={{0,8},{1,6},{2,10},{3,4},{4,12},{5,2},{6,14},{7,0},{8,15},{9,1},{1... | collective-permute-start | bytes 589832 | tf_op jit(solution)/shard_map/ppermute | solution.py:241
  31.5 10.3 %collective-permute-start.7 = (bf16[48,2048]{1,0:T(8,128)(2,1)S(1)}, bf16[48,2048]{1,0:T(8,128)(2,1)S(1)}, u32[]{:S(2)}, u32[]{:S(2)}) collective-permute-start(bf16[48,2048]{1,0:T(8,128)(2,1)S(1)} %add_convert_fusion.mine_ref), channel_id=1, source_target_pairs={{0,14},{1,2},{2,12},{3,0},{4,10},{5,6},{6,8},{7,4},{8,11},{9,7},{1... | collective-permute-start | bytes 589832 | tf_op jit(solution)/shard_map/ppermute | solution.py:241
  37.9 6.7 %collective-permute-start.6 = (bf16[48,2048]{1,0:T(8,128)(2,1)S(1)}, bf16[48,2048]{1,0:T(8,128)(2,1)S(1)}, u32[]{:S(2)}, u32[]{:S(2)}) collective-permute-start(bf16[48,2048]{1,0:T(8,128)(2,1)S(1)} %shard_map.44.refs_0_), channel_id=1, source_target_pairs={{0,4},{1,5},{2,6},{3,7},{4,0},{5,1},{6,2},{7,3},{8,12},{9,13},{10,... | collective-permute-start | bytes 589832 | tf_op jit(solution)/shard_map/ppermute | solution.py:241
  38.7 8.1 %collective-permute-start.9 = (bf16[48,2048]{1,0:T(8,128)(2,1)S(1)}, bf16[48,2048]{1,0:T(8,128)(2,1)S(1)}, u32[]{:S(2)}, u32[]{:S(2)}) collective-permute-start(bf16[48,2048]{1,0:T(8,128)(2,1)S(1)} %shard_map.44.refs_0_), channel_id=1, source_target_pairs={{0,16},{1,3},{2,18},{3,1},{4,20},{5,7},{6,22},{7,5},{8,10},{9,25},... | collective-permute-start | bytes 589832 | tf_op jit(solution)/shard_map/ppermute | solution.py:241
  41.7 7.4 %collective-permute-start.10 = (bf16[48,2048]{1,0:T(8,128)(2,1)S(1)}, bf16[48,2048]{1,0:T(8,128)(2,1)S(1)}, u32[]{:S(2)}, u32[]{:S(2)}) collective-permute-start(bf16[48,2048]{1,0:T(8,128)(2,1)S(1)} %shard_map.44.refs_0_), channel_id=1, source_target_pairs={{0,16},{1,17},{2,18},{3,19},{4,20},{5,21},{6,22},{7,23},{8,24},{9,... | collective-permute-start | bytes 589832 | tf_op jit(solution)/shard_map/ppermute | solution.py:241
  44.7 8.1 %copy-start.1 = (bf16[96,2048]{1,0:T(8,128)(2,1)S(1)}, bf16[96,2048]{1,0:T(8,128)(2,1)}, u32[]{:S(2)}) copy-start(bf16[96,2048]{1,0:T(8,128)(2,1)} %param.3) | copy-start | bytes 1179652
  47.0 3.9 %collective-permute-start.11 = (f32[48,128]{1,0:T(8,128)S(1)}, f32[48,128]{1,0:T(8,128)S(1)}, u32[]{:S(2)}, u32[]{:S(2)}) collective-permute-start(f32[48,128]{1,0:T(8,128)S(1)} %shard_map.48), channel_id=1, source_target_pairs={{0,16},{1,17},{2,18},{3,19},{4,20},{5,21},{6,22},{7,23},{8,24},{9,... | collective-permute-start | bytes 73736 | tf_op jit(solution)/shard_map/ppermute | solution.py:241
  50.9 1.3 %collective-permute-start.12 = (f32[48,128]{1,0:T(8,128)S(1)}, f32[48,128]{1,0:T(8,128)S(1)}, u32[]{:S(2)}, u32[]{:S(2)}) collective-permute-start(f32[48,128]{1,0:T(8,128)S(1)} %get-tuple-element.62), channel_id=1, source_target_pairs={{0,1},{1,0},{2,3},{3,2},{4,5},{5,4},{6,7},{7,6},{8,9},{9,8},{10,11... | collective-permute-start | bytes 73736 | tf_op jit(solution)/shard_map/ppermute | solution.py:241

commit v25 on v22

--- a/solution.py
+++ b/solution.py
@@ -263,25 +263,48 @@
                 return sy, sz + 2 if sd == 0 else sz - 2, sx, sd
             return sy, sz ^ 1, 1 - sx, 1 - sd
 
+        def help_beside(sy, sz, sx, sd):
+            su = sz if sd == 0 else nz - 1 - sz
+            return sy, sz if su < near else sz ^ 1, sx, 1 - sd
+
+        def help_across(sy, sz, sx, sd):
+            su = sz if sd == 0 else nz - 1 - sz
+            return sy, sz, sx if su < near else 1 - sx, 1 - sd
+
+        def among_far(flip_z, flip_x):
+            def target(sy, sz, sx, sd):
+                su = sz if sd == 0 else nz - 1 - sz
+                if su < near:
+                    return 1 - sy, sz, sx, sd
+                return sy, sz ^ flip_z, sx ^ flip_x, sd
+
+            return target
+
         came = move(own, start)
         if direct:
-            corner = along_z(own, {0: 3, 1: 2}, True)
+            helped = [move(own, help_beside), move(own, help_across)]
         first = pick(dims, own, came, after)
+        if direct:
+            beside, across, corner = (move(first, among_far(*f)) for f in ((1, 0), (0, 1), (1, 1)))
+            beside, *helped = lax.optimization_barrier((beside, *helped))
+
+            def later(mine, other):
+                def take(after):
+                    ready, _ = lax.optimization_barrier((mine, after))
+                    return pick(dims, ready, other)
+
+                return take
+
+            return first, later(helped[0], beside), later(helped[1], across), later(came, corner)
+
         pairs = {0: 1, 1: 0, 2: 3, 3: 2}
-        beside = along_z(first, pairs)
+
+        def corner(before, after):
+            ready, _ = lax.optimization_barrier((first, before))
+            return lax.optimization_barrier((along_z(ready, pairs, True), after))[0]
+
         across = along_z(first, {0: 0, 1: 1, 2: 2, 3: 3}, True)
-        if direct:
-            beside, corner = lax.optimization_barrier((beside, corner))
-
-        def last(before, after):
-            if direct:
-                ready, _ = lax.optimization_barrier((came, after))
-                return pick(dims, ready, corner)
-            ready, _ = lax.optimization_barrier((first, before))
-            piece, _ = lax.optimization_barrier((along_z(ready, pairs, True), after))
-            return piece
-
-        return first, beside, across, last
+        return first, along_z(first, pairs), across, corner
 
     rows, width = nq // ny, queries.shape[1]
     to_y = cut(stored_grads, ORDER[1:], dims, width)
@@ -291,22 +314,23 @@
     other_grads = swap_y(to_y)
     step = functools.partial(fisher_step, inverse_fisher, dims, width)
     half, quarter = inverse_fisher.shape[0] // 2, inverse_fisher.shape[0] // 4
-    a0, a1, b0, b1 = step(((0, 0, half), (0, half, half), (1, 0, half), (1, half, half)))
+    a0, a1, b0, b1 = step(((0, 0, half), (0, half, half), (1, 0, half), (1, half, quarter)))
     q0, q1, q2, last = gather(own, False, (a0,))
-    total0, c0, c1 = step(((2, 0, half), (2, half, quarter)), q0, (a0, a1))
-    total, c2, d0 = step(((2, half + quarter, quarter), (3, 0, half)), q1, (b0, b1), total0)
-    total, d1 = step(((3, half, half),), q2, (c0, c1, c2), total)
-    (total,) = step((), last(total0, total), (d0, d1), total)
+    total0, b2, c0 = step(((1, half + quarter, quarter), (2, 0, half)), q0, (a0, a1))
+    total, c1, d0 = step(((2, half, half), (3, 0, quarter)), q1, (b0, b1, b2), total0)
+    total, d1, d2 = step(((3, quarter, quarter), (3, half, half)), q2, (c0, c1), total)
+    (total,) = step((), last(total0, total), (d0, d1, d2), total)
     panel = (total + swap_core(total)).astype(jnp.bfloat16)
 
-    p0, p1, p2, last = gather(panel, True)
+    p0, second, third, fourth = gather(panel, True)
     swapped = swap_y(p0)
+    p1 = second(p0)
     p1, other_grads = lax.optimization_barrier((p1, other_grads))
-    p3 = last(p1, p1)
-    other = score_dot([p1, p3], (0, 2), None, other_grads)
-    p2, _ = lax.optimization_barrier((p2, other))
-    other = score_dot([p2], (1,), None, other_grads, other)
-    p2, swapped, _ = lax.optimization_barrier((p2, swapped, other))
+    p2 = third(p1)
+    other = score_dot([p1, p2], (0, 1), None, other_grads)
+    p3 = fourth(other)
+    other = score_dot([p3], (2,), None, other_grads, other)
+    p3, swapped, _ = lax.optimization_barrier((p3, swapped, other))
     mine = score_dot([p0, p1, p2, p3], ORDER, dims, stored_grads)
     theirs = score_dot([swapped], ORDER[:1], dims, stored_grads)
 

time: 52.3 us -> 56.8 us (1.086)
  waiting for transfers between devices: 10.4 us -> 17.5 us
  starting transfers between devices: 20.3 us -> 18.2 us
    ppermute x13 -> x15, waiting for transfers between devices: 10.4 us -> 17.5 us  [move(): return lax.ppermute(value, AXES, pairs)]
    ppermute x13 -> x15, starting transfers between devices: 20.3 us -> 18.2 us  [move(): return lax.ppermute(value, AXES, pairs)]
  transfers between devices with their start and end apart: 13 -> 15, of which waited for: 9 -> 10; matrix products, arithmetic and copies ran while one was open for 0% -> 0% of each run, Pallas kernels for 37% -> 33%
where the time goes in v25:
time: 56.8 us; the launch traced here: 56.7 us
  Pallas kernels  20.2 us (36%)
  starting transfers between devices  18.2 us (32%)
  waiting for transfers between devices  17.5 us (31%)
  other arithmetic  0.65 us (1%)
    ppermute x15, starting transfers between devices, move(): return lax.ppermute(value, AXES, pairs)  18.2 us
    ppermute x15, waiting for transfers between devices, move(): return lax.ppermute(value, AXES, pairs)  17.5 us
    pallas_call x5, Pallas kernels, fisher_step(): pl.pallas_call(functools.partial(fisher_kernel, dims, len(parts), has_bas...  16.7 us
    pallas_call x4, Pallas kernels, score_dot(): pl.pallas_call(functools.partial(score_kernel, dims, order, base is not N...  1.9 us
    pallas_call x1, Pallas kernels, cut(): pl.pallas_call(functools.partial(cut_kernel, dims, order), out_shape=jax....  1.43 us
  transfers between devices with their start and end apart: 15, of which 10 were waited for; matrix products, arithmetic and copies ran while one was open for 0% of the time, Pallas kernels for 33%

profile of v25, /device:TPU:0, one launch (start us, length us, event | category | flops | bytes accessed | tf_op | source)
XLA Modules:
  0.0 56.7 jit_solution(13926632422097479598)
XLA Ops:
  0.0 1.4 %shard_map.37 = bf16[128,6144]{1,0:T(8,128)(2,1)S(1)} custom-call(bf16[128,8192]{1,0:T(8,128)(2,1)} %refs_1_.1), custom_call_target="tpu_custom_call" | custom-call | bytes 1572864 | tf_op jit(solution)/shard_map/pallas_call | solution.py:172
  1.5 4.1 %collective-permute-start = (bf16[48,2048]{1,0:T(8,128)(2,1)S(1)}, bf16[48,2048]{1,0:T(8,128)(2,1)S(1)}, u32[]{:S(2)}, u32[]{:S(2)}) collective-permute-start(bf16[48,2048]{1,0:T(8,128)(2,1)S(1)} %constant_dynamic-slice_fusion.mine_ref), channel_id=1, source_target_pairs={{0,8},{1,6},{2,10},{3,4},{4,12},{5,2},{6,14},{7,0},{8,15},{9,1},{1... | collective-permute-start | bytes 589832 | tf_op jit(solution)/shard_map/ppermute | solution.py:241
  5.6 1.5 %collective-permute-start.9 = (bf16[128,6144]{1,0:T(8,128)(2,1)S(1)}, bf16[128,6144]{1,0:T(8,128)(2,1)S(1)}, u32[]{:S(2)}, u32[]{:S(2)}) collective-permute-start(bf16[128,6144]{1,0:T(8,128)(2,1)S(1)} %shard_map.37), channel_id=1, source_target_pairs={{0,16},{1,17},{2,18},{3,19},{4,20},{5,21},{6,22},{7,23},{8,24},{9,... | collective-permute-start | bytes 4718600 | tf_op jit(solution)/shard_map/ppermute | solution.py:241
  7.1 5.3 %shard_map.38 = (bf16[1024,2048]{1,0:T(8,128)(2,1)S(1)}, bf16[1024,2048]{1,0:T(8,128)(2,1)S(1)}, bf16[1024,2048]{1,0:T(8,128)(2,1)S(1)}, bf16[512,2048]{1,0:T(8,128)(2,1)S(1)}) custom-call(bf16[2048,8192]{1,0:T(8,128)(2,1)} %refs_0_.7), custom_call_target="tpu_custom_call" | custom-call | bytes 14680064 | tf_op jit(solution)/shard_map/pallas_call | solution.py:107
  12.5 1.6 %collective-permute-start.3 = (bf16[48,2048]{1,0:T(8,128)(2,1)S(1)}, bf16[48,2048]{1,0:T(8,128)(2,1)S(1)}, u32[]{:S(2)}, u32[]{:S(2)}) collective-permute-start(bf16[48,2048]{1,0:T(8,128)(2,1)S(1)} %shard_map.39.refs_1_), channel_id=1, source_target_pairs={{0,4},{1,5},{2,6},{3,7},{4,0},{5,1},{6,2},{7,3},{8,12},{9,13},{10,... | collective-permute-start | bytes 589832 | tf_op jit(solution)/shard_map/ppermute | solution.py:241
  14.2 1.5 %collective-permute-start.2 = (bf16[48,2048]{1,0:T(8,128)(2,1)S(1)}, bf16[48,2048]{1,0:T(8,128)(2,1)S(1)}, u32[]{:S(2)}, u32[]{:S(2)}) collective-permute-start(bf16[48,2048]{1,0:T(8,128)(2,1)S(1)} %shard_map.39.refs_1_), channel_id=1, source_target_pairs={{0,2},{1,3},{2,0},{3,1},{4,6},{5,7},{6,4},{7,5},{8,10},{9,11},{10,... | collective-permute-start | bytes 589832 | tf_op jit(solution)/shard_map/ppermute | solution.py:241
  15.7 2.9 %shard_map.40 = (f32[48,2048]{1,0:T(8,128)S(1)}, bf16[512,2048]{1,0:T(8,128)(2,1)S(1)}, bf16[1024,2048]{1,0:T(8,128)(2,1)S(1)}) custom-call(bf16[2048,8192]{1,0:T(8,128)(2,1)} %refs_0_.7, bf16[48,2048]{1,0:T(8,128)(2,1)S(1)} %shard_map.39.refs_1_, bf16[1024,2048]{1,0:T(8,128)(2,1)S(1)} %get-tuple-element.39.refs_0_.refs_2_, ...), custom_call_target="tpu_custom_call" | custom-call | flops 402653184 | bytes 14680064 | tf_op jit(solution)/shard_map/pallas_call | solution.py:107
  18.6 0.5 collective-permute-start.1
  19.1 2.9 %shard_map.41 = (f32[48,2048]{1,0:T(8,128)S(1)}, bf16[1024,2048]{1,0:T(8,128)(2,1)S(1)}, bf16[512,2048]{1,0:T(8,128)(2,1)S(1)}) custom-call(bf16[2048,8192]{1,0:T(8,128)(2,1)} %refs_0_.7, bf16[48,2048]{1,0:T(8,128)(2,1)S(1)} %collective-permute-done.3.refs_1_, bf16[1024,2048]{1,0:T(8,128)(2,1)S(1)} %get-tuple-element.44.refs_2_, ...), custom_call_target="tpu_custom_call" | custom-call | flops 402653184 | bytes 14680064 | tf_op jit(solution)/shard_map/pallas_call | solution.py:107
  22.1 2.9 %shard_map.42 = (f32[48,2048]{1,0:T(8,128)S(1)}, bf16[512,2048]{1,0:T(8,128)(2,1)S(1)}, bf16[1024,2048]{1,0:T(8,128)(2,1)S(1)}) custom-call(bf16[2048,8192]{1,0:T(8,128)(2,1)} %refs_0_.7, bf16[48,2048]{1,0:T(8,128)(2,1)S(1)} %collective-permute-done.2.refs_1_, bf16[1024,2048]{1,0:T(8,128)(2,1)S(1)} %get-tuple-element.43.refs_2_, ...), custom_call_target="tpu_custom_call" | custom-call | flops 402653184 | bytes 14680064 | tf_op jit(solution)/shard_map/pallas_call | solution.py:107
  25.2 2.6 %shard_map.43 = f32[48,2048]{1,0:T(8,128)S(1)} custom-call(bf16[48,2048]{1,0:T(8,128)(2,1)S(1)} %collective-permute-done.1.refs_0_, bf16[512,2048]{1,0:T(8,128)(2,1)S(1)} %get-tuple-element.51.refs_1_, bf16[512,2048]{1,0:T(8,128)(2,1)S(1)} %get-tuple-element.52.refs_2_, bf16[1024,2048]{1,0:T(8,128)(2,1)S(1)} %get-tuple-element.53.refs_3_, ...), custom_call_target="tpu_custom_call" | custom-call | flops 402653184 | bytes 8388608 | tf_op jit(solution)/shard_map/pallas_call | solution.py:107
  27.9 1.7 %collective-permute-done.4 = f32[48,2048]{1,0:T(8,128)S(1)} collective-permute-done((f32[48,2048]{1,0:T(8,128)S(1)}, f32[48,2048]{1,0:T(8,128)S(1)}, u32[]{:S(2)}, u32[]{:S(2)}) %collective-permute-start.4) | collective-permute-done | bytes 393248 | tf_op jit(solution)/shard_map/ppermute | solution.py:241
  29.7 1.8 %collective-permute-start.5 = (bf16[48,2048]{1,0:T(8,128)(2,1)S(1)}, bf16[48,2048]{1,0:T(8,128)(2,1)S(1)}, u32[]{:S(2)}, u32[]{:S(2)}) collective-permute-start(bf16[48,2048]{1,0:T(8,128)(2,1)S(1)} %add_convert_fusion.mine_ref), channel_id=1, source_target_pairs={{0,8},{1,6},{2,10},{3,4},{4,12},{5,2},{6,14},{7,0},{8,15},{9,1},{1... | collective-permute-start | bytes 589832 | tf_op jit(solution)/shard_map/ppermute | solution.py:241
  31.5 0.6 %collective-permute-start.8 = (bf16[48,2048]{1,0:T(8,128)(2,1)S(1)}, bf16[48,2048]{1,0:T(8,128)(2,1)S(1)}, u32[]{:S(2)}, u32[]{:S(2)}) collective-permute-start(bf16[48,2048]{1,0:T(8,128)(2,1)S(1)} %add_convert_fusion.mine_ref), channel_id=1, source_target_pairs={{0,1},{1,2},{2,3},{3,0},{4,5},{5,6},{6,7},{7,4},{8,11},{9,8},{10,9... | collective-permute-start | bytes 589832 | tf_op jit(solution)/shard_map/ppermute | solution.py:241
  32.1 0.7 %collective-permute-start.7 = (bf16[48,2048]{1,0:T(8,128)(2,1)S(1)}, bf16[48,2048]{1,0:T(8,128)(2,1)S(1)}, u32[]{:S(2)}, u32[]{:S(2)}) collective-permute-start(bf16[48,2048]{1,0:T(8,128)(2,1)S(1)} %add_convert_fusion.mine_ref), channel_id=1, source_target_pairs={{0,1},{1,4},{2,3},{3,6},{4,5},{5,0},{6,7},{7,2},{8,13},{9,8},{10,1... | collective-permute-start | bytes 589832 | tf_op jit(solution)/shard_map/ppermute | solution.py:241
  32.8 5.1 %collective-permute-done.5.other_ref.mine_ref = bf16[48,2048]{1,0:T(8,128)(2,1)S(1)} collective-permute-done((bf16[48,2048]{1,0:T(8,128)(2,1)S(1)}, bf16[48,2048]{1,0:T(8,128)(2,1)S(1)}, u32[]{:S(2)}, u32[]{:S(2)}) %collective-permute-start.5) | collective-permute-done | bytes 196640 | tf_op jit(solution)/shard_map/ppermute | solution.py:241
  37.9 0.5 collective-permute-start.6
  38.4 1.6 %collective-permute-start.10 = (bf16[48,2048]{1,0:T(8,128)(2,1)S(1)}, bf16[48,2048]{1,0:T(8,128)(2,1)S(1)}, u32[]{:S(2)}, u32[]{:S(2)}) collective-permute-start(bf16[48,2048]{1,0:T(8,128)(2,1)S(1)} %shard_map.44.refs_0_), channel_id=1, source_target_pairs={{0,16},{1,3},{2,18},{3,1},{4,20},{5,7},{6,22},{7,5},{8,10},{9,25},... | collective-permute-start | bytes 589832 | tf_op jit(solution)/shard_map/ppermute | solution.py:241
  40.0 0.4 collective-permute-start.11
  40.4 1.6 %collective-permute-start.12 = (bf16[48,2048]{1,0:T(8,128)(2,1)S(1)}, bf16[48,2048]{1,0:T(8,128)(2,1)S(1)}, u32[]{:S(2)}, u32[]{:S(2)}) collective-permute-start(bf16[48,2048]{1,0:T(8,128)(2,1)S(1)} %shard_map.44.refs_0_), channel_id=1, source_target_pairs={{0,16},{1,17},{2,18},{3,19},{4,20},{5,21},{6,22},{7,23},{8,24},{9,... | collective-permute-start | bytes 589832 | tf_op jit(solution)/shard_map/ppermute | solution.py:241
  42.1 3.0 %collective-permute-done.6.other_ref = bf16[48,2048]{1,0:T(8,128)(2,1)S(1)} collective-permute-done((bf16[48,2048]{1,0:T(8,128)(2,1)S(1)}, bf16[48,2048]{1,0:T(8,128)(2,1)S(1)}, u32[]{:S(2)}, u32[]{:S(2)}) %collective-permute-start.6) | collective-permute-done | bytes 196640 | tf_op jit(solution)/shard_map/ppermute | solution.py:241
  45.1 3.1 %collective-permute-done.10.other_ref = bf16[48,2048]{1,0:T(8,128)(2,1)S(1)} collective-permute-done((bf16[48,2048]{1,0:T(8,128)(2,1)S(1)}, bf16[48,2048]{1,0:T(8,128)(2,1)S(1)}, u32[]{:S(2)}, u32[]{:S(2)}) %collective-permute-start.10) | collective-permute-done | bytes 196640 | tf_op jit(solution)/shard_map/ppermute | solution.py:241
  48.3 0.5 shard_map.47.refs_2_
  48.7 1.9 %collective-permute-done.11.other_ref = bf16[48,2048]{1,0:T(8,128)(2,1)S(1)} collective-permute-done((bf16[48,2048]{1,0:T(8,128)(2,1)S(1)}, bf16[48,2048]{1,0:T(8,128)(2,1)S(1)}, u32[]{:S(2)}, u32[]{:S(2)}) %collective-permute-start.11) | collective-permute-done | bytes 196640 | tf_op jit(solution)/shard_map/ppermute | solution.py:241
  50.6 0.3 shard_map.49
  50.9 1.6 %collective-permute-start.13 = (f32[48,128]{1,0:T(8,128)S(1)}, f32[48,128]{1,0:T(8,128)S(1)}, u32[]{:S(2)}, u32[]{:S(2)}) collective-permute-start(f32[48,128]{1,0:T(8,128)S(1)} %shard_map.49), channel_id=1, source_target_pairs={{0,16},{1,17},{2,18},{3,19},{4,20},{5,21},{6,22},{7,23},{8,24},{9,... | collective-permute-start | bytes 73736 | tf_op jit(solution)/shard_map/ppermute | solution.py:241
  52.5 0.2 collective-permute-done.12.refs_0_
  52.7 0.3 shard_map.51.theirs_ref
  53.0 0.9 %shard_map.50.mine_ref = f32[48,128]{1,0:T(8,128)S(1)} custom-call(bf16[48,2048]{1,0:T(8,128)(2,1)S(1)} %shard_map.44.refs_0_, bf16[48,2048]{1,0:T(8,128)(2,1)S(1)} %shard_map.45.refs_0_.refs_1_, bf16[48,2048]{1,0:T(8,128)(2,1)S(1)} %shard_map.46.refs_1_.refs_2_, bf16[48,2048]{1,0:T(8,128)(2,1)S(1)} %shard_map.48.refs_0_.refs_3_, bf16[128,8192]{1,0:T(8,128)(2,1)S(1)} %copy-done.2), custom_call_target="tpu_custom_call" | custom-call | flops 100663296 | bytes 2097152 | tf_op jit(solution)/shard_map/pallas_call | solution.py:140
  53.9 0.9 %collective-permute-done.13.other_ref = f32[48,128]{1,0:T(8,128)S(1)} collective-permute-done((f32[48,128]{1,0:T(8,128)S(1)}, f32[48,128]{1,0:T(8,128)S(1)}, u32[]{:S(2)}, u32[]{:S(2)}) %collective-permute-start.13) | collective-permute-done | bytes 24608 | tf_op jit(solution)/shard_map/ppermute | solution.py:241
  54.9 1.2 %collective-permute-done.14 = f32[48,128]{1,0:T(8,128)S(1)} collective-permute-done((f32[48,128]{1,0:T(8,128)S(1)}, f32[48,128]{1,0:T(8,128)S(1)}, u32[]{:S(2)}, u32[]{:S(2)}) %collective-permute-start.14) | collective-permute-done | bytes 24608 | tf_op jit(solution)/shard_map/ppermute | solution.py:241
  56.1 0.6 %add.11 = f32[48,128]{1,0:T(8,128)} add(f32[48,128]{1,0:T(8,128)S(1)} %get-tuple-element.65, f32[48,128]{1,0:T(8,128)S(1)} %collective-permute-done.14) | non-fusion elementwise | flops 6144 | bytes 73728 | tf_op jit(solution)/shard_map/add | solution.py:338
  (23 shorter events, 0.6 us)
Async XLA Ops:
  0.0 1.5 %copy-start = (bf16[96,2048]{1,0:T(8,128)(2,1)S(1)}, bf16[96,2048]{1,0:T(8,128)(2,1)}, u32[]{:S(2)}) copy-start(bf16[96,2048]{1,0:T(8,128)(2,1)} %param.3) | copy-start | bytes 1179652
  1.5 11.0 %collective-permute-start = (bf16[48,2048]{1,0:T(8,128)(2,1)S(1)}, bf16[48,2048]{1,0:T(8,128)(2,1)S(1)}, u32[]{:S(2)}, u32[]{:S(2)}) collective-permute-start(bf16[48,2048]{1,0:T(8,128)(2,1)S(1)} %constant_dynamic-slice_fusion.mine_ref), channel_id=1, source_target_pairs={{0,8},{1,6},{2,10},{3,4},{4,12},{5,2},{6,14},{7,0},{8,15},{9,1},{1... | collective-permute-start | bytes 589832 | tf_op jit(solution)/shard_map/ppermute | solution.py:241
  5.6 39.5 %collective-permute-start.9 = (bf16[128,6144]{1,0:T(8,128)(2,1)S(1)}, bf16[128,6144]{1,0:T(8,128)(2,1)S(1)}, u32[]{:S(2)}, u32[]{:S(2)}) collective-permute-start(bf16[128,6144]{1,0:T(8,128)(2,1)S(1)} %shard_map.37), channel_id=1, source_target_pairs={{0,16},{1,17},{2,18},{3,19},{4,20},{5,21},{6,22},{7,23},{8,24},{9,... | collective-permute-start | bytes 4718600 | tf_op jit(solution)/shard_map/ppermute | solution.py:241
  12.5 6.6 %collective-permute-start.3 = (bf16[48,2048]{1,0:T(8,128)(2,1)S(1)}, bf16[48,2048]{1,0:T(8,128)(2,1)S(1)}, u32[]{:S(2)}, u32[]{:S(2)}) collective-permute-start(bf16[48,2048]{1,0:T(8,128)(2,1)S(1)} %shard_map.39.refs_1_), channel_id=1, source_target_pairs={{0,4},{1,5},{2,6},{3,7},{4,0},{5,1},{6,2},{7,3},{8,12},{9,13},{10,... | collective-permute-start | bytes 589832 | tf_op jit(solution)/shard_map/ppermute | solution.py:241
  14.2 7.9 %collective-permute-start.2 = (bf16[48,2048]{1,0:T(8,128)(2,1)S(1)}, bf16[48,2048]{1,0:T(8,128)(2,1)S(1)}, u32[]{:S(2)}, u32[]{:S(2)}) collective-permute-start(bf16[48,2048]{1,0:T(8,128)(2,1)S(1)} %shard_map.39.refs_1_), channel_id=1, source_target_pairs={{0,2},{1,3},{2,0},{3,1},{4,6},{5,7},{6,4},{7,5},{8,10},{9,11},{10,... | collective-permute-start | bytes 589832 | tf_op jit(solution)/shard_map/ppermute | solution.py:241
  18.6 6.6 %collective-permute-start.1 = (bf16[48,2048]{1,0:T(8,128)(2,1)S(1)}, bf16[48,2048]{1,0:T(8,128)(2,1)S(1)}, u32[]{:S(2)}, u32[]{:S(2)}) collective-permute-start(bf16[48,2048]{1,0:T(8,128)(2,1)S(1)} %shard_map.39.refs_1_), channel_id=1, source_target_pairs={{0,6},{1,7},{2,4},{3,5},{4,2},{5,3},{6,0},{7,1},{8,14},{9,15},{10,... | collective-permute-start | bytes 589832 | tf_op jit(solution)/shard_map/ppermute | solution.py:241
  27.8 24.9 %copy-start.2 = (bf16[128,8192]{1,0:T(8,128)(2,1)S(1)}, bf16[128,8192]{1,0:T(8,128)(2,1)}, u32[]{:S(2)}) copy-start(bf16[128,8192]{1,0:T(8,128)(2,1)} %refs_1_.1) | copy-start | bytes 6291460
  27.9 1.8 %collective-permute-start.4 = (f32[48,2048]{1,0:T(8,128)S(1)}, f32[48,2048]{1,0:T(8,128)S(1)}, u32[]{:S(2)}, u32[]{:S(2)}) collective-permute-start(f32[48,2048]{1,0:T(8,128)S(1)} %shard_map.43), channel_id=1, source_target_pairs={{0,1},{1,0},{2,3},{3,2},{4,5},{5,4},{6,7},{7,6},{8,9},{9,8},{10,11... | collective-permute-start | bytes 1179656 | tf_op jit(solution)/shard_map/ppermute | solution.py:241
  29.7 8.2 %collective-permute-start.5 = (bf16[48,2048]{1,0:T(8,128)(2,1)S(1)}, bf16[48,2048]{1,0:T(8,128)(2,1)S(1)}, u32[]{:S(2)}, u32[]{:S(2)}) collective-permute-start(bf16[48,2048]{1,0:T(8,128)(2,1)S(1)} %add_convert_fusion.mine_ref), channel_id=1, source_target_pairs={{0,8},{1,6},{2,10},{3,4},{4,12},{5,2},{6,14},{7,0},{8,15},{9,1},{1... | collective-permute-start | bytes 589832 | tf_op jit(solution)/shard_map/ppermute | solution.py:241
  31.5 8.5 %collective-permute-start.8 = (bf16[48,2048]{1,0:T(8,128)(2,1)S(1)}, bf16[48,2048]{1,0:T(8,128)(2,1)S(1)}, u32[]{:S(2)}, u32[]{:S(2)}) collective-permute-start(bf16[48,2048]{1,0:T(8,128)(2,1)S(1)} %add_convert_fusion.mine_ref), channel_id=1, source_target_pairs={{0,1},{1,2},{2,3},{3,0},{4,5},{5,6},{6,7},{7,4},{8,11},{9,8},{10,9... | collective-permute-start | bytes 589832 | tf_op jit(solution)/shard_map/ppermute | solution.py:241
  32.1 8.3 %collective-permute-start.7 = (bf16[48,2048]{1,0:T(8,128)(2,1)S(1)}, bf16[48,2048]{1,0:T(8,128)(2,1)S(1)}, u32[]{:S(2)}, u32[]{:S(2)}) collective-permute-start(bf16[48,2048]{1,0:T(8,128)(2,1)S(1)} %add_convert_fusion.mine_ref), channel_id=1, source_target_pairs={{0,1},{1,4},{2,3},{3,6},{4,5},{5,0},{6,7},{7,2},{8,13},{9,8},{10,1... | collective-permute-start | bytes 589832 | tf_op jit(solution)/shard_map/ppermute | solution.py:241
  37.9 7.1 %collective-permute-start.6 = (bf16[48,2048]{1,0:T(8,128)(2,1)S(1)}, bf16[48,2048]{1,0:T(8,128)(2,1)S(1)}, u32[]{:S(2)}, u32[]{:S(2)}) collective-permute-start(bf16[48,2048]{1,0:T(8,128)(2,1)S(1)} %shard_map.44.refs_0_), channel_id=1, source_target_pairs={{0,16},{1,5},{2,18},{3,7},{4,20},{5,1},{6,22},{7,3},{8,12},{9,25},... | collective-permute-start | bytes 589832 | tf_op jit(solution)/shard_map/ppermute | solution.py:241
  38.4 9.8 %collective-permute-start.10 = (bf16[48,2048]{1,0:T(8,128)(2,1)S(1)}, bf16[48,2048]{1,0:T(8,128)(2,1)S(1)}, u32[]{:S(2)}, u32[]{:S(2)}) collective-permute-start(bf16[48,2048]{1,0:T(8,128)(2,1)S(1)} %shard_map.44.refs_0_), channel_id=1, source_target_pairs={{0,16},{1,3},{2,18},{3,1},{4,20},{5,7},{6,22},{7,5},{8,10},{9,25},... | collective-permute-start | bytes 589832 | tf_op jit(solution)/shard_map/ppermute | solution.py:241
  40.0 10.6 %collective-permute-start.11 = (bf16[48,2048]{1,0:T(8,128)(2,1)S(1)}, bf16[48,2048]{1,0:T(8,128)(2,1)S(1)}, u32[]{:S(2)}, u32[]{:S(2)}) collective-permute-start(bf16[48,2048]{1,0:T(8,128)(2,1)S(1)} %shard_map.44.refs_0_), channel_id=1, source_target_pairs={{0,16},{1,7},{2,18},{3,5},{4,20},{5,3},{6,22},{7,1},{8,14},{9,25},... | collective-permute-start | bytes 589832 | tf_op jit(solution)/shard_map/ppermute | solution.py:241
  40.4 12.3 %collective-permute-start.12 = (bf16[48,2048]{1,0:T(8,128)(2,1)S(1)}, bf16[48,2048]{1,0:T(8,128)(2,1)S(1)}, u32[]{:S(2)}, u32[]{:S(2)}) collective-permute-start(bf16[48,2048]{1,0:T(8,128)(2,1)S(1)} %shard_map.44.refs_0_), channel_id=1, source_target_pairs={{0,16},{1,17},{2,18},{3,19},{4,20},{5,21},{6,22},{7,23},{8,24},{9,... | collective-permute-start | bytes 589832 | tf_op jit(solution)/shard_map/ppermute | solution.py:241
  48.3 8.4 %copy-start.1 = (bf16[96,2048]{1,0:T(8,128)(2,1)S(1)}, bf16[96,2048]{1,0:T(8,128)(2,1)}, u32[]{:S(2)}) copy-start(bf16[96,2048]{1,0:T(8,128)(2,1)} %param.3) | copy-start | bytes 1179652
  50.9 3.9 %collective-permute-start.13 = (f32[48,128]{1,0:T(8,128)S(1)}, f32[48,128]{1,0:T(8,128)S(1)}, u32[]{:S(2)}, u32[]{:S(2)}) collective-permute-start(f32[48,128]{1,0:T(8,128)S(1)} %shard_map.49), channel_id=1, source_target_pairs={{0,16},{1,17},{2,18},{3,19},{4,20},{5,21},{6,22},{7,23},{8,24},{9,... | collective-permute-start | bytes 73736 | tf_op jit(solution)/shard_map/ppermute | solution.py:241
  54.8 1.3 %collective-permute-start.14 = (f32[48,128]{1,0:T(8,128)S(1)}, f32[48,128]{1,0:T(8,128)S(1)}, u32[]{:S(2)}, u32[]{:S(2)}) collective-permute-start(f32[48,128]{1,0:T(8,128)S(1)} %get-tuple-element.66), channel_id=1, source_target_pairs={{0,1},{1,0},{2,3},{3,2},{4,5},{5,4},{6,7},{7,6},{8,9},{9,8},{10,11... | collective-permute-start | bytes 73736 | tf_op jit(solution)/shard_map/ppermute | solution.py:241

commit v26 on v25

--- a/solution.py
+++ b/solution.py
@@ -275,7 +275,7 @@
             def target(sy, sz, sx, sd):
                 su = sz if sd == 0 else nz - 1 - sz
                 if su < near:
-                    return 1 - sy, sz, sx, sd
+                    return sy, sz, sx, sd
                 return sy, sz ^ flip_z, sx ^ flip_x, sd
 
             return target

time: 56.8 us -> 57.8 us (1.018)
  the two profiles are of different devices: /device:TPU:0 before, /device:TPU:17 now
where the time goes in v26:
time: 57.8 us; the launch traced here: 57.7 us
  starting transfers between devices  24.9 us (43%)
  Pallas kernels  20.2 us (35%)
  waiting for transfers between devices  11.6 us (20%)
  other arithmetic  0.65 us (1%)
    ppermute x15, starting transfers between devices, move(): return lax.ppermute(value, AXES, pairs)  24.9 us
    pallas_call x5, Pallas kernels, fisher_step(): pl.pallas_call(functools.partial(fisher_kernel, dims, len(parts), has_bas...  16.7 us
    ppermute x15, waiting for transfers between devices, move(): return lax.ppermute(value, AXES, pairs)  11.6 us
    pallas_call x4, Pallas kernels, score_dot(): pl.pallas_call(functools.partial(score_kernel, dims, order, base is not N...  1.9 us
    pallas_call x1, Pallas kernels, cut(): pl.pallas_call(functools.partial(cut_kernel, dims, order), out_shape=jax....  1.43 us
  transfers between devices with their start and end apart: 15, of which 5 were waited for; matrix products, arithmetic and copies ran while one was open for 0% of the time, Pallas kernels for 32%

profile of v26, /device:TPU:17, one launch (start us, length us, event | category | flops | bytes accessed | tf_op | source)
XLA Modules:
  0.0 57.7 jit_solution(12984856657604772884)
XLA Ops:
  0.0 1.4 %shard_map.37 = bf16[128,6144]{1,0:T(8,128)(2,1)S(1)} custom-call(bf16[128,8192]{1,0:T(8,128)(2,1)} %refs_1_.1), custom_call_target="tpu_custom_call" | custom-call | bytes 1572864 | tf_op jit(solution)/shard_map/pallas_call | solution.py:172
  1.4 0.0 copy-done
  1.5 0.1 collective-permute-start
  1.6 1.3 %collective-permute-start.9 = (bf16[128,6144]{1,0:T(8,128)(2,1)S(1)}, bf16[128,6144]{1,0:T(8,128)(2,1)S(1)}, u32[]{:S(2)}, u32[]{:S(2)}) collective-permute-start(bf16[128,6144]{1,0:T(8,128)(2,1)S(1)} %shard_map.37), channel_id=1, source_target_pairs={{0,16},{1,17},{2,18},{3,19},{4,20},{5,21},{6,22},{7,23},{8,24},{9,... | collective-permute-start | bytes 4718600 | tf_op jit(solution)/shard_map/ppermute | solution.py:241
  2.9 5.3 %shard_map.38 = (bf16[1024,2048]{1,0:T(8,128)(2,1)S(1)}, bf16[1024,2048]{1,0:T(8,128)(2,1)S(1)}, bf16[1024,2048]{1,0:T(8,128)(2,1)S(1)}, bf16[512,2048]{1,0:T(8,128)(2,1)S(1)}) custom-call(bf16[2048,8192]{1,0:T(8,128)(2,1)} %refs_0_.7), custom_call_target="tpu_custom_call" | custom-call | bytes 14680064 | tf_op jit(solution)/shard_map/pallas_call | solution.py:107
  8.2 1.1 %collective-permute-done.other_ref = bf16[48,2048]{1,0:T(8,128)(2,1)S(1)} collective-permute-done((bf16[48,2048]{1,0:T(8,128)(2,1)S(1)}, bf16[48,2048]{1,0:T(8,128)(2,1)S(1)}, u32[]{:S(2)}, u32[]{:S(2)}) %collective-permute-start) | collective-permute-done | bytes 196640 | tf_op jit(solution)/shard_map/ppermute | solution.py:241
  9.3 0.4 collective-permute-start.3
  9.7 2.2 %collective-permute-start.2 = (bf16[48,2048]{1,0:T(8,128)(2,1)S(1)}, bf16[48,2048]{1,0:T(8,128)(2,1)S(1)}, u32[]{:S(2)}, u32[]{:S(2)}) collective-permute-start(bf16[48,2048]{1,0:T(8,128)(2,1)S(1)} %shard_map.39.refs_1_), channel_id=1, source_target_pairs={{0,2},{1,3},{2,0},{3,1},{4,6},{5,7},{6,4},{7,5},{8,10},{9,11},{10,... | collective-permute-start | bytes 589832 | tf_op jit(solution)/shard_map/ppermute | solution.py:241
  12.0 2.9 %shard_map.40 = (f32[48,2048]{1,0:T(8,128)S(1)}, bf16[512,2048]{1,0:T(8,128)(2,1)S(1)}, bf16[1024,2048]{1,0:T(8,128)(2,1)S(1)}) custom-call(bf16[2048,8192]{1,0:T(8,128)(2,1)} %refs_0_.7, bf16[48,2048]{1,0:T(8,128)(2,1)S(1)} %shard_map.39.refs_1_, bf16[1024,2048]{1,0:T(8,128)(2,1)S(1)} %get-tuple-element.39.refs_0_.refs_2_, ...), custom_call_target="tpu_custom_call" | custom-call | flops 402653184 | bytes 14680064 | tf_op jit(solution)/shard_map/pallas_call | solution.py:107
  14.9 0.1 collective-permute-start.1
  15.0 2.9 %shard_map.41 = (f32[48,2048]{1,0:T(8,128)S(1)}, bf16[1024,2048]{1,0:T(8,128)(2,1)S(1)}, bf16[512,2048]{1,0:T(8,128)(2,1)S(1)}) custom-call(bf16[2048,8192]{1,0:T(8,128)(2,1)} %refs_0_.7, bf16[48,2048]{1,0:T(8,128)(2,1)S(1)} %collective-permute-done.3.refs_1_, bf16[1024,2048]{1,0:T(8,128)(2,1)S(1)} %get-tuple-element.44.refs_2_, ...), custom_call_target="tpu_custom_call" | custom-call | flops 402653184 | bytes 14680064 | tf_op jit(solution)/shard_map/pallas_call | solution.py:107
  17.9 2.9 %shard_map.42 = (f32[48,2048]{1,0:T(8,128)S(1)}, bf16[512,2048]{1,0:T(8,128)(2,1)S(1)}, bf16[1024,2048]{1,0:T(8,128)(2,1)S(1)}) custom-call(bf16[2048,8192]{1,0:T(8,128)(2,1)} %refs_0_.7, bf16[48,2048]{1,0:T(8,128)(2,1)S(1)} %collective-permute-done.2.refs_1_, bf16[1024,2048]{1,0:T(8,128)(2,1)S(1)} %get-tuple-element.43.refs_2_, ...), custom_call_target="tpu_custom_call" | custom-call | flops 402653184 | bytes 14680064 | tf_op jit(solution)/shard_map/pallas_call | solution.py:107
  20.9 2.6 %shard_map.43 = f32[48,2048]{1,0:T(8,128)S(1)} custom-call(bf16[48,2048]{1,0:T(8,128)(2,1)S(1)} %collective-permute-done.1.refs_0_, bf16[512,2048]{1,0:T(8,128)(2,1)S(1)} %get-tuple-element.51.refs_1_, bf16[512,2048]{1,0:T(8,128)(2,1)S(1)} %get-tuple-element.52.refs_2_, bf16[1024,2048]{1,0:T(8,128)(2,1)S(1)} %get-tuple-element.53.refs_3_, ...), custom_call_target="tpu_custom_call" | custom-call | flops 402653184 | bytes 8388608 | tf_op jit(solution)/shard_map/pallas_call | solution.py:107
  23.5 0.0 copy-start.2
  23.5 2.8 %collective-permute-start.4 = (f32[48,2048]{1,0:T(8,128)S(1)}, f32[48,2048]{1,0:T(8,128)S(1)}, u32[]{:S(2)}, u32[]{:S(2)}) collective-permute-start(f32[48,2048]{1,0:T(8,128)S(1)} %shard_map.43), channel_id=1, source_target_pairs={{0,1},{1,0},{2,3},{3,2},{4,5},{5,4},{6,7},{7,6},{8,9},{9,8},{10,11... | collective-permute-start | bytes 1179656 | tf_op jit(solution)/shard_map/ppermute | solution.py:241
  26.3 1.3 %collective-permute-done.4 = f32[48,2048]{1,0:T(8,128)S(1)} collective-permute-done((f32[48,2048]{1,0:T(8,128)S(1)}, f32[48,2048]{1,0:T(8,128)S(1)}, u32[]{:S(2)}, u32[]{:S(2)}) %collective-permute-start.4) | collective-permute-done | bytes 393248 | tf_op jit(solution)/shard_map/ppermute | solution.py:241
  27.7 1.0 %collective-permute-start.5 = (bf16[48,2048]{1,0:T(8,128)(2,1)S(1)}, bf16[48,2048]{1,0:T(8,128)(2,1)S(1)}, u32[]{:S(2)}, u32[]{:S(2)}) collective-permute-start(bf16[48,2048]{1,0:T(8,128)(2,1)S(1)} %add_convert_fusion.mine_ref), channel_id=1, source_target_pairs={{0,8},{1,6},{2,10},{3,4},{4,12},{5,2},{6,14},{7,0},{8,15},{9,1},{1... | collective-permute-start | bytes 589832 | tf_op jit(solution)/shard_map/ppermute | solution.py:241
  28.7 1.4 %collective-permute-start.8 = (bf16[48,2048]{1,0:T(8,128)(2,1)S(1)}, bf16[48,2048]{1,0:T(8,128)(2,1)S(1)}, u32[]{:S(2)}, u32[]{:S(2)}) collective-permute-start(bf16[48,2048]{1,0:T(8,128)(2,1)S(1)} %add_convert_fusion.mine_ref), channel_id=1, source_target_pairs={{0,1},{1,2},{2,3},{3,0},{4,5},{5,6},{6,7},{7,4},{8,11},{9,8},{10,9... | collective-permute-start | bytes 589832 | tf_op jit(solution)/shard_map/ppermute | solution.py:241
  30.1 6.0 %collective-permute-done.5.other_ref.mine_ref = bf16[48,2048]{1,0:T(8,128)(2,1)S(1)} collective-permute-done((bf16[48,2048]{1,0:T(8,128)(2,1)S(1)}, bf16[48,2048]{1,0:T(8,128)(2,1)S(1)}, u32[]{:S(2)}, u32[]{:S(2)}) %collective-permute-start.5) | collective-permute-done | bytes 196640 | tf_op jit(solution)/shard_map/ppermute | solution.py:241
  36.1 0.7 %collective-permute-start.6 = (bf16[48,2048]{1,0:T(8,128)(2,1)S(1)}, bf16[48,2048]{1,0:T(8,128)(2,1)S(1)}, u32[]{:S(2)}, u32[]{:S(2)}) collective-permute-start(bf16[48,2048]{1,0:T(8,128)(2,1)S(1)} %shard_map.44.refs_0_), channel_id=1, source_target_pairs={{0,0},{1,5},{2,2},{3,7},{4,4},{5,1},{6,6},{7,3},{8,12},{9,9},{10,1... | collective-permute-start | bytes 589832 | tf_op jit(solution)/shard_map/ppermute | solution.py:241
  36.8 0.7 %collective-permute-start.10 = (bf16[48,2048]{1,0:T(8,128)(2,1)S(1)}, bf16[48,2048]{1,0:T(8,128)(2,1)S(1)}, u32[]{:S(2)}, u32[]{:S(2)}) collective-permute-start(bf16[48,2048]{1,0:T(8,128)(2,1)S(1)} %shard_map.44.refs_0_), channel_id=1, source_target_pairs={{0,0},{1,3},{2,2},{3,1},{4,4},{5,7},{6,6},{7,5},{8,10},{9,9},{10,8... | collective-permute-start | bytes 589832 | tf_op jit(solution)/shard_map/ppermute | solution.py:241
  37.5 0.7 %collective-permute-start.11 = (bf16[48,2048]{1,0:T(8,128)(2,1)S(1)}, bf16[48,2048]{1,0:T(8,128)(2,1)S(1)}, u32[]{:S(2)}, u32[]{:S(2)}) collective-permute-start(bf16[48,2048]{1,0:T(8,128)(2,1)S(1)} %shard_map.44.refs_0_), channel_id=1, source_target_pairs={{0,0},{1,7},{2,2},{3,5},{4,4},{5,3},{6,6},{7,1},{8,14},{9,9},{10,1... | collective-permute-start | bytes 589832 | tf_op jit(solution)/shard_map/ppermute | solution.py:241
  38.1 0.4 collective-permute-start.12
  38.7 0.5 shard_map.47.refs_2_
  39.2 0.3 shard_map.49
  39.5 1.2 %collective-permute-start.13 = (f32[48,128]{1,0:T(8,128)S(1)}, f32[48,128]{1,0:T(8,128)S(1)}, u32[]{:S(2)}, u32[]{:S(2)}) collective-permute-start(f32[48,128]{1,0:T(8,128)S(1)} %shard_map.49), channel_id=1, source_target_pairs={{0,16},{1,17},{2,18},{3,19},{4,20},{5,21},{6,22},{7,23},{8,24},{9,... | collective-permute-start | bytes 73736 | tf_op jit(solution)/shard_map/ppermute | solution.py:241
  40.7 2.4 %collective-permute-done.12.refs_0_ = bf16[48,2048]{1,0:T(8,128)(2,1)S(1)} collective-permute-done((bf16[48,2048]{1,0:T(8,128)(2,1)S(1)}, bf16[48,2048]{1,0:T(8,128)(2,1)S(1)}, u32[]{:S(2)}, u32[]{:S(2)}) %collective-permute-start.12) | collective-permute-done | bytes 196640 | tf_op jit(solution)/shard_map/ppermute | solution.py:241
  43.0 0.3 shard_map.51.theirs_ref
  43.3 0.9 %shard_map.50.mine_ref = f32[48,128]{1,0:T(8,128)S(1)} custom-call(bf16[48,2048]{1,0:T(8,128)(2,1)S(1)} %shard_map.44.refs_0_, bf16[48,2048]{1,0:T(8,128)(2,1)S(1)} %shard_map.45.refs_0_.refs_1_, bf16[48,2048]{1,0:T(8,128)(2,1)S(1)} %shard_map.46.refs_1_.refs_2_, bf16[48,2048]{1,0:T(8,128)(2,1)S(1)} %shard_map.48.refs_0_.refs_3_, bf16[128,8192]{1,0:T(8,128)(2,1)S(1)} %copy-done.2), custom_call_target="tpu_custom_call" | custom-call | flops 100663296 | bytes 2097152 | tf_op jit(solution)/shard_map/pallas_call | solution.py:140
  44.2 12.0 %collective-permute-start.14 = (f32[48,128]{1,0:T(8,128)S(1)}, f32[48,128]{1,0:T(8,128)S(1)}, u32[]{:S(2)}, u32[]{:S(2)}) collective-permute-start(f32[48,128]{1,0:T(8,128)S(1)} %get-tuple-element.66), channel_id=1, source_target_pairs={{0,1},{1,0},{2,3},{3,2},{4,5},{5,4},{6,7},{7,6},{8,9},{9,8},{10,11... | collective-permute-start | bytes 73736 | tf_op jit(solution)/shard_map/ppermute | solution.py:241
  56.2 0.8 %collective-permute-done.14 = f32[48,128]{1,0:T(8,128)S(1)} collective-permute-done((f32[48,128]{1,0:T(8,128)S(1)}, f32[48,128]{1,0:T(8,128)S(1)}, u32[]{:S(2)}, u32[]{:S(2)}) %collective-permute-start.14) | collective-permute-done | bytes 24608 | tf_op jit(solution)/shard_map/ppermute | solution.py:241
  57.0 0.6 %add.11 = f32[48,128]{1,0:T(8,128)} add(f32[48,128]{1,0:T(8,128)S(1)} %get-tuple-element.65, f32[48,128]{1,0:T(8,128)S(1)} %collective-permute-done.14) | non-fusion elementwise | flops 6144 | bytes 73728 | tf_op jit(solution)/shard_map/add | solution.py:338
  (23 shorter events, 0.2 us)
Async XLA Ops:
  0.0 1.5 %copy-start = (bf16[96,2048]{1,0:T(8,128)(2,1)S(1)}, bf16[96,2048]{1,0:T(8,128)(2,1)}, u32[]{:S(2)}) copy-start(bf16[96,2048]{1,0:T(8,128)(2,1)} %param.3) | copy-start | bytes 1179652
  1.5 7.8 %collective-permute-start = (bf16[48,2048]{1,0:T(8,128)(2,1)S(1)}, bf16[48,2048]{1,0:T(8,128)(2,1)S(1)}, u32[]{:S(2)}, u32[]{:S(2)}) collective-permute-start(bf16[48,2048]{1,0:T(8,128)(2,1)S(1)} %constant_dynamic-slice_fusion.mine_ref), channel_id=1, source_target_pairs={{0,8},{1,6},{2,10},{3,4},{4,12},{5,2},{6,14},{7,0},{8,15},{9,1},{1... | collective-permute-start | bytes 589832 | tf_op jit(solution)/shard_map/ppermute | solution.py:241
  1.6 37.1 %collective-permute-start.9 = (bf16[128,6144]{1,0:T(8,128)(2,1)S(1)}, bf16[128,6144]{1,0:T(8,128)(2,1)S(1)}, u32[]{:S(2)}, u32[]{:S(2)}) collective-permute-start(bf16[128,6144]{1,0:T(8,128)(2,1)S(1)} %shard_map.37), channel_id=1, source_target_pairs={{0,16},{1,17},{2,18},{3,19},{4,20},{5,21},{6,22},{7,23},{8,24},{9,... | collective-permute-start | bytes 4718600 | tf_op jit(solution)/shard_map/ppermute | solution.py:241
  9.3 5.7 %collective-permute-start.3 = (bf16[48,2048]{1,0:T(8,128)(2,1)S(1)}, bf16[48,2048]{1,0:T(8,128)(2,1)S(1)}, u32[]{:S(2)}, u32[]{:S(2)}) collective-permute-start(bf16[48,2048]{1,0:T(8,128)(2,1)S(1)} %shard_map.39.refs_1_), channel_id=1, source_target_pairs={{0,4},{1,5},{2,6},{3,7},{4,0},{5,1},{6,2},{7,3},{8,12},{9,13},{10,... | collective-permute-start | bytes 589832 | tf_op jit(solution)/shard_map/ppermute | solution.py:241
  9.7 8.2 %collective-permute-start.2 = (bf16[48,2048]{1,0:T(8,128)(2,1)S(1)}, bf16[48,2048]{1,0:T(8,128)(2,1)S(1)}, u32[]{:S(2)}, u32[]{:S(2)}) collective-permute-start(bf16[48,2048]{1,0:T(8,128)(2,1)S(1)} %shard_map.39.refs_1_), channel_id=1, source_target_pairs={{0,2},{1,3},{2,0},{3,1},{4,6},{5,7},{6,4},{7,5},{8,10},{9,11},{10,... | collective-permute-start | bytes 589832 | tf_op jit(solution)/shard_map/ppermute | solution.py:241
  14.9 6.0 %collective-permute-start.1 = (bf16[48,2048]{1,0:T(8,128)(2,1)S(1)}, bf16[48,2048]{1,0:T(8,128)(2,1)S(1)}, u32[]{:S(2)}, u32[]{:S(2)}) collective-permute-start(bf16[48,2048]{1,0:T(8,128)(2,1)S(1)} %shard_map.39.refs_1_), channel_id=1, source_target_pairs={{0,6},{1,7},{2,4},{3,5},{4,2},{5,3},{6,0},{7,1},{8,14},{9,15},{10,... | collective-permute-start | bytes 589832 | tf_op jit(solution)/shard_map/ppermute | solution.py:241
  23.5 19.5 %copy-start.2 = (bf16[128,8192]{1,0:T(8,128)(2,1)S(1)}, bf16[128,8192]{1,0:T(8,128)(2,1)}, u32[]{:S(2)}) copy-start(bf16[128,8192]{1,0:T(8,128)(2,1)} %refs_1_.1) | copy-start | bytes 6291460
  23.5 4.1 %collective-permute-start.4 = (f32[48,2048]{1,0:T(8,128)S(1)}, f32[48,2048]{1,0:T(8,128)S(1)}, u32[]{:S(2)}, u32[]{:S(2)}) collective-permute-start(f32[48,2048]{1,0:T(8,128)S(1)} %shard_map.43), channel_id=1, source_target_pairs={{0,1},{1,0},{2,3},{3,2},{4,5},{5,4},{6,7},{7,6},{8,9},{9,8},{10,11... | collective-permute-start | bytes 1179656 | tf_op jit(solution)/shard_map/ppermute | solution.py:241
  27.7 8.4 %collective-permute-start.5 = (bf16[48,2048]{1,0:T(8,128)(2,1)S(1)}, bf16[48,2048]{1,0:T(8,128)(2,1)S(1)}, u32[]{:S(2)}, u32[]{:S(2)}) collective-permute-start(bf16[48,2048]{1,0:T(8,128)(2,1)S(1)} %add_convert_fusion.mine_ref), channel_id=1, source_target_pairs={{0,8},{1,6},{2,10},{3,4},{4,12},{5,2},{6,14},{7,0},{8,15},{9,1},{1... | collective-permute-start | bytes 589832 | tf_op jit(solution)/shard_map/ppermute | solution.py:241
  28.7 8.8 %collective-permute-start.8 = (bf16[48,2048]{1,0:T(8,128)(2,1)S(1)}, bf16[48,2048]{1,0:T(8,128)(2,1)S(1)}, u32[]{:S(2)}, u32[]{:S(2)}) collective-permute-start(bf16[48,2048]{1,0:T(8,128)(2,1)S(1)} %add_convert_fusion.mine_ref), channel_id=1, source_target_pairs={{0,1},{1,2},{2,3},{3,0},{4,5},{5,6},{6,7},{7,4},{8,11},{9,8},{10,9... | collective-permute-start | bytes 589832 | tf_op jit(solution)/shard_map/ppermute | solution.py:241
  30.1 8.0 %collective-permute-start.7 = (bf16[48,2048]{1,0:T(8,128)(2,1)S(1)}, bf16[48,2048]{1,0:T(8,128)(2,1)S(1)}, u32[]{:S(2)}, u32[]{:S(2)}) collective-permute-start(bf16[48,2048]{1,0:T(8,128)(2,1)S(1)} %add_convert_fusion.mine_ref), channel_id=1, source_target_pairs={{0,1},{1,4},{2,3},{3,6},{4,5},{5,0},{6,7},{7,2},{8,13},{9,8},{10,1... | collective-permute-start | bytes 589832 | tf_op jit(solution)/shard_map/ppermute | solution.py:241
  36.1 2.5 %collective-permute-start.6 = (bf16[48,2048]{1,0:T(8,128)(2,1)S(1)}, bf16[48,2048]{1,0:T(8,128)(2,1)S(1)}, u32[]{:S(2)}, u32[]{:S(2)}) collective-permute-start(bf16[48,2048]{1,0:T(8,128)(2,1)S(1)} %shard_map.44.refs_0_), channel_id=1, source_target_pairs={{0,0},{1,5},{2,2},{3,7},{4,4},{5,1},{6,6},{7,3},{8,12},{9,9},{10,1... | collective-permute-start | bytes 589832 | tf_op jit(solution)/shard_map/ppermute | solution.py:241
  36.8 1.9 %collective-permute-start.10 = (bf16[48,2048]{1,0:T(8,128)(2,1)S(1)}, bf16[48,2048]{1,0:T(8,128)(2,1)S(1)}, u32[]{:S(2)}, u32[]{:S(2)}) collective-permute-start(bf16[48,2048]{1,0:T(8,128)(2,1)S(1)} %shard_map.44.refs_0_), channel_id=1, source_target_pairs={{0,0},{1,3},{2,2},{3,1},{4,4},{5,7},{6,6},{7,5},{8,10},{9,9},{10,8... | collective-permute-start | bytes 589832 | tf_op jit(solution)/shard_map/ppermute | solution.py:241
  37.5 1.7 %collective-permute-start.11 = (bf16[48,2048]{1,0:T(8,128)(2,1)S(1)}, bf16[48,2048]{1,0:T(8,128)(2,1)S(1)}, u32[]{:S(2)}, u32[]{:S(2)}) collective-permute-start(bf16[48,2048]{1,0:T(8,128)(2,1)S(1)} %shard_map.44.refs_0_), channel_id=1, source_target_pairs={{0,0},{1,7},{2,2},{3,5},{4,4},{5,3},{6,6},{7,1},{8,14},{9,9},{10,1... | collective-permute-start | bytes 589832 | tf_op jit(solution)/shard_map/ppermute | solution.py:241
  38.1 4.9 %collective-permute-start.12 = (bf16[48,2048]{1,0:T(8,128)(2,1)S(1)}, bf16[48,2048]{1,0:T(8,128)(2,1)S(1)}, u32[]{:S(2)}, u32[]{:S(2)}) collective-permute-start(bf16[48,2048]{1,0:T(8,128)(2,1)S(1)} %shard_map.44.refs_0_), channel_id=1, source_target_pairs={{0,16},{1,17},{2,18},{3,19},{4,20},{5,21},{6,22},{7,23},{8,24},{9,... | collective-permute-start | bytes 589832 | tf_op jit(solution)/shard_map/ppermute | solution.py:241
  38.7 19.0 %copy-start.1 = (bf16[96,2048]{1,0:T(8,128)(2,1)S(1)}, bf16[96,2048]{1,0:T(8,128)(2,1)}, u32[]{:S(2)}) copy-start(bf16[96,2048]{1,0:T(8,128)(2,1)} %param.3) | copy-start | bytes 1179652
  39.5 4.7 %collective-permute-start.13 = (f32[48,128]{1,0:T(8,128)S(1)}, f32[48,128]{1,0:T(8,128)S(1)}, u32[]{:S(2)}, u32[]{:S(2)}) collective-permute-start(f32[48,128]{1,0:T(8,128)S(1)} %shard_map.49), channel_id=1, source_target_pairs={{0,16},{1,17},{2,18},{3,19},{4,20},{5,21},{6,22},{7,23},{8,24},{9,... | collective-permute-start | bytes 73736 | tf_op jit(solution)/shard_map/ppermute | solution.py:241
  44.2 12.8 %collective-permute-start.14 = (f32[48,128]{1,0:T(8,128)S(1)}, f32[48,128]{1,0:T(8,128)S(1)}, u32[]{:S(2)}, u32[]{:S(2)}) collective-permute-start(f32[48,128]{1,0:T(8,128)S(1)} %get-tuple-element.66), channel_id=1, source_target_pairs={{0,1},{1,0},{2,3},{3,2},{4,5},{5,4},{6,7},{7,6},{8,9},{9,8},{10,11... | collective-permute-start | bytes 73736 | tf_op jit(solution)/shard_map/ppermute | solution.py:241

commit v27 on v22

--- a/solution.py
+++ b/solution.py
@@ -291,12 +291,12 @@
     other_grads = swap_y(to_y)
     step = functools.partial(fisher_step, inverse_fisher, dims, width)
     half, quarter = inverse_fisher.shape[0] // 2, inverse_fisher.shape[0] // 4
-    a0, a1, b0, b1 = step(((0, 0, half), (0, half, half), (1, 0, half), (1, half, half)))
+    a0, a1, b0, b1 = step(((0, 0, half), (0, half, half), (1, 0, half), (1, half, quarter)))
     q0, q1, q2, last = gather(own, False, (a0,))
-    total0, c0, c1 = step(((2, 0, half), (2, half, quarter)), q0, (a0, a1))
-    total, c2, d0 = step(((2, half + quarter, quarter), (3, 0, half)), q1, (b0, b1), total0)
-    total, d1 = step(((3, half, half),), q2, (c0, c1, c2), total)
-    (total,) = step((), last(total0, total), (d0, d1), total)
+    total0, b2, c0 = step(((1, half + quarter, quarter), (2, 0, half)), q0, (a0, a1))
+    total, c1, d0 = step(((2, half, half), (3, 0, quarter)), q1, (b0, b1, b2), total0)
+    total, d1, d2 = step(((3, quarter, quarter), (3, half, half)), q2, (c0, c1), total)
+    (total,) = step((), last(total0, total), (d0, d1, d2), total)
     panel = (total + swap_core(total)).astype(jnp.bfloat16)
 
     p0, p1, p2, last = gather(panel, True)

time: 52.3 us -> 51.8 us (level)
  transfers between devices with their start and end apart: 13 -> 13, of which waited for: 9 -> 9; matrix products, arithmetic and copies ran while one was open for 0% -> 0% of each run, Pallas kernels for 37% -> 36%
where the time goes in v27:
time: 51.8 us; the launch traced here: 51.7 us
  starting transfers between devices  20.5 us (40%)
  Pallas kernels  20.1 us (39%)
  waiting for transfers between devices  10.2 us (20%)
  other arithmetic  0.65 us (1%)
    ppermute x13, starting transfers between devices, move(): return lax.ppermute(value, AXES, pairs)  20.5 us
    pallas_call x5, Pallas kernels, fisher_step(): pl.pallas_call(functools.partial(fisher_kernel, dims, len(parts), has_bas...  16.7 us
    ppermute x13, waiting for transfers between devices, move(): return lax.ppermute(value, AXES, pairs)  10.2 us
    pallas_call x4, Pallas kernels, score_dot(): pl.pallas_call(functools.partial(score_kernel, dims, order, base is not N...  1.89 us
    pallas_call x1, Pallas kernels, cut(): pl.pallas_call(functools.partial(cut_kernel, dims, order), out_shape=jax....  1.43 us
  transfers between devices with their start and end apart: 13, of which 9 were waited for; matrix products, arithmetic and copies ran while one was open for 0% of the time, Pallas kernels for 36%

profile of v27, /device:TPU:0, one launch (start us, length us, event | category | flops | bytes accessed | tf_op | source)
XLA Modules:
  0.0 51.7 jit_solution(7023305063490994974)
XLA Ops:
  0.0 1.4 %shard_map.37 = bf16[128,6144]{1,0:T(8,128)(2,1)S(1)} custom-call(bf16[128,8192]{1,0:T(8,128)(2,1)} %refs_1_.1), custom_call_target="tpu_custom_call" | custom-call | bytes 1572864 | tf_op jit(solution)/shard_map/pallas_call | solution.py:172
  1.5 4.1 %collective-permute-start = (bf16[48,2048]{1,0:T(8,128)(2,1)S(1)}, bf16[48,2048]{1,0:T(8,128)(2,1)S(1)}, u32[]{:S(2)}, u32[]{:S(2)}) collective-permute-start(bf16[48,2048]{1,0:T(8,128)(2,1)S(1)} %constant_dynamic-slice_fusion.mine_ref), channel_id=1, source_target_pairs={{0,8},{1,6},{2,10},{3,4},{4,12},{5,2},{6,14},{7,0},{8,15},{9,1},{1... | collective-permute-start | bytes 589832 | tf_op jit(solution)/shard_map/ppermute | solution.py:241
  5.6 1.5 %collective-permute-start.8 = (bf16[128,6144]{1,0:T(8,128)(2,1)S(1)}, bf16[128,6144]{1,0:T(8,128)(2,1)S(1)}, u32[]{:S(2)}, u32[]{:S(2)}) collective-permute-start(bf16[128,6144]{1,0:T(8,128)(2,1)S(1)} %shard_map.37), channel_id=1, source_target_pairs={{0,16},{1,17},{2,18},{3,19},{4,20},{5,21},{6,22},{7,23},{8,24},{9,... | collective-permute-start | bytes 4718600 | tf_op jit(solution)/shard_map/ppermute | solution.py:241
  7.1 5.3 %shard_map.38 = (bf16[1024,2048]{1,0:T(8,128)(2,1)S(1)}, bf16[1024,2048]{1,0:T(8,128)(2,1)S(1)}, bf16[1024,2048]{1,0:T(8,128)(2,1)S(1)}, bf16[512,2048]{1,0:T(8,128)(2,1)S(1)}) custom-call(bf16[2048,8192]{1,0:T(8,128)(2,1)} %refs_0_.7), custom_call_target="tpu_custom_call" | custom-call | bytes 14680064 | tf_op jit(solution)/shard_map/pallas_call | solution.py:107
  12.5 1.6 %collective-permute-start.3 = (bf16[48,2048]{1,0:T(8,128)(2,1)S(1)}, bf16[48,2048]{1,0:T(8,128)(2,1)S(1)}, u32[]{:S(2)}, u32[]{:S(2)}) collective-permute-start(bf16[48,2048]{1,0:T(8,128)(2,1)S(1)} %shard_map.39.refs_1_), channel_id=1, source_target_pairs={{0,4},{1,5},{2,6},{3,7},{4,0},{5,1},{6,2},{7,3},{8,12},{9,13},{10,... | collective-permute-start | bytes 589832 | tf_op jit(solution)/shard_map/ppermute | solution.py:241
  14.2 1.5 %collective-permute-start.2 = (bf16[48,2048]{1,0:T(8,128)(2,1)S(1)}, bf16[48,2048]{1,0:T(8,128)(2,1)S(1)}, u32[]{:S(2)}, u32[]{:S(2)}) collective-permute-start(bf16[48,2048]{1,0:T(8,128)(2,1)S(1)} %shard_map.39.refs_1_), channel_id=1, source_target_pairs={{0,2},{1,3},{2,0},{3,1},{4,6},{5,7},{6,4},{7,5},{8,10},{9,11},{10,... | collective-permute-start | bytes 589832 | tf_op jit(solution)/shard_map/ppermute | solution.py:241
  15.7 2.9 %shard_map.40 = (f32[48,2048]{1,0:T(8,128)S(1)}, bf16[512,2048]{1,0:T(8,128)(2,1)S(1)}, bf16[1024,2048]{1,0:T(8,128)(2,1)S(1)}) custom-call(bf16[2048,8192]{1,0:T(8,128)(2,1)} %refs_0_.7, bf16[48,2048]{1,0:T(8,128)(2,1)S(1)} %shard_map.39.refs_1_, bf16[1024,2048]{1,0:T(8,128)(2,1)S(1)} %get-tuple-element.37.refs_0_.refs_2_, ...), custom_call_target="tpu_custom_call" | custom-call | flops 402653184 | bytes 14680064 | tf_op jit(solution)/shard_map/pallas_call | solution.py:107
  18.6 0.5 collective-permute-start.1
  19.0 0.1 collective-permute-done.3.refs_1_
  19.1 2.9 %shard_map.41 = (f32[48,2048]{1,0:T(8,128)S(1)}, bf16[1024,2048]{1,0:T(8,128)(2,1)S(1)}, bf16[512,2048]{1,0:T(8,128)(2,1)S(1)}) custom-call(bf16[2048,8192]{1,0:T(8,128)(2,1)} %refs_0_.7, bf16[48,2048]{1,0:T(8,128)(2,1)S(1)} %collective-permute-done.3.refs_1_, bf16[1024,2048]{1,0:T(8,128)(2,1)S(1)} %get-tuple-element.42.refs_2_, ...), custom_call_target="tpu_custom_call" | custom-call | flops 402653184 | bytes 14680064 | tf_op jit(solution)/shard_map/pallas_call | solution.py:107
  22.1 2.9 %shard_map.42 = (f32[48,2048]{1,0:T(8,128)S(1)}, bf16[512,2048]{1,0:T(8,128)(2,1)S(1)}, bf16[1024,2048]{1,0:T(8,128)(2,1)S(1)}) custom-call(bf16[2048,8192]{1,0:T(8,128)(2,1)} %refs_0_.7, bf16[48,2048]{1,0:T(8,128)(2,1)S(1)} %collective-permute-done.2.refs_1_, bf16[1024,2048]{1,0:T(8,128)(2,1)S(1)} %get-tuple-element.41.refs_2_, ...), custom_call_target="tpu_custom_call" | custom-call | flops 402653184 | bytes 14680064 | tf_op jit(solution)/shard_map/pallas_call | solution.py:107
  25.0 0.2 collective-permute-done.1.refs_0_
  25.2 2.6 %shard_map.43 = f32[48,2048]{1,0:T(8,128)S(1)} custom-call(bf16[48,2048]{1,0:T(8,128)(2,1)S(1)} %collective-permute-done.1.refs_0_, bf16[512,2048]{1,0:T(8,128)(2,1)S(1)} %get-tuple-element.49.refs_1_, bf16[512,2048]{1,0:T(8,128)(2,1)S(1)} %get-tuple-element.50.refs_2_, bf16[1024,2048]{1,0:T(8,128)(2,1)S(1)} %get-tuple-element.51.refs_3_, ...), custom_call_target="tpu_custom_call" | custom-call | flops 402653184 | bytes 8388608 | tf_op jit(solution)/shard_map/pallas_call | solution.py:107
  27.9 1.7 %collective-permute-done.4 = f32[48,2048]{1,0:T(8,128)S(1)} collective-permute-done((f32[48,2048]{1,0:T(8,128)S(1)}, f32[48,2048]{1,0:T(8,128)S(1)}, u32[]{:S(2)}, u32[]{:S(2)}) %collective-permute-start.4) | collective-permute-done | bytes 393248 | tf_op jit(solution)/shard_map/ppermute | solution.py:241
  29.7 1.8 %collective-permute-start.5 = (bf16[48,2048]{1,0:T(8,128)(2,1)S(1)}, bf16[48,2048]{1,0:T(8,128)(2,1)S(1)}, u32[]{:S(2)}, u32[]{:S(2)}) collective-permute-start(bf16[48,2048]{1,0:T(8,128)(2,1)S(1)} %add_convert_fusion.mine_ref), channel_id=1, source_target_pairs={{0,8},{1,6},{2,10},{3,4},{4,12},{5,2},{6,14},{7,0},{8,15},{9,1},{1... | collective-permute-start | bytes 589832 | tf_op jit(solution)/shard_map/ppermute | solution.py:241
  31.5 4.0 %collective-permute-start.7 = (bf16[48,2048]{1,0:T(8,128)(2,1)S(1)}, bf16[48,2048]{1,0:T(8,128)(2,1)S(1)}, u32[]{:S(2)}, u32[]{:S(2)}) collective-permute-start(bf16[48,2048]{1,0:T(8,128)(2,1)S(1)} %add_convert_fusion.mine_ref), channel_id=1, source_target_pairs={{0,14},{2,12},{4,10},{6,8},{9,7},{11,5},{13,3},{15,1},{16,30},{18,... | collective-permute-start | bytes 589832 | tf_op jit(solution)/shard_map/ppermute | solution.py:241
  35.5 2.3 %collective-permute-done.5.other_ref.mine_ref = bf16[48,2048]{1,0:T(8,128)(2,1)S(1)} collective-permute-done((bf16[48,2048]{1,0:T(8,128)(2,1)S(1)}, bf16[48,2048]{1,0:T(8,128)(2,1)S(1)}, u32[]{:S(2)}, u32[]{:S(2)}) %collective-permute-start.5) | collective-permute-done | bytes 196640 | tf_op jit(solution)/shard_map/ppermute | solution.py:241
  37.9 0.7 %collective-permute-start.6 = (bf16[48,2048]{1,0:T(8,128)(2,1)S(1)}, bf16[48,2048]{1,0:T(8,128)(2,1)S(1)}, u32[]{:S(2)}, u32[]{:S(2)}) collective-permute-start(bf16[48,2048]{1,0:T(8,128)(2,1)S(1)} %shard_map.44.refs_0_), channel_id=1, source_target_pairs={{0,4},{1,5},{2,6},{3,7},{4,0},{5,1},{6,2},{7,3},{8,12},{9,13},{10,... | collective-permute-start | bytes 589832 | tf_op jit(solution)/shard_map/ppermute | solution.py:241
  38.6 3.1 %collective-permute-start.9 = (bf16[48,2048]{1,0:T(8,128)(2,1)S(1)}, bf16[48,2048]{1,0:T(8,128)(2,1)S(1)}, u32[]{:S(2)}, u32[]{:S(2)}) collective-permute-start(bf16[48,2048]{1,0:T(8,128)(2,1)S(1)} %shard_map.44.refs_0_), channel_id=1, source_target_pairs={{0,2},{1,3},{2,0},{3,1},{4,6},{5,7},{6,4},{7,5},{8,10},{9,11},{10,... | collective-permute-start | bytes 589832 | tf_op jit(solution)/shard_map/ppermute | solution.py:241
  41.7 0.7 %collective-permute-start.10 = (bf16[48,2048]{1,0:T(8,128)(2,1)S(1)}, bf16[48,2048]{1,0:T(8,128)(2,1)S(1)}, u32[]{:S(2)}, u32[]{:S(2)}) collective-permute-start(bf16[48,2048]{1,0:T(8,128)(2,1)S(1)} %shard_map.44.refs_0_), channel_id=1, source_target_pairs={{0,16},{1,17},{2,18},{3,19},{4,20},{5,21},{6,22},{7,23},{8,24},{9,... | collective-permute-start | bytes 589832 | tf_op jit(solution)/shard_map/ppermute | solution.py:241
  42.4 2.4 %collective-permute-done.6.refs_0_.refs_1_ = bf16[48,2048]{1,0:T(8,128)(2,1)S(1)} collective-permute-done((bf16[48,2048]{1,0:T(8,128)(2,1)S(1)}, bf16[48,2048]{1,0:T(8,128)(2,1)S(1)}, u32[]{:S(2)}, u32[]{:S(2)}) %collective-permute-start.6) | collective-permute-done | bytes 196640 | tf_op jit(solution)/shard_map/ppermute | solution.py:241
  44.8 0.5 shard_map.46.refs_2_
  45.3 0.4 collective-permute-done.9.refs_0_.refs_2_
  45.6 0.3 shard_map.47
  45.9 0.8 %collective-permute-start.11 = (f32[48,128]{1,0:T(8,128)S(1)}, f32[48,128]{1,0:T(8,128)S(1)}, u32[]{:S(2)}, u32[]{:S(2)}) collective-permute-start(f32[48,128]{1,0:T(8,128)S(1)} %shard_map.47), channel_id=1, source_target_pairs={{0,16},{1,17},{2,18},{3,19},{4,20},{5,21},{6,22},{7,23},{8,24},{9,... | collective-permute-start | bytes 73736 | tf_op jit(solution)/shard_map/ppermute | solution.py:241
  46.7 0.7 %collective-permute-done.10.refs_0_ = bf16[48,2048]{1,0:T(8,128)(2,1)S(1)} collective-permute-done((bf16[48,2048]{1,0:T(8,128)(2,1)S(1)}, bf16[48,2048]{1,0:T(8,128)(2,1)S(1)}, u32[]{:S(2)}, u32[]{:S(2)}) %collective-permute-start.10) | collective-permute-done | bytes 196640 | tf_op jit(solution)/shard_map/ppermute | solution.py:241
  47.4 0.3 shard_map.49.theirs_ref
  47.7 0.8 %shard_map.48.mine_ref = f32[48,128]{1,0:T(8,128)S(1)} custom-call(bf16[48,2048]{1,0:T(8,128)(2,1)S(1)} %shard_map.44.refs_0_, bf16[48,2048]{1,0:T(8,128)(2,1)S(1)} %collective-permute-done.6.refs_0_.refs_1_, bf16[48,2048]{1,0:T(8,128)(2,1)S(1)} %collective-permute-done.9.refs_0_.refs_2_, bf16[48,2048]{1,0:T(8,128)(2,1)S(1)} %shard_map.45.refs_1_.refs_3_, ...), custom_call_target="tpu_custom_call" | custom-call | flops 100663296 | bytes 2097152 | tf_op jit(solution)/shard_map/pallas_call | solution.py:140
  48.5 1.3 %collective-permute-done.11.other_ref = f32[48,128]{1,0:T(8,128)S(1)} collective-permute-done((f32[48,128]{1,0:T(8,128)S(1)}, f32[48,128]{1,0:T(8,128)S(1)}, u32[]{:S(2)}, u32[]{:S(2)}) %collective-permute-start.11) | collective-permute-done | bytes 24608 | tf_op jit(solution)/shard_map/ppermute | solution.py:241
  49.8 0.1 collective-permute-start.12
  49.9 1.2 %collective-permute-done.12 = f32[48,128]{1,0:T(8,128)S(1)} collective-permute-done((f32[48,128]{1,0:T(8,128)S(1)}, f32[48,128]{1,0:T(8,128)S(1)}, u32[]{:S(2)}, u32[]{:S(2)}) %collective-permute-start.12) | collective-permute-done | bytes 24608 | tf_op jit(solution)/shard_map/ppermute | solution.py:241
  51.1 0.6 %add.11 = f32[48,128]{1,0:T(8,128)} add(f32[48,128]{1,0:T(8,128)S(1)} %get-tuple-element.61, f32[48,128]{1,0:T(8,128)S(1)} %collective-permute-done.12) | non-fusion elementwise | flops 6144 | bytes 73728 | tf_op jit(solution)/shard_map/add | solution.py:314
  (17 shorter events, 0.2 us)
Async XLA Ops:
  0.0 1.5 %copy-start = (bf16[96,2048]{1,0:T(8,128)(2,1)S(1)}, bf16[96,2048]{1,0:T(8,128)(2,1)}, u32[]{:S(2)}) copy-start(bf16[96,2048]{1,0:T(8,128)(2,1)} %param.3) | copy-start | bytes 1179652
  1.5 11.0 %collective-permute-start = (bf16[48,2048]{1,0:T(8,128)(2,1)S(1)}, bf16[48,2048]{1,0:T(8,128)(2,1)S(1)}, u32[]{:S(2)}, u32[]{:S(2)}) collective-permute-start(bf16[48,2048]{1,0:T(8,128)(2,1)S(1)} %constant_dynamic-slice_fusion.mine_ref), channel_id=1, source_target_pairs={{0,8},{1,6},{2,10},{3,4},{4,12},{5,2},{6,14},{7,0},{8,15},{9,1},{1... | collective-permute-start | bytes 589832 | tf_op jit(solution)/shard_map/ppermute | solution.py:241
  5.6 39.2 %collective-permute-start.8 = (bf16[128,6144]{1,0:T(8,128)(2,1)S(1)}, bf16[128,6144]{1,0:T(8,128)(2,1)S(1)}, u32[]{:S(2)}, u32[]{:S(2)}) collective-permute-start(bf16[128,6144]{1,0:T(8,128)(2,1)S(1)} %shard_map.37), channel_id=1, source_target_pairs={{0,16},{1,17},{2,18},{3,19},{4,20},{5,21},{6,22},{7,23},{8,24},{9,... | collective-permute-start | bytes 4718600 | tf_op jit(solution)/shard_map/ppermute | solution.py:241
  12.5 6.6 %collective-permute-start.3 = (bf16[48,2048]{1,0:T(8,128)(2,1)S(1)}, bf16[48,2048]{1,0:T(8,128)(2,1)S(1)}, u32[]{:S(2)}, u32[]{:S(2)}) collective-permute-start(bf16[48,2048]{1,0:T(8,128)(2,1)S(1)} %shard_map.39.refs_1_), channel_id=1, source_target_pairs={{0,4},{1,5},{2,6},{3,7},{4,0},{5,1},{6,2},{7,3},{8,12},{9,13},{10,... | collective-permute-start | bytes 589832 | tf_op jit(solution)/shard_map/ppermute | solution.py:241
  14.2 7.9 %collective-permute-start.2 = (bf16[48,2048]{1,0:T(8,128)(2,1)S(1)}, bf16[48,2048]{1,0:T(8,128)(2,1)S(1)}, u32[]{:S(2)}, u32[]{:S(2)}) collective-permute-start(bf16[48,2048]{1,0:T(8,128)(2,1)S(1)} %shard_map.39.refs_1_), channel_id=1, source_target_pairs={{0,2},{1,3},{2,0},{3,1},{4,6},{5,7},{6,4},{7,5},{8,10},{9,11},{10,... | collective-permute-start | bytes 589832 | tf_op jit(solution)/shard_map/ppermute | solution.py:241
  18.6 6.6 %collective-permute-start.1 = (bf16[48,2048]{1,0:T(8,128)(2,1)S(1)}, bf16[48,2048]{1,0:T(8,128)(2,1)S(1)}, u32[]{:S(2)}, u32[]{:S(2)}) collective-permute-start(bf16[48,2048]{1,0:T(8,128)(2,1)S(1)} %shard_map.39.refs_1_), channel_id=1, source_target_pairs={{0,6},{1,7},{2,4},{3,5},{4,2},{5,3},{6,0},{7,1},{8,14},{9,15},{10,... | collective-permute-start | bytes 589832 | tf_op jit(solution)/shard_map/ppermute | solution.py:241
  27.8 19.5 %copy-start.2 = (bf16[128,8192]{1,0:T(8,128)(2,1)S(1)}, bf16[128,8192]{1,0:T(8,128)(2,1)}, u32[]{:S(2)}) copy-start(bf16[128,8192]{1,0:T(8,128)(2,1)} %refs_1_.1) | copy-start | bytes 6291460
  27.9 1.8 %collective-permute-start.4 = (f32[48,2048]{1,0:T(8,128)S(1)}, f32[48,2048]{1,0:T(8,128)S(1)}, u32[]{:S(2)}, u32[]{:S(2)}) collective-permute-start(f32[48,2048]{1,0:T(8,128)S(1)} %shard_map.43), channel_id=1, source_target_pairs={{0,1},{1,0},{2,3},{3,2},{4,5},{5,4},{6,7},{7,6},{8,9},{9,8},{10,11... | collective-permute-start | bytes 1179656 | tf_op jit(solution)/shard_map/ppermute | solution.py:241
  29.7 8.2 %collective-permute-start.5 = (bf16[48,2048]{1,0:T(8,128)(2,1)S(1)}, bf16[48,2048]{1,0:T(8,128)(2,1)S(1)}, u32[]{:S(2)}, u32[]{:S(2)}) collective-permute-start(bf16[48,2048]{1,0:T(8,128)(2,1)S(1)} %add_convert_fusion.mine_ref), channel_id=1, source_target_pairs={{0,8},{1,6},{2,10},{3,4},{4,12},{5,2},{6,14},{7,0},{8,15},{9,1},{1... | collective-permute-start | bytes 589832 | tf_op jit(solution)/shard_map/ppermute | solution.py:241
  31.5 10.9 %collective-permute-start.7 = (bf16[48,2048]{1,0:T(8,128)(2,1)S(1)}, bf16[48,2048]{1,0:T(8,128)(2,1)S(1)}, u32[]{:S(2)}, u32[]{:S(2)}) collective-permute-start(bf16[48,2048]{1,0:T(8,128)(2,1)S(1)} %add_convert_fusion.mine_ref), channel_id=1, source_target_pairs={{0,14},{2,12},{4,10},{6,8},{9,7},{11,5},{13,3},{15,1},{16,30},{18,... | collective-permute-start | bytes 589832 | tf_op jit(solution)/shard_map/ppermute | solution.py:241
  37.9 6.9 %collective-permute-start.6 = (bf16[48,2048]{1,0:T(8,128)(2,1)S(1)}, bf16[48,2048]{1,0:T(8,128)(2,1)S(1)}, u32[]{:S(2)}, u32[]{:S(2)}) collective-permute-start(bf16[48,2048]{1,0:T(8,128)(2,1)S(1)} %shard_map.44.refs_0_), channel_id=1, source_target_pairs={{0,4},{1,5},{2,6},{3,7},{4,0},{5,1},{6,2},{7,3},{8,12},{9,13},{10,... | collective-permute-start | bytes 589832 | tf_op jit(solution)/shard_map/ppermute | solution.py:241
  38.6 7.0 %collective-permute-start.9 = (bf16[48,2048]{1,0:T(8,128)(2,1)S(1)}, bf16[48,2048]{1,0:T(8,128)(2,1)S(1)}, u32[]{:S(2)}, u32[]{:S(2)}) collective-permute-start(bf16[48,2048]{1,0:T(8,128)(2,1)S(1)} %shard_map.44.refs_0_), channel_id=1, source_target_pairs={{0,2},{1,3},{2,0},{3,1},{4,6},{5,7},{6,4},{7,5},{8,10},{9,11},{10,... | collective-permute-start | bytes 589832 | tf_op jit(solution)/shard_map/ppermute | solution.py:241
  41.7 5.7 %collective-permute-start.10 = (bf16[48,2048]{1,0:T(8,128)(2,1)S(1)}, bf16[48,2048]{1,0:T(8,128)(2,1)S(1)}, u32[]{:S(2)}, u32[]{:S(2)}) collective-permute-start(bf16[48,2048]{1,0:T(8,128)(2,1)S(1)} %shard_map.44.refs_0_), channel_id=1, source_target_pairs={{0,16},{1,17},{2,18},{3,19},{4,20},{5,21},{6,22},{7,23},{8,24},{9,... | collective-permute-start | bytes 589832 | tf_op jit(solution)/shard_map/ppermute | solution.py:241
  44.8 6.9 %copy-start.1 = (bf16[96,2048]{1,0:T(8,128)(2,1)S(1)}, bf16[96,2048]{1,0:T(8,128)(2,1)}, u32[]{:S(2)}) copy-start(bf16[96,2048]{1,0:T(8,128)(2,1)} %param.3) | copy-start | bytes 1179652
  45.9 3.9 %collective-permute-start.11 = (f32[48,128]{1,0:T(8,128)S(1)}, f32[48,128]{1,0:T(8,128)S(1)}, u32[]{:S(2)}, u32[]{:S(2)}) collective-permute-start(f32[48,128]{1,0:T(8,128)S(1)} %shard_map.47), channel_id=1, source_target_pairs={{0,16},{1,17},{2,18},{3,19},{4,20},{5,21},{6,22},{7,23},{8,24},{9,... | collective-permute-start | bytes 73736 | tf_op jit(solution)/shard_map/ppermute | solution.py:241
  49.8 1.3 %collective-permute-start.12 = (f32[48,128]{1,0:T(8,128)S(1)}, f32[48,128]{1,0:T(8,128)S(1)}, u32[]{:S(2)}, u32[]{:S(2)}) collective-permute-start(f32[48,128]{1,0:T(8,128)S(1)} %get-tuple-element.62), channel_id=1, source_target_pairs={{0,1},{1,0},{2,3},{3,2},{4,5},{5,4},{6,7},{7,6},{8,9},{9,8},{10,11... | collective-permute-start | bytes 73736 | tf_op jit(solution)/shard_map/ppermute | solution.py:241

commit v28 on v27

--- a/solution.py
+++ b/solution.py
@@ -271,7 +271,7 @@
         beside = along_z(first, pairs)
         across = along_z(first, {0: 0, 1: 1, 2: 2, 3: 3}, True)
         if direct:
-            beside, corner = lax.optimization_barrier((beside, corner))
+            across, corner = lax.optimization_barrier((across, corner))
 
         def last(before, after):
             if direct:
@@ -301,12 +301,12 @@
 
     p0, p1, p2, last = gather(panel, True)
     swapped = swap_y(p0)
-    p1, other_grads = lax.optimization_barrier((p1, other_grads))
-    p3 = last(p1, p1)
-    other = score_dot([p1, p3], (0, 2), None, other_grads)
-    p2, _ = lax.optimization_barrier((p2, other))
-    other = score_dot([p2], (1,), None, other_grads, other)
-    p2, swapped, _ = lax.optimization_barrier((p2, swapped, other))
+    p2, other_grads = lax.optimization_barrier((p2, other_grads))
+    p3 = last(p2, p2)
+    other = score_dot([p2, p3], (1, 2), None, other_grads)
+    p1, _ = lax.optimization_barrier((p1, other))
+    other = score_dot([p1], (0,), None, other_grads, other)
+    p1, swapped, _ = lax.optimization_barrier((p1, swapped, other))
     mine = score_dot([p0, p1, p2, p3], ORDER, dims, stored_grads)
     theirs = score_dot([swapped], ORDER[:1], dims, stored_grads)
 

time: 51.8 us -> 52.3 us (level)
  transfers between devices with their start and end apart: 13 -> 13, of which waited for: 9 -> 8; matrix products, arithmetic and copies ran while one was open for 0% -> 0% of each run, Pallas kernels for 36% -> 36%
where the time goes in v28:
time: 52.3 us; the launch traced here: 52.2 us
  starting transfers between devices  20.6 us (39%)
  Pallas kernels  20.1 us (38%)
  waiting for transfers between devices  10.6 us (20%)
  other arithmetic  0.65 us (1%)
    ppermute x13, starting transfers between devices, move(): return lax.ppermute(value, AXES, pairs)  20.6 us
    pallas_call x5, Pallas kernels, fisher_step(): pl.pallas_call(functools.partial(fisher_kernel, dims, len(parts), has_bas...  16.7 us
    ppermute x13, waiting for transfers between devices, move(): return lax.ppermute(value, AXES, pairs)  10.6 us
    pallas_call x4, Pallas kernels, score_dot(): pl.pallas_call(functools.partial(score_kernel, dims, order, base is not N...  1.9 us
    pallas_call x1, Pallas kernels, cut(): pl.pallas_call(functools.partial(cut_kernel, dims, order), out_shape=jax....  1.43 us
  transfers between devices with their start and end apart: 13, of which 8 were waited for; matrix products, arithmetic and copies ran while one was open for 0% of the time, Pallas kernels for 36%

profile of v28, /device:TPU:0, one launch (start us, length us, event | category | flops | bytes accessed | tf_op | source)
XLA Modules:
  0.0 52.2 jit_solution(7107777565404868934)
XLA Ops:
  0.0 1.4 %shard_map.37 = bf16[128,6144]{1,0:T(8,128)(2,1)S(1)} custom-call(bf16[128,8192]{1,0:T(8,128)(2,1)} %refs_1_.1), custom_call_target="tpu_custom_call" | custom-call | bytes 1572864 | tf_op jit(solution)/shard_map/pallas_call | solution.py:172
  1.5 4.1 %collective-permute-start = (bf16[48,2048]{1,0:T(8,128)(2,1)S(1)}, bf16[48,2048]{1,0:T(8,128)(2,1)S(1)}, u32[]{:S(2)}, u32[]{:S(2)}) collective-permute-start(bf16[48,2048]{1,0:T(8,128)(2,1)S(1)} %constant_dynamic-slice_fusion.mine_ref), channel_id=1, source_target_pairs={{0,8},{1,6},{2,10},{3,4},{4,12},{5,2},{6,14},{7,0},{8,15},{9,1},{1... | collective-permute-start | bytes 589832 | tf_op jit(solution)/shard_map/ppermute | solution.py:241
  5.6 1.5 %collective-permute-start.9 = (bf16[128,6144]{1,0:T(8,128)(2,1)S(1)}, bf16[128,6144]{1,0:T(8,128)(2,1)S(1)}, u32[]{:S(2)}, u32[]{:S(2)}) collective-permute-start(bf16[128,6144]{1,0:T(8,128)(2,1)S(1)} %shard_map.37), channel_id=1, source_target_pairs={{0,16},{1,17},{2,18},{3,19},{4,20},{5,21},{6,22},{7,23},{8,24},{9,... | collective-permute-start | bytes 4718600 | tf_op jit(solution)/shard_map/ppermute | solution.py:241
  7.1 5.3 %shard_map.38 = (bf16[1024,2048]{1,0:T(8,128)(2,1)S(1)}, bf16[1024,2048]{1,0:T(8,128)(2,1)S(1)}, bf16[1024,2048]{1,0:T(8,128)(2,1)S(1)}, bf16[512,2048]{1,0:T(8,128)(2,1)S(1)}) custom-call(bf16[2048,8192]{1,0:T(8,128)(2,1)} %refs_0_.7), custom_call_target="tpu_custom_call" | custom-call | bytes 14680064 | tf_op jit(solution)/shard_map/pallas_call | solution.py:107
  12.5 1.6 %collective-permute-start.3 = (bf16[48,2048]{1,0:T(8,128)(2,1)S(1)}, bf16[48,2048]{1,0:T(8,128)(2,1)S(1)}, u32[]{:S(2)}, u32[]{:S(2)}) collective-permute-start(bf16[48,2048]{1,0:T(8,128)(2,1)S(1)} %shard_map.39.refs_1_), channel_id=1, source_target_pairs={{0,4},{1,5},{2,6},{3,7},{4,0},{5,1},{6,2},{7,3},{8,12},{9,13},{10,... | collective-permute-start | bytes 589832 | tf_op jit(solution)/shard_map/ppermute | solution.py:241
  14.2 1.5 %collective-permute-start.2 = (bf16[48,2048]{1,0:T(8,128)(2,1)S(1)}, bf16[48,2048]{1,0:T(8,128)(2,1)S(1)}, u32[]{:S(2)}, u32[]{:S(2)}) collective-permute-start(bf16[48,2048]{1,0:T(8,128)(2,1)S(1)} %shard_map.39.refs_1_), channel_id=1, source_target_pairs={{0,2},{1,3},{2,0},{3,1},{4,6},{5,7},{6,4},{7,5},{8,10},{9,11},{10,... | collective-permute-start | bytes 589832 | tf_op jit(solution)/shard_map/ppermute | solution.py:241
  15.7 2.9 %shard_map.40 = (f32[48,2048]{1,0:T(8,128)S(1)}, bf16[512,2048]{1,0:T(8,128)(2,1)S(1)}, bf16[1024,2048]{1,0:T(8,128)(2,1)S(1)}) custom-call(bf16[2048,8192]{1,0:T(8,128)(2,1)} %refs_0_.7, bf16[48,2048]{1,0:T(8,128)(2,1)S(1)} %shard_map.39.refs_1_, bf16[1024,2048]{1,0:T(8,128)(2,1)S(1)} %get-tuple-element.37.refs_0_.refs_2_, ...), custom_call_target="tpu_custom_call" | custom-call | flops 402653184 | bytes 14680064 | tf_op jit(solution)/shard_map/pallas_call | solution.py:107
  18.6 0.5 collective-permute-start.1
  19.0 0.1 collective-permute-done.3.refs_1_
  19.1 2.9 %shard_map.41 = (f32[48,2048]{1,0:T(8,128)S(1)}, bf16[1024,2048]{1,0:T(8,128)(2,1)S(1)}, bf16[512,2048]{1,0:T(8,128)(2,1)S(1)}) custom-call(bf16[2048,8192]{1,0:T(8,128)(2,1)} %refs_0_.7, bf16[48,2048]{1,0:T(8,128)(2,1)S(1)} %collective-permute-done.3.refs_1_, bf16[1024,2048]{1,0:T(8,128)(2,1)S(1)} %get-tuple-element.42.refs_2_, ...), custom_call_target="tpu_custom_call" | custom-call | flops 402653184 | bytes 14680064 | tf_op jit(solution)/shard_map/pallas_call | solution.py:107
  22.1 2.9 %shard_map.42 = (f32[48,2048]{1,0:T(8,128)S(1)}, bf16[512,2048]{1,0:T(8,128)(2,1)S(1)}, bf16[1024,2048]{1,0:T(8,128)(2,1)S(1)}) custom-call(bf16[2048,8192]{1,0:T(8,128)(2,1)} %refs_0_.7, bf16[48,2048]{1,0:T(8,128)(2,1)S(1)} %collective-permute-done.2.refs_1_, bf16[1024,2048]{1,0:T(8,128)(2,1)S(1)} %get-tuple-element.41.refs_2_, ...), custom_call_target="tpu_custom_call" | custom-call | flops 402653184 | bytes 14680064 | tf_op jit(solution)/shard_map/pallas_call | solution.py:107
  25.0 0.2 collective-permute-done.1.refs_0_
  25.2 2.6 %shard_map.43 = f32[48,2048]{1,0:T(8,128)S(1)} custom-call(bf16[48,2048]{1,0:T(8,128)(2,1)S(1)} %collective-permute-done.1.refs_0_, bf16[512,2048]{1,0:T(8,128)(2,1)S(1)} %get-tuple-element.49.refs_1_, bf16[512,2048]{1,0:T(8,128)(2,1)S(1)} %get-tuple-element.50.refs_2_, bf16[1024,2048]{1,0:T(8,128)(2,1)S(1)} %get-tuple-element.51.refs_3_, ...), custom_call_target="tpu_custom_call" | custom-call | flops 402653184 | bytes 8388608 | tf_op jit(solution)/shard_map/pallas_call | solution.py:107
  27.9 0.1 collective-permute-start.4
  27.9 1.7 %collective-permute-done.4 = f32[48,2048]{1,0:T(8,128)S(1)} collective-permute-done((f32[48,2048]{1,0:T(8,128)S(1)}, f32[48,2048]{1,0:T(8,128)S(1)}, u32[]{:S(2)}, u32[]{:S(2)}) %collective-permute-start.4) | collective-permute-done | bytes 393248 | tf_op jit(solution)/shard_map/ppermute | solution.py:241
  29.7 1.8 %collective-permute-start.5 = (bf16[48,2048]{1,0:T(8,128)(2,1)S(1)}, bf16[48,2048]{1,0:T(8,128)(2,1)S(1)}, u32[]{:S(2)}, u32[]{:S(2)}) collective-permute-start(bf16[48,2048]{1,0:T(8,128)(2,1)S(1)} %add_convert_fusion.mine_ref), channel_id=1, source_target_pairs={{0,8},{1,6},{2,10},{3,4},{4,12},{5,2},{6,14},{7,0},{8,15},{9,1},{1... | collective-permute-start | bytes 589832 | tf_op jit(solution)/shard_map/ppermute | solution.py:241
  31.5 4.0 %collective-permute-start.8 = (bf16[48,2048]{1,0:T(8,128)(2,1)S(1)}, bf16[48,2048]{1,0:T(8,128)(2,1)S(1)}, u32[]{:S(2)}, u32[]{:S(2)}) collective-permute-start(bf16[48,2048]{1,0:T(8,128)(2,1)S(1)} %add_convert_fusion.mine_ref), channel_id=1, source_target_pairs={{0,14},{2,12},{4,10},{6,8},{9,7},{11,5},{13,3},{15,1},{16,30},{18,... | collective-permute-start | bytes 589832 | tf_op jit(solution)/shard_map/ppermute | solution.py:241
  35.5 2.3 %collective-permute-done.5.other_ref.mine_ref = bf16[48,2048]{1,0:T(8,128)(2,1)S(1)} collective-permute-done((bf16[48,2048]{1,0:T(8,128)(2,1)S(1)}, bf16[48,2048]{1,0:T(8,128)(2,1)S(1)}, u32[]{:S(2)}, u32[]{:S(2)}) %collective-permute-start.5) | collective-permute-done | bytes 196640 | tf_op jit(solution)/shard_map/ppermute | solution.py:241
  37.9 1.3 %collective-permute-start.7 = (bf16[48,2048]{1,0:T(8,128)(2,1)S(1)}, bf16[48,2048]{1,0:T(8,128)(2,1)S(1)}, u32[]{:S(2)}, u32[]{:S(2)}) collective-permute-start(bf16[48,2048]{1,0:T(8,128)(2,1)S(1)} %shard_map.44.refs_0_), channel_id=1, source_target_pairs={{0,2},{1,3},{2,0},{3,1},{4,6},{5,7},{6,4},{7,5},{8,10},{9,11},{10,... | collective-permute-start | bytes 589832 | tf_op jit(solution)/shard_map/ppermute | solution.py:241
  39.1 2.6 %collective-permute-start.6 = (bf16[48,2048]{1,0:T(8,128)(2,1)S(1)}, bf16[48,2048]{1,0:T(8,128)(2,1)S(1)}, u32[]{:S(2)}, u32[]{:S(2)}) collective-permute-start(bf16[48,2048]{1,0:T(8,128)(2,1)S(1)} %shard_map.44.refs_0_), channel_id=1, source_target_pairs={{0,4},{1,5},{2,6},{3,7},{4,0},{5,1},{6,2},{7,3},{8,12},{9,13},{10,... | collective-permute-start | bytes 589832 | tf_op jit(solution)/shard_map/ppermute | solution.py:241
  41.7 0.7 %collective-permute-start.10 = (bf16[48,2048]{1,0:T(8,128)(2,1)S(1)}, bf16[48,2048]{1,0:T(8,128)(2,1)S(1)}, u32[]{:S(2)}, u32[]{:S(2)}) collective-permute-start(bf16[48,2048]{1,0:T(8,128)(2,1)S(1)} %shard_map.44.refs_0_), channel_id=1, source_target_pairs={{0,16},{1,17},{2,18},{3,19},{4,20},{5,21},{6,22},{7,23},{8,24},{9,... | collective-permute-start | bytes 589832 | tf_op jit(solution)/shard_map/ppermute | solution.py:241
  42.5 3.1 %collective-permute-done.7.refs_0_.refs_2_ = bf16[48,2048]{1,0:T(8,128)(2,1)S(1)} collective-permute-done((bf16[48,2048]{1,0:T(8,128)(2,1)S(1)}, bf16[48,2048]{1,0:T(8,128)(2,1)S(1)}, u32[]{:S(2)}, u32[]{:S(2)}) %collective-permute-start.7) | collective-permute-done | bytes 196640 | tf_op jit(solution)/shard_map/ppermute | solution.py:241
  45.6 0.5 shard_map.46.refs_2_
  46.1 0.3 shard_map.47
  46.4 0.8 %collective-permute-start.11 = (f32[48,128]{1,0:T(8,128)S(1)}, f32[48,128]{1,0:T(8,128)S(1)}, u32[]{:S(2)}, u32[]{:S(2)}) collective-permute-start(f32[48,128]{1,0:T(8,128)S(1)} %shard_map.47), channel_id=1, source_target_pairs={{0,16},{1,17},{2,18},{3,19},{4,20},{5,21},{6,22},{7,23},{8,24},{9,... | collective-permute-start | bytes 73736 | tf_op jit(solution)/shard_map/ppermute | solution.py:241
  47.2 0.2 collective-permute-done.10.refs_0_
  47.4 0.3 shard_map.49.theirs_ref
  47.7 0.9 %shard_map.48.mine_ref = f32[48,128]{1,0:T(8,128)S(1)} custom-call(bf16[48,2048]{1,0:T(8,128)(2,1)S(1)} %shard_map.44.refs_0_, bf16[48,2048]{1,0:T(8,128)(2,1)S(1)} %collective-permute-done.6.refs_0_.refs_1_, bf16[48,2048]{1,0:T(8,128)(2,1)S(1)} %collective-permute-done.7.refs_0_.refs_2_, bf16[48,2048]{1,0:T(8,128)(2,1)S(1)} %shard_map.45.refs_1_.refs_3_, ...), custom_call_target="tpu_custom_call" | custom-call | flops 100663296 | bytes 2097152 | tf_op jit(solution)/shard_map/pallas_call | solution.py:140
  48.5 1.7 %collective-permute-done.11.other_ref = f32[48,128]{1,0:T(8,128)S(1)} collective-permute-done((f32[48,128]{1,0:T(8,128)S(1)}, f32[48,128]{1,0:T(8,128)S(1)}, u32[]{:S(2)}, u32[]{:S(2)}) %collective-permute-start.11) | collective-permute-done | bytes 24608 | tf_op jit(solution)/shard_map/ppermute | solution.py:241
  50.3 0.1 collective-permute-start.12
  50.4 1.2 %collective-permute-done.12 = f32[48,128]{1,0:T(8,128)S(1)} collective-permute-done((f32[48,128]{1,0:T(8,128)S(1)}, f32[48,128]{1,0:T(8,128)S(1)}, u32[]{:S(2)}, u32[]{:S(2)}) %collective-permute-start.12) | collective-permute-done | bytes 24608 | tf_op jit(solution)/shard_map/ppermute | solution.py:241
  51.6 0.6 %add.11 = f32[48,128]{1,0:T(8,128)} add(f32[48,128]{1,0:T(8,128)S(1)} %get-tuple-element.61, f32[48,128]{1,0:T(8,128)S(1)} %collective-permute-done.12) | non-fusion elementwise | flops 6144 | bytes 73728 | tf_op jit(solution)/shard_map/add | solution.py:314
  (17 shorter events, 0.2 us)
Async XLA Ops:
  0.0 1.5 %copy-start = (bf16[96,2048]{1,0:T(8,128)(2,1)S(1)}, bf16[96,2048]{1,0:T(8,128)(2,1)}, u32[]{:S(2)}) copy-start(bf16[96,2048]{1,0:T(8,128)(2,1)} %param.3) | copy-start | bytes 1179652
  1.5 11.0 %collective-permute-start = (bf16[48,2048]{1,0:T(8,128)(2,1)S(1)}, bf16[48,2048]{1,0:T(8,128)(2,1)S(1)}, u32[]{:S(2)}, u32[]{:S(2)}) collective-permute-start(bf16[48,2048]{1,0:T(8,128)(2,1)S(1)} %constant_dynamic-slice_fusion.mine_ref), channel_id=1, source_target_pairs={{0,8},{1,6},{2,10},{3,4},{4,12},{5,2},{6,14},{7,0},{8,15},{9,1},{1... | collective-permute-start | bytes 589832 | tf_op jit(solution)/shard_map/ppermute | solution.py:241
  5.6 40.0 %collective-permute-start.9 = (bf16[128,6144]{1,0:T(8,128)(2,1)S(1)}, bf16[128,6144]{1,0:T(8,128)(2,1)S(1)}, u32[]{:S(2)}, u32[]{:S(2)}) collective-permute-start(bf16[128,6144]{1,0:T(8,128)(2,1)S(1)} %shard_map.37), channel_id=1, source_target_pairs={{0,16},{1,17},{2,18},{3,19},{4,20},{5,21},{6,22},{7,23},{8,24},{9,... | collective-permute-start | bytes 4718600 | tf_op jit(solution)/shard_map/ppermute | solution.py:241
  12.5 6.6 %collective-permute-start.3 = (bf16[48,2048]{1,0:T(8,128)(2,1)S(1)}, bf16[48,2048]{1,0:T(8,128)(2,1)S(1)}, u32[]{:S(2)}, u32[]{:S(2)}) collective-permute-start(bf16[48,2048]{1,0:T(8,128)(2,1)S(1)} %shard_map.39.refs_1_), channel_id=1, source_target_pairs={{0,4},{1,5},{2,6},{3,7},{4,0},{5,1},{6,2},{7,3},{8,12},{9,13},{10,... | collective-permute-start | bytes 589832 | tf_op jit(solution)/shard_map/ppermute | solution.py:241
  14.2 7.9 %collective-permute-start.2 = (bf16[48,2048]{1,0:T(8,128)(2,1)S(1)}, bf16[48,2048]{1,0:T(8,128)(2,1)S(1)}, u32[]{:S(2)}, u32[]{:S(2)}) collective-permute-start(bf16[48,2048]{1,0:T(8,128)(2,1)S(1)} %shard_map.39.refs_1_), channel_id=1, source_target_pairs={{0,2},{1,3},{2,0},{3,1},{4,6},{5,7},{6,4},{7,5},{8,10},{9,11},{10,... | collective-permute-start | bytes 589832 | tf_op jit(solution)/shard_map/ppermute | solution.py:241
  18.6 6.6 %collective-permute-start.1 = (bf16[48,2048]{1,0:T(8,128)(2,1)S(1)}, bf16[48,2048]{1,0:T(8,128)(2,1)S(1)}, u32[]{:S(2)}, u32[]{:S(2)}) collective-permute-start(bf16[48,2048]{1,0:T(8,128)(2,1)S(1)} %shard_map.39.refs_1_), channel_id=1, source_target_pairs={{0,6},{1,7},{2,4},{3,5},{4,2},{5,3},{6,0},{7,1},{8,14},{9,15},{10,... | collective-permute-start | bytes 589832 | tf_op jit(solution)/shard_map/ppermute | solution.py:241
  27.8 19.5 %copy-start.2 = (bf16[128,8192]{1,0:T(8,128)(2,1)S(1)}, bf16[128,8192]{1,0:T(8,128)(2,1)}, u32[]{:S(2)}) copy-start(bf16[128,8192]{1,0:T(8,128)(2,1)} %refs_1_.1) | copy-start | bytes 6291460
  27.9 1.8 %collective-permute-start.4 = (f32[48,2048]{1,0:T(8,128)S(1)}, f32[48,2048]{1,0:T(8,128)S(1)}, u32[]{:S(2)}, u32[]{:S(2)}) collective-permute-start(f32[48,2048]{1,0:T(8,128)S(1)} %shard_map.43), channel_id=1, source_target_pairs={{0,1},{1,0},{2,3},{3,2},{4,5},{5,4},{6,7},{7,6},{8,9},{9,8},{10,11... | collective-permute-start | bytes 1179656 | tf_op jit(solution)/shard_map/ppermute | solution.py:241
  29.7 8.2 %collective-permute-start.5 = (bf16[48,2048]{1,0:T(8,128)(2,1)S(1)}, bf16[48,2048]{1,0:T(8,128)(2,1)S(1)}, u32[]{:S(2)}, u32[]{:S(2)}) collective-permute-start(bf16[48,2048]{1,0:T(8,128)(2,1)S(1)} %add_convert_fusion.mine_ref), channel_id=1, source_target_pairs={{0,8},{1,6},{2,10},{3,4},{4,12},{5,2},{6,14},{7,0},{8,15},{9,1},{1... | collective-permute-start | bytes 589832 | tf_op jit(solution)/shard_map/ppermute | solution.py:241
  31.5 11.0 %collective-permute-start.8 = (bf16[48,2048]{1,0:T(8,128)(2,1)S(1)}, bf16[48,2048]{1,0:T(8,128)(2,1)S(1)}, u32[]{:S(2)}, u32[]{:S(2)}) collective-permute-start(bf16[48,2048]{1,0:T(8,128)(2,1)S(1)} %add_convert_fusion.mine_ref), channel_id=1, source_target_pairs={{0,14},{2,12},{4,10},{6,8},{9,7},{11,5},{13,3},{15,1},{16,30},{18,... | collective-permute-start | bytes 589832 | tf_op jit(solution)/shard_map/ppermute | solution.py:241
  37.9 7.7 %collective-permute-start.7 = (bf16[48,2048]{1,0:T(8,128)(2,1)S(1)}, bf16[48,2048]{1,0:T(8,128)(2,1)S(1)}, u32[]{:S(2)}, u32[]{:S(2)}) collective-permute-start(bf16[48,2048]{1,0:T(8,128)(2,1)S(1)} %shard_map.44.refs_0_), channel_id=1, source_target_pairs={{0,2},{1,3},{2,0},{3,1},{4,6},{5,7},{6,4},{7,5},{8,10},{9,11},{10,... | collective-permute-start | bytes 589832 | tf_op jit(solution)/shard_map/ppermute | solution.py:241
  39.1 7.0 %collective-permute-start.6 = (bf16[48,2048]{1,0:T(8,128)(2,1)S(1)}, bf16[48,2048]{1,0:T(8,128)(2,1)S(1)}, u32[]{:S(2)}, u32[]{:S(2)}) collective-permute-start(bf16[48,2048]{1,0:T(8,128)(2,1)S(1)} %shard_map.44.refs_0_), channel_id=1, source_target_pairs={{0,4},{1,5},{2,6},{3,7},{4,0},{5,1},{6,2},{7,3},{8,12},{9,13},{10,... | collective-permute-start | bytes 589832 | tf_op jit(solution)/shard_map/ppermute | solution.py:241
  41.7 5.7 %collective-permute-start.10 = (bf16[48,2048]{1,0:T(8,128)(2,1)S(1)}, bf16[48,2048]{1,0:T(8,128)(2,1)S(1)}, u32[]{:S(2)}, u32[]{:S(2)}) collective-permute-start(bf16[48,2048]{1,0:T(8,128)(2,1)S(1)} %shard_map.44.refs_0_), channel_id=1, source_target_pairs={{0,16},{1,17},{2,18},{3,19},{4,20},{5,21},{6,22},{7,23},{8,24},{9,... | collective-permute-start | bytes 589832 | tf_op jit(solution)/shard_map/ppermute | solution.py:241
  45.6 6.6 %copy-start.1 = (bf16[96,2048]{1,0:T(8,128)(2,1)S(1)}, bf16[96,2048]{1,0:T(8,128)(2,1)}, u32[]{:S(2)}) copy-start(bf16[96,2048]{1,0:T(8,128)(2,1)} %param.3) | copy-start | bytes 1179652
  46.4 3.9 %collective-permute-start.11 = (f32[48,128]{1,0:T(8,128)S(1)}, f32[48,128]{1,0:T(8,128)S(1)}, u32[]{:S(2)}, u32[]{:S(2)}) collective-permute-start(f32[48,128]{1,0:T(8,128)S(1)} %shard_map.47), channel_id=1, source_target_pairs={{0,16},{1,17},{2,18},{3,19},{4,20},{5,21},{6,22},{7,23},{8,24},{9,... | collective-permute-start | bytes 73736 | tf_op jit(solution)/shard_map/ppermute | solution.py:241
  50.3 1.3 %collective-permute-start.12 = (f32[48,128]{1,0:T(8,128)S(1)}, f32[48,128]{1,0:T(8,128)S(1)}, u32[]{:S(2)}, u32[]{:S(2)}) collective-permute-start(f32[48,128]{1,0:T(8,128)S(1)} %get-tuple-element.62), channel_id=1, source_target_pairs={{0,1},{1,0},{2,3},{3,2},{4,5},{5,4},{6,7},{7,6},{8,9},{9,8},{10,11... | collective-permute-start | bytes 73736 | tf_op jit(solution)/shard_map/ppermute | solution.py:241

commit v29 on v27

--- a/solution.py
+++ b/solution.py
@@ -63,7 +63,7 @@
     return lax.dot_general(chunk_ref[...], fisher, NT, preferred_element_type=jnp.float32)
 
 
-def fisher_kernel(dims, n_parts, has_base, fetch, *refs):
+def fisher_kernel(dims, n_parts, has_base, fetch, first, *refs):
     if fetch:
         column = Place(*dims).column
         fisher_ref, *refs = refs
@@ -88,24 +88,25 @@
                 rows = part_ref.shape[0]
                 step = rows // loops
                 start = pl.multiple_of(i * step, step)
-                columns = pl.ds(before + start, step)
                 term = times(chunk_ref, part_ref[pl.ds(start, step), :])
-                outs[0][:, columns] = term + base_ref[:, columns] if has_base else term
+                if has_base:
+                    term = term + base_ref[:, pl.ds(first + before + start, step)]
+                outs[0][:, pl.ds(before + start, step)] = term
                 before += rows
 
     for copy in copies:
         copy.wait()
 
 
-def fisher_step(fisher, dims, width, fetch, chunk=None, parts=(), base=None):
-    total = fisher.shape[0]
+def fisher_step(fisher, dims, width, fetch, chunk=None, parts=(), base=None, first=0):
+    total = sum(part.shape[0] for part in parts)
     ins = [] if chunk is None else [chunk, *parts]
     has_base = base is not None
     out_shape = [] if chunk is None else [jax.ShapeDtypeStruct((chunk.shape[0], total), jnp.float32)]
     out_shape += [jax.ShapeDtypeStruct((rows, width), fisher.dtype) for _, _, rows in fetch]
     fetched = sum(rows for _, _, rows in fetch)
     return pl.pallas_call(
-        functools.partial(fisher_kernel, dims, len(parts), has_base, fetch),
+        functools.partial(fisher_kernel, dims, len(parts), has_base, fetch, first),
         out_shape=out_shape,
         in_specs=[HBM] * bool(fetch) + [VMEM] * (len(ins) + has_base),
         out_specs=[VMEM] * len(out_shape),
@@ -223,6 +224,22 @@
     )(mine, other, theirs)
 
 
+def join_kernel(low_ref, high_ref, other_high_ref, out_ref):
+    width = low_ref.shape[1]
+    out_ref[:, :width] = low_ref[...].astype(out_ref.dtype)
+    out_ref[:, width:] = (high_ref[...] + other_high_ref[...]).astype(out_ref.dtype)
+
+
+def join(low, high, other_high):
+    return pl.pallas_call(
+        join_kernel,
+        out_shape=jax.ShapeDtypeStruct((low.shape[0], 2 * low.shape[1]), jnp.bfloat16),
+        in_specs=[VMEM] * 3,
+        out_specs=VMEM,
+        compiler_params=limit(2),
+    )(low, high, other_high)
+
+
 def per_device_quad(nz, nx, ny, queries, inverse_fisher, stored_grads):
     nex, dims = nz * nx, (nz, nx)
     near = nz // 2
@@ -296,8 +313,13 @@
     total0, b2, c0 = step(((1, half + quarter, quarter), (2, 0, half)), q0, (a0, a1))
     total, c1, d0 = step(((2, half, half), (3, 0, quarter)), q1, (b0, b1, b2), total0)
     total, d1, d2 = step(((3, quarter, quarter), (3, half, half)), q2, (c0, c1), total)
-    (total,) = step((), last(total0, total), (d0, d1, d2), total)
-    panel = (total + swap_core(total)).astype(jnp.bfloat16)
+    q3 = last(total0, total)
+    (low,) = step((), q3, (d0, d1), total)
+    other_low = swap_core(low)
+    after_low, _ = lax.optimization_barrier((total, low))
+    (high,) = step((), q3, (d2,), after_low, half)
+    low, high = lax.optimization_barrier((low + other_low, high))
+    panel = join(low, high, swap_core(high))
 
     p0, p1, p2, last = gather(panel, True)
     swapped = swap_y(p0)

time: 51.8 us -> 52.8 us (1.019)
  starting transfers between devices: 20.5 us -> 22.2 us
  waiting for transfers between devices: 10.2 us -> 9.25 us
    ppermute x13 -> x14, starting transfers between devices: 20.5 us -> 22.2 us  [move(): return lax.ppermute(value, AXES, pairs)]
    ppermute x13 -> x14, waiting for transfers between devices: 10.2 us -> 9.25 us  [move(): return lax.ppermute(value, AXES, pairs)]
    pallas_call x5 -> x6, Pallas kernels: 16.7 us -> 16.9 us  [fisher_step(): pl.pallas_call(functools.partial(fisher_kernel, dims, len(parts), has_bas...]
  transfers between devices with their start and end apart: 13 -> 14, of which waited for: 9 -> 7; matrix products, arithmetic and copies ran while one was open for 0% -> 0% of each run, Pallas kernels for 36% -> 36%
where the time goes in v29:
time: 52.8 us; the launch traced here: 52.6 us
  starting transfers between devices  22.2 us (42%)
  Pallas kernels  20.3 us (38%)
  waiting for transfers between devices  9.25 us (18%)
  other arithmetic  0.64 us (1%)
    ppermute x14, starting transfers between devices, move(): return lax.ppermute(value, AXES, pairs)  22.2 us
    pallas_call x6, Pallas kernels, fisher_step(): pl.pallas_call(functools.partial(fisher_kernel, dims, len(parts), has_bas...  16.9 us
    ppermute x14, waiting for transfers between devices, move(): return lax.ppermute(value, AXES, pairs)  9.25 us
    pallas_call x4, Pallas kernels, score_dot(): pl.pallas_call(functools.partial(score_kernel, dims, order, base is not N...  1.9 us
    pallas_call x1, Pallas kernels, cut(): pl.pallas_call(functools.partial(cut_kernel, dims, order), out_shape=jax....  1.43 us
  transfers between devices with their start and end apart: 14, of which 7 were waited for; matrix products, arithmetic and copies ran while one was open for 0% of the time, Pallas kernels for 36%

profile of v29, /device:TPU:0, one launch (start us, length us, event | category | flops | bytes accessed | tf_op | source)
XLA Modules:
  0.0 52.6 jit_solution(11150919376010028726)
XLA Ops:
  0.0 1.4 %shard_map.37 = bf16[128,6144]{1,0:T(8,128)(2,1)S(1)} custom-call(bf16[128,8192]{1,0:T(8,128)(2,1)} %refs_1_.1), custom_call_target="tpu_custom_call" | custom-call | bytes 1572864 | tf_op jit(solution)/shard_map/pallas_call | solution.py:173
  1.5 3.0 %collective-permute-start.9 = (bf16[128,6144]{1,0:T(8,128)(2,1)S(1)}, bf16[128,6144]{1,0:T(8,128)(2,1)S(1)}, u32[]{:S(2)}, u32[]{:S(2)}) collective-permute-start(bf16[128,6144]{1,0:T(8,128)(2,1)S(1)} %shard_map.37), channel_id=1, source_target_pairs={{0,16},{1,17},{2,18},{3,19},{4,20},{5,21},{6,22},{7,23},{8,24},{9,... | collective-permute-start | bytes 4718600 | tf_op jit(solution)/shard_map/ppermute | solution.py:258
  4.5 2.6 %collective-permute-start = (bf16[48,2048]{1,0:T(8,128)(2,1)S(1)}, bf16[48,2048]{1,0:T(8,128)(2,1)S(1)}, u32[]{:S(2)}, u32[]{:S(2)}) collective-permute-start(bf16[48,2048]{1,0:T(8,128)(2,1)S(1)} %constant_dynamic-slice_fusion.mine_ref), channel_id=1, source_target_pairs={{0,8},{1,6},{2,10},{3,4},{4,12},{5,2},{6,14},{7,0},{8,15},{9,1},{1... | collective-permute-start | bytes 589832 | tf_op jit(solution)/shard_map/ppermute | solution.py:258
  7.1 5.3 %shard_map.38 = (bf16[1024,2048]{1,0:T(8,128)(2,1)S(1)}, bf16[1024,2048]{1,0:T(8,128)(2,1)S(1)}, bf16[1024,2048]{1,0:T(8,128)(2,1)S(1)}, bf16[512,2048]{1,0:T(8,128)(2,1)S(1)}) custom-call(bf16[2048,8192]{1,0:T(8,128)(2,1)} %refs_0_.7), custom_call_target="tpu_custom_call" | custom-call | bytes 14680064 | tf_op jit(solution)/shard_map/pallas_call | solution.py:108
  12.5 1.6 %collective-permute-start.3 = (bf16[48,2048]{1,0:T(8,128)(2,1)S(1)}, bf16[48,2048]{1,0:T(8,128)(2,1)S(1)}, u32[]{:S(2)}, u32[]{:S(2)}) collective-permute-start(bf16[48,2048]{1,0:T(8,128)(2,1)S(1)} %shard_map.39.refs_1_), channel_id=1, source_target_pairs={{0,4},{1,5},{2,6},{3,7},{4,0},{5,1},{6,2},{7,3},{8,12},{9,13},{10,... | collective-permute-start | bytes 589832 | tf_op jit(solution)/shard_map/ppermute | solution.py:258
  14.2 1.5 %collective-permute-start.2 = (bf16[48,2048]{1,0:T(8,128)(2,1)S(1)}, bf16[48,2048]{1,0:T(8,128)(2,1)S(1)}, u32[]{:S(2)}, u32[]{:S(2)}) collective-permute-start(bf16[48,2048]{1,0:T(8,128)(2,1)S(1)} %shard_map.39.refs_1_), channel_id=1, source_target_pairs={{0,2},{1,3},{2,0},{3,1},{4,6},{5,7},{6,4},{7,5},{8,10},{9,11},{10,... | collective-permute-start | bytes 589832 | tf_op jit(solution)/shard_map/ppermute | solution.py:258
  15.7 2.9 %shard_map.40 = (f32[48,2048]{1,0:T(8,128)S(1)}, bf16[512,2048]{1,0:T(8,128)(2,1)S(1)}, bf16[1024,2048]{1,0:T(8,128)(2,1)S(1)}) custom-call(bf16[2048,8192]{1,0:T(8,128)(2,1)} %refs_0_.7, bf16[48,2048]{1,0:T(8,128)(2,1)S(1)} %shard_map.39.refs_1_, bf16[1024,2048]{1,0:T(8,128)(2,1)S(1)} %get-tuple-element.40.refs_0_.refs_2_, ...), custom_call_target="tpu_custom_call" | custom-call | flops 402653184 | bytes 14680064 | tf_op jit(solution)/shard_map/pallas_call | solution.py:108
  18.6 0.5 collective-permute-start.1
  19.0 0.4 collective-permute-done.3.refs_1_
  19.4 2.9 %shard_map.41 = (f32[48,2048]{1,0:T(8,128)S(1)}, bf16[1024,2048]{1,0:T(8,128)(2,1)S(1)}, bf16[512,2048]{1,0:T(8,128)(2,1)S(1)}) custom-call(bf16[2048,8192]{1,0:T(8,128)(2,1)} %refs_0_.7, bf16[48,2048]{1,0:T(8,128)(2,1)S(1)} %collective-permute-done.3.refs_1_, bf16[1024,2048]{1,0:T(8,128)(2,1)S(1)} %get-tuple-element.45.refs_2_, ...), custom_call_target="tpu_custom_call" | custom-call | flops 402653184 | bytes 14680064 | tf_op jit(solution)/shard_map/pallas_call | solution.py:108
  22.3 2.9 %shard_map.42 = (f32[48,2048]{1,0:T(8,128)S(1)}, bf16[512,2048]{1,0:T(8,128)(2,1)S(1)}, bf16[1024,2048]{1,0:T(8,128)(2,1)S(1)}) custom-call(bf16[2048,8192]{1,0:T(8,128)(2,1)} %refs_0_.7, bf16[48,2048]{1,0:T(8,128)(2,1)S(1)} %collective-permute-done.2.refs_1_, bf16[1024,2048]{1,0:T(8,128)(2,1)S(1)} %get-tuple-element.44.refs_2_, ...), custom_call_target="tpu_custom_call" | custom-call | flops 402653184 | bytes 14680064 | tf_op jit(solution)/shard_map/pallas_call | solution.py:108
  25.3 1.4 %shard_map.43 = f32[48,1024]{1,0:T(8,128)S(1)} custom-call(bf16[48,2048]{1,0:T(8,128)(2,1)S(1)} %collective-permute-done.1.refs_0_, bf16[512,2048]{1,0:T(8,128)(2,1)S(1)} %get-tuple-element.52.refs_1_, bf16[512,2048]{1,0:T(8,128)(2,1)S(1)} %get-tuple-element.53.refs_2_, f32[48,2048]{1,0:T(8,128)S(1)} %get-tuple-element.55.refs_3_.refs_2_), custom_call_target="tpu_custom_call" | custom-call | flops 201326592 | bytes 4194304 | tf_op jit(solution)/shard_map/pallas_call | solution.py:108
  26.7 0.1 collective-permute-start.4
  26.8 1.4 %shard_map.44.high_ref = f32[48,1024]{1,0:T(8,128)S(1)} custom-call(bf16[48,2048]{1,0:T(8,128)(2,1)S(1)} %collective-permute-done.1.refs_0_, bf16[1024,2048]{1,0:T(8,128)(2,1)S(1)} %get-tuple-element.54.refs_1_, f32[48,2048]{1,0:T(8,128)S(1)} %get-tuple-element.55.refs_3_.refs_2_), custom_call_target="tpu_custom_call" | custom-call | flops 201326592 | bytes 4194304 | tf_op jit(solution)/shard_map/pallas_call | solution.py:108
  28.2 0.6 %collective-permute-start.5 = (f32[48,1024]{1,0:T(8,128)S(1)}, f32[48,1024]{1,0:T(8,128)S(1)}, u32[]{:S(2)}, u32[]{:S(2)}) collective-permute-start(f32[48,1024]{1,0:T(8,128)S(1)} %shard_map.44.high_ref), channel_id=1, source_target_pairs={{0,1},{1,0},{2,3},{3,2},{4,5},{5,4},{6,7},{7,6},{8,9},{9,8},{10,11... | collective-permute-start | bytes 589832 | tf_op jit(solution)/shard_map/ppermute | solution.py:258
  28.8 1.1 %collective-permute-done.5.other_high_ref = f32[48,1024]{1,0:T(8,128)S(1)} collective-permute-done((f32[48,1024]{1,0:T(8,128)S(1)}, f32[48,1024]{1,0:T(8,128)S(1)}, u32[]{:S(2)}, u32[]{:S(2)}) %collective-permute-start.5) | collective-permute-done | bytes 196640 | tf_op jit(solution)/shard_map/ppermute | solution.py:258
  29.9 3.2 %collective-permute-start.6 = (bf16[48,2048]{1,0:T(8,128)(2,1)S(1)}, bf16[48,2048]{1,0:T(8,128)(2,1)S(1)}, u32[]{:S(2)}, u32[]{:S(2)}) collective-permute-start(bf16[48,2048]{1,0:T(8,128)(2,1)S(1)} %shard_map.45.mine_ref), channel_id=1, source_target_pairs={{0,8},{1,6},{2,10},{3,4},{4,12},{5,2},{6,14},{7,0},{8,15},{9,1},{1... | collective-permute-start | bytes 589832 | tf_op jit(solution)/shard_map/ppermute | solution.py:258
  33.1 4.2 %collective-permute-start.8 = (bf16[48,2048]{1,0:T(8,128)(2,1)S(1)}, bf16[48,2048]{1,0:T(8,128)(2,1)S(1)}, u32[]{:S(2)}, u32[]{:S(2)}) collective-permute-start(bf16[48,2048]{1,0:T(8,128)(2,1)S(1)} %shard_map.45.mine_ref), channel_id=1, source_target_pairs={{0,14},{2,12},{4,10},{6,8},{9,7},{11,5},{13,3},{15,1},{16,30},{18,... | collective-permute-start | bytes 589832 | tf_op jit(solution)/shard_map/ppermute | solution.py:258
  37.4 2.3 %collective-permute-start.7 = (bf16[48,2048]{1,0:T(8,128)(2,1)S(1)}, bf16[48,2048]{1,0:T(8,128)(2,1)S(1)}, u32[]{:S(2)}, u32[]{:S(2)}) collective-permute-start(bf16[48,2048]{1,0:T(8,128)(2,1)S(1)} %shard_map.46.refs_0_), channel_id=1, source_target_pairs={{0,4},{1,5},{2,6},{3,7},{4,0},{5,1},{6,2},{7,3},{8,12},{9,13},{10,... | collective-permute-start | bytes 589832 | tf_op jit(solution)/shard_map/ppermute | solution.py:258
  39.7 1.4 %collective-permute-start.10 = (bf16[48,2048]{1,0:T(8,128)(2,1)S(1)}, bf16[48,2048]{1,0:T(8,128)(2,1)S(1)}, u32[]{:S(2)}, u32[]{:S(2)}) collective-permute-start(bf16[48,2048]{1,0:T(8,128)(2,1)S(1)} %shard_map.46.refs_0_), channel_id=1, source_target_pairs={{0,2},{1,3},{2,0},{3,1},{4,6},{5,7},{6,4},{7,5},{8,10},{9,11},{10,... | collective-permute-start | bytes 589832 | tf_op jit(solution)/shard_map/ppermute | solution.py:258
  41.1 0.5 collective-permute-start.11
  41.6 0.6 %collective-permute-done.8.other_ref = bf16[48,2048]{1,0:T(8,128)(2,1)S(1)} collective-permute-done((bf16[48,2048]{1,0:T(8,128)(2,1)S(1)}, bf16[48,2048]{1,0:T(8,128)(2,1)S(1)}, u32[]{:S(2)}, u32[]{:S(2)}) %collective-permute-start.8) | collective-permute-done | bytes 196640 | tf_op jit(solution)/shard_map/ppermute | solution.py:258
  42.2 3.5 %collective-permute-done.7.refs_0_.refs_1_ = bf16[48,2048]{1,0:T(8,128)(2,1)S(1)} collective-permute-done((bf16[48,2048]{1,0:T(8,128)(2,1)S(1)}, bf16[48,2048]{1,0:T(8,128)(2,1)S(1)}, u32[]{:S(2)}, u32[]{:S(2)}) %collective-permute-start.7) | collective-permute-done | bytes 196640 | tf_op jit(solution)/shard_map/ppermute | solution.py:258
  45.7 0.5 shard_map.48.refs_2_
  46.2 0.4 collective-permute-done.10.refs_0_.refs_2_
  46.6 0.3 shard_map.49
  46.9 0.6 %collective-permute-start.12 = (f32[48,128]{1,0:T(8,128)S(1)}, f32[48,128]{1,0:T(8,128)S(1)}, u32[]{:S(2)}, u32[]{:S(2)}) collective-permute-start(f32[48,128]{1,0:T(8,128)S(1)} %shard_map.49), channel_id=1, source_target_pairs={{0,16},{1,17},{2,18},{3,19},{4,20},{5,21},{6,22},{7,23},{8,24},{9,... | collective-permute-start | bytes 73736 | tf_op jit(solution)/shard_map/ppermute | solution.py:258
  47.4 0.3 shard_map.51.theirs_ref
  47.7 0.8 %shard_map.50.mine_ref = f32[48,128]{1,0:T(8,128)S(1)} custom-call(bf16[48,2048]{1,0:T(8,128)(2,1)S(1)} %shard_map.46.refs_0_, bf16[48,2048]{1,0:T(8,128)(2,1)S(1)} %collective-permute-done.7.refs_0_.refs_1_, bf16[48,2048]{1,0:T(8,128)(2,1)S(1)} %collective-permute-done.10.refs_0_.refs_2_, bf16[48,2048]{1,0:T(8,128)(2,1)S(1)} %shard_map.47.refs_1_.refs_3_, ...), custom_call_target="tpu_custom_call" | custom-call | flops 100663296 | bytes 2097152 | tf_op jit(solution)/shard_map/pallas_call | solution.py:141
  48.6 2.1 %collective-permute-done.12.other_ref = f32[48,128]{1,0:T(8,128)S(1)} collective-permute-done((f32[48,128]{1,0:T(8,128)S(1)}, f32[48,128]{1,0:T(8,128)S(1)}, u32[]{:S(2)}, u32[]{:S(2)}) %collective-permute-start.12) | collective-permute-done | bytes 24608 | tf_op jit(solution)/shard_map/ppermute | solution.py:258
  50.8 1.2 %collective-permute-done.13 = f32[48,128]{1,0:T(8,128)S(1)} collective-permute-done((f32[48,128]{1,0:T(8,128)S(1)}, f32[48,128]{1,0:T(8,128)S(1)}, u32[]{:S(2)}, u32[]{:S(2)}) %collective-permute-start.13) | collective-permute-done | bytes 24608 | tf_op jit(solution)/shard_map/ppermute | solution.py:258
  52.0 0.6 %add.11 = f32[48,128]{1,0:T(8,128)} add(f32[48,128]{1,0:T(8,128)S(1)} %get-tuple-element.67, f32[48,128]{1,0:T(8,128)S(1)} %collective-permute-done.13) | non-fusion elementwise | flops 6144 | bytes 73728 | tf_op jit(solution)/shard_map/add | solution.py:336
  (21 shorter events, 0.3 us)
Async XLA Ops:
  0.0 1.5 %copy-start = (bf16[96,2048]{1,0:T(8,128)(2,1)S(1)}, bf16[96,2048]{1,0:T(8,128)(2,1)}, u32[]{:S(2)}) copy-start(bf16[96,2048]{1,0:T(8,128)(2,1)} %param.3) | copy-start | bytes 1179652
  1.5 44.2 %collective-permute-start.9 = (bf16[128,6144]{1,0:T(8,128)(2,1)S(1)}, bf16[128,6144]{1,0:T(8,128)(2,1)S(1)}, u32[]{:S(2)}, u32[]{:S(2)}) collective-permute-start(bf16[128,6144]{1,0:T(8,128)(2,1)S(1)} %shard_map.37), channel_id=1, source_target_pairs={{0,16},{1,17},{2,18},{3,19},{4,20},{5,21},{6,22},{7,23},{8,24},{9,... | collective-permute-start | bytes 4718600 | tf_op jit(solution)/shard_map/ppermute | solution.py:258
  4.5 7.9 %collective-permute-start = (bf16[48,2048]{1,0:T(8,128)(2,1)S(1)}, bf16[48,2048]{1,0:T(8,128)(2,1)S(1)}, u32[]{:S(2)}, u32[]{:S(2)}) collective-permute-start(bf16[48,2048]{1,0:T(8,128)(2,1)S(1)} %constant_dynamic-slice_fusion.mine_ref), channel_id=1, source_target_pairs={{0,8},{1,6},{2,10},{3,4},{4,12},{5,2},{6,14},{7,0},{8,15},{9,1},{1... | collective-permute-start | bytes 589832 | tf_op jit(solution)/shard_map/ppermute | solution.py:258
  12.5 6.9 %collective-permute-start.3 = (bf16[48,2048]{1,0:T(8,128)(2,1)S(1)}, bf16[48,2048]{1,0:T(8,128)(2,1)S(1)}, u32[]{:S(2)}, u32[]{:S(2)}) collective-permute-start(bf16[48,2048]{1,0:T(8,128)(2,1)S(1)} %shard_map.39.refs_1_), channel_id=1, source_target_pairs={{0,4},{1,5},{2,6},{3,7},{4,0},{5,1},{6,2},{7,3},{8,12},{9,13},{10,... | collective-permute-start | bytes 589832 | tf_op jit(solution)/shard_map/ppermute | solution.py:258
  14.2 8.2 %collective-permute-start.2 = (bf16[48,2048]{1,0:T(8,128)(2,1)S(1)}, bf16[48,2048]{1,0:T(8,128)(2,1)S(1)}, u32[]{:S(2)}, u32[]{:S(2)}) collective-permute-start(bf16[48,2048]{1,0:T(8,128)(2,1)S(1)} %shard_map.39.refs_1_), channel_id=1, source_target_pairs={{0,2},{1,3},{2,0},{3,1},{4,6},{5,7},{6,4},{7,5},{8,10},{9,11},{10,... | collective-permute-start | bytes 589832 | tf_op jit(solution)/shard_map/ppermute | solution.py:258
  18.6 6.7 %collective-permute-start.1 = (bf16[48,2048]{1,0:T(8,128)(2,1)S(1)}, bf16[48,2048]{1,0:T(8,128)(2,1)S(1)}, u32[]{:S(2)}, u32[]{:S(2)}) collective-permute-start(bf16[48,2048]{1,0:T(8,128)(2,1)S(1)} %shard_map.39.refs_1_), channel_id=1, source_target_pairs={{0,6},{1,7},{2,4},{3,5},{4,2},{5,3},{6,0},{7,1},{8,14},{9,15},{10,... | collective-permute-start | bytes 589832 | tf_op jit(solution)/shard_map/ppermute | solution.py:258
  26.7 1.5 %collective-permute-start.4 = (f32[48,1024]{1,0:T(8,128)S(1)}, f32[48,1024]{1,0:T(8,128)S(1)}, u32[]{:S(2)}, u32[]{:S(2)}) collective-permute-start(f32[48,1024]{1,0:T(8,128)S(1)} %shard_map.43), channel_id=1, source_target_pairs={{0,1},{1,0},{2,3},{3,2},{4,5},{5,4},{6,7},{7,6},{8,9},{9,8},{10,11... | collective-permute-start | bytes 589832 | tf_op jit(solution)/shard_map/ppermute | solution.py:258
  28.2 19.3 %copy-start.2 = (bf16[128,8192]{1,0:T(8,128)(2,1)S(1)}, bf16[128,8192]{1,0:T(8,128)(2,1)}, u32[]{:S(2)}) copy-start(bf16[128,8192]{1,0:T(8,128)(2,1)} %refs_1_.1) | copy-start | bytes 6291460
  28.2 1.6 %collective-permute-start.5 = (f32[48,1024]{1,0:T(8,128)S(1)}, f32[48,1024]{1,0:T(8,128)S(1)}, u32[]{:S(2)}, u32[]{:S(2)}) collective-permute-start(f32[48,1024]{1,0:T(8,128)S(1)} %shard_map.44.high_ref), channel_id=1, source_target_pairs={{0,1},{1,0},{2,3},{3,2},{4,5},{5,4},{6,7},{7,6},{8,9},{9,8},{10,11... | collective-permute-start | bytes 589832 | tf_op jit(solution)/shard_map/ppermute | solution.py:258
  29.9 7.5 %collective-permute-start.6 = (bf16[48,2048]{1,0:T(8,128)(2,1)S(1)}, bf16[48,2048]{1,0:T(8,128)(2,1)S(1)}, u32[]{:S(2)}, u32[]{:S(2)}) collective-permute-start(bf16[48,2048]{1,0:T(8,128)(2,1)S(1)} %shard_map.45.mine_ref), channel_id=1, source_target_pairs={{0,8},{1,6},{2,10},{3,4},{4,12},{5,2},{6,14},{7,0},{8,15},{9,1},{1... | collective-permute-start | bytes 589832 | tf_op jit(solution)/shard_map/ppermute | solution.py:258
  33.1 9.1 %collective-permute-start.8 = (bf16[48,2048]{1,0:T(8,128)(2,1)S(1)}, bf16[48,2048]{1,0:T(8,128)(2,1)S(1)}, u32[]{:S(2)}, u32[]{:S(2)}) collective-permute-start(bf16[48,2048]{1,0:T(8,128)(2,1)S(1)} %shard_map.45.mine_ref), channel_id=1, source_target_pairs={{0,14},{2,12},{4,10},{6,8},{9,7},{11,5},{13,3},{15,1},{16,30},{18,... | collective-permute-start | bytes 589832 | tf_op jit(solution)/shard_map/ppermute | solution.py:258
  37.4 8.3 %collective-permute-start.7 = (bf16[48,2048]{1,0:T(8,128)(2,1)S(1)}, bf16[48,2048]{1,0:T(8,128)(2,1)S(1)}, u32[]{:S(2)}, u32[]{:S(2)}) collective-permute-start(bf16[48,2048]{1,0:T(8,128)(2,1)S(1)} %shard_map.46.refs_0_), channel_id=1, source_target_pairs={{0,4},{1,5},{2,6},{3,7},{4,0},{5,1},{6,2},{7,3},{8,12},{9,13},{10,... | collective-permute-start | bytes 589832 | tf_op jit(solution)/shard_map/ppermute | solution.py:258
  39.7 6.8 %collective-permute-start.10 = (bf16[48,2048]{1,0:T(8,128)(2,1)S(1)}, bf16[48,2048]{1,0:T(8,128)(2,1)S(1)}, u32[]{:S(2)}, u32[]{:S(2)}) collective-permute-start(bf16[48,2048]{1,0:T(8,128)(2,1)S(1)} %shard_map.46.refs_0_), channel_id=1, source_target_pairs={{0,2},{1,3},{2,0},{3,1},{4,6},{5,7},{6,4},{7,5},{8,10},{9,11},{10,... | collective-permute-start | bytes 589832 | tf_op jit(solution)/shard_map/ppermute | solution.py:258
  41.1 6.3 %collective-permute-start.11 = (bf16[48,2048]{1,0:T(8,128)(2,1)S(1)}, bf16[48,2048]{1,0:T(8,128)(2,1)S(1)}, u32[]{:S(2)}, u32[]{:S(2)}) collective-permute-start(bf16[48,2048]{1,0:T(8,128)(2,1)S(1)} %shard_map.46.refs_0_), channel_id=1, source_target_pairs={{0,16},{1,17},{2,18},{3,19},{4,20},{5,21},{6,22},{7,23},{8,24},{9,... | collective-permute-start | bytes 589832 | tf_op jit(solution)/shard_map/ppermute | solution.py:258
  45.7 6.9 %copy-start.1 = (bf16[96,2048]{1,0:T(8,128)(2,1)S(1)}, bf16[96,2048]{1,0:T(8,128)(2,1)}, u32[]{:S(2)}) copy-start(bf16[96,2048]{1,0:T(8,128)(2,1)} %param.3) | copy-start | bytes 1179652
  46.9 3.9 %collective-permute-start.12 = (f32[48,128]{1,0:T(8,128)S(1)}, f32[48,128]{1,0:T(8,128)S(1)}, u32[]{:S(2)}, u32[]{:S(2)}) collective-permute-start(f32[48,128]{1,0:T(8,128)S(1)} %shard_map.49), channel_id=1, source_target_pairs={{0,16},{1,17},{2,18},{3,19},{4,20},{5,21},{6,22},{7,23},{8,24},{9,... | collective-permute-start | bytes 73736 | tf_op jit(solution)/shard_map/ppermute | solution.py:258
  50.8 1.3 %collective-permute-start.13 = (f32[48,128]{1,0:T(8,128)S(1)}, f32[48,128]{1,0:T(8,128)S(1)}, u32[]{:S(2)}, u32[]{:S(2)}) collective-permute-start(f32[48,128]{1,0:T(8,128)S(1)} %get-tuple-element.68), channel_id=1, source_target_pairs={{0,1},{1,0},{2,3},{3,2},{4,5},{5,4},{6,7},{7,6},{8,9},{9,8},{10,11... | collective-permute-start | bytes 73736 | tf_op jit(solution)/shard_map/ppermute | solution.py:258

commit v30 on v27

--- a/solution.py
+++ b/solution.py
@@ -47,7 +47,7 @@
 
 def block_copies(fisher_ref, block, start, held_ref, sem):
     rows, width = held_ref.shape
-    step = 512
+    step = 256
     columns = pl.ds(pl.multiple_of(block * width, width), width)
     return [
         pltpu.make_async_copy(
@@ -109,7 +109,7 @@
         out_shape=out_shape,
         in_specs=[HBM] * bool(fetch) + [VMEM] * (len(ins) + has_base),
         out_specs=[VMEM] * len(out_shape),
-        scratch_shapes=[pltpu.SemaphoreType.DMA((max(len(fetch), 1), 2))],
+        scratch_shapes=[pltpu.SemaphoreType.DMA((max(len(fetch), 1), 4))],
         compiler_params=limit(34 if chunk is None else 20),
         cost_estimate=pl.CostEstimate(
             flops=0 if chunk is None else 2 * chunk.shape[0] * width * total,

time: 51.8 us -> 51.8 us (level)
  no operation moved by 1% of the time
where the time goes in v30:
time: 51.8 us; the launch traced here: 51.6 us
  starting transfers between devices  20.3 us (39%)
  Pallas kernels  20.1 us (39%)
  waiting for transfers between devices  10.4 us (20%)
  other arithmetic  0.65 us (1%)
    ppermute x13, starting transfers between devices, move(): return lax.ppermute(value, AXES, pairs)  20.3 us
    pallas_call x5, Pallas kernels, fisher_step(): pl.pallas_call(functools.partial(fisher_kernel, dims, len(parts), has_bas...  16.7 us
    ppermute x13, waiting for transfers between devices, move(): return lax.ppermute(value, AXES, pairs)  10.4 us
    pallas_call x4, Pallas kernels, score_dot(): pl.pallas_call(functools.partial(score_kernel, dims, order, base is not N...  1.89 us
    pallas_call x1, Pallas kernels, cut(): pl.pallas_call(functools.partial(cut_kernel, dims, order), out_shape=jax....  1.43 us
  transfers between devices with their start and end apart: 13, of which 9 were waited for; matrix products, arithmetic and copies ran while one was open for 0% of the time, Pallas kernels for 36%

profile of v30, /device:TPU:0, one launch (start us, length us, event | category | flops | bytes accessed | tf_op | source)
XLA Modules:
  0.0 51.6 jit_solution(5544696085686567458)
XLA Ops:
  0.0 1.4 %shard_map.37 = bf16[128,6144]{1,0:T(8,128)(2,1)S(1)} custom-call(bf16[128,8192]{1,0:T(8,128)(2,1)} %refs_1_.1), custom_call_target="tpu_custom_call" | custom-call | bytes 1572864 | tf_op jit(solution)/shard_map/pallas_call | solution.py:172
  1.5 4.1 %collective-permute-start = (bf16[48,2048]{1,0:T(8,128)(2,1)S(1)}, bf16[48,2048]{1,0:T(8,128)(2,1)S(1)}, u32[]{:S(2)}, u32[]{:S(2)}) collective-permute-start(bf16[48,2048]{1,0:T(8,128)(2,1)S(1)} %constant_dynamic-slice_fusion.mine_ref), channel_id=1, source_target_pairs={{0,8},{1,6},{2,10},{3,4},{4,12},{5,2},{6,14},{7,0},{8,15},{9,1},{1... | collective-permute-start | bytes 589832 | tf_op jit(solution)/shard_map/ppermute | solution.py:241
  5.6 1.5 %collective-permute-start.8 = (bf16[128,6144]{1,0:T(8,128)(2,1)S(1)}, bf16[128,6144]{1,0:T(8,128)(2,1)S(1)}, u32[]{:S(2)}, u32[]{:S(2)}) collective-permute-start(bf16[128,6144]{1,0:T(8,128)(2,1)S(1)} %shard_map.37), channel_id=1, source_target_pairs={{0,16},{1,17},{2,18},{3,19},{4,20},{5,21},{6,22},{7,23},{8,24},{9,... | collective-permute-start | bytes 4718600 | tf_op jit(solution)/shard_map/ppermute | solution.py:241
  7.1 5.4 %shard_map.38 = (bf16[1024,2048]{1,0:T(8,128)(2,1)S(1)}, bf16[1024,2048]{1,0:T(8,128)(2,1)S(1)}, bf16[1024,2048]{1,0:T(8,128)(2,1)S(1)}, bf16[512,2048]{1,0:T(8,128)(2,1)S(1)}) custom-call(bf16[2048,8192]{1,0:T(8,128)(2,1)} %refs_0_.7), custom_call_target="tpu_custom_call" | custom-call | bytes 14680064 | tf_op jit(solution)/shard_map/pallas_call | solution.py:107
  12.5 1.6 %collective-permute-start.3 = (bf16[48,2048]{1,0:T(8,128)(2,1)S(1)}, bf16[48,2048]{1,0:T(8,128)(2,1)S(1)}, u32[]{:S(2)}, u32[]{:S(2)}) collective-permute-start(bf16[48,2048]{1,0:T(8,128)(2,1)S(1)} %shard_map.39.refs_1_), channel_id=1, source_target_pairs={{0,4},{1,5},{2,6},{3,7},{4,0},{5,1},{6,2},{7,3},{8,12},{9,13},{10,... | collective-permute-start | bytes 589832 | tf_op jit(solution)/shard_map/ppermute | solution.py:241
  14.2 1.5 %collective-permute-start.2 = (bf16[48,2048]{1,0:T(8,128)(2,1)S(1)}, bf16[48,2048]{1,0:T(8,128)(2,1)S(1)}, u32[]{:S(2)}, u32[]{:S(2)}) collective-permute-start(bf16[48,2048]{1,0:T(8,128)(2,1)S(1)} %shard_map.39.refs_1_), channel_id=1, source_target_pairs={{0,2},{1,3},{2,0},{3,1},{4,6},{5,7},{6,4},{7,5},{8,10},{9,11},{10,... | collective-permute-start | bytes 589832 | tf_op jit(solution)/shard_map/ppermute | solution.py:241
  15.7 2.9 %shard_map.40 = (f32[48,2048]{1,0:T(8,128)S(1)}, bf16[512,2048]{1,0:T(8,128)(2,1)S(1)}, bf16[1024,2048]{1,0:T(8,128)(2,1)S(1)}) custom-call(bf16[2048,8192]{1,0:T(8,128)(2,1)} %refs_0_.7, bf16[48,2048]{1,0:T(8,128)(2,1)S(1)} %shard_map.39.refs_1_, bf16[1024,2048]{1,0:T(8,128)(2,1)S(1)} %get-tuple-element.37.refs_0_.refs_2_, ...), custom_call_target="tpu_custom_call" | custom-call | flops 402653184 | bytes 14680064 | tf_op jit(solution)/shard_map/pallas_call | solution.py:107
  18.5 0.5 collective-permute-start.1
  19.0 0.1 collective-permute-done.3.refs_1_
  19.1 2.9 %shard_map.41 = (f32[48,2048]{1,0:T(8,128)S(1)}, bf16[1024,2048]{1,0:T(8,128)(2,1)S(1)}, bf16[512,2048]{1,0:T(8,128)(2,1)S(1)}) custom-call(bf16[2048,8192]{1,0:T(8,128)(2,1)} %refs_0_.7, bf16[48,2048]{1,0:T(8,128)(2,1)S(1)} %collective-permute-done.3.refs_1_, bf16[1024,2048]{1,0:T(8,128)(2,1)S(1)} %get-tuple-element.42.refs_2_, ...), custom_call_target="tpu_custom_call" | custom-call | flops 402653184 | bytes 14680064 | tf_op jit(solution)/shard_map/pallas_call | solution.py:107
  22.0 2.9 %shard_map.42 = (f32[48,2048]{1,0:T(8,128)S(1)}, bf16[512,2048]{1,0:T(8,128)(2,1)S(1)}, bf16[1024,2048]{1,0:T(8,128)(2,1)S(1)}) custom-call(bf16[2048,8192]{1,0:T(8,128)(2,1)} %refs_0_.7, bf16[48,2048]{1,0:T(8,128)(2,1)S(1)} %collective-permute-done.2.refs_1_, bf16[1024,2048]{1,0:T(8,128)(2,1)S(1)} %get-tuple-element.41.refs_2_, ...), custom_call_target="tpu_custom_call" | custom-call | flops 402653184 | bytes 14680064 | tf_op jit(solution)/shard_map/pallas_call | solution.py:107
  25.0 0.2 collective-permute-done.1.refs_0_
  25.2 2.7 %shard_map.43 = f32[48,2048]{1,0:T(8,128)S(1)} custom-call(bf16[48,2048]{1,0:T(8,128)(2,1)S(1)} %collective-permute-done.1.refs_0_, bf16[512,2048]{1,0:T(8,128)(2,1)S(1)} %get-tuple-element.49.refs_1_, bf16[512,2048]{1,0:T(8,128)(2,1)S(1)} %get-tuple-element.50.refs_2_, bf16[1024,2048]{1,0:T(8,128)(2,1)S(1)} %get-tuple-element.51.refs_3_, ...), custom_call_target="tpu_custom_call" | custom-call | flops 402653184 | bytes 8388608 | tf_op jit(solution)/shard_map/pallas_call | solution.py:107
  27.9 0.1 collective-permute-start.4
  27.9 1.7 %collective-permute-done.4 = f32[48,2048]{1,0:T(8,128)S(1)} collective-permute-done((f32[48,2048]{1,0:T(8,128)S(1)}, f32[48,2048]{1,0:T(8,128)S(1)}, u32[]{:S(2)}, u32[]{:S(2)}) %collective-permute-start.4) | collective-permute-done | bytes 393248 | tf_op jit(solution)/shard_map/ppermute | solution.py:241
  29.7 1.8 %collective-permute-start.5 = (bf16[48,2048]{1,0:T(8,128)(2,1)S(1)}, bf16[48,2048]{1,0:T(8,128)(2,1)S(1)}, u32[]{:S(2)}, u32[]{:S(2)}) collective-permute-start(bf16[48,2048]{1,0:T(8,128)(2,1)S(1)} %add_convert_fusion.mine_ref), channel_id=1, source_target_pairs={{0,8},{1,6},{2,10},{3,4},{4,12},{5,2},{6,14},{7,0},{8,15},{9,1},{1... | collective-permute-start | bytes 589832 | tf_op jit(solution)/shard_map/ppermute | solution.py:241
  31.5 4.0 %collective-permute-start.7 = (bf16[48,2048]{1,0:T(8,128)(2,1)S(1)}, bf16[48,2048]{1,0:T(8,128)(2,1)S(1)}, u32[]{:S(2)}, u32[]{:S(2)}) collective-permute-start(bf16[48,2048]{1,0:T(8,128)(2,1)S(1)} %add_convert_fusion.mine_ref), channel_id=1, source_target_pairs={{0,14},{2,12},{4,10},{6,8},{9,7},{11,5},{13,3},{15,1},{16,30},{18,... | collective-permute-start | bytes 589832 | tf_op jit(solution)/shard_map/ppermute | solution.py:241
  35.5 2.4 %collective-permute-done.5.other_ref.mine_ref = bf16[48,2048]{1,0:T(8,128)(2,1)S(1)} collective-permute-done((bf16[48,2048]{1,0:T(8,128)(2,1)S(1)}, bf16[48,2048]{1,0:T(8,128)(2,1)S(1)}, u32[]{:S(2)}, u32[]{:S(2)}) %collective-permute-start.5) | collective-permute-done | bytes 196640 | tf_op jit(solution)/shard_map/ppermute | solution.py:241
  37.9 0.6 %collective-permute-start.6 = (bf16[48,2048]{1,0:T(8,128)(2,1)S(1)}, bf16[48,2048]{1,0:T(8,128)(2,1)S(1)}, u32[]{:S(2)}, u32[]{:S(2)}) collective-permute-start(bf16[48,2048]{1,0:T(8,128)(2,1)S(1)} %shard_map.44.refs_0_), channel_id=1, source_target_pairs={{0,4},{1,5},{2,6},{3,7},{4,0},{5,1},{6,2},{7,3},{8,12},{9,13},{10,... | collective-permute-start | bytes 589832 | tf_op jit(solution)/shard_map/ppermute | solution.py:241
  38.5 3.2 %collective-permute-start.9 = (bf16[48,2048]{1,0:T(8,128)(2,1)S(1)}, bf16[48,2048]{1,0:T(8,128)(2,1)S(1)}, u32[]{:S(2)}, u32[]{:S(2)}) collective-permute-start(bf16[48,2048]{1,0:T(8,128)(2,1)S(1)} %shard_map.44.refs_0_), channel_id=1, source_target_pairs={{0,2},{1,3},{2,0},{3,1},{4,6},{5,7},{6,4},{7,5},{8,10},{9,11},{10,... | collective-permute-start | bytes 589832 | tf_op jit(solution)/shard_map/ppermute | solution.py:241
  41.7 0.6 %collective-permute-start.10 = (bf16[48,2048]{1,0:T(8,128)(2,1)S(1)}, bf16[48,2048]{1,0:T(8,128)(2,1)S(1)}, u32[]{:S(2)}, u32[]{:S(2)}) collective-permute-start(bf16[48,2048]{1,0:T(8,128)(2,1)S(1)} %shard_map.44.refs_0_), channel_id=1, source_target_pairs={{0,16},{1,17},{2,18},{3,19},{4,20},{5,21},{6,22},{7,23},{8,24},{9,... | collective-permute-start | bytes 589832 | tf_op jit(solution)/shard_map/ppermute | solution.py:241
  42.2 2.5 %collective-permute-done.6.refs_0_.refs_1_ = bf16[48,2048]{1,0:T(8,128)(2,1)S(1)} collective-permute-done((bf16[48,2048]{1,0:T(8,128)(2,1)S(1)}, bf16[48,2048]{1,0:T(8,128)(2,1)S(1)}, u32[]{:S(2)}, u32[]{:S(2)}) %collective-permute-start.6) | collective-permute-done | bytes 196640 | tf_op jit(solution)/shard_map/ppermute | solution.py:241
  44.8 0.5 shard_map.46.refs_2_
  45.2 0.3 collective-permute-done.9.refs_0_.refs_2_
  45.6 0.3 shard_map.47
  45.9 0.8 %collective-permute-start.11 = (f32[48,128]{1,0:T(8,128)S(1)}, f32[48,128]{1,0:T(8,128)S(1)}, u32[]{:S(2)}, u32[]{:S(2)}) collective-permute-start(f32[48,128]{1,0:T(8,128)S(1)} %shard_map.47), channel_id=1, source_target_pairs={{0,16},{1,17},{2,18},{3,19},{4,20},{5,21},{6,22},{7,23},{8,24},{9,... | collective-permute-start | bytes 73736 | tf_op jit(solution)/shard_map/ppermute | solution.py:241
  46.7 0.7 %collective-permute-done.10.refs_0_ = bf16[48,2048]{1,0:T(8,128)(2,1)S(1)} collective-permute-done((bf16[48,2048]{1,0:T(8,128)(2,1)S(1)}, bf16[48,2048]{1,0:T(8,128)(2,1)S(1)}, u32[]{:S(2)}, u32[]{:S(2)}) %collective-permute-start.10) | collective-permute-done | bytes 196640 | tf_op jit(solution)/shard_map/ppermute | solution.py:241
  47.4 0.3 shard_map.49.theirs_ref
  47.7 0.8 %shard_map.48.mine_ref = f32[48,128]{1,0:T(8,128)S(1)} custom-call(bf16[48,2048]{1,0:T(8,128)(2,1)S(1)} %shard_map.44.refs_0_, bf16[48,2048]{1,0:T(8,128)(2,1)S(1)} %collective-permute-done.6.refs_0_.refs_1_, bf16[48,2048]{1,0:T(8,128)(2,1)S(1)} %collective-permute-done.9.refs_0_.refs_2_, bf16[48,2048]{1,0:T(8,128)(2,1)S(1)} %shard_map.45.refs_1_.refs_3_, ...), custom_call_target="tpu_custom_call" | custom-call | flops 100663296 | bytes 2097152 | tf_op jit(solution)/shard_map/pallas_call | solution.py:140
  48.5 1.2 %collective-permute-done.11.other_ref = f32[48,128]{1,0:T(8,128)S(1)} collective-permute-done((f32[48,128]{1,0:T(8,128)S(1)}, f32[48,128]{1,0:T(8,128)S(1)}, u32[]{:S(2)}, u32[]{:S(2)}) %collective-permute-start.11) | collective-permute-done | bytes 24608 | tf_op jit(solution)/shard_map/ppermute | solution.py:241
  49.8 1.2 %collective-permute-done.12 = f32[48,128]{1,0:T(8,128)S(1)} collective-permute-done((f32[48,128]{1,0:T(8,128)S(1)}, f32[48,128]{1,0:T(8,128)S(1)}, u32[]{:S(2)}, u32[]{:S(2)}) %collective-permute-start.12) | collective-permute-done | bytes 24608 | tf_op jit(solution)/shard_map/ppermute | solution.py:241
  51.0 0.6 %add.11 = f32[48,128]{1,0:T(8,128)} add(f32[48,128]{1,0:T(8,128)S(1)} %get-tuple-element.61, f32[48,128]{1,0:T(8,128)S(1)} %collective-permute-done.12) | non-fusion elementwise | flops 6144 | bytes 73728 | tf_op jit(solution)/shard_map/add | solution.py:314
  (17 shorter events, 0.2 us)
Async XLA Ops:
  0.0 1.5 %copy-start = (bf16[96,2048]{1,0:T(8,128)(2,1)S(1)}, bf16[96,2048]{1,0:T(8,128)(2,1)}, u32[]{:S(2)}) copy-start(bf16[96,2048]{1,0:T(8,128)(2,1)} %param.3) | copy-start | bytes 1179652
  1.5 11.0 %collective-permute-start = (bf16[48,2048]{1,0:T(8,128)(2,1)S(1)}, bf16[48,2048]{1,0:T(8,128)(2,1)S(1)}, u32[]{:S(2)}, u32[]{:S(2)}) collective-permute-start(bf16[48,2048]{1,0:T(8,128)(2,1)S(1)} %constant_dynamic-slice_fusion.mine_ref), channel_id=1, source_target_pairs={{0,8},{1,6},{2,10},{3,4},{4,12},{5,2},{6,14},{7,0},{8,15},{9,1},{1... | collective-permute-start | bytes 589832 | tf_op jit(solution)/shard_map/ppermute | solution.py:241
  5.6 39.1 %collective-permute-start.8 = (bf16[128,6144]{1,0:T(8,128)(2,1)S(1)}, bf16[128,6144]{1,0:T(8,128)(2,1)S(1)}, u32[]{:S(2)}, u32[]{:S(2)}) collective-permute-start(bf16[128,6144]{1,0:T(8,128)(2,1)S(1)} %shard_map.37), channel_id=1, source_target_pairs={{0,16},{1,17},{2,18},{3,19},{4,20},{5,21},{6,22},{7,23},{8,24},{9,... | collective-permute-start | bytes 4718600 | tf_op jit(solution)/shard_map/ppermute | solution.py:241
  12.5 6.6 %collective-permute-start.3 = (bf16[48,2048]{1,0:T(8,128)(2,1)S(1)}, bf16[48,2048]{1,0:T(8,128)(2,1)S(1)}, u32[]{:S(2)}, u32[]{:S(2)}) collective-permute-start(bf16[48,2048]{1,0:T(8,128)(2,1)S(1)} %shard_map.39.refs_1_), channel_id=1, source_target_pairs={{0,4},{1,5},{2,6},{3,7},{4,0},{5,1},{6,2},{7,3},{8,12},{9,13},{10,... | collective-permute-start | bytes 589832 | tf_op jit(solution)/shard_map/ppermute | solution.py:241
  14.2 7.9 %collective-permute-start.2 = (bf16[48,2048]{1,0:T(8,128)(2,1)S(1)}, bf16[48,2048]{1,0:T(8,128)(2,1)S(1)}, u32[]{:S(2)}, u32[]{:S(2)}) collective-permute-start(bf16[48,2048]{1,0:T(8,128)(2,1)S(1)} %shard_map.39.refs_1_), channel_id=1, source_target_pairs={{0,2},{1,3},{2,0},{3,1},{4,6},{5,7},{6,4},{7,5},{8,10},{9,11},{10,... | collective-permute-start | bytes 589832 | tf_op jit(solution)/shard_map/ppermute | solution.py:241
  18.5 6.6 %collective-permute-start.1 = (bf16[48,2048]{1,0:T(8,128)(2,1)S(1)}, bf16[48,2048]{1,0:T(8,128)(2,1)S(1)}, u32[]{:S(2)}, u32[]{:S(2)}) collective-permute-start(bf16[48,2048]{1,0:T(8,128)(2,1)S(1)} %shard_map.39.refs_1_), channel_id=1, source_target_pairs={{0,6},{1,7},{2,4},{3,5},{4,2},{5,3},{6,0},{7,1},{8,14},{9,15},{10,... | collective-permute-start | bytes 589832 | tf_op jit(solution)/shard_map/ppermute | solution.py:241
  27.9 19.5 %copy-start.2 = (bf16[128,8192]{1,0:T(8,128)(2,1)S(1)}, bf16[128,8192]{1,0:T(8,128)(2,1)}, u32[]{:S(2)}) copy-start(bf16[128,8192]{1,0:T(8,128)(2,1)} %refs_1_.1) | copy-start | bytes 6291460
  27.9 1.8 %collective-permute-start.4 = (f32[48,2048]{1,0:T(8,128)S(1)}, f32[48,2048]{1,0:T(8,128)S(1)}, u32[]{:S(2)}, u32[]{:S(2)}) collective-permute-start(f32[48,2048]{1,0:T(8,128)S(1)} %shard_map.43), channel_id=1, source_target_pairs={{0,1},{1,0},{2,3},{3,2},{4,5},{5,4},{6,7},{7,6},{8,9},{9,8},{10,11... | collective-permute-start | bytes 1179656 | tf_op jit(solution)/shard_map/ppermute | solution.py:241
  29.7 8.2 %collective-permute-start.5 = (bf16[48,2048]{1,0:T(8,128)(2,1)S(1)}, bf16[48,2048]{1,0:T(8,128)(2,1)S(1)}, u32[]{:S(2)}, u32[]{:S(2)}) collective-permute-start(bf16[48,2048]{1,0:T(8,128)(2,1)S(1)} %add_convert_fusion.mine_ref), channel_id=1, source_target_pairs={{0,8},{1,6},{2,10},{3,4},{4,12},{5,2},{6,14},{7,0},{8,15},{9,1},{1... | collective-permute-start | bytes 589832 | tf_op jit(solution)/shard_map/ppermute | solution.py:241
  31.5 10.7 %collective-permute-start.7 = (bf16[48,2048]{1,0:T(8,128)(2,1)S(1)}, bf16[48,2048]{1,0:T(8,128)(2,1)S(1)}, u32[]{:S(2)}, u32[]{:S(2)}) collective-permute-start(bf16[48,2048]{1,0:T(8,128)(2,1)S(1)} %add_convert_fusion.mine_ref), channel_id=1, source_target_pairs={{0,14},{2,12},{4,10},{6,8},{9,7},{11,5},{13,3},{15,1},{16,30},{18,... | collective-permute-start | bytes 589832 | tf_op jit(solution)/shard_map/ppermute | solution.py:241
  37.9 6.8 %collective-permute-start.6 = (bf16[48,2048]{1,0:T(8,128)(2,1)S(1)}, bf16[48,2048]{1,0:T(8,128)(2,1)S(1)}, u32[]{:S(2)}, u32[]{:S(2)}) collective-permute-start(bf16[48,2048]{1,0:T(8,128)(2,1)S(1)} %shard_map.44.refs_0_), channel_id=1, source_target_pairs={{0,4},{1,5},{2,6},{3,7},{4,0},{5,1},{6,2},{7,3},{8,12},{9,13},{10,... | collective-permute-start | bytes 589832 | tf_op jit(solution)/shard_map/ppermute | solution.py:241
  38.5 7.1 %collective-permute-start.9 = (bf16[48,2048]{1,0:T(8,128)(2,1)S(1)}, bf16[48,2048]{1,0:T(8,128)(2,1)S(1)}, u32[]{:S(2)}, u32[]{:S(2)}) collective-permute-start(bf16[48,2048]{1,0:T(8,128)(2,1)S(1)} %shard_map.44.refs_0_), channel_id=1, source_target_pairs={{0,2},{1,3},{2,0},{3,1},{4,6},{5,7},{6,4},{7,5},{8,10},{9,11},{10,... | collective-permute-start | bytes 589832 | tf_op jit(solution)/shard_map/ppermute | solution.py:241
  41.7 5.7 %collective-permute-start.10 = (bf16[48,2048]{1,0:T(8,128)(2,1)S(1)}, bf16[48,2048]{1,0:T(8,128)(2,1)S(1)}, u32[]{:S(2)}, u32[]{:S(2)}) collective-permute-start(bf16[48,2048]{1,0:T(8,128)(2,1)S(1)} %shard_map.44.refs_0_), channel_id=1, source_target_pairs={{0,16},{1,17},{2,18},{3,19},{4,20},{5,21},{6,22},{7,23},{8,24},{9,... | collective-permute-start | bytes 589832 | tf_op jit(solution)/shard_map/ppermute | solution.py:241
  44.7 6.9 %copy-start.1 = (bf16[96,2048]{1,0:T(8,128)(2,1)S(1)}, bf16[96,2048]{1,0:T(8,128)(2,1)}, u32[]{:S(2)}) copy-start(bf16[96,2048]{1,0:T(8,128)(2,1)} %param.3) | copy-start | bytes 1179652
  45.9 3.9 %collective-permute-start.11 = (f32[48,128]{1,0:T(8,128)S(1)}, f32[48,128]{1,0:T(8,128)S(1)}, u32[]{:S(2)}, u32[]{:S(2)}) collective-permute-start(f32[48,128]{1,0:T(8,128)S(1)} %shard_map.47), channel_id=1, source_target_pairs={{0,16},{1,17},{2,18},{3,19},{4,20},{5,21},{6,22},{7,23},{8,24},{9,... | collective-permute-start | bytes 73736 | tf_op jit(solution)/shard_map/ppermute | solution.py:241
  49.8 1.3 %collective-permute-start.12 = (f32[48,128]{1,0:T(8,128)S(1)}, f32[48,128]{1,0:T(8,128)S(1)}, u32[]{:S(2)}, u32[]{:S(2)}) collective-permute-start(f32[48,128]{1,0:T(8,128)S(1)} %get-tuple-element.62), channel_id=1, source_target_pairs={{0,1},{1,0},{2,3},{3,2},{4,5},{5,4},{6,7},{7,6},{8,9},{9,8},{10,11... | collective-permute-start | bytes 73736 | tf_op jit(solution)/shard_map/ppermute | solution.py:241
